TPU v7x, 32 devices: a whole 2x2x4 slice. The times are simulated.
32 devices in a mesh: ctx: 8 (over y, x, core), head: 4 (over z).
Axes of the slice: x: 2, y: 2, z: 4, core: 2. Of those that a mesh axis runs over, the one named last changes fastest.
Arguments:
- hidden_in: bfloat16 [2048, 2048], P('ctx'), may hold values from -6 to 6
- gain_attn: float32 [2048], replicated, may hold values from 0.1 to 1.9
- w_qkv: bfloat16 [2048, 3, 2048], P(None, None, 'head'), may hold values from -0.125 to 0.125
- conv_w: float32 [4, 3, 2048], P(None, None, 'head'), may hold values from -3 to 3
- log_decay: float32 [2048, 16], P('ctx', 'head'), may hold values from -1 to 0, as said below
- norm_gain: float32 [2048], P('head'), may hold values from 0.1 to 1.9
- w_out: bfloat16 [2048, 2048], P('head'), may hold values from -0.125 to 0.125
- gain_moe: float32 [2048], replicated, may hold values from 0.1 to 1.9
- expert_ids: int32 [2048, 8], P('ctx'), may hold values from 0 to 15, all different within a row; in each aligned block of 256 rows (0 to 255, 256 to 511, ...) at most 192 rows name the same one
- route_weights: float32 [2048, 8], P('ctx'), may hold values from 0.05 to 1
- w_gate: bfloat16 [32, 2048, 512], P(('ctx', 'head')), may hold values from -0.125 to 0.125
- w_up: bfloat16 [32, 2048, 512], P(('ctx', 'head')), may hold values from -0.125 to 0.125
- w_down: bfloat16 [32, 512, 2048], P(('ctx', 'head')), may hold values from -0.1875 to 0.1875
- grad_core: bfloat16 [2048, 2048], P('ctx', 'head'), may hold values from -6 to 6
Outputs:
- layer_out: bfloat16 [2048, 2048], P('ctx', 'head')
- grad_q: bfloat16 [2048, 2048], P('ctx', 'head')
- grad_k: bfloat16 [2048, 2048], P('ctx', 'head')
- grad_v: bfloat16 [2048, 2048], P('ctx', 'head')
Inputs may be any that keep to these rules, and one draw needn't show every extreme that they name: `expert_ids`: in each aligned block of 256 rows (the tokens of one index of ctx) no expert is chosen by more than 192 rows, a bound that some block reaches; the 8 experts of a row differ. `log_decay`: every entry is negative.
All inputs are finite; a program needn't handle non-finite values.
Results may differ from a plain program's by a relative error of at most 0.023.
Values may be sent and summed in bfloat16 or wider, within the bound.
No kernel may reach another device: no remote copies, remote signals or barrier semaphores. Data moves between devices by JAX's collectives and lax.ppermute only.
A program may use at most 128 MiB of HBM per device.

v0:
```python
import jax
import jax.numpy as jnp
from jax import lax
from jax.sharding import PartitionSpec as P

KERNEL = 4
TOP = 8
EXP_CTX = 2


def shifted(value, axis, steps):
    count = lax.axis_size(axis)
    first, last = (max(0, -steps), min(count, count - steps))
    return lax.ppermute(value, axis, [(source, source + steps) for source in range(first, last)])


def entering(value, axis, join, neutral, backward):
    count, mine = (lax.axis_size(axis), lax.axis_index(axis))
    pieces = jax.tree.map(lambda part: lax.all_gather(part, axis), value)
    if backward:
        pieces = jax.tree.map(lambda part: part[::-1], pieces)
        mine = count - 1 - mine
    total = jax.tree.map(
        lambda part, zero: jnp.full_like(part, 0) + jnp.asarray(zero, part.dtype), value, neutral
    )

    def hop(position, total):
        longer = join(total, jax.tree.map(lambda part: part[position], pieces))
        return jax.tree.map(lambda new, old: jnp.where(position < mine, new, old), longer, total)

    return lax.fori_loop(0, count - 1, hop, total)


def rms_norm(values, gain):
    return values * lax.rsqrt(jnp.mean(values * values, axis=-1, keepdims=True) + 1e-06) * gain


def link(earlier, later):
    return (earlier[0] * later[0], later[0][:, None, None] * earlier[1] + later[1])


def body(
    hidden_in,
    gain_attn,
    w_qkv,
    conv_w,
    log_decay,
    norm_gain,
    w_out,
    gain_moe,
    expert_ids,
    route_weights,
    w_gate,
    w_up,
    w_down,
    grad_core,
):
    hi = lax.Precision.HIGHEST
    n_ctx = lax.axis_size("ctx")
    n_head = lax.axis_size("head")
    my_head = lax.axis_index("head")
    tok_dev, width = hidden_in.shape
    chans = w_qkv.shape[2]
    heads_here = log_decay.shape[1]
    head_size = chans // heads_here
    experts = EXP_CTX * n_ctx
    cap = 3 * tok_dev * TOP // (2 * experts)
    shards = n_head // EXP_CTX
    local_expert = my_head // shards
    cols = width // n_head
    x_float = hidden_in.astype(jnp.float32)
    normed = rms_norm(x_float, gain_attn).astype(jnp.bfloat16)
    mixed = jnp.einsum("ti,icj->tcj", normed, w_qkv, preferred_element_type=jnp.float32).astype(
        jnp.bfloat16
    )
    rim = shifted(mixed[tok_dev - (KERNEL - 1) :], "ctx", 1)
    padded = jnp.concatenate([rim, mixed], axis=0).astype(jnp.float32)
    conv_out = jnp.zeros(mixed.shape, jnp.float32)
    for offset in range(KERNEL):
        conv_out = (
            conv_out + conv_w[offset] * padded[KERNEL - 1 - offset : KERNEL - 1 - offset + tok_dev]
        )
    activ = jax.nn.silu(conv_out)
    shape3 = (tok_dev, heads_here, head_size)
    queries = (activ[:, 0] * head_size ** (-0.5)).astype(jnp.bfloat16).reshape(shape3)
    key_rows = activ[:, 1].astype(jnp.bfloat16).reshape(shape3)
    val_rows = activ[:, 2].astype(jnp.bfloat16).reshape(shape3)
    query_f = queries.astype(jnp.float32)
    key_f = key_rows.astype(jnp.float32)
    value_f = val_rows.astype(jnp.float32)
    cot_rows = grad_core.reshape(shape3)
    cot_f = cot_rows.astype(jnp.float32)
    cum_decay = jnp.cumsum(log_decay, axis=0)
    cum_t = cum_decay.T
    diff = cum_t[:, :, None] - cum_t[:, None, :]
    lower = (jnp.arange(tok_dev)[:, None] >= jnp.arange(tok_dev)[None, :])[None]
    decay_mask = jnp.where(lower, jnp.exp(jnp.where(lower, diff, 0.0)), 0.0)
    scores = (
        jnp.einsum("thd,shd->hts", queries, key_rows, preferred_element_type=jnp.float32)
        * decay_mask
    )
    tail = jnp.exp(cum_decay[-1][None, :] - cum_decay)
    lead_decay = jnp.exp(cum_decay)
    summary = jnp.einsum("shd,she->hde", key_f * tail[:, :, None], value_f, precision=hi)
    backsum = jnp.einsum("thd,the->hde", query_f * lead_decay[:, :, None], cot_f, precision=hi)
    zeros_state = jnp.zeros((heads_here, head_size, head_size), jnp.float32)
    block_decay = jnp.exp(cum_decay[-1])
    identity = (jnp.ones((heads_here,), jnp.float32), zeros_state)
    _, state_in = entering((block_decay, summary), "ctx", link, identity, False)
    _, grad_in = entering((block_decay, backsum), "ctx", link, identity, True)
    local = jnp.einsum("hts,shd->thd", scores, value_f, precision=hi)
    carried = jnp.einsum("thd,hde->the", query_f, state_in, precision=hi) * lead_decay[:, :, None]
    attended = local + carried
    dov = (
        jnp.einsum("thd,shd->hts", cot_rows, val_rows, preferred_element_type=jnp.float32)
        * decay_mask
    )
    grad_q = jnp.einsum("hts,shd->thd", dov, key_f, precision=hi)
    grad_q = grad_q + lead_decay[:, :, None] * jnp.einsum(
        "the,hde->thd", cot_f, state_in, precision=hi
    )
    grad_k = jnp.einsum("hts,thd->shd", dov, query_f, precision=hi)
    grad_k = grad_k + tail[:, :, None] * jnp.einsum("the,hde->thd", value_f, grad_in, precision=hi)
    grad_v = jnp.einsum("hts,the->she", scores, cot_f, precision=hi)
    grad_v = grad_v + tail[:, :, None] * jnp.einsum("thd,hde->the", key_f, grad_in, precision=hi)
    headed = rms_norm(attended, norm_gain.reshape(heads_here, head_size)).reshape(tok_dev, chans)
    headed = headed.astype(jnp.bfloat16)
    partial_out = jnp.dot(headed, w_out, preferred_element_type=jnp.float32)
    attn_total = lax.psum(partial_out.astype(jnp.bfloat16), "head").astype(jnp.float32)
    resid_full = x_float + attn_total
    moe_in = rms_norm(resid_full, gain_moe).astype(jnp.bfloat16)
    resid_mine = lax.dynamic_slice_in_dim(resid_full, my_head * cols, cols, 1)
    hot = (expert_ids[:, :, None] == jnp.arange(experts, dtype=jnp.int32)).astype(jnp.int32)
    counts = jnp.sum(hot, axis=1)
    ranks = jnp.cumsum(counts, axis=0) - counts
    slot = jnp.sum(hot * ranks[:, None, :], axis=-1)
    owner = expert_ids // EXP_CTX
    local_id = expert_ids % EXP_CTX
    picked = local_id == local_expert
    source_rows = jnp.broadcast_to(moe_in[:, None, :], (tok_dev, TOP, width)).reshape(-1, width)
    total = jnp.zeros((tok_dev, width), jnp.float32)
    positions = jnp.where(picked, owner * cap + slot, n_ctx * cap).reshape(-1)
    buffer = (
        jnp.zeros((n_ctx * cap, width), jnp.bfloat16).at[positions].set(source_rows, mode="drop")
    )
    buffer = buffer.reshape(n_ctx, cap, width)
    batch = lax.all_to_all(buffer, "ctx", split_axis=0, concat_axis=0, tiled=True)
    gate_val = jnp.einsum("ncd,df->ncf", batch, w_gate[0], preferred_element_type=jnp.float32)
    up_val = jnp.einsum("ncd,df->ncf", batch, w_up[0], preferred_element_type=jnp.float32)
    inner = (jax.nn.silu(gate_val) * up_val).astype(jnp.bfloat16)
    returned = lax.all_to_all(
        jnp.einsum("ncf,fd->ncd", inner, w_down[0], preferred_element_type=jnp.float32).astype(
            jnp.bfloat16
        ),
        "ctx",
        split_axis=0,
        concat_axis=0,
        tiled=True,
    )
    flat_back = returned.reshape(n_ctx * cap, width)
    fetch = jnp.where(picked, owner * cap + slot, 0)
    weights = jnp.where(picked, route_weights, 0.0)
    for chosen in range(TOP):
        total = total + weights[:, chosen, None] * flat_back[fetch[:, chosen]].astype(jnp.float32)
    moe_out = lax.psum_scatter(
        total.astype(jnp.bfloat16), "head", scatter_dimension=1, tiled=True
    ).astype(jnp.float32)
    layer_out = (resid_mine + moe_out).astype(jnp.bfloat16)
    return (
        layer_out,
        grad_q.reshape(tok_dev, chans).astype(jnp.bfloat16),
        grad_k.reshape(tok_dev, chans).astype(jnp.bfloat16),
        grad_v.reshape(tok_dev, chans).astype(jnp.bfloat16),
    )


def solution(mesh):
    in_specs = (
        P("ctx", None),
        P(),
        P(None, None, "head"),
        P(None, None, "head"),
        P("ctx", "head"),
        P("head"),
        P("head", None),
        P(),
        P("ctx", None),
        P("ctx", None),
        P(("ctx", "head"), None, None),
        P(("ctx", "head"), None, None),
        P(("ctx", "head"), None, None),
        P("ctx", "head"),
    )
    out_specs = (P("ctx", "head"), P("ctx", "head"), P("ctx", "head"), P("ctx", "head"))
    return jax.shard_map(body, mesh=mesh, in_specs=in_specs, out_specs=out_specs, check_vma=False)
```

profile of v0, /device:TPU:0, one launch (start us, length us, event | category | flops | bytes accessed | tf_op | source)
XLA Modules:
  0.0 413.9 jit_solution(15171023460581118956)
XLA Ops:
  7.2 1.6 fusion.6
  8.9 5.0 %convolution_convert_fusion.2 = bf16[256,3,512]{2,0,1:T(8,128)(2,1)S(1)} fusion(bf16[2048,3,512]{2,0,1:T(8,128)(2,1)} %param.20, bf16[256,2048]{1,0:T(8,128)(2,1)} %param.18, f32[2048]{0:T(1024)} %param.19, f32[256]{0:T(256)S(1)} %add_rsqrt_fusion.2), kind=kOutput, calls=%fused_computation.43 | convolution fusion | flops 1613103104 | bytes 8135680 | tf_op jit(solution)/shard_map/ti,icj->tcj/dot_general | solution.py:73
  13.9 2.4 collective-permute-start
  16.3 1.2 reduce-window.14
  17.9 0.2 slice_reduce_fusion.1
  18.3 0.2 maximum_convert_fusion
  18.5 2.1 fusion.58
  21.0 1.1 fusion.38
  22.2 12.0 %all-gather.2 = f32[8,1,4]{2,1,0:T(1,128)S(1)} all-gather(f32[1,1,4]{2,1,0:T(1,128)S(1)} %bitcast.220), channel_id=1, replica_groups=mesh['ctx'=8,'head'=4] {'ctx'}, dimensions={0}, use_global_device_ids=true | all-gather | bytes 144 | tf_op jit(solution)/shard_map/all_gather | solution.py:19
  34.3 0.5 copy-done.21
  34.9 0.6 reduce-window.16
  35.5 0.2 slice_reduce_fusion
  35.7 1.1 fusion.34
  37.0 1.4 convolution_multiply_fusion
  38.5 15.1 %all-gather.6.cloned.1.call-done = f32[32,128,128]{2,1,0:T(8,128)} async-done(((f32[4,128,128]{2,1,0:T(8,128)}), f32[32,128,128]{2,1,0:T(8,128)}) %all-gather.6.cloned.1.call-update) | async-done | bytes 2097168 | tf_op jit(solution)/shard_map/all_gather | solution.py:19
  53.6 7.6 %while.28 = (s32[]{:T(128)}, f32[4,128,128]{2,1,0:T(8,128)S(1)}, s32[]{:T(128)}, f32[8,4]{1,0:T(8,128)S(1)}, f32[8,4,128,128]{3,2,1,0:T(8,128)}, /*index=5*/s32[]{:T(128)}, s32[]{:T(128)}) while((s32[]{:T(128)}, f32[4,128,128]{2,1,0:T(8,128)S(1)}, s32[]{:T(128)}, f32[8,4]{1,0:T(8,128)S(1)}, f32[8,4,128,128]{3,2,1,0:T(8,128)}, ...), condition=%wide.region_4.5_spmd.clone, body=%wide.region_3.4_spmd.clone.sunk | while | flops 262148 | bytes 786593 | solution.py:31
  53.6 1.1 fusion.86
  54.7 1.1 fusion.86
  55.8 1.1 fusion.86
  56.8 1.1 fusion.86
  57.9 1.1 fusion.86
  59.0 1.1 fusion.86
  60.1 1.1 fusion.86
  61.2 0.4 fusion.21
  61.7 2.1 multiply_reduce_fusion.1
  64.0 1.7 convolution_convert_fusion.1
  65.9 0.6 broadcast_select_fusion.1
  66.5 0.6 broadcast_select_fusion.2
  67.4 50.3 %all-reduce.2.cloned.1.call-done = bf16[256,2048]{1,0:T(8,128)(2,1)} async-done(((bf16[256,2048]{1,0:T(8,128)(2,1)}), bf16[256,2048]{1,0:T(8,128)(2,1)}) %all-reduce.2.cloned.1.call-update) | async-done | bytes 1048592 | tf_op jit(solution)/shard_map/psum | solution.py:129
  117.7 3.0 convert_add_fusion
  120.7 1.5 multiply_convert_fusion.1
  122.2 16.3 %scatter_custom_fusion = bf16[1536,2048]{1,0:T(8,128)(2,1)} fusion(s32[2048]{0:T(1024)S(1)} %bitcast.200, bf16[256,2048]{1,0:T(8,128)(2,1)} %multiply_convert_fusion.1, bf16[]{:T(256)} %constant.128.clone.1), kind=kCustom, calls=%fused_computation.15 | custom fusion | bytes 7340034 | tf_op jit(solution)/shard_map/scatter | solution.py:144
  138.5 75.8 %all_to_all.10 = bf16[8,192,2048]{2,1,0:T(8,128)(2,1)S(1)} all-to-all(bf16[8,192,2048]{2,1,0:T(8,128)(2,1)} %bitcast.180), channel_id=1, replica_groups=mesh['ctx'=8,'head'=4] {'ctx'}, dimensions={0} | all-to-all | bytes 12582912 | tf_op jit(solution)/shard_map/all_to_all | solution.py:147
  214.3 2.7 copy-done.3
  217.0 5.1 %fusion.10 = f32[8,192,512]{2,1,0:T(8,128)} fusion(bf16[8,192,2048]{2,1,0:T(8,128)(2,1)S(1)} %all_to_all.10, bf16[1,2048,512]{2,1,0:T(8,128)(2,1)S(1)} %copy-done.32), kind=kOutput, calls=%fused_computation.29 | convolution fusion | flops 3221225472 | bytes 11534336 | tf_op jit(solution)/shard_map/ncd,df->ncf/dot_general | solution.py:149
  222.1 11.9 %convolution_convert_fusion = bf16[8,192,2048]{2,1,0:T(8,128)(2,1)} fusion(bf16[1,512,2048]{2,1,0:T(8,128)(2,1)S(1)} %copy-done, f32[8,192,512]{2,1,0:T(8,128)} %fusion.10, bf16[8,192,2048]{2,1,0:T(8,128)(2,1)} %copy-done.3, bf16[1,2048,512]{2,1,0:T(8,128)(2,1)} %param.28), kind=kOutput, calls=%fused_computation.17 | convolution fusion | flops 6450315264 | bytes 19922944 | tf_op jit(solution)/shard_map/ncf,fd->ncd/dot_general | solution.py:152
  234.1 4.9 %all-to-all-start.1 = ((bf16[8,192,2048]{2,1,0:T(8,128)(2,1)}), bf16[8,192,2048]{2,1,0:T(8,128)(2,1)}, u32[]{:S(2)}, u32[]{:S(2)}) async-start(bf16[8,192,2048]{2,1,0:T(8,128)(2,1)} %convolution_convert_fusion), calls=%async_computation.1 | async-start | bytes 12582912 | tf_op jit(solution)/shard_map/all_to_all | solution.py:151
  239.2 1.1 fusion.35
  240.7 0.6 fusion.61
  241.4 1.4 fusion.16
  242.8 49.8 %all-gather.8.cloned.1.call-done = f32[32,128,128]{2,1,0:T(8,128)} async-done(((f32[4,128,128]{2,1,0:T(8,128)}), f32[32,128,128]{2,1,0:T(8,128)}) %all-gather.8.cloned.1.call-update) | async-done | bytes 2097168 | tf_op jit(solution)/shard_map/all_gather | solution.py:19
  292.6 1.8 rev.7
  294.4 24.6 %all-to-all-done.1 = bf16[8,192,2048]{2,1,0:T(8,128)(2,1)} async-done(((bf16[8,192,2048]{2,1,0:T(8,128)(2,1)}), bf16[8,192,2048]{2,1,0:T(8,128)(2,1)}, u32[]{:S(2)}, u32[]{:S(2)}) %all-to-all-start.1) | async-done | bytes 6291488 | tf_op jit(solution)/shard_map/all_to_all | solution.py:151
  319.0 6.9 %gather_fusion.7 = bf16[256,2048]{1,0:T(8,128)(2,1)} fusion(bf16[1536,2048]{1,0:T(8,128)(2,1)} %bitcast.22, s32[1024]{0:T(1024)S(1)} %pad_clamp_fusion), kind=kCustom, calls=%fused_computation.7 | custom fusion | bytes 2098176 | tf_op jit(solution)/shard_map/gather | solution.py:164
  326.0 6.9 %gather_fusion.6 = bf16[256,2048]{1,0:T(8,128)(2,1)} fusion(bf16[1536,2048]{1,0:T(8,128)(2,1)} %bitcast.22, s32[1024]{0:T(1024)S(1)} %pad_clamp_fusion.1), kind=kCustom, calls=%fused_computation.6 | custom fusion | bytes 2098176 | tf_op jit(solution)/shard_map/gather | solution.py:164
  332.9 7.0 %gather_fusion.5 = bf16[256,2048]{1,0:T(8,128)(2,1)} fusion(bf16[1536,2048]{1,0:T(8,128)(2,1)} %bitcast.22, s32[1024]{0:T(1024)S(1)} %pad_clamp_fusion.2), kind=kCustom, calls=%fused_computation.5 | custom fusion | bytes 2098176 | tf_op jit(solution)/shard_map/gather | solution.py:164
  339.9 7.0 %gather_fusion.4 = bf16[256,2048]{1,0:T(8,128)(2,1)} fusion(bf16[1536,2048]{1,0:T(8,128)(2,1)} %bitcast.22, s32[1024]{0:T(1024)S(1)} %pad_clamp_fusion.3), kind=kCustom, calls=%fused_computation.4 | custom fusion | bytes 2098176 | tf_op jit(solution)/shard_map/gather | solution.py:164
  347.0 7.1 %gather_fusion.3 = bf16[256,2048]{1,0:T(8,128)(2,1)} fusion(bf16[1536,2048]{1,0:T(8,128)(2,1)} %bitcast.22, s32[1024]{0:T(1024)S(1)} %pad_clamp_fusion.4), kind=kCustom, calls=%fused_computation.3 | custom fusion | bytes 2098176 | tf_op jit(solution)/shard_map/gather | solution.py:164
  354.1 6.9 %gather_fusion.2 = bf16[256,2048]{1,0:T(8,128)(2,1)} fusion(bf16[1536,2048]{1,0:T(8,128)(2,1)} %bitcast.22, s32[1024]{0:T(1024)S(1)} %pad_clamp_fusion.5), kind=kCustom, calls=%fused_computation.2 | custom fusion | bytes 2098176 | tf_op jit(solution)/shard_map/gather | solution.py:164
  361.0 7.0 %gather_fusion.1 = bf16[256,2048]{1,0:T(8,128)(2,1)} fusion(bf16[1536,2048]{1,0:T(8,128)(2,1)} %bitcast.22, s32[1024]{0:T(1024)S(1)} %pad_clamp_fusion.6), kind=kCustom, calls=%fused_computation.1 | custom fusion | bytes 2098176 | tf_op jit(solution)/shard_map/gather | solution.py:164
  368.0 7.0 %gather_fusion = bf16[256,2048]{1,0:T(8,128)(2,1)} fusion(bf16[1536,2048]{1,0:T(8,128)(2,1)} %bitcast.22, s32[1024]{0:T(1024)S(1)} %pad_clamp_fusion.7), kind=kCustom, calls=%fused_computation | custom fusion | bytes 2098176 | tf_op jit(solution)/shard_map/gather | solution.py:164
  375.0 5.3 %add_convert_fusion = bf16[256,2048]{1,0:T(8,128)(2,1)} fusion(bf16[256,2048]{1,0:T(8,128)(2,1)} %gather_fusion.7, bf16[256,2048]{1,0:T(8,128)(2,1)} %gather_fusion.6, bf16[256,2048]{1,0:T(8,128)(2,1)} %gather_fusion.5, bf16[256,2048]{1,0:T(8,128)(2,1)} %gather_fusion.4, bf16[256,2048]{1,0:T(8,128)(2,1)} %gather_fusion.3, ...), kind=kLoop, calls=%fused_computation.32 | loop fusion | flops 12582912 | bytes 9445376 | tf_op jit(solution)/shard_map/convert_element_type | solution.py:166
  380.3 1.0 while.29
  381.4 1.4 fusion.24
  382.7 1.9 fusion.27
  384.6 0.8 copy.211
  385.5 0.4 fusion.22
  385.9 0.7 fusion.25
  386.6 0.8 copy.209
  387.4 0.4 fusion.23
  387.8 1.9 fusion.26
  389.7 0.8 copy.210
  390.6 14.7 %reduce-scatter.2.cloned.1.call-done = bf16[256,512]{1,0:T(8,128)(2,1)} async-done(((bf16[256,2048]{1,0:T(8,128)(2,1)}), bf16[256,512]{1,0:T(8,128)(2,1)}) %reduce-scatter.2.cloned.1.call-update) | async-done | bytes 262160 | tf_op jit(solution)/shard_map/reduce_scatter | solution.py:165
  405.2 1.9 add_convert_fusion.1
  (143 shorter events, 3.4 us)
Async XLA Ops:
  7.2 215.0 %copy-start = (bf16[1,512,2048]{2,1,0:T(8,128)(2,1)S(1)}, bf16[1,512,2048]{2,1,0:T(8,128)(2,1)}, u32[]{:S(2)}) copy-start(bf16[1,512,2048]{2,1,0:T(8,128)(2,1)} %param.30) | copy-start | bytes 6291460
  7.2 46.4 %all-gather.6.cloned.1.call-start = ((), (), s32[]{:S(2)}) async-start(), calls=%async_computation.5 | async-start | bytes 2359296 | tf_op jit(solution)/shard_map/all_gather | solution.py:19
  8.9 7.4 %copy-start.28 = (f32[256,4]{0,1:T(4,128)S(1)}, f32[256,4]{0,1:T(4,128)}, u32[]{:S(2)}) copy-start(f32[256,4]{0,1:T(4,128)} %param.22) | copy-start | bytes 12292
  8.9 9.2 %copy-start.20 = (f32[4,3,512]{2,0,1:T(4,128)S(1)}, f32[4,3,512]{2,0,1:T(4,128)}, u32[]{:S(2)}) copy-start(f32[4,3,512]{2,0,1:T(4,128)} %param.21) | copy-start | bytes 73732
  13.9 4.4 %collective-permute-start = (bf16[3,3,512]{2,0,1:T(4,128)(2,1)S(1)}, bf16[3,3,512]{2,0,1:T(4,128)(2,1)S(1)}, u32[]{:S(2)}, u32[]{:S(2)}) collective-permute-start(bf16[3,3,512]{2,0,1:T(4,128)(2,1)S(1)} %slice.151), channel_id=1, source_target_pairs={{0,4},{4,8},{8,12},{12,16},{16,20},{20,24},{24,28},{1,5},{5,9},{9,... | collective-permute-start | bytes 27656 | tf_op jit(solution)/shard_map/ppermute | solution.py:14
  17.9 19.1 %copy-start.23 = (f32[1,4,2,128]{3,1,2,0:T(4,128)}, f32[1,4,2,128]{3,1,2,0:T(4,128)S(1)}, u32[]{:S(2)}) copy-start(f32[1,4,2,128]{3,1,2,0:T(4,128)S(1)} %copy.251) | copy-start | bytes 12292
  20.6 14.2 %copy-start.15 = (s32[256,8]{0,1:T(8,128)S(1)}, s32[256,8]{0,1:T(8,128)}, u32[]{:S(2)}) copy-start(s32[256,8]{0,1:T(8,128)} %param.26) | copy-start | bytes 24580
  20.7 40.9 %copy-start.5 = (bf16[256,4,128]{2,1,0:T(4,128)(2,1)}, bf16[256,4,128]{2,1,0:T(4,128)(2,1)S(1)}, u32[]{:S(2)}) copy-start(bf16[256,4,128]{2,1,0:T(4,128)(2,1)S(1)} %convert_element_type.116) | copy-start | bytes 786436
  20.8 17.6 %copy-start.10 = (bf16[256,4,128]{2,1,0:T(4,128)(2,1)}, bf16[256,4,128]{2,1,0:T(4,128)(2,1)S(1)}, u32[]{:S(2)}) copy-start(bf16[256,4,128]{2,1,0:T(4,128)(2,1)S(1)} %convert_element_type.119) | copy-start | bytes 786436
  21.0 13.2 %copy-start.11 = (bf16[256,4,128]{0,2,1:T(8,128)(2,1)}, bf16[256,4,128]{0,2,1:T(8,128)(2,1)S(1)}, u32[]{:S(2)}) copy-start(bf16[256,4,128]{0,2,1:T(8,128)(2,1)S(1)} %copy.188) | copy-start | bytes 786436
  22.1 95.6 %all-reduce.2.cloned.1.call-start = ((), (), s32[]{:S(2)}) async-start(), calls=%async_computation.3 | async-start | bytes 2097152 | tf_op jit(solution)/shard_map/psum | solution.py:129
  34.3 0.6 copy-start.21
  35.7 17.8 %copy-start.27 = (s32[16,3]{0,1:T(4,128)}, s32[16,3]{0,1:T(4,128)S(1)}, u32[]{:S(2)}) copy-start(s32[16,3]{0,1:T(4,128)S(1)} %reduce-window.19) | copy-start | bytes 580
  35.7 17.8 %copy-start.16 = (pred[256,256]{1,0:T(8,128)(4,1)}, pred[256,256]{1,0:T(8,128)(4,1)S(1)}, u32[]{:S(2)}) copy-start(pred[256,256]{1,0:T(8,128)(4,1)S(1)} %iota_compare_fusion) | copy-start | bytes 196612
  37.0 24.2 %copy-start.8 = (bf16[256,1,512]{0,2,1:T(8,128)(2,1)}, bf16[256,1,512]{0,2,1:T(8,128)(2,1)S(1)}, u32[]{:S(2)}) copy-start(bf16[256,1,512]{0,2,1:T(8,128)(2,1)S(1)} %copy.219) | copy-start | bytes 786436
  61.2 2.6 copy-start.31
  61.2 2.8 copy-start.13
  64.0 1.8 slice-start
  64.0 1.9 copy-start.26
  64.0 53.7 %copy-start.2 = (bf16[256,2048]{1,0:T(8,128)(2,1)S(1)}, bf16[256,2048]{1,0:T(8,128)(2,1)}, u32[]{:S(2)}) copy-start(bf16[256,2048]{1,0:T(8,128)(2,1)} %param.18) | copy-start | bytes 3145732
  67.4 53.3 %copy-start.25 = (f32[2048]{0:T(1024)S(1)}, f32[2048]{0:T(1024)}, u32[]{:S(2)}) copy-start(f32[2048]{0:T(1024)} %param.25) | copy-start | bytes 24580
  117.7 3.0 copy-start.4
  138.5 78.5 %copy-start.32 = (bf16[1,2048,512]{2,1,0:T(8,128)(2,1)S(1)}, bf16[1,2048,512]{2,1,0:T(8,128)(2,1)}, u32[]{:S(2)}) copy-start(bf16[1,2048,512]{2,1,0:T(8,128)(2,1)} %param.29) | copy-start | bytes 6291460
  214.3 2.7 copy-start.3
  234.1 5.0 %copy-start.14 = (bf16[256,512]{1,0:T(8,128)(2,1)S(1)}, bf16[256,512]{1,0:T(8,128)(2,1)}, u32[]{:S(2)}) copy-start(bf16[256,512]{1,0:T(8,128)(2,1)} %param.31) | copy-start | bytes 786436
  234.1 5.2 %copy-start.9 = (bf16[256,1,512]{0,2,1:T(8,128)(2,1)S(1)}, bf16[256,1,512]{0,2,1:T(8,128)(2,1)}, u32[]{:S(2)}) copy-start(bf16[256,1,512]{0,2,1:T(8,128)(2,1)} %copy-done.8) | copy-start | bytes 786436
  234.1 6.3 %copy-start.22 = (f32[8,1,4]{0,2,1:T(4,128)S(1)}, f32[8,1,4]{0,2,1:T(4,128)}, u32[]{:S(2)}) copy-start(f32[8,1,4]{0,2,1:T(4,128)} %copy-done.21) | copy-start | bytes 388
  234.1 6.5 %copy-start.18 = (s32[256,8]{0,1:T(8,128)S(1)}, s32[256,8]{0,1:T(8,128)}, u32[]{:S(2)}) copy-start(s32[256,8]{0,1:T(8,128)} %get-tuple-element.348) | copy-start | bytes 24580
  234.1 6.6 %copy-start.19 = (f32[256,8]{0,1:T(8,128)S(1)}, f32[256,8]{0,1:T(8,128)}, u32[]{:S(2)}) copy-start(f32[256,8]{0,1:T(8,128)} %get-tuple-element.336) | copy-start | bytes 24580
  234.1 7.3 %copy-start.6 = (bf16[256,4,128]{2,1,0:T(4,128)(2,1)S(1)}, bf16[256,4,128]{2,1,0:T(4,128)(2,1)}, u32[]{:S(2)}) copy-start(bf16[256,4,128]{2,1,0:T(4,128)(2,1)} %copy-done.5) | copy-start | bytes 786436
  234.1 7.2 %copy-start.17 = (pred[256,256]{1,0:T(8,128)(4,1)S(1)}, pred[256,256]{1,0:T(8,128)(4,1)}, u32[]{:S(2)}) copy-start(pred[256,256]{1,0:T(8,128)(4,1)} %copy-done.16) | copy-start | bytes 196612
  234.1 7.2 %copy-start.24 = (f32[1,4,2,128]{3,1,2,0:T(4,128)S(1)}, f32[1,4,2,128]{3,1,2,0:T(4,128)}, u32[]{:S(2)}) copy-start(f32[1,4,2,128]{3,1,2,0:T(4,128)} %copy-done.23) | copy-start | bytes 12292
  234.1 84.9 %all-to-all-start.1 = ((bf16[8,192,2048]{2,1,0:T(8,128)(2,1)}), bf16[8,192,2048]{2,1,0:T(8,128)(2,1)}, u32[]{:S(2)}, u32[]{:S(2)}) async-start(bf16[8,192,2048]{2,1,0:T(8,128)(2,1)} %convolution_convert_fusion), calls=%async_computation.1 | async-start | bytes 12582912 | tf_op jit(solution)/shard_map/all_to_all | solution.py:151
  239.0 53.6 %all-gather.8.cloned.1.call-start = ((), (), s32[]{:S(2)}) async-start(), calls=%async_computation.6 | async-start | bytes 2359296 | tf_op jit(solution)/shard_map/all_gather | solution.py:19
  240.4 164.9 %reduce-scatter.2.cloned.1.call-start = ((), (), s32[]{:S(2)}) async-start(), calls=%async_computation.4 | async-start | bytes 1310720 | tf_op jit(solution)/shard_map/reduce_scatter | solution.py:165
  368.0 7.0 %copy-start.29 = (f32[256,1]{0,1:T(1,128)S(1)}, f32[256,1]{0,1:T(1,128)}, u32[]{:S(2)}) copy-start(f32[256,1]{0,1:T(1,128)} %get-tuple-element.356) | copy-start | bytes 3076
  368.0 7.0 %copy-start.30 = (f32[256,1]{0,1:T(1,128)S(1)}, f32[256,1]{0,1:T(1,128)}, u32[]{:S(2)}) copy-start(f32[256,1]{0,1:T(1,128)} %get-tuple-element.357) | copy-start | bytes 3076
  382.7 3.1 copy-start.7
  382.7 3.1 copy-start.12
  387.4 19.7 %copy-start.1 = (bf16[1,512,2048]{2,1,0:T(8,128)(2,1)S(1)}, bf16[1,512,2048]{2,1,0:T(8,128)(2,1)}, u32[]{:S(2)}) copy-start(bf16[1,512,2048]{2,1,0:T(8,128)(2,1)} %param.30) | copy-start | bytes 6291460
Sparse Core Ops, SparseCore 0:
  22.3 31.2 all-gather.5
  65.9 51.8 all-reduce.1
  242.5 50.1 all-gather.7
  380.4 24.7 reduce-scatter.1
where the time goes:
time: 418 us; the launch traced here: 414 us
  waiting for transfers between devices  155 us (37%)
  blocking collectives  87.8 us (21%)
  local copies, waits for them, and re-layouts  82.5 us (20%)
  matrix products  38 us (9%)
  other arithmetic  28.5 us (7%)
  between operations  14.6 us (3%)
  starting transfers between devices  7.41 us (2%)
    all_to_all x1, blocking collectives, body(): lax.all_to_all(buffer, 'ctx', split_axis=0, concat_axis=0, tiled=True)  75.8 us
    all_gather x2, waiting for transfers between devices, entering(): pieces = jax.tree.map(lambda part: lax.all_gather(part, axis), value)  64.9 us
    gather x8, local copies, waits for them, and re-layouts, body(): flat_back[fetch[:, chosen]].astype(jnp.float32)  55.9 us
    psum x1, waiting for transfers between devices, body(): lax.psum(partial_out.astype(jnp.bfloat16), 'head').astype(jnp.float32)  50.3 us
    all_to_all x1, waiting for transfers between devices, body(): lax.all_to_all(jnp.einsum('ncf,fd->ncd', inner, w_down[0], preferred_elem...  24.6 us
    scatter x1, local copies, waits for them, and re-layouts, body(): jnp.zeros((n_ctx * cap, width), jnp.bfloat16).at[positions]  16.3 us
    reduce_scatter x1, waiting for transfers between devices, body(): lax.psum_scatter(total.astype(jnp.bfloat16), 'head', scatter_dimension=1,...  14.7 us
    all_gather x1, blocking collectives, entering(): pieces = jax.tree.map(lambda part: lax.all_gather(part, axis), value)  12 us
  transfers between devices with their start and end apart: 6, of which 5 were waited for; matrix products, arithmetic and copies ran while one was open for 5% of the time, Pallas kernels for 0%

commit v1 on v0

v1 whole, which is shorter than its diff:
```python
import functools

import jax
import jax.numpy as jnp
from jax import lax
from jax.experimental import pallas as pl
from jax.experimental.pallas import tpu as pltpu
from jax.sharding import PartitionSpec as P

KERNEL = 4
EXP_CTX = 2
LANES = 128
RIM = 16
VMEM_BYTES = 48 * 1024 * 1024
HI = lax.Precision.HIGHEST
BF = jnp.bfloat16
F32 = jnp.float32
NT = (((1,), (1,)), ((), ()))
TN = (((0,), (0,)), ((), ()))
NN = (((1,), (0,)), ((), ()))


def params():
    return pltpu.CompilerParams(vmem_limit_bytes=VMEM_BYTES)


def mm(a, b, dims=NN):
    return lax.dot_general(a, b, dims, preferred_element_type=F32)


def pick_block(extent, target):
    return target if extent % target == 0 else extent


def qkv_kernel(x_ref, gain_ref, w_ref, mixed_ref, rim_ref, normed_ref):
    @pl.when(pl.program_id(0) == 0)
    def _():
        values = x_ref[...].astype(F32)
        scale = lax.rsqrt(jnp.mean(values * values, axis=-1, keepdims=True) + 1e-06)
        normed_ref[...] = (values * scale * gain_ref[...]).astype(BF)

    out = mm(normed_ref[...], w_ref[0]).astype(BF)
    mixed_ref[0] = out
    rim_ref[0] = out[out.shape[0] - RIM :]


def project(x, gain, weights):
    rows, width = x.shape
    kinds, _, chans = weights.shape
    block = pick_block(chans, 256)
    per = chans // block
    return pl.pallas_call(
        qkv_kernel,
        grid=(kinds * per,),
        in_specs=[
            pl.BlockSpec((rows, width), lambda i: (0, 0)),
            pl.BlockSpec((1, width), lambda i: (0, 0)),
            pl.BlockSpec((1, width, block), lambda i: (i // per, 0, i % per)),
        ],
        out_specs=[
            pl.BlockSpec((1, rows, block), lambda i: (i // per, 0, i % per)),
            pl.BlockSpec((1, RIM, block), lambda i: (i // per, 0, i % per)),
        ],
        out_shape=[
            jax.ShapeDtypeStruct((kinds, rows, chans), BF),
            jax.ShapeDtypeStruct((kinds, RIM, chans), BF),
        ],
        scratch_shapes=[pltpu.VMEM((rows, width), BF)],
        compiler_params=params(),
        name="qkv_projection",
    )(x, gain.reshape(1, width), weights)


def decay_sums(steps):
    rows = steps.shape[1]
    row_at = lax.broadcasted_iota(jnp.int32, (rows, rows), 0)
    col_at = lax.broadcasted_iota(jnp.int32, (rows, rows), 1)
    lower = row_at >= col_at
    tri = jnp.where(lower, 1.0, 0.0).astype(F32)
    along = lax.dot_general(steps, tri, NT, precision=HI, preferred_element_type=F32)
    down = lax.dot_general(tri, steps, NT, precision=HI, preferred_element_type=F32)
    return along, down, lower


def payload_tail(total, size):
    full = jnp.broadcast_to(total, (RIM, size))
    first = full.astype(BF).astype(F32)
    second = (full - first).astype(BF).astype(F32)
    third = full - first - second
    at = lax.broadcasted_iota(jnp.int32, (RIM, size), 0)
    return jnp.where(at == 0, first, jnp.where(at == 1, second, jnp.where(at == 2, third, 0.0)))


def conv_kernel(mixed_ref, rim_ref, taps_ref, steps_ref, cot_ref, qkv_ref, fwd_ref, bwd_ref, pad_ref):
    kinds, rows, chans = mixed_ref.shape
    heads = steps_ref.shape[0]
    size = chans // heads
    along, down, _ = decay_sums(steps_ref[...])
    for kind in range(kinds):
        pad_ref[:RIM] = rim_ref[kind].astype(F32)
        pad_ref[RIM:] = mixed_ref[kind].astype(F32)
        total = taps_ref[kind, 0:1, :] * pad_ref[RIM:]
        for offset in range(1, KERNEL):
            total += taps_ref[kind, offset : offset + 1, :] * pad_ref[RIM - offset : RIM - offset + rows]
        activ = total * jax.nn.sigmoid(total)
        if kind == 0:
            activ = activ * size ** (-0.5)
        qkv_ref[kind] = activ.astype(BF)
    for head in range(heads):
        at = slice(head * size, (head + 1) * size)
        last = along[head : head + 1, rows - 1 : rows]
        lead = jnp.exp(down[:, head : head + 1])
        tail = jnp.exp(last - down[:, head : head + 1])
        key_out = (qkv_ref[1, :, at].astype(F32) * tail).astype(BF)
        query_out = (qkv_ref[0, :, at].astype(F32) * lead).astype(BF)
        ends = payload_tail(last, size).astype(BF)
        fwd_ref[head, :size] = mm(key_out, qkv_ref[2, :, at], TN).astype(BF)
        fwd_ref[head, size:] = ends
        bwd_ref[head, :size] = mm(query_out, cot_ref[:, at], TN).astype(BF)
        bwd_ref[head, size:] = ends


def local_states(mixed, rim, taps, steps, cot):
    kinds, rows, chans = mixed.shape
    heads = steps.shape[0]
    size = chans // heads
    state = jax.ShapeDtypeStruct((heads, size + RIM, size), BF)
    return pl.pallas_call(
        conv_kernel,
        out_shape=[jax.ShapeDtypeStruct((kinds, rows, chans), BF), state, state],
        scratch_shapes=[pltpu.VMEM((rows + RIM, chans), F32)],
        compiler_params=params(),
        name="conv_states",
    )(mixed, rim, taps, steps, cot)


def entering(states_ref, head, size, first, last, step):
    def hop(count, total):
        at = first + count * step
        ends = states_ref[at, head, size:, :].astype(F32)
        factor = jnp.exp(ends[0:1] + ends[1:2] + ends[2:3])
        return factor * total + states_ref[at, head, :size, :].astype(F32)

    return lax.fori_loop(0, (last - first) * step, hop, jnp.zeros((size, size), F32))


def core_kernel(me_ref, qkv_ref, steps_ref, states_ref, gain_ref, w_ref, out_ref, headed_ref):
    _, rows, chans = qkv_ref.shape
    heads = steps_ref.shape[0]
    size = chans // heads
    along, down, lower = decay_sums(steps_ref[...])
    for head in range(heads):
        at = slice(head * size, (head + 1) * size)
        state = entering(states_ref, head, size, 0, me_ref[0], 1).astype(BF)
        diff = down[:, head : head + 1] - along[head : head + 1, :]
        mask = jnp.exp(jnp.where(lower, diff, -jnp.inf))
        query = qkv_ref[0, :, at]
        scores = (mm(query, qkv_ref[1, :, at], NT) * mask).astype(BF)
        attended = mm(scores, qkv_ref[2, :, at])
        attended += mm(query, state) * jnp.exp(down[:, head : head + 1])
        scale = lax.rsqrt(jnp.mean(attended * attended, axis=-1, keepdims=True) + 1e-06)
        headed_ref[:, at] = (attended * scale * gain_ref[:, at]).astype(BF)
    out_ref[...] = mm(headed_ref[...], w_ref[...]).astype(BF)


def core_out(me, qkv, steps, states, gain, w_out):
    _, rows, chans = qkv.shape
    vmem = pl.BlockSpec(memory_space=pltpu.VMEM)
    return pl.pallas_call(
        core_kernel,
        in_specs=[pl.BlockSpec(memory_space=pltpu.SMEM)] + [vmem] * 5,
        out_shape=jax.ShapeDtypeStruct((rows, w_out.shape[1]), BF),
        scratch_shapes=[pltpu.VMEM((rows, chans), BF)],
        compiler_params=params(),
        name="core_out",
    )(me, qkv, steps, states, gain.reshape(1, chans), w_out)


def grad_kernel(count, me_ref, qkv_ref, cot_ref, steps_ref, fwd_ref, bwd_ref, gq_ref, gk_ref, gv_ref):
    _, rows, chans = qkv_ref.shape
    heads = steps_ref.shape[0]
    size = chans // heads
    along, down, lower = decay_sums(steps_ref[...])
    for head in range(heads):
        at = slice(head * size, (head + 1) * size)
        state = entering(fwd_ref, head, size, 0, me_ref[0], 1).astype(BF)
        after = entering(bwd_ref, head, size, count - 1, me_ref[0], -1).astype(BF)
        here = down[:, head : head + 1]
        lead = jnp.exp(here)
        tail = jnp.exp(along[head : head + 1, rows - 1 : rows] - here)
        mask = jnp.exp(jnp.where(lower, here - along[head : head + 1, :], -jnp.inf))
        query, key, val = qkv_ref[0, :, at], qkv_ref[1, :, at], qkv_ref[2, :, at]
        cot = cot_ref[:, at]
        scores = (mm(query, key, NT) * mask).astype(BF)
        dov = (mm(cot, val, NT) * mask).astype(BF)
        gq_ref[:, at] = (mm(dov, key) + lead * mm(cot, state, NT)).astype(BF)
        gk_ref[:, at] = (mm(dov, query, TN) + tail * mm(val, after, NT)).astype(BF)
        gv_ref[:, at] = (mm(scores, cot, TN) + tail * mm(key, after)).astype(BF)


def core_grads(count, me, qkv, cot, steps, fwd, bwd):
    _, rows, chans = qkv.shape
    vmem = pl.BlockSpec(memory_space=pltpu.VMEM)
    return pl.pallas_call(
        functools.partial(grad_kernel, count),
        in_specs=[pl.BlockSpec(memory_space=pltpu.SMEM)] + [vmem] * 5,
        out_shape=[jax.ShapeDtypeStruct((rows, chans), BF)] * 3,
        compiler_params=params(),
        name="core_grads",
    )(me, qkv, cot, steps, fwd, bwd)


def norm_kernel(head_ref, x_ref, attn_ref, gain_ref, routes_ref, out_ref):
    rows, width = attn_ref.shape
    start = pl.multiple_of(head_ref[0] * rows, rows)
    resid = x_ref[pl.ds(start, rows), :].astype(F32) + attn_ref[...].astype(F32)
    scale = lax.rsqrt(jnp.mean(resid * resid, axis=-1, keepdims=True) + 1e-06)
    out_ref[:, :width] = (resid * scale * gain_ref[...]).astype(BF)
    out_ref[:, width:] = routes_ref[pl.ds(start, rows), :]


def norm_rows(my_head, x, attn, gain, routes):
    rows, width = attn.shape
    vmem = pl.BlockSpec(memory_space=pltpu.VMEM)
    return pl.pallas_call(
        norm_kernel,
        in_specs=[pl.BlockSpec(memory_space=pltpu.SMEM)] + [vmem] * 4,
        out_shape=jax.ShapeDtypeStruct((rows, width + routes.shape[1]), BF),
        compiler_params=params(),
        name="moe_norm",
    )(my_head, x, attn, gain.reshape(1, width), routes)


def expert_kernel(experts, where_ref, rows_ref, gate_ref, up_ref, down_ref, attn_ref, out_ref):
    _, blocks, rows, cols = out_ref.shape
    width = blocks * cols
    part = attn_ref.shape[0]
    tokens = rows_ref[:, :width]
    routes = rows_ref[:, width:].astype(F32)
    lane = lax.broadcasted_iota(jnp.int32, routes.shape, 1)
    mine = (lane == where_ref[2]) | (lane == where_ref[2] + experts) | (lane == where_ref[2] + 2 * experts)
    weight = jnp.sum(jnp.where(mine, routes, 0.0), axis=1, keepdims=True)
    gate = mm(tokens, gate_ref[0])
    inner = (gate * jax.nn.sigmoid(gate) * mm(tokens, up_ref[0])).astype(BF)
    for block in range(blocks):
        at = slice(block * cols, (block + 1) * cols)
        out_ref[0, block] = (mm(inner, down_ref[0, :, at]) * weight).astype(BF)

    @pl.when(pl.program_id(0) == where_ref[0])
    def _():
        start = pl.multiple_of(where_ref[1] * part, part)
        for block in range(blocks):
            at = slice(block * cols, (block + 1) * cols)
            mine = out_ref[0, block, pl.ds(start, part), :].astype(F32)
            out_ref[0, block, pl.ds(start, part), :] = (mine + attn_ref[:, at].astype(F32)).astype(BF)


def expert_pieces(experts, where, rows, gate, up, down, attn, n_ctx, n_head):
    total, padded = rows.shape
    width = gate.shape[1]
    hidden = gate.shape[2]
    tok, cols = total // n_ctx, width // n_head
    once = pl.Buffered(1)
    return pl.pallas_call(
        functools.partial(expert_kernel, experts),
        grid=(n_ctx,),
        in_specs=[
            pl.BlockSpec(memory_space=pltpu.SMEM),
            pl.BlockSpec((tok, padded), lambda i: (i, 0)),
            pl.BlockSpec((1, width, hidden), lambda i: (0, 0, 0), pipeline_mode=once),
            pl.BlockSpec((1, width, hidden), lambda i: (0, 0, 0), pipeline_mode=once),
            pl.BlockSpec((1, hidden, width), lambda i: (0, 0, 0), pipeline_mode=once),
            pl.BlockSpec(attn.shape, lambda i: (0, 0), pipeline_mode=once),
        ],
        out_specs=pl.BlockSpec((1, n_head, tok, cols), lambda i: (i, 0, 0, 0)),
        out_shape=jax.ShapeDtypeStruct((n_ctx, n_head, tok, cols), BF),
        compiler_params=params(),
        name="expert_pieces",
    )(where, rows, gate, up, down, attn)


def route_table(expert_ids, route_weights, experts):
    hot = expert_ids[:, :, None] == jnp.arange(experts, dtype=jnp.int32)
    table = jnp.sum(jnp.where(hot, route_weights[:, :, None], 0.0), axis=1)
    first = table.astype(BF)
    left = table - first.astype(F32)
    second = left.astype(BF)
    third = (left - second.astype(F32)).astype(BF)
    joined = jnp.concatenate([first, second, third], axis=1)
    return jnp.pad(joined, ((0, 0), (0, -joined.shape[1] % LANES)))


def body(
    hidden_in,
    gain_attn,
    w_qkv,
    conv_w,
    log_decay,
    norm_gain,
    w_out,
    gain_moe,
    expert_ids,
    route_weights,
    w_gate,
    w_up,
    w_down,
    grad_core,
):
    n_ctx, n_head = lax.axis_size("ctx"), lax.axis_size("head")
    my_ctx, my_head = lax.axis_index("ctx"), lax.axis_index("head")
    tok_dev, width = hidden_in.shape
    experts = EXP_CTX * n_ctx
    shards = n_head // EXP_CTX
    cols = width // n_head
    me = my_ctx.astype(jnp.int32).reshape(1)
    head_at = my_head.astype(jnp.int32).reshape(1)
    routes = route_table(expert_ids, route_weights, experts)
    steps = log_decay.T

    mixed, rim = project(hidden_in, gain_attn, jnp.transpose(w_qkv, (1, 0, 2)))
    rim = lax.ppermute(rim, "ctx", [(at, at + 1) for at in range(n_ctx - 1)])
    qkv, fwd, bwd = local_states(mixed, rim, jnp.transpose(conv_w, (1, 0, 2)), steps, grad_core)
    fwd = lax.all_gather(fwd, "ctx")
    bwd = lax.all_gather(bwd, "ctx")
    partial = core_out(me, qkv, steps, fwd, norm_gain, w_out)
    attn = lax.psum_scatter(partial, "head", scatter_dimension=0, tiled=True)
    packed = norm_rows(head_at, hidden_in, attn, gain_moe, routes)
    rows = lax.all_gather(packed, ("ctx", "head"), tiled=True)
    where = jnp.stack([my_ctx, my_head, EXP_CTX * my_ctx + my_head // shards]).astype(jnp.int32)
    pieces = expert_pieces(experts, where, rows, w_gate, w_up, w_down, attn, n_ctx, n_head)
    moe = lax.psum_scatter(
        pieces.reshape(n_ctx * n_head, tok_dev, cols), ("ctx", "head"), scatter_dimension=0, tiled=True
    )
    grads = core_grads(n_ctx, me, qkv, grad_core, steps, fwd, bwd)
    own = lax.dynamic_slice_in_dim(hidden_in, my_head * cols, cols, 1)
    layer_out = (own.astype(F32) + moe[0].astype(F32)).astype(BF)
    return (layer_out, *grads)


def solution(mesh):
    in_specs = (
        P("ctx", None),
        P(),
        P(None, None, "head"),
        P(None, None, "head"),
        P("ctx", "head"),
        P("head"),
        P("head", None),
        P(),
        P("ctx", None),
        P("ctx", None),
        P(("ctx", "head"), None, None),
        P(("ctx", "head"), None, None),
        P(("ctx", "head"), None, None),
        P("ctx", "head"),
    )
    out_specs = (P("ctx", "head"), P("ctx", "head"), P("ctx", "head"), P("ctx", "head"))
    return jax.shard_map(body, mesh=mesh, in_specs=in_specs, out_specs=out_specs, check_vma=False)
```

time: 418 us -> 389 us (0.931)
  waiting for transfers between devices: 155 us -> 323 us
  blocking collectives: 87.8 us -> 0 us
  local copies, waits for them, and re-layouts: 82.5 us -> 10.4 us
  matrix products: 38 us -> 0 us
  Pallas kernels: 0 us -> 36.3 us
  other arithmetic: 28.5 us -> 1.84 us
  starting transfers between devices: 7.41 us -> 2.56 us
    reduce_scatter x1 -> x2, waiting for transfers between devices: 14.7 us -> 210 us  [the longest x1 183 us: body(): lax.psum_scatter(pieces.reshape(n_ctx * n_head, tok_dev, cols), ('ctx', '...]
    all_to_all x1 -> x0, blocking collectives: 75.8 us -> none  [body(): lax.all_to_all(buffer, 'ctx', split_axis=0, concat_axis=0, tiled=True)]
    gather x8 -> x0, local copies, waits for them, and re-layouts: 55.9 us -> none  [body(): flat_back[fetch[:, chosen]].astype(jnp.float32)]
    psum x1 -> x0, waiting for transfers between devices: 50.3 us -> none  [body(): lax.psum(partial_out.astype(jnp.bfloat16), 'head').astype(jnp.float32)]
    all_gather x2 -> x3, waiting for transfers between devices: 64.9 us -> 112 us  [the longest x1 78.9 us: body(): rows = lax.all_gather(packed, ('ctx', 'head'), tiled=True)]
    dot_general x16 -> x0, matrix products: 38 us -> none  [the longest x1 11.9 us: body(): jnp.einsum('ncf,fd->ncd', inner, w_down[0], preferred_element_type=jnp.fl...]
    pallas_call x0 -> x6, Pallas kernels: none -> 36.3 us  [the longest x1 18.3 us: expert_pieces(): pl.pallas_call(functools.partial(expert_kernel, experts), grid=(n_ctx,),...]
    all_to_all x1 -> x0, waiting for transfers between devices: 24.6 us -> none  [body(): lax.all_to_all(jnp.einsum('ncf,fd->ncd', inner, w_down[0], preferred_elem...]
  transfers between devices with their start and end apart: 6 -> 6, of which waited for: 5 -> 6; matrix products, arithmetic and copies ran while one was open for 5% -> 0% of each run, Pallas kernels for 0% -> 6%
where the time goes in v1:
time: 389 us; the launch traced here: 388 us
  waiting for transfers between devices  323 us (83%)
  Pallas kernels  36.3 us (9%)
  between operations  13.9 us (4%)
  local copies, waits for them, and re-layouts  10.4 us (3%)
    reduce_scatter x1, waiting for transfers between devices, body(): lax.psum_scatter(pieces.reshape(n_ctx * n_head, tok_dev, cols), ('ctx', '...  183 us
    all_gather x1, waiting for transfers between devices, body(): rows = lax.all_gather(packed, ('ctx', 'head'), tiled=True)  78.9 us
    all_gather x1, waiting for transfers between devices, body(): fwd = lax.all_gather(fwd, 'ctx')  29 us
    reduce_scatter x1, waiting for transfers between devices, body(): attn = lax.psum_scatter(partial, 'head', scatter_dimension=0, tiled=True)  27.6 us
    pallas_call x1, Pallas kernels, expert_pieces(): pl.pallas_call(functools.partial(expert_kernel, experts), grid=(n_ctx,),...  18.3 us
    unnamed x36, local copies, waits for them, and re-layouts  10.2 us
  transfers between devices with their start and end apart: 6, of which 6 were waited for; matrix products, arithmetic and copies ran while one was open for 0% of the time, Pallas kernels for 6%

profile of v1, /device:TPU:0, one launch (start us, length us, event | category | flops | bytes accessed | tf_op | source)
XLA Modules:
  0.0 388.3 jit_solution(8643308233071626657)
XLA Ops:
  7.2 0.0 all-gather.8.cloned.1.call-start
  7.2 0.0 copy-start
  7.2 1.2 copy-done
  8.4 0.0 copy-start.14
  8.4 0.7 copy-done.14
  9.1 0.0 copy-start.10
  9.1 0.0 copy-start.11
  9.1 0.0 copy-start.12
  9.1 0.0 copy-start.15
  9.1 6.3 %qkv_projection.1 = (bf16[3,256,512]{2,1,0:T(8,128)(2,1)S(1)}, bf16[3,16,512]{2,1,0:T(8,128)(2,1)S(1)}) custom-call(bf16[256,2048]{1,0:T(8,128)(2,1)S(1)} %copy-done, f32[1,2048]{1,0:T(1,128)S(1)} %bitcast.23, bf16[3,2048,512]{2,1,0:T(8,128)(2,1)} %bitcast.26), custom_call_target="tpu_custom_call" | custom-call | tf_op jit(solution)/shard_map/qkv_projection/pallas_call | solution.py:52
  15.4 2.4 collective-permute-start
  17.8 0.9 collective-permute-done.rim_ref
  18.7 0.0 copy-done.10
  18.7 0.0 copy-done.11
  18.7 0.0 copy-done.12
  18.7 2.9 conv_states.1
  21.5 0.0 all-gather.8.cloned.1.call-update
  21.5 0.0 reduce-scatter.3.cloned.1.call-start
  21.6 29.0 %all-gather.8.cloned.1.call-done = bf16[32,144,128]{2,1,0:T(8,128)(2,1)} async-done(((bf16[4,144,128]{2,1,0:T(8,128)(2,1)}), bf16[32,144,128]{2,1,0:T(8,128)(2,1)}) %all-gather.8.cloned.1.call-update) | async-done | bytes 1179664 | tf_op jit(solution)/shard_map/all_gather | solution.py:323
  50.6 0.0 copy-done.15
  50.6 0.0 copy-start.2
  50.6 1.3 copy-done.2
  51.9 0.0 copy-start.6
  51.9 1.6 copy-done.6
  53.5 0.0 copy-start.16
  53.5 0.0 copy-start.17
  53.5 0.0 copy-start.1
  53.5 0.0 copy-start.13
  53.5 4.0 %core_out.1 = bf16[256,2048]{1,0:T(8,128)(2,1)} custom-call(s32[1]{0:T(128)} %bitcast.me_ref, bf16[3,256,512]{2,1,0:T(8,128)(2,1)S(1)} %get-tuple-element.14.qkv_ref, f32[4,256]{1,0:T(4,128)S(1)} %bitcast.19, bf16[8,4,144,128]{3,2,1,0:T(8,128)(2,1)S(1)} %bitcast.15, f32[1,512]{1,0:T(1,128)S(1)} %bitcast.24, bf16[512,2048]{1,0:T(8,128)(2,1)S(1)} %copy-done.6), custom_call_target="tpu_custom_call" | custom-call | tf_op jit(solution)/shard_map/core_out/pallas_call | solution.py:169
  57.5 0.0 reduce-scatter.3.cloned.1.call-update
  57.5 0.0 all-gather.6.cloned.1.call-start
  57.6 0.0 copy-done.16
  57.6 0.0 copy-done.17
  57.6 0.1 copy.23
  57.8 27.6 %reduce-scatter.3.cloned.1.call-done.attn_ref = bf16[64,2048]{1,0:T(8,128)(2,1)} async-done(((bf16[256,2048]{1,0:T(8,128)(2,1)}), bf16[64,2048]{1,0:T(8,128)(2,1)}) %reduce-scatter.3.cloned.1.call-update) | async-done | bytes 262160 | tf_op jit(solution)/shard_map/reduce_scatter | solution.py:326
  85.3 0.0 copy-done.1
  85.3 0.0 copy-done.13
  85.3 0.0 copy-start.8
  85.3 0.9 copy-done.8
  86.3 0.0 copy-start.9
  86.3 0.9 moe_norm.1
  87.2 0.0 all-gather.6.cloned.1.call-update
  87.2 0.0 all-gather.10.cloned.1.call-start
  87.3 0.5 all-gather.10.cloned.1.call-update
  87.8 0.0 reduce-scatter.5.cloned.1.call-start
  87.9 0.1 pad_add_fusion.where_ref
  87.9 78.9 %all-gather.6.cloned.1.call-done.rows_ref = bf16[2048,2176]{1,0:T(8,128)(2,1)} async-done(((bf16[64,2176]{1,0:T(8,128)(2,1)}), bf16[2048,2176]{1,0:T(8,128)(2,1)}) %all-gather.6.cloned.1.call-update) | async-done | bytes 8912912 | tf_op jit(solution)/shard_map/all_gather | solution.py:328
  166.8 0.0 copy-done.9
  166.8 0.0 copy-start.4
  166.8 1.6 copy-done.4
  168.4 0.0 copy-start.5
  168.4 1.6 copy-done.5
  170.0 18.3 %expert_pieces.1 = bf16[8,4,256,512]{3,2,1,0:T(8,128)(2,1)} custom-call(s32[3]{0:T(128)S(1)} %pad_add_fusion.where_ref, bf16[2048,2176]{1,0:T(8,128)(2,1)} %all-gather.6.cloned.1.call-done.rows_ref, bf16[1,2048,512]{2,1,0:T(8,128)(2,1)S(1)} %copy-done.4, bf16[1,2048,512]{2,1,0:T(8,128)(2,1)S(1)} %copy-done.5, bf16[1,512,2048]{2,1,0:T(8,128)(2,1)} %down_ref.1, ...), custom_call_target="tpu_custom_call" | custom-call | tf_op jit(solution)/shard_map/expert_pieces/pallas_call | solution.py:264
  188.3 0.0 copy-start.3
  188.3 0.0 reduce-scatter.5.cloned.1.call-update
  188.3 3.7 all-gather.10.cloned.1.call-done
  192.0 0.0 copy-done.3
  192.0 0.0 copy-start.7
  192.0 1.3 copy-done.7
  193.3 4.0 %core_grads.1 = (bf16[256,512]{1,0:T(8,128)(2,1)}, bf16[256,512]{1,0:T(8,128)(2,1)}, bf16[256,512]{1,0:T(8,128)(2,1)}) custom-call(s32[1]{0:T(128)} %bitcast.me_ref, bf16[3,256,512]{2,1,0:T(8,128)(2,1)S(1)} %get-tuple-element.14.qkv_ref, bf16[256,512]{1,0:T(8,128)(2,1)S(1)} %copy-done.10, f32[4,256]{1,0:T(4,128)S(1)} %bitcast.20, ...), custom_call_target="tpu_custom_call" | custom-call | tf_op jit(solution)/shard_map/core_grads/pallas_call | solution.py:204
  197.3 182.8 %reduce-scatter.5.cloned.1.call-done = bf16[1,256,512]{2,1,0:T(8,128)(2,1)} async-done(((bf16[32,256,512]{2,1,0:T(8,128)(2,1)}), bf16[1,256,512]{2,1,0:T(8,128)(2,1)}) %reduce-scatter.5.cloned.1.call-update) | async-done | bytes 262160 | tf_op jit(solution)/shard_map/reduce_scatter | solution.py:331
  380.1 1.7 fusion
  (4 shorter events, 0.1 us)
Async XLA Ops:
  7.2 43.5 %all-gather.8.cloned.1.call-start = ((), (), s32[]{:S(2)}) async-start(), calls=%async_computation.5 | async-start | bytes 1327104 | tf_op jit(solution)/shard_map/all_gather | solution.py:323
  7.2 1.2 copy-start
  8.4 0.7 copy-start.14
  9.1 9.5 %copy-start.10 = (bf16[256,512]{1,0:T(8,128)(2,1)S(1)}, bf16[256,512]{1,0:T(8,128)(2,1)}, u32[]{:S(2)}) copy-start(bf16[256,512]{1,0:T(8,128)(2,1)} %cot_ref.3) | copy-start | bytes 786436
  9.1 9.5 %copy-start.11 = (f32[256,4]{0,1:T(4,128)S(1)}, f32[256,4]{0,1:T(4,128)}, u32[]{:S(2)}) copy-start(f32[256,4]{0,1:T(4,128)} %param.18) | copy-start | bytes 12292
  9.1 9.5 %copy-start.12 = (f32[4,3,512]{2,0,1:T(4,128)S(1)}, f32[4,3,512]{2,0,1:T(4,128)}, u32[]{:S(2)}) copy-start(f32[4,3,512]{2,0,1:T(4,128)} %param.17) | copy-start | bytes 73732
  9.1 41.5 %copy-start.15 = (f32[512]{0:T(512)S(1)}, f32[512]{0:T(512)}, u32[]{:S(2)}) copy-start(f32[512]{0:T(512)} %param.19) | copy-start | bytes 6148
  15.4 3.2 collective-permute-start
  21.5 63.8 %reduce-scatter.3.cloned.1.call-start = ((), (), s32[]{:S(2)}) async-start(), calls=%async_computation.2 | async-start | bytes 1310720 | tf_op jit(solution)/shard_map/reduce_scatter | solution.py:326
  50.6 1.3 copy-start.2
  51.9 1.6 copy-start.6
  53.5 4.1 %copy-start.16 = (f32[256,8]{0,1:T(8,128)S(1)}, f32[256,8]{0,1:T(8,128)}, u32[]{:S(2)}) copy-start(f32[256,8]{0,1:T(8,128)} %param.23) | copy-start | bytes 24580
  53.5 4.1 %copy-start.17 = (s32[256,8]{0,1:T(8,128)S(1)}, s32[256,8]{0,1:T(8,128)}, u32[]{:S(2)}) copy-start(s32[256,8]{0,1:T(8,128)} %param.22) | copy-start | bytes 24580
  53.5 31.8 %copy-start.1 = (bf16[256,2048]{1,0:T(8,128)(2,1)S(1)}, bf16[256,2048]{1,0:T(8,128)(2,1)}, u32[]{:S(2)}) copy-start(bf16[256,2048]{1,0:T(8,128)(2,1)} %x_ref.3) | copy-start | bytes 3145732
  53.5 31.8 %copy-start.13 = (f32[2048]{0:T(1024)S(1)}, f32[2048]{0:T(1024)}, u32[]{:S(2)}) copy-start(f32[2048]{0:T(1024)} %param.21) | copy-start | bytes 24580
  57.5 109.3 %all-gather.6.cloned.1.call-start = ((), (), s32[]{:S(2)}) async-start(), calls=%async_computation.3 | async-start | bytes 9191424 | tf_op jit(solution)/shard_map/all_gather | solution.py:328
  85.3 1.0 copy-start.8
  86.3 80.5 %copy-start.9 = (bf16[64,2048]{1,0:T(8,128)(2,1)S(1)}, bf16[64,2048]{1,0:T(8,128)(2,1)}, u32[]{:S(2)}) copy-start(bf16[64,2048]{1,0:T(8,128)(2,1)} %reduce-scatter.3.cloned.1.call-done.attn_ref) | copy-start | bytes 786436
  87.2 104.8 %all-gather.10.cloned.1.call-start = ((), (), s32[]{:S(2)}) async-start(), calls=%async_computation.6 | async-start | bytes 1327104 | tf_op jit(solution)/shard_map/all_gather | solution.py:324
  87.8 292.3 %reduce-scatter.5.cloned.1.call-start = ((), (), s32[]{:S(2)}) async-start(), calls=%async_computation.4 | async-start | bytes 8650752 | tf_op jit(solution)/shard_map/reduce_scatter | solution.py:331
  166.8 1.6 copy-start.4
  168.4 1.6 copy-start.5
  188.3 3.7 copy-start.3
  192.0 1.3 copy-start.7
Sparse Core Ops, SparseCore 0:
  21.7 28.9 all-gather.7
  57.6 27.6 reduce-scatter.2
  88.6 78.1 all-gather.5
  169.3 22.6 all-gather.9
  194.2 185.8 reduce-scatter.4

commit v2 on v1

--- a/solution.py
+++ b/solution.py
@@ -11,7 +11,7 @@
 EXP_CTX = 2
 LANES = 128
 RIM = 16
-VMEM_BYTES = 48 * 1024 * 1024
+MIB = 1024 * 1024
 HI = lax.Precision.HIGHEST
 BF = jnp.bfloat16
 F32 = jnp.float32
@@ -20,8 +20,8 @@
 NN = (((1,), (0,)), ((), ()))
 
 
-def params():
-    return pltpu.CompilerParams(vmem_limit_bytes=VMEM_BYTES)
+def params(mib):
+    return pltpu.CompilerParams(vmem_limit_bytes=mib * MIB)
 
 
 def mm(a, b, dims=NN):
@@ -66,7 +66,7 @@
             jax.ShapeDtypeStruct((kinds, RIM, chans), BF),
         ],
         scratch_shapes=[pltpu.VMEM((rows, width), BF)],
-        compiler_params=params(),
+        compiler_params=params(12),
         name="qkv_projection",
     )(x, gain.reshape(1, width), weights)
 
@@ -129,29 +129,36 @@
         conv_kernel,
         out_shape=[jax.ShapeDtypeStruct((kinds, rows, chans), BF), state, state],
         scratch_shapes=[pltpu.VMEM((rows + RIM, chans), F32)],
-        compiler_params=params(),
+        compiler_params=params(12),
         name="conv_states",
     )(mixed, rim, taps, steps, cot)
 
 
-def entering(states_ref, head, size, first, last, step):
+def arrange(me_ref, state_refs, held_ref):
+    for at, ref in enumerate(state_refs):
+        held_ref[me_ref[0] ^ at] = ref[...]
+
+
+def entering(held_ref, head, size, first, last, step):
     def hop(count, total):
         at = first + count * step
-        ends = states_ref[at, head, size:, :].astype(F32)
+        ends = held_ref[at, head, size:, :].astype(F32)
         factor = jnp.exp(ends[0:1] + ends[1:2] + ends[2:3])
-        return factor * total + states_ref[at, head, :size, :].astype(F32)
+        return factor * total + held_ref[at, head, :size, :].astype(F32)
 
     return lax.fori_loop(0, (last - first) * step, hop, jnp.zeros((size, size), F32))
 
 
-def core_kernel(me_ref, qkv_ref, steps_ref, states_ref, gain_ref, w_ref, out_ref, headed_ref):
+def core_kernel(count, me_ref, qkv_ref, steps_ref, gain_ref, w_ref, *refs):
+    state_refs, (out_ref, headed_ref, held_ref) = refs[:count], refs[count:]
     _, rows, chans = qkv_ref.shape
     heads = steps_ref.shape[0]
     size = chans // heads
+    arrange(me_ref, state_refs, held_ref)
     along, down, lower = decay_sums(steps_ref[...])
     for head in range(heads):
         at = slice(head * size, (head + 1) * size)
-        state = entering(states_ref, head, size, 0, me_ref[0], 1).astype(BF)
+        state = entering(held_ref, head, size, 0, me_ref[0], 1).astype(BF)
         diff = down[:, head : head + 1] - along[head : head + 1, :]
         mask = jnp.exp(jnp.where(lower, diff, -jnp.inf))
         query = qkv_ref[0, :, at]
@@ -165,21 +172,26 @@
 
 def core_out(me, qkv, steps, states, gain, w_out):
     _, rows, chans = qkv.shape
+    count = len(states)
     vmem = pl.BlockSpec(memory_space=pltpu.VMEM)
     return pl.pallas_call(
-        core_kernel,
-        in_specs=[pl.BlockSpec(memory_space=pltpu.SMEM)] + [vmem] * 5,
+        functools.partial(core_kernel, count),
+        in_specs=[pl.BlockSpec(memory_space=pltpu.SMEM)] + [vmem] * (4 + count),
         out_shape=jax.ShapeDtypeStruct((rows, w_out.shape[1]), BF),
-        scratch_shapes=[pltpu.VMEM((rows, chans), BF)],
-        compiler_params=params(),
+        scratch_shapes=[pltpu.VMEM((rows, chans), BF), pltpu.VMEM((count, *states[0].shape), BF)],
+        compiler_params=params(16),
         name="core_out",
-    )(me, qkv, steps, states, gain.reshape(1, chans), w_out)
-
-
-def grad_kernel(count, me_ref, qkv_ref, cot_ref, steps_ref, fwd_ref, bwd_ref, gq_ref, gk_ref, gv_ref):
+    )(me, qkv, steps, gain.reshape(1, chans), w_out, *states)
+
+
+def grad_kernel(count, me_ref, qkv_ref, cot_ref, steps_ref, *refs):
+    fwd_refs, bwd_refs = refs[:count], refs[count : 2 * count]
+    gq_ref, gk_ref, gv_ref, fwd_ref, bwd_ref = refs[2 * count :]
     _, rows, chans = qkv_ref.shape
     heads = steps_ref.shape[0]
     size = chans // heads
+    arrange(me_ref, fwd_refs, fwd_ref)
+    arrange(me_ref, bwd_refs, bwd_ref)
     along, down, lower = decay_sums(steps_ref[...])
     for head in range(heads):
         at = slice(head * size, (head + 1) * size)
@@ -198,85 +210,121 @@
         gv_ref[:, at] = (mm(scores, cot, TN) + tail * mm(key, after)).astype(BF)
 
 
-def core_grads(count, me, qkv, cot, steps, fwd, bwd):
+def core_grads(me, qkv, cot, steps, fwd, bwd):
     _, rows, chans = qkv.shape
+    count = len(fwd)
+    held = pltpu.VMEM((count, *fwd[0].shape), BF)
     vmem = pl.BlockSpec(memory_space=pltpu.VMEM)
     return pl.pallas_call(
         functools.partial(grad_kernel, count),
-        in_specs=[pl.BlockSpec(memory_space=pltpu.SMEM)] + [vmem] * 5,
+        in_specs=[pl.BlockSpec(memory_space=pltpu.SMEM)] + [vmem] * (3 + 2 * count),
         out_shape=[jax.ShapeDtypeStruct((rows, chans), BF)] * 3,
-        compiler_params=params(),
+        scratch_shapes=[held, held],
+        compiler_params=params(20),
         name="core_grads",
-    )(me, qkv, cot, steps, fwd, bwd)
-
-
-def norm_kernel(head_ref, x_ref, attn_ref, gain_ref, routes_ref, out_ref):
-    rows, width = attn_ref.shape
+    )(me, qkv, cot, steps, *fwd, *bwd)
+
+
+def norm_kernel(head_ref, x_ref, attn_ref, gain_ref, out_ref):
+    rows = attn_ref.shape[0]
     start = pl.multiple_of(head_ref[0] * rows, rows)
     resid = x_ref[pl.ds(start, rows), :].astype(F32) + attn_ref[...].astype(F32)
     scale = lax.rsqrt(jnp.mean(resid * resid, axis=-1, keepdims=True) + 1e-06)
-    out_ref[:, :width] = (resid * scale * gain_ref[...]).astype(BF)
-    out_ref[:, width:] = routes_ref[pl.ds(start, rows), :]
-
-
-def norm_rows(my_head, x, attn, gain, routes):
+    out_ref[...] = (resid * scale * gain_ref[...]).astype(BF)
+
+
+def norm_rows(my_head, x, attn, gain):
     rows, width = attn.shape
     vmem = pl.BlockSpec(memory_space=pltpu.VMEM)
     return pl.pallas_call(
         norm_kernel,
-        in_specs=[pl.BlockSpec(memory_space=pltpu.SMEM)] + [vmem] * 4,
-        out_shape=jax.ShapeDtypeStruct((rows, width + routes.shape[1]), BF),
-        compiler_params=params(),
+        in_specs=[pl.BlockSpec(memory_space=pltpu.SMEM)] + [vmem] * 3,
+        out_shape=jax.ShapeDtypeStruct((rows, width), BF),
+        compiler_params=params(8),
         name="moe_norm",
-    )(my_head, x, attn, gain.reshape(1, width), routes)
-
-
-def expert_kernel(experts, where_ref, rows_ref, gate_ref, up_ref, down_ref, attn_ref, out_ref):
-    _, blocks, rows, cols = out_ref.shape
-    width = blocks * cols
-    part = attn_ref.shape[0]
-    tokens = rows_ref[:, :width]
-    routes = rows_ref[:, width:].astype(F32)
+    )(my_head, x, attn, gain.reshape(1, width))
+
+
+def expert_kernel(layout, masks, experts, where_ref, gate_ref, up_ref, down_ref, routes_ref, *refs):
+    parts = 1 + max(operand for block in layout for operand, _ in block)
+    row_refs, (out_ref, rows_ref, sems) = refs[:parts], refs[parts:]
+    step = pl.program_id(0)
+    slot = lax.rem(step, 2)
+
+    def copies(at, block):
+        for operand, start in layout[block]:
+            size = row_refs[operand].shape[0]
+            yield pltpu.make_async_copy(
+                row_refs[operand], rows_ref.at[at, pl.ds(start, size)], sems.at[at]
+            )
+
+    @pl.when(step == 0)
+    def _():
+        for copy in copies(0, 0):
+            copy.start()
+
+    for block in range(1, len(layout)):
+
+        @pl.when(step == block - 1)
+        def _(block=block):
+            for copy in copies(block % 2, block):
+                copy.start()
+
+    pltpu.make_async_copy(rows_ref.at[slot], rows_ref.at[slot], sems.at[slot]).wait()
+
+    relative = jnp.int32(masks[0])
+    for block in range(1, len(layout)):
+        relative = jnp.where(step == block, masks[block], relative)
+    routes = routes_ref[where_ref[0] ^ relative].astype(F32)
     lane = lax.broadcasted_iota(jnp.int32, routes.shape, 1)
-    mine = (lane == where_ref[2]) | (lane == where_ref[2] + experts) | (lane == where_ref[2] + 2 * experts)
+    mine = (lane == where_ref[1]) | (lane == where_ref[1] + experts) | (lane == where_ref[1] + 2 * experts)
     weight = jnp.sum(jnp.where(mine, routes, 0.0), axis=1, keepdims=True)
+    tokens = rows_ref[slot]
     gate = mm(tokens, gate_ref[0])
     inner = (gate * jax.nn.sigmoid(gate) * mm(tokens, up_ref[0])).astype(BF)
-    for block in range(blocks):
-        at = slice(block * cols, (block + 1) * cols)
-        out_ref[0, block] = (mm(inner, down_ref[0, :, at]) * weight).astype(BF)
-
-    @pl.when(pl.program_id(0) == where_ref[0])
-    def _():
-        start = pl.multiple_of(where_ref[1] * part, part)
-        for block in range(blocks):
-            at = slice(block * cols, (block + 1) * cols)
-            mine = out_ref[0, block, pl.ds(start, part), :].astype(F32)
-            out_ref[0, block, pl.ds(start, part), :] = (mine + attn_ref[:, at].astype(F32)).astype(BF)
-
-
-def expert_pieces(experts, where, rows, gate, up, down, attn, n_ctx, n_head):
-    total, padded = rows.shape
-    width = gate.shape[1]
-    hidden = gate.shape[2]
-    tok, cols = total // n_ctx, width // n_head
+    width = out_ref.shape[2]
+    cols = pick_block(width, 512)
+    for start in range(0, width, cols):
+        at = slice(start, start + cols)
+        out_ref[0, :, at] = (mm(inner, down_ref[0, :, at]) * weight).astype(BF)
+
+
+def expert_pieces(where, blocks, masks, gate, up, down, routes):
+    tok, lanes = routes.shape[1:]
+    width, hidden = gate.shape[1:]
+    operands, layout = [], []
+    for block in blocks:
+        start, entry = 0, []
+        for part in block:
+            entry.append((len(operands), start))
+            operands.append(part)
+            start += part.shape[0]
+        layout.append(tuple(entry))
     once = pl.Buffered(1)
-    return pl.pallas_call(
-        functools.partial(expert_kernel, experts),
-        grid=(n_ctx,),
+    count = len(blocks)
+    experts = EXP_CTX * routes.shape[0]
+    return pl.pallas_call(
+        functools.partial(expert_kernel, tuple(layout), tuple(masks), experts),
+        grid=(count,),
         in_specs=[
             pl.BlockSpec(memory_space=pltpu.SMEM),
-            pl.BlockSpec((tok, padded), lambda i: (i, 0)),
             pl.BlockSpec((1, width, hidden), lambda i: (0, 0, 0), pipeline_mode=once),
             pl.BlockSpec((1, width, hidden), lambda i: (0, 0, 0), pipeline_mode=once),
             pl.BlockSpec((1, hidden, width), lambda i: (0, 0, 0), pipeline_mode=once),
-            pl.BlockSpec(attn.shape, lambda i: (0, 0), pipeline_mode=once),
-        ],
-        out_specs=pl.BlockSpec((1, n_head, tok, cols), lambda i: (i, 0, 0, 0)),
-        out_shape=jax.ShapeDtypeStruct((n_ctx, n_head, tok, cols), BF),
-        compiler_params=params(),
+            pl.BlockSpec(routes.shape, lambda i: (0, 0, 0), pipeline_mode=once),
+        ]
+        + [pl.BlockSpec(memory_space=pl.ANY)] * len(operands),
+        out_specs=pl.BlockSpec((1, tok, width), lambda i: (i, 0, 0)),
+        out_shape=jax.ShapeDtypeStruct((count, tok, width), BF),
+        scratch_shapes=[pltpu.VMEM((2, tok, width), BF), pltpu.SemaphoreType.DMA((2,))],
+        compiler_params=params(24),
+        cost_estimate=pl.CostEstimate(
+            flops=6 * count * tok * width * hidden,
+            bytes_accessed=2 * (2 * count * tok * width + 3 * width * hidden),
+            transcendentals=count * tok * hidden,
+        ),
         name="expert_pieces",
-    )(where, rows, gate, up, down, attn)
+    )(where, gate, up, down, routes, *operands)
 
 
 def route_table(expert_ids, route_weights, experts):
@@ -288,6 +336,97 @@
     third = (left - second.astype(F32)).astype(BF)
     joined = jnp.concatenate([first, second, third], axis=1)
     return jnp.pad(joined, ((0, 0), (0, -joined.shape[1] % LANES)))
+
+
+CORE, ROW, COL = 1, 2, 4
+PLANE = 8
+
+
+def swap(value, mask, keep=None):
+    count = lax.axis_size("ctx")
+    pairs = [(at, at ^ mask) for at in range(count)]
+    return lax.ppermute(value, "ctx", [pair for pair in pairs if keep is None or keep(*pair)])
+
+
+def spread_states(own, keep):
+    count = lax.axis_size("ctx")
+    near = jnp.stack([own] + [swap(own, mask, keep) for mask in range(2, count, 2)])
+    far = swap(near, CORE)
+    return [(far if mask % 2 else near)[mask // 2] for mask in range(count)]
+
+
+def spread_rows(own):
+    count = lax.axis_size("ctx")
+    rows = own.shape[0]
+    near = {0: [own]}
+    if count == PLANE:
+        half = rows // 2
+        near[ROW] = [swap(own, ROW)]
+        near[COL] = [swap(own, COL)]
+        near[ROW | COL] = [swap(near[ROW][0][:half], COL), swap(near[COL][0][half:], ROW)]
+    else:
+        for mask in range(2, count, 2):
+            near[mask] = [swap(own, mask)]
+    far = {mask | CORE: [swap(part, CORE) for part in parts] for mask, parts in near.items()}
+    return near | far
+
+
+def plus(*terms):
+    return functools.reduce(jnp.add, [term.astype(F32) for term in terms]).astype(BF)
+
+
+def collect_terms(near, far, evens):
+    arrived = swap(far, CORE)
+    sums = {mask: (near[at], arrived[at]) for at, mask in enumerate(evens)}
+    if lax.axis_size("ctx") == PLANE:
+        half = near.shape[1] // 2
+        across, along, down = sums[ROW | COL], sums[ROW], sums[COL]
+        lower = swap(plus(across[0][:half], across[1][:half]), ROW)
+        upper = swap(plus(across[0][half:], across[1][half:]), COL)
+        none = jnp.zeros_like(lower)
+        others = [
+            swap(plus(*along, jnp.concatenate([none, upper])), ROW),
+            swap(plus(*down, jnp.concatenate([lower, none])), COL),
+        ]
+    else:
+        others = [swap(plus(*sums[mask]), mask) for mask in evens[1:]]
+    return arrived, others
+
+
+def sum_kernel(head_ref, attn_ref, near_ref, arrived_ref, *refs):
+    others, out_ref = refs[:-1], refs[-1]
+    part = attn_ref.shape[0]
+    total = near_ref[0].astype(F32) + arrived_ref[0].astype(F32)
+    for ref in others:
+        total += ref[...].astype(F32)
+    out_ref[0] = total.astype(BF)
+    start = pl.multiple_of(head_ref[0] * part, part)
+    mine = near_ref[0, pl.ds(start, part), :].astype(F32) + arrived_ref[0, pl.ds(start, part), :].astype(F32)
+    for ref in others:
+        mine += ref[pl.ds(start, part), :].astype(F32)
+    out_ref[0, pl.ds(start, part), :] = (mine + attn_ref[...].astype(F32)).astype(BF)
+
+
+def sum_terms(my_head, attn, near, arrived, others, n_head):
+    _, tok, width = near.shape
+    part = attn.shape[0]
+    cols = width // n_head
+    first = pl.BlockSpec((1, tok, cols), lambda i: (0, 0, i))
+    return pl.pallas_call(
+        sum_kernel,
+        grid=(n_head,),
+        in_specs=[
+            pl.BlockSpec(memory_space=pltpu.SMEM),
+            pl.BlockSpec((part, cols), lambda i: (0, i)),
+            first,
+            first,
+        ]
+        + [pl.BlockSpec((tok, cols), lambda i: (0, i))] * len(others),
+        out_specs=pl.BlockSpec((1, tok, cols), lambda i: (i, 0, 0)),
+        out_shape=jax.ShapeDtypeStruct((n_head, tok, cols), BF),
+        compiler_params=params(16),
+        name="sum_terms",
+    )(my_head, attn, near, arrived, *others)
 
 
 def body(
@@ -317,21 +456,27 @@
     routes = route_table(expert_ids, route_weights, experts)
     steps = log_decay.T
 
+    routes = lax.all_gather(routes, "ctx")
     mixed, rim = project(hidden_in, gain_attn, jnp.transpose(w_qkv, (1, 0, 2)))
     rim = lax.ppermute(rim, "ctx", [(at, at + 1) for at in range(n_ctx - 1)])
     qkv, fwd, bwd = local_states(mixed, rim, jnp.transpose(conv_w, (1, 0, 2)), steps, grad_core)
-    fwd = lax.all_gather(fwd, "ctx")
-    bwd = lax.all_gather(bwd, "ctx")
+    fwd = spread_states(fwd, lambda source, target: source < target)
+    bwd = spread_states(bwd, lambda source, target: source > target)
     partial = core_out(me, qkv, steps, fwd, norm_gain, w_out)
     attn = lax.psum_scatter(partial, "head", scatter_dimension=0, tiled=True)
-    packed = norm_rows(head_at, hidden_in, attn, gain_moe, routes)
-    rows = lax.all_gather(packed, ("ctx", "head"), tiled=True)
-    where = jnp.stack([my_ctx, my_head, EXP_CTX * my_ctx + my_head // shards]).astype(jnp.int32)
-    pieces = expert_pieces(experts, where, rows, w_gate, w_up, w_down, attn, n_ctx, n_head)
-    moe = lax.psum_scatter(
-        pieces.reshape(n_ctx * n_head, tok_dev, cols), ("ctx", "head"), scatter_dimension=0, tiled=True
+    normed = norm_rows(head_at, hidden_in, attn, gain_moe)
+    rows = spread_rows(lax.all_gather(normed, "head", tiled=True))
+    where = jnp.stack([my_ctx, EXP_CTX * my_ctx + my_head // shards]).astype(jnp.int32)
+    evens = list(range(0, n_ctx, 2))
+    odds = [mask | CORE for mask in evens]
+    near, far = (
+        expert_pieces(where, [rows[mask] for mask in masks], masks, w_gate, w_up, w_down, routes)
+        for masks in (evens, odds)
     )
-    grads = core_grads(n_ctx, me, qkv, grad_core, steps, fwd, bwd)
+    arrived, others = collect_terms(near, far, evens)
+    total = sum_terms(head_at, attn, near, arrived, others, n_head)
+    moe = lax.psum_scatter(total, "head", scatter_dimension=0, tiled=True)
+    grads = core_grads(me, qkv, grad_core, steps, fwd, bwd)
     own = lax.dynamic_slice_in_dim(hidden_in, my_head * cols, cols, 1)
     layer_out = (own.astype(F32) + moe[0].astype(F32)).astype(BF)
     return (layer_out, *grads)

time: 389 us -> 264 us (0.68)
  waiting for transfers between devices: 323 us -> 143 us
  starting transfers between devices: 2.56 us -> 29.5 us
  local copies, waits for them, and re-layouts: 10.4 us -> 23.6 us
  blocking collectives: 0 us -> 12.7 us
    reduce_scatter x1, waiting for transfers between devices: 183 us -> 4.89 us  [body(): moe = lax.psum_scatter(total, 'head', scatter_dimension=0, tiled=True)]
    all_gather x3 -> x1, waiting for transfers between devices: 112 us -> 26.9 us  [body(): rows = spread_rows(lax.all_gather(normed, 'head', tiled=True))]
    ppermute x0 -> x22, waiting for transfers between devices: none -> 81.6 us  [swap(): lax.ppermute(value, 'ctx', [pair for pair in pairs if keep is None or kee...]
    ppermute x0 -> x22, starting transfers between devices: none -> 27 us  [swap(): lax.ppermute(value, 'ctx', [pair for pair in pairs if keep is None or kee...]
    all_gather x0 -> x1, blocking collectives: none -> 12.7 us  [body(): routes = lax.all_gather(routes, 'ctx')]
    unnamed x36 -> x48, local copies, waits for them, and re-layouts: 10.2 us -> 16.5 us
    pallas_call x2 -> x4, Pallas kernels: 22.2 us -> 25.4 us  [the longest x2 19.1 us: expert_pieces(): pl.pallas_call(functools.partial(expert_kernel, tuple(layout), tuple(mask...]
  transfers between devices with their start and end apart: 6 -> 26, of which waited for: 6 -> 18; matrix products, arithmetic and copies ran while one was open for 0% -> 3% of each run, Pallas kernels for 6% -> 5%
where the time goes in v2:
time: 264 us; the launch traced here: 263 us
  waiting for transfers between devices  143 us (54%)
  Pallas kernels  36.4 us (14%)
  starting transfers between devices  29.5 us (11%)
  local copies, waits for them, and re-layouts  23.6 us (9%)
  between operations  14 us (5%)
  blocking collectives  12.7 us (5%)
  other arithmetic  4.32 us (2%)
    ppermute x22, waiting for transfers between devices, swap(): lax.ppermute(value, 'ctx', [pair for pair in pairs if keep is None or kee...  81.6 us
    reduce_scatter x1, waiting for transfers between devices, body(): attn = lax.psum_scatter(partial, 'head', scatter_dimension=0, tiled=True)  28.7 us
    ppermute x22, starting transfers between devices, swap(): lax.ppermute(value, 'ctx', [pair for pair in pairs if keep is None or kee...  27 us
    all_gather x1, waiting for transfers between devices, body(): rows = spread_rows(lax.all_gather(normed, 'head', tiled=True))  26.9 us
    pallas_call x2, Pallas kernels, expert_pieces(): pl.pallas_call(functools.partial(expert_kernel, tuple(layout), tuple(mask...  19.1 us
    unnamed x48, local copies, waits for them, and re-layouts  16.5 us
    all_gather x1, blocking collectives, body(): routes = lax.all_gather(routes, 'ctx')  12.7 us
  transfers between devices with their start and end apart: 26, of which 18 were waited for; matrix products, arithmetic and copies ran while one was open for 3% of the time, Pallas kernels for 5%

profile of v2, /device:TPU:0, one launch (start us, length us, event | category | flops | bytes accessed | tf_op | source)
XLA Modules:
  0.0 263.5 jit_solution(15456317622349630727)
XLA Ops:
  7.2 2.8 %copy-done = bf16[2048,3,512]{2,0,1:T(8,128)(2,1)S(1)} copy-done((bf16[2048,3,512]{2,0,1:T(8,128)(2,1)S(1)}, bf16[2048,3,512]{2,0,1:T(8,128)(2,1)}, u32[]{:S(2)}) %copy-start) | copy-done | bytes 6291480
  10.0 1.2 copy-done.1
  11.2 0.7 copy-done.17
  11.9 3.8 %qkv_projection.1 = (bf16[3,256,512]{2,1,0:T(8,128)(2,1)S(1)}, bf16[3,16,512]{2,1,0:T(8,128)(2,1)S(1)}) custom-call(bf16[256,2048]{1,0:T(8,128)(2,1)S(1)} %copy-done.1, f32[1,2048]{1,0:T(1,128)S(1)} %bitcast.65, bf16[3,2048,512]{2,1,0:T(8,128)(2,1)S(1)} %bitcast.49), custom_call_target="tpu_custom_call" | custom-call | tf_op jit(solution)/shard_map/qkv_projection/pallas_call | solution.py:52
  15.8 2.4 collective-permute-start
  18.1 0.9 collective-permute-done.rim_ref
  19.0 2.2 conv_states.1
  21.2 8.0 %collective-permute-start.3 = (bf16[4,144,128]{2,1,0:T(8,128)(2,1)S(1)}, bf16[4,144,128]{2,1,0:T(8,128)(2,1)S(1)}, u32[]{:S(2)}, u32[]{:S(2)}) collective-permute-start(bf16[4,144,128]{2,1,0:T(8,128)(2,1)S(1)} %get-tuple-element.15.refs_0_), channel_id=1, source_target_pairs={{0,24},{4,28},{8,16},{12,20},{1,25},{5,29},{9,17},{13,21},{2,26},{... | collective-permute-start | bytes 442376 | tf_op jit(solution)/shard_map/ppermute | solution.py:348
  29.2 1.3 collective-permute-start.2
  30.5 3.4 %collective-permute-start.1 = (bf16[4,144,128]{2,1,0:T(8,128)(2,1)S(1)}, bf16[4,144,128]{2,1,0:T(8,128)(2,1)S(1)}, u32[]{:S(2)}, u32[]{:S(2)}) collective-permute-start(bf16[4,144,128]{2,1,0:T(8,128)(2,1)S(1)} %get-tuple-element.15.refs_0_), channel_id=1, source_target_pairs={{0,8},{4,12},{16,24},{20,28},{1,9},{5,13},{17,25},{21,29},{2,10},{... | collective-permute-start | bytes 442376 | tf_op jit(solution)/shard_map/ppermute | solution.py:348
  33.8 1.0 collective-permute-done.2.refs_4_
  34.8 1.7 collective-permute-done.1.refs_2_
  36.6 2.0 collective-permute-done.4
  38.7 1.6 copy-done.3
  40.3 4.1 %core_out.1 = bf16[256,2048]{1,0:T(8,128)(2,1)} custom-call(s32[1]{0:T(128)} %bitcast.1.me_ref, bf16[3,256,512]{2,1,0:T(8,128)(2,1)S(1)} %get-tuple-element.14.qkv_ref, f32[4,256]{1,0:T(4,128)S(1)} %bitcast.61, f32[1,512]{1,0:T(1,128)S(1)} %bitcast.66, bf16[512,2048]{1,0:T(8,128)(2,1)S(1)} %copy-done.3, bf16[4,144,128]{2,1,0:T(8,128)(2,1)S(1)} %get-tuple-element.15.refs_0_, ...), custom_call_target="tpu_custom_call" | custom-call | tf_op jit(solution)/shard_map/core_out/pallas_call | solution.py:177
  44.4 28.7 %reduce-scatter.3.cloned.1.call-done.attn_ref = bf16[64,2048]{1,0:T(8,128)(2,1)} async-done(((bf16[256,2048]{1,0:T(8,128)(2,1)}), bf16[64,2048]{1,0:T(8,128)(2,1)}) %reduce-scatter.3.cloned.1.call-update) | async-done | bytes 262160 | tf_op jit(solution)/shard_map/reduce_scatter | solution.py:466
  73.1 0.9 copy-done.5
  74.1 0.9 moe_norm.1
  75.0 26.9 %all-gather.3.cloned.1.call-done.refs_0_ = bf16[256,2048]{1,0:T(8,128)(2,1)} async-done(((bf16[64,2048]{1,0:T(8,128)(2,1)}), bf16[256,2048]{1,0:T(8,128)(2,1)}) %all-gather.3.cloned.1.call-update) | async-done | bytes 1048592 | tf_op jit(solution)/shard_map/all_gather | solution.py:468
  102.0 1.5 collective-permute-start.6
  103.4 1.5 collective-permute-start.5
  104.9 22.1 %collective-permute-done.6.refs_2_ = bf16[256,2048]{1,0:T(8,128)(2,1)} collective-permute-done((bf16[256,2048]{1,0:T(8,128)(2,1)}, bf16[256,2048]{1,0:T(8,128)(2,1)}, u32[]{:S(2)}, u32[]{:S(2)}) %collective-permute-start.6) | collective-permute-done | bytes 1048608 | tf_op jit(solution)/shard_map/ppermute | solution.py:348
  127.0 1.9 slice.87
  129.0 1.5 collective-permute-start.8
  130.4 1.9 slice.86
  132.4 1.5 collective-permute-start.7
  133.8 0.5 collective-permute-start.11
  134.4 7.5 %collective-permute-done.8.refs_4_ = bf16[128,2048]{1,0:T(8,128)(2,1)} collective-permute-done((bf16[128,2048]{1,0:T(8,128)(2,1)}, bf16[128,2048]{1,0:T(8,128)(2,1)}, u32[]{:S(2)}, u32[]{:S(2)}) %collective-permute-start.8) | collective-permute-done | bytes 524320 | tf_op jit(solution)/shard_map/ppermute | solution.py:348
  141.9 3.1 %collective-permute-done.7.refs_3_ = bf16[128,2048]{1,0:T(8,128)(2,1)} collective-permute-done((bf16[128,2048]{1,0:T(8,128)(2,1)}, bf16[128,2048]{1,0:T(8,128)(2,1)}, u32[]{:S(2)}, u32[]{:S(2)}) %collective-permute-start.7) | collective-permute-done | bytes 524320 | tf_op jit(solution)/shard_map/ppermute | solution.py:348
  145.1 12.7 %all-gather = bf16[2048,128]{0,1:T(8,128)(2,1)} all-gather(bf16[256,128]{0,1:T(8,128)(2,1)S(1)} %fusion.9), channel_id=2, replica_groups=mesh['ctx'=8,'head'=4] {'ctx'}, dimensions={0}, use_global_device_ids=true | all-gather | bytes 589824 | tf_op jit(solution)/shard_map/all_gather | solution.py:459
  157.8 2.0 copy.23
  159.9 1.0 copy-done.13
  161.0 1.6 copy-done.19
  162.6 1.6 copy-done.20
  164.2 1.6 copy-done.21
  165.8 9.5 %expert_pieces.3 = bf16[4,256,2048]{2,1,0:T(8,128)(2,1)S(1)} custom-call(s32[2]{0:T(128)S(1)} %pad_add_fusion.where_ref, bf16[1,2048,512]{2,1,0:T(8,128)(2,1)S(1)} %copy-done.19, bf16[1,2048,512]{2,1,0:T(8,128)(2,1)S(1)} %copy-done.20, bf16[1,512,2048]{2,1,0:T(8,128)(2,1)S(1)} %copy-done.21, bf16[8,256,128]{2,1,0:T(8,128)(2,1)S(1)} %bitcast.58, ...), custom_call_target="tpu_custom_call" | custom-call | flops 6442450944 | bytes 14680064 | tf_op jit(solution)/shard_map/expert_pieces/pallas_call | solution.py:306
  175.3 0.4 collective-permute-start.14
  175.7 9.5 %expert_pieces.2.near_ref = bf16[4,256,2048]{2,1,0:T(8,128)(2,1)S(1)} custom-call(s32[2]{0:T(128)S(1)} %pad_add_fusion.where_ref, bf16[1,2048,512]{2,1,0:T(8,128)(2,1)S(1)} %copy-done.19, bf16[1,2048,512]{2,1,0:T(8,128)(2,1)S(1)} %copy-done.20, bf16[1,512,2048]{2,1,0:T(8,128)(2,1)S(1)} %copy-done.21, bf16[8,256,128]{2,1,0:T(8,128)(2,1)S(1)} %bitcast.59, ...), custom_call_target="tpu_custom_call" | custom-call | flops 6442450944 | bytes 14680064 | tf_op jit(solution)/shard_map/expert_pieces/pallas_call | solution.py:306
  185.3 0.4 fusion.3
  185.6 1.2 collective-permute-start.17
  186.8 0.9 collective-permute-start.15
  187.7 12.0 %collective-permute-done.17 = bf16[128,2048]{1,0:T(8,128)(2,1)S(1)} collective-permute-done((bf16[128,2048]{1,0:T(8,128)(2,1)S(1)}, bf16[128,2048]{1,0:T(8,128)(2,1)S(1)}, u32[]{:S(2)}, u32[]{:S(2)}) %collective-permute-start.17) | collective-permute-done | bytes 524320 | tf_op jit(solution)/shard_map/ppermute | solution.py:348
  199.7 0.8 collective-permute-done.15
  200.5 1.2 fusion
  201.7 1.0 collective-permute-start.18
  202.7 0.6 collective-permute-start.16
  203.2 22.6 %collective-permute-done.18.refs_1_ = bf16[256,2048]{1,0:T(8,128)(2,1)S(1)} collective-permute-done((bf16[256,2048]{1,0:T(8,128)(2,1)S(1)}, bf16[256,2048]{1,0:T(8,128)(2,1)S(1)}, u32[]{:S(2)}, u32[]{:S(2)}) %collective-permute-start.18) | collective-permute-done | bytes 1048608 | tf_op jit(solution)/shard_map/ppermute | solution.py:348
  225.8 0.6 collective-permute-done.16.refs_0_
  226.5 2.2 sum_terms.1
  228.7 1.3 collective-permute-start.21
  230.0 1.3 collective-permute-start.20
  231.3 1.3 collective-permute-start.19
  232.6 5.3 %collective-permute-done.21.refs_14_ = bf16[4,144,128]{2,1,0:T(8,128)(2,1)S(1)} collective-permute-done((bf16[4,144,128]{2,1,0:T(8,128)(2,1)S(1)}, bf16[4,144,128]{2,1,0:T(8,128)(2,1)S(1)}, u32[]{:S(2)}, u32[]{:S(2)}) %collective-permute-start.21) | collective-permute-done | bytes 147488 | tf_op jit(solution)/shard_map/ppermute | solution.py:348
  237.9 0.4 collective-permute-done.20.refs_12_
  238.3 0.9 pad_maximum_fusion.1
  239.2 0.7 copy-done.7
  239.9 2.3 collective-permute-done.22
  242.2 1.2 slice_bitcast_fusion
  243.4 0.9 copy-done.8
  244.3 0.9 copy-done.10
  245.2 0.9 copy-done.12
  246.2 4.2 %core_grads.1 = (bf16[256,512]{1,0:T(8,128)(2,1)}, bf16[256,512]{1,0:T(8,128)(2,1)}, bf16[256,512]{1,0:T(8,128)(2,1)}) custom-call(s32[1]{0:T(128)} %bitcast.1.me_ref, bf16[3,256,512]{2,1,0:T(8,128)(2,1)S(1)} %get-tuple-element.14.qkv_ref, bf16[256,512]{1,0:T(8,128)(2,1)S(1)} %copy-done.4, f32[4,256]{1,0:T(4,128)S(1)} %bitcast.62, ...), custom_call_target="tpu_custom_call" | custom-call | tf_op jit(solution)/shard_map/core_grads/pallas_call | solution.py:218
  250.3 4.9 %reduce-scatter.5.cloned.1.call-done = bf16[1,256,512]{2,1,0:T(8,128)(2,1)} async-done(((bf16[4,256,512]{2,1,0:T(8,128)(2,1)}), bf16[1,256,512]{2,1,0:T(8,128)(2,1)}) %reduce-scatter.5.cloned.1.call-update) | async-done | bytes 262160 | tf_op jit(solution)/shard_map/reduce_scatter | solution.py:478
  255.2 1.7 fusion.4
  (62 shorter events, 0.7 us)
Async XLA Ops:
  7.2 66.0 %reduce-scatter.3.cloned.1.call-start = ((), (), s32[]{:S(2)}) async-start(), calls=%async_computation.2 | async-start | bytes 1310720 | tf_op jit(solution)/shard_map/reduce_scatter | solution.py:466
  7.2 2.8 %copy-start = (bf16[2048,3,512]{2,0,1:T(8,128)(2,1)S(1)}, bf16[2048,3,512]{2,0,1:T(8,128)(2,1)}, u32[]{:S(2)}) copy-start(bf16[2048,3,512]{2,0,1:T(8,128)(2,1)} %param.16) | copy-start | bytes 18874372
  10.0 1.2 copy-start.1
  11.2 0.7 copy-start.17
  11.9 7.1 %copy-start.4 = (bf16[256,512]{1,0:T(8,128)(2,1)S(1)}, bf16[256,512]{1,0:T(8,128)(2,1)}, u32[]{:S(2)}) copy-start(bf16[256,512]{1,0:T(8,128)(2,1)} %cot_ref.3) | copy-start | bytes 786436
  11.9 7.1 %copy-start.14 = (f32[256,4]{0,1:T(4,128)S(1)}, f32[256,4]{0,1:T(4,128)}, u32[]{:S(2)}) copy-start(f32[256,4]{0,1:T(4,128)} %param.18) | copy-start | bytes 12292
  11.9 7.1 %copy-start.15 = (f32[4,3,512]{2,0,1:T(4,128)S(1)}, f32[4,3,512]{2,0,1:T(4,128)}, u32[]{:S(2)}) copy-start(f32[4,3,512]{2,0,1:T(4,128)} %param.17) | copy-start | bytes 73732
  15.8 22.9 %copy-start.18 = (f32[512]{0:T(512)S(1)}, f32[512]{0:T(512)}, u32[]{:S(2)}) copy-start(f32[512]{0:T(512)} %param.19) | copy-start | bytes 6148
  15.8 3.2 %collective-permute-start = (bf16[3,16,512]{2,1,0:T(8,128)(2,1)S(1)}, bf16[3,16,512]{2,1,0:T(8,128)(2,1)S(1)}, u32[]{:S(2)}, u32[]{:S(2)}) collective-permute-start(bf16[3,16,512]{2,1,0:T(8,128)(2,1)S(1)} %get-tuple-element.13), channel_id=1, source_target_pairs={{0,4},{4,8},{8,12},{12,16},{16,20},{20,24},{24,28},{1,5},{5,9},{9,... | collective-permute-start | bytes 147464 | tf_op jit(solution)/shard_map/ppermute | solution.py:461
  21.2 12.7 %collective-permute-start.3 = (bf16[4,144,128]{2,1,0:T(8,128)(2,1)S(1)}, bf16[4,144,128]{2,1,0:T(8,128)(2,1)S(1)}, u32[]{:S(2)}, u32[]{:S(2)}) collective-permute-start(bf16[4,144,128]{2,1,0:T(8,128)(2,1)S(1)} %get-tuple-element.15.refs_0_), channel_id=1, source_target_pairs={{0,24},{4,28},{8,16},{12,20},{1,25},{5,29},{9,17},{13,21},{2,26},{... | collective-permute-start | bytes 442376 | tf_op jit(solution)/shard_map/ppermute | solution.py:348
  29.2 5.6 %collective-permute-start.2 = (bf16[4,144,128]{2,1,0:T(8,128)(2,1)S(1)}, bf16[4,144,128]{2,1,0:T(8,128)(2,1)S(1)}, u32[]{:S(2)}, u32[]{:S(2)}) collective-permute-start(bf16[4,144,128]{2,1,0:T(8,128)(2,1)S(1)} %get-tuple-element.15.refs_0_), channel_id=1, source_target_pairs={{0,16},{4,20},{8,24},{12,28},{1,17},{5,21},{9,25},{13,29},{2,18},{... | collective-permute-start | bytes 442376 | tf_op jit(solution)/shard_map/ppermute | solution.py:348
  30.5 6.0 %collective-permute-start.1 = (bf16[4,144,128]{2,1,0:T(8,128)(2,1)S(1)}, bf16[4,144,128]{2,1,0:T(8,128)(2,1)S(1)}, u32[]{:S(2)}, u32[]{:S(2)}) collective-permute-start(bf16[4,144,128]{2,1,0:T(8,128)(2,1)S(1)} %get-tuple-element.15.refs_0_), channel_id=1, source_target_pairs={{0,8},{4,12},{16,24},{20,28},{1,9},{5,13},{17,25},{21,29},{2,10},{... | collective-permute-start | bytes 442376 | tf_op jit(solution)/shard_map/ppermute | solution.py:348
  36.6 2.1 collective-permute-start.4
  38.7 1.6 copy-start.3
  40.3 32.9 %copy-start.2 = (bf16[256,2048]{1,0:T(8,128)(2,1)S(1)}, bf16[256,2048]{1,0:T(8,128)(2,1)}, u32[]{:S(2)}) copy-start(bf16[256,2048]{1,0:T(8,128)(2,1)} %x_ref.3) | copy-start | bytes 3145732
  40.3 32.9 %copy-start.16 = (f32[2048]{0:T(1024)S(1)}, f32[2048]{0:T(1024)}, u32[]{:S(2)}) copy-start(f32[2048]{0:T(1024)} %param.21) | copy-start | bytes 24580
  44.3 90.0 %copy-start.22 = (f32[256,8]{0,1:T(8,128)S(1)}, f32[256,8]{0,1:T(8,128)}, u32[]{:S(2)}) copy-start(f32[256,8]{0,1:T(8,128)} %param.23) | copy-start | bytes 24580
  44.3 90.0 %copy-start.23 = (s32[256,8]{0,1:T(8,128)S(1)}, s32[256,8]{0,1:T(8,128)}, u32[]{:S(2)}) copy-start(s32[256,8]{0,1:T(8,128)} %param.22) | copy-start | bytes 24580
  44.4 57.6 %all-gather.3.cloned.1.call-start = ((), (), s32[]{:S(2)}) async-start(), calls=%async_computation.3 | async-start | bytes 1310720 | tf_op jit(solution)/shard_map/all_gather | solution.py:468
  73.1 1.0 copy-start.5
  75.0 180.2 %reduce-scatter.5.cloned.1.call-start = ((), (), s32[]{:S(2)}) async-start(), calls=%async_computation.4 | async-start | bytes 1310720 | tf_op jit(solution)/shard_map/reduce_scatter | solution.py:478
  102.0 25.1 %collective-permute-start.6 = (bf16[256,2048]{1,0:T(8,128)(2,1)}, bf16[256,2048]{1,0:T(8,128)(2,1)}, u32[]{:S(2)}, u32[]{:S(2)}) collective-permute-start(bf16[256,2048]{1,0:T(8,128)(2,1)} %all-gather.3.cloned.1.call-done.refs_0_), channel_id=1, source_target_pairs={{0,16},{4,20},{8,24},{12,28},{16,0},{20,4},{24,8},{28,12},{1,17},{... | collective-permute-start | bytes 3145736 | tf_op jit(solution)/shard_map/ppermute | solution.py:348
  103.4 27.0 %collective-permute-start.5 = (bf16[256,2048]{1,0:T(8,128)(2,1)}, bf16[256,2048]{1,0:T(8,128)(2,1)}, u32[]{:S(2)}, u32[]{:S(2)}) collective-permute-start(bf16[256,2048]{1,0:T(8,128)(2,1)} %all-gather.3.cloned.1.call-done.refs_0_), channel_id=1, source_target_pairs={{0,8},{4,12},{8,0},{12,4},{16,24},{20,28},{24,16},{28,20},{1,9},{5... | collective-permute-start | bytes 3145736 | tf_op jit(solution)/shard_map/ppermute | solution.py:348
  129.0 12.9 %collective-permute-start.8 = (bf16[128,2048]{1,0:T(8,128)(2,1)}, bf16[128,2048]{1,0:T(8,128)(2,1)}, u32[]{:S(2)}, u32[]{:S(2)}) collective-permute-start(bf16[128,2048]{1,0:T(8,128)(2,1)} %slice.87), channel_id=1, source_target_pairs={{0,8},{4,12},{8,0},{12,4},{16,24},{20,28},{24,16},{28,20},{1,9},{5... | collective-permute-start | bytes 1572872 | tf_op jit(solution)/shard_map/ppermute | solution.py:348
  132.4 12.7 %collective-permute-start.7 = (bf16[128,2048]{1,0:T(8,128)(2,1)}, bf16[128,2048]{1,0:T(8,128)(2,1)}, u32[]{:S(2)}, u32[]{:S(2)}) collective-permute-start(bf16[128,2048]{1,0:T(8,128)(2,1)} %slice.86), channel_id=1, source_target_pairs={{0,16},{4,20},{8,24},{12,28},{16,0},{20,4},{24,8},{28,12},{1,17},{... | collective-permute-start | bytes 1572872 | tf_op jit(solution)/shard_map/ppermute | solution.py:348
  133.8 26.1 %collective-permute-start.9 = (bf16[256,2048]{1,0:T(8,128)(2,1)}, bf16[256,2048]{1,0:T(8,128)(2,1)}, u32[]{:S(2)}, u32[]{:S(2)}) collective-permute-start(bf16[256,2048]{1,0:T(8,128)(2,1)} %all-gather.3.cloned.1.call-done.refs_0_), channel_id=1, source_target_pairs={{0,4},{4,0},{8,12},{12,8},{16,20},{20,16},{24,28},{28,24},{1,5},{5... | collective-permute-start | bytes 3145736 | tf_op jit(solution)/shard_map/ppermute | solution.py:348
  133.8 26.1 %collective-permute-start.11 = (bf16[256,2048]{1,0:T(8,128)(2,1)}, bf16[256,2048]{1,0:T(8,128)(2,1)}, u32[]{:S(2)}, u32[]{:S(2)}) collective-permute-start(bf16[256,2048]{1,0:T(8,128)(2,1)} %collective-permute-done.6.refs_2_), channel_id=1, source_target_pairs={{0,4},{4,0},{8,12},{12,8},{16,20},{20,16},{24,28},{28,24},{1,5},{5... | collective-permute-start | bytes 3145736 | tf_op jit(solution)/shard_map/ppermute | solution.py:348
  134.4 25.6 %collective-permute-start.10 = (bf16[256,2048]{1,0:T(8,128)(2,1)}, bf16[256,2048]{1,0:T(8,128)(2,1)}, u32[]{:S(2)}, u32[]{:S(2)}) collective-permute-start(bf16[256,2048]{1,0:T(8,128)(2,1)} %collective-permute-done.5.refs_1_), channel_id=1, source_target_pairs={{0,4},{4,0},{8,12},{12,8},{16,20},{20,16},{24,28},{28,24},{1,5},{5... | collective-permute-start | bytes 3145736 | tf_op jit(solution)/shard_map/ppermute | solution.py:348
  141.9 18.0 %collective-permute-start.13 = (bf16[128,2048]{1,0:T(8,128)(2,1)}, bf16[128,2048]{1,0:T(8,128)(2,1)}, u32[]{:S(2)}, u32[]{:S(2)}) collective-permute-start(bf16[128,2048]{1,0:T(8,128)(2,1)} %collective-permute-done.8.refs_4_), channel_id=1, source_target_pairs={{0,4},{4,0},{8,12},{12,8},{16,20},{20,16},{24,28},{28,24},{1,5},{5... | collective-permute-start | bytes 1572872 | tf_op jit(solution)/shard_map/ppermute | solution.py:348
  145.0 14.9 %collective-permute-start.12 = (bf16[128,2048]{1,0:T(8,128)(2,1)}, bf16[128,2048]{1,0:T(8,128)(2,1)}, u32[]{:S(2)}, u32[]{:S(2)}) collective-permute-start(bf16[128,2048]{1,0:T(8,128)(2,1)} %collective-permute-done.7.refs_3_), channel_id=1, source_target_pairs={{0,4},{4,0},{8,12},{12,8},{16,20},{20,16},{24,28},{28,24},{1,5},{5... | collective-permute-start | bytes 1572872 | tf_op jit(solution)/shard_map/ppermute | solution.py:348
  159.9 1.0 copy-start.13
  161.0 1.6 copy-start.19
  162.6 1.6 copy-start.20
  164.2 1.6 copy-start.21
  175.3 10.0 %collective-permute-start.14 = (bf16[4,256,2048]{2,1,0:T(8,128)(2,1)S(1)}, bf16[4,256,2048]{2,1,0:T(8,128)(2,1)S(1)}, u32[]{:S(2)}, u32[]{:S(2)}) collective-permute-start(bf16[4,256,2048]{2,1,0:T(8,128)(2,1)S(1)} %expert_pieces.3), channel_id=1, source_target_pairs={{0,4},{4,0},{8,12},{12,8},{16,20},{20,16},{24,28},{28,24},{1,5},{5... | collective-permute-start | bytes 12582920 | tf_op jit(solution)/shard_map/ppermute | solution.py:348
  185.6 14.1 %collective-permute-start.17 = (bf16[128,2048]{1,0:T(8,128)(2,1)S(1)}, bf16[128,2048]{1,0:T(8,128)(2,1)S(1)}, u32[]{:S(2)}, u32[]{:S(2)}) collective-permute-start(bf16[128,2048]{1,0:T(8,128)(2,1)S(1)} %get-tuple-element.22), channel_id=1, source_target_pairs={{0,8},{4,12},{8,0},{12,4},{16,24},{20,28},{24,16},{28,20},{1,9},{5... | collective-permute-start | bytes 1572872 | tf_op jit(solution)/shard_map/ppermute | solution.py:348
  186.8 39.7 %copy-start.6 = (bf16[64,2048]{1,0:T(8,128)(2,1)S(1)}, bf16[64,2048]{1,0:T(8,128)(2,1)}, u32[]{:S(2)}) copy-start(bf16[64,2048]{1,0:T(8,128)(2,1)} %reduce-scatter.3.cloned.1.call-done.attn_ref) | copy-start | bytes 786436
  186.8 13.7 %collective-permute-start.15 = (bf16[128,2048]{1,0:T(8,128)(2,1)S(1)}, bf16[128,2048]{1,0:T(8,128)(2,1)S(1)}, u32[]{:S(2)}, u32[]{:S(2)}) collective-permute-start(bf16[128,2048]{1,0:T(8,128)(2,1)S(1)} %get-tuple-element.23), channel_id=1, source_target_pairs={{0,16},{4,20},{8,24},{12,28},{16,0},{20,4},{24,8},{28,12},{1,17},{... | collective-permute-start | bytes 1572872 | tf_op jit(solution)/shard_map/ppermute | solution.py:348
  201.7 24.1 %collective-permute-start.18 = (bf16[256,2048]{1,0:T(8,128)(2,1)S(1)}, bf16[256,2048]{1,0:T(8,128)(2,1)S(1)}, u32[]{:S(2)}, u32[]{:S(2)}) collective-permute-start(bf16[256,2048]{1,0:T(8,128)(2,1)S(1)} %get-tuple-element.20), channel_id=1, source_target_pairs={{0,16},{4,20},{8,24},{12,28},{16,0},{20,4},{24,8},{28,12},{1,17},{... | collective-permute-start | bytes 3145736 | tf_op jit(solution)/shard_map/ppermute | solution.py:348
  202.7 23.8 %collective-permute-start.16 = (bf16[256,2048]{1,0:T(8,128)(2,1)S(1)}, bf16[256,2048]{1,0:T(8,128)(2,1)S(1)}, u32[]{:S(2)}, u32[]{:S(2)}) collective-permute-start(bf16[256,2048]{1,0:T(8,128)(2,1)S(1)} %get-tuple-element.21), channel_id=1, source_target_pairs={{0,8},{4,12},{8,0},{12,4},{16,24},{20,28},{24,16},{28,20},{1,9},{5... | collective-permute-start | bytes 3145736 | tf_op jit(solution)/shard_map/ppermute | solution.py:348
  228.7 9.2 %collective-permute-start.21 = (bf16[4,144,128]{2,1,0:T(8,128)(2,1)S(1)}, bf16[4,144,128]{2,1,0:T(8,128)(2,1)S(1)}, u32[]{:S(2)}, u32[]{:S(2)}) collective-permute-start(bf16[4,144,128]{2,1,0:T(8,128)(2,1)S(1)} %get-tuple-element.16.refs_8_), channel_id=1, source_target_pairs={{16,8},{20,12},{24,0},{28,4},{17,9},{21,13},{25,1},{29,5},{18,10},... | collective-permute-start | bytes 442376 | tf_op jit(solution)/shard_map/ppermute | solution.py:348
  230.0 8.2 %collective-permute-start.20 = (bf16[4,144,128]{2,1,0:T(8,128)(2,1)S(1)}, bf16[4,144,128]{2,1,0:T(8,128)(2,1)S(1)}, u32[]{:S(2)}, u32[]{:S(2)}) collective-permute-start(bf16[4,144,128]{2,1,0:T(8,128)(2,1)S(1)} %get-tuple-element.16.refs_8_), channel_id=1, source_target_pairs={{16,0},{20,4},{24,8},{28,12},{17,1},{21,5},{25,9},{29,13},{18,2},{... | collective-permute-start | bytes 442376 | tf_op jit(solution)/shard_map/ppermute | solution.py:348
  231.3 7.0 %collective-permute-start.19 = (bf16[4,144,128]{2,1,0:T(8,128)(2,1)S(1)}, bf16[4,144,128]{2,1,0:T(8,128)(2,1)S(1)}, u32[]{:S(2)}, u32[]{:S(2)}) collective-permute-start(bf16[4,144,128]{2,1,0:T(8,128)(2,1)S(1)} %get-tuple-element.16.refs_8_), channel_id=1, source_target_pairs={{8,0},{12,4},{24,16},{28,20},{9,1},{13,5},{25,17},{29,21},{10,2},{... | collective-permute-start | bytes 442376 | tf_op jit(solution)/shard_map/ppermute | solution.py:348
  238.2 1.0 copy-start.9
  238.3 0.9 copy-start.11
  239.2 0.7 copy-start.7
  239.9 2.3 collective-permute-start.22
  243.4 0.9 copy-start.8
  244.3 0.9 copy-start.10
  245.2 0.9 copy-start.12
Sparse Core Ops, SparseCore 0:
  44.5 28.5 reduce-scatter.2
  75.3 26.5 all-gather.2
  228.8 26.3 reduce-scatter.4

commit v3 on v2

v3 whole, which is shorter than its diff:
```python
import functools

import jax
import jax.numpy as jnp
from jax import lax
from jax.experimental import pallas as pl
from jax.experimental.pallas import tpu as pltpu
from jax.sharding import PartitionSpec as P

KERNEL = 4
EXP_CTX = 2
LANES = 128
RIM = 16
MIB = 1024 * 1024
HI = lax.Precision.HIGHEST
BF = jnp.bfloat16
F32 = jnp.float32
NT = (((1,), (1,)), ((), ()))
TN = (((0,), (0,)), ((), ()))
NN = (((1,), (0,)), ((), ()))


def params(mib):
    return pltpu.CompilerParams(vmem_limit_bytes=mib * MIB)


def mm(a, b, dims=NN):
    return lax.dot_general(a, b, dims, preferred_element_type=F32)


def pick_block(extent, target):
    return target if extent % target == 0 else extent


def qkv_kernel(x_hbm, gain_ref, w_hbm, mixed_ref, rim_ref, x_ref, w_ref, normed_ref, x_sem, sems):
    kinds, width, chans = w_ref.shape
    load = pltpu.make_async_copy(x_hbm, x_ref, x_sem)
    load.start()
    copies = [pltpu.make_async_copy(w_hbm.at[kind], w_ref.at[kind], sems.at[kind]) for kind in range(kinds)]
    for copy in copies:
        copy.start()
    load.wait()
    values = x_ref[...].astype(F32)
    scale = lax.rsqrt(jnp.mean(values * values, axis=-1, keepdims=True) + 1e-06)
    normed_ref[...] = (values * scale * gain_ref[...]).astype(BF)
    for kind in range(kinds):
        copies[kind].wait()
        out = mm(normed_ref[...], w_ref[kind]).astype(BF)
        mixed_ref[kind] = out
        rim_ref[kind] = out[out.shape[0] - RIM :]


def project(x, gain, weights):
    rows, width = x.shape
    kinds, _, chans = weights.shape
    vmem = pl.BlockSpec(memory_space=pltpu.VMEM)
    hbm = pl.BlockSpec(memory_space=pltpu.HBM)
    return pl.pallas_call(
        qkv_kernel,
        in_specs=[hbm, vmem, hbm],
        out_shape=[
            jax.ShapeDtypeStruct((kinds, rows, chans), BF),
            jax.ShapeDtypeStruct((kinds, RIM, chans), BF),
        ],
        scratch_shapes=[
            pltpu.VMEM((rows, width), BF),
            pltpu.VMEM((kinds, width, chans), BF),
            pltpu.VMEM((rows, width), BF),
            pltpu.SemaphoreType.DMA,
            pltpu.SemaphoreType.DMA((kinds,)),
        ],
        compiler_params=params(24),
        name="qkv_projection",
    )(x, gain.reshape(1, width), weights)


def decay_sums(steps):
    rows = steps.shape[1]
    row_at = lax.broadcasted_iota(jnp.int32, (rows, rows), 0)
    col_at = lax.broadcasted_iota(jnp.int32, (rows, rows), 1)
    lower = row_at >= col_at
    tri = jnp.where(lower, 1.0, 0.0).astype(F32)
    along = lax.dot_general(steps, tri, NT, precision=HI, preferred_element_type=F32)
    down = lax.dot_general(tri, steps, NT, precision=HI, preferred_element_type=F32)
    return along, down, lower


def payload_tail(total, size):
    full = jnp.broadcast_to(total, (RIM, size))
    first = full.astype(BF).astype(F32)
    second = (full - first).astype(BF).astype(F32)
    third = full - first - second
    at = lax.broadcasted_iota(jnp.int32, (RIM, size), 0)
    return jnp.where(at == 0, first, jnp.where(at == 1, second, jnp.where(at == 2, third, 0.0)))


def route_rows(ids_ref, weights_ref, experts):
    top, tok = ids_ref.shape
    expert = lax.broadcasted_iota(jnp.int32, (experts, tok), 0)
    table = jnp.zeros((experts, tok), F32)
    for choice in range(top):
        table += jnp.where(expert == ids_ref[choice : choice + 1, :], weights_ref[choice : choice + 1, :], 0.0)
    first = table.astype(BF).astype(F32)
    second = (table - first).astype(BF).astype(F32)
    return jnp.concatenate([first, second, table - first - second], axis=0)


def conv_kernel(
    experts, mixed_ref, rim_ref, taps_ref, steps_ref, cot_ref, ids_ref, weights_ref, qkv_ref, fwd_ref, bwd_ref, pad_ref
):
    kinds, rows, chans = mixed_ref.shape
    heads = steps_ref.shape[0]
    size = chans // heads
    along, down, _ = decay_sums(steps_ref[...])
    for kind in range(kinds):
        pad_ref[:RIM] = rim_ref[kind].astype(F32)
        pad_ref[RIM:] = mixed_ref[kind].astype(F32)
        total = taps_ref[kind, 0:1, :] * pad_ref[RIM:]
        for offset in range(1, KERNEL):
            total += taps_ref[kind, offset : offset + 1, :] * pad_ref[RIM - offset : RIM - offset + rows]
        activ = total * jax.nn.sigmoid(total)
        if kind == 0:
            activ = activ * size ** (-0.5)
        qkv_ref[kind] = activ.astype(BF)
    for head in range(heads):
        at = slice(head * size, (head + 1) * size)
        base = head * (size + RIM)
        last = along[head : head + 1, rows - 1 : rows]
        lead = jnp.exp(down[:, head : head + 1])
        tail = jnp.exp(last - down[:, head : head + 1])
        key_out = (qkv_ref[1, :, at].astype(F32) * tail).astype(BF)
        query_out = (qkv_ref[0, :, at].astype(F32) * lead).astype(BF)
        ends = payload_tail(last, size).astype(BF)
        fwd_ref[base : base + size] = mm(key_out, qkv_ref[2, :, at], TN).astype(BF)
        fwd_ref[base + size : base + size + RIM] = ends
        bwd_ref[base : base + size] = mm(query_out, cot_ref[:, at], TN).astype(BF)
        bwd_ref[base + size : base + size + RIM] = ends
    base = heads * (size + RIM)
    table = route_rows(ids_ref, weights_ref, experts).astype(BF)
    for part in range(rows // LANES):
        bwd_ref[base : base + 3 * experts] = table[:, part * LANES : (part + 1) * LANES]
        base += 3 * experts


def local_states(mixed, rim, taps, steps, cot, ids, weights, experts):
    kinds, rows, chans = mixed.shape
    heads = steps.shape[0]
    size = chans // heads
    states = heads * (size + RIM)
    return pl.pallas_call(
        functools.partial(conv_kernel, experts),
        out_shape=[
            jax.ShapeDtypeStruct((kinds, rows, chans), BF),
            jax.ShapeDtypeStruct((states, size), BF),
            jax.ShapeDtypeStruct((states + rows // LANES * 3 * experts, size), BF),
        ],
        scratch_shapes=[pltpu.VMEM((rows + RIM, chans), F32)],
        compiler_params=params(12),
        name="conv_states",
    )(mixed, rim, taps, steps, cot, ids, weights)


def arrange(me_ref, near_ref, far_ref, held_ref):
    for at in range(near_ref.shape[0]):
        held_ref[me_ref[0] ^ (2 * at)] = near_ref[at]
        held_ref[me_ref[0] ^ (2 * at + 1)] = far_ref[at]


def entering(held_ref, head, size, first, last, step):
    base = head * (size + RIM)

    def hop(count, total):
        at = first + count * step
        ends = held_ref[at, base + size : base + size + RIM, :].astype(F32)
        factor = jnp.exp(ends[0:1] + ends[1:2] + ends[2:3])
        return factor * total + held_ref[at, base : base + size, :].astype(F32)

    return lax.fori_loop(0, (last - first) * step, hop, jnp.zeros((size, size), F32))


def core_kernel(me_ref, qkv_ref, steps_ref, gain_ref, near_ref, far_ref, w_hbm, *refs):
    out_refs, (headed_ref, held_ref, w_ref, sem) = refs[:-4], refs[-4:]
    load = pltpu.make_async_copy(w_hbm, w_ref, sem)
    load.start()
    _, rows, chans = qkv_ref.shape
    heads = steps_ref.shape[0]
    size = chans // heads
    arrange(me_ref, near_ref, far_ref, held_ref)
    along, down, lower = decay_sums(steps_ref[...])
    for head in range(heads):
        at = slice(head * size, (head + 1) * size)
        state = entering(held_ref, head, size, 0, me_ref[0], 1).astype(BF)
        diff = down[:, head : head + 1] - along[head : head + 1, :]
        mask = jnp.exp(jnp.where(lower, diff, -jnp.inf))
        query = qkv_ref[0, :, at]
        scores = (mm(query, qkv_ref[1, :, at], NT) * mask).astype(BF)
        attended = mm(scores, qkv_ref[2, :, at])
        attended += mm(query, state) * jnp.exp(down[:, head : head + 1])
        scale = lax.rsqrt(jnp.mean(attended * attended, axis=-1, keepdims=True) + 1e-06)
        headed_ref[:, at] = (attended * scale * gain_ref[:, at]).astype(BF)
    load.wait()
    part = rows // len(out_refs)
    out = mm(headed_ref[...], w_ref[...]).astype(BF)
    for chunk, ref in enumerate(out_refs):
        ref[...] = out[chunk * part : (chunk + 1) * part]


def core_out(me, qkv, steps, near, far, gain, w_out, chunks):
    _, rows, chans = qkv.shape
    width = w_out.shape[1]
    vmem = pl.BlockSpec(memory_space=pltpu.VMEM)
    return pl.pallas_call(
        core_kernel,
        in_specs=[pl.BlockSpec(memory_space=pltpu.SMEM)] + [vmem] * 5 + [pl.BlockSpec(memory_space=pltpu.HBM)],
        out_shape=[jax.ShapeDtypeStruct((rows // chunks, width), BF)] * chunks,
        scratch_shapes=[
            pltpu.VMEM((rows, chans), BF),
            pltpu.VMEM((2 * near.shape[0], *near.shape[1:]), BF),
            pltpu.VMEM(w_out.shape, BF),
            pltpu.SemaphoreType.DMA,
        ],
        compiler_params=params(20),
        name="core_out",
    )(me, qkv, steps, gain.reshape(1, chans), near, far, w_out)


def grad_kernel(
    experts, me_ref, qkv_ref, cot_ref, steps_ref, fwd_near, fwd_far, bwd_near, bwd_far, gate_hbm, up_hbm, down_hbm,
    gq_ref, gk_ref, gv_ref, columns_ref, gate_ref, up_ref, down_ref, fwd_ref, bwd_ref, sems,
):
    copies = [
        pltpu.make_async_copy(source, target, sems.at[at])
        for at, (source, target) in enumerate(((gate_hbm, gate_ref), (up_hbm, up_ref), (down_hbm, down_ref)))
    ]
    for copy in copies:
        copy.start()
    _, rows, chans = qkv_ref.shape
    heads = steps_ref.shape[0]
    size = chans // heads
    count = fwd_ref.shape[0]
    arrange(me_ref, fwd_near, fwd_far, fwd_ref)
    arrange(me_ref, bwd_near, bwd_far, bwd_ref)
    along, down, lower = decay_sums(steps_ref[...])
    for head in range(heads):
        at = slice(head * size, (head + 1) * size)
        state = entering(fwd_ref, head, size, 0, me_ref[0], 1).astype(BF)
        after = entering(bwd_ref, head, size, count - 1, me_ref[0], -1).astype(BF)
        here = down[:, head : head + 1]
        lead = jnp.exp(here)
        tail = jnp.exp(along[head : head + 1, rows - 1 : rows] - here)
        mask = jnp.exp(jnp.where(lower, here - along[head : head + 1, :], -jnp.inf))
        query, key, val = qkv_ref[0, :, at], qkv_ref[1, :, at], qkv_ref[2, :, at]
        cot = cot_ref[:, at]
        scores = (mm(query, key, NT) * mask).astype(BF)
        dov = (mm(cot, val, NT) * mask).astype(BF)
        gq_ref[:, at] = (mm(dov, key) + lead * mm(cot, state, NT)).astype(BF)
        gk_ref[:, at] = (mm(dov, query, TN) + tail * mm(val, after, NT)).astype(BF)
        gv_ref[:, at] = (mm(scores, cot, TN) + tail * mm(key, after)).astype(BF)

    here = lax.broadcasted_iota(jnp.int32, (3 * experts, LANES), 0)
    mine = (here == me_ref[1]) | (here == me_ref[1] + experts) | (here == me_ref[1] + 2 * experts)
    diagonal = lax.broadcasted_iota(jnp.int32, (LANES, LANES), 0) == lax.broadcasted_iota(jnp.int32, (LANES, LANES), 1)
    for mask in range(count):
        source = bwd_far if mask % 2 else bwd_near
        base = heads * (size + RIM)
        for part in range(rows // LANES):
            table = source[mask // 2, base : base + 3 * experts, :].astype(F32)
            row = jnp.sum(jnp.where(mine, table, 0.0), axis=0, keepdims=True)
            column = jnp.sum(jnp.where(diagonal, jnp.broadcast_to(row, (LANES, LANES)), 0.0), axis=1, keepdims=True)
            columns_ref[mask, part * LANES : (part + 1) * LANES, :] = jnp.broadcast_to(column, (LANES, LANES))
            base += 3 * experts
    for copy in copies:
        copy.wait()


def core_grads(where, qkv, cot, steps, fwd, bwd, gate, up, down, experts):
    _, rows, chans = qkv.shape
    count = 2 * fwd[0].shape[0]
    vmem = pl.BlockSpec(memory_space=pltpu.VMEM)
    hbm = pl.BlockSpec(memory_space=pltpu.HBM)
    grad = jax.ShapeDtypeStruct((rows, chans), BF)
    return pl.pallas_call(
        functools.partial(grad_kernel, experts),
        in_specs=[pl.BlockSpec(memory_space=pltpu.SMEM)] + [vmem] * 7 + [hbm] * 3,
        out_specs=[vmem] * 7,
        out_shape=[grad, grad, grad, jax.ShapeDtypeStruct((count, rows, LANES), F32)]
        + [jax.ShapeDtypeStruct(part.shape, BF) for part in (gate, up, down)],
        scratch_shapes=[
            pltpu.VMEM((count, *fwd[0].shape[1:]), BF),
            pltpu.VMEM((count, *bwd[0].shape[1:]), BF),
            pltpu.SemaphoreType.DMA((3,)),
        ],
        compiler_params=params(24),
        name="core_grads",
    )(where, qkv, cot, steps, *fwd, *bwd, gate, up, down)


def norm_kernel(chunk, head_ref, x_ref, attn_ref, gain_ref, out_ref):
    rows = attn_ref.shape[0]
    start = pl.multiple_of(chunk + head_ref[0] * rows, rows)
    resid = x_ref[pl.ds(start, rows), :].astype(F32) + attn_ref[...].astype(F32)
    scale = lax.rsqrt(jnp.mean(resid * resid, axis=-1, keepdims=True) + 1e-06)
    out_ref[...] = (resid * scale * gain_ref[...]).astype(BF)


def norm_rows(chunk, my_head, x, attn, gain):
    rows, width = attn.shape
    vmem = pl.BlockSpec(memory_space=pltpu.VMEM)
    return pl.pallas_call(
        functools.partial(norm_kernel, chunk),
        in_specs=[pl.BlockSpec(memory_space=pltpu.SMEM)] + [vmem] * 3,
        out_shape=jax.ShapeDtypeStruct((rows, width), BF),
        compiler_params=params(8),
        name="moe_norm",
    )(my_head, x, attn, gain.reshape(1, width))


PAIR = 2


def expert_kernel(masks, chunk, gate_ref, up_ref, down_ref, columns_ref, *refs):
    row_refs, (out_ref, rows_ref, sems) = refs[: len(masks)], refs[len(masks) :]
    _, tok, width = out_ref.shape
    steps = len(masks) // PAIR
    step = pl.program_id(0)
    slot = lax.rem(step, 2)

    def start(at):
        for part in range(PAIR):
            target = rows_ref.at[at % 2, pl.ds(part * tok, tok)]
            pltpu.make_async_copy(row_refs[PAIR * at + part], target, sems.at[at % 2]).start()

    @pl.when(step == 0)
    def _():
        start(0)

    for at in range(1, steps):

        @pl.when(step == at - 1)
        def _(at=at):
            start(at)

    pltpu.make_async_copy(rows_ref.at[slot], rows_ref.at[slot], sems.at[slot]).wait()
    tokens = rows_ref[slot]
    gate = mm(tokens, gate_ref[0])
    inner = (gate * jax.nn.sigmoid(gate) * mm(tokens, up_ref[0])).astype(BF)
    cols = pick_block(width, 512)
    weights = []
    for part in range(PAIR):
        mask = jnp.int32(masks[part])
        for at in range(1, steps):
            mask = jnp.where(step == at, masks[PAIR * at + part], mask)
        weights.append(columns_ref[mask, chunk : chunk + tok, :1])
    for begin in range(0, width, cols):
        piece = mm(inner, down_ref[0, :, begin : begin + cols])
        for part in range(PAIR):
            scaled = piece[part * tok : (part + 1) * tok] * weights[part]
            out_ref[part, :, begin : begin + cols] = scaled.astype(BF)


def expert_pieces(chunk, blocks, masks, gate, up, down, columns):
    tok, width = blocks[0].shape
    hidden = gate.shape[2]
    count = len(blocks)
    vmem = pl.BlockSpec(memory_space=pltpu.VMEM)
    return pl.pallas_call(
        functools.partial(expert_kernel, tuple(masks), chunk),
        grid=(count // PAIR,),
        in_specs=[vmem] * 4 + [pl.BlockSpec(memory_space=pl.ANY)] * count,
        out_specs=pl.BlockSpec((PAIR, tok, width), lambda i: (i, 0, 0)),
        out_shape=jax.ShapeDtypeStruct((count, tok, width), BF),
        scratch_shapes=[pltpu.VMEM((2, PAIR * tok, width), BF), pltpu.SemaphoreType.DMA((2,))],
        compiler_params=params(16),
        cost_estimate=pl.CostEstimate(
            flops=6 * count * tok * width * hidden,
            bytes_accessed=4 * count * tok * width,
            transcendentals=count * tok * hidden,
        ),
        name="expert_pieces",
    )(gate, up, down, columns, *blocks)


CORE, ROW, COL = 1, 2, 4
PLANE = 8


def swap(value, mask, keep=None):
    count = lax.axis_size("ctx")
    pairs = [(at, at ^ mask) for at in range(count)]
    return lax.ppermute(value, "ctx", [pair for pair in pairs if keep is None or keep(*pair)])


def spread_states(own, keep=None):
    near = jnp.stack([own] + [swap(own, mask, keep) for mask in range(2, lax.axis_size("ctx"), 2)])
    return near, swap(near, CORE)


def hops(chunk):
    return (ROW, COL) if chunk % 2 == 0 else (COL, ROW)


def spread_rows(own, chunk):
    count = lax.axis_size("ctx")
    near = {0: own}
    if count == PLANE:
        first, second = hops(chunk)
        near[first] = swap(own, first)
        near[second] = swap(own, second)
        near[ROW | COL] = swap(near[first], second)
    else:
        for mask in range(2, count, 2):
            near[mask] = swap(own, mask)
    return near | {mask | CORE: swap(rows, CORE) for mask, rows in near.items()}


def plus(*terms):
    return functools.reduce(jnp.add, [term.astype(F32) for term in terms]).astype(BF)


def collect_terms(near, far, evens, chunk):
    arrived = swap(far, CORE)
    sums = {mask: (near[at], arrived[at]) for at, mask in enumerate(evens)}
    if lax.axis_size("ctx") == PLANE:
        first, second = hops(chunk)
        across = swap(plus(*sums[ROW | COL]), second)
        direct, across = lax.optimization_barrier((plus(*sums[second]), across))
        others = [swap(plus(*sums[first], across), first), swap(direct, second)]
    else:
        others = [swap(plus(*sums[mask]), mask) for mask in evens[1:]]
    return arrived, others


def sum_kernel(head_ref, attn_ref, near_ref, arrived_ref, *refs):
    others, out_ref = refs[:-1], refs[-1]
    part = attn_ref.shape[0]
    total = near_ref[0].astype(F32) + arrived_ref[0].astype(F32)
    for ref in others:
        total += ref[...].astype(F32)
    out_ref[0] = total.astype(BF)
    start = pl.multiple_of(head_ref[0] * part, part)
    mine = near_ref[0, pl.ds(start, part), :].astype(F32) + arrived_ref[0, pl.ds(start, part), :].astype(F32)
    for ref in others:
        mine += ref[pl.ds(start, part), :].astype(F32)
    out_ref[0, pl.ds(start, part), :] = (mine + attn_ref[...].astype(F32)).astype(BF)


def sum_terms(my_head, attn, near, arrived, others, n_head):
    _, tok, width = near.shape
    part = attn.shape[0]
    cols = width // n_head
    first = pl.BlockSpec((1, tok, cols), lambda i: (0, 0, i))
    return pl.pallas_call(
        sum_kernel,
        grid=(n_head,),
        in_specs=[
            pl.BlockSpec(memory_space=pltpu.SMEM),
            pl.BlockSpec((part, cols), lambda i: (0, i)),
            first,
            first,
        ]
        + [pl.BlockSpec((tok, cols), lambda i: (0, i))] * len(others),
        out_specs=pl.BlockSpec((1, tok, cols), lambda i: (i, 0, 0)),
        out_shape=jax.ShapeDtypeStruct((n_head, tok, cols), BF),
        compiler_params=params(16),
        name="sum_terms",
    )(my_head, attn, near, arrived, *others)


def final_kernel(head_ref, x_ref, *refs):
    del head_ref
    moe_refs, out_ref = refs[:-1], refs[-1]
    rows = moe_refs[0].shape[1]
    for chunk, ref in enumerate(moe_refs):
        at = slice(chunk * rows, (chunk + 1) * rows)
        out_ref[at] = (x_ref[at].astype(F32) + ref[0].astype(F32)).astype(BF)


def final_sum(my_head, x, moe):
    rows = x.shape[0]
    cols = moe[0].shape[2]
    return pl.pallas_call(
        final_kernel,
        grid_spec=pltpu.PrefetchScalarGridSpec(
            num_scalar_prefetch=1,
            grid=(1,),
            in_specs=[pl.BlockSpec((rows, cols), lambda i, head: (0, head[0]))]
            + [pl.BlockSpec(part.shape, lambda i, head: (0, 0, 0)) for part in moe],
            out_specs=pl.BlockSpec((rows, cols), lambda i, head: (0, 0)),
        ),
        out_shape=jax.ShapeDtypeStruct((rows, cols), BF),
        compiler_params=params(8),
        name="layer_out",
    )(my_head, x, *moe)


CHUNKS = 2


def body(
    hidden_in,
    gain_attn,
    w_qkv,
    conv_w,
    log_decay,
    norm_gain,
    w_out,
    gain_moe,
    expert_ids,
    route_weights,
    w_gate,
    w_up,
    w_down,
    grad_core,
):
    n_ctx, n_head = lax.axis_size("ctx"), lax.axis_size("head")
    my_ctx, my_head = lax.axis_index("ctx"), lax.axis_index("head")
    tok_dev = hidden_in.shape[0]
    experts = EXP_CTX * n_ctx
    shards = n_head // EXP_CTX
    where = jnp.stack([my_ctx, EXP_CTX * my_ctx + my_head // shards]).astype(jnp.int32)
    head_at = my_head.astype(jnp.int32).reshape(1)
    steps = log_decay.T
    chunk_rows = tok_dev // CHUNKS

    mixed, rim = project(hidden_in, gain_attn, jnp.transpose(w_qkv, (1, 0, 2)))
    rim = lax.ppermute(rim, "ctx", [(at, at + 1) for at in range(n_ctx - 1)])
    qkv, fwd, bwd = local_states(
        mixed, rim, jnp.transpose(conv_w, (1, 0, 2)), steps, grad_core, expert_ids.T, route_weights.T, experts
    )
    fwd = spread_states(fwd, lambda source, target: source < target)
    partials = core_out(where, qkv, steps, *fwd, norm_gain, w_out, CHUNKS)
    bwd, partials = lax.optimization_barrier((bwd, partials))
    attn = [lax.psum_scatter(part, "head", scatter_dimension=0, tiled=True) for part in partials]
    bwd = spread_states(bwd)
    *grads, columns, gate, up, down = core_grads(
        where, qkv, grad_core, steps, fwd, bwd, w_gate, w_up, w_down, experts
    )
    attn[0], columns = lax.optimization_barrier((attn[0], columns))
    own = []
    for chunk in range(CHUNKS):
        normed = norm_rows(chunk * chunk_rows, head_at, hidden_in, attn[chunk], gain_moe)
        own.append(lax.all_gather(normed, "head", tiled=True))
    moe = []
    for chunk in range(CHUNKS):
        rows = spread_rows(own[chunk], chunk)
        evens = [mask for mask in rows if not mask & CORE]
        near, far = (
            expert_pieces(chunk * chunk_rows, [rows[mask] for mask in masks], masks, gate, up, down, columns)
            for masks in (evens, [mask | CORE for mask in evens])
        )
        arrived, others = collect_terms(near, far, evens, chunk)
        total = sum_terms(head_at, attn[chunk], near, arrived, others, n_head)
        moe.append(lax.psum_scatter(total, "head", scatter_dimension=0, tiled=True))
    return (final_sum(head_at, hidden_in, moe), *grads)


def solution(mesh):
    in_specs = (
        P("ctx", None),
        P(),
        P(None, None, "head"),
        P(None, None, "head"),
        P("ctx", "head"),
        P("head"),
        P("head", None),
        P(),
        P("ctx", None),
        P("ctx", None),
        P(("ctx", "head"), None, None),
        P(("ctx", "head"), None, None),
        P(("ctx", "head"), None, None),
        P("ctx", "head"),
    )
    out_specs = (P("ctx", "head"), P("ctx", "head"), P("ctx", "head"), P("ctx", "head"))
    return jax.shard_map(body, mesh=mesh, in_specs=in_specs, out_specs=out_specs, check_vma=False)
```

time: 264 us -> 284 us (1.076)
  blocking collectives: 12.7 us -> 32.7 us
  waiting for transfers between devices: 143 us -> 136 us
  local copies, waits for them, and re-layouts: 23.6 us -> 29 us
  starting transfers between devices: 29.5 us -> 32.7 us
    all_gather x1 -> x0, waiting for transfers between devices: 26.9 us -> none  [body(): rows = spread_rows(lax.all_gather(normed, 'head', tiled=True))]
    all_gather x1 -> x2, blocking collectives: 12.7 us -> 32.7 us  [body(): own.append(lax.all_gather(normed, 'head', tiled=True))]
    unnamed x48 -> x78, local copies, waits for them, and re-layouts: 16.5 us -> 29 us
    reduce_scatter x2 -> x4, waiting for transfers between devices: 33.6 us -> 45.7 us  [the longest x2 24.4 us: body(): lax.psum_scatter(part, 'head', scatter_dimension=0, tiled=True)]
    ppermute x22 -> x30, waiting for transfers between devices: 81.6 us -> 89.6 us  [swap(): lax.ppermute(value, 'ctx', [pair for pair in pairs if keep is None or kee...]
    slice x2 -> x0, local copies, waits for them, and re-layouts: 3.87 us -> none  [the longest x1 1.94 us: spread_rows(): near[ROW][0][:half]]
    ppermute x22 -> x30, starting transfers between devices: 27 us -> 30.2 us  [swap(): lax.ppermute(value, 'ctx', [pair for pair in pairs if keep is None or kee...]
    pallas_call x7 -> x11, Pallas kernels: 34.2 us -> 33.7 us  [the longest x4 18.3 us: expert_pieces(): pl.pallas_call(functools.partial(expert_kernel, tuple(masks), chunk), gri...]
  transfers between devices with their start and end apart: 26 -> 35, of which waited for: 18 -> 19; matrix products, arithmetic and copies ran while one was open for 3% -> 1% of each run, Pallas kernels for 5% -> 9%
where the time goes in v3:
time: 284 us; the launch traced here: 283 us
  waiting for transfers between devices  136 us (48%)
  Pallas kernels  34.9 us (12%)
  starting transfers between devices  32.7 us (12%)
  blocking collectives  32.7 us (12%)
  local copies, waits for them, and re-layouts  29 us (10%)
  between operations  14.2 us (5%)
  other arithmetic  3.69 us (1%)
    ppermute x30, waiting for transfers between devices, swap(): lax.ppermute(value, 'ctx', [pair for pair in pairs if keep is None or kee...  89.6 us
    all_gather x2, blocking collectives, body(): own.append(lax.all_gather(normed, 'head', tiled=True))  32.7 us
    ppermute x30, starting transfers between devices, swap(): lax.ppermute(value, 'ctx', [pair for pair in pairs if keep is None or kee...  30.2 us
    unnamed x78, local copies, waits for them, and re-layouts  29 us
    reduce_scatter x2, waiting for transfers between devices, body(): lax.psum_scatter(part, 'head', scatter_dimension=0, tiled=True)  24.4 us
    reduce_scatter x2, waiting for transfers between devices, body(): moe.append(lax.psum_scatter(total, 'head', scatter_dimension=0, tiled=True))  21.3 us
    pallas_call x4, Pallas kernels, expert_pieces(): pl.pallas_call(functools.partial(expert_kernel, tuple(masks), chunk), gri...  18.3 us
  transfers between devices with their start and end apart: 35, of which 19 were waited for; matrix products, arithmetic and copies ran while one was open for 1% of the time, Pallas kernels for 9%

profile of v3, /device:TPU:0, one launch (start us, length us, event | category | flops | bytes accessed | tf_op | source)
XLA Modules:
  0.0 283.3 jit_solution(5226789721156580214)
XLA Ops:
  7.2 1.2 copy-done
  8.4 2.8 copy-done.4
  11.9 3.1 %qkv_projection.1 = (bf16[3,256,512]{2,1,0:T(8,128)(2,1)S(1)}, bf16[3,16,512]{2,1,0:T(8,128)(2,1)S(1)}) custom-call(bf16[256,2048]{1,0:T(8,128)(2,1)S(1)} %copy-done, f32[1,2048]{1,0:T(1,128)S(1)} %bitcast.46, bf16[3,2048,512]{2,1,0:T(8,128)(2,1)S(1)} %bitcast.35), custom_call_target="tpu_custom_call" | custom-call | tf_op jit(solution)/shard_map/qkv_projection/pallas_call | solution.py:58
  15.0 2.4 collective-permute-start
  17.4 0.9 collective-permute-done.rim_ref
  18.3 2.1 conv_states.1
  20.4 7.0 %collective-permute-start.1 = (bf16[576,128]{1,0:T(8,128)(2,1)S(1)}, bf16[576,128]{1,0:T(8,128)(2,1)S(1)}, u32[]{:S(2)}, u32[]{:S(2)}) collective-permute-start(bf16[576,128]{1,0:T(8,128)(2,1)S(1)} %get-tuple-element.31), channel_id=1, source_target_pairs={{0,8},{4,12},{16,24},{20,28},{1,9},{5,13},{17,25},{21,29},{2,10},{... | collective-permute-start | bytes 442376 | tf_op jit(solution)/shard_map/ppermute | solution.py:390
  27.5 3.4 %collective-permute-start.2 = (bf16[576,128]{1,0:T(8,128)(2,1)S(1)}, bf16[576,128]{1,0:T(8,128)(2,1)S(1)}, u32[]{:S(2)}, u32[]{:S(2)}) collective-permute-start(bf16[576,128]{1,0:T(8,128)(2,1)S(1)} %get-tuple-element.31), channel_id=1, source_target_pairs={{0,16},{4,20},{8,24},{12,28},{1,17},{5,21},{9,25},{13,29},{2,18},{... | collective-permute-start | bytes 442376 | tf_op jit(solution)/shard_map/ppermute | solution.py:390
  30.9 1.3 collective-permute-start.3
  32.2 1.6 collective-permute-done.2
  33.8 1.1 collective-permute-done.3
  35.1 1.9 collective-permute-done.4.far_ref.fwd_far
  37.0 1.6 copy-done.7
  38.6 3.8 %core_out.1 = (bf16[128,2048]{1,0:T(8,128)(2,1)S(1)}, bf16[128,2048]{1,0:T(8,128)(2,1)S(1)}) custom-call(s32[2]{0:T(128)S(1)} %pad_add_fusion.me_ref, bf16[3,256,512]{2,1,0:T(8,128)(2,1)S(1)} %get-tuple-element.30.qkv_ref, f32[4,256]{1,0:T(4,128)S(1)} %bitcast.39, f32[1,512]{1,0:T(1,128)S(1)} %bitcast.47, ...), custom_call_target="tpu_custom_call" | custom-call | tf_op jit(solution)/shard_map/core_out/pallas_call | solution.py:212
  43.2 0.8 copy-done.17
  44.1 24.4 %reduce-scatter.9.cloned.1.call-done.attn_ref = bf16[32,2048]{1,0:T(8,128)(2,1)} async-done(((bf16[128,2048]{1,0:T(8,128)(2,1)}), bf16[32,2048]{1,0:T(8,128)(2,1)}) %reduce-scatter.9.cloned.1.call-update) | async-done | bytes 131088 | tf_op jit(solution)/shard_map/reduce_scatter | solution.py:533
  68.5 0.9 copy-done.14
  69.6 16.6 %all_gather.7.refs_0_ = bf16[128,2048]{1,0:T(8,128)(2,1)} all-gather(bf16[32,2048]{1,0:T(8,128)(2,1)S(1)} %moe_norm.3), channel_id=1, replica_groups=mesh['ctx'=8,'head'=4] {'head'}, dimensions={0}, use_global_device_ids=true | all-gather | bytes 655360 | tf_op jit(solution)/shard_map/all_gather | solution.py:542
  86.2 1.3 collective-permute-start.20
  87.5 1.7 collective-permute-start.5
  89.8 1.3 collective-permute-start.7
  91.1 1.7 collective-permute-start.21
  92.8 7.9 %collective-permute-done.20.refs_1_ = bf16[128,2048]{1,0:T(8,128)(2,1)} collective-permute-done((bf16[128,2048]{1,0:T(8,128)(2,1)}, bf16[128,2048]{1,0:T(8,128)(2,1)}, u32[]{:S(2)}, u32[]{:S(2)}) %collective-permute-start.20) | collective-permute-done | bytes 524320 | tf_op jit(solution)/shard_map/ppermute | solution.py:390
  100.6 1.4 collective-permute-start.22
  103.1 6.6 %collective-permute-done.21.refs_2_ = bf16[128,2048]{1,0:T(8,128)(2,1)} collective-permute-done((bf16[128,2048]{1,0:T(8,128)(2,1)}, bf16[128,2048]{1,0:T(8,128)(2,1)}, u32[]{:S(2)}, u32[]{:S(2)}) %collective-permute-start.21) | collective-permute-done | bytes 524320 | tf_op jit(solution)/shard_map/ppermute | solution.py:390
  109.8 5.6 %collective-permute-done.22.refs_3_ = bf16[128,2048]{1,0:T(8,128)(2,1)} collective-permute-done((bf16[128,2048]{1,0:T(8,128)(2,1)}, bf16[128,2048]{1,0:T(8,128)(2,1)}, u32[]{:S(2)}, u32[]{:S(2)}) %collective-permute-start.22) | collective-permute-done | bytes 524320 | tf_op jit(solution)/shard_map/ppermute | solution.py:390
  115.4 1.6 copy-done.8
  117.0 1.6 copy-done.9
  118.6 1.6 copy-done.10
  120.2 5.4 %core_grads.1 = (bf16[256,512]{1,0:T(8,128)(2,1)}, bf16[256,512]{1,0:T(8,128)(2,1)}, bf16[256,512]{1,0:T(8,128)(2,1)}, f32[8,256,128]{2,1,0:T(8,128)S(1)}, bf16[...) custom-call(s32[2]{0:T(128)S(1)} %pad_add_fusion.me_ref, ...), custom_call_target="tpu_custom_call" | custom-call | tf_op jit(solution)/shard_map/core_grads/pallas_call | solution.py:282
  125.5 1.4 copy-done.27
  126.9 1.4 copy-done.30
  128.3 1.3 copy-done.33
  129.6 1.0 copy-done.36
  130.6 0.9 copy-done.12
  131.6 16.1 %all_gather.6.refs_0_ = bf16[128,2048]{1,0:T(8,128)(2,1)S(1)} all-gather(bf16[32,2048]{1,0:T(8,128)(2,1)S(1)} %moe_norm.2), channel_id=1, replica_groups=mesh['ctx'=8,'head'=4] {'head'}, dimensions={0}, use_global_device_ids=true | all-gather | bytes 655360 | tf_op jit(solution)/shard_map/all_gather | solution.py:542
  147.7 0.9 collective-permute-start.9
  148.7 1.6 copy-done.28
  150.2 1.6 copy-done.31
  151.8 1.6 copy-done.34
  153.4 1.2 copy-done.37
  154.7 5.2 %expert_pieces.7 = bf16[4,128,2048]{2,1,0:T(8,128)(2,1)S(1)} custom-call(bf16[1,2048,512]{2,1,0:T(8,128)(2,1)S(1)} %copy-done.28, bf16[1,2048,512]{2,1,0:T(8,128)(2,1)S(1)} %copy-done.31, bf16[1,512,2048]{2,1,0:T(8,128)(2,1)S(1)} %copy-done.34, f32[8,256,128]{2,1,0:T(8,128)S(1)} %copy-done.37, bf16[128,2048]{1,0:T(8,128)(2,1)} %collective-permute-done.23.refs_0_, ...), custom_call_target="tpu_custom_call" | custom-call | flops 3221225472 | bytes 4194304 | tf_op jit(solution)/shard_map/expert_pieces/pallas_call | solution.py:366
  160.7 1.3 collective-permute-start.11
  162.5 12.2 %collective-permute-done.10.refs_2_ = bf16[128,2048]{1,0:T(8,128)(2,1)S(1)} collective-permute-done((bf16[128,2048]{1,0:T(8,128)(2,1)S(1)}, bf16[128,2048]{1,0:T(8,128)(2,1)S(1)}, u32[]{:S(2)}, u32[]{:S(2)}) %collective-permute-start.10) | collective-permute-done | bytes 524320 | tf_op jit(solution)/shard_map/ppermute | solution.py:390
  174.7 10.8 %collective-permute-done.11.refs_3_ = bf16[128,2048]{1,0:T(8,128)(2,1)S(1)} collective-permute-done((bf16[128,2048]{1,0:T(8,128)(2,1)S(1)}, bf16[128,2048]{1,0:T(8,128)(2,1)S(1)}, u32[]{:S(2)}, u32[]{:S(2)}) %collective-permute-start.11) | collective-permute-done | bytes 524320 | tf_op jit(solution)/shard_map/ppermute | solution.py:390
  185.5 1.9 collective-permute-done.15.refs_3_
  187.4 4.0 %expert_pieces.5 = bf16[4,128,2048]{2,1,0:T(8,128)(2,1)S(1)} custom-call(bf16[1,2048,512]{2,1,0:T(8,128)(2,1)S(1)} %copy-done.29, bf16[1,2048,512]{2,1,0:T(8,128)(2,1)S(1)} %copy-done.31, bf16[1,512,2048]{2,1,0:T(8,128)(2,1)S(1)} %copy-done.34, f32[8,256,128]{2,1,0:T(8,128)S(1)} %copy-done.38, bf16[128,2048]{1,0:T(8,128)(2,1)S(1)} %collective-permute-done.12.refs_0_, ...), custom_call_target="tpu_custom_call" | custom-call | flops 3221225472 | bytes 4194304 | tf_op jit(solution)/shard_map/expert_pieces/pallas_call | solution.py:366
  191.6 5.1 %expert_pieces.6.near_ref = bf16[4,128,2048]{2,1,0:T(8,128)(2,1)S(1)} custom-call(bf16[1,2048,512]{2,1,0:T(8,128)(2,1)S(1)} %copy-done.29, bf16[1,2048,512]{2,1,0:T(8,128)(2,1)S(1)} %copy-done.32, bf16[1,512,2048]{2,1,0:T(8,128)(2,1)S(1)} %copy-done.34, f32[8,256,128]{2,1,0:T(8,128)S(1)} %copy-done.38, bf16[128,2048]{1,0:T(8,128)(2,1)} %all_gather.7.refs_0_, ...), custom_call_target="tpu_custom_call" | custom-call | flops 3221225472 | bytes 4194304 | tf_op jit(solution)/shard_map/expert_pieces/pallas_call | solution.py:366
  197.2 1.2 collective-permute-start.28
  198.3 4.0 %expert_pieces.4.near_ref = bf16[4,128,2048]{2,1,0:T(8,128)(2,1)S(1)} custom-call(bf16[1,2048,512]{2,1,0:T(8,128)(2,1)S(1)} %copy-done.29, bf16[1,2048,512]{2,1,0:T(8,128)(2,1)S(1)} %copy-done.32, bf16[1,512,2048]{2,1,0:T(8,128)(2,1)S(1)} %copy-done.35, f32[8,256,128]{2,1,0:T(8,128)S(1)} %copy-done.38, bf16[128,2048]{1,0:T(8,128)(2,1)S(1)} %all_gather.6.refs_0_, ...), custom_call_target="tpu_custom_call" | custom-call | flops 3221225472 | bytes 4194304 | tf_op jit(solution)/shard_map/expert_pieces/pallas_call | solution.py:366
  202.4 9.0 %collective-permute-done.28 = bf16[128,2048]{1,0:T(8,128)(2,1)S(1)} collective-permute-done((bf16[128,2048]{1,0:T(8,128)(2,1)S(1)}, bf16[128,2048]{1,0:T(8,128)(2,1)S(1)}, u32[]{:S(2)}, u32[]{:S(2)}) %collective-permute-start.28) | collective-permute-done | bytes 524320 | tf_op jit(solution)/shard_map/ppermute | solution.py:390
  212.3 1.1 collective-permute-start.30
  213.4 1.4 fusion.3
  214.8 1.5 collective-permute-start.17
  216.3 10.3 %collective-permute-done.29.refs_0_ = bf16[128,2048]{1,0:T(8,128)(2,1)S(1)} collective-permute-done((bf16[128,2048]{1,0:T(8,128)(2,1)S(1)}, bf16[128,2048]{1,0:T(8,128)(2,1)S(1)}, u32[]{:S(2)}, u32[]{:S(2)}) %collective-permute-start.29) | collective-permute-done | bytes 524320 | tf_op jit(solution)/shard_map/ppermute | solution.py:390
  227.2 0.8 copy-done.5
  228.1 8.3 %collective-permute-done.17 = bf16[128,2048]{1,0:T(8,128)(2,1)} collective-permute-done((bf16[128,2048]{1,0:T(8,128)(2,1)}, bf16[128,2048]{1,0:T(8,128)(2,1)}, u32[]{:S(2)}, u32[]{:S(2)}) %collective-permute-start.17) | collective-permute-done | bytes 524320 | tf_op jit(solution)/shard_map/ppermute | solution.py:390
  236.4 1.4 fusion.1
  237.9 1.2 collective-permute-start.18
  239.6 10.8 %collective-permute-done.18.refs_0_ = bf16[128,2048]{1,0:T(8,128)(2,1)S(1)} collective-permute-done((bf16[128,2048]{1,0:T(8,128)(2,1)S(1)}, bf16[128,2048]{1,0:T(8,128)(2,1)S(1)}, u32[]{:S(2)}, u32[]{:S(2)}) %collective-permute-start.18) | collective-permute-done | bytes 524320 | tf_op jit(solution)/shard_map/ppermute | solution.py:390
  250.4 1.0 collective-permute-done.19.refs_1_
  252.9 21.3 %reduce-scatter.7.cloned.1.call-done.refs_0_ = bf16[1,128,512]{2,1,0:T(8,128)(2,1)} async-done(((bf16[4,128,512]{2,1,0:T(8,128)(2,1)}), bf16[1,128,512]{2,1,0:T(8,128)(2,1)}) %reduce-scatter.7.cloned.1.call-update) | async-done | bytes 131088 | tf_op jit(solution)/shard_map/reduce_scatter | solution.py:553
  274.2 0.9 copy-done.18
  275.1 0.9 copy-done.19
  (110 shorter events, 10.2 us)
Async XLA Ops:
  7.2 61.3 %reduce-scatter.9.cloned.1.call-start = ((), (), s32[]{:S(2)}) async-start(), calls=%async_computation.6 | async-start | bytes 655360 | tf_op jit(solution)/shard_map/reduce_scatter | solution.py:533
  7.2 1.2 copy-start
  8.4 2.8 copy-start.4
  11.9 6.3 %copy-start.11 = (bf16[256,512]{1,0:T(8,128)(2,1)S(1)}, bf16[256,512]{1,0:T(8,128)(2,1)}, u32[]{:S(2)}) copy-start(bf16[256,512]{1,0:T(8,128)(2,1)} %cot_ref.3) | copy-start | bytes 786436
  11.9 6.3 %copy-start.20 = (f32[256,4]{0,1:T(4,128)S(1)}, f32[256,4]{0,1:T(4,128)}, u32[]{:S(2)}) copy-start(f32[256,4]{0,1:T(4,128)} %param.18) | copy-start | bytes 12292
  11.9 6.3 %copy-start.22 = (f32[4,3,512]{2,0,1:T(4,128)S(1)}, f32[4,3,512]{2,0,1:T(4,128)}, u32[]{:S(2)}) copy-start(f32[4,3,512]{2,0,1:T(4,128)} %param.17) | copy-start | bytes 73732
  11.9 6.3 %copy-start.23 = (s32[256,8]{0,1:T(8,128)S(1)}, s32[256,8]{0,1:T(8,128)}, u32[]{:S(2)}) copy-start(s32[256,8]{0,1:T(8,128)} %param.22) | copy-start | bytes 24580
  11.9 6.3 %copy-start.24 = (f32[256,8]{0,1:T(8,128)S(1)}, f32[256,8]{0,1:T(8,128)}, u32[]{:S(2)}) copy-start(f32[256,8]{0,1:T(8,128)} %param.23) | copy-start | bytes 24580
  15.0 22.0 %copy-start.26 = (f32[512]{0:T(512)S(1)}, f32[512]{0:T(512)}, u32[]{:S(2)}) copy-start(f32[512]{0:T(512)} %param.19) | copy-start | bytes 6148
  15.0 3.2 %collective-permute-start = (bf16[3,16,512]{2,1,0:T(8,128)(2,1)S(1)}, bf16[3,16,512]{2,1,0:T(8,128)(2,1)S(1)}, u32[]{:S(2)}, u32[]{:S(2)}) collective-permute-start(bf16[3,16,512]{2,1,0:T(8,128)(2,1)S(1)} %get-tuple-element.28), channel_id=1, source_target_pairs={{0,4},{4,8},{8,12},{12,16},{16,20},{20,24},{24,28},{1,5},{5,9},{9,... | collective-permute-start | bytes 147464 | tf_op jit(solution)/shard_map/ppermute | solution.py:526
  20.4 11.8 %collective-permute-start.1 = (bf16[576,128]{1,0:T(8,128)(2,1)S(1)}, bf16[576,128]{1,0:T(8,128)(2,1)S(1)}, u32[]{:S(2)}, u32[]{:S(2)}) collective-permute-start(bf16[576,128]{1,0:T(8,128)(2,1)S(1)} %get-tuple-element.31), channel_id=1, source_target_pairs={{0,8},{4,12},{16,24},{20,28},{1,9},{5,13},{17,25},{21,29},{2,10},{... | collective-permute-start | bytes 442376 | tf_op jit(solution)/shard_map/ppermute | solution.py:390
  27.5 6.3 %collective-permute-start.2 = (bf16[576,128]{1,0:T(8,128)(2,1)S(1)}, bf16[576,128]{1,0:T(8,128)(2,1)S(1)}, u32[]{:S(2)}, u32[]{:S(2)}) collective-permute-start(bf16[576,128]{1,0:T(8,128)(2,1)S(1)} %get-tuple-element.31), channel_id=1, source_target_pairs={{0,16},{4,20},{8,24},{12,28},{1,17},{5,21},{9,25},{13,29},{2,18},{... | collective-permute-start | bytes 442376 | tf_op jit(solution)/shard_map/ppermute | solution.py:390
  30.9 4.0 %collective-permute-start.3 = (bf16[576,128]{1,0:T(8,128)(2,1)S(1)}, bf16[576,128]{1,0:T(8,128)(2,1)S(1)}, u32[]{:S(2)}, u32[]{:S(2)}) collective-permute-start(bf16[576,128]{1,0:T(8,128)(2,1)S(1)} %get-tuple-element.31), channel_id=1, source_target_pairs={{0,24},{4,28},{8,16},{12,20},{1,25},{5,29},{9,17},{13,21},{2,26},{... | collective-permute-start | bytes 442376 | tf_op jit(solution)/shard_map/ppermute | solution.py:390
  34.9 2.1 collective-permute-start.4
  37.0 1.6 copy-start.7
  38.6 29.9 %copy-start.1 = (bf16[256,2048]{1,0:T(8,128)(2,1)S(1)}, bf16[256,2048]{1,0:T(8,128)(2,1)}, u32[]{:S(2)}) copy-start(bf16[256,2048]{1,0:T(8,128)(2,1)} %x_ref.5) | copy-start | bytes 3145732
  38.6 29.9 %copy-start.21 = (f32[2048]{0:T(1024)S(1)}, f32[2048]{0:T(1024)}, u32[]{:S(2)}) copy-start(f32[2048]{0:T(1024)} %param.21) | copy-start | bytes 24580
  44.0 86.5 %reduce-scatter.5.cloned.1.call-start = ((), (), s32[]{:S(2)}) async-start(), calls=%async_computation.4 | async-start | bytes 655360 | tf_op jit(solution)/shard_map/reduce_scatter | solution.py:533
  86.2 14.5 %collective-permute-start.20 = (bf16[128,2048]{1,0:T(8,128)(2,1)}, bf16[128,2048]{1,0:T(8,128)(2,1)}, u32[]{:S(2)}, u32[]{:S(2)}) collective-permute-start(bf16[128,2048]{1,0:T(8,128)(2,1)} %all_gather.7.refs_0_), channel_id=1, source_target_pairs={{0,16},{4,20},{8,24},{12,28},{16,0},{20,4},{24,8},{28,12},{1,17},{... | collective-permute-start | bytes 1572872 | tf_op jit(solution)/shard_map/ppermute | solution.py:390
  87.5 165.4 %reduce-scatter.11.cloned.1.call-start = ((), (), s32[]{:S(2)}) async-start(), calls=%async_computation.7 | async-start | bytes 655360 | tf_op jit(solution)/shard_map/reduce_scatter | solution.py:553
  87.5 14.5 %collective-permute-start.5 = (bf16[672,128]{1,0:T(8,128)(2,1)S(1)}, bf16[672,128]{1,0:T(8,128)(2,1)S(1)}, u32[]{:S(2)}, u32[]{:S(2)}) collective-permute-start(bf16[672,128]{1,0:T(8,128)(2,1)S(1)} %get-tuple-element.35), channel_id=1, source_target_pairs={{0,8},{4,12},{8,0},{12,4},{16,24},{20,28},{24,16},{28,20},{1,9},{5... | collective-permute-start | bytes 516104 | tf_op jit(solution)/shard_map/ppermute | solution.py:390
  89.3 13.1 %collective-permute-start.6 = (bf16[672,128]{1,0:T(8,128)(2,1)S(1)}, bf16[672,128]{1,0:T(8,128)(2,1)S(1)}, u32[]{:S(2)}, u32[]{:S(2)}) collective-permute-start(bf16[672,128]{1,0:T(8,128)(2,1)S(1)} %get-tuple-element.35), channel_id=1, source_target_pairs={{0,16},{4,20},{8,24},{12,28},{16,0},{20,4},{24,8},{28,12},{1,17},{... | collective-permute-start | bytes 516104 | tf_op jit(solution)/shard_map/ppermute | solution.py:390
  89.8 12.5 %collective-permute-start.7 = (bf16[672,128]{1,0:T(8,128)(2,1)S(1)}, bf16[672,128]{1,0:T(8,128)(2,1)S(1)}, u32[]{:S(2)}, u32[]{:S(2)}) collective-permute-start(bf16[672,128]{1,0:T(8,128)(2,1)S(1)} %get-tuple-element.35), channel_id=1, source_target_pairs={{0,24},{4,28},{8,16},{12,20},{16,8},{20,12},{24,0},{28,4},{1,25},{... | collective-permute-start | bytes 516104 | tf_op jit(solution)/shard_map/ppermute | solution.py:390
  91.1 18.7 %collective-permute-start.21 = (bf16[128,2048]{1,0:T(8,128)(2,1)}, bf16[128,2048]{1,0:T(8,128)(2,1)}, u32[]{:S(2)}, u32[]{:S(2)}) collective-permute-start(bf16[128,2048]{1,0:T(8,128)(2,1)} %all_gather.7.refs_0_), channel_id=1, source_target_pairs={{0,8},{4,12},{8,0},{12,4},{16,24},{20,28},{24,16},{28,20},{1,9},{5... | collective-permute-start | bytes 1572872 | tf_op jit(solution)/shard_map/ppermute | solution.py:390
  100.6 14.7 %collective-permute-start.22 = (bf16[128,2048]{1,0:T(8,128)(2,1)}, bf16[128,2048]{1,0:T(8,128)(2,1)}, u32[]{:S(2)}, u32[]{:S(2)}) collective-permute-start(bf16[128,2048]{1,0:T(8,128)(2,1)} %collective-permute-done.20.refs_1_), channel_id=1, source_target_pairs={{0,8},{4,12},{8,0},{12,4},{16,24},{20,28},{24,16},{28,20},{1,9},{5... | collective-permute-start | bytes 1572872 | tf_op jit(solution)/shard_map/ppermute | solution.py:390
  102.5 12.9 %collective-permute-start.8 = (bf16[4,672,128]{2,1,0:T(8,128)(2,1)S(1)}, bf16[4,672,128]{2,1,0:T(8,128)(2,1)S(1)}, u32[]{:S(2)}, u32[]{:S(2)}) collective-permute-start(bf16[4,672,128]{2,1,0:T(8,128)(2,1)S(1)} %pad_maximum_fusion.bwd_near), channel_id=1, source_target_pairs={{0,4},{4,0},{8,12},{12,8},{16,20},{20,16},{24,28},{28,24},{1,5},{5... | collective-permute-start | bytes 2064392 | tf_op jit(solution)/shard_map/ppermute | solution.py:390
  102.5 46.1 %collective-permute-start.23 = (bf16[128,2048]{1,0:T(8,128)(2,1)}, bf16[128,2048]{1,0:T(8,128)(2,1)}, u32[]{:S(2)}, u32[]{:S(2)}) collective-permute-start(bf16[128,2048]{1,0:T(8,128)(2,1)} %all_gather.7.refs_0_), channel_id=1, source_target_pairs={{0,4},{4,0},{8,12},{12,8},{16,20},{20,16},{24,28},{28,24},{1,5},{5... | collective-permute-start | bytes 1572872 | tf_op jit(solution)/shard_map/ppermute | solution.py:390
  103.0 45.6 %collective-permute-start.24 = (bf16[128,2048]{1,0:T(8,128)(2,1)}, bf16[128,2048]{1,0:T(8,128)(2,1)}, u32[]{:S(2)}, u32[]{:S(2)}) collective-permute-start(bf16[128,2048]{1,0:T(8,128)(2,1)} %collective-permute-done.20.refs_1_), channel_id=1, source_target_pairs={{0,4},{4,0},{8,12},{12,8},{16,20},{20,16},{24,28},{28,24},{1,5},{5... | collective-permute-start | bytes 1572872 | tf_op jit(solution)/shard_map/ppermute | solution.py:390
  109.8 38.9 %collective-permute-start.25 = (bf16[128,2048]{1,0:T(8,128)(2,1)}, bf16[128,2048]{1,0:T(8,128)(2,1)}, u32[]{:S(2)}, u32[]{:S(2)}) collective-permute-start(bf16[128,2048]{1,0:T(8,128)(2,1)} %collective-permute-done.21.refs_2_), channel_id=1, source_target_pairs={{0,4},{4,0},{8,12},{12,8},{16,20},{20,16},{24,28},{28,24},{1,5},{5... | collective-permute-start | bytes 1572872 | tf_op jit(solution)/shard_map/ppermute | solution.py:390
  115.4 33.3 %collective-permute-start.26 = (bf16[128,2048]{1,0:T(8,128)(2,1)}, bf16[128,2048]{1,0:T(8,128)(2,1)}, u32[]{:S(2)}, u32[]{:S(2)}) collective-permute-start(bf16[128,2048]{1,0:T(8,128)(2,1)} %collective-permute-done.22.refs_3_), channel_id=1, source_target_pairs={{0,4},{4,0},{8,12},{12,8},{16,20},{20,16},{24,28},{28,24},{1,5},{5... | collective-permute-start | bytes 1572872 | tf_op jit(solution)/shard_map/ppermute | solution.py:390
  115.4 1.6 copy-start.8
  117.0 1.6 copy-start.9
  118.6 1.6 copy-start.10
  125.5 1.4 copy-start.27
  126.9 1.4 copy-start.30
  128.3 1.3 copy-start.33
  147.7 13.0 %collective-permute-start.9 = (bf16[128,2048]{1,0:T(8,128)(2,1)S(1)}, bf16[128,2048]{1,0:T(8,128)(2,1)S(1)}, u32[]{:S(2)}, u32[]{:S(2)}) collective-permute-start(bf16[128,2048]{1,0:T(8,128)(2,1)S(1)} %all_gather.6.refs_0_), channel_id=1, source_target_pairs={{0,8},{4,12},{8,0},{12,4},{16,24},{20,28},{24,16},{28,20},{1,9},{5... | collective-permute-start | bytes 1572872 | tf_op jit(solution)/shard_map/ppermute | solution.py:390
  148.6 1.6 copy-start.28
  150.2 1.6 copy-start.31
  151.8 1.6 copy-start.34
  153.4 1.2 copy-start.37
  154.6 32.8 %copy-start.29 = (bf16[1,2048,512]{2,1,0:T(8,128)(2,1)S(1)}, bf16[1,2048,512]{2,1,0:T(8,128)(2,1)}, u32[]{:S(2)}) copy-start(bf16[1,2048,512]{2,1,0:T(8,128)(2,1)} %copy-done.27) | copy-start | bytes 6291460
  154.7 32.8 %copy-start.38 = (f32[8,256,128]{2,1,0:T(8,128)S(1)}, f32[8,256,128]{2,1,0:T(8,128)}, u32[]{:S(2)}) copy-start(f32[8,256,128]{2,1,0:T(8,128)} %copy-done.36) | copy-start | bytes 3145732
  159.8 31.8 %copy-start.32 = (bf16[1,2048,512]{2,1,0:T(8,128)(2,1)S(1)}, bf16[1,2048,512]{2,1,0:T(8,128)(2,1)}, u32[]{:S(2)}) copy-start(bf16[1,2048,512]{2,1,0:T(8,128)(2,1)} %copy-done.30) | copy-start | bytes 6291460
  159.8 36.9 %collective-permute-start.27 = (bf16[4,128,2048]{2,1,0:T(8,128)(2,1)S(1)}, bf16[4,128,2048]{2,1,0:T(8,128)(2,1)S(1)}, u32[]{:S(2)}, u32[]{:S(2)}) collective-permute-start(bf16[4,128,2048]{2,1,0:T(8,128)(2,1)S(1)} %expert_pieces.7), channel_id=1, source_target_pairs={{0,4},{4,0},{8,12},{12,8},{16,20},{20,16},{24,28},{28,24},{1,5},{5... | collective-permute-start | bytes 6291464 | tf_op jit(solution)/shard_map/ppermute | solution.py:390
  159.9 14.8 %collective-permute-start.10 = (bf16[128,2048]{1,0:T(8,128)(2,1)S(1)}, bf16[128,2048]{1,0:T(8,128)(2,1)S(1)}, u32[]{:S(2)}, u32[]{:S(2)}) collective-permute-start(bf16[128,2048]{1,0:T(8,128)(2,1)S(1)} %all_gather.6.refs_0_), channel_id=1, source_target_pairs={{0,16},{4,20},{8,24},{12,28},{16,0},{20,4},{24,8},{28,12},{1,17},{... | collective-permute-start | bytes 1572872 | tf_op jit(solution)/shard_map/ppermute | solution.py:390
  160.7 24.8 %collective-permute-start.11 = (bf16[128,2048]{1,0:T(8,128)(2,1)S(1)}, bf16[128,2048]{1,0:T(8,128)(2,1)S(1)}, u32[]{:S(2)}, u32[]{:S(2)}) collective-permute-start(bf16[128,2048]{1,0:T(8,128)(2,1)S(1)} %collective-permute-done.9.refs_1_), channel_id=1, source_target_pairs={{0,16},{4,20},{8,24},{12,28},{16,0},{20,4},{24,8},{28,12},{1,17},{... | collective-permute-start | bytes 1572872 | tf_op jit(solution)/shard_map/ppermute | solution.py:390
  162.0 23.5 %collective-permute-start.12 = (bf16[128,2048]{1,0:T(8,128)(2,1)S(1)}, bf16[128,2048]{1,0:T(8,128)(2,1)S(1)}, u32[]{:S(2)}, u32[]{:S(2)}) collective-permute-start(bf16[128,2048]{1,0:T(8,128)(2,1)S(1)} %all_gather.6.refs_0_), channel_id=1, source_target_pairs={{0,4},{4,0},{8,12},{12,8},{16,20},{20,16},{24,28},{28,24},{1,5},{5... | collective-permute-start | bytes 1572872 | tf_op jit(solution)/shard_map/ppermute | solution.py:390
  162.0 23.5 %collective-permute-start.13 = (bf16[128,2048]{1,0:T(8,128)(2,1)S(1)}, bf16[128,2048]{1,0:T(8,128)(2,1)S(1)}, u32[]{:S(2)}, u32[]{:S(2)}) collective-permute-start(bf16[128,2048]{1,0:T(8,128)(2,1)S(1)} %collective-permute-done.9.refs_1_), channel_id=1, source_target_pairs={{0,4},{4,0},{8,12},{12,8},{16,20},{20,16},{24,28},{28,24},{1,5},{5... | collective-permute-start | bytes 1572872 | tf_op jit(solution)/shard_map/ppermute | solution.py:390
  174.7 10.8 %collective-permute-start.14 = (bf16[128,2048]{1,0:T(8,128)(2,1)S(1)}, bf16[128,2048]{1,0:T(8,128)(2,1)S(1)}, u32[]{:S(2)}, u32[]{:S(2)}) collective-permute-start(bf16[128,2048]{1,0:T(8,128)(2,1)S(1)} %collective-permute-done.10.refs_2_), channel_id=1, source_target_pairs={{0,4},{4,0},{8,12},{12,8},{16,20},{20,16},{24,28},{28,24},{1,5},{5... | collective-permute-start | bytes 1572872 | tf_op jit(solution)/shard_map/ppermute | solution.py:390
  185.5 1.9 collective-permute-start.15
  191.4 22.0 %collective-permute-start.16 = (bf16[4,128,2048]{2,1,0:T(8,128)(2,1)S(1)}, bf16[4,128,2048]{2,1,0:T(8,128)(2,1)S(1)}, u32[]{:S(2)}, u32[]{:S(2)}) collective-permute-start(bf16[4,128,2048]{2,1,0:T(8,128)(2,1)S(1)} %expert_pieces.5), channel_id=1, source_target_pairs={{0,4},{4,0},{8,12},{12,8},{16,20},{20,16},{24,28},{28,24},{1,5},{5... | collective-permute-start | bytes 6291464 | tf_op jit(solution)/shard_map/ppermute | solution.py:390
  196.7 1.6 copy-start.35
  197.2 14.2 %collective-permute-start.28 = (bf16[128,2048]{1,0:T(8,128)(2,1)S(1)}, bf16[128,2048]{1,0:T(8,128)(2,1)S(1)}, u32[]{:S(2)}, u32[]{:S(2)}) collective-permute-start(bf16[128,2048]{1,0:T(8,128)(2,1)S(1)} %get-tuple-element.50), channel_id=1, source_target_pairs={{0,8},{4,12},{8,0},{12,4},{16,24},{20,28},{24,16},{28,20},{1,9},{5... | collective-permute-start | bytes 1572872 | tf_op jit(solution)/shard_map/ppermute | solution.py:390
  202.4 12.4 %copy-start.2 = (bf16[4,128,2048]{2,1,0:T(8,128)(2,1)}, bf16[4,128,2048]{2,1,0:T(8,128)(2,1)S(1)}, u32[]{:S(2)}) copy-start(bf16[4,128,2048]{2,1,0:T(8,128)(2,1)S(1)} %expert_pieces.4.near_ref) | copy-start | bytes 6291460
  211.6 14.9 %copy-start.15 = (bf16[32,2048]{1,0:T(8,128)(2,1)S(1)}, bf16[32,2048]{1,0:T(8,128)(2,1)}, u32[]{:S(2)}) copy-start(bf16[32,2048]{1,0:T(8,128)(2,1)} %reduce-scatter.9.cloned.1.call-done.attn_ref) | copy-start | bytes 393220
  211.7 14.9 %collective-permute-start.29 = (bf16[128,2048]{1,0:T(8,128)(2,1)S(1)}, bf16[128,2048]{1,0:T(8,128)(2,1)S(1)}, u32[]{:S(2)}, u32[]{:S(2)}) collective-permute-start(bf16[128,2048]{1,0:T(8,128)(2,1)S(1)} %fusion), channel_id=1, source_target_pairs={{0,16},{4,20},{8,24},{12,28},{16,0},{20,4},{24,8},{28,12},{1,17},{... | collective-permute-start | bytes 1572872 | tf_op jit(solution)/shard_map/ppermute | solution.py:390
  212.3 14.3 %collective-permute-start.30 = (bf16[128,2048]{1,0:T(8,128)(2,1)S(1)}, bf16[128,2048]{1,0:T(8,128)(2,1)S(1)}, u32[]{:S(2)}, u32[]{:S(2)}) collective-permute-start(bf16[128,2048]{1,0:T(8,128)(2,1)S(1)} %get-tuple-element.46), channel_id=1, source_target_pairs={{0,8},{4,12},{8,0},{12,4},{16,24},{20,28},{24,16},{28,20},{1,9},{5... | collective-permute-start | bytes 1572872 | tf_op jit(solution)/shard_map/ppermute | solution.py:390
  214.8 21.7 %collective-permute-start.17 = (bf16[128,2048]{1,0:T(8,128)(2,1)}, bf16[128,2048]{1,0:T(8,128)(2,1)}, u32[]{:S(2)}, u32[]{:S(2)}) collective-permute-start(bf16[128,2048]{1,0:T(8,128)(2,1)} %get-tuple-element.52), channel_id=1, source_target_pairs={{0,16},{4,20},{8,24},{12,28},{16,0},{20,4},{24,8},{28,12},{1,17},{... | collective-permute-start | bytes 1572872 | tf_op jit(solution)/shard_map/ppermute | solution.py:390
  228.0 23.4 %copy-start.13 = (bf16[32,2048]{1,0:T(8,128)(2,1)S(1)}, bf16[32,2048]{1,0:T(8,128)(2,1)}, u32[]{:S(2)}) copy-start(bf16[32,2048]{1,0:T(8,128)(2,1)} %reduce-scatter.5.cloned.1.call-done.attn_ref) | copy-start | bytes 393220
  228.0 46.2 %reduce-scatter.7.cloned.1.call-start = ((), (), s32[]{:S(2)}) async-start(), calls=%async_computation.5 | async-start | bytes 655360 | tf_op jit(solution)/shard_map/reduce_scatter | solution.py:553
  228.1 23.4 %copy-start.3 = (bf16[4,128,2048]{2,1,0:T(8,128)(2,1)S(1)}, bf16[4,128,2048]{2,1,0:T(8,128)(2,1)}, u32[]{:S(2)}) copy-start(bf16[4,128,2048]{2,1,0:T(8,128)(2,1)} %copy-done.2) | copy-start | bytes 6291460
  237.9 12.5 %collective-permute-start.18 = (bf16[128,2048]{1,0:T(8,128)(2,1)S(1)}, bf16[128,2048]{1,0:T(8,128)(2,1)S(1)}, u32[]{:S(2)}, u32[]{:S(2)}) collective-permute-start(bf16[128,2048]{1,0:T(8,128)(2,1)S(1)} %fusion.1), channel_id=1, source_target_pairs={{0,8},{4,12},{8,0},{12,4},{16,24},{20,28},{24,16},{28,20},{1,9},{5... | collective-permute-start | bytes 1572872 | tf_op jit(solution)/shard_map/ppermute | solution.py:390
  239.0 12.4 %collective-permute-start.19 = (bf16[128,2048]{1,0:T(8,128)(2,1)}, bf16[128,2048]{1,0:T(8,128)(2,1)S(1)}, u32[]{:S(2)}, u32[]{:S(2)}) collective-permute-start(bf16[128,2048]{1,0:T(8,128)(2,1)} %get-tuple-element.43), channel_id=1, source_target_pairs={{0,16},{4,20},{8,24},{12,28},{16,0},{20,4},{24,8},{28,12},{1,17},{... | collective-permute-start | bytes 1572872 | tf_op jit(solution)/shard_map/ppermute | solution.py:390
  (10 other events, 8.6 us)
Sparse Core Ops, SparseCore 0:
  44.2 24.2 reduce-scatter.8
  87.6 19.0 reduce-scatter.4
  228.1 21.1 reduce-scatter.10
  253.0 21.1 reduce-scatter.6

commit v4 on v3

v4 whole, which is shorter than its diff:
```python
import functools

import jax
import jax.numpy as jnp
from jax import lax
from jax.experimental import pallas as pl
from jax.experimental.pallas import tpu as pltpu
from jax.sharding import PartitionSpec as P

KERNEL = 4
EXP_CTX = 2
LANES = 128
RIM = 16
MIB = 1024 * 1024
HI = lax.Precision.HIGHEST
BF = jnp.bfloat16
F32 = jnp.float32
NT = (((1,), (1,)), ((), ()))
TN = (((0,), (0,)), ((), ()))
NN = (((1,), (0,)), ((), ()))


def params(mib):
    return pltpu.CompilerParams(vmem_limit_bytes=mib * MIB)


def mm(a, b, dims=NN):
    return lax.dot_general(a, b, dims, preferred_element_type=F32)


def pick_block(extent, target):
    return target if extent % target == 0 else extent


def qkv_kernel(x_hbm, gain_ref, w_hbm, mixed_ref, rim_ref, x_ref, w_ref, normed_ref, x_sem, sems):
    kinds, width, chans = w_ref.shape
    load = pltpu.make_async_copy(x_hbm, x_ref, x_sem)
    load.start()
    copies = [pltpu.make_async_copy(w_hbm.at[kind], w_ref.at[kind], sems.at[kind]) for kind in range(kinds)]
    for copy in copies:
        copy.start()
    load.wait()
    values = x_ref[...].astype(F32)
    scale = lax.rsqrt(jnp.mean(values * values, axis=-1, keepdims=True) + 1e-06)
    normed_ref[...] = (values * scale * gain_ref[...]).astype(BF)
    for kind in range(kinds):
        copies[kind].wait()
        out = mm(normed_ref[...], w_ref[kind]).astype(BF)
        mixed_ref[kind] = out
        rim_ref[kind] = out[out.shape[0] - RIM :]


def project(x, gain, weights):
    rows, width = x.shape
    kinds, _, chans = weights.shape
    vmem = pl.BlockSpec(memory_space=pltpu.VMEM)
    hbm = pl.BlockSpec(memory_space=pltpu.HBM)
    return pl.pallas_call(
        qkv_kernel,
        in_specs=[hbm, vmem, hbm],
        out_shape=[
            jax.ShapeDtypeStruct((kinds, rows, chans), BF),
            jax.ShapeDtypeStruct((kinds, RIM, chans), BF),
        ],
        scratch_shapes=[
            pltpu.VMEM((rows, width), BF),
            pltpu.VMEM((kinds, width, chans), BF),
            pltpu.VMEM((rows, width), BF),
            pltpu.SemaphoreType.DMA,
            pltpu.SemaphoreType.DMA((kinds,)),
        ],
        compiler_params=params(61),
        name="qkv_projection",
    )(x, gain.reshape(1, width), weights)


def decay_sums(steps):
    rows = steps.shape[1]
    row_at = lax.broadcasted_iota(jnp.int32, (rows, rows), 0)
    col_at = lax.broadcasted_iota(jnp.int32, (rows, rows), 1)
    lower = row_at >= col_at
    tri = jnp.where(lower, 1.0, 0.0).astype(F32)
    along = lax.dot_general(steps, tri, NT, precision=HI, preferred_element_type=F32)
    down = lax.dot_general(tri, steps, NT, precision=HI, preferred_element_type=F32)
    return along, down, lower


def payload_tail(total, size):
    full = jnp.broadcast_to(total, (RIM, size))
    first = full.astype(BF).astype(F32)
    second = (full - first).astype(BF).astype(F32)
    third = full - first - second
    at = lax.broadcasted_iota(jnp.int32, (RIM, size), 0)
    return jnp.where(at == 0, first, jnp.where(at == 1, second, jnp.where(at == 2, third, 0.0)))


def route_rows(ids_ref, weights_ref, experts):
    top, tok = ids_ref.shape
    expert = lax.broadcasted_iota(jnp.int32, (experts, tok), 0)
    table = jnp.zeros((experts, tok), F32)
    for choice in range(top):
        table += jnp.where(expert == ids_ref[choice : choice + 1, :], weights_ref[choice : choice + 1, :], 0.0)
    first = table.astype(BF).astype(F32)
    second = (table - first).astype(BF).astype(F32)
    return jnp.concatenate([first, second, table - first - second], axis=0)


def conv_kernel(
    experts, mixed_ref, rim_ref, taps_ref, steps_ref, cot_ref, ids_ref, weights_ref, qkv_ref, fwd_ref, bwd_ref, pad_ref
):
    kinds, rows, chans = mixed_ref.shape
    heads = steps_ref.shape[0]
    size = chans // heads
    along, down, _ = decay_sums(steps_ref[...])
    for kind in range(kinds):
        pad_ref[:RIM] = rim_ref[kind].astype(F32)
        pad_ref[RIM:] = mixed_ref[kind].astype(F32)
        total = taps_ref[kind, 0:1, :] * pad_ref[RIM:]
        for offset in range(1, KERNEL):
            total += taps_ref[kind, offset : offset + 1, :] * pad_ref[RIM - offset : RIM - offset + rows]
        activ = total * jax.nn.sigmoid(total)
        if kind == 0:
            activ = activ * size ** (-0.5)
        qkv_ref[kind] = activ.astype(BF)
    routes = rows // LANES * 3 * experts
    table = route_rows(ids_ref, weights_ref, experts).astype(BF)
    for part in range(rows // LANES):
        bwd_ref[part * 3 * experts : (part + 1) * 3 * experts] = table[:, part * LANES : (part + 1) * LANES]
    for head in range(heads):
        at = slice(head * size, (head + 1) * size)
        base = head * (size + RIM)
        last = along[head : head + 1, rows - 1 : rows]
        lead = jnp.exp(down[:, head : head + 1])
        tail = jnp.exp(last - down[:, head : head + 1])
        key_out = (qkv_ref[1, :, at].astype(F32) * tail).astype(BF)
        query_out = (qkv_ref[0, :, at].astype(F32) * lead).astype(BF)
        ends = payload_tail(last, size).astype(BF)
        fwd_ref[base : base + size] = mm(key_out, qkv_ref[2, :, at], TN).astype(BF)
        fwd_ref[base + size : base + size + RIM] = ends
        base += routes
        bwd_ref[base : base + size] = mm(query_out, cot_ref[:, at], TN).astype(BF)
        bwd_ref[base + size : base + size + RIM] = ends


def local_states(mixed, rim, taps, steps, cot, ids, weights, experts):
    kinds, rows, chans = mixed.shape
    heads = steps.shape[0]
    size = chans // heads
    states = heads * (size + RIM)
    return pl.pallas_call(
        functools.partial(conv_kernel, experts),
        out_shape=[
            jax.ShapeDtypeStruct((kinds, rows, chans), BF),
            jax.ShapeDtypeStruct((states, size), BF),
            jax.ShapeDtypeStruct((states + rows // LANES * 3 * experts, size), BF),
        ],
        scratch_shapes=[pltpu.VMEM((rows + RIM, chans), F32)],
        compiler_params=params(12),
        name="conv_states",
    )(mixed, rim, taps, steps, cot, ids, weights)


def arrange(me_ref, near_ref, far_ref, held_ref):
    for at in range(near_ref.shape[0]):
        held_ref[me_ref[0] ^ (2 * at)] = near_ref[at]
        held_ref[me_ref[0] ^ (2 * at + 1)] = far_ref[at]


def entering(held_ref, heads, head, size, first, last, step):
    base = held_ref.shape[1] - (heads - head) * (size + RIM)

    def hop(count, total):
        at = first + count * step
        ends = held_ref[at, base + size : base + size + RIM, :].astype(F32)
        factor = jnp.exp(ends[0:1] + ends[1:2] + ends[2:3])
        return factor * total + held_ref[at, base : base + size, :].astype(F32)

    return lax.fori_loop(0, (last - first) * step, hop, jnp.zeros((size, size), F32))


def core_kernel(parts, me_ref, qkv_ref, steps_ref, gain_ref, near_ref, far_ref, w_hbm, *refs):
    out_refs, (headed_ref, held_ref, w_ref, whole_ref, sem) = refs[:-5], refs[-5:]
    load = pltpu.make_async_copy(w_hbm, w_ref, sem)
    load.start()
    _, rows, chans = qkv_ref.shape
    heads = steps_ref.shape[0]
    size = chans // heads
    arrange(me_ref, near_ref, far_ref, held_ref)
    along, down, lower = decay_sums(steps_ref[...])
    for head in range(heads):
        at = slice(head * size, (head + 1) * size)
        state = entering(held_ref, heads, head, size, 0, me_ref[0], 1).astype(BF)
        diff = down[:, head : head + 1] - along[head : head + 1, :]
        mask = jnp.exp(jnp.where(lower, diff, -jnp.inf))
        query = qkv_ref[0, :, at]
        scores = (mm(query, qkv_ref[1, :, at], NT) * mask).astype(BF)
        attended = mm(scores, qkv_ref[2, :, at])
        attended += mm(query, state) * jnp.exp(down[:, head : head + 1])
        scale = lax.rsqrt(jnp.mean(attended * attended, axis=-1, keepdims=True) + 1e-06)
        headed_ref[:, at] = (attended * scale * gain_ref[:, at]).astype(BF)
    load.wait()
    whole_ref[...] = mm(headed_ref[...], w_ref[...]).astype(BF)
    part = rows // len(out_refs)
    for at, ref in enumerate(out_refs):
        chunk, mask = divmod(at, parts)
        start = chunk * parts * part + (me_ref[2] ^ mask) * part
        ref[...] = whole_ref[pl.ds(pl.multiple_of(start, part), part), :]


def core_out(where, qkv, steps, near, far, gain, w_out, chunks, parts):
    _, rows, chans = qkv.shape
    width = w_out.shape[1]
    vmem = pl.BlockSpec(memory_space=pltpu.VMEM)
    outs = pl.pallas_call(
        functools.partial(core_kernel, parts),
        in_specs=[pl.BlockSpec(memory_space=pltpu.SMEM)] + [vmem] * 5 + [pl.BlockSpec(memory_space=pltpu.HBM)],
        out_shape=[jax.ShapeDtypeStruct((rows // chunks // parts, width), BF)] * (chunks * parts),
        scratch_shapes=[
            pltpu.VMEM((rows, chans), BF),
            pltpu.VMEM((2 * near.shape[0], *near.shape[1:]), BF),
            pltpu.VMEM(w_out.shape, BF),
            pltpu.VMEM((rows, width), BF),
            pltpu.SemaphoreType.DMA,
        ],
        compiler_params=params(56),
        name="core_out",
    )(where, qkv, steps, gain.reshape(1, chans), near, far, w_out)
    return [outs[chunk * parts : (chunk + 1) * parts] for chunk in range(chunks)]


def grad_kernel(
    me_ref, qkv_ref, cot_ref, steps_ref, fwd_near, fwd_far, bwd_near, bwd_far, gq_ref, gk_ref, gv_ref, fwd_ref, bwd_ref
):
    _, rows, chans = qkv_ref.shape
    heads = steps_ref.shape[0]
    size = chans // heads
    count = fwd_ref.shape[0]
    arrange(me_ref, fwd_near, fwd_far, fwd_ref)
    arrange(me_ref, bwd_near, bwd_far, bwd_ref)
    along, down, lower = decay_sums(steps_ref[...])
    for head in range(heads):
        at = slice(head * size, (head + 1) * size)
        state = entering(fwd_ref, heads, head, size, 0, me_ref[0], 1).astype(BF)
        after = entering(bwd_ref, heads, head, size, count - 1, me_ref[0], -1).astype(BF)
        here = down[:, head : head + 1]
        lead = jnp.exp(here)
        tail = jnp.exp(along[head : head + 1, rows - 1 : rows] - here)
        mask = jnp.exp(jnp.where(lower, here - along[head : head + 1, :], -jnp.inf))
        query, key, val = qkv_ref[0, :, at], qkv_ref[1, :, at], qkv_ref[2, :, at]
        cot = cot_ref[:, at]
        scores = (mm(query, key, NT) * mask).astype(BF)
        dov = (mm(cot, val, NT) * mask).astype(BF)
        gq_ref[:, at] = (mm(dov, key) + lead * mm(cot, state, NT)).astype(BF)
        gk_ref[:, at] = (mm(dov, query, TN) + tail * mm(val, after, NT)).astype(BF)
        gv_ref[:, at] = (mm(scores, cot, TN) + tail * mm(key, after)).astype(BF)


def core_grads(where, qkv, cot, steps, fwd, bwd):
    _, rows, chans = qkv.shape
    count = 2 * fwd[0].shape[0]
    vmem = pl.BlockSpec(memory_space=pltpu.VMEM)
    return pl.pallas_call(
        grad_kernel,
        in_specs=[pl.BlockSpec(memory_space=pltpu.SMEM)] + [vmem] * 7,
        out_shape=[jax.ShapeDtypeStruct((rows, chans), BF)] * 3,
        scratch_shapes=[pltpu.VMEM((count, *fwd[0].shape[1:]), BF), pltpu.VMEM((count, *bwd[0].shape[1:]), BF)],
        compiler_params=params(24),
        name="core_grads",
    )(where, qkv, cot, steps, *fwd, *bwd)


def norm_kernel(where_ref, x_ref, gain_ref, *refs):
    del where_ref
    parts, (out_ref, attn_ref) = refs[:-2], refs[-2:]
    attn = functools.reduce(jnp.add, [part[...].astype(F32) for part in parts])
    attn_ref[...] = attn
    resid = x_ref[...].astype(F32) + attn
    scale = lax.rsqrt(jnp.mean(resid * resid, axis=-1, keepdims=True) + 1e-06)
    out_ref[...] = (resid * scale * gain_ref[...]).astype(BF)


def norm_rows(chunk, where, x, parts, gain):
    rows, width = parts[0].shape
    count = len(parts)
    block = pl.BlockSpec((rows, width), lambda i, where: (0, 0))
    return pl.pallas_call(
        norm_kernel,
        grid_spec=pltpu.PrefetchScalarGridSpec(
            num_scalar_prefetch=1,
            grid=(1,),
            in_specs=[
                pl.BlockSpec((rows, width), lambda i, where: (chunk * count + where[2], 0)),
                pl.BlockSpec((1, width), lambda i, where: (0, 0)),
            ]
            + [block] * count,
            out_specs=[block, block],
        ),
        out_shape=[jax.ShapeDtypeStruct((rows, width), BF), jax.ShapeDtypeStruct((rows, width), F32)],
        compiler_params=params(56),
        name="moe_norm",
    )(where, x, gain.reshape(1, width), *parts)


def join_kernel(where_ref, *refs):
    parts, out_ref = refs[:-1], refs[-1]
    rows = parts[0].shape[0]
    for mask, ref in enumerate(parts):
        out_ref[pl.ds(pl.multiple_of((where_ref[2] ^ mask) * rows, rows), rows), :] = ref[...]


def join_rows(where, parts):
    rows, width = parts[0].shape
    vmem = pl.BlockSpec(memory_space=pltpu.VMEM)
    return pl.pallas_call(
        join_kernel,
        in_specs=[pl.BlockSpec(memory_space=pltpu.SMEM)] + [vmem] * len(parts),
        out_shape=jax.ShapeDtypeStruct((len(parts) * rows, width), BF),
        compiler_params=params(16),
        name="join_rows",
    )(where, *parts)


PAIR = 2


def expert_kernel(masks, chunk, experts, where_ref, routes_ref, gate_hbm, up_hbm, down_hbm, *refs):
    row_refs, (out_ref, rows_ref, gate_ref, up_ref, down_ref, sems, weight_sems) = refs[: len(masks)], refs[len(masks) :]
    _, tok, width = out_ref.shape
    steps = len(masks) // PAIR
    step = pl.program_id(0)
    slot = lax.rem(step, 2)
    loads = [
        pltpu.make_async_copy(source.at[0], target, weight_sems.at[at])
        for at, (source, target) in enumerate(((gate_hbm, gate_ref), (up_hbm, up_ref), (down_hbm, down_ref)))
    ]

    def start(at):
        for part in range(PAIR):
            target = rows_ref.at[at % 2, pl.ds(part * tok, tok)]
            pltpu.make_async_copy(row_refs[PAIR * at + part], target, sems.at[at % 2]).start()

    def ready(at):
        @pl.when(step == 0)
        def _():
            loads[at].wait()

    @pl.when(step == 0)
    def _():
        start(0)
        for load in loads:
            load.start()

    for at in range(1, steps):

        @pl.when(step == at - 1)
        def _(at=at):
            start(at)

    here = lax.broadcasted_iota(jnp.int32, (3 * experts, LANES), 0)
    mine = (here == where_ref[1]) | (here == where_ref[1] + experts) | (here == where_ref[1] + 2 * experts)
    square = (LANES, LANES)
    diagonal = lax.broadcasted_iota(jnp.int32, square, 0) == lax.broadcasted_iota(jnp.int32, square, 1)
    weights = []
    for part in range(PAIR):
        index = jnp.int32(masks[part] // 2)
        for at in range(1, steps):
            index = jnp.where(step == at, masks[PAIR * at + part] // 2, index)
        for block in range(tok // LANES):
            base = (chunk // LANES + block) * 3 * experts
            table = routes_ref[index, base : base + 3 * experts, :].astype(F32)
            row = jnp.sum(jnp.where(mine, table, 0.0), axis=0, keepdims=True)
            weights.append(jnp.sum(jnp.where(diagonal, jnp.broadcast_to(row, square), 0.0), axis=1, keepdims=True))

    pltpu.make_async_copy(rows_ref.at[slot], rows_ref.at[slot], sems.at[slot]).wait()
    tokens = rows_ref[slot]
    ready(0)
    gate = mm(tokens, gate_ref[...])
    ready(1)
    inner = (gate * jax.nn.sigmoid(gate) * mm(tokens, up_ref[...])).astype(BF)
    ready(2)
    cols = pick_block(width, 512)
    for begin in range(0, width, cols):
        piece = mm(inner, down_ref[:, begin : begin + cols])
        for at, weight in enumerate(weights):
            part, row = divmod(at * LANES, tok)
            scaled = piece[at * LANES : (at + 1) * LANES] * weight
            out_ref[part, row : row + LANES, begin : begin + cols] = scaled.astype(BF)


def expert_pieces(chunk, where, blocks, masks, gate, up, down, routes):
    tok, width = blocks[0].shape
    hidden = gate.shape[2]
    count = len(blocks)
    experts = 2 * EXP_CTX * routes.shape[0]
    route_rows = CHUNKS * tok // LANES * 3 * experts
    hbm = pl.BlockSpec(memory_space=pltpu.HBM)
    return pl.pallas_call(
        functools.partial(expert_kernel, tuple(masks), chunk, experts),
        grid=(count // PAIR,),
        in_specs=[
            pl.BlockSpec(memory_space=pltpu.SMEM),
            pl.BlockSpec((routes.shape[0], route_rows, LANES), lambda i: (0, 0, 0)),
        ]
        + [hbm] * 3
        + [pl.BlockSpec(memory_space=pl.ANY)] * count,
        out_specs=pl.BlockSpec((PAIR, tok, width), lambda i: (i, 0, 0)),
        out_shape=jax.ShapeDtypeStruct((count, tok, width), BF),
        scratch_shapes=[
            pltpu.VMEM((2, PAIR * tok, width), BF),
            pltpu.VMEM(gate.shape[1:], BF),
            pltpu.VMEM(up.shape[1:], BF),
            pltpu.VMEM(down.shape[1:], BF),
            pltpu.SemaphoreType.DMA((2,)),
            pltpu.SemaphoreType.DMA((3,)),
        ],
        compiler_params=params(60),
        cost_estimate=pl.CostEstimate(
            flops=6 * count * tok * width * hidden,
            bytes_accessed=4 * count * tok * width,
            transcendentals=count * tok * hidden,
        ),
        name="expert_pieces",
    )(where, routes, gate, up, down, *blocks)


CORE, ROW, COL = 1, 2, 4
PLANE = 8


def swap(value, mask, keep=None):
    count = lax.axis_size("ctx")
    pairs = [(at, at ^ mask) for at in range(count)]
    return lax.ppermute(value, "ctx", [pair for pair in pairs if keep is None or keep(*pair)])


def send_heads(parts):
    count = lax.axis_size("head")
    return [parts[0]] + [
        lax.ppermute(parts[mask], "head", [(at, at ^ mask) for at in range(count)]) for mask in range(1, count)
    ]


def spread_states(own, keep=None):
    near = jnp.stack([own] + [swap(own, mask, keep) for mask in range(2, lax.axis_size("ctx"), 2)])
    return near, swap(near, CORE)


def hops(chunk):
    return (ROW, COL) if chunk % 2 == 0 else (COL, ROW)


def spread_rows(own, chunk):
    count = lax.axis_size("ctx")
    near = {0: own}
    if count == PLANE:
        first, second = hops(chunk)
        near[first] = swap(own, first)
        near[second] = swap(own, second)
        near[ROW | COL] = swap(near[first], second)
    else:
        for mask in range(2, count, 2):
            near[mask] = swap(own, mask)
    return near | {mask | CORE: swap(rows, CORE) for mask, rows in near.items()}


def plus(*terms):
    return functools.reduce(jnp.add, [term.astype(F32) for term in terms]).astype(BF)


def collect_terms(near, far, evens, chunk):
    arrived = swap(far, CORE)
    sums = {mask: (near[at], arrived[at]) for at, mask in enumerate(evens)}
    if lax.axis_size("ctx") == PLANE:
        first, second = hops(chunk)
        across = swap(plus(*sums[ROW | COL]), second)
        direct, across = lax.optimization_barrier((plus(*sums[second]), across))
        others = [swap(plus(*sums[first], across), first), swap(direct, second)]
    else:
        others = [swap(plus(*sums[mask]), mask) for mask in evens[1:]]
    return arrived, others


def sum_kernel(where_ref, attn_ref, near_ref, arrived_ref, *refs):
    parts = attn_ref.shape[1] // refs[-1].shape[1]
    others, outs, total_ref = refs[: -parts - 1], refs[-parts - 1 : -1], refs[-1]
    part, width = attn_ref.shape
    cols = width // parts
    own = pl.ds(pl.multiple_of(where_ref[2] * part, part), part)
    for mask, out_ref in enumerate(outs):
        at = pl.ds(pl.multiple_of((where_ref[2] ^ mask) * cols, cols), cols)
        total = near_ref[0, :, at].astype(F32) + arrived_ref[0, :, at].astype(F32)
        for ref in others:
            total += ref[:, at].astype(F32)
        total_ref[...] = total
        total_ref[own, :] += attn_ref[:, at]
        out_ref[...] = total_ref[...].astype(BF)


def sum_terms(where, attn, near, arrived, others, parts):
    _, tok, width = near.shape
    part = attn.shape[0]
    cols = width // parts
    first = pl.BlockSpec((1, tok, width), lambda i: (0, 0, 0))
    return pl.pallas_call(
        sum_kernel,
        grid=(1,),
        in_specs=[
            pl.BlockSpec(memory_space=pltpu.SMEM),
            pl.BlockSpec((part, width), lambda i: (0, 0)),
            first,
            first,
        ]
        + [pl.BlockSpec((tok, width), lambda i: (0, 0))] * len(others),
        out_specs=[pl.BlockSpec((tok, cols), lambda i: (0, 0))] * parts,
        out_shape=[jax.ShapeDtypeStruct((tok, cols), BF)] * parts,
        scratch_shapes=[pltpu.VMEM((tok, cols), F32)],
        compiler_params=params(24),
        name="sum_terms",
    )(where, attn, near, arrived, *others)


def final_kernel(where_ref, x_ref, *refs):
    del where_ref
    out_ref = refs[-1]
    terms = [x_ref[...]] + [ref[...] for ref in refs[:-1]]
    out_ref[...] = functools.reduce(jnp.add, [term.astype(F32) for term in terms]).astype(BF)


def final_sum(chunk, where, x, parts):
    rows, cols = parts[0].shape
    block = pl.BlockSpec((rows, cols), lambda i, where: (0, 0))
    return pl.pallas_call(
        final_kernel,
        grid_spec=pltpu.PrefetchScalarGridSpec(
            num_scalar_prefetch=1,
            grid=(1,),
            in_specs=[pl.BlockSpec((rows, cols), lambda i, where: (chunk, where[2]))] + [block] * len(parts),
            out_specs=block,
        ),
        out_shape=jax.ShapeDtypeStruct((rows, cols), BF),
        compiler_params=params(56),
        name="layer_out",
    )(where, x, *parts)


CHUNKS = 2


def body(
    hidden_in,
    gain_attn,
    w_qkv,
    conv_w,
    log_decay,
    norm_gain,
    w_out,
    gain_moe,
    expert_ids,
    route_weights,
    w_gate,
    w_up,
    w_down,
    grad_core,
):
    n_ctx, n_head = lax.axis_size("ctx"), lax.axis_size("head")
    my_ctx, my_head = lax.axis_index("ctx"), lax.axis_index("head")
    experts = EXP_CTX * n_ctx
    shards = n_head // EXP_CTX
    where = jnp.stack([my_ctx, EXP_CTX * my_ctx + my_head // shards, my_head]).astype(jnp.int32)
    steps = log_decay.T
    chunk_rows = hidden_in.shape[0] // CHUNKS

    mixed, rim = project(hidden_in, gain_attn, jnp.transpose(w_qkv, (1, 0, 2)))
    rim = lax.ppermute(rim, "ctx", [(at, at + 1) for at in range(n_ctx - 1)])
    qkv, fwd, bwd = local_states(
        mixed, rim, jnp.transpose(conv_w, (1, 0, 2)), steps, grad_core, expert_ids.T, route_weights.T, experts
    )
    fwd = spread_states(fwd, lambda source, target: source < target)
    partials = core_out(where, qkv, steps, *fwd, norm_gain, w_out, CHUNKS, n_head)
    bwd, partials = lax.optimization_barrier((bwd, partials))
    parts = [send_heads(chunk) for chunk in partials]
    bwd = spread_states(bwd)
    parts[1], bwd = lax.optimization_barrier((parts[1], bwd))
    attn, own = [], []
    for chunk in range(CHUNKS):
        normed, total = norm_rows(chunk, where, hidden_in, parts[chunk], gain_moe)
        attn.append(total)
        own.append(join_rows(where, send_heads([normed] * n_head)))
    layer_out = []
    for chunk in range(CHUNKS):
        rows = spread_rows(own[chunk], chunk)
        evens = [mask for mask in rows if not mask & CORE]
        near, far = (
            expert_pieces(
                chunk * chunk_rows, where, [rows[mask] for mask in masks], masks, w_gate, w_up, w_down, routes
            )
            for masks, routes in ((evens, bwd[0]), ([mask | CORE for mask in evens], bwd[1]))
        )
        arrived, others = collect_terms(near, far, evens, chunk)
        sums = send_heads(sum_terms(where, attn[chunk], near, arrived, others, n_head))
        layer_out.append(final_sum(chunk, where, hidden_in, sums))
    grads = core_grads(where, qkv, grad_core, steps, fwd, bwd)
    return (jnp.concatenate(layer_out), *grads)


def solution(mesh):
    in_specs = (
        P("ctx", None),
        P(),
        P(None, None, "head"),
        P(None, None, "head"),
        P("ctx", "head"),
        P("head"),
        P("head", None),
        P(),
        P("ctx", None),
        P("ctx", None),
        P(("ctx", "head"), None, None),
        P(("ctx", "head"), None, None),
        P(("ctx", "head"), None, None),
        P("ctx", "head"),
    )
    out_specs = (P("ctx", "head"), P("ctx", "head"), P("ctx", "head"), P("ctx", "head"))
    return jax.shard_map(body, mesh=mesh, in_specs=in_specs, out_specs=out_specs, check_vma=False)
```

time: 284 us -> 246 us (0.87)
  waiting for transfers between devices: 136 us -> 98.6 us
  Pallas kernels: 34.9 us -> 67.7 us
  blocking collectives: 32.7 us -> 0 us
  starting transfers between devices: 32.7 us -> 62 us
  local copies, waits for them, and re-layouts: 29 us -> 8.13 us
  between operations: 14.2 us -> 1.31 us
  other arithmetic: 3.69 us -> 7.93 us
    reduce_scatter x4 -> x0, waiting for transfers between devices: 45.7 us -> none  [the longest x2 24.4 us: body(): lax.psum_scatter(part, 'head', scatter_dimension=0, tiled=True)]
    ppermute x0 -> x18, waiting for transfers between devices: none -> 37.2 us  [send_heads(): lax.ppermute(parts[mask], 'head', [(at, at ^ mask) for at in range(count)])]
    all_gather x2 -> x0, blocking collectives: 32.7 us -> none  [body(): own.append(lax.all_gather(normed, 'head', tiled=True))]
    ppermute x30, waiting for transfers between devices: 89.6 us -> 60.3 us  [swap(): lax.ppermute(value, 'ctx', [pair for pair in pairs if keep is None or kee...]
    ppermute x0 -> x18, starting transfers between devices: none -> 27.1 us  [send_heads(): lax.ppermute(parts[mask], 'head', [(at, at ^ mask) for at in range(count)])]
    pallas_call x10 -> x12, Pallas kernels: 28.9 us -> 53.8 us  [the longest x4 34.3 us: expert_pieces(): pl.pallas_call(functools.partial(expert_kernel, tuple(masks), chunk, expe...]
    unnamed x78 -> x104, local copies, waits for them, and re-layouts: 29 us -> 8.13 us
    pallas_call x1 -> x2, Pallas kernels: 0.76 us -> 5.12 us  [final_sum(): pl.pallas_call(final_kernel, grid_spec=pltpu.PrefetchScalarGridSpec(num_s...]
  transfers between devices with their start and end apart: 35 -> 49, of which waited for: 19 -> 24; matrix products, arithmetic and copies ran while one was open for 1% -> 2% of each run, Pallas kernels for 9% -> 21%
where the time goes in v4:
time: 246 us
  waiting for transfers between devices  98.6 us (40%)
  Pallas kernels  67.7 us (28%)
  starting transfers between devices  62 us (25%)
  local copies, waits for them, and re-layouts  8.13 us (3%)
  other arithmetic  7.93 us (3%)
    ppermute x30, waiting for transfers between devices, swap(): lax.ppermute(value, 'ctx', [pair for pair in pairs if keep is None or kee...  60.3 us
    ppermute x18, waiting for transfers between devices, send_heads(): lax.ppermute(parts[mask], 'head', [(at, at ^ mask) for at in range(count)])  37.2 us
    pallas_call x4, Pallas kernels, expert_pieces(): pl.pallas_call(functools.partial(expert_kernel, tuple(masks), chunk, expe...  34.3 us
    ppermute x30, starting transfers between devices, swap(): lax.ppermute(value, 'ctx', [pair for pair in pairs if keep is None or kee...  32.6 us
    ppermute x18, starting transfers between devices, send_heads(): lax.ppermute(parts[mask], 'head', [(at, at ^ mask) for at in range(count)])  27.1 us
    unnamed x104, local copies, waits for them, and re-layouts  8.13 us
    pallas_call x1, Pallas kernels, project(): pl.pallas_call(qkv_kernel, in_specs=[hbm, vmem, hbm], out_shape=[jax.Shap...  6.66 us
    pallas_call x1, Pallas kernels, core_out(): pl.pallas_call(functools.partial(core_kernel, parts), in_specs=[pl.BlockS...  5.57 us
  transfers between devices with their start and end apart: 49, of which 24 were waited for; matrix products, arithmetic and copies ran while one was open for 2% of the time, Pallas kernels for 21%

profile of v4, /device:TPU:0, one launch (start us, length us, event | category | flops | bytes accessed | tf_op | source)
XLA Modules:
  0.0 245.6 jit_solution(9758114441567934450)
XLA Ops:
  0.7 6.7 %qkv_projection.1 = (bf16[3,256,512]{2,1,0:T(8,128)(2,1)}, bf16[3,16,512]{2,1,0:T(8,128)(2,1)}) custom-call(bf16[256,2048]{1,0:T(8,128)(2,1)} %x_ref.7, f32[1,2048]{1,0:T(1,128)} %bitcast.52, bf16[3,2048,512]{2,1,0:T(8,128)(2,1)} %bitcast.43), custom_call_target="tpu_custom_call" | custom-call | tf_op jit(solution)/shard_map/qkv_projection/pallas_call | solution.py:58
  7.4 2.4 collective-permute-start
  10.8 1.1 copy-done.11
  12.0 2.1 conv_states.1
  15.0 7.0 %collective-permute-start.1 = (bf16[576,128]{1,0:T(8,128)(2,1)S(1)}, bf16[576,128]{1,0:T(8,128)(2,1)S(1)}, u32[]{:S(2)}, u32[]{:S(2)}) collective-permute-start(bf16[576,128]{1,0:T(8,128)(2,1)S(1)} %get-tuple-element.55), channel_id=1, source_target_pairs={{0,8},{4,12},{16,24},{20,28},{1,9},{5,13},{17,25},{21,29},{2,10},{... | collective-permute-start | bytes 442376 | tf_op jit(solution)/shard_map/ppermute | solution.py:433
  22.0 3.4 %collective-permute-start.2 = (bf16[576,128]{1,0:T(8,128)(2,1)S(1)}, bf16[576,128]{1,0:T(8,128)(2,1)S(1)}, u32[]{:S(2)}, u32[]{:S(2)}) collective-permute-start(bf16[576,128]{1,0:T(8,128)(2,1)S(1)} %get-tuple-element.55), channel_id=1, source_target_pairs={{0,16},{4,20},{8,24},{12,28},{1,17},{5,21},{9,25},{13,29},{2,18},{... | collective-permute-start | bytes 442376 | tf_op jit(solution)/shard_map/ppermute | solution.py:433
  25.5 1.3 collective-permute-start.3
  26.8 1.6 collective-permute-done.2
  30.2 1.4 collective-permute-done.4.far_ref.fwd_far
  32.4 5.6 %core_out.1 = (bf16[32,2048]{1,0:T(8,128)(2,1)}, bf16[32,2048]{1,0:T(8,128)(2,1)}, bf16[32,2048]{1,0:T(8,128)(2,1)}, bf16[32,2048]{1,0:T(8,128)(2,1)}, bf16[32,2...) custom-call(s32[3]{0:T(128)} %pad_add_fusion.me_ref.where_ref, ...), custom_call_target="tpu_custom_call" | custom-call | tf_op jit(solution)/shard_map/core_out/pallas_call | solution.py:214
  38.0 1.7 collective-permute-start.11
  39.7 2.8 %collective-permute-start.12 = (bf16[672,128]{1,0:T(8,128)(2,1)S(1)}, bf16[672,128]{1,0:T(8,128)(2,1)S(1)}, u32[]{:S(2)}, u32[]{:S(2)}) collective-permute-start(bf16[672,128]{1,0:T(8,128)(2,1)S(1)} %get-tuple-element.73), channel_id=1, source_target_pairs={{0,16},{4,20},{8,24},{12,28},{16,0},{20,4},{24,8},{28,12},{1,17},{... | collective-permute-start | bytes 516104 | tf_op jit(solution)/shard_map/ppermute | solution.py:433
  43.3 1.4 collective-permute-done.11
  44.7 5.3 %collective-permute-done.12 = bf16[672,128]{1,0:T(8,128)(2,1)S(1)} collective-permute-done((bf16[672,128]{1,0:T(8,128)(2,1)S(1)}, bf16[672,128]{1,0:T(8,128)(2,1)S(1)}, u32[]{:S(2)}, u32[]{:S(2)}) %collective-permute-start.12) | collective-permute-done | bytes 172064 | tf_op jit(solution)/shard_map/ppermute | solution.py:433
  49.9 1.5 collective-permute-done.13
  51.6 1.6 collective-permute-start.5
  53.2 2.6 %collective-permute-start.6 = (bf16[32,2048]{1,0:T(8,128)(2,1)}, bf16[32,2048]{1,0:T(8,128)(2,1)S(1)}, u32[]{:S(2)}, u32[]{:S(2)}) collective-permute-start(bf16[32,2048]{1,0:T(8,128)(2,1)} %get-tuple-element.66), channel_id=1, source_target_pairs={{0,2},{1,3},{2,0},{3,1},{4,6},{5,7},{6,4},{7,5},{8,10},{9,11},{10,... | collective-permute-start | bytes 393224 | tf_op jit(solution)/shard_map/ppermute | solution.py:439
  56.1 3.9 %collective-permute-done.5.refs_1_ = bf16[32,2048]{1,0:T(8,128)(2,1)S(1)} collective-permute-done((bf16[32,2048]{1,0:T(8,128)(2,1)}, bf16[32,2048]{1,0:T(8,128)(2,1)S(1)}, u32[]{:S(2)}, u32[]{:S(2)}) %collective-permute-start.5) | collective-permute-done | bytes 131104 | tf_op jit(solution)/shard_map/ppermute | solution.py:439
  60.0 6.4 %collective-permute-done.6.refs_2_ = bf16[32,2048]{1,0:T(8,128)(2,1)S(1)} collective-permute-done((bf16[32,2048]{1,0:T(8,128)(2,1)}, bf16[32,2048]{1,0:T(8,128)(2,1)S(1)}, u32[]{:S(2)}, u32[]{:S(2)}) %collective-permute-start.6) | collective-permute-done | bytes 131104 | tf_op jit(solution)/shard_map/ppermute | solution.py:439
  67.1 2.8 %moe_norm.2 = (bf16[32,2048]{1,0:T(8,128)(2,1)}, f32[32,2048]{1,0:T(8,128)}) custom-call(s32[3]{0:T(128)} %pad_add_fusion.me_ref.where_ref, bf16[256,2048]{1,0:T(8,128)(2,1)} %x_ref.7, f32[1,2048]{1,0:T(1,128)} %bitcast.50, bf16[32,2048]{1,0:T(8,128)(2,1)} %get-tuple-element.64.refs_0_, bf16[32,2048]{1,0:T(8,128)(2,1)} %copy-done.37, ...), custom_call_target="tpu_custom_call" | custom-call | tf_op jit(solution)/shard_map/moe_norm/pallas_call | solution.py:286
  69.9 2.6 %collective-permute-start.15 = (bf16[32,2048]{1,0:T(8,128)(2,1)}, bf16[32,2048]{1,0:T(8,128)(2,1)S(1)}, u32[]{:S(2)}, u32[]{:S(2)}) collective-permute-start(bf16[32,2048]{1,0:T(8,128)(2,1)} %get-tuple-element.75.refs_0_), channel_id=1, source_target_pairs={{0,1},{1,0},{2,3},{3,2},{4,5},{5,4},{6,7},{7,6},{8,9},{9,8},{10,11... | collective-permute-start | bytes 393224 | tf_op jit(solution)/shard_map/ppermute | solution.py:439
  73.4 1.5 collective-permute-start.17
  74.9 2.0 collective-permute-done.15.refs_1_
  76.9 8.1 %collective-permute-done.16.refs_2_ = bf16[32,2048]{1,0:T(8,128)(2,1)S(1)} collective-permute-done((bf16[32,2048]{1,0:T(8,128)(2,1)}, bf16[32,2048]{1,0:T(8,128)(2,1)S(1)}, u32[]{:S(2)}, u32[]{:S(2)}) %collective-permute-start.16) | collective-permute-done | bytes 131104 | tf_op jit(solution)/shard_map/ppermute | solution.py:439
  87.4 1.9 collective-permute-start.10
  89.3 1.5 collective-permute-start.8
  91.8 3.9 %collective-permute-done.10.refs_3_ = bf16[32,2048]{1,0:T(8,128)(2,1)S(1)} collective-permute-done((bf16[32,2048]{1,0:T(8,128)(2,1)S(1)}, bf16[32,2048]{1,0:T(8,128)(2,1)S(1)}, u32[]{:S(2)}, u32[]{:S(2)}) %collective-permute-start.10) | collective-permute-done | bytes 131104 | tf_op jit(solution)/shard_map/ppermute | solution.py:439
  95.7 5.1 %collective-permute-done.9.refs_2_ = bf16[32,2048]{1,0:T(8,128)(2,1)S(1)} collective-permute-done((bf16[32,2048]{1,0:T(8,128)(2,1)S(1)}, bf16[32,2048]{1,0:T(8,128)(2,1)S(1)}, u32[]{:S(2)}, u32[]{:S(2)}) %collective-permute-start.9) | collective-permute-done | bytes 131104 | tf_op jit(solution)/shard_map/ppermute | solution.py:439
  101.4 2.7 %moe_norm.3 = (bf16[32,2048]{1,0:T(8,128)(2,1)}, f32[32,2048]{1,0:T(8,128)}) custom-call(s32[3]{0:T(128)} %pad_add_fusion.me_ref.where_ref, bf16[256,2048]{1,0:T(8,128)(2,1)} %x_ref.7, f32[1,2048]{1,0:T(1,128)} %bitcast.51, bf16[32,2048]{1,0:T(8,128)(2,1)} %get-tuple-element.83.refs_0_, bf16[32,2048]{1,0:T(8,128)(2,1)} %copy-done.38, ...), custom_call_target="tpu_custom_call" | custom-call | tf_op jit(solution)/shard_map/moe_norm/pallas_call | solution.py:286
  104.1 2.8 %collective-permute-start.33 = (bf16[32,2048]{1,0:T(8,128)(2,1)}, bf16[32,2048]{1,0:T(8,128)(2,1)S(1)}, u32[]{:S(2)}, u32[]{:S(2)}) collective-permute-start(bf16[32,2048]{1,0:T(8,128)(2,1)} %get-tuple-element.88.refs_0_), channel_id=1, source_target_pairs={{0,2},{1,3},{2,0},{3,1},{4,6},{5,7},{6,4},{7,5},{8,10},{9,11},{10,... | collective-permute-start | bytes 393224 | tf_op jit(solution)/shard_map/ppermute | solution.py:439
  106.9 1.6 collective-permute-start.34
  108.5 1.6 collective-permute-start.19
  110.5 6.3 %collective-permute-done.33.refs_2_ = bf16[32,2048]{1,0:T(8,128)(2,1)S(1)} collective-permute-done((bf16[32,2048]{1,0:T(8,128)(2,1)}, bf16[32,2048]{1,0:T(8,128)(2,1)S(1)}, u32[]{:S(2)}, u32[]{:S(2)}) %collective-permute-start.33) | collective-permute-done | bytes 131104 | tf_op jit(solution)/shard_map/ppermute | solution.py:439
  118.3 1.7 collective-permute-start.35
  120.4 3.0 %collective-permute-done.19.refs_2_ = bf16[128,2048]{1,0:T(8,128)(2,1)S(1)} collective-permute-done((bf16[128,2048]{1,0:T(8,128)(2,1)S(1)}, bf16[128,2048]{1,0:T(8,128)(2,1)S(1)}, u32[]{:S(2)}, u32[]{:S(2)}) %collective-permute-start.19) | collective-permute-done | bytes 524320 | tf_op jit(solution)/shard_map/ppermute | solution.py:433
  123.4 1.4 collective-permute-start.36
  124.8 9.8 %collective-permute-done.35.refs_1_ = bf16[128,2048]{1,0:T(8,128)(2,1)S(1)} collective-permute-done((bf16[128,2048]{1,0:T(8,128)(2,1)S(1)}, bf16[128,2048]{1,0:T(8,128)(2,1)S(1)}, u32[]{:S(2)}, u32[]{:S(2)}) %collective-permute-start.35) | collective-permute-done | bytes 524320 | tf_op jit(solution)/shard_map/ppermute | solution.py:433
  134.6 1.3 collective-permute-start.37
  135.9 7.0 %collective-permute-done.20.refs_3_ = bf16[128,2048]{1,0:T(8,128)(2,1)S(1)} collective-permute-done((bf16[128,2048]{1,0:T(8,128)(2,1)S(1)}, bf16[128,2048]{1,0:T(8,128)(2,1)S(1)}, u32[]{:S(2)}, u32[]{:S(2)}) %collective-permute-start.20) | collective-permute-done | bytes 524320 | tf_op jit(solution)/shard_map/ppermute | solution.py:433
  144.0 5.1 %collective-permute-done.37.refs_3_ = bf16[128,2048]{1,0:T(8,128)(2,1)} collective-permute-done((bf16[128,2048]{1,0:T(8,128)(2,1)S(1)}, bf16[128,2048]{1,0:T(8,128)(2,1)}, u32[]{:S(2)}, u32[]{:S(2)}) %collective-permute-start.37) | collective-permute-done | bytes 524320 | tf_op jit(solution)/shard_map/ppermute | solution.py:433
  149.1 8.7 %expert_pieces.5 = bf16[4,128,2048]{2,1,0:T(8,128)(2,1)} custom-call(s32[3]{0:T(128)} %pad_add_fusion.me_ref.where_ref, bf16[4,672,128]{2,1,0:T(8,128)(2,1)} %copy-done.12, bf16[1,2048,512]{2,1,0:T(8,128)(2,1)} %gate_hbm.7, bf16[1,2048,512]{2,1,0:T(8,128)(2,1)} %up_hbm.7, bf16[1,512,2048]{2,1,0:T(8,128)(2,1)} %down_hbm.7, bf16[128,2048]{1,0:T(8,128)(2,1)} %copy-done.46, ...), custom_call_target="tpu_custom_call" | custom-call | flops 3221225472 | bytes 4194304 | tf_op jit(solution)/shard_map/expert_pieces/pallas_call | solution.py:397
  158.5 8.6 %expert_pieces.7 = bf16[4,128,2048]{2,1,0:T(8,128)(2,1)} custom-call(s32[3]{0:T(128)} %pad_add_fusion.me_ref.where_ref, bf16[4,672,128]{2,1,0:T(8,128)(2,1)} %copy-done.12, bf16[1,2048,512]{2,1,0:T(8,128)(2,1)} %gate_hbm.7, bf16[1,2048,512]{2,1,0:T(8,128)(2,1)} %up_hbm.7, bf16[1,512,2048]{2,1,0:T(8,128)(2,1)} %down_hbm.7, ...), custom_call_target="tpu_custom_call" | custom-call | flops 3221225472 | bytes 4194304 | tf_op jit(solution)/shard_map/expert_pieces/pallas_call | solution.py:397
  167.2 8.5 %expert_pieces.4.near_ref = bf16[4,128,2048]{2,1,0:T(8,128)(2,1)} custom-call(s32[3]{0:T(128)} %pad_add_fusion.me_ref.where_ref, bf16[4,672,128]{2,1,0:T(8,128)(2,1)} %copy-done.6, bf16[1,2048,512]{2,1,0:T(8,128)(2,1)} %gate_hbm.7, bf16[1,2048,512]{2,1,0:T(8,128)(2,1)} %up_hbm.7, bf16[1,512,2048]{2,1,0:T(8,128)(2,1)} %down_hbm.7, ...), custom_call_target="tpu_custom_call" | custom-call | flops 3221225472 | bytes 4194304 | tf_op jit(solution)/shard_map/expert_pieces/pallas_call | solution.py:397
  175.7 1.9 fusion.3
  177.6 1.7 collective-permute-start.26
  179.3 8.5 %expert_pieces.6.near_ref = bf16[4,128,2048]{2,1,0:T(8,128)(2,1)} custom-call(s32[3]{0:T(128)} %pad_add_fusion.me_ref.where_ref, bf16[4,672,128]{2,1,0:T(8,128)(2,1)} %copy-done.6, bf16[1,2048,512]{2,1,0:T(8,128)(2,1)} %gate_hbm.7, bf16[1,2048,512]{2,1,0:T(8,128)(2,1)} %up_hbm.7, bf16[1,512,2048]{2,1,0:T(8,128)(2,1)} %down_hbm.7, ...), custom_call_target="tpu_custom_call" | custom-call | flops 3221225472 | bytes 4194304 | tf_op jit(solution)/shard_map/expert_pieces/pallas_call | solution.py:397
  187.8 1.7 fusion.5
  190.3 1.6 collective-permute-done.26
  192.0 1.6 fusion.1
  193.6 1.4 collective-permute-start.27
  195.9 8.4 %collective-permute-done.43 = bf16[128,2048]{1,0:T(8,128)(2,1)S(1)} collective-permute-done((bf16[128,2048]{1,0:T(8,128)(2,1)S(1)}, bf16[128,2048]{1,0:T(8,128)(2,1)S(1)}, u32[]{:S(2)}, u32[]{:S(2)}) %collective-permute-start.43) | collective-permute-done | bytes 524320 | tf_op jit(solution)/shard_map/ppermute | solution.py:433
  205.1 1.3 collective-permute-start.45
  206.4 9.2 %collective-permute-done.27.refs_0_ = bf16[128,2048]{1,0:T(8,128)(2,1)S(1)} collective-permute-done((bf16[128,2048]{1,0:T(8,128)(2,1)S(1)}, bf16[128,2048]{1,0:T(8,128)(2,1)S(1)}, u32[]{:S(2)}, u32[]{:S(2)}) %collective-permute-start.27) | collective-permute-done | bytes 524320 | tf_op jit(solution)/shard_map/ppermute | solution.py:433
  215.6 1.5 sum_terms.2
  217.8 2.2 collective-permute-start.30
  220.0 2.2 collective-permute-start.31
  222.2 3.8 %collective-permute-done.45.refs_1_ = bf16[128,2048]{1,0:T(8,128)(2,1)S(1)} collective-permute-done((bf16[128,2048]{1,0:T(8,128)(2,1)S(1)}, bf16[128,2048]{1,0:T(8,128)(2,1)S(1)}, u32[]{:S(2)}, u32[]{:S(2)}) %collective-permute-start.45) | collective-permute-done | bytes 524320 | tf_op jit(solution)/shard_map/ppermute | solution.py:433
  227.2 2.2 collective-permute-start.47
  229.4 2.2 collective-permute-start.48
  231.6 4.7 %core_grads.1 = (bf16[256,512]{1,0:T(8,128)(2,1)}, bf16[256,512]{1,0:T(8,128)(2,1)}, bf16[256,512]{1,0:T(8,128)(2,1)}) custom-call(s32[3]{0:T(128)S(1)} %copy-done.24, bf16[3,256,512]{2,1,0:T(8,128)(2,1)S(1)} %copy-done.5, bf16[256,512]{1,0:T(8,128)(2,1)S(1)} %copy-done.10, f32[4,256]{1,0:T(4,128)S(1)} %bitcast.39, bf16[4,576,128]{2,1,0:T(8,128)(2,1)S(1)} %copy-done.3, ...), custom_call_target="tpu_custom_call" | custom-call | tf_op jit(solution)/shard_map/core_grads/pallas_call | solution.py:262
  237.0 2.6 %layer_out.2 = bf16[128,512]{1,0:T(8,128)(2,1)} custom-call(s32[3]{0:T(128)} %pad_add_fusion.me_ref.where_ref, bf16[256,2048]{1,0:T(8,128)(2,1)} %x_ref.7, bf16[128,512]{1,0:T(8,128)(2,1)} %copy-done.18, bf16[128,512]{1,0:T(8,128)(2,1)} %copy-done.30, bf16[128,512]{1,0:T(8,128)(2,1)} %copy-done.31, bf16[128,512]{1,0:T(8,128)(2,1)} %copy-done.32), custom_call_target="tpu_custom_call" | custom-call | tf_op jit(solution)/shard_map/layer_out/pallas_call | solution.py:532
  239.6 1.1 collective-permute-done.47.refs_2_
  241.4 2.6 %layer_out.3 = bf16[128,512]{1,0:T(8,128)(2,1)} custom-call(s32[3]{0:T(128)} %pad_add_fusion.me_ref.where_ref, bf16[256,2048]{1,0:T(8,128)(2,1)} %x_ref.7, bf16[128,512]{1,0:T(8,128)(2,1)} %copy-done.19, bf16[128,512]{1,0:T(8,128)(2,1)} %copy-done.33, bf16[128,512]{1,0:T(8,128)(2,1)} %copy-done.34, bf16[128,512]{1,0:T(8,128)(2,1)} %copy-done.35), custom_call_target="tpu_custom_call" | custom-call | tf_op jit(solution)/shard_map/layer_out/pallas_call | solution.py:532
  243.9 1.7 pad_maximum_fusion.2
  (162 shorter events, 21.0 us)
Async XLA Ops:
  7.4 3.4 %collective-permute-start = (bf16[3,16,512]{2,1,0:T(8,128)(2,1)}, bf16[3,16,512]{2,1,0:T(8,128)(2,1)S(1)}, u32[]{:S(2)}, u32[]{:S(2)}) collective-permute-start(bf16[3,16,512]{2,1,0:T(8,128)(2,1)} %get-tuple-element.52), channel_id=1, source_target_pairs={{0,4},{4,8},{8,12},{12,16},{16,20},{20,24},{24,28},{1,5},{5,9},{9,... | collective-permute-start | bytes 147464 | tf_op jit(solution)/shard_map/ppermute | solution.py:574
  15.0 11.8 %collective-permute-start.1 = (bf16[576,128]{1,0:T(8,128)(2,1)S(1)}, bf16[576,128]{1,0:T(8,128)(2,1)S(1)}, u32[]{:S(2)}, u32[]{:S(2)}) collective-permute-start(bf16[576,128]{1,0:T(8,128)(2,1)S(1)} %get-tuple-element.55), channel_id=1, source_target_pairs={{0,8},{4,12},{16,24},{20,28},{1,9},{5,13},{17,25},{21,29},{2,10},{... | collective-permute-start | bytes 442376 | tf_op jit(solution)/shard_map/ppermute | solution.py:433
  22.0 6.3 %collective-permute-start.2 = (bf16[576,128]{1,0:T(8,128)(2,1)S(1)}, bf16[576,128]{1,0:T(8,128)(2,1)S(1)}, u32[]{:S(2)}, u32[]{:S(2)}) collective-permute-start(bf16[576,128]{1,0:T(8,128)(2,1)S(1)} %get-tuple-element.55), channel_id=1, source_target_pairs={{0,16},{4,20},{8,24},{12,28},{1,17},{5,21},{9,25},{13,29},{2,18},{... | collective-permute-start | bytes 442376 | tf_op jit(solution)/shard_map/ppermute | solution.py:433
  25.5 4.0 %collective-permute-start.3 = (bf16[576,128]{1,0:T(8,128)(2,1)S(1)}, bf16[576,128]{1,0:T(8,128)(2,1)S(1)}, u32[]{:S(2)}, u32[]{:S(2)}) collective-permute-start(bf16[576,128]{1,0:T(8,128)(2,1)S(1)} %get-tuple-element.55), channel_id=1, source_target_pairs={{0,24},{4,28},{8,16},{12,20},{1,25},{5,29},{9,17},{13,21},{2,26},{... | collective-permute-start | bytes 442376 | tf_op jit(solution)/shard_map/ppermute | solution.py:433
  29.5 2.1 collective-permute-start.4
  38.0 47.1 %copy-start.22 = (s32[3]{0:T(128)S(1)}, s32[3]{0:T(128)}, u32[]{:S(2)}) copy-start(s32[3]{0:T(128)} %pad_add_fusion.me_ref.where_ref) | copy-start | bytes 40
  38.0 49.4 %copy-start.51 = (bf16[32,2048]{1,0:T(8,128)(2,1)S(1)}, bf16[32,2048]{1,0:T(8,128)(2,1)}, u32[]{:S(2)}) copy-start(bf16[32,2048]{1,0:T(8,128)(2,1)} %get-tuple-element.72) | copy-start | bytes 393220
  38.0 51.3 %copy-start.50 = (bf16[32,2048]{1,0:T(8,128)(2,1)S(1)}, bf16[32,2048]{1,0:T(8,128)(2,1)}, u32[]{:S(2)}) copy-start(bf16[32,2048]{1,0:T(8,128)(2,1)} %get-tuple-element.70) | copy-start | bytes 393220
  38.0 52.9 %copy-start.49 = (bf16[32,2048]{1,0:T(8,128)(2,1)S(1)}, bf16[32,2048]{1,0:T(8,128)(2,1)}, u32[]{:S(2)}) copy-start(bf16[32,2048]{1,0:T(8,128)(2,1)} %get-tuple-element.71) | copy-start | bytes 393220
  38.0 6.6 %collective-permute-start.11 = (bf16[672,128]{1,0:T(8,128)(2,1)S(1)}, bf16[672,128]{1,0:T(8,128)(2,1)S(1)}, u32[]{:S(2)}, u32[]{:S(2)}) collective-permute-start(bf16[672,128]{1,0:T(8,128)(2,1)S(1)} %get-tuple-element.73), channel_id=1, source_target_pairs={{0,8},{4,12},{8,0},{12,4},{16,24},{20,28},{24,16},{28,20},{1,9},{5... | collective-permute-start | bytes 516104 | tf_op jit(solution)/shard_map/ppermute | solution.py:433
  39.7 10.2 %collective-permute-start.12 = (bf16[672,128]{1,0:T(8,128)(2,1)S(1)}, bf16[672,128]{1,0:T(8,128)(2,1)S(1)}, u32[]{:S(2)}, u32[]{:S(2)}) collective-permute-start(bf16[672,128]{1,0:T(8,128)(2,1)S(1)} %get-tuple-element.73), channel_id=1, source_target_pairs={{0,16},{4,20},{8,24},{12,28},{16,0},{20,4},{24,8},{28,12},{1,17},{... | collective-permute-start | bytes 516104 | tf_op jit(solution)/shard_map/ppermute | solution.py:433
  42.5 8.9 %collective-permute-start.13 = (bf16[672,128]{1,0:T(8,128)(2,1)S(1)}, bf16[672,128]{1,0:T(8,128)(2,1)S(1)}, u32[]{:S(2)}, u32[]{:S(2)}) collective-permute-start(bf16[672,128]{1,0:T(8,128)(2,1)S(1)} %get-tuple-element.73), channel_id=1, source_target_pairs={{0,24},{4,28},{8,16},{12,20},{16,8},{20,12},{24,0},{28,4},{1,25},{... | collective-permute-start | bytes 516104 | tf_op jit(solution)/shard_map/ppermute | solution.py:433
  51.5 52.6 %copy-start.6 = (bf16[4,672,128]{2,1,0:T(8,128)(2,1)}, bf16[4,672,128]{2,1,0:T(8,128)(2,1)S(1)}, u32[]{:S(2)}) copy-start(bf16[4,672,128]{2,1,0:T(8,128)(2,1)S(1)} %pad_maximum_fusion.routes_ref.bwd_near) | copy-start | bytes 2064388
  51.5 49.3 %collective-permute-start.14 = (bf16[4,672,128]{2,1,0:T(8,128)(2,1)S(1)}, bf16[4,672,128]{2,1,0:T(8,128)(2,1)S(1)}, u32[]{:S(2)}, u32[]{:S(2)}) collective-permute-start(bf16[4,672,128]{2,1,0:T(8,128)(2,1)S(1)} %pad_maximum_fusion.routes_ref.bwd_near), channel_id=1, source_target_pairs={{0,4},{4,0},{8,12},{12,8},{16,20},{20,16},{24,28},{28,24},{1,5},{5... | collective-permute-start | bytes 2064392 | tf_op jit(solution)/shard_map/ppermute | solution.py:433
  51.6 8.4 %collective-permute-start.5 = (bf16[32,2048]{1,0:T(8,128)(2,1)}, bf16[32,2048]{1,0:T(8,128)(2,1)S(1)}, u32[]{:S(2)}, u32[]{:S(2)}) collective-permute-start(bf16[32,2048]{1,0:T(8,128)(2,1)} %get-tuple-element.65), channel_id=1, source_target_pairs={{0,1},{1,0},{2,3},{3,2},{4,5},{5,4},{6,7},{7,6},{8,9},{9,8},{10,11... | collective-permute-start | bytes 393224 | tf_op jit(solution)/shard_map/ppermute | solution.py:439
  53.2 13.1 %collective-permute-start.6 = (bf16[32,2048]{1,0:T(8,128)(2,1)}, bf16[32,2048]{1,0:T(8,128)(2,1)S(1)}, u32[]{:S(2)}, u32[]{:S(2)}) collective-permute-start(bf16[32,2048]{1,0:T(8,128)(2,1)} %get-tuple-element.66), channel_id=1, source_target_pairs={{0,2},{1,3},{2,0},{3,1},{4,6},{5,7},{6,4},{7,5},{8,10},{9,11},{10,... | collective-permute-start | bytes 393224 | tf_op jit(solution)/shard_map/ppermute | solution.py:439
  55.8 10.5 %collective-permute-start.7 = (bf16[32,2048]{1,0:T(8,128)(2,1)}, bf16[32,2048]{1,0:T(8,128)(2,1)S(1)}, u32[]{:S(2)}, u32[]{:S(2)}) collective-permute-start(bf16[32,2048]{1,0:T(8,128)(2,1)} %get-tuple-element.67), channel_id=1, source_target_pairs={{0,3},{1,2},{2,1},{3,0},{4,7},{5,6},{6,5},{7,4},{8,11},{9,10},{10,... | collective-permute-start | bytes 393224 | tf_op jit(solution)/shard_map/ppermute | solution.py:439
  67.1 49.7 %copy-start.23 = (s32[3]{0:T(128)S(1)}, s32[3]{0:T(128)}, u32[]{:S(2)}) copy-start(s32[3]{0:T(128)} %pad_add_fusion.me_ref.where_ref) | copy-start | bytes 40
  69.9 7.1 %collective-permute-start.15 = (bf16[32,2048]{1,0:T(8,128)(2,1)}, bf16[32,2048]{1,0:T(8,128)(2,1)S(1)}, u32[]{:S(2)}, u32[]{:S(2)}) collective-permute-start(bf16[32,2048]{1,0:T(8,128)(2,1)} %get-tuple-element.75.refs_0_), channel_id=1, source_target_pairs={{0,1},{1,0},{2,3},{3,2},{4,5},{5,4},{6,7},{7,6},{8,9},{9,8},{10,11... | collective-permute-start | bytes 393224 | tf_op jit(solution)/shard_map/ppermute | solution.py:439
  72.4 12.6 %collective-permute-start.16 = (bf16[32,2048]{1,0:T(8,128)(2,1)}, bf16[32,2048]{1,0:T(8,128)(2,1)S(1)}, u32[]{:S(2)}, u32[]{:S(2)}) collective-permute-start(bf16[32,2048]{1,0:T(8,128)(2,1)} %get-tuple-element.75.refs_0_), channel_id=1, source_target_pairs={{0,2},{1,3},{2,0},{3,1},{4,6},{5,7},{6,4},{7,5},{8,10},{9,11},{10,... | collective-permute-start | bytes 393224 | tf_op jit(solution)/shard_map/ppermute | solution.py:439
  73.4 11.6 %collective-permute-start.17 = (bf16[32,2048]{1,0:T(8,128)(2,1)}, bf16[32,2048]{1,0:T(8,128)(2,1)S(1)}, u32[]{:S(2)}, u32[]{:S(2)}) collective-permute-start(bf16[32,2048]{1,0:T(8,128)(2,1)} %get-tuple-element.75.refs_0_), channel_id=1, source_target_pairs={{0,3},{1,2},{2,1},{3,0},{4,7},{5,6},{6,5},{7,4},{8,11},{9,10},{10,... | collective-permute-start | bytes 393224 | tf_op jit(solution)/shard_map/ppermute | solution.py:439
  86.6 71.3 %copy-start.14 = (bf16[128,2048]{1,0:T(8,128)(2,1)}, bf16[128,2048]{1,0:T(8,128)(2,1)S(1)}, u32[]{:S(2)}) copy-start(bf16[128,2048]{1,0:T(8,128)(2,1)S(1)} %join_rows.2.refs_0_) | copy-start | bytes 1572868
  86.6 33.3 %collective-permute-start.18 = (bf16[128,2048]{1,0:T(8,128)(2,1)S(1)}, bf16[128,2048]{1,0:T(8,128)(2,1)S(1)}, u32[]{:S(2)}, u32[]{:S(2)}) collective-permute-start(bf16[128,2048]{1,0:T(8,128)(2,1)S(1)} %join_rows.2.refs_0_), channel_id=1, source_target_pairs={{0,8},{4,12},{8,0},{12,4},{16,24},{20,28},{24,16},{28,20},{1,9},{5... | collective-permute-start | bytes 1572872 | tf_op jit(solution)/shard_map/ppermute | solution.py:433
  87.4 8.3 %collective-permute-start.10 = (bf16[32,2048]{1,0:T(8,128)(2,1)S(1)}, bf16[32,2048]{1,0:T(8,128)(2,1)S(1)}, u32[]{:S(2)}, u32[]{:S(2)}) collective-permute-start(bf16[32,2048]{1,0:T(8,128)(2,1)S(1)} %copy-done.51), channel_id=1, source_target_pairs={{0,3},{1,2},{2,1},{3,0},{4,7},{5,6},{6,5},{7,4},{8,11},{9,10},{10,... | collective-permute-start | bytes 393224 | tf_op jit(solution)/shard_map/ppermute | solution.py:439
  89.3 6.4 %collective-permute-start.8 = (bf16[32,2048]{1,0:T(8,128)(2,1)S(1)}, bf16[32,2048]{1,0:T(8,128)(2,1)S(1)}, u32[]{:S(2)}, u32[]{:S(2)}) collective-permute-start(bf16[32,2048]{1,0:T(8,128)(2,1)S(1)} %copy-done.50), channel_id=1, source_target_pairs={{0,1},{1,0},{2,3},{3,2},{4,5},{5,4},{6,7},{7,6},{8,9},{9,8},{10,11... | collective-permute-start | bytes 393224 | tf_op jit(solution)/shard_map/ppermute | solution.py:439
  90.9 9.9 %collective-permute-start.9 = (bf16[32,2048]{1,0:T(8,128)(2,1)S(1)}, bf16[32,2048]{1,0:T(8,128)(2,1)S(1)}, u32[]{:S(2)}, u32[]{:S(2)}) collective-permute-start(bf16[32,2048]{1,0:T(8,128)(2,1)S(1)} %copy-done.49), channel_id=1, source_target_pairs={{0,2},{1,3},{2,0},{3,1},{4,6},{5,7},{6,4},{7,5},{8,10},{9,11},{10,... | collective-permute-start | bytes 393224 | tf_op jit(solution)/shard_map/ppermute | solution.py:439
  101.4 47.7 %copy-start.12 = (bf16[4,672,128]{2,1,0:T(8,128)(2,1)}, bf16[4,672,128]{2,1,0:T(8,128)(2,1)S(1)}, u32[]{:S(2)}) copy-start(bf16[4,672,128]{2,1,0:T(8,128)(2,1)S(1)} %collective-permute-done.14.routes_ref.bwd_far) | copy-start | bytes 2064388
  104.1 6.4 %collective-permute-start.32 = (bf16[32,2048]{1,0:T(8,128)(2,1)}, bf16[32,2048]{1,0:T(8,128)(2,1)S(1)}, u32[]{:S(2)}, u32[]{:S(2)}) collective-permute-start(bf16[32,2048]{1,0:T(8,128)(2,1)} %get-tuple-element.88.refs_0_), channel_id=1, source_target_pairs={{0,1},{1,0},{2,3},{3,2},{4,5},{5,4},{6,7},{7,6},{8,9},{9,8},{10,11... | collective-permute-start | bytes 393224 | tf_op jit(solution)/shard_map/ppermute | solution.py:439
  104.1 12.6 %collective-permute-start.33 = (bf16[32,2048]{1,0:T(8,128)(2,1)}, bf16[32,2048]{1,0:T(8,128)(2,1)S(1)}, u32[]{:S(2)}, u32[]{:S(2)}) collective-permute-start(bf16[32,2048]{1,0:T(8,128)(2,1)} %get-tuple-element.88.refs_0_), channel_id=1, source_target_pairs={{0,2},{1,3},{2,0},{3,1},{4,6},{5,7},{6,4},{7,5},{8,10},{9,11},{10,... | collective-permute-start | bytes 393224 | tf_op jit(solution)/shard_map/ppermute | solution.py:439
  106.9 9.9 %collective-permute-start.34 = (bf16[32,2048]{1,0:T(8,128)(2,1)}, bf16[32,2048]{1,0:T(8,128)(2,1)S(1)}, u32[]{:S(2)}, u32[]{:S(2)}) collective-permute-start(bf16[32,2048]{1,0:T(8,128)(2,1)} %get-tuple-element.88.refs_0_), channel_id=1, source_target_pairs={{0,3},{1,2},{2,1},{3,0},{4,7},{5,6},{6,5},{7,4},{8,11},{9,10},{10,... | collective-permute-start | bytes 393224 | tf_op jit(solution)/shard_map/ppermute | solution.py:439
  108.5 14.9 %collective-permute-start.19 = (bf16[128,2048]{1,0:T(8,128)(2,1)S(1)}, bf16[128,2048]{1,0:T(8,128)(2,1)S(1)}, u32[]{:S(2)}, u32[]{:S(2)}) collective-permute-start(bf16[128,2048]{1,0:T(8,128)(2,1)S(1)} %join_rows.2.refs_0_), channel_id=1, source_target_pairs={{0,16},{4,20},{8,24},{12,28},{16,0},{20,4},{24,8},{28,12},{1,17},{... | collective-permute-start | bytes 1572872 | tf_op jit(solution)/shard_map/ppermute | solution.py:433
  110.5 12.9 %collective-permute-start.21 = (bf16[128,2048]{1,0:T(8,128)(2,1)S(1)}, bf16[128,2048]{1,0:T(8,128)(2,1)S(1)}, u32[]{:S(2)}, u32[]{:S(2)}) collective-permute-start(bf16[128,2048]{1,0:T(8,128)(2,1)S(1)} %join_rows.2.refs_0_), channel_id=1, source_target_pairs={{0,4},{4,0},{8,12},{12,8},{16,20},{20,16},{24,28},{28,24},{1,5},{5... | collective-permute-start | bytes 1572872 | tf_op jit(solution)/shard_map/ppermute | solution.py:433
  118.3 39.6 %copy-start.15 = (bf16[128,2048]{1,0:T(8,128)(2,1)}, bf16[128,2048]{1,0:T(8,128)(2,1)S(1)}, u32[]{:S(2)}) copy-start(bf16[128,2048]{1,0:T(8,128)(2,1)S(1)} %join_rows.3.refs_0_) | copy-start | bytes 1572868
  118.3 16.3 %collective-permute-start.35 = (bf16[128,2048]{1,0:T(8,128)(2,1)S(1)}, bf16[128,2048]{1,0:T(8,128)(2,1)S(1)}, u32[]{:S(2)}, u32[]{:S(2)}) collective-permute-start(bf16[128,2048]{1,0:T(8,128)(2,1)S(1)} %join_rows.3.refs_0_), channel_id=1, source_target_pairs={{0,16},{4,20},{8,24},{12,28},{16,0},{20,4},{24,8},{28,12},{1,17},{... | collective-permute-start | bytes 1572872 | tf_op jit(solution)/shard_map/ppermute | solution.py:433
  119.9 37.9 %copy-start.42 = (bf16[128,2048]{1,0:T(8,128)(2,1)}, bf16[128,2048]{1,0:T(8,128)(2,1)S(1)}, u32[]{:S(2)}) copy-start(bf16[128,2048]{1,0:T(8,128)(2,1)S(1)} %collective-permute-done.18.refs_1_) | copy-start | bytes 1572868
  119.9 23.0 %collective-permute-start.20 = (bf16[128,2048]{1,0:T(8,128)(2,1)S(1)}, bf16[128,2048]{1,0:T(8,128)(2,1)S(1)}, u32[]{:S(2)}, u32[]{:S(2)}) collective-permute-start(bf16[128,2048]{1,0:T(8,128)(2,1)S(1)} %collective-permute-done.18.refs_1_), channel_id=1, source_target_pairs={{0,16},{4,20},{8,24},{12,28},{16,0},{20,4},{24,8},{28,12},{1,17},{... | collective-permute-start | bytes 1572872 | tf_op jit(solution)/shard_map/ppermute | solution.py:433
  120.4 22.6 %collective-permute-start.22 = (bf16[128,2048]{1,0:T(8,128)(2,1)S(1)}, bf16[128,2048]{1,0:T(8,128)(2,1)S(1)}, u32[]{:S(2)}, u32[]{:S(2)}) collective-permute-start(bf16[128,2048]{1,0:T(8,128)(2,1)S(1)} %collective-permute-done.18.refs_1_), channel_id=1, source_target_pairs={{0,4},{4,0},{8,12},{12,8},{16,20},{20,16},{24,28},{28,24},{1,5},{5... | collective-permute-start | bytes 1572872 | tf_op jit(solution)/shard_map/ppermute | solution.py:433
  123.4 34.5 %copy-start.43 = (bf16[128,2048]{1,0:T(8,128)(2,1)}, bf16[128,2048]{1,0:T(8,128)(2,1)S(1)}, u32[]{:S(2)}) copy-start(bf16[128,2048]{1,0:T(8,128)(2,1)S(1)} %collective-permute-done.19.refs_2_) | copy-start | bytes 1572868
  123.4 20.1 %collective-permute-start.23 = (bf16[128,2048]{1,0:T(8,128)(2,1)S(1)}, bf16[128,2048]{1,0:T(8,128)(2,1)S(1)}, u32[]{:S(2)}, u32[]{:S(2)}) collective-permute-start(bf16[128,2048]{1,0:T(8,128)(2,1)S(1)} %collective-permute-done.19.refs_2_), channel_id=1, source_target_pairs={{0,4},{4,0},{8,12},{12,8},{16,20},{20,16},{24,28},{28,24},{1,5},{5... | collective-permute-start | bytes 1572872 | tf_op jit(solution)/shard_map/ppermute | solution.py:433
  123.4 25.7 %copy-start.46 = (bf16[128,2048]{1,0:T(8,128)(2,1)}, bf16[128,2048]{1,0:T(8,128)(2,1)S(1)}, u32[]{:S(2)}) copy-start(bf16[128,2048]{1,0:T(8,128)(2,1)S(1)} %collective-permute-done.21.refs_0_) | copy-start | bytes 1572868
  123.4 20.2 %collective-permute-start.36 = (bf16[128,2048]{1,0:T(8,128)(2,1)S(1)}, bf16[128,2048]{1,0:T(8,128)(2,1)}, u32[]{:S(2)}, u32[]{:S(2)}) collective-permute-start(bf16[128,2048]{1,0:T(8,128)(2,1)S(1)} %join_rows.3.refs_0_), channel_id=1, source_target_pairs={{0,8},{4,12},{8,0},{12,4},{16,24},{20,28},{24,16},{28,20},{1,9},{5... | collective-permute-start | bytes 1572872 | tf_op jit(solution)/shard_map/ppermute | solution.py:433
  134.6 14.5 %collective-permute-start.37 = (bf16[128,2048]{1,0:T(8,128)(2,1)S(1)}, bf16[128,2048]{1,0:T(8,128)(2,1)}, u32[]{:S(2)}, u32[]{:S(2)}) collective-permute-start(bf16[128,2048]{1,0:T(8,128)(2,1)S(1)} %collective-permute-done.35.refs_1_), channel_id=1, source_target_pairs={{0,8},{4,12},{8,0},{12,4},{16,24},{20,28},{24,16},{28,20},{1,9},{5... | collective-permute-start | bytes 1572872 | tf_op jit(solution)/shard_map/ppermute | solution.py:433
  143.0 6.2 %collective-permute-start.24 = (bf16[128,2048]{1,0:T(8,128)(2,1)S(1)}, bf16[128,2048]{1,0:T(8,128)(2,1)}, u32[]{:S(2)}, u32[]{:S(2)}) collective-permute-start(bf16[128,2048]{1,0:T(8,128)(2,1)S(1)} %collective-permute-done.20.refs_3_), channel_id=1, source_target_pairs={{0,4},{4,0},{8,12},{12,8},{16,20},{20,16},{24,28},{28,24},{1,5},{5... | collective-permute-start | bytes 1572872 | tf_op jit(solution)/shard_map/ppermute | solution.py:433
  143.0 15.5 %collective-permute-start.38 = (bf16[128,2048]{1,0:T(8,128)(2,1)S(1)}, bf16[128,2048]{1,0:T(8,128)(2,1)}, u32[]{:S(2)}, u32[]{:S(2)}) collective-permute-start(bf16[128,2048]{1,0:T(8,128)(2,1)S(1)} %join_rows.3.refs_0_), channel_id=1, source_target_pairs={{0,4},{4,0},{8,12},{12,8},{16,20},{20,16},{24,28},{28,24},{1,5},{5... | collective-permute-start | bytes 1572872 | tf_op jit(solution)/shard_map/ppermute | solution.py:433
  143.5 15.0 %collective-permute-start.39 = (bf16[128,2048]{1,0:T(8,128)(2,1)S(1)}, bf16[128,2048]{1,0:T(8,128)(2,1)}, u32[]{:S(2)}, u32[]{:S(2)}) collective-permute-start(bf16[128,2048]{1,0:T(8,128)(2,1)S(1)} %collective-permute-done.35.refs_1_), channel_id=1, source_target_pairs={{0,4},{4,0},{8,12},{12,8},{16,20},{20,16},{24,28},{28,24},{1,5},{5... | collective-permute-start | bytes 1572872 | tf_op jit(solution)/shard_map/ppermute | solution.py:433
  143.6 14.9 %collective-permute-start.40 = (bf16[128,2048]{1,0:T(8,128)(2,1)}, bf16[128,2048]{1,0:T(8,128)(2,1)}, u32[]{:S(2)}, u32[]{:S(2)}) collective-permute-start(bf16[128,2048]{1,0:T(8,128)(2,1)} %collective-permute-done.36.refs_2_), channel_id=1, source_target_pairs={{0,4},{4,0},{8,12},{12,8},{16,20},{20,16},{24,28},{28,24},{1,5},{5... | collective-permute-start | bytes 1572872 | tf_op jit(solution)/shard_map/ppermute | solution.py:433
  149.1 9.4 %collective-permute-start.41 = (bf16[128,2048]{1,0:T(8,128)(2,1)}, bf16[128,2048]{1,0:T(8,128)(2,1)}, u32[]{:S(2)}, u32[]{:S(2)}) collective-permute-start(bf16[128,2048]{1,0:T(8,128)(2,1)} %collective-permute-done.37.refs_3_), channel_id=1, source_target_pairs={{0,4},{4,0},{8,12},{12,8},{16,20},{20,16},{24,28},{28,24},{1,5},{5... | collective-permute-start | bytes 1572872 | tf_op jit(solution)/shard_map/ppermute | solution.py:433
  157.9 17.8 %collective-permute-start.25 = (bf16[4,128,2048]{2,1,0:T(8,128)(2,1)}, bf16[4,128,2048]{2,1,0:T(8,128)(2,1)}, u32[]{:S(2)}, u32[]{:S(2)}) collective-permute-start(bf16[4,128,2048]{2,1,0:T(8,128)(2,1)} %expert_pieces.5), channel_id=1, source_target_pairs={{0,4},{4,0},{8,12},{12,8},{16,20},{20,16},{24,28},{28,24},{1,5},{5... | collective-permute-start | bytes 6291464 | tf_op jit(solution)/shard_map/ppermute | solution.py:433
  167.1 20.7 %collective-permute-start.42 = (bf16[4,128,2048]{2,1,0:T(8,128)(2,1)}, bf16[4,128,2048]{2,1,0:T(8,128)(2,1)S(1)}, u32[]{:S(2)}, u32[]{:S(2)}) collective-permute-start(bf16[4,128,2048]{2,1,0:T(8,128)(2,1)} %expert_pieces.7), channel_id=1, source_target_pairs={{0,4},{4,0},{8,12},{12,8},{16,20},{20,16},{24,28},{28,24},{1,5},{5... | collective-permute-start | bytes 6291464 | tf_op jit(solution)/shard_map/ppermute | solution.py:433
  177.6 14.3 %collective-permute-start.26 = (bf16[128,2048]{1,0:T(8,128)(2,1)S(1)}, bf16[128,2048]{1,0:T(8,128)(2,1)S(1)}, u32[]{:S(2)}, u32[]{:S(2)}) collective-permute-start(bf16[128,2048]{1,0:T(8,128)(2,1)S(1)} %get-tuple-element.98), channel_id=1, source_target_pairs={{0,16},{4,20},{8,24},{12,28},{16,0},{20,4},{24,8},{28,12},{1,17},{... | collective-permute-start | bytes 1572872 | tf_op jit(solution)/shard_map/ppermute | solution.py:433
  189.5 14.8 %collective-permute-start.43 = (bf16[128,2048]{1,0:T(8,128)(2,1)S(1)}, bf16[128,2048]{1,0:T(8,128)(2,1)S(1)}, u32[]{:S(2)}, u32[]{:S(2)}) collective-permute-start(bf16[128,2048]{1,0:T(8,128)(2,1)S(1)} %get-tuple-element.100), channel_id=1, source_target_pairs={{0,8},{4,12},{8,0},{12,4},{16,24},{20,28},{24,16},{28,20},{1,9},{5... | collective-permute-start | bytes 1572872 | tf_op jit(solution)/shard_map/ppermute | solution.py:433
  192.0 23.6 %copy-start.1 = (bf16[4,128,2048]{2,1,0:T(8,128)(2,1)S(1)}, bf16[4,128,2048]{2,1,0:T(8,128)(2,1)}, u32[]{:S(2)}) copy-start(bf16[4,128,2048]{2,1,0:T(8,128)(2,1)} %expert_pieces.4.near_ref) | copy-start | bytes 6291460
  192.0 23.6 %copy-start.16 = (f32[32,2048]{1,0:T(8,128)S(1)}, f32[32,2048]{1,0:T(8,128)}, u32[]{:S(2)}) copy-start(f32[32,2048]{1,0:T(8,128)} %get-tuple-element.68.attn_ref) | copy-start | bytes 786436
  192.0 23.6 %copy-start.24 = (s32[3]{0:T(128)S(1)}, s32[3]{0:T(128)}, u32[]{:S(2)}) copy-start(s32[3]{0:T(128)} %pad_add_fusion.me_ref.where_ref) | copy-start | bytes 40
  193.6 22.0 %collective-permute-start.27 = (bf16[128,2048]{1,0:T(8,128)(2,1)S(1)}, bf16[128,2048]{1,0:T(8,128)(2,1)S(1)}, u32[]{:S(2)}, u32[]{:S(2)}) collective-permute-start(bf16[128,2048]{1,0:T(8,128)(2,1)S(1)} %fusion.1), channel_id=1, source_target_pairs={{0,8},{4,12},{8,0},{12,4},{16,24},{20,28},{24,16},{28,20},{1,9},{5... | collective-permute-start | bytes 1572872 | tf_op jit(solution)/shard_map/ppermute | solution.py:433
  194.9 20.7 %collective-permute-start.28 = (bf16[128,2048]{1,0:T(8,128)(2,1)S(1)}, bf16[128,2048]{1,0:T(8,128)(2,1)S(1)}, u32[]{:S(2)}, u32[]{:S(2)}) collective-permute-start(bf16[128,2048]{1,0:T(8,128)(2,1)S(1)} %get-tuple-element.78), channel_id=1, source_target_pairs={{0,16},{4,20},{8,24},{12,28},{16,0},{20,4},{24,8},{28,12},{1,17},{... | collective-permute-start | bytes 1572872 | tf_op jit(solution)/shard_map/ppermute | solution.py:433
  204.6 17.6 %collective-permute-start.44 = (bf16[128,2048]{1,0:T(8,128)(2,1)S(1)}, bf16[128,2048]{1,0:T(8,128)(2,1)S(1)}, u32[]{:S(2)}, u32[]{:S(2)}) collective-permute-start(bf16[128,2048]{1,0:T(8,128)(2,1)S(1)} %fusion), channel_id=1, source_target_pairs={{0,16},{4,20},{8,24},{12,28},{16,0},{20,4},{24,8},{28,12},{1,17},{... | collective-permute-start | bytes 1572872 | tf_op jit(solution)/shard_map/ppermute | solution.py:433
  205.1 21.0 %collective-permute-start.45 = (bf16[128,2048]{1,0:T(8,128)(2,1)S(1)}, bf16[128,2048]{1,0:T(8,128)(2,1)S(1)}, u32[]{:S(2)}, u32[]{:S(2)}) collective-permute-start(bf16[128,2048]{1,0:T(8,128)(2,1)S(1)} %get-tuple-element.90), channel_id=1, source_target_pairs={{0,8},{4,12},{8,0},{12,4},{16,24},{20,28},{24,16},{28,20},{1,9},{5... | collective-permute-start | bytes 1572872 | tf_op jit(solution)/shard_map/ppermute | solution.py:433
  217.8 11.5 %collective-permute-start.29 = (bf16[128,512]{1,0:T(8,128)(2,1)S(1)}, bf16[128,512]{1,0:T(8,128)(2,1)S(1)}, u32[]{:S(2)}, u32[]{:S(2)}) collective-permute-start(bf16[128,512]{1,0:T(8,128)(2,1)S(1)} %get-tuple-element.80), channel_id=1, source_target_pairs={{0,1},{1,0},{2,3},{3,2},{4,5},{5,4},{6,7},{7,6},{8,9},{9,8},{10,11... | collective-permute-start | bytes 393224 | tf_op jit(solution)/shard_map/ppermute | solution.py:439
  217.8 18.5 %collective-permute-start.30 = (bf16[128,512]{1,0:T(8,128)(2,1)S(1)}, bf16[128,512]{1,0:T(8,128)(2,1)S(1)}, u32[]{:S(2)}, u32[]{:S(2)}) collective-permute-start(bf16[128,512]{1,0:T(8,128)(2,1)S(1)} %get-tuple-element.81), channel_id=1, source_target_pairs={{0,2},{1,3},{2,0},{3,1},{4,6},{5,7},{6,4},{7,5},{8,10},{9,11},{10,... | collective-permute-start | bytes 393224 | tf_op jit(solution)/shard_map/ppermute | solution.py:439
  220.0 16.3 %collective-permute-start.31 = (bf16[128,512]{1,0:T(8,128)(2,1)S(1)}, bf16[128,512]{1,0:T(8,128)(2,1)S(1)}, u32[]{:S(2)}, u32[]{:S(2)}) collective-permute-start(bf16[128,512]{1,0:T(8,128)(2,1)S(1)} %get-tuple-element.82), channel_id=1, source_target_pairs={{0,3},{1,2},{2,1},{3,0},{4,7},{5,6},{6,5},{7,4},{8,11},{9,10},{10,... | collective-permute-start | bytes 393224 | tf_op jit(solution)/shard_map/ppermute | solution.py:439
  227.1 12.4 %collective-permute-start.46 = (bf16[128,512]{1,0:T(8,128)(2,1)S(1)}, bf16[128,512]{1,0:T(8,128)(2,1)S(1)}, u32[]{:S(2)}, u32[]{:S(2)}) collective-permute-start(bf16[128,512]{1,0:T(8,128)(2,1)S(1)} %get-tuple-element.92), channel_id=1, source_target_pairs={{0,1},{1,0},{2,3},{3,2},{4,5},{5,4},{6,7},{7,6},{8,9},{9,8},{10,11... | collective-permute-start | bytes 393224 | tf_op jit(solution)/shard_map/ppermute | solution.py:439
  227.2 13.5 %collective-permute-start.47 = (bf16[128,512]{1,0:T(8,128)(2,1)S(1)}, bf16[128,512]{1,0:T(8,128)(2,1)S(1)}, u32[]{:S(2)}, u32[]{:S(2)}) collective-permute-start(bf16[128,512]{1,0:T(8,128)(2,1)S(1)} %get-tuple-element.93), channel_id=1, source_target_pairs={{0,2},{1,3},{2,0},{3,1},{4,6},{5,7},{6,4},{7,5},{8,10},{9,11},{10,... | collective-permute-start | bytes 393224 | tf_op jit(solution)/shard_map/ppermute | solution.py:439
  229.4 11.3 %collective-permute-start.48 = (bf16[128,512]{1,0:T(8,128)(2,1)S(1)}, bf16[128,512]{1,0:T(8,128)(2,1)S(1)}, u32[]{:S(2)}, u32[]{:S(2)}) collective-permute-start(bf16[128,512]{1,0:T(8,128)(2,1)S(1)} %get-tuple-element.94), channel_id=1, source_target_pairs={{0,3},{1,2},{2,1},{3,0},{4,7},{5,6},{6,5},{7,4},{8,11},{9,10},{10,... | collective-permute-start | bytes 393224 | tf_op jit(solution)/shard_map/ppermute | solution.py:439
  (37 other events, 197.9 us)

commit v5 on v4

--- a/solution.py
+++ b/solution.py
@@ -178,7 +178,7 @@
     return lax.fori_loop(0, (last - first) * step, hop, jnp.zeros((size, size), F32))
 
 
-def core_kernel(parts, me_ref, qkv_ref, steps_ref, gain_ref, near_ref, far_ref, w_hbm, *refs):
+def core_kernel(chunks, me_ref, qkv_ref, steps_ref, gain_ref, near_ref, far_ref, w_hbm, *refs):
     out_refs, (headed_ref, held_ref, w_ref, whole_ref, sem) = refs[:-5], refs[-5:]
     load = pltpu.make_async_copy(w_hbm, w_ref, sem)
     load.start()
@@ -200,21 +200,21 @@
         headed_ref[:, at] = (attended * scale * gain_ref[:, at]).astype(BF)
     load.wait()
     whole_ref[...] = mm(headed_ref[...], w_ref[...]).astype(BF)
-    part = rows // len(out_refs)
-    for at, ref in enumerate(out_refs):
-        chunk, mask = divmod(at, parts)
-        start = chunk * parts * part + (me_ref[2] ^ mask) * part
-        ref[...] = whole_ref[pl.ds(pl.multiple_of(start, part), part), :]
+    part = rows // len(out_refs) // chunks
+    for mask, ref in enumerate(out_refs):
+        for chunk in range(chunks):
+            start = chunk * len(out_refs) * part + (me_ref[2] ^ mask) * part
+            ref[chunk * part : (chunk + 1) * part] = whole_ref[pl.ds(pl.multiple_of(start, part), part), :]
 
 
 def core_out(where, qkv, steps, near, far, gain, w_out, chunks, parts):
     _, rows, chans = qkv.shape
     width = w_out.shape[1]
     vmem = pl.BlockSpec(memory_space=pltpu.VMEM)
-    outs = pl.pallas_call(
-        functools.partial(core_kernel, parts),
+    return pl.pallas_call(
+        functools.partial(core_kernel, chunks),
         in_specs=[pl.BlockSpec(memory_space=pltpu.SMEM)] + [vmem] * 5 + [pl.BlockSpec(memory_space=pltpu.HBM)],
-        out_shape=[jax.ShapeDtypeStruct((rows // chunks // parts, width), BF)] * (chunks * parts),
+        out_shape=[jax.ShapeDtypeStruct((rows // parts, width), BF)] * parts,
         scratch_shapes=[
             pltpu.VMEM((rows, chans), BF),
             pltpu.VMEM((2 * near.shape[0], *near.shape[1:]), BF),
@@ -225,7 +225,6 @@
         compiler_params=params(56),
         name="core_out",
     )(where, qkv, steps, gain.reshape(1, chans), near, far, w_out)
-    return [outs[chunk * parts : (chunk + 1) * parts] for chunk in range(chunks)]
 
 
 def grad_kernel(
@@ -269,36 +268,32 @@
     )(where, qkv, cot, steps, *fwd, *bwd)
 
 
-def norm_kernel(where_ref, x_ref, gain_ref, *refs):
-    del where_ref
-    parts, (out_ref, attn_ref) = refs[:-2], refs[-2:]
-    attn = functools.reduce(jnp.add, [part[...].astype(F32) for part in parts])
-    attn_ref[...] = attn
-    resid = x_ref[...].astype(F32) + attn
-    scale = lax.rsqrt(jnp.mean(resid * resid, axis=-1, keepdims=True) + 1e-06)
-    out_ref[...] = (resid * scale * gain_ref[...]).astype(BF)
-
-
-def norm_rows(chunk, where, x, parts, gain):
-    rows, width = parts[0].shape
-    count = len(parts)
-    block = pl.BlockSpec((rows, width), lambda i, where: (0, 0))
-    return pl.pallas_call(
-        norm_kernel,
-        grid_spec=pltpu.PrefetchScalarGridSpec(
-            num_scalar_prefetch=1,
-            grid=(1,),
-            in_specs=[
-                pl.BlockSpec((rows, width), lambda i, where: (chunk * count + where[2], 0)),
-                pl.BlockSpec((1, width), lambda i, where: (0, 0)),
-            ]
-            + [block] * count,
-            out_specs=[block, block],
-        ),
-        out_shape=[jax.ShapeDtypeStruct((rows, width), BF), jax.ShapeDtypeStruct((rows, width), F32)],
-        compiler_params=params(56),
+def norm_kernel(count, where_ref, x_ref, gain_ref, *refs):
+    chunks = (len(refs) - count) // 2
+    parts, outs, attns = refs[:count], refs[count : count + chunks], refs[count + chunks :]
+    rows = outs[0].shape[0]
+    for chunk, (out_ref, attn_ref) in enumerate(zip(outs, attns)):
+        at = slice(chunk * rows, (chunk + 1) * rows)
+        attn = functools.reduce(jnp.add, [part[at].astype(F32) for part in parts])
+        attn_ref[...] = attn
+        start = pl.multiple_of((chunk * count + where_ref[2]) * rows, rows)
+        resid = x_ref[pl.ds(start, rows), :].astype(F32) + attn
+        scale = lax.rsqrt(jnp.mean(resid * resid, axis=-1, keepdims=True) + 1e-06)
+        out_ref[...] = (resid * scale * gain_ref[...]).astype(BF)
+
+
+def norm_rows(where, x, parts, gain, chunks):
+    rows, width = parts[0].shape[0] // chunks, parts[0].shape[1]
+    vmem = pl.BlockSpec(memory_space=pltpu.VMEM)
+    outs = pl.pallas_call(
+        functools.partial(norm_kernel, len(parts)),
+        in_specs=[pl.BlockSpec(memory_space=pltpu.SMEM)] + [vmem] * (2 + len(parts)),
+        out_shape=[jax.ShapeDtypeStruct((rows, width), BF)] * chunks
+        + [jax.ShapeDtypeStruct((rows, width), F32)] * chunks,
+        compiler_params=params(12),
         name="moe_norm",
     )(where, x, gain.reshape(1, width), *parts)
+    return outs[:chunks], outs[chunks:]
 
 
 def join_kernel(where_ref, *refs):
@@ -323,9 +318,12 @@
 PAIR = 2
 
 
-def expert_kernel(masks, chunk, experts, where_ref, routes_ref, gate_hbm, up_hbm, down_hbm, *refs):
-    row_refs, (out_ref, rows_ref, gate_ref, up_ref, down_ref, sems, weight_sems) = refs[: len(masks)], refs[len(masks) :]
-    _, tok, width = out_ref.shape
+def expert_kernel(masks, chunk, experts, where_ref, near_routes, far_routes, gate_hbm, up_hbm, down_hbm, *refs):
+    row_refs, (near_ref, far_ref, rows_ref, gate_ref, up_ref, down_ref, sems, weight_sems) = (
+        refs[: len(masks)],
+        refs[len(masks) :],
+    )
+    _, tok, width = near_ref.shape
     steps = len(masks) // PAIR
     step = pl.program_id(0)
     slot = lax.rem(step, 2)
@@ -360,6 +358,7 @@
     mine = (here == where_ref[1]) | (here == where_ref[1] + experts) | (here == where_ref[1] + 2 * experts)
     square = (LANES, LANES)
     diagonal = lax.broadcasted_iota(jnp.int32, square, 0) == lax.broadcasted_iota(jnp.int32, square, 1)
+    is_near = step < steps // 2
     weights = []
     for part in range(PAIR):
         index = jnp.int32(masks[part] // 2)
@@ -367,7 +366,8 @@
             index = jnp.where(step == at, masks[PAIR * at + part] // 2, index)
         for block in range(tok // LANES):
             base = (chunk // LANES + block) * 3 * experts
-            table = routes_ref[index, base : base + 3 * experts, :].astype(F32)
+            at = slice(base, base + 3 * experts)
+            table = jnp.where(is_near, near_routes[index, at, :].astype(F32), far_routes[index, at, :].astype(F32))
             row = jnp.sum(jnp.where(mine, table, 0.0), axis=0, keepdims=True)
             weights.append(jnp.sum(jnp.where(diagonal, jnp.broadcast_to(row, square), 0.0), axis=1, keepdims=True))
 
@@ -383,28 +383,40 @@
         piece = mm(inner, down_ref[:, begin : begin + cols])
         for at, weight in enumerate(weights):
             part, row = divmod(at * LANES, tok)
-            scaled = piece[at * LANES : (at + 1) * LANES] * weight
-            out_ref[part, row : row + LANES, begin : begin + cols] = scaled.astype(BF)
-
-
-def expert_pieces(chunk, where, blocks, masks, gate, up, down, routes):
+            scaled = (piece[at * LANES : (at + 1) * LANES] * weight).astype(BF)
+
+            @pl.when(is_near)
+            def _(scaled=scaled, part=part, row=row):
+                near_ref[part, row : row + LANES, begin : begin + cols] = scaled
+
+            @pl.when(jnp.logical_not(is_near))
+            def _(scaled=scaled, part=part, row=row):
+                far_ref[part, row : row + LANES, begin : begin + cols] = scaled
+
+
+def expert_pieces(chunk, where, rows, evens, gate, up, down, routes):
+    masks = list(evens) + [mask | CORE for mask in evens]
+    blocks = [rows[mask] for mask in masks]
     tok, width = blocks[0].shape
     hidden = gate.shape[2]
     count = len(blocks)
-    experts = 2 * EXP_CTX * routes.shape[0]
+    half = count // PAIR // 2
+    experts = EXP_CTX * count
     route_rows = CHUNKS * tok // LANES * 3 * experts
     hbm = pl.BlockSpec(memory_space=pltpu.HBM)
+    piece = jax.ShapeDtypeStruct((count // 2, tok, width), BF)
+    table = pl.BlockSpec((count // 2, route_rows, LANES), lambda i: (0, 0, 0))
     return pl.pallas_call(
         functools.partial(expert_kernel, tuple(masks), chunk, experts),
         grid=(count // PAIR,),
-        in_specs=[
-            pl.BlockSpec(memory_space=pltpu.SMEM),
-            pl.BlockSpec((routes.shape[0], route_rows, LANES), lambda i: (0, 0, 0)),
-        ]
+        in_specs=[pl.BlockSpec(memory_space=pltpu.SMEM), table, table]
         + [hbm] * 3
         + [pl.BlockSpec(memory_space=pl.ANY)] * count,
-        out_specs=pl.BlockSpec((PAIR, tok, width), lambda i: (i, 0, 0)),
-        out_shape=jax.ShapeDtypeStruct((count, tok, width), BF),
+        out_specs=[
+            pl.BlockSpec((PAIR, tok, width), lambda i: (jnp.minimum(i, half - 1), 0, 0)),
+            pl.BlockSpec((PAIR, tok, width), lambda i: (jnp.maximum(i - half, 0), 0, 0)),
+        ],
+        out_shape=[piece, piece],
         scratch_shapes=[
             pltpu.VMEM((2, PAIR * tok, width), BF),
             pltpu.VMEM(gate.shape[1:], BF),
@@ -420,11 +432,10 @@
             transcendentals=count * tok * hidden,
         ),
         name="expert_pieces",
-    )(where, routes, gate, up, down, *blocks)
-
-
-CORE, ROW, COL = 1, 2, 4
-PLANE = 8
+    )(where, *routes, gate, up, down, *blocks)
+
+
+CORE = 1
 
 
 def swap(value, mask, keep=None):
@@ -440,44 +451,16 @@
     ]
 
 
-def spread_states(own, keep=None):
-    near = jnp.stack([own] + [swap(own, mask, keep) for mask in range(2, lax.axis_size("ctx"), 2)])
-    return near, swap(near, CORE)
-
-
-def hops(chunk):
-    return (ROW, COL) if chunk % 2 == 0 else (COL, ROW)
-
-
-def spread_rows(own, chunk):
-    count = lax.axis_size("ctx")
-    near = {0: own}
-    if count == PLANE:
-        first, second = hops(chunk)
-        near[first] = swap(own, first)
-        near[second] = swap(own, second)
-        near[ROW | COL] = swap(near[first], second)
-    else:
-        for mask in range(2, count, 2):
-            near[mask] = swap(own, mask)
-    return near | {mask | CORE: swap(rows, CORE) for mask, rows in near.items()}
+def spread_near(own, keep=None):
+    return jnp.stack([own] + [swap(own, mask, keep) for mask in range(2, lax.axis_size("ctx"), 2)])
 
 
 def plus(*terms):
     return functools.reduce(jnp.add, [term.astype(F32) for term in terms]).astype(BF)
 
 
-def collect_terms(near, far, evens, chunk):
-    arrived = swap(far, CORE)
-    sums = {mask: (near[at], arrived[at]) for at, mask in enumerate(evens)}
-    if lax.axis_size("ctx") == PLANE:
-        first, second = hops(chunk)
-        across = swap(plus(*sums[ROW | COL]), second)
-        direct, across = lax.optimization_barrier((plus(*sums[second]), across))
-        others = [swap(plus(*sums[first], across), first), swap(direct, second)]
-    else:
-        others = [swap(plus(*sums[mask]), mask) for mask in evens[1:]]
-    return arrived, others
+def after(value, other):
+    return lax.optimization_barrier((value, other))[0]
 
 
 def sum_kernel(where_ref, attn_ref, near_ref, arrived_ref, *refs):
@@ -519,28 +502,33 @@
     )(where, attn, near, arrived, *others)
 
 
-def final_kernel(where_ref, x_ref, *refs):
+def final_kernel(count, where_ref, x_ref, *refs):
     del where_ref
     out_ref = refs[-1]
-    terms = [x_ref[...]] + [ref[...] for ref in refs[:-1]]
-    out_ref[...] = functools.reduce(jnp.add, [term.astype(F32) for term in terms]).astype(BF)
-
-
-def final_sum(chunk, where, x, parts):
-    rows, cols = parts[0].shape
+    rows = refs[0].shape[0]
+    for chunk in range((len(refs) - 1) // count):
+        at = slice(chunk * rows, (chunk + 1) * rows)
+        terms = [x_ref[at]] + [ref[...] for ref in refs[chunk * count : (chunk + 1) * count]]
+        out_ref[at] = functools.reduce(jnp.add, [term.astype(F32) for term in terms]).astype(BF)
+
+
+def final_sum(where, x, parts):
+    rows, cols = parts[0][0].shape
+    total = len(parts) * rows
     block = pl.BlockSpec((rows, cols), lambda i, where: (0, 0))
     return pl.pallas_call(
-        final_kernel,
+        functools.partial(final_kernel, len(parts[0])),
         grid_spec=pltpu.PrefetchScalarGridSpec(
             num_scalar_prefetch=1,
             grid=(1,),
-            in_specs=[pl.BlockSpec((rows, cols), lambda i, where: (chunk, where[2]))] + [block] * len(parts),
-            out_specs=block,
+            in_specs=[pl.BlockSpec((total, cols), lambda i, where: (0, where[2]))]
+            + [block] * (len(parts) * len(parts[0])),
+            out_specs=pl.BlockSpec((total, cols), lambda i, where: (0, 0)),
         ),
-        out_shape=jax.ShapeDtypeStruct((rows, cols), BF),
-        compiler_params=params(56),
+        out_shape=jax.ShapeDtypeStruct((total, cols), BF),
+        compiler_params=params(12),
         name="layer_out",
-    )(where, x, *parts)
+    )(where, x, *[part for chunk in parts for part in chunk])
 
 
 CHUNKS = 2
@@ -575,32 +563,42 @@
     qkv, fwd, bwd = local_states(
         mixed, rim, jnp.transpose(conv_w, (1, 0, 2)), steps, grad_core, expert_ids.T, route_weights.T, experts
     )
-    fwd = spread_states(fwd, lambda source, target: source < target)
-    partials = core_out(where, qkv, steps, *fwd, norm_gain, w_out, CHUNKS, n_head)
-    bwd, partials = lax.optimization_barrier((bwd, partials))
-    parts = [send_heads(chunk) for chunk in partials]
-    bwd = spread_states(bwd)
-    parts[1], bwd = lax.optimization_barrier((parts[1], bwd))
-    attn, own = [], []
+    fwd = spread_near(fwd, lambda source, target: source < target)
+    fwd = (fwd, swap(fwd, CORE))
+    parts = core_out(where, qkv, steps, *fwd, norm_gain, w_out, CHUNKS, n_head)
+    bwd = spread_near(after(bwd, parts))
+    normed, attn = norm_rows(where, hidden_in, after(send_heads(parts), bwd), gain_moe, CHUNKS)
+    bwd = after(bwd, normed)
+    bwd = (bwd, swap(bwd, CORE))
+
+    evens = list(range(0, n_ctx, 2))
+    near, rows = [], []
+    own = join_rows(where, send_heads([normed[0]] * n_head))
     for chunk in range(CHUNKS):
-        normed, total = norm_rows(chunk, where, hidden_in, parts[chunk], gain_moe)
-        attn.append(total)
-        own.append(join_rows(where, send_heads([normed] * n_head)))
-    layer_out = []
+        near.append([own] + [swap(own, mask) for mask in evens[1:]])
+        if chunk + 1 < CHUNKS:
+            own = join_rows(where, send_heads([after(normed[chunk + 1], own)] * n_head))
+            near[chunk] = after(near[chunk], own)
     for chunk in range(CHUNKS):
-        rows = spread_rows(own[chunk], chunk)
-        evens = [mask for mask in rows if not mask & CORE]
-        near, far = (
-            expert_pieces(
-                chunk * chunk_rows, where, [rows[mask] for mask in masks], masks, w_gate, w_up, w_down, routes
-            )
-            for masks, routes in ((evens, bwd[0]), ([mask | CORE for mask in evens], bwd[1]))
-        )
-        arrived, others = collect_terms(near, far, evens, chunk)
-        sums = send_heads(sum_terms(where, attn[chunk], near, arrived, others, n_head))
-        layer_out.append(final_sum(chunk, where, hidden_in, sums))
+        rows.append({mask: part for mask, part in zip(evens, near[chunk])})
+        rows[chunk] |= {mask | CORE: swap(part, CORE) for mask, part in rows[chunk].items()}
+
+    sums, pending = [], []
+    for chunk in range(CHUNKS):
+        here, far = expert_pieces(chunk * chunk_rows, where, rows[chunk], evens, w_gate, w_up, w_down, bwd)
+        arrived = swap(far, CORE)
+        leaving = [plus(here[at], arrived[at]) for at in range(1, len(evens))]
+        if chunk + 1 < CHUNKS:
+            rows[chunk + 1] = after(rows[chunk + 1], leaving)
+        others = [swap(part, mask) for part, mask in zip(leaving, evens[1:])]
+        pending.append((here, arrived, others, leaving))
+    for chunk in range(CHUNKS):
+        here, arrived, others, _ = pending[chunk]
+        if chunk + 1 < CHUNKS:
+            others = after(others, pending[chunk + 1][3])
+        sums.append(send_heads(sum_terms(where, attn[chunk], here, arrived, others, n_head)))
     grads = core_grads(where, qkv, grad_core, steps, fwd, bwd)
-    return (jnp.concatenate(layer_out), *grads)
+    return (final_sum(where, hidden_in, sums), *grads)
 
 
 def solution(mesh):

time: 246 us -> 246 us (level)
  waiting for transfers between devices: 98.6 us -> 109 us
  Pallas kernels: 67.7 us -> 57.9 us
    pallas_call x5 -> x3, Pallas kernels: 16.2 us -> 8.11 us  [the longest x1 5.85 us: core_out(): pl.pallas_call(functools.partial(core_kernel, chunks), in_specs=[pl.Block...]
    ppermute x30, waiting for transfers between devices: 60.3 us -> 66.5 us  [swap(): lax.ppermute(value, 'ctx', [pair for pair in pairs if keep is None or kee...]
    ppermute x18 -> x15, waiting for transfers between devices: 37.2 us -> 41.6 us  [send_heads(): lax.ppermute(parts[mask], 'head', [(at, at ^ mask) for at in range(count)])]
    pallas_call x4 -> x2, Pallas kernels: 34.3 us -> 32.9 us  [expert_pieces(): pl.pallas_call(functools.partial(expert_kernel, tuple(masks), chunk, expe...]
    unnamed x104 -> x88, local copies, waits for them, and re-layouts: 8.13 us -> 8.62 us
    convert_element_type x4 -> x2, other arithmetic: 5.48 us -> 5.01 us  [plus(): functools.reduce(jnp.add, [term.astype(F32) for term in terms]).astype(BF)]
    ppermute x18 -> x15, starting transfers between devices: 27.1 us -> 27.3 us  [send_heads(): lax.ppermute(parts[mask], 'head', [(at, at ^ mask) for at in range(count)])]
  transfers between devices with their start and end apart: 49 -> 46, of which waited for: 24 -> 22; matrix products, arithmetic and copies ran while one was open for 2% -> 2% of each run, Pallas kernels for 21% -> 3%
where the time goes in v5:
time: 246 us; the launch traced here: 245 us
  waiting for transfers between devices  109 us (44%)
  starting transfers between devices  62.5 us (25%)
  Pallas kernels  57.9 us (24%)
  local copies, waits for them, and re-layouts  8.62 us (4%)
  other arithmetic  5.84 us (2%)
    ppermute x30, waiting for transfers between devices, swap(): lax.ppermute(value, 'ctx', [pair for pair in pairs if keep is None or kee...  66.5 us
    ppermute x15, waiting for transfers between devices, send_heads(): lax.ppermute(parts[mask], 'head', [(at, at ^ mask) for at in range(count)])  41.6 us
    pallas_call x2, Pallas kernels, expert_pieces(): pl.pallas_call(functools.partial(expert_kernel, tuple(masks), chunk, expe...  32.9 us
    ppermute x30, starting transfers between devices, swap(): lax.ppermute(value, 'ctx', [pair for pair in pairs if keep is None or kee...  32.9 us
    ppermute x15, starting transfers between devices, send_heads(): lax.ppermute(parts[mask], 'head', [(at, at ^ mask) for at in range(count)])  27.3 us
    unnamed x88, local copies, waits for them, and re-layouts  8.62 us
    pallas_call x1, Pallas kernels, project(): pl.pallas_call(qkv_kernel, in_specs=[hbm, vmem, hbm], out_shape=[jax.Shap...  6.68 us
    pallas_call x1, Pallas kernels, core_out(): pl.pallas_call(functools.partial(core_kernel, chunks), in_specs=[pl.Block...  5.85 us
  transfers between devices with their start and end apart: 46, of which 22 were waited for; matrix products, arithmetic and copies ran while one was open for 2% of the time, Pallas kernels for 3%

profile of v5, /device:TPU:0, one launch (start us, length us, event | category | flops | bytes accessed | tf_op | source)
XLA Modules:
  0.0 245.2 jit_solution(15505263765142513619)
XLA Ops:
  0.7 6.7 %qkv_projection.1 = (bf16[3,256,512]{2,1,0:T(8,128)(2,1)}, bf16[3,16,512]{2,1,0:T(8,128)(2,1)}) custom-call(bf16[256,2048]{1,0:T(8,128)(2,1)} %x_ref.3, f32[1,2048]{1,0:T(1,128)} %bitcast.47, bf16[3,2048,512]{2,1,0:T(8,128)(2,1)} %bitcast.40), custom_call_target="tpu_custom_call" | custom-call | tf_op jit(solution)/shard_map/qkv_projection/pallas_call | solution.py:58
  7.4 2.4 collective-permute-start
  9.7 1.1 collective-permute-done.rim_ref
  10.8 1.1 copy-done.12
  12.0 2.2 conv_states.1
  14.1 1.0 copy-done.5
  15.1 8.0 %collective-permute-start.3 = (bf16[576,128]{1,0:T(8,128)(2,1)S(1)}, bf16[576,128]{1,0:T(8,128)(2,1)S(1)}, u32[]{:S(2)}, u32[]{:S(2)}) collective-permute-start(bf16[576,128]{1,0:T(8,128)(2,1)S(1)} %get-tuple-element.57), channel_id=1, source_target_pairs={{0,24},{4,28},{8,16},{12,20},{1,25},{5,29},{9,17},{13,21},{2,26},{... | collective-permute-start | bytes 442376 | tf_op jit(solution)/shard_map/ppermute | solution.py:444
  23.1 1.3 collective-permute-start.2
  24.4 3.3 %collective-permute-start.1 = (bf16[576,128]{1,0:T(8,128)(2,1)S(1)}, bf16[576,128]{1,0:T(8,128)(2,1)S(1)}, u32[]{:S(2)}, u32[]{:S(2)}) collective-permute-start(bf16[576,128]{1,0:T(8,128)(2,1)S(1)} %get-tuple-element.57), channel_id=1, source_target_pairs={{0,8},{4,12},{16,24},{20,28},{1,9},{5,13},{17,25},{21,29},{2,10},{... | collective-permute-start | bytes 442376 | tf_op jit(solution)/shard_map/ppermute | solution.py:444
  27.8 1.1 collective-permute-done.2
  28.8 1.6 collective-permute-done.1
  31.2 1.3 collective-permute-done.4.far_ref.fwd_far
  32.6 0.8 copy-done.9
  33.4 5.9 %core_out.1 = (bf16[64,2048]{1,0:T(8,128)(2,1)}, bf16[64,2048]{1,0:T(8,128)(2,1)}, bf16[64,2048]{1,0:T(8,128)(2,1)}, bf16[64,2048]{1,0:T(8,128)(2,1)}) custom-call(s32[3]{0:T(128)} %pad_add_fusion.me_ref.where_ref, bf16[3,256,512]{2,1,0:T(8,128)(2,1)} %copy-done.5, f32[4,256]{1,0:T(4,128)} %bitcast.33, f32[1,512]{1,0:T(1,128)} %bitcast.48, ...), custom_call_target="tpu_custom_call" | custom-call | tf_op jit(solution)/shard_map/core_out/pallas_call | solution.py:214
  39.2 1.2 collective-permute-start.10
  40.5 3.0 %collective-permute-start.9 = (bf16[672,128]{1,0:T(8,128)(2,1)S(1)}, bf16[672,128]{1,0:T(8,128)(2,1)S(1)}, u32[]{:S(2)}, u32[]{:S(2)}) collective-permute-start(bf16[672,128]{1,0:T(8,128)(2,1)S(1)} %get-tuple-element.63), channel_id=1, source_target_pairs={{0,16},{4,20},{8,24},{12,28},{16,0},{20,4},{24,8},{28,12},{1,17},{... | collective-permute-start | bytes 516104 | tf_op jit(solution)/shard_map/ppermute | solution.py:444
  43.4 1.6 collective-permute-start.5
  45.0 2.6 %collective-permute-start.6 = (bf16[64,2048]{1,0:T(8,128)(2,1)}, bf16[64,2048]{1,0:T(8,128)(2,1)S(1)}, u32[]{:S(2)}, u32[]{:S(2)}) collective-permute-start(bf16[64,2048]{1,0:T(8,128)(2,1)} %get-tuple-element.60), channel_id=1, source_target_pairs={{0,2},{1,3},{2,0},{3,1},{4,6},{5,7},{6,4},{7,5},{8,10},{9,11},{10,... | collective-permute-start | bytes 786440 | tf_op jit(solution)/shard_map/ppermute | solution.py:450
  47.6 3.5 %collective-permute-start.7 = (bf16[64,2048]{1,0:T(8,128)(2,1)}, bf16[64,2048]{1,0:T(8,128)(2,1)S(1)}, u32[]{:S(2)}, u32[]{:S(2)}) collective-permute-start(bf16[64,2048]{1,0:T(8,128)(2,1)} %get-tuple-element.61), channel_id=1, source_target_pairs={{0,3},{1,2},{2,1},{3,0},{4,7},{5,6},{6,5},{7,4},{8,11},{9,10},{10,... | collective-permute-start | bytes 786440 | tf_op jit(solution)/shard_map/ppermute | solution.py:450
  51.2 5.1 %collective-permute-done.5.refs_1_ = bf16[64,2048]{1,0:T(8,128)(2,1)S(1)} collective-permute-done((bf16[64,2048]{1,0:T(8,128)(2,1)}, bf16[64,2048]{1,0:T(8,128)(2,1)S(1)}, u32[]{:S(2)}, u32[]{:S(2)}) %collective-permute-start.5) | collective-permute-done | bytes 262176 | tf_op jit(solution)/shard_map/ppermute | solution.py:450
  56.3 10.3 %collective-permute-done.6.refs_2_ = bf16[64,2048]{1,0:T(8,128)(2,1)S(1)} collective-permute-done((bf16[64,2048]{1,0:T(8,128)(2,1)}, bf16[64,2048]{1,0:T(8,128)(2,1)S(1)}, u32[]{:S(2)}, u32[]{:S(2)}) %collective-permute-start.6) | collective-permute-done | bytes 262176 | tf_op jit(solution)/shard_map/ppermute | solution.py:450
  66.6 0.9 copy-done.22
  67.6 0.9 moe_norm.1
  69.8 2.5 %collective-permute-start.14 = (bf16[32,2048]{1,0:T(8,128)(2,1)S(1)}, bf16[32,2048]{1,0:T(8,128)(2,1)S(1)}, u32[]{:S(2)}, u32[]{:S(2)}) collective-permute-start(bf16[32,2048]{1,0:T(8,128)(2,1)S(1)} %get-tuple-element.69.refs_0_), channel_id=1, source_target_pairs={{0,3},{1,2},{2,1},{3,0},{4,7},{5,6},{6,5},{7,4},{8,11},{9,10},{10,... | collective-permute-start | bytes 393224 | tf_op jit(solution)/shard_map/ppermute | solution.py:450
  72.3 4.5 %collective-permute-start.13 = (bf16[32,2048]{1,0:T(8,128)(2,1)S(1)}, bf16[32,2048]{1,0:T(8,128)(2,1)S(1)}, u32[]{:S(2)}, u32[]{:S(2)}) collective-permute-start(bf16[32,2048]{1,0:T(8,128)(2,1)S(1)} %get-tuple-element.69.refs_0_), channel_id=1, source_target_pairs={{0,2},{1,3},{2,0},{3,1},{4,6},{5,7},{6,4},{7,5},{8,10},{9,11},{10,... | collective-permute-start | bytes 393224 | tf_op jit(solution)/shard_map/ppermute | solution.py:450
  77.4 7.4 %collective-permute-done.13.refs_2_ = bf16[32,2048]{1,0:T(8,128)(2,1)S(1)} collective-permute-done((bf16[32,2048]{1,0:T(8,128)(2,1)S(1)}, bf16[32,2048]{1,0:T(8,128)(2,1)S(1)}, u32[]{:S(2)}, u32[]{:S(2)}) %collective-permute-start.13) | collective-permute-done | bytes 131104 | tf_op jit(solution)/shard_map/ppermute | solution.py:450
  85.4 1.5 collective-permute-start.17
  86.9 1.5 collective-permute-start.16
  88.9 2.6 %collective-permute-start.20 = (bf16[32,2048]{1,0:T(8,128)(2,1)S(1)}, bf16[32,2048]{1,0:T(8,128)(2,1)S(1)}, u32[]{:S(2)}, u32[]{:S(2)}) collective-permute-start(bf16[32,2048]{1,0:T(8,128)(2,1)S(1)} %get-tuple-element.72.refs_0_), channel_id=1, source_target_pairs={{0,3},{1,2},{2,1},{3,0},{4,7},{5,6},{6,5},{7,4},{8,11},{9,10},{10,... | collective-permute-start | bytes 393224 | tf_op jit(solution)/shard_map/ppermute | solution.py:450
  91.5 4.5 %collective-permute-done.20.refs_3_ = bf16[32,2048]{1,0:T(8,128)(2,1)S(1)} collective-permute-done((bf16[32,2048]{1,0:T(8,128)(2,1)S(1)}, bf16[32,2048]{1,0:T(8,128)(2,1)S(1)}, u32[]{:S(2)}, u32[]{:S(2)}) %collective-permute-start.20) | collective-permute-done | bytes 131104 | tf_op jit(solution)/shard_map/ppermute | solution.py:450
  96.0 5.4 %collective-permute-done.19.refs_2_ = bf16[32,2048]{1,0:T(8,128)(2,1)S(1)} collective-permute-done((bf16[32,2048]{1,0:T(8,128)(2,1)S(1)}, bf16[32,2048]{1,0:T(8,128)(2,1)S(1)}, u32[]{:S(2)}, u32[]{:S(2)}) %collective-permute-start.19) | collective-permute-done | bytes 131104 | tf_op jit(solution)/shard_map/ppermute | solution.py:450
  101.4 5.0 %collective-permute-done.18.refs_1_ = bf16[32,2048]{1,0:T(8,128)(2,1)S(1)} collective-permute-done((bf16[32,2048]{1,0:T(8,128)(2,1)S(1)}, bf16[32,2048]{1,0:T(8,128)(2,1)S(1)}, u32[]{:S(2)}, u32[]{:S(2)}) %collective-permute-start.18) | collective-permute-done | bytes 131104 | tf_op jit(solution)/shard_map/ppermute | solution.py:450
  107.8 2.8 %collective-permute-done.16.refs_2_ = bf16[128,2048]{1,0:T(8,128)(2,1)S(1)} collective-permute-done((bf16[128,2048]{1,0:T(8,128)(2,1)S(1)}, bf16[128,2048]{1,0:T(8,128)(2,1)S(1)}, u32[]{:S(2)}, u32[]{:S(2)}) %collective-permute-start.16) | collective-permute-done | bytes 524320 | tf_op jit(solution)/shard_map/ppermute | solution.py:444
  111.7 0.9 collective-permute-done.21.refs_4_
  112.6 1.5 collective-permute-done.22.refs_5_
  114.9 0.8 copy-done.43
  115.8 16.6 %expert_pieces.2 = (bf16[4,128,2048]{2,1,0:T(8,128)(2,1)}, bf16[4,128,2048]{2,1,0:T(8,128)(2,1)}) custom-call(s32[3]{0:T(128)} %pad_add_fusion.me_ref.where_ref, bf16[4,672,128]{2,1,0:T(8,128)(2,1)} %copy-done.7, bf16[4,672,128]{2,1,0:T(8,128)(2,1)} %copy-done.13, bf16[1,2048,512]{2,1,0:T(8,128)(2,1)} %gate_hbm.3, bf16[1,2048,512]{2,1,0:T(8,128)(2,1)} %up_hbm.3, ...), custom_call_target="tpu_custom_call" | custom-call | flops 6442450944 | bytes 8388608 | tf_op jit(solution)/shard_map/expert_pieces/pallas_call | solution.py:409
  132.5 1.5 collective-permute-start.34
  134.0 0.9 collective-permute-start.32
  134.9 1.1 collective-permute-start.30
  136.0 12.2 %collective-permute-done.34.refs_3_ = bf16[128,2048]{1,0:T(8,128)(2,1)S(1)} collective-permute-done((bf16[128,2048]{1,0:T(8,128)(2,1)S(1)}, bf16[128,2048]{1,0:T(8,128)(2,1)S(1)}, u32[]{:S(2)}, u32[]{:S(2)}) %collective-permute-start.34) | collective-permute-done | bytes 524320 | tf_op jit(solution)/shard_map/ppermute | solution.py:444
  148.2 10.6 %collective-permute-done.32.refs_2_ = bf16[128,2048]{1,0:T(8,128)(2,1)S(1)} collective-permute-done((bf16[128,2048]{1,0:T(8,128)(2,1)S(1)}, bf16[128,2048]{1,0:T(8,128)(2,1)S(1)}, u32[]{:S(2)}, u32[]{:S(2)}) %collective-permute-start.32) | collective-permute-done | bytes 524320 | tf_op jit(solution)/shard_map/ppermute | solution.py:444
  159.4 2.9 %fusion.2 = (bf16[128,2048]{1,0:T(8,128)(2,1)}, bf16[128,2048]{1,0:T(8,128)(2,1)}, bf16[128,2048]{1,0:T(8,128)(2,1)}) fusion(bf16[4,128,2048]{2,1,0:T(8,128)(2,1)S(1)} %collective-permute-done.25.arrived_ref, bf16[4,128,2048]{2,1,0:T(8,128)(2,1)} %get-tuple-element.77.near_ref), kind=kLoop, calls=%fused_computation.10 | loop fusion | flops 3145728 | bytes 4718592 | tf_op jit(solution)/shard_map/convert_element_type | solution.py:459
  163.9 16.4 %expert_pieces.3 = (bf16[4,128,2048]{2,1,0:T(8,128)(2,1)}, bf16[4,128,2048]{2,1,0:T(8,128)(2,1)}) custom-call(s32[3]{0:T(128)} %pad_add_fusion.me_ref.where_ref, bf16[4,672,128]{2,1,0:T(8,128)(2,1)} %copy-done.7, bf16[4,672,128]{2,1,0:T(8,128)(2,1)} %copy-done.13, bf16[1,2048,512]{2,1,0:T(8,128)(2,1)} %gate_hbm.3, bf16[1,2048,512]{2,1,0:T(8,128)(2,1)} %up_hbm.3, ...), custom_call_target="tpu_custom_call" | custom-call | flops 6442450944 | bytes 8388608 | tf_op jit(solution)/shard_map/expert_pieces/pallas_call | solution.py:409
  180.6 1.5 collective-permute-start.28
  182.1 0.9 collective-permute-start.27
  183.0 1.1 collective-permute-start.26
  184.8 2.1 fusion.5
  186.9 1.5 collective-permute-start.42
  188.4 0.9 collective-permute-start.41
  189.3 7.2 %collective-permute-done.28.refs_2_ = bf16[128,2048]{1,0:T(8,128)(2,1)S(1)} collective-permute-done((bf16[128,2048]{1,0:T(8,128)(2,1)}, bf16[128,2048]{1,0:T(8,128)(2,1)S(1)}, u32[]{:S(2)}, u32[]{:S(2)}) %collective-permute-start.28) | collective-permute-done | bytes 524320 | tf_op jit(solution)/shard_map/ppermute | solution.py:444
  196.5 0.9 collective-permute-start.40
  197.4 10.4 %collective-permute-done.27.refs_1_ = bf16[128,2048]{1,0:T(8,128)(2,1)S(1)} collective-permute-done((bf16[128,2048]{1,0:T(8,128)(2,1)}, bf16[128,2048]{1,0:T(8,128)(2,1)S(1)}, u32[]{:S(2)}, u32[]{:S(2)}) %collective-permute-start.27) | collective-permute-done | bytes 524320 | tf_op jit(solution)/shard_map/ppermute | solution.py:444
  207.8 1.1 sum_terms.2
  209.0 2.8 %collective-permute-start.38 = (bf16[128,512]{1,0:T(8,128)(2,1)S(1)}, bf16[128,512]{1,0:T(8,128)(2,1)S(1)}, u32[]{:S(2)}, u32[]{:S(2)}) collective-permute-start(bf16[128,512]{1,0:T(8,128)(2,1)S(1)} %get-tuple-element.94), channel_id=1, source_target_pairs={{0,2},{1,3},{2,0},{3,1},{4,6},{5,7},{6,4},{7,5},{8,10},{9,11},{10,... | collective-permute-start | bytes 393224 | tf_op jit(solution)/shard_map/ppermute | solution.py:450
  211.8 7.2 %collective-permute-done.42.refs_2_ = bf16[128,2048]{1,0:T(8,128)(2,1)S(1)} collective-permute-done((bf16[128,2048]{1,0:T(8,128)(2,1)S(1)}, bf16[128,2048]{1,0:T(8,128)(2,1)S(1)}, u32[]{:S(2)}, u32[]{:S(2)}) %collective-permute-start.42) | collective-permute-done | bytes 524320 | tf_op jit(solution)/shard_map/ppermute | solution.py:444
  219.0 2.2 collective-permute-start.39
  221.3 8.3 %collective-permute-done.41.refs_1_ = bf16[128,2048]{1,0:T(8,128)(2,1)S(1)} collective-permute-done((bf16[128,2048]{1,0:T(8,128)(2,1)S(1)}, bf16[128,2048]{1,0:T(8,128)(2,1)S(1)}, u32[]{:S(2)}, u32[]{:S(2)}) %collective-permute-start.41) | collective-permute-done | bytes 524320 | tf_op jit(solution)/shard_map/ppermute | solution.py:444
  229.6 1.1 sum_terms.3
  230.8 2.8 %collective-permute-start.44 = (bf16[128,512]{1,0:T(8,128)(2,1)S(1)}, bf16[128,512]{1,0:T(8,128)(2,1)S(1)}, u32[]{:S(2)}, u32[]{:S(2)}) collective-permute-start(bf16[128,512]{1,0:T(8,128)(2,1)S(1)} %get-tuple-element.99), channel_id=1, source_target_pairs={{0,2},{1,3},{2,0},{3,1},{4,6},{5,7},{6,4},{7,5},{8,10},{9,11},{10,... | collective-permute-start | bytes 393224 | tf_op jit(solution)/shard_map/ppermute | solution.py:450
  233.6 1.6 collective-permute-start.45
  235.2 4.7 %core_grads.1 = (bf16[256,512]{1,0:T(8,128)(2,1)}, bf16[256,512]{1,0:T(8,128)(2,1)}, bf16[256,512]{1,0:T(8,128)(2,1)}) custom-call(s32[3]{0:T(128)S(1)} %copy-done.24, bf16[3,256,512]{2,1,0:T(8,128)(2,1)S(1)} %copy-done.6, bf16[256,512]{1,0:T(8,128)(2,1)S(1)} %copy-done.11, f32[4,256]{1,0:T(4,128)S(1)} %bitcast.35, bf16[4,576,128]{2,1,0:T(8,128)(2,1)S(1)} %copy-done.4, ...), custom_call_target="tpu_custom_call" | custom-call | tf_op jit(solution)/shard_map/core_grads/pallas_call | solution.py:261
  239.9 3.9 %collective-permute-done.44.refs_6_ = bf16[128,512]{1,0:T(8,128)(2,1)S(1)} collective-permute-done((bf16[128,512]{1,0:T(8,128)(2,1)S(1)}, bf16[128,512]{1,0:T(8,128)(2,1)S(1)}, u32[]{:S(2)}, u32[]{:S(2)}) %collective-permute-start.44) | collective-permute-done | bytes 131104 | tf_op jit(solution)/shard_map/ppermute | solution.py:450
  243.8 1.4 layer_out.1
  (133 shorter events, 10.9 us)
Async XLA Ops:
  0.6 10.2 %copy-start.11 = (bf16[256,512]{1,0:T(8,128)(2,1)S(1)}, bf16[256,512]{1,0:T(8,128)(2,1)}, u32[]{:S(2)}) copy-start(bf16[256,512]{1,0:T(8,128)(2,1)} %cot_ref.3) | copy-start | bytes 786436
  0.6 10.2 %copy-start.25 = (f32[256,4]{0,1:T(4,128)S(1)}, f32[256,4]{0,1:T(4,128)}, u32[]{:S(2)}) copy-start(f32[256,4]{0,1:T(4,128)} %param.18) | copy-start | bytes 12292
  0.7 10.2 %copy-start.27 = (f32[4,3,512]{2,0,1:T(4,128)S(1)}, f32[4,3,512]{2,0,1:T(4,128)}, u32[]{:S(2)}) copy-start(f32[4,3,512]{2,0,1:T(4,128)} %param.17) | copy-start | bytes 73732
  0.7 10.2 %copy-start.28 = (s32[256,8]{0,1:T(8,128)S(1)}, s32[256,8]{0,1:T(8,128)}, u32[]{:S(2)}) copy-start(s32[256,8]{0,1:T(8,128)} %param.22) | copy-start | bytes 24580
  0.7 10.2 %copy-start.29 = (f32[256,8]{0,1:T(8,128)S(1)}, f32[256,8]{0,1:T(8,128)}, u32[]{:S(2)}) copy-start(f32[256,8]{0,1:T(8,128)} %param.23) | copy-start | bytes 24580
  7.4 3.4 %collective-permute-start = (bf16[3,16,512]{2,1,0:T(8,128)(2,1)}, bf16[3,16,512]{2,1,0:T(8,128)(2,1)S(1)}, u32[]{:S(2)}, u32[]{:S(2)}) collective-permute-start(bf16[3,16,512]{2,1,0:T(8,128)(2,1)} %get-tuple-element.55), channel_id=1, source_target_pairs={{0,4},{4,8},{8,12},{12,16},{16,20},{20,24},{24,28},{1,5},{5,9},{9,... | collective-permute-start | bytes 147464 | tf_op jit(solution)/shard_map/ppermute | solution.py:562
  15.1 12.7 %collective-permute-start.3 = (bf16[576,128]{1,0:T(8,128)(2,1)S(1)}, bf16[576,128]{1,0:T(8,128)(2,1)S(1)}, u32[]{:S(2)}, u32[]{:S(2)}) collective-permute-start(bf16[576,128]{1,0:T(8,128)(2,1)S(1)} %get-tuple-element.57), channel_id=1, source_target_pairs={{0,24},{4,28},{8,16},{12,20},{1,25},{5,29},{9,17},{13,21},{2,26},{... | collective-permute-start | bytes 442376 | tf_op jit(solution)/shard_map/ppermute | solution.py:444
  23.1 5.7 %collective-permute-start.2 = (bf16[576,128]{1,0:T(8,128)(2,1)S(1)}, bf16[576,128]{1,0:T(8,128)(2,1)S(1)}, u32[]{:S(2)}, u32[]{:S(2)}) collective-permute-start(bf16[576,128]{1,0:T(8,128)(2,1)S(1)} %get-tuple-element.57), channel_id=1, source_target_pairs={{0,16},{4,20},{8,24},{12,28},{1,17},{5,21},{9,25},{13,29},{2,18},{... | collective-permute-start | bytes 442376 | tf_op jit(solution)/shard_map/ppermute | solution.py:444
  24.4 6.0 %collective-permute-start.1 = (bf16[576,128]{1,0:T(8,128)(2,1)S(1)}, bf16[576,128]{1,0:T(8,128)(2,1)S(1)}, u32[]{:S(2)}, u32[]{:S(2)}) collective-permute-start(bf16[576,128]{1,0:T(8,128)(2,1)S(1)} %get-tuple-element.57), channel_id=1, source_target_pairs={{0,8},{4,12},{16,24},{20,28},{1,9},{5,13},{17,25},{21,29},{2,10},{... | collective-permute-start | bytes 442376 | tf_op jit(solution)/shard_map/ppermute | solution.py:444
  30.5 2.1 collective-permute-start.4
  33.4 33.2 %copy-start = (bf16[256,2048]{1,0:T(8,128)(2,1)S(1)}, bf16[256,2048]{1,0:T(8,128)(2,1)}, u32[]{:S(2)}) copy-start(bf16[256,2048]{1,0:T(8,128)(2,1)} %x_ref.3) | copy-start | bytes 3145732
  33.4 33.2 %copy-start.23 = (s32[3]{0:T(128)S(1)}, s32[3]{0:T(128)}, u32[]{:S(2)}) copy-start(s32[3]{0:T(128)} %pad_add_fusion.me_ref.where_ref) | copy-start | bytes 40
  33.4 33.2 %copy-start.30 = (f32[2048]{0:T(1024)S(1)}, f32[2048]{0:T(1024)}, u32[]{:S(2)}) copy-start(f32[2048]{0:T(1024)} %param.21) | copy-start | bytes 24580
  39.2 8.4 %collective-permute-start.10 = (bf16[672,128]{1,0:T(8,128)(2,1)S(1)}, bf16[672,128]{1,0:T(8,128)(2,1)S(1)}, u32[]{:S(2)}, u32[]{:S(2)}) collective-permute-start(bf16[672,128]{1,0:T(8,128)(2,1)S(1)} %get-tuple-element.63), channel_id=1, source_target_pairs={{0,24},{4,28},{8,16},{12,20},{16,8},{20,12},{24,0},{28,4},{1,25},{... | collective-permute-start | bytes 516104 | tf_op jit(solution)/shard_map/ppermute | solution.py:444
  40.5 10.6 %collective-permute-start.9 = (bf16[672,128]{1,0:T(8,128)(2,1)S(1)}, bf16[672,128]{1,0:T(8,128)(2,1)S(1)}, u32[]{:S(2)}, u32[]{:S(2)}) collective-permute-start(bf16[672,128]{1,0:T(8,128)(2,1)S(1)} %get-tuple-element.63), channel_id=1, source_target_pairs={{0,16},{4,20},{8,24},{12,28},{16,0},{20,4},{24,8},{28,12},{1,17},{... | collective-permute-start | bytes 516104 | tf_op jit(solution)/shard_map/ppermute | solution.py:444
  43.4 7.6 %collective-permute-start.8 = (bf16[672,128]{1,0:T(8,128)(2,1)S(1)}, bf16[672,128]{1,0:T(8,128)(2,1)S(1)}, u32[]{:S(2)}, u32[]{:S(2)}) collective-permute-start(bf16[672,128]{1,0:T(8,128)(2,1)S(1)} %get-tuple-element.63), channel_id=1, source_target_pairs={{0,8},{4,12},{8,0},{12,4},{16,24},{20,28},{24,16},{28,20},{1,9},{5... | collective-permute-start | bytes 516104 | tf_op jit(solution)/shard_map/ppermute | solution.py:444
  43.4 12.8 %collective-permute-start.5 = (bf16[64,2048]{1,0:T(8,128)(2,1)}, bf16[64,2048]{1,0:T(8,128)(2,1)S(1)}, u32[]{:S(2)}, u32[]{:S(2)}) collective-permute-start(bf16[64,2048]{1,0:T(8,128)(2,1)} %get-tuple-element.59), channel_id=1, source_target_pairs={{0,1},{1,0},{2,3},{3,2},{4,5},{5,4},{6,7},{7,6},{8,9},{9,8},{10,11... | collective-permute-start | bytes 786440 | tf_op jit(solution)/shard_map/ppermute | solution.py:450
  45.0 21.6 %collective-permute-start.6 = (bf16[64,2048]{1,0:T(8,128)(2,1)}, bf16[64,2048]{1,0:T(8,128)(2,1)S(1)}, u32[]{:S(2)}, u32[]{:S(2)}) collective-permute-start(bf16[64,2048]{1,0:T(8,128)(2,1)} %get-tuple-element.60), channel_id=1, source_target_pairs={{0,2},{1,3},{2,0},{3,1},{4,6},{5,7},{6,4},{7,5},{8,10},{9,11},{10,... | collective-permute-start | bytes 786440 | tf_op jit(solution)/shard_map/ppermute | solution.py:450
  47.6 19.0 %collective-permute-start.7 = (bf16[64,2048]{1,0:T(8,128)(2,1)}, bf16[64,2048]{1,0:T(8,128)(2,1)S(1)}, u32[]{:S(2)}, u32[]{:S(2)}) collective-permute-start(bf16[64,2048]{1,0:T(8,128)(2,1)} %get-tuple-element.61), channel_id=1, source_target_pairs={{0,3},{1,2},{2,1},{3,0},{4,7},{5,6},{6,5},{7,4},{8,11},{9,10},{10,... | collective-permute-start | bytes 786440 | tf_op jit(solution)/shard_map/ppermute | solution.py:450
  51.2 55.8 %copy-start.7 = (bf16[4,672,128]{2,1,0:T(8,128)(2,1)}, bf16[4,672,128]{2,1,0:T(8,128)(2,1)S(1)}, u32[]{:S(2)}) copy-start(bf16[4,672,128]{2,1,0:T(8,128)(2,1)S(1)} %pad_maximum_fusion.near_routes.bwd_near) | copy-start | bytes 2064388
  69.8 7.5 %collective-permute-start.14 = (bf16[32,2048]{1,0:T(8,128)(2,1)S(1)}, bf16[32,2048]{1,0:T(8,128)(2,1)S(1)}, u32[]{:S(2)}, u32[]{:S(2)}) collective-permute-start(bf16[32,2048]{1,0:T(8,128)(2,1)S(1)} %get-tuple-element.69.refs_0_), channel_id=1, source_target_pairs={{0,3},{1,2},{2,1},{3,0},{4,7},{5,6},{6,5},{7,4},{8,11},{9,10},{10,... | collective-permute-start | bytes 393224 | tf_op jit(solution)/shard_map/ppermute | solution.py:450
  72.3 12.4 %collective-permute-start.13 = (bf16[32,2048]{1,0:T(8,128)(2,1)S(1)}, bf16[32,2048]{1,0:T(8,128)(2,1)S(1)}, u32[]{:S(2)}, u32[]{:S(2)}) collective-permute-start(bf16[32,2048]{1,0:T(8,128)(2,1)S(1)} %get-tuple-element.69.refs_0_), channel_id=1, source_target_pairs={{0,2},{1,3},{2,0},{3,1},{4,6},{5,7},{6,4},{7,5},{8,10},{9,11},{10,... | collective-permute-start | bytes 393224 | tf_op jit(solution)/shard_map/ppermute | solution.py:450
  76.8 7.9 %collective-permute-start.12 = (bf16[32,2048]{1,0:T(8,128)(2,1)S(1)}, bf16[32,2048]{1,0:T(8,128)(2,1)S(1)}, u32[]{:S(2)}, u32[]{:S(2)}) collective-permute-start(bf16[32,2048]{1,0:T(8,128)(2,1)S(1)} %get-tuple-element.69.refs_0_), channel_id=1, source_target_pairs={{0,1},{1,0},{2,3},{3,2},{4,5},{5,4},{6,7},{7,6},{8,9},{9,8},{10,11... | collective-permute-start | bytes 393224 | tf_op jit(solution)/shard_map/ppermute | solution.py:450
  85.4 30.4 %copy-start.17 = (bf16[128,2048]{1,0:T(8,128)(2,1)}, bf16[128,2048]{1,0:T(8,128)(2,1)S(1)}, u32[]{:S(2)}) copy-start(bf16[128,2048]{1,0:T(8,128)(2,1)S(1)} %join_rows.2.refs_0_) | copy-start | bytes 1572868
  85.4 22.4 %collective-permute-start.17 = (bf16[128,2048]{1,0:T(8,128)(2,1)S(1)}, bf16[128,2048]{1,0:T(8,128)(2,1)S(1)}, u32[]{:S(2)}, u32[]{:S(2)}) collective-permute-start(bf16[128,2048]{1,0:T(8,128)(2,1)S(1)} %join_rows.2.refs_0_), channel_id=1, source_target_pairs={{0,24},{4,28},{8,16},{12,20},{16,8},{20,12},{24,0},{28,4},{1,25},{... | collective-permute-start | bytes 1572872 | tf_op jit(solution)/shard_map/ppermute | solution.py:444
  86.9 23.7 %collective-permute-start.16 = (bf16[128,2048]{1,0:T(8,128)(2,1)S(1)}, bf16[128,2048]{1,0:T(8,128)(2,1)S(1)}, u32[]{:S(2)}, u32[]{:S(2)}) collective-permute-start(bf16[128,2048]{1,0:T(8,128)(2,1)S(1)} %join_rows.2.refs_0_), channel_id=1, source_target_pairs={{0,16},{4,20},{8,24},{12,28},{16,0},{20,4},{24,8},{28,12},{1,17},{... | collective-permute-start | bytes 1572872 | tf_op jit(solution)/shard_map/ppermute | solution.py:444
  88.4 22.3 %collective-permute-start.15 = (bf16[128,2048]{1,0:T(8,128)(2,1)S(1)}, bf16[128,2048]{1,0:T(8,128)(2,1)S(1)}, u32[]{:S(2)}, u32[]{:S(2)}) collective-permute-start(bf16[128,2048]{1,0:T(8,128)(2,1)S(1)} %join_rows.2.refs_0_), channel_id=1, source_target_pairs={{0,8},{4,12},{8,0},{12,4},{16,24},{20,28},{24,16},{28,20},{1,9},{5... | collective-permute-start | bytes 1572872 | tf_op jit(solution)/shard_map/ppermute | solution.py:444
  88.9 7.1 %collective-permute-start.20 = (bf16[32,2048]{1,0:T(8,128)(2,1)S(1)}, bf16[32,2048]{1,0:T(8,128)(2,1)S(1)}, u32[]{:S(2)}, u32[]{:S(2)}) collective-permute-start(bf16[32,2048]{1,0:T(8,128)(2,1)S(1)} %get-tuple-element.72.refs_0_), channel_id=1, source_target_pairs={{0,3},{1,2},{2,1},{3,0},{4,7},{5,6},{6,5},{7,4},{8,11},{9,10},{10,... | collective-permute-start | bytes 393224 | tf_op jit(solution)/shard_map/ppermute | solution.py:450
  91.5 10.0 %collective-permute-start.19 = (bf16[32,2048]{1,0:T(8,128)(2,1)S(1)}, bf16[32,2048]{1,0:T(8,128)(2,1)S(1)}, u32[]{:S(2)}, u32[]{:S(2)}) collective-permute-start(bf16[32,2048]{1,0:T(8,128)(2,1)S(1)} %get-tuple-element.72.refs_0_), channel_id=1, source_target_pairs={{0,2},{1,3},{2,0},{3,1},{4,6},{5,7},{6,4},{7,5},{8,10},{9,11},{10,... | collective-permute-start | bytes 393224 | tf_op jit(solution)/shard_map/ppermute | solution.py:450
  96.0 15.7 %collective-permute-start.11 = (bf16[4,672,128]{2,1,0:T(8,128)(2,1)S(1)}, bf16[4,672,128]{2,1,0:T(8,128)(2,1)S(1)}, u32[]{:S(2)}, u32[]{:S(2)}) collective-permute-start(bf16[4,672,128]{2,1,0:T(8,128)(2,1)S(1)} %pad_maximum_fusion.near_routes.bwd_near), channel_id=1, source_target_pairs={{0,4},{4,0},{8,12},{12,8},{16,20},{20,16},{24,28},{28,24},{1,5},{5... | collective-permute-start | bytes 2064392 | tf_op jit(solution)/shard_map/ppermute | solution.py:444
  101.4 5.0 %collective-permute-start.18 = (bf16[32,2048]{1,0:T(8,128)(2,1)S(1)}, bf16[32,2048]{1,0:T(8,128)(2,1)S(1)}, u32[]{:S(2)}, u32[]{:S(2)}) collective-permute-start(bf16[32,2048]{1,0:T(8,128)(2,1)S(1)} %get-tuple-element.72.refs_0_), channel_id=1, source_target_pairs={{0,1},{1,0},{2,3},{3,2},{4,5},{5,4},{6,7},{7,6},{8,9},{9,8},{10,11... | collective-permute-start | bytes 393224 | tf_op jit(solution)/shard_map/ppermute | solution.py:450
  107.8 8.0 %copy-start.31 = (bf16[128,2048]{1,0:T(8,128)(2,1)}, bf16[128,2048]{1,0:T(8,128)(2,1)S(1)}, u32[]{:S(2)}) copy-start(bf16[128,2048]{1,0:T(8,128)(2,1)S(1)} %collective-permute-done.17.refs_3_) | copy-start | bytes 1572868
  110.6 2.0 collective-permute-start.21
  110.7 3.4 %collective-permute-start.22 = (bf16[128,2048]{1,0:T(8,128)(2,1)S(1)}, bf16[128,2048]{1,0:T(8,128)(2,1)S(1)}, u32[]{:S(2)}, u32[]{:S(2)}) collective-permute-start(bf16[128,2048]{1,0:T(8,128)(2,1)S(1)} %collective-permute-done.15.refs_1_), channel_id=1, source_target_pairs={{0,4},{4,0},{8,12},{12,8},{16,20},{20,16},{24,28},{28,24},{1,5},{5... | collective-permute-start | bytes 1572872 | tf_op jit(solution)/shard_map/ppermute | solution.py:444
  111.2 3.6 %collective-permute-start.23 = (bf16[128,2048]{1,0:T(8,128)(2,1)S(1)}, bf16[128,2048]{1,0:T(8,128)(2,1)S(1)}, u32[]{:S(2)}, u32[]{:S(2)}) collective-permute-start(bf16[128,2048]{1,0:T(8,128)(2,1)S(1)} %collective-permute-done.16.refs_2_), channel_id=1, source_target_pairs={{0,4},{4,0},{8,12},{12,8},{16,20},{20,16},{24,28},{28,24},{1,5},{5... | collective-permute-start | bytes 1572872 | tf_op jit(solution)/shard_map/ppermute | solution.py:444
  111.3 4.5 %collective-permute-start.24 = (bf16[128,2048]{1,0:T(8,128)(2,1)S(1)}, bf16[128,2048]{1,0:T(8,128)(2,1)}, u32[]{:S(2)}, u32[]{:S(2)}) collective-permute-start(bf16[128,2048]{1,0:T(8,128)(2,1)S(1)} %collective-permute-done.17.refs_3_), channel_id=1, source_target_pairs={{0,4},{4,0},{8,12},{12,8},{16,20},{20,16},{24,28},{28,24},{1,5},{5... | collective-permute-start | bytes 1572872 | tf_op jit(solution)/shard_map/ppermute | solution.py:444
  111.7 20.8 %copy-start.16 = (bf16[128,2048]{1,0:T(8,128)(2,1)S(1)}, bf16[128,2048]{1,0:T(8,128)(2,1)}, u32[]{:S(2)}) copy-start(bf16[128,2048]{1,0:T(8,128)(2,1)} %copy-done.15) | copy-start | bytes 1572868
  132.3 27.1 %collective-permute-start.25 = (bf16[4,128,2048]{2,1,0:T(8,128)(2,1)}, bf16[4,128,2048]{2,1,0:T(8,128)(2,1)S(1)}, u32[]{:S(2)}, u32[]{:S(2)}) collective-permute-start(bf16[4,128,2048]{2,1,0:T(8,128)(2,1)} %get-tuple-element.78), channel_id=1, source_target_pairs={{0,4},{4,0},{8,12},{12,8},{16,20},{20,16},{24,28},{28,24},{1,5},{5... | collective-permute-start | bytes 6291464 | tf_op jit(solution)/shard_map/ppermute | solution.py:444
  132.5 15.7 %collective-permute-start.34 = (bf16[128,2048]{1,0:T(8,128)(2,1)S(1)}, bf16[128,2048]{1,0:T(8,128)(2,1)S(1)}, u32[]{:S(2)}, u32[]{:S(2)}) collective-permute-start(bf16[128,2048]{1,0:T(8,128)(2,1)S(1)} %copy-done.16), channel_id=1, source_target_pairs={{0,24},{4,28},{8,16},{12,20},{16,8},{20,12},{24,0},{28,4},{1,25},{... | collective-permute-start | bytes 1572872 | tf_op jit(solution)/shard_map/ppermute | solution.py:444
  134.0 24.9 %collective-permute-start.32 = (bf16[128,2048]{1,0:T(8,128)(2,1)S(1)}, bf16[128,2048]{1,0:T(8,128)(2,1)S(1)}, u32[]{:S(2)}, u32[]{:S(2)}) collective-permute-start(bf16[128,2048]{1,0:T(8,128)(2,1)S(1)} %copy-done.16), channel_id=1, source_target_pairs={{0,16},{4,20},{8,24},{12,28},{16,0},{20,4},{24,8},{28,12},{1,17},{... | collective-permute-start | bytes 1572872 | tf_op jit(solution)/shard_map/ppermute | solution.py:444
  134.9 24.0 %collective-permute-start.30 = (bf16[128,2048]{1,0:T(8,128)(2,1)S(1)}, bf16[128,2048]{1,0:T(8,128)(2,1)S(1)}, u32[]{:S(2)}, u32[]{:S(2)}) collective-permute-start(bf16[128,2048]{1,0:T(8,128)(2,1)S(1)} %copy-done.16), channel_id=1, source_target_pairs={{0,8},{4,12},{8,0},{12,4},{16,24},{20,28},{24,16},{28,20},{1,9},{5... | collective-permute-start | bytes 1572872 | tf_op jit(solution)/shard_map/ppermute | solution.py:444
  136.0 26.3 %collective-permute-start.29 = (bf16[128,2048]{1,0:T(8,128)(2,1)S(1)}, bf16[128,2048]{1,0:T(8,128)(2,1)S(1)}, u32[]{:S(2)}, u32[]{:S(2)}) collective-permute-start(bf16[128,2048]{1,0:T(8,128)(2,1)S(1)} %copy-done.16), channel_id=1, source_target_pairs={{0,4},{4,0},{8,12},{12,8},{16,20},{20,16},{24,28},{28,24},{1,5},{5... | collective-permute-start | bytes 1572872 | tf_op jit(solution)/shard_map/ppermute | solution.py:444
  148.2 14.1 %copy-start.34 = (bf16[128,2048]{1,0:T(8,128)(2,1)}, bf16[128,2048]{1,0:T(8,128)(2,1)S(1)}, u32[]{:S(2)}) copy-start(bf16[128,2048]{1,0:T(8,128)(2,1)S(1)} %collective-permute-done.34.refs_3_) | copy-start | bytes 1572868
  148.2 14.1 %collective-permute-start.35 = (bf16[128,2048]{1,0:T(8,128)(2,1)S(1)}, bf16[128,2048]{1,0:T(8,128)(2,1)S(1)}, u32[]{:S(2)}, u32[]{:S(2)}) collective-permute-start(bf16[128,2048]{1,0:T(8,128)(2,1)S(1)} %collective-permute-done.34.refs_3_), channel_id=1, source_target_pairs={{0,4},{4,0},{8,12},{12,8},{16,20},{20,16},{24,28},{28,24},{1,5},{5... | collective-permute-start | bytes 1572872 | tf_op jit(solution)/shard_map/ppermute | solution.py:444
  158.9 3.5 %collective-permute-start.33 = (bf16[128,2048]{1,0:T(8,128)(2,1)S(1)}, bf16[128,2048]{1,0:T(8,128)(2,1)S(1)}, u32[]{:S(2)}, u32[]{:S(2)}) collective-permute-start(bf16[128,2048]{1,0:T(8,128)(2,1)S(1)} %collective-permute-done.32.refs_2_), channel_id=1, source_target_pairs={{0,4},{4,0},{8,12},{12,8},{16,20},{20,16},{24,28},{28,24},{1,5},{5... | collective-permute-start | bytes 1572872 | tf_op jit(solution)/shard_map/ppermute | solution.py:444
  158.9 3.5 %collective-permute-start.31 = (bf16[128,2048]{1,0:T(8,128)(2,1)S(1)}, bf16[128,2048]{1,0:T(8,128)(2,1)S(1)}, u32[]{:S(2)}, u32[]{:S(2)}) collective-permute-start(bf16[128,2048]{1,0:T(8,128)(2,1)S(1)} %collective-permute-done.30.refs_1_), channel_id=1, source_target_pairs={{0,4},{4,0},{8,12},{12,8},{16,20},{20,16},{24,28},{28,24},{1,5},{5... | collective-permute-start | bytes 1572872 | tf_op jit(solution)/shard_map/ppermute | solution.py:444
  180.3 4.4 %collective-permute-start.36 = (bf16[4,128,2048]{2,1,0:T(8,128)(2,1)}, bf16[4,128,2048]{2,1,0:T(8,128)(2,1)S(1)}, u32[]{:S(2)}, u32[]{:S(2)}) collective-permute-start(bf16[4,128,2048]{2,1,0:T(8,128)(2,1)} %get-tuple-element.88), channel_id=1, source_target_pairs={{0,4},{4,0},{8,12},{12,8},{16,20},{20,16},{24,28},{28,24},{1,5},{5... | collective-permute-start | bytes 6291464 | tf_op jit(solution)/shard_map/ppermute | solution.py:444
  180.6 15.9 %collective-permute-start.28 = (bf16[128,2048]{1,0:T(8,128)(2,1)}, bf16[128,2048]{1,0:T(8,128)(2,1)S(1)}, u32[]{:S(2)}, u32[]{:S(2)}) collective-permute-start(bf16[128,2048]{1,0:T(8,128)(2,1)} %get-tuple-element.107), channel_id=1, source_target_pairs={{0,24},{4,28},{8,16},{12,20},{16,8},{20,12},{24,0},{28,4},{1,25},{... | collective-permute-start | bytes 1572872 | tf_op jit(solution)/shard_map/ppermute | solution.py:444
  182.1 25.7 %collective-permute-start.27 = (bf16[128,2048]{1,0:T(8,128)(2,1)}, bf16[128,2048]{1,0:T(8,128)(2,1)S(1)}, u32[]{:S(2)}, u32[]{:S(2)}) collective-permute-start(bf16[128,2048]{1,0:T(8,128)(2,1)} %get-tuple-element.108), channel_id=1, source_target_pairs={{0,16},{4,20},{8,24},{12,28},{16,0},{20,4},{24,8},{28,12},{1,17},{... | collective-permute-start | bytes 1572872 | tf_op jit(solution)/shard_map/ppermute | solution.py:444
  183.0 24.8 %collective-permute-start.26 = (bf16[128,2048]{1,0:T(8,128)(2,1)}, bf16[128,2048]{1,0:T(8,128)(2,1)S(1)}, u32[]{:S(2)}, u32[]{:S(2)}) collective-permute-start(bf16[128,2048]{1,0:T(8,128)(2,1)} %get-tuple-element.109), channel_id=1, source_target_pairs={{0,8},{4,12},{8,0},{12,4},{16,24},{20,28},{24,16},{28,20},{1,9},{5... | collective-permute-start | bytes 1572872 | tf_op jit(solution)/shard_map/ppermute | solution.py:444
  184.8 23.0 %copy-start.1 = (bf16[4,128,2048]{2,1,0:T(8,128)(2,1)S(1)}, bf16[4,128,2048]{2,1,0:T(8,128)(2,1)}, u32[]{:S(2)}) copy-start(bf16[4,128,2048]{2,1,0:T(8,128)(2,1)} %get-tuple-element.77.near_ref) | copy-start | bytes 6291460
  184.8 23.0 %copy-start.21 = (f32[32,2048]{1,0:T(8,128)S(1)}, f32[32,2048]{1,0:T(8,128)}, u32[]{:S(2)}) copy-start(f32[32,2048]{1,0:T(8,128)} %copy-done.20) | copy-start | bytes 786436
  184.8 23.0 %copy-start.24 = (s32[3]{0:T(128)S(1)}, s32[3]{0:T(128)}, u32[]{:S(2)}) copy-start(s32[3]{0:T(128)} %pad_add_fusion.me_ref.where_ref) | copy-start | bytes 40
  186.9 32.1 %collective-permute-start.42 = (bf16[128,2048]{1,0:T(8,128)(2,1)S(1)}, bf16[128,2048]{1,0:T(8,128)(2,1)S(1)}, u32[]{:S(2)}, u32[]{:S(2)}) collective-permute-start(bf16[128,2048]{1,0:T(8,128)(2,1)S(1)} %get-tuple-element.104), channel_id=1, source_target_pairs={{0,24},{4,28},{8,16},{12,20},{16,8},{20,12},{24,0},{28,4},{1,25},{... | collective-permute-start | bytes 1572872 | tf_op jit(solution)/shard_map/ppermute | solution.py:444
  188.4 41.2 %collective-permute-start.41 = (bf16[128,2048]{1,0:T(8,128)(2,1)S(1)}, bf16[128,2048]{1,0:T(8,128)(2,1)S(1)}, u32[]{:S(2)}, u32[]{:S(2)}) collective-permute-start(bf16[128,2048]{1,0:T(8,128)(2,1)S(1)} %get-tuple-element.105), channel_id=1, source_target_pairs={{0,16},{4,20},{8,24},{12,28},{16,0},{20,4},{24,8},{28,12},{1,17},{... | collective-permute-start | bytes 1572872 | tf_op jit(solution)/shard_map/ppermute | solution.py:444
  196.5 33.1 %collective-permute-start.40 = (bf16[128,2048]{1,0:T(8,128)(2,1)S(1)}, bf16[128,2048]{1,0:T(8,128)(2,1)S(1)}, u32[]{:S(2)}, u32[]{:S(2)}) collective-permute-start(bf16[128,2048]{1,0:T(8,128)(2,1)S(1)} %get-tuple-element.106), channel_id=1, source_target_pairs={{0,8},{4,12},{8,0},{12,4},{16,24},{20,28},{24,16},{28,20},{1,9},{5... | collective-permute-start | bytes 1572872 | tf_op jit(solution)/shard_map/ppermute | solution.py:444
  207.8 21.8 %copy-start.2 = (bf16[4,128,2048]{2,1,0:T(8,128)(2,1)S(1)}, bf16[4,128,2048]{2,1,0:T(8,128)(2,1)}, u32[]{:S(2)}) copy-start(bf16[4,128,2048]{2,1,0:T(8,128)(2,1)} %get-tuple-element.87.near_ref) | copy-start | bytes 6291460
  207.8 21.7 %copy-start.19 = (f32[32,2048]{1,0:T(8,128)S(1)}, f32[32,2048]{1,0:T(8,128)}, u32[]{:S(2)}) copy-start(f32[32,2048]{1,0:T(8,128)} %copy-done.18) | copy-start | bytes 786436
  208.9 24.7 %collective-permute-start.37 = (bf16[128,512]{1,0:T(8,128)(2,1)S(1)}, bf16[128,512]{1,0:T(8,128)(2,1)S(1)}, u32[]{:S(2)}, u32[]{:S(2)}) collective-permute-start(bf16[128,512]{1,0:T(8,128)(2,1)S(1)} %get-tuple-element.93), channel_id=1, source_target_pairs={{0,1},{1,0},{2,3},{3,2},{4,5},{5,4},{6,7},{7,6},{8,9},{9,8},{10,11... | collective-permute-start | bytes 393224 | tf_op jit(solution)/shard_map/ppermute | solution.py:450
  209.0 30.9 %collective-permute-start.38 = (bf16[128,512]{1,0:T(8,128)(2,1)S(1)}, bf16[128,512]{1,0:T(8,128)(2,1)S(1)}, u32[]{:S(2)}, u32[]{:S(2)}) collective-permute-start(bf16[128,512]{1,0:T(8,128)(2,1)S(1)} %get-tuple-element.94), channel_id=1, source_target_pairs={{0,2},{1,3},{2,0},{3,1},{4,6},{5,7},{6,4},{7,5},{8,10},{9,11},{10,... | collective-permute-start | bytes 393224 | tf_op jit(solution)/shard_map/ppermute | solution.py:450
  219.0 20.9 %collective-permute-start.39 = (bf16[128,512]{1,0:T(8,128)(2,1)S(1)}, bf16[128,512]{1,0:T(8,128)(2,1)S(1)}, u32[]{:S(2)}, u32[]{:S(2)}) collective-permute-start(bf16[128,512]{1,0:T(8,128)(2,1)S(1)} %get-tuple-element.95), channel_id=1, source_target_pairs={{0,3},{1,2},{2,1},{3,0},{4,7},{5,6},{6,5},{7,4},{8,11},{9,10},{10,... | collective-permute-start | bytes 393224 | tf_op jit(solution)/shard_map/ppermute | solution.py:450
  230.7 9.2 %collective-permute-start.43 = (bf16[128,512]{1,0:T(8,128)(2,1)S(1)}, bf16[128,512]{1,0:T(8,128)(2,1)S(1)}, u32[]{:S(2)}, u32[]{:S(2)}) collective-permute-start(bf16[128,512]{1,0:T(8,128)(2,1)S(1)} %get-tuple-element.98), channel_id=1, source_target_pairs={{0,1},{1,0},{2,3},{3,2},{4,5},{5,4},{6,7},{7,6},{8,9},{9,8},{10,11... | collective-permute-start | bytes 393224 | tf_op jit(solution)/shard_map/ppermute | solution.py:450
  230.8 13.0 %collective-permute-start.44 = (bf16[128,512]{1,0:T(8,128)(2,1)S(1)}, bf16[128,512]{1,0:T(8,128)(2,1)S(1)}, u32[]{:S(2)}, u32[]{:S(2)}) collective-permute-start(bf16[128,512]{1,0:T(8,128)(2,1)S(1)} %get-tuple-element.99), channel_id=1, source_target_pairs={{0,2},{1,3},{2,0},{3,1},{4,6},{5,7},{6,4},{7,5},{8,10},{9,11},{10,... | collective-permute-start | bytes 393224 | tf_op jit(solution)/shard_map/ppermute | solution.py:450
  233.6 10.2 %collective-permute-start.45 = (bf16[128,512]{1,0:T(8,128)(2,1)S(1)}, bf16[128,512]{1,0:T(8,128)(2,1)S(1)}, u32[]{:S(2)}, u32[]{:S(2)}) collective-permute-start(bf16[128,512]{1,0:T(8,128)(2,1)S(1)} %get-tuple-element.100), channel_id=1, source_target_pairs={{0,3},{1,2},{2,1},{3,0},{4,7},{5,6},{6,5},{7,4},{8,11},{9,10},{10,... | collective-permute-start | bytes 393224 | tf_op jit(solution)/shard_map/ppermute | solution.py:450
  (26 other events, 66.5 us)

commit v6 on v5

--- a/solution.py
+++ b/solution.py
@@ -293,7 +293,7 @@
         compiler_params=params(12),
         name="moe_norm",
     )(where, x, gain.reshape(1, width), *parts)
-    return outs[:chunks], outs[chunks:]
+    return list(outs[:chunks]), list(outs[chunks:])
 
 
 def join_kernel(where_ref, *refs):
@@ -318,35 +318,21 @@
 PAIR = 2
 
 
-def expert_kernel(masks, chunk, experts, where_ref, near_routes, far_routes, gate_hbm, up_hbm, down_hbm, *refs):
-    row_refs, (near_ref, far_ref, rows_ref, gate_ref, up_ref, down_ref, sems, weight_sems) = (
-        refs[: len(masks)],
-        refs[len(masks) :],
-    )
+def expert_kernel(masks, chunk, experts, where_ref, near_routes, far_routes, gate_ref, up_ref, down_ref, *refs):
+    row_refs, (near_ref, far_ref, rows_ref, sems) = refs[: len(masks)], refs[len(masks) :]
     _, tok, width = near_ref.shape
     steps = len(masks) // PAIR
     step = pl.program_id(0)
     slot = lax.rem(step, 2)
-    loads = [
-        pltpu.make_async_copy(source.at[0], target, weight_sems.at[at])
-        for at, (source, target) in enumerate(((gate_hbm, gate_ref), (up_hbm, up_ref), (down_hbm, down_ref)))
-    ]
 
     def start(at):
         for part in range(PAIR):
             target = rows_ref.at[at % 2, pl.ds(part * tok, tok)]
             pltpu.make_async_copy(row_refs[PAIR * at + part], target, sems.at[at % 2]).start()
 
-    def ready(at):
-        @pl.when(step == 0)
-        def _():
-            loads[at].wait()
-
     @pl.when(step == 0)
     def _():
         start(0)
-        for load in loads:
-            load.start()
 
     for at in range(1, steps):
 
@@ -373,14 +359,11 @@
 
     pltpu.make_async_copy(rows_ref.at[slot], rows_ref.at[slot], sems.at[slot]).wait()
     tokens = rows_ref[slot]
-    ready(0)
-    gate = mm(tokens, gate_ref[...])
-    ready(1)
-    inner = (gate * jax.nn.sigmoid(gate) * mm(tokens, up_ref[...])).astype(BF)
-    ready(2)
+    gate = mm(tokens, gate_ref[0])
+    inner = (gate * jax.nn.sigmoid(gate) * mm(tokens, up_ref[0])).astype(BF)
     cols = pick_block(width, 512)
     for begin in range(0, width, cols):
-        piece = mm(inner, down_ref[:, begin : begin + cols])
+        piece = mm(inner, down_ref[0, :, begin : begin + cols])
         for at, weight in enumerate(weights):
             part, row = divmod(at * LANES, tok)
             scaled = (piece[at * LANES : (at + 1) * LANES] * weight).astype(BF)
@@ -392,6 +375,24 @@
             @pl.when(jnp.logical_not(is_near))
             def _(scaled=scaled, part=part, row=row):
                 far_ref[part, row : row + LANES, begin : begin + cols] = scaled
+
+
+def stage_kernel(where_ref, *refs):
+    out_ref = refs[-1]
+    for at in range(where_ref.shape[0]):
+        out_ref[at] = where_ref[at]
+
+
+def stage(where, *weights):
+    smem = pl.BlockSpec(memory_space=pltpu.SMEM)
+    return pl.pallas_call(
+        stage_kernel,
+        in_specs=[smem] + [pl.BlockSpec(memory_space=pltpu.VMEM)] * len(weights),
+        out_specs=smem,
+        out_shape=jax.ShapeDtypeStruct(where.shape, where.dtype),
+        compiler_params=params(2),
+        name="stage_weights",
+    )(where, *weights)
 
 
 def expert_pieces(chunk, where, rows, evens, gate, up, down, routes):
@@ -403,14 +404,14 @@
     half = count // PAIR // 2
     experts = EXP_CTX * count
     route_rows = CHUNKS * tok // LANES * 3 * experts
-    hbm = pl.BlockSpec(memory_space=pltpu.HBM)
+    vmem = pl.BlockSpec(memory_space=pltpu.VMEM)
     piece = jax.ShapeDtypeStruct((count // 2, tok, width), BF)
     table = pl.BlockSpec((count // 2, route_rows, LANES), lambda i: (0, 0, 0))
     return pl.pallas_call(
         functools.partial(expert_kernel, tuple(masks), chunk, experts),
         grid=(count // PAIR,),
         in_specs=[pl.BlockSpec(memory_space=pltpu.SMEM), table, table]
-        + [hbm] * 3
+        + [vmem] * 3
         + [pl.BlockSpec(memory_space=pl.ANY)] * count,
         out_specs=[
             pl.BlockSpec((PAIR, tok, width), lambda i: (jnp.minimum(i, half - 1), 0, 0)),
@@ -419,13 +420,9 @@
         out_shape=[piece, piece],
         scratch_shapes=[
             pltpu.VMEM((2, PAIR * tok, width), BF),
-            pltpu.VMEM(gate.shape[1:], BF),
-            pltpu.VMEM(up.shape[1:], BF),
-            pltpu.VMEM(down.shape[1:], BF),
             pltpu.SemaphoreType.DMA((2,)),
-            pltpu.SemaphoreType.DMA((3,)),
         ],
-        compiler_params=params(60),
+        compiler_params=params(20),
         cost_estimate=pl.CostEstimate(
             flops=6 * count * tok * width * hidden,
             bytes_accessed=4 * count * tok * width,
@@ -566,14 +563,14 @@
     fwd = spread_near(fwd, lambda source, target: source < target)
     fwd = (fwd, swap(fwd, CORE))
     parts = core_out(where, qkv, steps, *fwd, norm_gain, w_out, CHUNKS, n_head)
+    where = stage(after(where, parts), w_gate, w_up, w_down)
     bwd = spread_near(after(bwd, parts))
     normed, attn = norm_rows(where, hidden_in, after(send_heads(parts), bwd), gain_moe, CHUNKS)
-    bwd = after(bwd, normed)
-    bwd = (bwd, swap(bwd, CORE))
 
     evens = list(range(0, n_ctx, 2))
     near, rows = [], []
     own = join_rows(where, send_heads([normed[0]] * n_head))
+    bwd = (bwd, swap(after(bwd, own), CORE))
     for chunk in range(CHUNKS):
         near.append([own] + [swap(own, mask) for mask in evens[1:]])
         if chunk + 1 < CHUNKS:
@@ -586,7 +583,7 @@
     sums, pending = [], []
     for chunk in range(CHUNKS):
         here, far = expert_pieces(chunk * chunk_rows, where, rows[chunk], evens, w_gate, w_up, w_down, bwd)
-        arrived = swap(far, CORE)
+        arrived = swap(after(far, near[chunk + 1] if chunk + 1 < CHUNKS else pending[-1][2]), CORE)
         leaving = [plus(here[at], arrived[at]) for at in range(1, len(evens))]
         if chunk + 1 < CHUNKS:
             rows[chunk + 1] = after(rows[chunk + 1], leaving)

time: 246 us -> 214 us (0.87)
  waiting for transfers between devices: 109 us -> 87.7 us
  Pallas kernels: 57.9 us -> 49.2 us
  starting transfers between devices: 62.5 us -> 67 us
  other arithmetic: 5.84 us -> 1.99 us
    ppermute x30, waiting for transfers between devices: 66.5 us -> 48.1 us  [swap(): lax.ppermute(value, 'ctx', [pair for pair in pairs if keep is None or kee...]
    pallas_call x2, Pallas kernels: 32.9 us -> 23.1 us  [expert_pieces(): pl.pallas_call(functools.partial(expert_kernel, tuple(masks), chunk, expe...]
    convert_element_type x2, other arithmetic: 5.01 us -> 1.24 us  [plus(): functools.reduce(jnp.add, [term.astype(F32) for term in terms]).astype(BF)]
    ppermute x15, starting transfers between devices: 27.3 us -> 30.9 us  [send_heads(): lax.ppermute(parts[mask], 'head', [(at, at ^ mask) for at in range(count)])]
    ppermute x15, waiting for transfers between devices: 41.6 us -> 38.6 us  [send_heads(): lax.ppermute(parts[mask], 'head', [(at, at ^ mask) for at in range(count)])]
    unnamed x88 -> x48, local copies, waits for them, and re-layouts: 8.62 us -> 6.8 us
  transfers between devices with their start and end apart: 46 -> 46, of which waited for: 22 -> 19; matrix products, arithmetic and copies ran while one was open for 2% -> 1% of each run, Pallas kernels for 3% -> 15%
where the time goes in v6:
time: 214 us
  waiting for transfers between devices  87.7 us (41%)
  starting transfers between devices  67 us (31%)
  Pallas kernels  49.2 us (23%)
  local copies, waits for them, and re-layouts  6.8 us (3%)
    ppermute x30, waiting for transfers between devices, swap(): lax.ppermute(value, 'ctx', [pair for pair in pairs if keep is None or kee...  48.1 us
    ppermute x15, waiting for transfers between devices, send_heads(): lax.ppermute(parts[mask], 'head', [(at, at ^ mask) for at in range(count)])  38.6 us
    ppermute x30, starting transfers between devices, swap(): lax.ppermute(value, 'ctx', [pair for pair in pairs if keep is None or kee...  33.7 us
    ppermute x15, starting transfers between devices, send_heads(): lax.ppermute(parts[mask], 'head', [(at, at ^ mask) for at in range(count)])  30.9 us
    pallas_call x2, Pallas kernels, expert_pieces(): pl.pallas_call(functools.partial(expert_kernel, tuple(masks), chunk, expe...  23.1 us
    unnamed x48, local copies, waits for them, and re-layouts  6.8 us
    pallas_call x1, Pallas kernels, project(): pl.pallas_call(qkv_kernel, in_specs=[hbm, vmem, hbm], out_shape=[jax.Shap...  6.72 us
    pallas_call x1, Pallas kernels, core_out(): pl.pallas_call(functools.partial(core_kernel, chunks), in_specs=[pl.Block...  5.76 us
  transfers between devices with their start and end apart: 46, of which 19 were waited for; matrix products, arithmetic and copies ran while one was open for 1% of the time, Pallas kernels for 15%

profile of v6, /device:TPU:0, one launch (start us, length us, event | category | flops | bytes accessed | tf_op | source)
XLA Modules:
  0.0 213.8 jit_solution(681432623088244962)
XLA Ops:
  0.7 6.7 %qkv_projection.1 = (bf16[3,256,512]{2,1,0:T(8,128)(2,1)}, bf16[3,16,512]{2,1,0:T(8,128)(2,1)}) custom-call(bf16[256,2048]{1,0:T(8,128)(2,1)} %x_ref.3, f32[1,2048]{1,0:T(1,128)} %bitcast.47, bf16[3,2048,512]{2,1,0:T(8,128)(2,1)} %bitcast.40), custom_call_target="tpu_custom_call" | custom-call | tf_op jit(solution)/shard_map/qkv_projection/pallas_call | solution.py:58
  7.4 2.4 %collective-permute-start = (bf16[3,16,512]{2,1,0:T(8,128)(2,1)}, bf16[3,16,512]{2,1,0:T(8,128)(2,1)S(1)}, u32[]{:S(2)}, u32[]{:S(2)}) collective-permute-start(bf16[3,16,512]{2,1,0:T(8,128)(2,1)} %get-tuple-element.58), channel_id=1, source_target_pairs={{0,4},{4,8},{8,12},{12,16},{16,20},{20,24},{24,28},{1,5},{5,9},{9,... | collective-permute-start | bytes 147464 | tf_op jit(solution)/shard_map/ppermute | solution.py:559
  9.8 1.1 collective-permute-done.rim_ref
  10.9 1.1 copy-done.13
  12.0 2.1 %conv_states.1 = (bf16[3,256,512]{2,1,0:T(8,128)(2,1)S(1)}, bf16[576,128]{1,0:T(8,128)(2,1)S(1)}, bf16[672,128]{1,0:T(8,128)(2,1)S(1)}) custom-call(bf16[3,256,512]{2,1,0:T(8,128)(2,1)S(1)} %copy-done.13, bf16[3,16,512]{2,1,0:T(8,128)(2,1)S(1)} %collective-permute-done.rim_ref, f32[3,4,512]{2,1,0:T(4,128)S(1)} %bitcast.36, f32[4,256]{1,0:T(4,128)S(1)} %bitcast.34, ...), custom_call_target="tpu_custom_call" | custom-call | tf_op jit(solution)/shard_map/conv_states/pallas_call | solution.py:150
  14.2 0.9 copy-done.3
  15.1 0.7 copy-done.15
  15.8 8.0 %collective-permute-start.3 = (bf16[576,128]{1,0:T(8,128)(2,1)S(1)}, bf16[576,128]{1,0:T(8,128)(2,1)S(1)}, u32[]{:S(2)}, u32[]{:S(2)}) collective-permute-start(bf16[576,128]{1,0:T(8,128)(2,1)S(1)} %get-tuple-element.60), channel_id=1, source_target_pairs={{0,24},{4,28},{8,16},{12,20},{1,25},{5,29},{9,17},{13,21},{2,26},{... | collective-permute-start | bytes 442376 | tf_op jit(solution)/shard_map/ppermute | solution.py:441
  23.7 1.3 collective-permute-start.2
  25.1 3.3 %collective-permute-start.1 = (bf16[576,128]{1,0:T(8,128)(2,1)S(1)}, bf16[576,128]{1,0:T(8,128)(2,1)S(1)}, u32[]{:S(2)}, u32[]{:S(2)}) collective-permute-start(bf16[576,128]{1,0:T(8,128)(2,1)S(1)} %get-tuple-element.60), channel_id=1, source_target_pairs={{0,8},{4,12},{16,24},{20,28},{1,9},{5,13},{17,25},{21,29},{2,10},{... | collective-permute-start | bytes 442376 | tf_op jit(solution)/shard_map/ppermute | solution.py:441
  28.4 1.1 collective-permute-done.2
  29.5 1.6 collective-permute-done.1
  31.3 0.6 pad_add_fusion.me_ref.where_ref
  31.9 1.4 collective-permute-done.4.far_ref.fwd_far
  33.2 0.8 copy-done.5
  34.1 5.8 %core_out.1 = (bf16[64,2048]{1,0:T(8,128)(2,1)}, bf16[64,2048]{1,0:T(8,128)(2,1)}, bf16[64,2048]{1,0:T(8,128)(2,1)}, bf16[64,2048]{1,0:T(8,128)(2,1)}) custom-call(s32[3]{0:T(128)} %pad_add_fusion.me_ref.where_ref, bf16[3,256,512]{2,1,0:T(8,128)(2,1)} %copy-done.3, f32[4,256]{1,0:T(4,128)} %bitcast.33, f32[1,512]{1,0:T(1,128)} %bitcast.48, ...), custom_call_target="tpu_custom_call" | custom-call | tf_op jit(solution)/shard_map/core_out/pallas_call | solution.py:214
  39.8 1.2 collective-permute-start.10
  41.1 3.0 %collective-permute-start.9 = (bf16[672,128]{1,0:T(8,128)(2,1)S(1)}, bf16[672,128]{1,0:T(8,128)(2,1)S(1)}, u32[]{:S(2)}, u32[]{:S(2)}) collective-permute-start(bf16[672,128]{1,0:T(8,128)(2,1)S(1)} %copy-done.16), channel_id=1, source_target_pairs={{0,16},{4,20},{8,24},{12,28},{16,0},{20,4},{24,8},{28,12},{1,17},{... | collective-permute-start | bytes 516104 | tf_op jit(solution)/shard_map/ppermute | solution.py:441
  44.0 1.6 collective-permute-start.5
  45.6 2.6 %collective-permute-start.6 = (bf16[64,2048]{1,0:T(8,128)(2,1)}, bf16[64,2048]{1,0:T(8,128)(2,1)S(1)}, u32[]{:S(2)}, u32[]{:S(2)}) collective-permute-start(bf16[64,2048]{1,0:T(8,128)(2,1)} %get-tuple-element.63), channel_id=1, source_target_pairs={{0,2},{1,3},{2,0},{3,1},{4,6},{5,7},{6,4},{7,5},{8,10},{9,11},{10,... | collective-permute-start | bytes 786440 | tf_op jit(solution)/shard_map/ppermute | solution.py:447
  48.2 3.5 %collective-permute-start.7 = (bf16[64,2048]{1,0:T(8,128)(2,1)}, bf16[64,2048]{1,0:T(8,128)(2,1)S(1)}, u32[]{:S(2)}, u32[]{:S(2)}) collective-permute-start(bf16[64,2048]{1,0:T(8,128)(2,1)} %get-tuple-element.64), channel_id=1, source_target_pairs={{0,3},{1,2},{2,1},{3,0},{4,7},{5,6},{6,5},{7,4},{8,11},{9,10},{10,... | collective-permute-start | bytes 786440 | tf_op jit(solution)/shard_map/ppermute | solution.py:447
  51.7 1.6 copy-done.8
  53.3 1.6 copy-done.10
  54.8 1.1 stage_weights.1.where_ref.me_ref
  56.1 0.7 collective-permute-done.5.refs_1_
  56.9 10.3 %collective-permute-done.6.refs_2_ = bf16[64,2048]{1,0:T(8,128)(2,1)S(1)} collective-permute-done((bf16[64,2048]{1,0:T(8,128)(2,1)}, bf16[64,2048]{1,0:T(8,128)(2,1)S(1)}, u32[]{:S(2)}, u32[]{:S(2)}) %collective-permute-start.6) | collective-permute-done | bytes 262176 | tf_op jit(solution)/shard_map/ppermute | solution.py:447
  67.2 0.8 moe_norm.1
  68.1 2.5 %collective-permute-start.13 = (bf16[32,2048]{1,0:T(8,128)(2,1)S(1)}, bf16[32,2048]{1,0:T(8,128)(2,1)S(1)}, u32[]{:S(2)}, u32[]{:S(2)}) collective-permute-start(bf16[32,2048]{1,0:T(8,128)(2,1)S(1)} %get-tuple-element.73.refs_0_), channel_id=1, source_target_pairs={{0,3},{1,2},{2,1},{3,0},{4,7},{5,6},{6,5},{7,4},{8,11},{9,10},{10,... | collective-permute-start | bytes 393224 | tf_op jit(solution)/shard_map/ppermute | solution.py:447
  70.6 5.0 %collective-permute-start.12 = (bf16[32,2048]{1,0:T(8,128)(2,1)S(1)}, bf16[32,2048]{1,0:T(8,128)(2,1)S(1)}, u32[]{:S(2)}, u32[]{:S(2)}) collective-permute-start(bf16[32,2048]{1,0:T(8,128)(2,1)S(1)} %get-tuple-element.73.refs_0_), channel_id=1, source_target_pairs={{0,2},{1,3},{2,0},{3,1},{4,6},{5,7},{6,4},{7,5},{8,10},{9,11},{10,... | collective-permute-start | bytes 393224 | tf_op jit(solution)/shard_map/ppermute | solution.py:447
  75.7 7.6 %collective-permute-done.12.refs_2_ = bf16[32,2048]{1,0:T(8,128)(2,1)S(1)} collective-permute-done((bf16[32,2048]{1,0:T(8,128)(2,1)S(1)}, bf16[32,2048]{1,0:T(8,128)(2,1)S(1)}, u32[]{:S(2)}, u32[]{:S(2)}) %collective-permute-start.12) | collective-permute-done | bytes 131104 | tf_op jit(solution)/shard_map/ppermute | solution.py:447
  83.9 1.5 collective-permute-start.17
  85.5 2.0 collective-permute-start.16
  87.5 2.5 %collective-permute-start.20 = (bf16[32,2048]{1,0:T(8,128)(2,1)S(1)}, bf16[32,2048]{1,0:T(8,128)(2,1)S(1)}, u32[]{:S(2)}, u32[]{:S(2)}) collective-permute-start(bf16[32,2048]{1,0:T(8,128)(2,1)S(1)} %get-tuple-element.76.refs_0_), channel_id=1, source_target_pairs={{0,3},{1,2},{2,1},{3,0},{4,7},{5,6},{6,5},{7,4},{8,11},{9,10},{10,... | collective-permute-start | bytes 393224 | tf_op jit(solution)/shard_map/ppermute | solution.py:447
  90.0 4.3 %collective-permute-done.20.refs_3_ = bf16[32,2048]{1,0:T(8,128)(2,1)S(1)} collective-permute-done((bf16[32,2048]{1,0:T(8,128)(2,1)S(1)}, bf16[32,2048]{1,0:T(8,128)(2,1)S(1)}, u32[]{:S(2)}, u32[]{:S(2)}) %collective-permute-start.20) | collective-permute-done | bytes 131104 | tf_op jit(solution)/shard_map/ppermute | solution.py:447
  94.3 5.4 %collective-permute-done.19.refs_2_ = bf16[32,2048]{1,0:T(8,128)(2,1)S(1)} collective-permute-done((bf16[32,2048]{1,0:T(8,128)(2,1)S(1)}, bf16[32,2048]{1,0:T(8,128)(2,1)S(1)}, u32[]{:S(2)}, u32[]{:S(2)}) %collective-permute-start.19) | collective-permute-done | bytes 131104 | tf_op jit(solution)/shard_map/ppermute | solution.py:447
  99.6 5.0 %collective-permute-done.18.refs_1_ = bf16[32,2048]{1,0:T(8,128)(2,1)S(1)} collective-permute-done((bf16[32,2048]{1,0:T(8,128)(2,1)S(1)}, bf16[32,2048]{1,0:T(8,128)(2,1)S(1)}, u32[]{:S(2)}, u32[]{:S(2)}) %collective-permute-start.18) | collective-permute-done | bytes 131104 | tf_op jit(solution)/shard_map/ppermute | solution.py:447
  105.2 2.5 %collective-permute-done.16.refs_2_ = bf16[128,2048]{1,0:T(8,128)(2,1)S(1)} collective-permute-done((bf16[128,2048]{1,0:T(8,128)(2,1)S(1)}, bf16[128,2048]{1,0:T(8,128)(2,1)S(1)}, u32[]{:S(2)}, u32[]{:S(2)}) %collective-permute-start.16) | collective-permute-done | bytes 524320 | tf_op jit(solution)/shard_map/ppermute | solution.py:441
  108.7 2.6 %collective-permute-start.27 = (bf16[128,2048]{1,0:T(8,128)(2,1)S(1)}, bf16[128,2048]{1,0:T(8,128)(2,1)S(1)}, u32[]{:S(2)}, u32[]{:S(2)}) collective-permute-start(bf16[128,2048]{1,0:T(8,128)(2,1)S(1)} %join_rows.3.refs_0_), channel_id=1, source_target_pairs={{0,24},{4,28},{8,16},{12,20},{16,8},{20,12},{24,0},{28,4},{1,25},{... | collective-permute-start | bytes 1572872 | tf_op jit(solution)/shard_map/ppermute | solution.py:441
  111.4 0.6 collective-permute-start.26
  112.0 0.8 collective-permute-start.25
  112.8 11.6 %expert_pieces.2 = (bf16[4,128,2048]{2,1,0:T(8,128)(2,1)S(1)}, bf16[4,128,2048]{2,1,0:T(8,128)(2,1)S(1)}) custom-call(s32[3]{0:T(128)S(1)} %stage_weights.1.where_ref.me_ref, bf16[4,672,128]{2,1,0:T(8,128)(2,1)S(1)} %pad_maximum_fusion.near_routes.bwd_near, bf16[4,672,128]{2,1,0:T(8,128)(2,1)S(1)} %collective-permute-done.14.far_routes.bwd_far, ...), custom_call_target="tpu_custom_call" | custom-call | flops 6442450944 | bytes 8388608 | tf_op jit(solution)/shard_map/expert_pieces/pallas_call | solution.py:410
  124.5 10.3 %collective-permute-done.26.refs_2_ = bf16[128,2048]{1,0:T(8,128)(2,1)S(1)} collective-permute-done((bf16[128,2048]{1,0:T(8,128)(2,1)S(1)}, bf16[128,2048]{1,0:T(8,128)(2,1)S(1)}, u32[]{:S(2)}, u32[]{:S(2)}) %collective-permute-start.26) | collective-permute-done | bytes 524320 | tf_op jit(solution)/shard_map/ppermute | solution.py:441
  135.8 3.1 %collective-permute-done.28.arrived_ref = bf16[4,128,2048]{2,1,0:T(8,128)(2,1)S(1)} collective-permute-done((bf16[4,128,2048]{2,1,0:T(8,128)(2,1)S(1)}, bf16[4,128,2048]{2,1,0:T(8,128)(2,1)S(1)}, u32[]{:S(2)}, u32[]{:S(2)}) %collective-permute-start.28) | collective-permute-done | bytes 2097184 | tf_op jit(solution)/shard_map/ppermute | solution.py:441
  139.5 2.7 %collective-permute-start.31 = (bf16[128,2048]{1,0:T(8,128)(2,1)S(1)}, bf16[128,2048]{1,0:T(8,128)(2,1)S(1)}, u32[]{:S(2)}, u32[]{:S(2)}) collective-permute-start(bf16[128,2048]{1,0:T(8,128)(2,1)S(1)} %get-tuple-element.113), channel_id=1, source_target_pairs={{0,24},{4,28},{8,16},{12,20},{16,8},{20,12},{24,0},{28,4},{1,25},{... | collective-permute-start | bytes 1572872 | tf_op jit(solution)/shard_map/ppermute | solution.py:441
  142.2 0.6 collective-permute-start.30
  143.0 11.6 %expert_pieces.3 = (bf16[4,128,2048]{2,1,0:T(8,128)(2,1)S(1)}, bf16[4,128,2048]{2,1,0:T(8,128)(2,1)S(1)}) custom-call(s32[3]{0:T(128)S(1)} %stage_weights.1.where_ref.me_ref, bf16[4,672,128]{2,1,0:T(8,128)(2,1)S(1)} %pad_maximum_fusion.near_routes.bwd_near, bf16[4,672,128]{2,1,0:T(8,128)(2,1)S(1)} %collective-permute-done.14.far_routes.bwd_far, ...), custom_call_target="tpu_custom_call" | custom-call | flops 6442450944 | bytes 8388608 | tf_op jit(solution)/shard_map/expert_pieces/pallas_call | solution.py:410
  154.6 0.6 collective-permute-done.31.refs_2_
  155.3 10.4 %collective-permute-done.30.refs_1_ = bf16[128,2048]{1,0:T(8,128)(2,1)S(1)} collective-permute-done((bf16[128,2048]{1,0:T(8,128)(2,1)S(1)}, bf16[128,2048]{1,0:T(8,128)(2,1)S(1)}, u32[]{:S(2)}, u32[]{:S(2)}) %collective-permute-start.30) | collective-permute-done | bytes 524320 | tf_op jit(solution)/shard_map/ppermute | solution.py:441
  165.7 4.1 %collective-permute-done.36.arrived_ref = bf16[4,128,2048]{2,1,0:T(8,128)(2,1)S(1)} collective-permute-done((bf16[4,128,2048]{2,1,0:T(8,128)(2,1)S(1)}, bf16[4,128,2048]{2,1,0:T(8,128)(2,1)S(1)}, u32[]{:S(2)}, u32[]{:S(2)}) %collective-permute-start.36) | collective-permute-done | bytes 2097184 | tf_op jit(solution)/shard_map/ppermute | solution.py:441
  169.8 0.6 fusion.5
  170.5 1.9 collective-permute-start.42
  172.3 1.4 collective-permute-start.41
  174.0 1.1 sum_terms.2
  175.1 1.2 collective-permute-start.37
  176.3 3.4 %collective-permute-start.38 = (bf16[128,512]{1,0:T(8,128)(2,1)S(1)}, bf16[128,512]{1,0:T(8,128)(2,1)S(1)}, u32[]{:S(2)}, u32[]{:S(2)}) collective-permute-start(bf16[128,512]{1,0:T(8,128)(2,1)S(1)} %get-tuple-element.100), channel_id=1, source_target_pairs={{0,2},{1,3},{2,0},{3,1},{4,6},{5,7},{6,4},{7,5},{8,10},{9,11},{10,... | collective-permute-start | bytes 393224 | tf_op jit(solution)/shard_map/ppermute | solution.py:447
  179.7 6.5 %collective-permute-done.42.refs_2_ = bf16[128,2048]{1,0:T(8,128)(2,1)S(1)} collective-permute-done((bf16[128,2048]{1,0:T(8,128)(2,1)S(1)}, bf16[128,2048]{1,0:T(8,128)(2,1)S(1)}, u32[]{:S(2)}, u32[]{:S(2)}) %collective-permute-start.42) | collective-permute-done | bytes 524320 | tf_op jit(solution)/shard_map/ppermute | solution.py:441
  186.2 4.0 %collective-permute-start.39 = (bf16[128,512]{1,0:T(8,128)(2,1)S(1)}, bf16[128,512]{1,0:T(8,128)(2,1)S(1)}, u32[]{:S(2)}, u32[]{:S(2)}) collective-permute-start(bf16[128,512]{1,0:T(8,128)(2,1)S(1)} %get-tuple-element.101), channel_id=1, source_target_pairs={{0,3},{1,2},{2,1},{3,0},{4,7},{5,6},{6,5},{7,4},{8,11},{9,10},{10,... | collective-permute-start | bytes 393224 | tf_op jit(solution)/shard_map/ppermute | solution.py:447
  190.2 6.4 %collective-permute-done.41.refs_1_ = bf16[128,2048]{1,0:T(8,128)(2,1)S(1)} collective-permute-done((bf16[128,2048]{1,0:T(8,128)(2,1)S(1)}, bf16[128,2048]{1,0:T(8,128)(2,1)S(1)}, u32[]{:S(2)}, u32[]{:S(2)}) %collective-permute-start.41) | collective-permute-done | bytes 524320 | tf_op jit(solution)/shard_map/ppermute | solution.py:441
  196.7 1.1 sum_terms.3
  197.8 1.2 collective-permute-start.43
  199.0 3.4 %collective-permute-start.44 = (bf16[128,512]{1,0:T(8,128)(2,1)S(1)}, bf16[128,512]{1,0:T(8,128)(2,1)S(1)}, u32[]{:S(2)}, u32[]{:S(2)}) collective-permute-start(bf16[128,512]{1,0:T(8,128)(2,1)S(1)} %get-tuple-element.105), channel_id=1, source_target_pairs={{0,2},{1,3},{2,0},{3,1},{4,6},{5,7},{6,4},{7,5},{8,10},{9,11},{10,... | collective-permute-start | bytes 393224 | tf_op jit(solution)/shard_map/ppermute | solution.py:447
  202.4 4.7 %core_grads.1 = (bf16[256,512]{1,0:T(8,128)(2,1)}, bf16[256,512]{1,0:T(8,128)(2,1)}, bf16[256,512]{1,0:T(8,128)(2,1)}) custom-call(s32[3]{0:T(128)S(1)} %stage_weights.1.where_ref.me_ref, bf16[3,256,512]{2,1,0:T(8,128)(2,1)S(1)} %copy-done.4, bf16[256,512]{1,0:T(8,128)(2,1)S(1)} %copy-done.12, f32[4,256]{1,0:T(4,128)S(1)} %bitcast.35, ...), custom_call_target="tpu_custom_call" | custom-call | tf_op jit(solution)/shard_map/core_grads/pallas_call | solution.py:261
  207.1 5.2 %collective-permute-done.44.refs_6_ = bf16[128,512]{1,0:T(8,128)(2,1)S(1)} collective-permute-done((bf16[128,512]{1,0:T(8,128)(2,1)S(1)}, bf16[128,512]{1,0:T(8,128)(2,1)S(1)}, u32[]{:S(2)}, u32[]{:S(2)}) %collective-permute-start.44) | collective-permute-done | bytes 131104 | tf_op jit(solution)/shard_map/ppermute | solution.py:447
  212.4 1.4 layer_out.1
  (94 shorter events, 4.9 us)
Async XLA Ops:
  0.6 10.2 %copy-start.12 = (bf16[256,512]{1,0:T(8,128)(2,1)S(1)}, bf16[256,512]{1,0:T(8,128)(2,1)}, u32[]{:S(2)}) copy-start(bf16[256,512]{1,0:T(8,128)(2,1)} %cot_ref.3) | copy-start | bytes 786436
  0.6 10.2 %copy-start.17 = (f32[256,4]{0,1:T(4,128)S(1)}, f32[256,4]{0,1:T(4,128)}, u32[]{:S(2)}) copy-start(f32[256,4]{0,1:T(4,128)} %param.18) | copy-start | bytes 12292
  0.7 10.2 %copy-start.19 = (f32[4,3,512]{2,0,1:T(4,128)S(1)}, f32[4,3,512]{2,0,1:T(4,128)}, u32[]{:S(2)}) copy-start(f32[4,3,512]{2,0,1:T(4,128)} %param.17) | copy-start | bytes 73732
  0.7 10.2 %copy-start.20 = (s32[256,8]{0,1:T(8,128)S(1)}, s32[256,8]{0,1:T(8,128)}, u32[]{:S(2)}) copy-start(s32[256,8]{0,1:T(8,128)} %param.22) | copy-start | bytes 24580
  0.7 10.2 %copy-start.21 = (f32[256,8]{0,1:T(8,128)S(1)}, f32[256,8]{0,1:T(8,128)}, u32[]{:S(2)}) copy-start(f32[256,8]{0,1:T(8,128)} %param.23) | copy-start | bytes 24580
  7.4 3.4 %collective-permute-start = (bf16[3,16,512]{2,1,0:T(8,128)(2,1)}, bf16[3,16,512]{2,1,0:T(8,128)(2,1)S(1)}, u32[]{:S(2)}, u32[]{:S(2)}) collective-permute-start(bf16[3,16,512]{2,1,0:T(8,128)(2,1)} %get-tuple-element.58), channel_id=1, source_target_pairs={{0,4},{4,8},{8,12},{12,16},{16,20},{20,24},{24,28},{1,5},{5,9},{9,... | collective-permute-start | bytes 147464 | tf_op jit(solution)/shard_map/ppermute | solution.py:559
  15.8 12.7 %collective-permute-start.3 = (bf16[576,128]{1,0:T(8,128)(2,1)S(1)}, bf16[576,128]{1,0:T(8,128)(2,1)S(1)}, u32[]{:S(2)}, u32[]{:S(2)}) collective-permute-start(bf16[576,128]{1,0:T(8,128)(2,1)S(1)} %get-tuple-element.60), channel_id=1, source_target_pairs={{0,24},{4,28},{8,16},{12,20},{1,25},{5,29},{9,17},{13,21},{2,26},{... | collective-permute-start | bytes 442376 | tf_op jit(solution)/shard_map/ppermute | solution.py:441
  23.7 5.7 %collective-permute-start.2 = (bf16[576,128]{1,0:T(8,128)(2,1)S(1)}, bf16[576,128]{1,0:T(8,128)(2,1)S(1)}, u32[]{:S(2)}, u32[]{:S(2)}) collective-permute-start(bf16[576,128]{1,0:T(8,128)(2,1)S(1)} %get-tuple-element.60), channel_id=1, source_target_pairs={{0,16},{4,20},{8,24},{12,28},{1,17},{5,21},{9,25},{13,29},{2,18},{... | collective-permute-start | bytes 442376 | tf_op jit(solution)/shard_map/ppermute | solution.py:441
  25.1 6.0 %collective-permute-start.1 = (bf16[576,128]{1,0:T(8,128)(2,1)S(1)}, bf16[576,128]{1,0:T(8,128)(2,1)S(1)}, u32[]{:S(2)}, u32[]{:S(2)}) collective-permute-start(bf16[576,128]{1,0:T(8,128)(2,1)S(1)} %get-tuple-element.60), channel_id=1, source_target_pairs={{0,8},{4,12},{16,24},{20,28},{1,9},{5,13},{17,25},{21,29},{2,10},{... | collective-permute-start | bytes 442376 | tf_op jit(solution)/shard_map/ppermute | solution.py:441
  31.1 2.1 copy-start.1
  31.1 20.5 %copy-start.7 = (bf16[1,2048,512]{2,1,0:T(8,128)(2,1)S(1)}, bf16[1,2048,512]{2,1,0:T(8,128)(2,1)}, u32[]{:S(2)}) copy-start(bf16[1,2048,512]{2,1,0:T(8,128)(2,1)} %gate_ref.3) | copy-start | bytes 6291460
  31.2 2.1 collective-permute-start.4
  31.3 8.6 %copy-start.16 = (bf16[672,128]{1,0:T(8,128)(2,1)S(1)}, bf16[672,128]{1,0:T(8,128)(2,1)}, u32[]{:S(2)}) copy-start(bf16[672,128]{1,0:T(8,128)(2,1)} %copy-done.15) | copy-start | bytes 516100
  31.9 19.8 %copy-start.23 = (s32[3]{0:T(128)S(1)}, s32[3]{0:T(128)}, u32[]{:S(2)}) copy-start(s32[3]{0:T(128)} %pad_add_fusion.me_ref.where_ref) | copy-start | bytes 40
  39.8 27.4 %copy-start.22 = (f32[2048]{0:T(1024)S(1)}, f32[2048]{0:T(1024)}, u32[]{:S(2)}) copy-start(f32[2048]{0:T(1024)} %param.21) | copy-start | bytes 24580
  39.8 8.3 %collective-permute-start.10 = (bf16[672,128]{1,0:T(8,128)(2,1)S(1)}, bf16[672,128]{1,0:T(8,128)(2,1)S(1)}, u32[]{:S(2)}, u32[]{:S(2)}) collective-permute-start(bf16[672,128]{1,0:T(8,128)(2,1)S(1)} %copy-done.16), channel_id=1, source_target_pairs={{0,24},{4,28},{8,16},{12,20},{16,8},{20,12},{24,0},{28,4},{1,25},{... | collective-permute-start | bytes 516104 | tf_op jit(solution)/shard_map/ppermute | solution.py:441
  41.1 15.0 %collective-permute-start.9 = (bf16[672,128]{1,0:T(8,128)(2,1)S(1)}, bf16[672,128]{1,0:T(8,128)(2,1)S(1)}, u32[]{:S(2)}, u32[]{:S(2)}) collective-permute-start(bf16[672,128]{1,0:T(8,128)(2,1)S(1)} %copy-done.16), channel_id=1, source_target_pairs={{0,16},{4,20},{8,24},{12,28},{16,0},{20,4},{24,8},{28,12},{1,17},{... | collective-permute-start | bytes 516104 | tf_op jit(solution)/shard_map/ppermute | solution.py:441
  44.0 12.0 %collective-permute-start.8 = (bf16[672,128]{1,0:T(8,128)(2,1)S(1)}, bf16[672,128]{1,0:T(8,128)(2,1)S(1)}, u32[]{:S(2)}, u32[]{:S(2)}) collective-permute-start(bf16[672,128]{1,0:T(8,128)(2,1)S(1)} %copy-done.16), channel_id=1, source_target_pairs={{0,8},{4,12},{8,0},{12,4},{16,24},{20,28},{24,16},{28,20},{1,9},{5... | collective-permute-start | bytes 516104 | tf_op jit(solution)/shard_map/ppermute | solution.py:441
  44.0 12.8 %collective-permute-start.5 = (bf16[64,2048]{1,0:T(8,128)(2,1)}, bf16[64,2048]{1,0:T(8,128)(2,1)S(1)}, u32[]{:S(2)}, u32[]{:S(2)}) collective-permute-start(bf16[64,2048]{1,0:T(8,128)(2,1)} %get-tuple-element.62), channel_id=1, source_target_pairs={{0,1},{1,0},{2,3},{3,2},{4,5},{5,4},{6,7},{7,6},{8,9},{9,8},{10,11... | collective-permute-start | bytes 786440 | tf_op jit(solution)/shard_map/ppermute | solution.py:447
  45.6 21.6 %collective-permute-start.6 = (bf16[64,2048]{1,0:T(8,128)(2,1)}, bf16[64,2048]{1,0:T(8,128)(2,1)S(1)}, u32[]{:S(2)}, u32[]{:S(2)}) collective-permute-start(bf16[64,2048]{1,0:T(8,128)(2,1)} %get-tuple-element.63), channel_id=1, source_target_pairs={{0,2},{1,3},{2,0},{3,1},{4,6},{5,7},{6,4},{7,5},{8,10},{9,11},{10,... | collective-permute-start | bytes 786440 | tf_op jit(solution)/shard_map/ppermute | solution.py:447
  48.2 19.0 %collective-permute-start.7 = (bf16[64,2048]{1,0:T(8,128)(2,1)}, bf16[64,2048]{1,0:T(8,128)(2,1)S(1)}, u32[]{:S(2)}, u32[]{:S(2)}) collective-permute-start(bf16[64,2048]{1,0:T(8,128)(2,1)} %get-tuple-element.64), channel_id=1, source_target_pairs={{0,3},{1,2},{2,1},{3,0},{4,7},{5,6},{6,5},{7,4},{8,11},{9,10},{10,... | collective-permute-start | bytes 786440 | tf_op jit(solution)/shard_map/ppermute | solution.py:447
  54.8 12.4 %copy-start.14 = (bf16[64,2048]{1,0:T(8,128)(2,1)S(1)}, bf16[64,2048]{1,0:T(8,128)(2,1)}, u32[]{:S(2)}) copy-start(bf16[64,2048]{1,0:T(8,128)(2,1)} %get-tuple-element.68.refs_0_) | copy-start | bytes 786436
  56.0 11.2 %copy-start = (bf16[256,2048]{1,0:T(8,128)(2,1)S(1)}, bf16[256,2048]{1,0:T(8,128)(2,1)}, u32[]{:S(2)}) copy-start(bf16[256,2048]{1,0:T(8,128)(2,1)} %x_ref.3) | copy-start | bytes 3145732
  67.2 45.6 %copy-start.9 = (bf16[1,2048,512]{2,1,0:T(8,128)(2,1)S(1)}, bf16[1,2048,512]{2,1,0:T(8,128)(2,1)}, u32[]{:S(2)}) copy-start(bf16[1,2048,512]{2,1,0:T(8,128)(2,1)} %up_ref.3) | copy-start | bytes 6291460
  67.2 45.6 %copy-start.11 = (bf16[1,512,2048]{2,1,0:T(8,128)(2,1)S(1)}, bf16[1,512,2048]{2,1,0:T(8,128)(2,1)}, u32[]{:S(2)}) copy-start(bf16[1,512,2048]{2,1,0:T(8,128)(2,1)} %down_ref.3) | copy-start | bytes 6291460
  68.1 7.6 %collective-permute-start.13 = (bf16[32,2048]{1,0:T(8,128)(2,1)S(1)}, bf16[32,2048]{1,0:T(8,128)(2,1)S(1)}, u32[]{:S(2)}, u32[]{:S(2)}) collective-permute-start(bf16[32,2048]{1,0:T(8,128)(2,1)S(1)} %get-tuple-element.73.refs_0_), channel_id=1, source_target_pairs={{0,3},{1,2},{2,1},{3,0},{4,7},{5,6},{6,5},{7,4},{8,11},{9,10},{10,... | collective-permute-start | bytes 393224 | tf_op jit(solution)/shard_map/ppermute | solution.py:447
  70.6 12.7 %collective-permute-start.12 = (bf16[32,2048]{1,0:T(8,128)(2,1)S(1)}, bf16[32,2048]{1,0:T(8,128)(2,1)S(1)}, u32[]{:S(2)}, u32[]{:S(2)}) collective-permute-start(bf16[32,2048]{1,0:T(8,128)(2,1)S(1)} %get-tuple-element.73.refs_0_), channel_id=1, source_target_pairs={{0,2},{1,3},{2,0},{3,1},{4,6},{5,7},{6,4},{7,5},{8,10},{9,11},{10,... | collective-permute-start | bytes 393224 | tf_op jit(solution)/shard_map/ppermute | solution.py:447
  75.6 7.8 %collective-permute-start.11 = (bf16[32,2048]{1,0:T(8,128)(2,1)S(1)}, bf16[32,2048]{1,0:T(8,128)(2,1)S(1)}, u32[]{:S(2)}, u32[]{:S(2)}) collective-permute-start(bf16[32,2048]{1,0:T(8,128)(2,1)S(1)} %get-tuple-element.73.refs_0_), channel_id=1, source_target_pairs={{0,1},{1,0},{2,3},{3,2},{4,5},{5,4},{6,7},{7,6},{8,9},{9,8},{10,11... | collective-permute-start | bytes 393224 | tf_op jit(solution)/shard_map/ppermute | solution.py:447
  83.9 21.2 %collective-permute-start.17 = (bf16[128,2048]{1,0:T(8,128)(2,1)S(1)}, bf16[128,2048]{1,0:T(8,128)(2,1)S(1)}, u32[]{:S(2)}, u32[]{:S(2)}) collective-permute-start(bf16[128,2048]{1,0:T(8,128)(2,1)S(1)} %join_rows.2.refs_0_), channel_id=1, source_target_pairs={{0,24},{4,28},{8,16},{12,20},{16,8},{20,12},{24,0},{28,4},{1,25},{... | collective-permute-start | bytes 1572872 | tf_op jit(solution)/shard_map/ppermute | solution.py:441
  85.5 22.2 %collective-permute-start.16 = (bf16[128,2048]{1,0:T(8,128)(2,1)S(1)}, bf16[128,2048]{1,0:T(8,128)(2,1)S(1)}, u32[]{:S(2)}, u32[]{:S(2)}) collective-permute-start(bf16[128,2048]{1,0:T(8,128)(2,1)S(1)} %join_rows.2.refs_0_), channel_id=1, source_target_pairs={{0,16},{4,20},{8,24},{12,28},{16,0},{20,4},{24,8},{28,12},{1,17},{... | collective-permute-start | bytes 1572872 | tf_op jit(solution)/shard_map/ppermute | solution.py:441
  87.5 20.2 %collective-permute-start.15 = (bf16[128,2048]{1,0:T(8,128)(2,1)S(1)}, bf16[128,2048]{1,0:T(8,128)(2,1)S(1)}, u32[]{:S(2)}, u32[]{:S(2)}) collective-permute-start(bf16[128,2048]{1,0:T(8,128)(2,1)S(1)} %join_rows.2.refs_0_), channel_id=1, source_target_pairs={{0,8},{4,12},{8,0},{12,4},{16,24},{20,28},{24,16},{28,20},{1,9},{5... | collective-permute-start | bytes 1572872 | tf_op jit(solution)/shard_map/ppermute | solution.py:441
  87.5 6.8 %collective-permute-start.20 = (bf16[32,2048]{1,0:T(8,128)(2,1)S(1)}, bf16[32,2048]{1,0:T(8,128)(2,1)S(1)}, u32[]{:S(2)}, u32[]{:S(2)}) collective-permute-start(bf16[32,2048]{1,0:T(8,128)(2,1)S(1)} %get-tuple-element.76.refs_0_), channel_id=1, source_target_pairs={{0,3},{1,2},{2,1},{3,0},{4,7},{5,6},{6,5},{7,4},{8,11},{9,10},{10,... | collective-permute-start | bytes 393224 | tf_op jit(solution)/shard_map/ppermute | solution.py:447
  90.0 9.7 %collective-permute-start.19 = (bf16[32,2048]{1,0:T(8,128)(2,1)S(1)}, bf16[32,2048]{1,0:T(8,128)(2,1)S(1)}, u32[]{:S(2)}, u32[]{:S(2)}) collective-permute-start(bf16[32,2048]{1,0:T(8,128)(2,1)S(1)} %get-tuple-element.76.refs_0_), channel_id=1, source_target_pairs={{0,2},{1,3},{2,0},{3,1},{4,6},{5,7},{6,4},{7,5},{8,10},{9,11},{10,... | collective-permute-start | bytes 393224 | tf_op jit(solution)/shard_map/ppermute | solution.py:447
  94.3 14.5 %collective-permute-start.14 = (bf16[4,672,128]{2,1,0:T(8,128)(2,1)S(1)}, bf16[4,672,128]{2,1,0:T(8,128)(2,1)S(1)}, u32[]{:S(2)}, u32[]{:S(2)}) collective-permute-start(bf16[4,672,128]{2,1,0:T(8,128)(2,1)S(1)} %pad_maximum_fusion.near_routes.bwd_near), channel_id=1, source_target_pairs={{0,4},{4,0},{8,12},{12,8},{16,20},{20,16},{24,28},{28,24},{1,5},{5... | collective-permute-start | bytes 2064392 | tf_op jit(solution)/shard_map/ppermute | solution.py:441
  99.6 5.0 %collective-permute-start.18 = (bf16[32,2048]{1,0:T(8,128)(2,1)S(1)}, bf16[32,2048]{1,0:T(8,128)(2,1)S(1)}, u32[]{:S(2)}, u32[]{:S(2)}) collective-permute-start(bf16[32,2048]{1,0:T(8,128)(2,1)S(1)} %get-tuple-element.76.refs_0_), channel_id=1, source_target_pairs={{0,1},{1,0},{2,3},{3,2},{4,5},{5,4},{6,7},{7,6},{8,9},{9,8},{10,11... | collective-permute-start | bytes 393224 | tf_op jit(solution)/shard_map/ppermute | solution.py:447
  107.7 3.7 %collective-permute-start.21 = (bf16[128,2048]{1,0:T(8,128)(2,1)S(1)}, bf16[128,2048]{1,0:T(8,128)(2,1)S(1)}, u32[]{:S(2)}, u32[]{:S(2)}) collective-permute-start(bf16[128,2048]{1,0:T(8,128)(2,1)S(1)} %join_rows.2.refs_0_), channel_id=1, source_target_pairs={{0,4},{4,0},{8,12},{12,8},{16,20},{20,16},{24,28},{28,24},{1,5},{5... | collective-permute-start | bytes 1572872 | tf_op jit(solution)/shard_map/ppermute | solution.py:441
  107.7 4.2 %collective-permute-start.22 = (bf16[128,2048]{1,0:T(8,128)(2,1)S(1)}, bf16[128,2048]{1,0:T(8,128)(2,1)S(1)}, u32[]{:S(2)}, u32[]{:S(2)}) collective-permute-start(bf16[128,2048]{1,0:T(8,128)(2,1)S(1)} %collective-permute-done.15.refs_1_), channel_id=1, source_target_pairs={{0,4},{4,0},{8,12},{12,8},{16,20},{20,16},{24,28},{28,24},{1,5},{5... | collective-permute-start | bytes 1572872 | tf_op jit(solution)/shard_map/ppermute | solution.py:441
  108.2 4.6 %collective-permute-start.23 = (bf16[128,2048]{1,0:T(8,128)(2,1)S(1)}, bf16[128,2048]{1,0:T(8,128)(2,1)S(1)}, u32[]{:S(2)}, u32[]{:S(2)}) collective-permute-start(bf16[128,2048]{1,0:T(8,128)(2,1)S(1)} %collective-permute-done.16.refs_2_), channel_id=1, source_target_pairs={{0,4},{4,0},{8,12},{12,8},{16,20},{20,16},{24,28},{28,24},{1,5},{5... | collective-permute-start | bytes 1572872 | tf_op jit(solution)/shard_map/ppermute | solution.py:441
  108.2 4.6 %collective-permute-start.24 = (bf16[128,2048]{1,0:T(8,128)(2,1)S(1)}, bf16[128,2048]{1,0:T(8,128)(2,1)S(1)}, u32[]{:S(2)}, u32[]{:S(2)}) collective-permute-start(bf16[128,2048]{1,0:T(8,128)(2,1)S(1)} %collective-permute-done.17.refs_3_), channel_id=1, source_target_pairs={{0,4},{4,0},{8,12},{12,8},{16,20},{20,16},{24,28},{28,24},{1,5},{5... | collective-permute-start | bytes 1572872 | tf_op jit(solution)/shard_map/ppermute | solution.py:441
  108.7 15.7 %collective-permute-start.27 = (bf16[128,2048]{1,0:T(8,128)(2,1)S(1)}, bf16[128,2048]{1,0:T(8,128)(2,1)S(1)}, u32[]{:S(2)}, u32[]{:S(2)}) collective-permute-start(bf16[128,2048]{1,0:T(8,128)(2,1)S(1)} %join_rows.3.refs_0_), channel_id=1, source_target_pairs={{0,24},{4,28},{8,16},{12,20},{16,8},{20,12},{24,0},{28,4},{1,25},{... | collective-permute-start | bytes 1572872 | tf_op jit(solution)/shard_map/ppermute | solution.py:441
  111.4 23.4 %collective-permute-start.26 = (bf16[128,2048]{1,0:T(8,128)(2,1)S(1)}, bf16[128,2048]{1,0:T(8,128)(2,1)S(1)}, u32[]{:S(2)}, u32[]{:S(2)}) collective-permute-start(bf16[128,2048]{1,0:T(8,128)(2,1)S(1)} %join_rows.3.refs_0_), channel_id=1, source_target_pairs={{0,16},{4,20},{8,24},{12,28},{16,0},{20,4},{24,8},{28,12},{1,17},{... | collective-permute-start | bytes 1572872 | tf_op jit(solution)/shard_map/ppermute | solution.py:441
  112.0 22.7 %collective-permute-start.25 = (bf16[128,2048]{1,0:T(8,128)(2,1)S(1)}, bf16[128,2048]{1,0:T(8,128)(2,1)S(1)}, u32[]{:S(2)}, u32[]{:S(2)}) collective-permute-start(bf16[128,2048]{1,0:T(8,128)(2,1)S(1)} %join_rows.3.refs_0_), channel_id=1, source_target_pairs={{0,8},{4,12},{8,0},{12,4},{16,24},{20,28},{24,16},{28,20},{1,9},{5... | collective-permute-start | bytes 1572872 | tf_op jit(solution)/shard_map/ppermute | solution.py:441
  134.7 4.2 %collective-permute-start.28 = (bf16[4,128,2048]{2,1,0:T(8,128)(2,1)S(1)}, bf16[4,128,2048]{2,1,0:T(8,128)(2,1)S(1)}, u32[]{:S(2)}, u32[]{:S(2)}) collective-permute-start(bf16[4,128,2048]{2,1,0:T(8,128)(2,1)S(1)} %get-tuple-element.83), channel_id=1, source_target_pairs={{0,4},{4,0},{8,12},{12,8},{16,20},{20,16},{24,28},{28,24},{1,5},{5... | collective-permute-start | bytes 6291464 | tf_op jit(solution)/shard_map/ppermute | solution.py:441
  134.7 7.4 %collective-permute-start.32 = (bf16[128,2048]{1,0:T(8,128)(2,1)S(1)}, bf16[128,2048]{1,0:T(8,128)(2,1)S(1)}, u32[]{:S(2)}, u32[]{:S(2)}) collective-permute-start(bf16[128,2048]{1,0:T(8,128)(2,1)S(1)} %join_rows.3.refs_0_), channel_id=1, source_target_pairs={{0,4},{4,0},{8,12},{12,8},{16,20},{20,16},{24,28},{28,24},{1,5},{5... | collective-permute-start | bytes 1572872 | tf_op jit(solution)/shard_map/ppermute | solution.py:441
  135.2 7.5 %collective-permute-start.35 = (bf16[128,2048]{1,0:T(8,128)(2,1)S(1)}, bf16[128,2048]{1,0:T(8,128)(2,1)S(1)}, u32[]{:S(2)}, u32[]{:S(2)}) collective-permute-start(bf16[128,2048]{1,0:T(8,128)(2,1)S(1)} %collective-permute-done.27.refs_3_), channel_id=1, source_target_pairs={{0,4},{4,0},{8,12},{12,8},{16,20},{20,16},{24,28},{28,24},{1,5},{5... | collective-permute-start | bytes 1572872 | tf_op jit(solution)/shard_map/ppermute | solution.py:441
  135.2 7.8 %collective-permute-start.34 = (bf16[128,2048]{1,0:T(8,128)(2,1)S(1)}, bf16[128,2048]{1,0:T(8,128)(2,1)S(1)}, u32[]{:S(2)}, u32[]{:S(2)}) collective-permute-start(bf16[128,2048]{1,0:T(8,128)(2,1)S(1)} %collective-permute-done.26.refs_2_), channel_id=1, source_target_pairs={{0,4},{4,0},{8,12},{12,8},{16,20},{20,16},{24,28},{28,24},{1,5},{5... | collective-permute-start | bytes 1572872 | tf_op jit(solution)/shard_map/ppermute | solution.py:441
  135.7 7.3 %collective-permute-start.33 = (bf16[128,2048]{1,0:T(8,128)(2,1)S(1)}, bf16[128,2048]{1,0:T(8,128)(2,1)S(1)}, u32[]{:S(2)}, u32[]{:S(2)}) collective-permute-start(bf16[128,2048]{1,0:T(8,128)(2,1)S(1)} %collective-permute-done.25.refs_1_), channel_id=1, source_target_pairs={{0,4},{4,0},{8,12},{12,8},{16,20},{20,16},{24,28},{28,24},{1,5},{5... | collective-permute-start | bytes 1572872 | tf_op jit(solution)/shard_map/ppermute | solution.py:441
  139.5 15.8 %collective-permute-start.31 = (bf16[128,2048]{1,0:T(8,128)(2,1)S(1)}, bf16[128,2048]{1,0:T(8,128)(2,1)S(1)}, u32[]{:S(2)}, u32[]{:S(2)}) collective-permute-start(bf16[128,2048]{1,0:T(8,128)(2,1)S(1)} %get-tuple-element.113), channel_id=1, source_target_pairs={{0,24},{4,28},{8,16},{12,20},{16,8},{20,12},{24,0},{28,4},{1,25},{... | collective-permute-start | bytes 1572872 | tf_op jit(solution)/shard_map/ppermute | solution.py:441
  142.2 23.5 %collective-permute-start.30 = (bf16[128,2048]{1,0:T(8,128)(2,1)S(1)}, bf16[128,2048]{1,0:T(8,128)(2,1)S(1)}, u32[]{:S(2)}, u32[]{:S(2)}) collective-permute-start(bf16[128,2048]{1,0:T(8,128)(2,1)S(1)} %get-tuple-element.114), channel_id=1, source_target_pairs={{0,16},{4,20},{8,24},{12,28},{16,0},{20,4},{24,8},{28,12},{1,17},{... | collective-permute-start | bytes 1572872 | tf_op jit(solution)/shard_map/ppermute | solution.py:441
  142.8 22.9 %collective-permute-start.29 = (bf16[128,2048]{1,0:T(8,128)(2,1)S(1)}, bf16[128,2048]{1,0:T(8,128)(2,1)S(1)}, u32[]{:S(2)}, u32[]{:S(2)}) collective-permute-start(bf16[128,2048]{1,0:T(8,128)(2,1)S(1)} %get-tuple-element.115), channel_id=1, source_target_pairs={{0,8},{4,12},{8,0},{12,4},{16,24},{20,28},{24,16},{28,20},{1,9},{5... | collective-permute-start | bytes 1572872 | tf_op jit(solution)/shard_map/ppermute | solution.py:441
  165.6 4.2 %collective-permute-start.36 = (bf16[4,128,2048]{2,1,0:T(8,128)(2,1)S(1)}, bf16[4,128,2048]{2,1,0:T(8,128)(2,1)S(1)}, u32[]{:S(2)}, u32[]{:S(2)}) collective-permute-start(bf16[4,128,2048]{2,1,0:T(8,128)(2,1)S(1)} %get-tuple-element.94), channel_id=1, source_target_pairs={{0,4},{4,0},{8,12},{12,8},{16,20},{20,16},{24,28},{28,24},{1,5},{5... | collective-permute-start | bytes 6291464 | tf_op jit(solution)/shard_map/ppermute | solution.py:441
  170.5 15.8 %collective-permute-start.42 = (bf16[128,2048]{1,0:T(8,128)(2,1)S(1)}, bf16[128,2048]{1,0:T(8,128)(2,1)S(1)}, u32[]{:S(2)}, u32[]{:S(2)}) collective-permute-start(bf16[128,2048]{1,0:T(8,128)(2,1)S(1)} %get-tuple-element.110), channel_id=1, source_target_pairs={{0,24},{4,28},{8,16},{12,20},{16,8},{20,12},{24,0},{28,4},{1,25},{... | collective-permute-start | bytes 1572872 | tf_op jit(solution)/shard_map/ppermute | solution.py:441
  172.3 24.3 %collective-permute-start.41 = (bf16[128,2048]{1,0:T(8,128)(2,1)S(1)}, bf16[128,2048]{1,0:T(8,128)(2,1)S(1)}, u32[]{:S(2)}, u32[]{:S(2)}) collective-permute-start(bf16[128,2048]{1,0:T(8,128)(2,1)S(1)} %get-tuple-element.111), channel_id=1, source_target_pairs={{0,16},{4,20},{8,24},{12,28},{16,0},{20,4},{24,8},{28,12},{1,17},{... | collective-permute-start | bytes 1572872 | tf_op jit(solution)/shard_map/ppermute | solution.py:441
  173.7 22.9 %collective-permute-start.40 = (bf16[128,2048]{1,0:T(8,128)(2,1)S(1)}, bf16[128,2048]{1,0:T(8,128)(2,1)S(1)}, u32[]{:S(2)}, u32[]{:S(2)}) collective-permute-start(bf16[128,2048]{1,0:T(8,128)(2,1)S(1)} %get-tuple-element.112), channel_id=1, source_target_pairs={{0,8},{4,12},{8,0},{12,4},{16,24},{20,28},{24,16},{28,20},{1,9},{5... | collective-permute-start | bytes 1572872 | tf_op jit(solution)/shard_map/ppermute | solution.py:441
  175.1 27.3 %collective-permute-start.37 = (bf16[128,512]{1,0:T(8,128)(2,1)S(1)}, bf16[128,512]{1,0:T(8,128)(2,1)S(1)}, u32[]{:S(2)}, u32[]{:S(2)}) collective-permute-start(bf16[128,512]{1,0:T(8,128)(2,1)S(1)} %get-tuple-element.99), channel_id=1, source_target_pairs={{0,1},{1,0},{2,3},{3,2},{4,5},{5,4},{6,7},{7,6},{8,9},{9,8},{10,11... | collective-permute-start | bytes 393224 | tf_op jit(solution)/shard_map/ppermute | solution.py:447
  176.3 30.8 %collective-permute-start.38 = (bf16[128,512]{1,0:T(8,128)(2,1)S(1)}, bf16[128,512]{1,0:T(8,128)(2,1)S(1)}, u32[]{:S(2)}, u32[]{:S(2)}) collective-permute-start(bf16[128,512]{1,0:T(8,128)(2,1)S(1)} %get-tuple-element.100), channel_id=1, source_target_pairs={{0,2},{1,3},{2,0},{3,1},{4,6},{5,7},{6,4},{7,5},{8,10},{9,11},{10,... | collective-permute-start | bytes 393224 | tf_op jit(solution)/shard_map/ppermute | solution.py:447
  186.2 20.9 %collective-permute-start.39 = (bf16[128,512]{1,0:T(8,128)(2,1)S(1)}, bf16[128,512]{1,0:T(8,128)(2,1)S(1)}, u32[]{:S(2)}, u32[]{:S(2)}) collective-permute-start(bf16[128,512]{1,0:T(8,128)(2,1)S(1)} %get-tuple-element.101), channel_id=1, source_target_pairs={{0,3},{1,2},{2,1},{3,0},{4,7},{5,6},{6,5},{7,4},{8,11},{9,10},{10,... | collective-permute-start | bytes 393224 | tf_op jit(solution)/shard_map/ppermute | solution.py:447
  196.6 5.7 %copy-start.2 = (bf16[4,576,128]{2,1,0:T(8,128)(2,1)S(1)}, bf16[4,576,128]{2,1,0:T(8,128)(2,1)}, u32[]{:S(2)}) copy-start(bf16[4,576,128]{2,1,0:T(8,128)(2,1)} %copy-done.1) | copy-start | bytes 1769476
  196.6 5.7 %copy-start.4 = (bf16[3,256,512]{2,1,0:T(8,128)(2,1)S(1)}, bf16[3,256,512]{2,1,0:T(8,128)(2,1)}, u32[]{:S(2)}) copy-start(bf16[3,256,512]{2,1,0:T(8,128)(2,1)} %copy-done.3) | copy-start | bytes 2359300
  196.6 5.8 %copy-start.6 = (bf16[4,576,128]{2,1,0:T(8,128)(2,1)S(1)}, bf16[4,576,128]{2,1,0:T(8,128)(2,1)}, u32[]{:S(2)}) copy-start(bf16[4,576,128]{2,1,0:T(8,128)(2,1)} %copy-done.5) | copy-start | bytes 1769476
  196.6 5.8 %copy-start.18 = (f32[256,4]{0,1:T(4,128)S(1)}, f32[256,4]{0,1:T(4,128)}, u32[]{:S(2)}) copy-start(f32[256,4]{0,1:T(4,128)} %param.18) | copy-start | bytes 12292
  197.8 9.4 %collective-permute-start.43 = (bf16[128,512]{1,0:T(8,128)(2,1)S(1)}, bf16[128,512]{1,0:T(8,128)(2,1)S(1)}, u32[]{:S(2)}, u32[]{:S(2)}) collective-permute-start(bf16[128,512]{1,0:T(8,128)(2,1)S(1)} %get-tuple-element.104), channel_id=1, source_target_pairs={{0,1},{1,0},{2,3},{3,2},{4,5},{5,4},{6,7},{7,6},{8,9},{9,8},{10,11... | collective-permute-start | bytes 393224 | tf_op jit(solution)/shard_map/ppermute | solution.py:447
  199.0 13.4 %collective-permute-start.44 = (bf16[128,512]{1,0:T(8,128)(2,1)S(1)}, bf16[128,512]{1,0:T(8,128)(2,1)S(1)}, u32[]{:S(2)}, u32[]{:S(2)}) collective-permute-start(bf16[128,512]{1,0:T(8,128)(2,1)S(1)} %get-tuple-element.105), channel_id=1, source_target_pairs={{0,2},{1,3},{2,0},{3,1},{4,6},{5,7},{6,4},{7,5},{8,10},{9,11},{10,... | collective-permute-start | bytes 393224 | tf_op jit(solution)/shard_map/ppermute | solution.py:447
  202.4 10.0 %collective-permute-start.45 = (bf16[128,512]{1,0:T(8,128)(2,1)S(1)}, bf16[128,512]{1,0:T(8,128)(2,1)S(1)}, u32[]{:S(2)}, u32[]{:S(2)}) collective-permute-start(bf16[128,512]{1,0:T(8,128)(2,1)S(1)} %get-tuple-element.106), channel_id=1, source_target_pairs={{0,3},{1,2},{2,1},{3,0},{4,7},{5,6},{6,5},{7,4},{8,11},{9,10},{10,... | collective-permute-start | bytes 393224 | tf_op jit(solution)/shard_map/ppermute | solution.py:447
  (6 other events, 6.7 us)

commit v7 on v6

--- a/solution.py
+++ b/solution.py
@@ -58,6 +58,7 @@
     return pl.pallas_call(
         qkv_kernel,
         in_specs=[hbm, vmem, hbm],
+        out_specs=[vmem, vmem],
         out_shape=[
             jax.ShapeDtypeStruct((kinds, rows, chans), BF),
             jax.ShapeDtypeStruct((kinds, RIM, chans), BF),
@@ -69,7 +70,7 @@
             pltpu.SemaphoreType.DMA,
             pltpu.SemaphoreType.DMA((kinds,)),
         ],
-        compiler_params=params(61),
+        compiler_params=params(60),
         name="qkv_projection",
     )(x, gain.reshape(1, width), weights)
 
@@ -149,6 +150,7 @@
     states = heads * (size + RIM)
     return pl.pallas_call(
         functools.partial(conv_kernel, experts),
+        out_specs=[pl.BlockSpec(memory_space=pltpu.VMEM)] * 3,
         out_shape=[
             jax.ShapeDtypeStruct((kinds, rows, chans), BF),
             jax.ShapeDtypeStruct((states, size), BF),
@@ -178,10 +180,8 @@
     return lax.fori_loop(0, (last - first) * step, hop, jnp.zeros((size, size), F32))
 
 
-def core_kernel(chunks, me_ref, qkv_ref, steps_ref, gain_ref, near_ref, far_ref, w_hbm, *refs):
-    out_refs, (headed_ref, held_ref, w_ref, whole_ref, sem) = refs[:-5], refs[-5:]
-    load = pltpu.make_async_copy(w_hbm, w_ref, sem)
-    load.start()
+def core_kernel(chunks, me_ref, qkv_ref, steps_ref, gain_ref, near_ref, far_ref, w_ref, *refs):
+    out_refs, (headed_ref, held_ref, whole_ref) = refs[:-3], refs[-3:]
     _, rows, chans = qkv_ref.shape
     heads = steps_ref.shape[0]
     size = chans // heads
@@ -198,7 +198,6 @@
         attended += mm(query, state) * jnp.exp(down[:, head : head + 1])
         scale = lax.rsqrt(jnp.mean(attended * attended, axis=-1, keepdims=True) + 1e-06)
         headed_ref[:, at] = (attended * scale * gain_ref[:, at]).astype(BF)
-    load.wait()
     whole_ref[...] = mm(headed_ref[...], w_ref[...]).astype(BF)
     part = rows // len(out_refs) // chunks
     for mask, ref in enumerate(out_refs):
@@ -213,16 +212,14 @@
     vmem = pl.BlockSpec(memory_space=pltpu.VMEM)
     return pl.pallas_call(
         functools.partial(core_kernel, chunks),
-        in_specs=[pl.BlockSpec(memory_space=pltpu.SMEM)] + [vmem] * 5 + [pl.BlockSpec(memory_space=pltpu.HBM)],
+        in_specs=[pl.BlockSpec(memory_space=pltpu.SMEM)] + [vmem] * 6,
         out_shape=[jax.ShapeDtypeStruct((rows // parts, width), BF)] * parts,
         scratch_shapes=[
             pltpu.VMEM((rows, chans), BF),
             pltpu.VMEM((2 * near.shape[0], *near.shape[1:]), BF),
-            pltpu.VMEM(w_out.shape, BF),
             pltpu.VMEM((rows, width), BF),
-            pltpu.SemaphoreType.DMA,
         ],
-        compiler_params=params(56),
+        compiler_params=params(16),
         name="core_out",
     )(where, qkv, steps, gain.reshape(1, chans), near, far, w_out)
 
@@ -432,7 +429,8 @@
     )(where, *routes, gate, up, down, *blocks)
 
 
-CORE = 1
+CORE, ROW, COL = 1, 2, 4
+PLANE = 8
 
 
 def swap(value, mask, keep=None):
@@ -460,7 +458,50 @@
     return lax.optimization_barrier((value, other))[0]
 
 
-def sum_kernel(where_ref, attn_ref, near_ref, arrived_ref, *refs):
+def depart(own):
+    masks = (ROW, COL) if lax.axis_size("ctx") == PLANE else range(2, lax.axis_size("ctx"), 2)
+    return {mask: swap(own, mask) for mask in masks}
+
+
+def forward(own, came):
+    came = {0: own} | came
+    if lax.axis_size("ctx") == PLANE:
+        half = own.shape[0] // 2
+        upper, lower = swap(came[ROW][:half], COL), swap(came[COL][half:], ROW)
+        came[ROW | COL] = jnp.concatenate([upper, lower])
+    return [came[mask] for mask in range(0, lax.axis_size("ctx"), 2)]
+
+
+def first_sums(here, arrived):
+    if lax.axis_size("ctx") != PLANE:
+        return [(2 * at, 0, plus(here[at], arrived[at])) for at in range(1, here.shape[0])]
+    half = here.shape[1] // 2
+    row, col, across = ROW // 2, COL // 2, (ROW | COL) // 2
+    upper, lower = slice(0, half), slice(half, 2 * half)
+    return [
+        (ROW, 0, plus(here[across, upper], arrived[across, upper])),
+        (COL, half, plus(here[across, lower], arrived[across, lower])),
+        (ROW, 0, plus(here[row, upper], arrived[row, upper])),
+        (COL, half, plus(here[col, lower], arrived[col, lower])),
+    ]
+
+
+def last_sums(here, arrived, came):
+    if lax.axis_size("ctx") != PLANE:
+        return []
+    half = here.shape[1] // 2
+    row, col = ROW // 2, COL // 2
+    return [
+        (COL, 0, plus(here[col, :half], arrived[col, :half], came[0])),
+        (ROW, half, plus(here[row, half:], arrived[row, half:], came[1])),
+    ]
+
+
+def send_sums(sums):
+    return [swap(rows, mask) for mask, _, rows in sums]
+
+
+def sum_kernel(starts, where_ref, attn_ref, near_ref, arrived_ref, *refs):
     parts = attn_ref.shape[1] // refs[-1].shape[1]
     others, outs, total_ref = refs[: -parts - 1], refs[-parts - 1 : -1], refs[-1]
     part, width = attn_ref.shape
@@ -469,20 +510,20 @@
     for mask, out_ref in enumerate(outs):
         at = pl.ds(pl.multiple_of((where_ref[2] ^ mask) * cols, cols), cols)
         total = near_ref[0, :, at].astype(F32) + arrived_ref[0, :, at].astype(F32)
-        for ref in others:
-            total += ref[:, at].astype(F32)
         total_ref[...] = total
+        for start, ref in zip(starts, others):
+            total_ref[start : start + ref.shape[0]] += ref[:, at].astype(F32)
         total_ref[own, :] += attn_ref[:, at]
         out_ref[...] = total_ref[...].astype(BF)
 
 
-def sum_terms(where, attn, near, arrived, others, parts):
+def sum_terms(where, attn, near, arrived, others, starts, parts):
     _, tok, width = near.shape
     part = attn.shape[0]
     cols = width // parts
     first = pl.BlockSpec((1, tok, width), lambda i: (0, 0, 0))
     return pl.pallas_call(
-        sum_kernel,
+        functools.partial(sum_kernel, tuple(starts)),
         grid=(1,),
         in_specs=[
             pl.BlockSpec(memory_space=pltpu.SMEM),
@@ -490,7 +531,7 @@
             first,
             first,
         ]
-        + [pl.BlockSpec((tok, width), lambda i: (0, 0))] * len(others),
+        + [pl.BlockSpec(part.shape, lambda i: (0, 0)) for part in others],
         out_specs=[pl.BlockSpec((tok, cols), lambda i: (0, 0))] * parts,
         out_shape=[jax.ShapeDtypeStruct((tok, cols), BF)] * parts,
         scratch_shapes=[pltpu.VMEM((tok, cols), F32)],
@@ -562,38 +603,49 @@
     )
     fwd = spread_near(fwd, lambda source, target: source < target)
     fwd = (fwd, swap(fwd, CORE))
+    where = stage(after(where, qkv), w_out)
     parts = core_out(where, qkv, steps, *fwd, norm_gain, w_out, CHUNKS, n_head)
     where = stage(after(where, parts), w_gate, w_up, w_down)
-    bwd = spread_near(after(bwd, parts))
-    normed, attn = norm_rows(where, hidden_in, after(send_heads(parts), bwd), gain_moe, CHUNKS)
-
-    evens = list(range(0, n_ctx, 2))
-    near, rows = [], []
+    normed, attn = norm_rows(where, hidden_in, send_heads(parts), gain_moe, CHUNKS)
+    bwd = spread_near(after(bwd, normed))
+
+    near, came, owns = [], [], []
     own = join_rows(where, send_heads([normed[0]] * n_head))
     bwd = (bwd, swap(after(bwd, own), CORE))
     for chunk in range(CHUNKS):
-        near.append([own] + [swap(own, mask) for mask in evens[1:]])
+        owns.append(own)
+        came.append(depart(own))
         if chunk + 1 < CHUNKS:
             own = join_rows(where, send_heads([after(normed[chunk + 1], own)] * n_head))
-            near[chunk] = after(near[chunk], own)
+            came[chunk] = after(came[chunk], own)
+    evens = list(range(0, n_ctx, 2))
+    rows = []
     for chunk in range(CHUNKS):
-        rows.append({mask: part for mask, part in zip(evens, near[chunk])})
+        near = forward(owns[chunk], came[chunk])
+        rows.append({mask: part for mask, part in zip(evens, near)})
         rows[chunk] |= {mask | CORE: swap(part, CORE) for mask, part in rows[chunk].items()}
 
-    sums, pending = [], []
+    pending, sums = [], []
     for chunk in range(CHUNKS):
         here, far = expert_pieces(chunk * chunk_rows, where, rows[chunk], evens, w_gate, w_up, w_down, bwd)
-        arrived = swap(after(far, near[chunk + 1] if chunk + 1 < CHUNKS else pending[-1][2]), CORE)
-        leaving = [plus(here[at], arrived[at]) for at in range(1, len(evens))]
+        arrived = swap(after(far, came[chunk + 1] if chunk + 1 < CHUNKS else pending[-1][3]), CORE)
+        if pending:
+            pending[-1] += (last_sums(*pending[-1][:2], pending[-1][3]),)
+            arrived = after(arrived, [part for _, _, part in pending[-1][4]])
+        first = first_sums(here, arrived)
         if chunk + 1 < CHUNKS:
-            rows[chunk + 1] = after(rows[chunk + 1], leaving)
-        others = [swap(part, mask) for part, mask in zip(leaving, evens[1:])]
-        pending.append((here, arrived, others, leaving))
+            rows[chunk + 1] = after(rows[chunk + 1], [part for _, _, part in first])
+        pending.append((here, arrived, first, send_sums(first)))
+    pending[-1] += (last_sums(*pending[-1][:2], pending[-1][3]),)
     for chunk in range(CHUNKS):
-        here, arrived, others, _ = pending[chunk]
+        here, arrived, first, received, last = pending[chunk]
+        terms = list(zip([start for _, start, _ in first], received))
+        if last:
+            terms = terms[2:] + list(zip([start for _, start, _ in last], send_sums(last)))
+        starts, others = zip(*terms)
         if chunk + 1 < CHUNKS:
-            others = after(others, pending[chunk + 1][3])
-        sums.append(send_heads(sum_terms(where, attn[chunk], here, arrived, others, n_head)))
+            others = after(others, [part for _, _, part in pending[chunk + 1][2]])
+        sums.append(send_heads(sum_terms(where, attn[chunk], here, arrived, others, starts, n_head)))
     grads = core_grads(where, qkv, grad_core, steps, fwd, bwd)
     return (final_sum(where, hidden_in, sums), *grads)
 

time: 214 us -> 196 us (0.916)
  waiting for transfers between devices: 87.7 us -> 71.2 us
  local copies, waits for them, and re-layouts: 6.8 us -> 3.59 us
    ppermute x30 -> x38, waiting for transfers between devices: 48.1 us -> 33.5 us  [swap(): lax.ppermute(value, 'ctx', [pair for pair in pairs if keep is None or kee...]
    ppermute x30 -> x38, starting transfers between devices: 33.7 us -> 39.8 us  [swap(): lax.ppermute(value, 'ctx', [pair for pair in pairs if keep is None or kee...]
    ppermute x15, starting transfers between devices: 30.9 us -> 26.6 us  [send_heads(): lax.ppermute(parts[mask], 'head', [(at, at ^ mask) for at in range(count)])]
    unnamed x48 -> x36, local copies, waits for them, and re-layouts: 6.8 us -> 3.48 us
  transfers between devices with their start and end apart: 46 -> 54, of which waited for: 19 -> 22; matrix products, arithmetic and copies ran while one was open for 1% -> 1% of each run, Pallas kernels for 15% -> 17%
where the time goes in v7:
time: 196 us
  waiting for transfers between devices  71.2 us (36%)
  starting transfers between devices  68.9 us (35%)
  Pallas kernels  49.4 us (25%)
  local copies, waits for them, and re-layouts  3.59 us (2%)
    ppermute x38, starting transfers between devices, swap(): lax.ppermute(value, 'ctx', [pair for pair in pairs if keep is None or kee...  39.8 us
    ppermute x15, waiting for transfers between devices, send_heads(): lax.ppermute(parts[mask], 'head', [(at, at ^ mask) for at in range(count)])  36.7 us
    ppermute x38, waiting for transfers between devices, swap(): lax.ppermute(value, 'ctx', [pair for pair in pairs if keep is None or kee...  33.5 us
    ppermute x15, starting transfers between devices, send_heads(): lax.ppermute(parts[mask], 'head', [(at, at ^ mask) for at in range(count)])  26.6 us
    pallas_call x2, Pallas kernels, expert_pieces(): pl.pallas_call(functools.partial(expert_kernel, tuple(masks), chunk, expe...  23.4 us
    pallas_call x1, Pallas kernels, project(): pl.pallas_call(qkv_kernel, in_specs=[hbm, vmem, hbm], out_specs=[vmem, vm...  6.69 us
    pallas_call x1, Pallas kernels, core_grads(): pl.pallas_call(grad_kernel, in_specs=[pl.BlockSpec(memory_space=pltpu.SME...  5.23 us
    pallas_call x1, Pallas kernels, core_out(): pl.pallas_call(functools.partial(core_kernel, chunks), in_specs=[pl.Block...  4.34 us
  transfers between devices with their start and end apart: 54, of which 22 were waited for; matrix products, arithmetic and copies ran while one was open for 1% of the time, Pallas kernels for 17%

profile of v7, /device:TPU:0, one launch (start us, length us, event | category | flops | bytes accessed | tf_op | source)
XLA Modules:
  0.0 195.7 jit_solution(17986926654204181057)
XLA Ops:
  0.7 6.7 %qkv_projection.1 = (bf16[3,256,512]{2,1,0:T(8,128)(2,1)}, bf16[3,16,512]{2,1,0:T(8,128)(2,1)}) custom-call(bf16[256,2048]{1,0:T(8,128)(2,1)} %x_ref.3, f32[1,2048]{1,0:T(1,128)} %bitcast.68, bf16[3,2048,512]{2,1,0:T(8,128)(2,1)} %bitcast.61), custom_call_target="tpu_custom_call" | custom-call | tf_op jit(solution)/shard_map/qkv_projection/pallas_call | solution.py:58
  7.4 2.5 %collective-permute-start = (bf16[3,16,512]{2,1,0:T(8,128)(2,1)}, bf16[3,16,512]{2,1,0:T(8,128)(2,1)S(1)}, u32[]{:S(2)}, u32[]{:S(2)}) collective-permute-start(bf16[3,16,512]{2,1,0:T(8,128)(2,1)} %get-tuple-element.55), channel_id=1, source_target_pairs={{0,4},{4,8},{8,12},{12,16},{16,20},{20,24},{24,28},{1,5},{5,9},{9,... | collective-permute-start | bytes 147464 | tf_op jit(solution)/shard_map/ppermute | solution.py:600
  9.9 1.1 collective-permute-done.rim_ref
  11.0 1.1 copy-done.8
  12.1 2.1 %conv_states.1 = (bf16[3,256,512]{2,1,0:T(8,128)(2,1)S(1)}, bf16[576,128]{1,0:T(8,128)(2,1)S(1)}, bf16[672,128]{1,0:T(8,128)(2,1)S(1)}) custom-call(bf16[3,256,512]{2,1,0:T(8,128)(2,1)S(1)} %copy-done.8, bf16[3,16,512]{2,1,0:T(8,128)(2,1)S(1)} %collective-permute-done.rim_ref, f32[3,4,512]{2,1,0:T(4,128)S(1)} %bitcast.56, f32[4,256]{1,0:T(4,128)S(1)} %bitcast.53, ...), custom_call_target="tpu_custom_call" | custom-call | tf_op jit(solution)/shard_map/conv_states/pallas_call | solution.py:151
  14.9 8.0 %collective-permute-start.3 = (bf16[576,128]{1,0:T(8,128)(2,1)S(1)}, bf16[576,128]{1,0:T(8,128)(2,1)S(1)}, u32[]{:S(2)}, u32[]{:S(2)}) collective-permute-start(bf16[576,128]{1,0:T(8,128)(2,1)S(1)} %get-tuple-element.58), channel_id=1, source_target_pairs={{0,24},{4,28},{8,16},{12,20},{1,25},{5,29},{9,17},{13,21},{2,26},{... | collective-permute-start | bytes 442376 | tf_op jit(solution)/shard_map/ppermute | solution.py:439
  22.9 1.3 collective-permute-start.2
  24.2 3.3 %collective-permute-start.1 = (bf16[576,128]{1,0:T(8,128)(2,1)S(1)}, bf16[576,128]{1,0:T(8,128)(2,1)S(1)}, u32[]{:S(2)}, u32[]{:S(2)}) collective-permute-start(bf16[576,128]{1,0:T(8,128)(2,1)S(1)} %get-tuple-element.58), channel_id=1, source_target_pairs={{0,8},{4,12},{16,24},{20,28},{1,9},{5,13},{17,25},{21,29},{2,10},{... | collective-permute-start | bytes 442376 | tf_op jit(solution)/shard_map/ppermute | solution.py:439
  27.6 1.1 collective-permute-done.2
  28.7 1.6 collective-permute-done.1
  30.5 1.1 stage_weights.2.me_ref.where_ref
  32.5 4.3 %core_out.1 = (bf16[64,2048]{1,0:T(8,128)(2,1)S(1)}, bf16[64,2048]{1,0:T(8,128)(2,1)S(1)}, bf16[64,2048]{1,0:T(8,128)(2,1)S(1)}, bf16[64,2048]{1,0:T(8,128)(2,1)S(1)}) custom-call(s32[3]{0:T(128)S(1)} %stage_weights.2.me_ref.where_ref, bf16[3,256,512]{2,1,0:T(8,128)(2,1)S(1)} %get-tuple-element.56.qkv_ref, f32[4,256]{1,0:T(4,128)S(1)} %bitcast.54, ...), custom_call_target="tpu_custom_call" | custom-call | tf_op jit(solution)/shard_map/core_out/pallas_call | solution.py:213
  36.9 1.6 collective-permute-start.5
  38.5 2.6 %collective-permute-start.6 = (bf16[64,2048]{1,0:T(8,128)(2,1)S(1)}, bf16[64,2048]{1,0:T(8,128)(2,1)S(1)}, u32[]{:S(2)}, u32[]{:S(2)}) collective-permute-start(bf16[64,2048]{1,0:T(8,128)(2,1)S(1)} %get-tuple-element.61), channel_id=1, source_target_pairs={{0,2},{1,3},{2,0},{3,1},{4,6},{5,7},{6,4},{7,5},{8,10},{9,11},{10,... | collective-permute-start | bytes 786440 | tf_op jit(solution)/shard_map/ppermute | solution.py:445
  41.3 1.6 copy-done.4
  42.9 1.1 stage_weights.3.where_ref.me_ref
  44.1 6.5 %collective-permute-done.5.refs_1_ = bf16[64,2048]{1,0:T(8,128)(2,1)S(1)} collective-permute-done((bf16[64,2048]{1,0:T(8,128)(2,1)S(1)}, bf16[64,2048]{1,0:T(8,128)(2,1)S(1)}, u32[]{:S(2)}, u32[]{:S(2)}) %collective-permute-start.5) | collective-permute-done | bytes 262176 | tf_op jit(solution)/shard_map/ppermute | solution.py:445
  50.6 9.3 %collective-permute-done.6.refs_2_ = bf16[64,2048]{1,0:T(8,128)(2,1)S(1)} collective-permute-done((bf16[64,2048]{1,0:T(8,128)(2,1)S(1)}, bf16[64,2048]{1,0:T(8,128)(2,1)S(1)}, u32[]{:S(2)}, u32[]{:S(2)}) %collective-permute-start.6) | collective-permute-done | bytes 262176 | tf_op jit(solution)/shard_map/ppermute | solution.py:445
  60.7 2.5 %collective-permute-start.13 = (bf16[32,2048]{1,0:T(8,128)(2,1)S(1)}, bf16[32,2048]{1,0:T(8,128)(2,1)S(1)}, u32[]{:S(2)}, u32[]{:S(2)}) collective-permute-start(bf16[32,2048]{1,0:T(8,128)(2,1)S(1)} %get-tuple-element.66.refs_0_), channel_id=1, source_target_pairs={{0,3},{1,2},{2,1},{3,0},{4,7},{5,6},{6,5},{7,4},{8,11},{9,10},{10,... | collective-permute-start | bytes 393224 | tf_op jit(solution)/shard_map/ppermute | solution.py:445
  63.3 5.7 %collective-permute-start.12 = (bf16[32,2048]{1,0:T(8,128)(2,1)S(1)}, bf16[32,2048]{1,0:T(8,128)(2,1)S(1)}, u32[]{:S(2)}, u32[]{:S(2)}) collective-permute-start(bf16[32,2048]{1,0:T(8,128)(2,1)S(1)} %get-tuple-element.66.refs_0_), channel_id=1, source_target_pairs={{0,2},{1,3},{2,0},{3,1},{4,6},{5,7},{6,4},{7,5},{8,10},{9,11},{10,... | collective-permute-start | bytes 393224 | tf_op jit(solution)/shard_map/ppermute | solution.py:445
  69.1 7.9 %collective-permute-done.12.refs_2_ = bf16[32,2048]{1,0:T(8,128)(2,1)S(1)} collective-permute-done((bf16[32,2048]{1,0:T(8,128)(2,1)S(1)}, bf16[32,2048]{1,0:T(8,128)(2,1)S(1)}, u32[]{:S(2)}, u32[]{:S(2)}) %collective-permute-start.12) | collective-permute-done | bytes 131104 | tf_op jit(solution)/shard_map/ppermute | solution.py:445
  77.6 1.3 collective-permute-start.16
  78.8 1.5 collective-permute-start.15
  80.3 2.6 %collective-permute-start.19 = (bf16[32,2048]{1,0:T(8,128)(2,1)S(1)}, bf16[32,2048]{1,0:T(8,128)(2,1)S(1)}, u32[]{:S(2)}, u32[]{:S(2)}) collective-permute-start(bf16[32,2048]{1,0:T(8,128)(2,1)S(1)} %get-tuple-element.70.refs_0_), channel_id=1, source_target_pairs={{0,3},{1,2},{2,1},{3,0},{4,7},{5,6},{6,5},{7,4},{8,11},{9,10},{10,... | collective-permute-start | bytes 393224 | tf_op jit(solution)/shard_map/ppermute | solution.py:445
  82.9 1.7 collective-permute-start.17
  84.7 3.5 %collective-permute-done.19.refs_3_ = bf16[32,2048]{1,0:T(8,128)(2,1)S(1)} collective-permute-done((bf16[32,2048]{1,0:T(8,128)(2,1)S(1)}, bf16[32,2048]{1,0:T(8,128)(2,1)S(1)}, u32[]{:S(2)}, u32[]{:S(2)}) %collective-permute-start.19) | collective-permute-done | bytes 131104 | tf_op jit(solution)/shard_map/ppermute | solution.py:445
  88.2 1.4 collective-permute-start.10
  89.6 2.7 %collective-permute-done.18.refs_2_ = bf16[32,2048]{1,0:T(8,128)(2,1)S(1)} collective-permute-done((bf16[32,2048]{1,0:T(8,128)(2,1)S(1)}, bf16[32,2048]{1,0:T(8,128)(2,1)S(1)}, u32[]{:S(2)}, u32[]{:S(2)}) %collective-permute-start.18) | collective-permute-done | bytes 131104 | tf_op jit(solution)/shard_map/ppermute | solution.py:445
  92.3 1.7 collective-permute-start.9
  95.4 1.7 collective-permute-start.21
  97.2 2.5 %collective-permute-done.9 = bf16[672,128]{1,0:T(8,128)(2,1)S(1)} collective-permute-done((bf16[672,128]{1,0:T(8,128)(2,1)S(1)}, bf16[672,128]{1,0:T(8,128)(2,1)S(1)}, u32[]{:S(2)}, u32[]{:S(2)}) %collective-permute-start.9) | collective-permute-done | bytes 172064 | tf_op jit(solution)/shard_map/ppermute | solution.py:439
  100.8 3.0 %collective-permute-done.20 = bf16[64,2048]{1,0:T(8,128)(2,1)S(1)} collective-permute-done((bf16[64,2048]{1,0:T(8,128)(2,1)S(1)}, bf16[64,2048]{1,0:T(8,128)(2,1)S(1)}, u32[]{:S(2)}, u32[]{:S(2)}) %collective-permute-start.20) | collective-permute-done | bytes 262176 | tf_op jit(solution)/shard_map/ppermute | solution.py:439
  103.9 1.2 collective-permute-done.21
  105.1 1.5 collective-permute-start.27
  106.6 1.1 collective-permute-start.26
  107.8 11.7 %expert_pieces.2 = (bf16[4,128,2048]{2,1,0:T(8,128)(2,1)S(1)}, bf16[4,128,2048]{2,1,0:T(8,128)(2,1)S(1)}) custom-call(s32[3]{0:T(128)S(1)} %stage_weights.3.where_ref.me_ref, bf16[4,672,128]{2,1,0:T(8,128)(2,1)S(1)} %pad_maximum_fusion.near_routes.bwd_near, bf16[4,672,128]{2,1,0:T(8,128)(2,1)S(1)} %collective-permute-done.14.far_routes.bwd_far, ...), custom_call_target="tpu_custom_call" | custom-call | flops 6442450944 | bytes 8388608 | tf_op jit(solution)/shard_map/expert_pieces/pallas_call | solution.py:407
  120.3 1.0 collective-permute-start.38
  121.3 0.9 collective-permute-start.39
  122.8 6.3 %collective-permute-done.38 = bf16[64,2048]{1,0:T(8,128)(2,1)S(1)} collective-permute-done((bf16[64,2048]{1,0:T(8,128)(2,1)S(1)}, bf16[64,2048]{1,0:T(8,128)(2,1)S(1)}, u32[]{:S(2)}, u32[]{:S(2)}) %collective-permute-start.38) | collective-permute-done | bytes 262176 | tf_op jit(solution)/shard_map/ppermute | solution.py:439
  130.3 1.1 collective-permute-start.33
  131.4 1.5 collective-permute-start.31
  134.4 11.7 %expert_pieces.3 = (bf16[4,128,2048]{2,1,0:T(8,128)(2,1)S(1)}, bf16[4,128,2048]{2,1,0:T(8,128)(2,1)S(1)}) custom-call(s32[3]{0:T(128)S(1)} %stage_weights.3.where_ref.me_ref, bf16[4,672,128]{2,1,0:T(8,128)(2,1)S(1)} %pad_maximum_fusion.near_routes.bwd_near, bf16[4,672,128]{2,1,0:T(8,128)(2,1)S(1)} %collective-permute-done.14.far_routes.bwd_far, ...), custom_call_target="tpu_custom_call" | custom-call | flops 6442450944 | bytes 8388608 | tf_op jit(solution)/shard_map/expert_pieces/pallas_call | solution.py:407
  146.5 3.9 %collective-permute-done.41.arrived_ref = bf16[4,128,2048]{2,1,0:T(8,128)(2,1)S(1)} collective-permute-done((bf16[4,128,2048]{2,1,0:T(8,128)(2,1)S(1)}, bf16[4,128,2048]{2,1,0:T(8,128)(2,1)S(1)}, u32[]{:S(2)}, u32[]{:S(2)}) %collective-permute-start.41) | collective-permute-done | bytes 2097184 | tf_op jit(solution)/shard_map/ppermute | solution.py:439
  150.8 1.1 collective-permute-start.49
  151.9 1.5 collective-permute-start.47
  153.9 1.0 collective-permute-start.32
  154.9 1.1 collective-permute-start.46
  156.0 4.0 %collective-permute-done.49 = bf16[64,2048]{1,0:T(8,128)(2,1)S(1)} collective-permute-done((bf16[64,2048]{1,0:T(8,128)(2,1)S(1)}, bf16[64,2048]{1,0:T(8,128)(2,1)S(1)}, u32[]{:S(2)}, u32[]{:S(2)}) %collective-permute-start.49) | collective-permute-done | bytes 262176 | tf_op jit(solution)/shard_map/ppermute | solution.py:439
  160.0 1.2 collective-permute-start.45
  161.5 1.4 collective-permute-start.50
  162.9 3.8 %collective-permute-done.34.refs_3_ = bf16[64,2048]{1,0:T(8,128)(2,1)S(1)} collective-permute-done((bf16[64,2048]{1,0:T(8,128)(2,1)S(1)}, bf16[64,2048]{1,0:T(8,128)(2,1)S(1)}, u32[]{:S(2)}, u32[]{:S(2)}) %collective-permute-start.34) | collective-permute-done | bytes 262176 | tf_op jit(solution)/shard_map/ppermute | solution.py:439
  166.7 1.0 collective-permute-start.48
  167.7 1.0 sum_terms.2
  168.7 1.1 collective-permute-start.42
  169.8 1.5 collective-permute-done.46.refs_1_
  171.2 2.3 %collective-permute-start.43 = (bf16[128,512]{1,0:T(8,128)(2,1)S(1)}, bf16[128,512]{1,0:T(8,128)(2,1)S(1)}, u32[]{:S(2)}, u32[]{:S(2)}) collective-permute-start(bf16[128,512]{1,0:T(8,128)(2,1)S(1)} %get-tuple-element.94), channel_id=1, source_target_pairs={{0,2},{1,3},{2,0},{3,1},{4,6},{5,7},{6,4},{7,5},{8,10},{9,11},{10,... | collective-permute-start | bytes 393224 | tf_op jit(solution)/shard_map/ppermute | solution.py:445
  173.6 1.5 collective-permute-start.44
  175.1 1.7 collective-permute-done.50.refs_3_
  176.8 1.0 sum_terms.3
  178.6 2.6 %collective-permute-start.52 = (bf16[128,512]{1,0:T(8,128)(2,1)S(1)}, bf16[128,512]{1,0:T(8,128)(2,1)S(1)}, u32[]{:S(2)}, u32[]{:S(2)}) collective-permute-start(bf16[128,512]{1,0:T(8,128)(2,1)S(1)} %get-tuple-element.99), channel_id=1, source_target_pairs={{0,2},{1,3},{2,0},{3,1},{4,6},{5,7},{6,4},{7,5},{8,10},{9,11},{10,... | collective-permute-start | bytes 393224 | tf_op jit(solution)/shard_map/ppermute | solution.py:445
  181.2 1.1 collective-permute-start.53
  182.3 5.2 %core_grads.1 = (bf16[256,512]{1,0:T(8,128)(2,1)}, bf16[256,512]{1,0:T(8,128)(2,1)}, bf16[256,512]{1,0:T(8,128)(2,1)}) custom-call(s32[3]{0:T(128)S(1)} %stage_weights.3.where_ref.me_ref, bf16[3,256,512]{2,1,0:T(8,128)(2,1)S(1)} %get-tuple-element.56.qkv_ref, bf16[256,512]{1,0:T(8,128)(2,1)S(1)} %copy-done.7, f32[4,256]{1,0:T(4,128)S(1)} %bitcast.55, ...), custom_call_target="tpu_custom_call" | custom-call | tf_op jit(solution)/shard_map/core_grads/pallas_call | solution.py:258
  187.5 6.7 %collective-permute-done.52.refs_6_ = bf16[128,512]{1,0:T(8,128)(2,1)S(1)} collective-permute-done((bf16[128,512]{1,0:T(8,128)(2,1)S(1)}, bf16[128,512]{1,0:T(8,128)(2,1)S(1)}, u32[]{:S(2)}, u32[]{:S(2)}) %collective-permute-start.52) | collective-permute-done | bytes 131104 | tf_op jit(solution)/shard_map/ppermute | solution.py:445
  194.3 1.4 layer_out.1
  (107 shorter events, 12.7 us)
Async XLA Ops:
  0.6 10.3 %copy-start.6 = (bf16[256,512]{1,0:T(8,128)(2,1)S(1)}, bf16[256,512]{1,0:T(8,128)(2,1)}, u32[]{:S(2)}) copy-start(bf16[256,512]{1,0:T(8,128)(2,1)} %cot_ref.3) | copy-start | bytes 786436
  0.6 10.3 %copy-start.11 = (f32[256,4]{0,1:T(4,128)S(1)}, f32[256,4]{0,1:T(4,128)}, u32[]{:S(2)}) copy-start(f32[256,4]{0,1:T(4,128)} %param.18) | copy-start | bytes 12292
  0.7 10.3 %copy-start.12 = (f32[4,3,512]{2,0,1:T(4,128)S(1)}, f32[4,3,512]{2,0,1:T(4,128)}, u32[]{:S(2)}) copy-start(f32[4,3,512]{2,0,1:T(4,128)} %param.17) | copy-start | bytes 73732
  7.4 23.1 %copy-start.1 = (bf16[512,2048]{1,0:T(8,128)(2,1)S(1)}, bf16[512,2048]{1,0:T(8,128)(2,1)}, u32[]{:S(2)}) copy-start(bf16[512,2048]{1,0:T(8,128)(2,1)} %w_ref.1) | copy-start | bytes 6291460
  7.4 3.6 %collective-permute-start = (bf16[3,16,512]{2,1,0:T(8,128)(2,1)}, bf16[3,16,512]{2,1,0:T(8,128)(2,1)S(1)}, u32[]{:S(2)}, u32[]{:S(2)}) collective-permute-start(bf16[3,16,512]{2,1,0:T(8,128)(2,1)} %get-tuple-element.55), channel_id=1, source_target_pairs={{0,4},{4,8},{8,12},{12,16},{16,20},{20,24},{24,28},{1,5},{5,9},{9,... | collective-permute-start | bytes 147464 | tf_op jit(solution)/shard_map/ppermute | solution.py:600
  12.1 20.4 %copy-start.16 = (f32[512]{0:T(512)S(1)}, f32[512]{0:T(512)}, u32[]{:S(2)}) copy-start(f32[512]{0:T(512)} %param.19) | copy-start | bytes 6148
  14.9 12.7 %collective-permute-start.3 = (bf16[576,128]{1,0:T(8,128)(2,1)S(1)}, bf16[576,128]{1,0:T(8,128)(2,1)S(1)}, u32[]{:S(2)}, u32[]{:S(2)}) collective-permute-start(bf16[576,128]{1,0:T(8,128)(2,1)S(1)} %get-tuple-element.58), channel_id=1, source_target_pairs={{0,24},{4,28},{8,16},{12,20},{1,25},{5,29},{9,17},{13,21},{2,26},{... | collective-permute-start | bytes 442376 | tf_op jit(solution)/shard_map/ppermute | solution.py:439
  22.9 5.7 %collective-permute-start.2 = (bf16[576,128]{1,0:T(8,128)(2,1)S(1)}, bf16[576,128]{1,0:T(8,128)(2,1)S(1)}, u32[]{:S(2)}, u32[]{:S(2)}) collective-permute-start(bf16[576,128]{1,0:T(8,128)(2,1)S(1)} %get-tuple-element.58), channel_id=1, source_target_pairs={{0,16},{4,20},{8,24},{12,28},{1,17},{5,21},{9,25},{13,29},{2,18},{... | collective-permute-start | bytes 442376 | tf_op jit(solution)/shard_map/ppermute | solution.py:439
  24.2 6.0 %collective-permute-start.1 = (bf16[576,128]{1,0:T(8,128)(2,1)S(1)}, bf16[576,128]{1,0:T(8,128)(2,1)S(1)}, u32[]{:S(2)}, u32[]{:S(2)}) collective-permute-start(bf16[576,128]{1,0:T(8,128)(2,1)S(1)} %get-tuple-element.58), channel_id=1, source_target_pairs={{0,8},{4,12},{16,24},{20,28},{1,9},{5,13},{17,25},{21,29},{2,10},{... | collective-permute-start | bytes 442376 | tf_op jit(solution)/shard_map/ppermute | solution.py:439
  30.3 2.2 %collective-permute-start.4 = (bf16[4,576,128]{2,1,0:T(8,128)(2,1)S(1)}, bf16[4,576,128]{2,1,0:T(8,128)(2,1)}, u32[]{:S(2)}, u32[]{:S(2)}) collective-permute-start(bf16[4,576,128]{2,1,0:T(8,128)(2,1)S(1)} %pad_maximum_fusion.1.near_ref.fwd_near), channel_id=1, source_target_pairs={{0,4},{4,0},{8,12},{12,8},{16,20},{20,16},{24,28},{28,24},{1,5},{5... | collective-permute-start | bytes 1769480 | tf_op jit(solution)/shard_map/ppermute | solution.py:439
  30.5 10.8 %copy-start.3 = (bf16[1,2048,512]{2,1,0:T(8,128)(2,1)S(1)}, bf16[1,2048,512]{2,1,0:T(8,128)(2,1)}, u32[]{:S(2)}) copy-start(bf16[1,2048,512]{2,1,0:T(8,128)(2,1)} %up_ref.3) | copy-start | bytes 6291460
  36.9 13.7 %collective-permute-start.5 = (bf16[64,2048]{1,0:T(8,128)(2,1)S(1)}, bf16[64,2048]{1,0:T(8,128)(2,1)S(1)}, u32[]{:S(2)}, u32[]{:S(2)}) collective-permute-start(bf16[64,2048]{1,0:T(8,128)(2,1)S(1)} %get-tuple-element.60), channel_id=1, source_target_pairs={{0,1},{1,0},{2,3},{3,2},{4,5},{5,4},{6,7},{7,6},{8,9},{9,8},{10,11... | collective-permute-start | bytes 786440 | tf_op jit(solution)/shard_map/ppermute | solution.py:445
  38.5 21.3 %collective-permute-start.6 = (bf16[64,2048]{1,0:T(8,128)(2,1)S(1)}, bf16[64,2048]{1,0:T(8,128)(2,1)S(1)}, u32[]{:S(2)}, u32[]{:S(2)}) collective-permute-start(bf16[64,2048]{1,0:T(8,128)(2,1)S(1)} %get-tuple-element.61), channel_id=1, source_target_pairs={{0,2},{1,3},{2,0},{3,1},{4,6},{5,7},{6,4},{7,5},{8,10},{9,11},{10,... | collective-permute-start | bytes 786440 | tf_op jit(solution)/shard_map/ppermute | solution.py:445
  41.1 18.7 %collective-permute-start.7 = (bf16[64,2048]{1,0:T(8,128)(2,1)S(1)}, bf16[64,2048]{1,0:T(8,128)(2,1)S(1)}, u32[]{:S(2)}, u32[]{:S(2)}) collective-permute-start(bf16[64,2048]{1,0:T(8,128)(2,1)S(1)} %get-tuple-element.62), channel_id=1, source_target_pairs={{0,3},{1,2},{2,1},{3,0},{4,7},{5,6},{6,5},{7,4},{8,11},{9,10},{10,... | collective-permute-start | bytes 786440 | tf_op jit(solution)/shard_map/ppermute | solution.py:445
  42.9 16.9 %copy-start = (bf16[256,2048]{1,0:T(8,128)(2,1)S(1)}, bf16[256,2048]{1,0:T(8,128)(2,1)}, u32[]{:S(2)}) copy-start(bf16[256,2048]{1,0:T(8,128)(2,1)} %x_ref.3) | copy-start | bytes 3145732
  42.9 16.9 %copy-start.15 = (f32[2048]{0:T(1024)S(1)}, f32[2048]{0:T(1024)}, u32[]{:S(2)}) copy-start(f32[2048]{0:T(1024)} %param.21) | copy-start | bytes 24580
  44.1 44.1 %copy-start.10 = (bf16[672,128]{1,0:T(8,128)(2,1)S(1)}, bf16[672,128]{1,0:T(8,128)(2,1)}, u32[]{:S(2)}) copy-start(bf16[672,128]{1,0:T(8,128)(2,1)} %copy-done.9) | copy-start | bytes 516100
  60.7 8.3 %collective-permute-start.13 = (bf16[32,2048]{1,0:T(8,128)(2,1)S(1)}, bf16[32,2048]{1,0:T(8,128)(2,1)S(1)}, u32[]{:S(2)}, u32[]{:S(2)}) collective-permute-start(bf16[32,2048]{1,0:T(8,128)(2,1)S(1)} %get-tuple-element.66.refs_0_), channel_id=1, source_target_pairs={{0,3},{1,2},{2,1},{3,0},{4,7},{5,6},{6,5},{7,4},{8,11},{9,10},{10,... | collective-permute-start | bytes 393224 | tf_op jit(solution)/shard_map/ppermute | solution.py:445
  63.3 13.7 %collective-permute-start.12 = (bf16[32,2048]{1,0:T(8,128)(2,1)S(1)}, bf16[32,2048]{1,0:T(8,128)(2,1)S(1)}, u32[]{:S(2)}, u32[]{:S(2)}) collective-permute-start(bf16[32,2048]{1,0:T(8,128)(2,1)S(1)} %get-tuple-element.66.refs_0_), channel_id=1, source_target_pairs={{0,2},{1,3},{2,0},{3,1},{4,6},{5,7},{6,4},{7,5},{8,10},{9,11},{10,... | collective-permute-start | bytes 393224 | tf_op jit(solution)/shard_map/ppermute | solution.py:445
  68.9 8.0 %collective-permute-start.11 = (bf16[32,2048]{1,0:T(8,128)(2,1)S(1)}, bf16[32,2048]{1,0:T(8,128)(2,1)S(1)}, u32[]{:S(2)}, u32[]{:S(2)}) collective-permute-start(bf16[32,2048]{1,0:T(8,128)(2,1)S(1)} %get-tuple-element.66.refs_0_), channel_id=1, source_target_pairs={{0,1},{1,0},{2,3},{3,2},{4,5},{5,4},{6,7},{7,6},{8,9},{9,8},{10,11... | collective-permute-start | bytes 393224 | tf_op jit(solution)/shard_map/ppermute | solution.py:445
  77.6 17.3 %collective-permute-start.16 = (bf16[128,2048]{1,0:T(8,128)(2,1)S(1)}, bf16[128,2048]{1,0:T(8,128)(2,1)S(1)}, u32[]{:S(2)}, u32[]{:S(2)}) collective-permute-start(bf16[128,2048]{1,0:T(8,128)(2,1)S(1)} %join_rows.2.refs_0_), channel_id=1, source_target_pairs={{0,16},{4,20},{8,24},{12,28},{16,0},{20,4},{24,8},{28,12},{1,17},{... | collective-permute-start | bytes 1572872 | tf_op jit(solution)/shard_map/ppermute | solution.py:439
  78.8 16.0 %collective-permute-start.15 = (bf16[128,2048]{1,0:T(8,128)(2,1)S(1)}, bf16[128,2048]{1,0:T(8,128)(2,1)S(1)}, u32[]{:S(2)}, u32[]{:S(2)}) collective-permute-start(bf16[128,2048]{1,0:T(8,128)(2,1)S(1)} %join_rows.2.refs_0_), channel_id=1, source_target_pairs={{0,8},{4,12},{8,0},{12,4},{16,24},{20,28},{24,16},{28,20},{1,9},{5... | collective-permute-start | bytes 1572872 | tf_op jit(solution)/shard_map/ppermute | solution.py:439
  80.3 7.9 %collective-permute-start.19 = (bf16[32,2048]{1,0:T(8,128)(2,1)S(1)}, bf16[32,2048]{1,0:T(8,128)(2,1)S(1)}, u32[]{:S(2)}, u32[]{:S(2)}) collective-permute-start(bf16[32,2048]{1,0:T(8,128)(2,1)S(1)} %get-tuple-element.70.refs_0_), channel_id=1, source_target_pairs={{0,3},{1,2},{2,1},{3,0},{4,7},{5,6},{6,5},{7,4},{8,11},{9,10},{10,... | collective-permute-start | bytes 393224 | tf_op jit(solution)/shard_map/ppermute | solution.py:445
  82.9 9.4 %collective-permute-start.18 = (bf16[32,2048]{1,0:T(8,128)(2,1)S(1)}, bf16[32,2048]{1,0:T(8,128)(2,1)S(1)}, u32[]{:S(2)}, u32[]{:S(2)}) collective-permute-start(bf16[32,2048]{1,0:T(8,128)(2,1)S(1)} %get-tuple-element.70.refs_0_), channel_id=1, source_target_pairs={{0,2},{1,3},{2,0},{3,1},{4,6},{5,7},{6,4},{7,5},{8,10},{9,11},{10,... | collective-permute-start | bytes 393224 | tf_op jit(solution)/shard_map/ppermute | solution.py:445
  82.9 11.0 %collective-permute-start.17 = (bf16[32,2048]{1,0:T(8,128)(2,1)S(1)}, bf16[32,2048]{1,0:T(8,128)(2,1)S(1)}, u32[]{:S(2)}, u32[]{:S(2)}) collective-permute-start(bf16[32,2048]{1,0:T(8,128)(2,1)S(1)} %get-tuple-element.70.refs_0_), channel_id=1, source_target_pairs={{0,1},{1,0},{2,3},{3,2},{4,5},{5,4},{6,7},{7,6},{8,9},{9,8},{10,11... | collective-permute-start | bytes 393224 | tf_op jit(solution)/shard_map/ppermute | solution.py:445
  84.7 23.1 %copy-start.5 = (bf16[1,512,2048]{2,1,0:T(8,128)(2,1)S(1)}, bf16[1,512,2048]{2,1,0:T(8,128)(2,1)}, u32[]{:S(2)}) copy-start(bf16[1,512,2048]{2,1,0:T(8,128)(2,1)} %down_ref.3) | copy-start | bytes 6291460
  88.2 7.2 %collective-permute-start.10 = (bf16[672,128]{1,0:T(8,128)(2,1)S(1)}, bf16[672,128]{1,0:T(8,128)(2,1)S(1)}, u32[]{:S(2)}, u32[]{:S(2)}) collective-permute-start(bf16[672,128]{1,0:T(8,128)(2,1)S(1)} %copy-done.10), channel_id=1, source_target_pairs={{0,24},{4,28},{8,16},{12,20},{16,8},{20,12},{24,0},{28,4},{1,25},{... | collective-permute-start | bytes 516104 | tf_op jit(solution)/shard_map/ppermute | solution.py:439
  92.3 7.3 %collective-permute-start.9 = (bf16[672,128]{1,0:T(8,128)(2,1)S(1)}, bf16[672,128]{1,0:T(8,128)(2,1)S(1)}, u32[]{:S(2)}, u32[]{:S(2)}) collective-permute-start(bf16[672,128]{1,0:T(8,128)(2,1)S(1)} %copy-done.10), channel_id=1, source_target_pairs={{0,16},{4,20},{8,24},{12,28},{16,0},{20,4},{24,8},{28,12},{1,17},{... | collective-permute-start | bytes 516104 | tf_op jit(solution)/shard_map/ppermute | solution.py:439
  94.0 6.2 %collective-permute-start.8 = (bf16[672,128]{1,0:T(8,128)(2,1)S(1)}, bf16[672,128]{1,0:T(8,128)(2,1)S(1)}, u32[]{:S(2)}, u32[]{:S(2)}) collective-permute-start(bf16[672,128]{1,0:T(8,128)(2,1)S(1)} %copy-done.10), channel_id=1, source_target_pairs={{0,8},{4,12},{8,0},{12,4},{16,24},{20,28},{24,16},{28,20},{1,9},{5... | collective-permute-start | bytes 516104 | tf_op jit(solution)/shard_map/ppermute | solution.py:439
  94.9 8.9 %collective-permute-start.20 = (bf16[64,2048]{1,0:T(8,128)(2,1)S(1)}, bf16[64,2048]{1,0:T(8,128)(2,1)S(1)}, u32[]{:S(2)}, u32[]{:S(2)}) collective-permute-start(bf16[64,2048]{1,0:T(8,128)(2,1)S(1)} %slice.84), channel_id=1, source_target_pairs={{0,16},{4,20},{8,24},{12,28},{16,0},{20,4},{24,8},{28,12},{1,17},{... | collective-permute-start | bytes 786440 | tf_op jit(solution)/shard_map/ppermute | solution.py:439
  95.4 9.7 %collective-permute-start.22 = (bf16[128,2048]{1,0:T(8,128)(2,1)S(1)}, bf16[128,2048]{1,0:T(8,128)(2,1)S(1)}, u32[]{:S(2)}, u32[]{:S(2)}) collective-permute-start(bf16[128,2048]{1,0:T(8,128)(2,1)S(1)} %join_rows.2.refs_0_), channel_id=1, source_target_pairs={{0,4},{4,0},{8,12},{12,8},{16,20},{20,16},{24,28},{28,24},{1,5},{5... | collective-permute-start | bytes 1572872 | tf_op jit(solution)/shard_map/ppermute | solution.py:439
  95.4 9.6 %collective-permute-start.21 = (bf16[64,2048]{1,0:T(8,128)(2,1)S(1)}, bf16[64,2048]{1,0:T(8,128)(2,1)S(1)}, u32[]{:S(2)}, u32[]{:S(2)}) collective-permute-start(bf16[64,2048]{1,0:T(8,128)(2,1)S(1)} %slice.85), channel_id=1, source_target_pairs={{0,8},{4,12},{8,0},{12,4},{16,24},{20,28},{24,16},{28,20},{1,9},{5... | collective-permute-start | bytes 786440 | tf_op jit(solution)/shard_map/ppermute | solution.py:439
  100.3 6.3 %collective-permute-start.14 = (bf16[4,672,128]{2,1,0:T(8,128)(2,1)S(1)}, bf16[4,672,128]{2,1,0:T(8,128)(2,1)S(1)}, u32[]{:S(2)}, u32[]{:S(2)}) collective-permute-start(bf16[4,672,128]{2,1,0:T(8,128)(2,1)S(1)} %pad_maximum_fusion.near_routes.bwd_near), channel_id=1, source_target_pairs={{0,4},{4,0},{8,12},{12,8},{16,20},{20,16},{24,28},{28,24},{1,5},{5... | collective-permute-start | bytes 2064392 | tf_op jit(solution)/shard_map/ppermute | solution.py:439
  100.3 7.4 %collective-permute-start.23 = (bf16[128,2048]{1,0:T(8,128)(2,1)S(1)}, bf16[128,2048]{1,0:T(8,128)(2,1)S(1)}, u32[]{:S(2)}, u32[]{:S(2)}) collective-permute-start(bf16[128,2048]{1,0:T(8,128)(2,1)S(1)} %collective-permute-done.15.refs_1_), channel_id=1, source_target_pairs={{0,4},{4,0},{8,12},{12,8},{16,20},{20,16},{24,28},{28,24},{1,5},{5... | collective-permute-start | bytes 1572872 | tf_op jit(solution)/shard_map/ppermute | solution.py:439
  103.8 3.9 %collective-permute-start.24 = (bf16[128,2048]{1,0:T(8,128)(2,1)S(1)}, bf16[128,2048]{1,0:T(8,128)(2,1)S(1)}, u32[]{:S(2)}, u32[]{:S(2)}) collective-permute-start(bf16[128,2048]{1,0:T(8,128)(2,1)S(1)} %collective-permute-done.16.refs_2_), channel_id=1, source_target_pairs={{0,4},{4,0},{8,12},{12,8},{16,20},{20,16},{24,28},{28,24},{1,5},{5... | collective-permute-start | bytes 1572872 | tf_op jit(solution)/shard_map/ppermute | solution.py:439
  105.0 2.7 %collective-permute-start.25 = (bf16[128,2048]{1,0:T(8,128)(2,1)S(1)}, bf16[128,2048]{1,0:T(8,128)(2,1)S(1)}, u32[]{:S(2)}, u32[]{:S(2)}) collective-permute-start(bf16[128,2048]{1,0:T(8,128)(2,1)S(1)} %constant_dynamic-update-slice_fusion.refs_3_), channel_id=1, source_target_pairs={{0,4},{4,0},{8,12},{12,8},{16,20},{20,16},{24,28},{28,24},{1,5},{5... | collective-permute-start | bytes 1572872 | tf_op jit(solution)/shard_map/ppermute | solution.py:439
  105.1 14.3 %collective-permute-start.27 = (bf16[128,2048]{1,0:T(8,128)(2,1)S(1)}, bf16[128,2048]{1,0:T(8,128)(2,1)S(1)}, u32[]{:S(2)}, u32[]{:S(2)}) collective-permute-start(bf16[128,2048]{1,0:T(8,128)(2,1)S(1)} %join_rows.3.refs_0_), channel_id=1, source_target_pairs={{0,16},{4,20},{8,24},{12,28},{16,0},{20,4},{24,8},{28,12},{1,17},{... | collective-permute-start | bytes 1572872 | tf_op jit(solution)/shard_map/ppermute | solution.py:439
  106.6 13.6 %collective-permute-start.26 = (bf16[128,2048]{1,0:T(8,128)(2,1)S(1)}, bf16[128,2048]{1,0:T(8,128)(2,1)S(1)}, u32[]{:S(2)}, u32[]{:S(2)}) collective-permute-start(bf16[128,2048]{1,0:T(8,128)(2,1)S(1)} %join_rows.3.refs_0_), channel_id=1, source_target_pairs={{0,8},{4,12},{8,0},{12,4},{16,24},{20,28},{24,16},{28,20},{1,9},{5... | collective-permute-start | bytes 1572872 | tf_op jit(solution)/shard_map/ppermute | solution.py:439
  120.2 9.7 %collective-permute-start.28 = (bf16[4,128,2048]{2,1,0:T(8,128)(2,1)S(1)}, bf16[4,128,2048]{2,1,0:T(8,128)(2,1)S(1)}, u32[]{:S(2)}, u32[]{:S(2)}) collective-permute-start(bf16[4,128,2048]{2,1,0:T(8,128)(2,1)S(1)} %get-tuple-element.75), channel_id=1, source_target_pairs={{0,4},{4,0},{8,12},{12,8},{16,20},{20,16},{24,28},{28,24},{1,5},{5... | collective-permute-start | bytes 6291464 | tf_op jit(solution)/shard_map/ppermute | solution.py:439
  120.3 8.8 %collective-permute-start.38 = (bf16[64,2048]{1,0:T(8,128)(2,1)S(1)}, bf16[64,2048]{1,0:T(8,128)(2,1)S(1)}, u32[]{:S(2)}, u32[]{:S(2)}) collective-permute-start(bf16[64,2048]{1,0:T(8,128)(2,1)S(1)} %slice.118), channel_id=1, source_target_pairs={{0,16},{4,20},{8,24},{12,28},{16,0},{20,4},{24,8},{28,12},{1,17},{... | collective-permute-start | bytes 786440 | tf_op jit(solution)/shard_map/ppermute | solution.py:439
  121.3 8.5 %collective-permute-start.39 = (bf16[64,2048]{1,0:T(8,128)(2,1)S(1)}, bf16[64,2048]{1,0:T(8,128)(2,1)S(1)}, u32[]{:S(2)}, u32[]{:S(2)}) collective-permute-start(bf16[64,2048]{1,0:T(8,128)(2,1)S(1)} %slice.119), channel_id=1, source_target_pairs={{0,8},{4,12},{8,0},{12,4},{16,24},{20,28},{24,16},{28,20},{1,9},{5... | collective-permute-start | bytes 786440 | tf_op jit(solution)/shard_map/ppermute | solution.py:439
  122.3 9.2 %collective-permute-start.35 = (bf16[128,2048]{1,0:T(8,128)(2,1)S(1)}, bf16[128,2048]{1,0:T(8,128)(2,1)S(1)}, u32[]{:S(2)}, u32[]{:S(2)}) collective-permute-start(bf16[128,2048]{1,0:T(8,128)(2,1)S(1)} %join_rows.3.refs_0_), channel_id=1, source_target_pairs={{0,4},{4,0},{8,12},{12,8},{16,20},{20,16},{24,28},{28,24},{1,5},{5... | collective-permute-start | bytes 1572872 | tf_op jit(solution)/shard_map/ppermute | solution.py:439
  122.3 10.7 %collective-permute-start.37 = (bf16[128,2048]{1,0:T(8,128)(2,1)S(1)}, bf16[128,2048]{1,0:T(8,128)(2,1)S(1)}, u32[]{:S(2)}, u32[]{:S(2)}) collective-permute-start(bf16[128,2048]{1,0:T(8,128)(2,1)S(1)} %collective-permute-done.27.refs_2_), channel_id=1, source_target_pairs={{0,4},{4,0},{8,12},{12,8},{16,20},{20,16},{24,28},{28,24},{1,5},{5... | collective-permute-start | bytes 1572872 | tf_op jit(solution)/shard_map/ppermute | solution.py:439
  129.0 4.6 %collective-permute-start.36 = (bf16[128,2048]{1,0:T(8,128)(2,1)S(1)}, bf16[128,2048]{1,0:T(8,128)(2,1)S(1)}, u32[]{:S(2)}, u32[]{:S(2)}) collective-permute-start(bf16[128,2048]{1,0:T(8,128)(2,1)S(1)} %collective-permute-done.26.refs_1_), channel_id=1, source_target_pairs={{0,4},{4,0},{8,12},{12,8},{16,20},{20,16},{24,28},{28,24},{1,5},{5... | collective-permute-start | bytes 1572872 | tf_op jit(solution)/shard_map/ppermute | solution.py:439
  129.8 4.6 %collective-permute-start.40 = (bf16[128,2048]{1,0:T(8,128)(2,1)S(1)}, bf16[128,2048]{1,0:T(8,128)(2,1)S(1)}, u32[]{:S(2)}, u32[]{:S(2)}) collective-permute-start(bf16[128,2048]{1,0:T(8,128)(2,1)S(1)} %constant_dynamic-update-slice_fusion.2.refs_3_), channel_id=1, source_target_pairs={{0,4},{4,0},{8,12},{12,8},{16,20},{20,16},{24,28},{28,24},{1,5},{5... | collective-permute-start | bytes 1572872 | tf_op jit(solution)/shard_map/ppermute | solution.py:439
  130.3 15.8 %collective-permute-start.33 = (bf16[64,2048]{1,0:T(8,128)(2,1)S(1)}, bf16[64,2048]{1,0:T(8,128)(2,1)S(1)}, u32[]{:S(2)}, u32[]{:S(2)}) collective-permute-start(bf16[64,2048]{1,0:T(8,128)(2,1)S(1)} %get-tuple-element.112), channel_id=1, source_target_pairs={{0,16},{4,20},{8,24},{12,28},{16,0},{20,4},{24,8},{28,12},{1,17},{... | collective-permute-start | bytes 786440 | tf_op jit(solution)/shard_map/ppermute | solution.py:439
  131.4 14.7 %collective-permute-start.31 = (bf16[64,2048]{1,0:T(8,128)(2,1)S(1)}, bf16[64,2048]{1,0:T(8,128)(2,1)S(1)}, u32[]{:S(2)}, u32[]{:S(2)}) collective-permute-start(bf16[64,2048]{1,0:T(8,128)(2,1)S(1)} %get-tuple-element.113), channel_id=1, source_target_pairs={{0,8},{4,12},{8,0},{12,4},{16,24},{20,28},{24,16},{28,20},{1,9},{5... | collective-permute-start | bytes 786440 | tf_op jit(solution)/shard_map/ppermute | solution.py:439
  132.9 13.2 %collective-permute-start.30 = (bf16[64,2048]{1,0:T(8,128)(2,1)S(1)}, bf16[64,2048]{1,0:T(8,128)(2,1)S(1)}, u32[]{:S(2)}, u32[]{:S(2)}) collective-permute-start(bf16[64,2048]{1,0:T(8,128)(2,1)S(1)} %get-tuple-element.114), channel_id=1, source_target_pairs={{0,16},{4,20},{8,24},{12,28},{16,0},{20,4},{24,8},{28,12},{1,17},{... | collective-permute-start | bytes 786440 | tf_op jit(solution)/shard_map/ppermute | solution.py:439
  133.7 12.5 %collective-permute-start.29 = (bf16[64,2048]{1,0:T(8,128)(2,1)S(1)}, bf16[64,2048]{1,0:T(8,128)(2,1)S(1)}, u32[]{:S(2)}, u32[]{:S(2)}) collective-permute-start(bf16[64,2048]{1,0:T(8,128)(2,1)S(1)} %get-tuple-element.115), channel_id=1, source_target_pairs={{0,8},{4,12},{8,0},{12,4},{16,24},{20,28},{24,16},{28,20},{1,9},{5... | collective-permute-start | bytes 786440 | tf_op jit(solution)/shard_map/ppermute | solution.py:439
  146.2 4.2 %collective-permute-start.41 = (bf16[4,128,2048]{2,1,0:T(8,128)(2,1)S(1)}, bf16[4,128,2048]{2,1,0:T(8,128)(2,1)S(1)}, u32[]{:S(2)}, u32[]{:S(2)}) collective-permute-start(bf16[4,128,2048]{2,1,0:T(8,128)(2,1)S(1)} %get-tuple-element.86), channel_id=1, source_target_pairs={{0,4},{4,0},{8,12},{12,8},{16,20},{20,16},{24,28},{28,24},{1,5},{5... | collective-permute-start | bytes 6291464 | tf_op jit(solution)/shard_map/ppermute | solution.py:439
  150.8 9.2 %collective-permute-start.49 = (bf16[64,2048]{1,0:T(8,128)(2,1)S(1)}, bf16[64,2048]{1,0:T(8,128)(2,1)S(1)}, u32[]{:S(2)}, u32[]{:S(2)}) collective-permute-start(bf16[64,2048]{1,0:T(8,128)(2,1)S(1)} %get-tuple-element.108), channel_id=1, source_target_pairs={{0,16},{4,20},{8,24},{12,28},{16,0},{20,4},{24,8},{28,12},{1,17},{... | collective-permute-start | bytes 786440 | tf_op jit(solution)/shard_map/ppermute | solution.py:439
  151.9 9.3 %collective-permute-start.47 = (bf16[64,2048]{1,0:T(8,128)(2,1)S(1)}, bf16[64,2048]{1,0:T(8,128)(2,1)S(1)}, u32[]{:S(2)}, u32[]{:S(2)}) collective-permute-start(bf16[64,2048]{1,0:T(8,128)(2,1)S(1)} %get-tuple-element.109), channel_id=1, source_target_pairs={{0,8},{4,12},{8,0},{12,4},{16,24},{20,28},{24,16},{28,20},{1,9},{5... | collective-permute-start | bytes 786440 | tf_op jit(solution)/shard_map/ppermute | solution.py:439
  153.4 13.3 %collective-permute-start.34 = (bf16[64,2048]{1,0:T(8,128)(2,1)S(1)}, bf16[64,2048]{1,0:T(8,128)(2,1)S(1)}, u32[]{:S(2)}, u32[]{:S(2)}) collective-permute-start(bf16[64,2048]{1,0:T(8,128)(2,1)S(1)} %get-tuple-element.110), channel_id=1, source_target_pairs={{0,8},{4,12},{8,0},{12,4},{16,24},{20,28},{24,16},{28,20},{1,9},{5... | collective-permute-start | bytes 786440 | tf_op jit(solution)/shard_map/ppermute | solution.py:439
  153.9 13.8 %collective-permute-start.32 = (bf16[64,2048]{1,0:T(8,128)(2,1)S(1)}, bf16[64,2048]{1,0:T(8,128)(2,1)S(1)}, u32[]{:S(2)}, u32[]{:S(2)}) collective-permute-start(bf16[64,2048]{1,0:T(8,128)(2,1)S(1)} %get-tuple-element.111), channel_id=1, source_target_pairs={{0,16},{4,20},{8,24},{12,28},{16,0},{20,4},{24,8},{28,12},{1,17},{... | collective-permute-start | bytes 786440 | tf_op jit(solution)/shard_map/ppermute | solution.py:439
  154.9 16.3 %collective-permute-start.46 = (bf16[64,2048]{1,0:T(8,128)(2,1)S(1)}, bf16[64,2048]{1,0:T(8,128)(2,1)S(1)}, u32[]{:S(2)}, u32[]{:S(2)}) collective-permute-start(bf16[64,2048]{1,0:T(8,128)(2,1)S(1)} %get-tuple-element.106), channel_id=1, source_target_pairs={{0,16},{4,20},{8,24},{12,28},{16,0},{20,4},{24,8},{28,12},{1,17},{... | collective-permute-start | bytes 786440 | tf_op jit(solution)/shard_map/ppermute | solution.py:439
  160.0 13.6 %collective-permute-start.45 = (bf16[64,2048]{1,0:T(8,128)(2,1)S(1)}, bf16[64,2048]{1,0:T(8,128)(2,1)S(1)}, u32[]{:S(2)}, u32[]{:S(2)}) collective-permute-start(bf16[64,2048]{1,0:T(8,128)(2,1)S(1)} %get-tuple-element.107), channel_id=1, source_target_pairs={{0,8},{4,12},{8,0},{12,4},{16,24},{20,28},{24,16},{28,20},{1,9},{5... | collective-permute-start | bytes 786440 | tf_op jit(solution)/shard_map/ppermute | solution.py:439
  161.5 15.3 %collective-permute-start.50 = (bf16[64,2048]{1,0:T(8,128)(2,1)S(1)}, bf16[64,2048]{1,0:T(8,128)(2,1)S(1)}, u32[]{:S(2)}, u32[]{:S(2)}) collective-permute-start(bf16[64,2048]{1,0:T(8,128)(2,1)S(1)} %get-tuple-element.104), channel_id=1, source_target_pairs={{0,8},{4,12},{8,0},{12,4},{16,24},{20,28},{24,16},{28,20},{1,9},{5... | collective-permute-start | bytes 786440 | tf_op jit(solution)/shard_map/ppermute | solution.py:439
  166.7 10.1 %collective-permute-start.48 = (bf16[64,2048]{1,0:T(8,128)(2,1)S(1)}, bf16[64,2048]{1,0:T(8,128)(2,1)S(1)}, u32[]{:S(2)}, u32[]{:S(2)}) collective-permute-start(bf16[64,2048]{1,0:T(8,128)(2,1)S(1)} %get-tuple-element.105), channel_id=1, source_target_pairs={{0,16},{4,20},{8,24},{12,28},{16,0},{20,4},{24,8},{28,12},{1,17},{... | collective-permute-start | bytes 786440 | tf_op jit(solution)/shard_map/ppermute | solution.py:439
  168.7 12.5 %collective-permute-start.42 = (bf16[128,512]{1,0:T(8,128)(2,1)S(1)}, bf16[128,512]{1,0:T(8,128)(2,1)S(1)}, u32[]{:S(2)}, u32[]{:S(2)}) collective-permute-start(bf16[128,512]{1,0:T(8,128)(2,1)S(1)} %get-tuple-element.93), channel_id=1, source_target_pairs={{0,1},{1,0},{2,3},{3,2},{4,5},{5,4},{6,7},{7,6},{8,9},{9,8},{10,11... | collective-permute-start | bytes 393224 | tf_op jit(solution)/shard_map/ppermute | solution.py:445
  171.2 16.3 %collective-permute-start.43 = (bf16[128,512]{1,0:T(8,128)(2,1)S(1)}, bf16[128,512]{1,0:T(8,128)(2,1)S(1)}, u32[]{:S(2)}, u32[]{:S(2)}) collective-permute-start(bf16[128,512]{1,0:T(8,128)(2,1)S(1)} %get-tuple-element.94), channel_id=1, source_target_pairs={{0,2},{1,3},{2,0},{3,1},{4,6},{5,7},{6,4},{7,5},{8,10},{9,11},{10,... | collective-permute-start | bytes 393224 | tf_op jit(solution)/shard_map/ppermute | solution.py:445
  173.6 13.9 %collective-permute-start.44 = (bf16[128,512]{1,0:T(8,128)(2,1)S(1)}, bf16[128,512]{1,0:T(8,128)(2,1)S(1)}, u32[]{:S(2)}, u32[]{:S(2)}) collective-permute-start(bf16[128,512]{1,0:T(8,128)(2,1)S(1)} %get-tuple-element.95), channel_id=1, source_target_pairs={{0,3},{1,2},{2,1},{3,0},{4,7},{5,6},{6,5},{7,4},{8,11},{9,10},{10,... | collective-permute-start | bytes 393224 | tf_op jit(solution)/shard_map/ppermute | solution.py:445
  177.8 9.7 %collective-permute-start.51 = (bf16[128,512]{1,0:T(8,128)(2,1)S(1)}, bf16[128,512]{1,0:T(8,128)(2,1)S(1)}, u32[]{:S(2)}, u32[]{:S(2)}) collective-permute-start(bf16[128,512]{1,0:T(8,128)(2,1)S(1)} %get-tuple-element.98), channel_id=1, source_target_pairs={{0,1},{1,0},{2,3},{3,2},{4,5},{5,4},{6,7},{7,6},{8,9},{9,8},{10,11... | collective-permute-start | bytes 393224 | tf_op jit(solution)/shard_map/ppermute | solution.py:445
  178.6 15.7 %collective-permute-start.52 = (bf16[128,512]{1,0:T(8,128)(2,1)S(1)}, bf16[128,512]{1,0:T(8,128)(2,1)S(1)}, u32[]{:S(2)}, u32[]{:S(2)}) collective-permute-start(bf16[128,512]{1,0:T(8,128)(2,1)S(1)} %get-tuple-element.99), channel_id=1, source_target_pairs={{0,2},{1,3},{2,0},{3,1},{4,6},{5,7},{6,4},{7,5},{8,10},{9,11},{10,... | collective-permute-start | bytes 393224 | tf_op jit(solution)/shard_map/ppermute | solution.py:445
  181.2 13.1 %collective-permute-start.53 = (bf16[128,512]{1,0:T(8,128)(2,1)S(1)}, bf16[128,512]{1,0:T(8,128)(2,1)S(1)}, u32[]{:S(2)}, u32[]{:S(2)}) collective-permute-start(bf16[128,512]{1,0:T(8,128)(2,1)S(1)} %get-tuple-element.100), channel_id=1, source_target_pairs={{0,3},{1,2},{2,1},{3,0},{4,7},{5,6},{6,5},{7,4},{8,11},{9,10},{10,... | collective-permute-start | bytes 393224 | tf_op jit(solution)/shard_map/ppermute | solution.py:445
  (7 other events, 39.1 us)

commit v8 on v7

--- a/solution.py
+++ b/solution.py
@@ -36,15 +36,25 @@
     kinds, width, chans = w_ref.shape
     load = pltpu.make_async_copy(x_hbm, x_ref, x_sem)
     load.start()
-    copies = [pltpu.make_async_copy(w_hbm.at[kind], w_ref.at[kind], sems.at[kind]) for kind in range(kinds)]
-    for copy in copies:
-        copy.start()
+    part = width // sems.shape[1]
+    copies = []
+    for kind in range(kinds):
+        at = [pl.ds(piece * part, part) for piece in range(sems.shape[1])]
+        copies.append(
+            [
+                pltpu.make_async_copy(w_hbm.at[kind, rows], w_ref.at[kind, rows], sems.at[kind, piece])
+                for piece, rows in enumerate(at)
+            ]
+        )
+        for copy in copies[kind]:
+            copy.start()
     load.wait()
     values = x_ref[...].astype(F32)
     scale = lax.rsqrt(jnp.mean(values * values, axis=-1, keepdims=True) + 1e-06)
     normed_ref[...] = (values * scale * gain_ref[...]).astype(BF)
     for kind in range(kinds):
-        copies[kind].wait()
+        for copy in copies[kind]:
+            copy.wait()
         out = mm(normed_ref[...], w_ref[kind]).astype(BF)
         mixed_ref[kind] = out
         rim_ref[kind] = out[out.shape[0] - RIM :]
@@ -68,7 +78,7 @@
             pltpu.VMEM((kinds, width, chans), BF),
             pltpu.VMEM((rows, width), BF),
             pltpu.SemaphoreType.DMA,
-            pltpu.SemaphoreType.DMA((kinds,)),
+            pltpu.SemaphoreType.DMA((kinds, 4)),
         ],
         compiler_params=params(60),
         name="qkv_projection",
@@ -107,13 +117,18 @@
 
 
 def conv_kernel(
-    experts, mixed_ref, rim_ref, taps_ref, steps_ref, cot_ref, ids_ref, weights_ref, qkv_ref, fwd_ref, bwd_ref, pad_ref
+    experts, mixed_any, rim_ref, taps_ref, steps_ref, cot_ref, ids_ref, weights_ref, qkv_ref, fwd_ref, bwd_ref,
+    pad_ref, mixed_ref, sems,
 ):
     kinds, rows, chans = mixed_ref.shape
+    copies = [pltpu.make_async_copy(mixed_any.at[kind], mixed_ref.at[kind], sems.at[kind]) for kind in range(kinds)]
+    for copy in copies:
+        copy.start()
     heads = steps_ref.shape[0]
     size = chans // heads
     along, down, _ = decay_sums(steps_ref[...])
     for kind in range(kinds):
+        copies[kind].wait()
         pad_ref[:RIM] = rim_ref[kind].astype(F32)
         pad_ref[RIM:] = mixed_ref[kind].astype(F32)
         total = taps_ref[kind, 0:1, :] * pad_ref[RIM:]
@@ -126,19 +141,19 @@
     routes = rows // LANES * 3 * experts
     table = route_rows(ids_ref, weights_ref, experts).astype(BF)
     for part in range(rows // LANES):
-        bwd_ref[part * 3 * experts : (part + 1) * 3 * experts] = table[:, part * LANES : (part + 1) * LANES]
+        fwd_ref[part * 3 * experts : (part + 1) * 3 * experts] = table[:, part * LANES : (part + 1) * LANES]
     for head in range(heads):
         at = slice(head * size, (head + 1) * size)
         base = head * (size + RIM)
+        behind = routes + base
         last = along[head : head + 1, rows - 1 : rows]
         lead = jnp.exp(down[:, head : head + 1])
         tail = jnp.exp(last - down[:, head : head + 1])
         key_out = (qkv_ref[1, :, at].astype(F32) * tail).astype(BF)
         query_out = (qkv_ref[0, :, at].astype(F32) * lead).astype(BF)
         ends = payload_tail(last, size).astype(BF)
-        fwd_ref[base : base + size] = mm(key_out, qkv_ref[2, :, at], TN).astype(BF)
-        fwd_ref[base + size : base + size + RIM] = ends
-        base += routes
+        fwd_ref[behind : behind + size] = mm(key_out, qkv_ref[2, :, at], TN).astype(BF)
+        fwd_ref[behind + size : behind + size + RIM] = ends
         bwd_ref[base : base + size] = mm(query_out, cot_ref[:, at], TN).astype(BF)
         bwd_ref[base + size : base + size + RIM] = ends
 
@@ -150,13 +165,18 @@
     states = heads * (size + RIM)
     return pl.pallas_call(
         functools.partial(conv_kernel, experts),
+        in_specs=[pl.BlockSpec(memory_space=pl.ANY)] + [pl.BlockSpec(memory_space=pltpu.VMEM)] * 6,
         out_specs=[pl.BlockSpec(memory_space=pltpu.VMEM)] * 3,
         out_shape=[
             jax.ShapeDtypeStruct((kinds, rows, chans), BF),
+            jax.ShapeDtypeStruct((states + rows // LANES * 3 * experts, size), BF),
             jax.ShapeDtypeStruct((states, size), BF),
-            jax.ShapeDtypeStruct((states + rows // LANES * 3 * experts, size), BF),
         ],
-        scratch_shapes=[pltpu.VMEM((rows + RIM, chans), F32)],
+        scratch_shapes=[
+            pltpu.VMEM((rows + RIM, chans), F32),
+            pltpu.VMEM(mixed.shape, BF),
+            pltpu.SemaphoreType.DMA((kinds,)),
+        ],
         compiler_params=params(12),
         name="conv_states",
     )(mixed, rim, taps, steps, cot, ids, weights)
@@ -315,9 +335,10 @@
 PAIR = 2
 
 
-def expert_kernel(masks, chunk, experts, where_ref, near_routes, far_routes, gate_ref, up_ref, down_ref, *refs):
-    row_refs, (near_ref, far_ref, rows_ref, sems) = refs[: len(masks)], refs[len(masks) :]
-    _, tok, width = near_ref.shape
+def expert_kernel(groups, chunk, experts, where_ref, near_routes, far_routes, gate_ref, up_ref, down_ref, *refs):
+    masks = [mask for group in groups for mask in group]
+    row_refs, outs, (rows_ref, sems) = refs[: len(masks)], refs[len(masks) : -2], refs[-2:]
+    _, tok, width = outs[0].shape
     steps = len(masks) // PAIR
     step = pl.program_id(0)
     slot = lax.rem(step, 2)
@@ -341,16 +362,17 @@
     mine = (here == where_ref[1]) | (here == where_ref[1] + experts) | (here == where_ref[1] + 2 * experts)
     square = (LANES, LANES)
     diagonal = lax.broadcasted_iota(jnp.int32, square, 0) == lax.broadcasted_iota(jnp.int32, square, 1)
-    is_near = step < steps // 2
     weights = []
     for part in range(PAIR):
-        index = jnp.int32(masks[part] // 2)
+        mask = jnp.int32(masks[part])
         for at in range(1, steps):
-            index = jnp.where(step == at, masks[PAIR * at + part] // 2, index)
+            mask = jnp.where(step == at, masks[PAIR * at + part], mask)
+        index = lax.shift_right_logical(mask, 1)
         for block in range(tok // LANES):
             base = (chunk // LANES + block) * 3 * experts
             at = slice(base, base + 3 * experts)
-            table = jnp.where(is_near, near_routes[index, at, :].astype(F32), far_routes[index, at, :].astype(F32))
+            near, far = near_routes[index, at, :].astype(F32), far_routes[index, at, :].astype(F32)
+            table = jnp.where((mask & CORE) == 0, near, far)
             row = jnp.sum(jnp.where(mine, table, 0.0), axis=0, keepdims=True)
             weights.append(jnp.sum(jnp.where(diagonal, jnp.broadcast_to(row, square), 0.0), axis=1, keepdims=True))
 
@@ -359,19 +381,17 @@
     gate = mm(tokens, gate_ref[0])
     inner = (gate * jax.nn.sigmoid(gate) * mm(tokens, up_ref[0])).astype(BF)
     cols = pick_block(width, 512)
+    per = steps // len(outs)
     for begin in range(0, width, cols):
         piece = mm(inner, down_ref[0, :, begin : begin + cols])
         for at, weight in enumerate(weights):
             part, row = divmod(at * LANES, tok)
             scaled = (piece[at * LANES : (at + 1) * LANES] * weight).astype(BF)
-
-            @pl.when(is_near)
-            def _(scaled=scaled, part=part, row=row):
-                near_ref[part, row : row + LANES, begin : begin + cols] = scaled
-
-            @pl.when(jnp.logical_not(is_near))
-            def _(scaled=scaled, part=part, row=row):
-                far_ref[part, row : row + LANES, begin : begin + cols] = scaled
+            for group, out_ref in enumerate(outs):
+
+                @pl.when((step >= group * per) & (step < (group + 1) * per))
+                def _(scaled=scaled, part=part, row=row, out_ref=out_ref):
+                    out_ref[part, row : row + LANES, begin : begin + cols] = scaled
 
 
 def stage_kernel(where_ref, *refs):
@@ -392,29 +412,28 @@
     )(where, *weights)
 
 
-def expert_pieces(chunk, where, rows, evens, gate, up, down, routes):
-    masks = list(evens) + [mask | CORE for mask in evens]
-    blocks = [rows[mask] for mask in masks]
+def expert_pieces(chunk, where, rows, groups, gate, up, down, routes):
+    blocks = [rows[mask] for group in groups for mask in group]
     tok, width = blocks[0].shape
     hidden = gate.shape[2]
-    count = len(blocks)
-    half = count // PAIR // 2
-    experts = EXP_CTX * count
+    count, each = len(blocks), len(groups[0])
+    per = each // PAIR
+    experts = EXP_CTX * 2 * routes[0].shape[0]
     route_rows = CHUNKS * tok // LANES * 3 * experts
     vmem = pl.BlockSpec(memory_space=pltpu.VMEM)
-    piece = jax.ShapeDtypeStruct((count // 2, tok, width), BF)
-    table = pl.BlockSpec((count // 2, route_rows, LANES), lambda i: (0, 0, 0))
-    return pl.pallas_call(
-        functools.partial(expert_kernel, tuple(masks), chunk, experts),
+    table = pl.BlockSpec((routes[0].shape[0], route_rows, LANES), lambda i: (0, 0, 0))
+
+    def out_spec(group):
+        return pl.BlockSpec((PAIR, tok, width), lambda i: (jnp.clip(i - group * per, 0, per - 1), 0, 0))
+
+    return pl.pallas_call(
+        functools.partial(expert_kernel, tuple(map(tuple, groups)), chunk, experts),
         grid=(count // PAIR,),
         in_specs=[pl.BlockSpec(memory_space=pltpu.SMEM), table, table]
         + [vmem] * 3
         + [pl.BlockSpec(memory_space=pl.ANY)] * count,
-        out_specs=[
-            pl.BlockSpec((PAIR, tok, width), lambda i: (jnp.minimum(i, half - 1), 0, 0)),
-            pl.BlockSpec((PAIR, tok, width), lambda i: (jnp.maximum(i - half, 0), 0, 0)),
-        ],
-        out_shape=[piece, piece],
+        out_specs=[out_spec(group) for group in range(len(groups))],
+        out_shape=[jax.ShapeDtypeStruct((each, tok, width), BF)] * len(groups),
         scratch_shapes=[
             pltpu.VMEM((2, PAIR * tok, width), BF),
             pltpu.SemaphoreType.DMA((2,)),
@@ -433,10 +452,8 @@
 PLANE = 8
 
 
-def swap(value, mask, keep=None):
-    count = lax.axis_size("ctx")
-    pairs = [(at, at ^ mask) for at in range(count)]
-    return lax.ppermute(value, "ctx", [pair for pair in pairs if keep is None or keep(*pair)])
+def swap(value, mask):
+    return lax.ppermute(value, "ctx", [(at, at ^ mask) for at in range(lax.axis_size("ctx"))])
 
 
 def send_heads(parts):
@@ -446,8 +463,12 @@
     ]
 
 
-def spread_near(own, keep=None):
-    return jnp.stack([own] + [swap(own, mask, keep) for mask in range(2, lax.axis_size("ctx"), 2)])
+def spread_near(own):
+    return jnp.stack([own] + [swap(own, mask) for mask in range(2, lax.axis_size("ctx"), 2)])
+
+
+def double(near, mask):
+    return jnp.concatenate([near, swap(near, mask)])
 
 
 def plus(*terms):
@@ -463,12 +484,12 @@
     return {mask: swap(own, mask) for mask in masks}
 
 
-def forward(own, came):
+def forward(own, came, leaving=None):
     came = {0: own} | came
     if lax.axis_size("ctx") == PLANE:
         half = own.shape[0] // 2
-        upper, lower = swap(came[ROW][:half], COL), swap(came[COL][half:], ROW)
-        came[ROW | COL] = jnp.concatenate([upper, lower])
+        halves = [swap(came[ROW][:half], COL), swap(came[COL][half:], ROW)]
+        came[ROW | COL] = jnp.concatenate(halves if leaving is None else after(halves, leaving))
     return [came[mask] for mask in range(0, lax.axis_size("ctx"), 2)]
 
 
@@ -601,16 +622,19 @@
     qkv, fwd, bwd = local_states(
         mixed, rim, jnp.transpose(conv_w, (1, 0, 2)), steps, grad_core, expert_ids.T, route_weights.T, experts
     )
-    fwd = spread_near(fwd, lambda source, target: source < target)
+    fwd = spread_near(fwd)
     fwd = (fwd, swap(fwd, CORE))
     where = stage(after(where, qkv), w_out)
     parts = core_out(where, qkv, steps, *fwd, norm_gain, w_out, CHUNKS, n_head)
     where = stage(after(where, parts), w_gate, w_up, w_down)
-    normed, attn = norm_rows(where, hidden_in, send_heads(parts), gain_moe, CHUNKS)
-    bwd = spread_near(after(bwd, normed))
-
-    near, came, owns = [], [], []
-    own = join_rows(where, send_heads([normed[0]] * n_head))
+    bwd = double(after(bwd, parts)[None], ROW)
+    normed, attn = norm_rows(where, hidden_in, after(send_heads(parts), bwd), gain_moe, CHUNKS)
+    bwd = after(bwd, normed)
+    while bwd.shape[0] < n_ctx // 2:
+        bwd = double(bwd, 2 * bwd.shape[0])
+
+    came, owns = [], []
+    own = join_rows(where, after(send_heads([normed[0]] * n_head), bwd))
     bwd = (bwd, swap(after(bwd, own), CORE))
     for chunk in range(CHUNKS):
         owns.append(own)
@@ -619,29 +643,40 @@
             own = join_rows(where, send_heads([after(normed[chunk + 1], own)] * n_head))
             came[chunk] = after(came[chunk], own)
     evens = list(range(0, n_ctx, 2))
-    rows = []
+    odds = [mask | CORE for mask in evens]
+    pending, sums, first = [], [], None
     for chunk in range(CHUNKS):
-        near = forward(owns[chunk], came[chunk])
-        rows.append({mask: part for mask, part in zip(evens, near)})
-        rows[chunk] |= {mask | CORE: swap(part, CORE) for mask, part in rows[chunk].items()}
-
-    pending, sums = [], []
-    for chunk in range(CHUNKS):
-        here, far = expert_pieces(chunk * chunk_rows, where, rows[chunk], evens, w_gate, w_up, w_down, bwd)
-        arrived = swap(after(far, came[chunk + 1] if chunk + 1 < CHUNKS else pending[-1][3]), CORE)
+        near = forward(owns[chunk], came[chunk], first and [part for _, _, part in first])
+        rows = {mask: part for mask, part in zip(evens, near)}
+        rows |= {mask | CORE: swap(part, CORE) for mask, part in rows.items()}
         if pending:
-            pending[-1] += (last_sums(*pending[-1][:2], pending[-1][3]),)
-            arrived = after(arrived, [part for _, _, part in pending[-1][4]])
+            rows = after(rows, [part for _, _, part in first])
+        experts_of = functools.partial(
+            expert_pieces, chunk * chunk_rows, where, gate=w_gate, up=w_up, down=w_down, routes=fwd
+        )
+        if chunk + 1 < CHUNKS:
+            here, far = experts_of(rows=rows, groups=[evens, odds])
+            arrived = swap(after(far, came[chunk + 1]), CORE)
+        else:
+            (far,) = experts_of(rows=rows, groups=[odds])
+            ready = [far]
+            arrived = swap(after(far, pending[-1][3]) if pending else far, CORE)
+            if pending:
+                last = last_sums(*pending[-1][:2], pending[-1][3])
+                ready += [part for _, _, part in last]
+                last = [(mask, start, swap(part, mask)) for mask, start, part in last]
+                pending[-1] += (last,)
+                arrived = after(arrived, [part for _, _, part in last])
+            (here,) = experts_of(rows=after(rows, ready), groups=[evens])
         first = first_sums(here, arrived)
-        if chunk + 1 < CHUNKS:
-            rows[chunk + 1] = after(rows[chunk + 1], [part for _, _, part in first])
         pending.append((here, arrived, first, send_sums(first)))
-    pending[-1] += (last_sums(*pending[-1][:2], pending[-1][3]),)
+    last = last_sums(*pending[-1][:2], pending[-1][3])
+    pending[-1] += ([(mask, start, swap(part, mask)) for mask, start, part in last],)
     for chunk in range(CHUNKS):
         here, arrived, first, received, last = pending[chunk]
-        terms = list(zip([start for _, start, _ in first], received))
+        terms = [(start, part) for (_, start, _), part in zip(first, received)]
         if last:
-            terms = terms[2:] + list(zip([start for _, start, _ in last], send_sums(last)))
+            terms = terms[2:] + [(start, part) for _, start, part in last]
         starts, others = zip(*terms)
         if chunk + 1 < CHUNKS:
             others = after(others, [part for _, _, part in pending[chunk + 1][2]])

time: 196 us -> 192 us (0.980)
  starting transfers between devices: 68.9 us -> 60.8 us
    ppermute x38 -> x37, starting transfers between devices: 39.8 us -> 32.5 us  [swap(): lax.ppermute(value, 'ctx', [(at, at ^ mask) for at in range(lax.axis_size...]
    ppermute x38 -> x37, waiting for transfers between devices: 33.5 us -> 35.4 us  [swap(): lax.ppermute(value, 'ctx', [(at, at ^ mask) for at in range(lax.axis_size...]
    pallas_call x3 -> x4, Pallas kernels: 25.5 us -> 27.1 us  [the longest x3 24.1 us: expert_pieces(): pl.pallas_call(functools.partial(expert_kernel, tuple(map(tuple, groups))...]
    unnamed x36 -> x41, local copies, waits for them, and re-layouts: 3.48 us -> 4.41 us
  transfers between devices with their start and end apart: 54 -> 53, of which waited for: 22 -> 27; matrix products, arithmetic and copies ran while one was open for 1% -> 1% of each run, Pallas kernels for 17% -> 18%
where the time goes in v8:
time: 192 us; the launch traced here: 191 us
  waiting for transfers between devices  73.1 us (38%)
  starting transfers between devices  60.8 us (32%)
  Pallas kernels  50.3 us (26%)
  local copies, waits for them, and re-layouts  4.56 us (2%)
    ppermute x15, waiting for transfers between devices, send_heads(): lax.ppermute(parts[mask], 'head', [(at, at ^ mask) for at in range(count)])  36.6 us
    ppermute x37, waiting for transfers between devices, swap(): lax.ppermute(value, 'ctx', [(at, at ^ mask) for at in range(lax.axis_size...  35.4 us
    ppermute x37, starting transfers between devices, swap(): lax.ppermute(value, 'ctx', [(at, at ^ mask) for at in range(lax.axis_size...  32.5 us
    ppermute x15, starting transfers between devices, send_heads(): lax.ppermute(parts[mask], 'head', [(at, at ^ mask) for at in range(count)])  25.8 us
    pallas_call x3, Pallas kernels, expert_pieces(): pl.pallas_call(functools.partial(expert_kernel, tuple(map(tuple, groups))...  24.1 us
    pallas_call x1, Pallas kernels, project(): pl.pallas_call(qkv_kernel, in_specs=[hbm, vmem, hbm], out_specs=[vmem, vm...  7.26 us
    pallas_call x1, Pallas kernels, core_grads(): pl.pallas_call(grad_kernel, in_specs=[pl.BlockSpec(memory_space=pltpu.SME...  4.69 us
    unnamed x41, local copies, waits for them, and re-layouts  4.41 us
  transfers between devices with their start and end apart: 53, of which 27 were waited for; matrix products, arithmetic and copies ran while one was open for 1% of the time, Pallas kernels for 18%

profile of v8, /device:TPU:0, one launch (start us, length us, event | category | flops | bytes accessed | tf_op | source)
XLA Modules:
  0.0 191.3 jit_solution(26553977875528604)
XLA Ops:
  0.7 7.3 %qkv_projection.1 = (bf16[3,256,512]{2,1,0:T(8,128)(2,1)}, bf16[3,16,512]{2,1,0:T(8,128)(2,1)}) custom-call(bf16[256,2048]{1,0:T(8,128)(2,1)} %x_ref.3, f32[1,2048]{1,0:T(1,128)} %bitcast.63, bf16[3,2048,512]{2,1,0:T(8,128)(2,1)} %bitcast.59), custom_call_target="tpu_custom_call" | custom-call | tf_op jit(solution)/shard_map/qkv_projection/pallas_call | solution.py:68
  8.0 2.5 %collective-permute-start = (bf16[3,16,512]{2,1,0:T(8,128)(2,1)}, bf16[3,16,512]{2,1,0:T(8,128)(2,1)S(1)}, u32[]{:S(2)}, u32[]{:S(2)}) collective-permute-start(bf16[3,16,512]{2,1,0:T(8,128)(2,1)} %get-tuple-element.68), channel_id=1, source_target_pairs={{0,4},{4,8},{8,12},{12,16},{16,20},{20,24},{24,28},{1,5},{5,9},{9,... | collective-permute-start | bytes 147464 | tf_op jit(solution)/shard_map/ppermute | solution.py:621
  10.5 1.1 collective-permute-done.rim_ref
  11.6 1.1 copy-done.10
  12.7 3.0 %conv_states.1 = (bf16[3,256,512]{2,1,0:T(8,128)(2,1)S(1)}, bf16[672,128]{1,0:T(8,128)(2,1)S(1)}, bf16[576,128]{1,0:T(8,128)(2,1)S(1)}) custom-call(bf16[3,256,512]{2,1,0:T(8,128)(2,1)S(1)} %copy-done.10, bf16[3,16,512]{2,1,0:T(8,128)(2,1)S(1)} %collective-permute-done.rim_ref, f32[3,4,512]{2,1,0:T(4,128)S(1)} %bitcast.54, f32[4,256]{1,0:T(4,128)S(1)} %bitcast.51, ...), custom_call_target="tpu_custom_call" | custom-call | tf_op jit(solution)/shard_map/conv_states/pallas_call | solution.py:166
  15.7 0.9 copy-done.2
  17.3 6.1 %collective-permute-start.3 = (bf16[672,128]{1,0:T(8,128)(2,1)S(1)}, bf16[672,128]{1,0:T(8,128)(2,1)S(1)}, u32[]{:S(2)}, u32[]{:S(2)}) collective-permute-start(bf16[672,128]{1,0:T(8,128)(2,1)S(1)} %get-tuple-element.71), channel_id=1, source_target_pairs={{0,24},{4,28},{8,16},{12,20},{16,8},{20,12},{24,0},{28,4},{1,25},{... | collective-permute-start | bytes 516104 | tf_op jit(solution)/shard_map/ppermute | solution.py:456
  23.9 0.9 collective-permute-start.1
  24.8 3.8 %collective-permute-done.3 = bf16[672,128]{1,0:T(8,128)(2,1)S(1)} collective-permute-done((bf16[672,128]{1,0:T(8,128)(2,1)S(1)}, bf16[672,128]{1,0:T(8,128)(2,1)S(1)}, u32[]{:S(2)}, u32[]{:S(2)}) %collective-permute-start.3) | collective-permute-done | bytes 172064 | tf_op jit(solution)/shard_map/ppermute | solution.py:456
  28.7 2.5 %collective-permute-done.2 = bf16[672,128]{1,0:T(8,128)(2,1)S(1)} collective-permute-done((bf16[672,128]{1,0:T(8,128)(2,1)S(1)}, bf16[672,128]{1,0:T(8,128)(2,1)S(1)}, u32[]{:S(2)}, u32[]{:S(2)}) %collective-permute-start.2) | collective-permute-done | bytes 172064 | tf_op jit(solution)/shard_map/ppermute | solution.py:456
  31.5 1.1 stage_weights.2.me_ref.where_ref
  32.6 0.9 collective-permute-done.4.far_ref.far_routes.fwd_far
  33.5 3.7 %core_out.1 = (bf16[64,2048]{1,0:T(8,128)(2,1)S(1)}, bf16[64,2048]{1,0:T(8,128)(2,1)S(1)}, bf16[64,2048]{1,0:T(8,128)(2,1)S(1)}, bf16[64,2048]{1,0:T(8,128)(2,1)S(1)}) custom-call(s32[3]{0:T(128)S(1)} %stage_weights.2.me_ref.where_ref, bf16[3,256,512]{2,1,0:T(8,128)(2,1)S(1)} %copy-done.3, f32[4,256]{1,0:T(4,128)S(1)} %bitcast.52, f32[1,512]{1,0:T(1,128)S(1)} %bitcast.58, ...), custom_call_target="tpu_custom_call" | custom-call | tf_op jit(solution)/shard_map/core_out/pallas_call | solution.py:233
  37.2 1.7 collective-permute-start.8
  38.9 1.6 collective-permute-start.5
  40.5 2.6 %collective-permute-start.6 = (bf16[64,2048]{1,0:T(8,128)(2,1)S(1)}, bf16[64,2048]{1,0:T(8,128)(2,1)S(1)}, u32[]{:S(2)}, u32[]{:S(2)}) collective-permute-start(bf16[64,2048]{1,0:T(8,128)(2,1)S(1)} %get-tuple-element.74), channel_id=1, source_target_pairs={{0,2},{1,3},{2,0},{3,1},{4,6},{5,7},{6,4},{7,5},{8,10},{9,11},{10,... | collective-permute-start | bytes 786440 | tf_op jit(solution)/shard_map/ppermute | solution.py:462
  43.3 1.6 copy-done.6
  44.9 1.1 stage_weights.3.where_ref.me_ref
  46.1 5.9 %collective-permute-done.5.refs_1_ = bf16[64,2048]{1,0:T(8,128)(2,1)S(1)} collective-permute-done((bf16[64,2048]{1,0:T(8,128)(2,1)S(1)}, bf16[64,2048]{1,0:T(8,128)(2,1)S(1)}, u32[]{:S(2)}, u32[]{:S(2)}) %collective-permute-start.5) | collective-permute-done | bytes 262176 | tf_op jit(solution)/shard_map/ppermute | solution.py:462
  52.0 9.9 %collective-permute-done.6.refs_2_ = bf16[64,2048]{1,0:T(8,128)(2,1)S(1)} collective-permute-done((bf16[64,2048]{1,0:T(8,128)(2,1)S(1)}, bf16[64,2048]{1,0:T(8,128)(2,1)S(1)}, u32[]{:S(2)}, u32[]{:S(2)}) %collective-permute-start.6) | collective-permute-done | bytes 262176 | tf_op jit(solution)/shard_map/ppermute | solution.py:462
  62.7 1.0 collective-permute-start.12
  63.7 2.5 %collective-permute-start.11 = (bf16[32,2048]{1,0:T(8,128)(2,1)S(1)}, bf16[32,2048]{1,0:T(8,128)(2,1)S(1)}, u32[]{:S(2)}, u32[]{:S(2)}) collective-permute-start(bf16[32,2048]{1,0:T(8,128)(2,1)S(1)} %get-tuple-element.87.refs_0_), channel_id=1, source_target_pairs={{0,3},{1,2},{2,1},{3,0},{4,7},{5,6},{6,5},{7,4},{8,11},{9,10},{10,... | collective-permute-start | bytes 393224 | tf_op jit(solution)/shard_map/ppermute | solution.py:462
  66.2 5.2 %collective-permute-start.10 = (bf16[32,2048]{1,0:T(8,128)(2,1)S(1)}, bf16[32,2048]{1,0:T(8,128)(2,1)S(1)}, u32[]{:S(2)}, u32[]{:S(2)}) collective-permute-start(bf16[32,2048]{1,0:T(8,128)(2,1)S(1)} %get-tuple-element.87.refs_0_), channel_id=1, source_target_pairs={{0,2},{1,3},{2,0},{3,1},{4,6},{5,7},{6,4},{7,5},{8,10},{9,11},{10,... | collective-permute-start | bytes 393224 | tf_op jit(solution)/shard_map/ppermute | solution.py:462
  71.6 7.3 %collective-permute-done.10.refs_2_ = bf16[32,2048]{1,0:T(8,128)(2,1)S(1)} collective-permute-done((bf16[32,2048]{1,0:T(8,128)(2,1)S(1)}, bf16[32,2048]{1,0:T(8,128)(2,1)S(1)}, u32[]{:S(2)}, u32[]{:S(2)}) %collective-permute-start.10) | collective-permute-done | bytes 131104 | tf_op jit(solution)/shard_map/ppermute | solution.py:462
  79.5 1.2 collective-permute-start.14
  81.1 2.6 %collective-permute-start.17 = (bf16[32,2048]{1,0:T(8,128)(2,1)S(1)}, bf16[32,2048]{1,0:T(8,128)(2,1)S(1)}, u32[]{:S(2)}, u32[]{:S(2)}) collective-permute-start(bf16[32,2048]{1,0:T(8,128)(2,1)S(1)} %get-tuple-element.91.refs_0_), channel_id=1, source_target_pairs={{0,3},{1,2},{2,1},{3,0},{4,7},{5,6},{6,5},{7,4},{8,11},{9,10},{10,... | collective-permute-start | bytes 393224 | tf_op jit(solution)/shard_map/ppermute | solution.py:462
  83.7 1.7 collective-permute-start.15
  85.5 3.7 %collective-permute-done.17.refs_3_ = bf16[32,2048]{1,0:T(8,128)(2,1)S(1)} collective-permute-done((bf16[32,2048]{1,0:T(8,128)(2,1)S(1)}, bf16[32,2048]{1,0:T(8,128)(2,1)S(1)}, u32[]{:S(2)}, u32[]{:S(2)}) %collective-permute-start.17) | collective-permute-done | bytes 131104 | tf_op jit(solution)/shard_map/ppermute | solution.py:462
  89.1 3.7 %collective-permute-done.16.refs_2_ = bf16[32,2048]{1,0:T(8,128)(2,1)S(1)} collective-permute-done((bf16[32,2048]{1,0:T(8,128)(2,1)S(1)}, bf16[32,2048]{1,0:T(8,128)(2,1)S(1)}, u32[]{:S(2)}, u32[]{:S(2)}) %collective-permute-start.16) | collective-permute-done | bytes 131104 | tf_op jit(solution)/shard_map/ppermute | solution.py:462
  93.5 1.7 collective-permute-start.18
  96.5 4.0 %collective-permute-done.18 = bf16[64,2048]{1,0:T(8,128)(2,1)S(1)} collective-permute-done((bf16[64,2048]{1,0:T(8,128)(2,1)S(1)}, bf16[64,2048]{1,0:T(8,128)(2,1)S(1)}, u32[]{:S(2)}, u32[]{:S(2)}) %collective-permute-start.18) | collective-permute-done | bytes 262176 | tf_op jit(solution)/shard_map/ppermute | solution.py:456
  100.6 1.5 collective-permute-done.19
  102.6 1.5 collective-permute-start.24
  104.1 11.9 %expert_pieces.3 = (bf16[4,128,2048]{2,1,0:T(8,128)(2,1)S(1)}, bf16[4,128,2048]{2,1,0:T(8,128)(2,1)S(1)}) custom-call(s32[3]{0:T(128)S(1)} %stage_weights.3.where_ref.me_ref, bf16[4,672,128]{2,1,0:T(8,128)(2,1)S(1)} %pad_maximum_fusion.near_ref.near_routes.fwd_near, bf16[4,672,128]{2,1,0:T(8,128)(2,1)S(1)} %collective-permute-done.4.far_ref.far_routes.fwd_far, ...), custom_call_target="tpu_custom_call" | custom-call | flops 6442450944 | bytes 8388608 | tf_op jit(solution)/shard_map/expert_pieces/pallas_call | solution.py:429
  117.1 1.6 collective-permute-start.37
  118.7 0.9 collective-permute-start.36
  119.6 1.1 collective-permute-done.26.arrived_ref
  121.2 4.2 %collective-permute-done.37 = bf16[64,2048]{1,0:T(8,128)(2,1)S(1)} collective-permute-done((bf16[64,2048]{1,0:T(8,128)(2,1)S(1)}, bf16[64,2048]{1,0:T(8,128)(2,1)S(1)}, u32[]{:S(2)}, u32[]{:S(2)}) %collective-permute-start.37) | collective-permute-done | bytes 262176 | tf_op jit(solution)/shard_map/ppermute | solution.py:456
  125.4 1.3 collective-permute-done.36
  126.8 0.9 collective-permute-start.31
  127.7 1.3 collective-permute-start.29
  129.4 1.5 collective-permute-start.27
  130.9 6.1 %expert_pieces.4 = bf16[4,128,2048]{2,1,0:T(8,128)(2,1)S(1)} custom-call(s32[3]{0:T(128)S(1)} %stage_weights.3.where_ref.me_ref, bf16[4,672,128]{2,1,0:T(8,128)(2,1)S(1)} %pad_maximum_fusion.near_ref.near_routes.fwd_near, bf16[4,672,128]{2,1,0:T(8,128)(2,1)S(1)} %collective-permute-done.4.far_ref.far_routes.fwd_far, bf16[1,2048,512]{2,1,0:T(8,128)(2,1)S(1)} %copy-done.4, ...), custom_call_target="tpu_custom_call" | custom-call | flops 3221225472 | bytes 4194304 | tf_op jit(solution)/shard_map/expert_pieces/pallas_call | solution.py:429
  137.1 4.1 %collective-permute-done.28.refs_1_ = bf16[64,2048]{1,0:T(8,128)(2,1)S(1)} collective-permute-done((bf16[64,2048]{1,0:T(8,128)(2,1)S(1)}, bf16[64,2048]{1,0:T(8,128)(2,1)S(1)}, u32[]{:S(2)}, u32[]{:S(2)}) %collective-permute-start.28) | collective-permute-done | bytes 262176 | tf_op jit(solution)/shard_map/ppermute | solution.py:456
  142.0 1.4 collective-permute-start.32
  143.7 6.1 %expert_pieces.5.near_ref = bf16[4,128,2048]{2,1,0:T(8,128)(2,1)S(1)} custom-call(s32[3]{0:T(128)S(1)} %stage_weights.3.where_ref.me_ref, bf16[4,672,128]{2,1,0:T(8,128)(2,1)S(1)} %pad_maximum_fusion.near_ref.near_routes.fwd_near, bf16[4,672,128]{2,1,0:T(8,128)(2,1)S(1)} %collective-permute-done.4.far_ref.far_routes.fwd_far, ...), custom_call_target="tpu_custom_call" | custom-call | flops 3221225472 | bytes 4194304 | tf_op jit(solution)/shard_map/expert_pieces/pallas_call | solution.py:429
  149.8 0.9 collective-permute-done.32.refs_3_
  150.8 1.0 collective-permute-done.30.refs_2_
  152.6 1.5 collective-permute-start.45
  154.2 0.9 collective-permute-start.44
  155.0 1.3 collective-permute-start.43
  156.3 5.2 %collective-permute-done.47 = bf16[64,2048]{1,0:T(8,128)(2,1)S(1)} collective-permute-done((bf16[64,2048]{1,0:T(8,128)(2,1)S(1)}, bf16[64,2048]{1,0:T(8,128)(2,1)S(1)}, u32[]{:S(2)}, u32[]{:S(2)}) %collective-permute-start.47) | collective-permute-done | bytes 262176 | tf_op jit(solution)/shard_map/ppermute | solution.py:456
  162.1 1.6 collective-permute-start.48
  164.6 1.0 sum_terms.2
  165.5 1.6 collective-permute-done.44.refs_1_
  167.5 2.5 %collective-permute-start.41 = (bf16[128,512]{1,0:T(8,128)(2,1)S(1)}, bf16[128,512]{1,0:T(8,128)(2,1)S(1)}, u32[]{:S(2)}, u32[]{:S(2)}) collective-permute-start(bf16[128,512]{1,0:T(8,128)(2,1)S(1)} %get-tuple-element.119), channel_id=1, source_target_pairs={{0,2},{1,3},{2,0},{3,1},{4,6},{5,7},{6,4},{7,5},{8,10},{9,11},{10,... | collective-permute-start | bytes 393224 | tf_op jit(solution)/shard_map/ppermute | solution.py:462
  170.0 1.3 collective-permute-done.48.refs_3_
  171.3 2.3 %collective-permute-start.42 = (bf16[128,512]{1,0:T(8,128)(2,1)S(1)}, bf16[128,512]{1,0:T(8,128)(2,1)S(1)}, u32[]{:S(2)}, u32[]{:S(2)}) collective-permute-start(bf16[128,512]{1,0:T(8,128)(2,1)S(1)} %get-tuple-element.120), channel_id=1, source_target_pairs={{0,3},{1,2},{2,1},{3,0},{4,7},{5,6},{6,5},{7,4},{8,11},{9,10},{10,... | collective-permute-start | bytes 393224 | tf_op jit(solution)/shard_map/ppermute | solution.py:462
  173.6 1.0 sum_terms.3
  174.7 2.1 %collective-permute-start.50 = (bf16[128,512]{1,0:T(8,128)(2,1)S(1)}, bf16[128,512]{1,0:T(8,128)(2,1)S(1)}, u32[]{:S(2)}, u32[]{:S(2)}) collective-permute-start(bf16[128,512]{1,0:T(8,128)(2,1)S(1)} %get-tuple-element.124), channel_id=1, source_target_pairs={{0,2},{1,3},{2,0},{3,1},{4,6},{5,7},{6,4},{7,5},{8,10},{9,11},{10,... | collective-permute-start | bytes 393224 | tf_op jit(solution)/shard_map/ppermute | solution.py:462
  176.7 2.3 %collective-permute-start.51 = (bf16[128,512]{1,0:T(8,128)(2,1)S(1)}, bf16[128,512]{1,0:T(8,128)(2,1)S(1)}, u32[]{:S(2)}, u32[]{:S(2)}) collective-permute-start(bf16[128,512]{1,0:T(8,128)(2,1)S(1)} %get-tuple-element.125), channel_id=1, source_target_pairs={{0,3},{1,2},{2,1},{3,0},{4,7},{5,6},{6,5},{7,4},{8,11},{9,10},{10,... | collective-permute-start | bytes 393224 | tf_op jit(solution)/shard_map/ppermute | solution.py:462
  179.0 4.7 %core_grads.1 = (bf16[256,512]{1,0:T(8,128)(2,1)}, bf16[256,512]{1,0:T(8,128)(2,1)}, bf16[256,512]{1,0:T(8,128)(2,1)}) custom-call(s32[3]{0:T(128)S(1)} %stage_weights.3.where_ref.me_ref, bf16[3,256,512]{2,1,0:T(8,128)(2,1)S(1)} %copy-done.3, bf16[256,512]{1,0:T(8,128)(2,1)S(1)} %copy-done.9, f32[4,256]{1,0:T(4,128)S(1)} %bitcast.53, ...), custom_call_target="tpu_custom_call" | custom-call | tf_op jit(solution)/shard_map/core_grads/pallas_call | solution.py:278
  183.7 6.2 %collective-permute-done.50.refs_6_ = bf16[128,512]{1,0:T(8,128)(2,1)S(1)} collective-permute-done((bf16[128,512]{1,0:T(8,128)(2,1)S(1)}, bf16[128,512]{1,0:T(8,128)(2,1)S(1)}, u32[]{:S(2)}, u32[]{:S(2)}) %collective-permute-start.50) | collective-permute-done | bytes 131104 | tf_op jit(solution)/shard_map/ppermute | solution.py:462
  189.9 1.4 layer_out.1
  (112 shorter events, 12.3 us)
Async XLA Ops:
  0.6 10.9 %copy-start.8 = (bf16[256,512]{1,0:T(8,128)(2,1)S(1)}, bf16[256,512]{1,0:T(8,128)(2,1)}, u32[]{:S(2)}) copy-start(bf16[256,512]{1,0:T(8,128)(2,1)} %cot_ref.3) | copy-start | bytes 786436
  0.6 10.9 %copy-start.13 = (f32[256,4]{0,1:T(4,128)S(1)}, f32[256,4]{0,1:T(4,128)}, u32[]{:S(2)}) copy-start(f32[256,4]{0,1:T(4,128)} %param.18) | copy-start | bytes 12292
  0.7 10.9 %copy-start.14 = (f32[4,3,512]{2,0,1:T(4,128)S(1)}, f32[4,3,512]{2,0,1:T(4,128)}, u32[]{:S(2)}) copy-start(f32[4,3,512]{2,0,1:T(4,128)} %param.17) | copy-start | bytes 73732
  0.7 10.9 %copy-start.15 = (s32[256,8]{0,1:T(8,128)S(1)}, s32[256,8]{0,1:T(8,128)}, u32[]{:S(2)}) copy-start(s32[256,8]{0,1:T(8,128)} %param.22) | copy-start | bytes 24580
  0.7 10.9 %copy-start.16 = (f32[256,8]{0,1:T(8,128)S(1)}, f32[256,8]{0,1:T(8,128)}, u32[]{:S(2)}) copy-start(f32[256,8]{0,1:T(8,128)} %param.23) | copy-start | bytes 24580
  8.0 23.5 %copy-start.1 = (bf16[512,2048]{1,0:T(8,128)(2,1)S(1)}, bf16[512,2048]{1,0:T(8,128)(2,1)}, u32[]{:S(2)}) copy-start(bf16[512,2048]{1,0:T(8,128)(2,1)} %w_ref.1) | copy-start | bytes 6291460
  8.0 3.6 %collective-permute-start = (bf16[3,16,512]{2,1,0:T(8,128)(2,1)}, bf16[3,16,512]{2,1,0:T(8,128)(2,1)S(1)}, u32[]{:S(2)}, u32[]{:S(2)}) collective-permute-start(bf16[3,16,512]{2,1,0:T(8,128)(2,1)} %get-tuple-element.68), channel_id=1, source_target_pairs={{0,4},{4,8},{8,12},{12,16},{16,20},{20,24},{24,28},{1,5},{5,9},{9,... | collective-permute-start | bytes 147464 | tf_op jit(solution)/shard_map/ppermute | solution.py:621
  12.7 20.8 %copy-start.18 = (f32[512]{0:T(512)S(1)}, f32[512]{0:T(512)}, u32[]{:S(2)}) copy-start(f32[512]{0:T(512)} %param.19) | copy-start | bytes 6148
  17.3 11.4 %collective-permute-start.3 = (bf16[672,128]{1,0:T(8,128)(2,1)S(1)}, bf16[672,128]{1,0:T(8,128)(2,1)S(1)}, u32[]{:S(2)}, u32[]{:S(2)}) collective-permute-start(bf16[672,128]{1,0:T(8,128)(2,1)S(1)} %get-tuple-element.71), channel_id=1, source_target_pairs={{0,24},{4,28},{8,16},{12,20},{16,8},{20,12},{24,0},{28,4},{1,25},{... | collective-permute-start | bytes 516104 | tf_op jit(solution)/shard_map/ppermute | solution.py:456
  23.4 7.8 %collective-permute-start.2 = (bf16[672,128]{1,0:T(8,128)(2,1)S(1)}, bf16[672,128]{1,0:T(8,128)(2,1)S(1)}, u32[]{:S(2)}, u32[]{:S(2)}) collective-permute-start(bf16[672,128]{1,0:T(8,128)(2,1)S(1)} %get-tuple-element.71), channel_id=1, source_target_pairs={{0,16},{4,20},{8,24},{12,28},{16,0},{20,4},{24,8},{28,12},{1,17},{... | collective-permute-start | bytes 516104 | tf_op jit(solution)/shard_map/ppermute | solution.py:456
  23.9 7.3 %collective-permute-start.1 = (bf16[672,128]{1,0:T(8,128)(2,1)S(1)}, bf16[672,128]{1,0:T(8,128)(2,1)S(1)}, u32[]{:S(2)}, u32[]{:S(2)}) collective-permute-start(bf16[672,128]{1,0:T(8,128)(2,1)S(1)} %get-tuple-element.71), channel_id=1, source_target_pairs={{0,8},{4,12},{8,0},{12,4},{16,24},{20,28},{24,16},{28,20},{1,9},{5... | collective-permute-start | bytes 516104 | tf_op jit(solution)/shard_map/ppermute | solution.py:456
  31.3 2.2 %collective-permute-start.4 = (bf16[4,672,128]{2,1,0:T(8,128)(2,1)S(1)}, bf16[4,672,128]{2,1,0:T(8,128)(2,1)S(1)}, u32[]{:S(2)}, u32[]{:S(2)}) collective-permute-start(bf16[4,672,128]{2,1,0:T(8,128)(2,1)S(1)} %pad_maximum_fusion.near_ref.near_routes.fwd_near), channel_id=1, source_target_pairs={{0,4},{4,0},{8,12},{12,8},{16,20},{20,16},{24,28},{28,24},{1,5},{5... | collective-permute-start | bytes 2064392 | tf_op jit(solution)/shard_map/ppermute | solution.py:456
  33.5 9.8 %copy-start.4 = (bf16[1,2048,512]{2,1,0:T(8,128)(2,1)S(1)}, bf16[1,2048,512]{2,1,0:T(8,128)(2,1)}, u32[]{:S(2)}) copy-start(bf16[1,2048,512]{2,1,0:T(8,128)(2,1)} %gate_ref.5) | copy-start | bytes 6291460
  33.5 9.8 %copy-start.5 = (bf16[1,2048,512]{2,1,0:T(8,128)(2,1)S(1)}, bf16[1,2048,512]{2,1,0:T(8,128)(2,1)}, u32[]{:S(2)}) copy-start(bf16[1,2048,512]{2,1,0:T(8,128)(2,1)} %up_ref.5) | copy-start | bytes 6291460
  37.2 24.6 %copy-start = (bf16[256,2048]{1,0:T(8,128)(2,1)S(1)}, bf16[256,2048]{1,0:T(8,128)(2,1)}, u32[]{:S(2)}) copy-start(bf16[256,2048]{1,0:T(8,128)(2,1)} %x_ref.3) | copy-start | bytes 3145732
  37.2 8.8 %collective-permute-start.8 = (bf16[1,576,128]{2,1,0:T(8,128)(2,1)S(1)}, bf16[1,576,128]{2,1,0:T(8,128)(2,1)S(1)}, u32[]{:S(2)}, u32[]{:S(2)}) collective-permute-start(bf16[1,576,128]{2,1,0:T(8,128)(2,1)S(1)} %bitcast.49), channel_id=1, source_target_pairs={{0,8},{4,12},{8,0},{12,4},{16,24},{20,28},{24,16},{28,20},{1,9},{5... | collective-permute-start | bytes 442376 | tf_op jit(solution)/shard_map/ppermute | solution.py:456
  38.9 13.1 %collective-permute-start.5 = (bf16[64,2048]{1,0:T(8,128)(2,1)S(1)}, bf16[64,2048]{1,0:T(8,128)(2,1)S(1)}, u32[]{:S(2)}, u32[]{:S(2)}) collective-permute-start(bf16[64,2048]{1,0:T(8,128)(2,1)S(1)} %get-tuple-element.73), channel_id=1, source_target_pairs={{0,1},{1,0},{2,3},{3,2},{4,5},{5,4},{6,7},{7,6},{8,9},{9,8},{10,11... | collective-permute-start | bytes 786440 | tf_op jit(solution)/shard_map/ppermute | solution.py:462
  40.5 21.4 %collective-permute-start.6 = (bf16[64,2048]{1,0:T(8,128)(2,1)S(1)}, bf16[64,2048]{1,0:T(8,128)(2,1)S(1)}, u32[]{:S(2)}, u32[]{:S(2)}) collective-permute-start(bf16[64,2048]{1,0:T(8,128)(2,1)S(1)} %get-tuple-element.74), channel_id=1, source_target_pairs={{0,2},{1,3},{2,0},{3,1},{4,6},{5,7},{6,4},{7,5},{8,10},{9,11},{10,... | collective-permute-start | bytes 786440 | tf_op jit(solution)/shard_map/ppermute | solution.py:462
  43.1 18.8 %collective-permute-start.7 = (bf16[64,2048]{1,0:T(8,128)(2,1)S(1)}, bf16[64,2048]{1,0:T(8,128)(2,1)S(1)}, u32[]{:S(2)}, u32[]{:S(2)}) collective-permute-start(bf16[64,2048]{1,0:T(8,128)(2,1)S(1)} %get-tuple-element.75), channel_id=1, source_target_pairs={{0,3},{1,2},{2,1},{3,0},{4,7},{5,6},{6,5},{7,4},{8,11},{9,10},{10,... | collective-permute-start | bytes 786440 | tf_op jit(solution)/shard_map/ppermute | solution.py:462
  44.9 17.0 %copy-start.17 = (f32[2048]{0:T(1024)S(1)}, f32[2048]{0:T(1024)}, u32[]{:S(2)}) copy-start(f32[2048]{0:T(1024)} %param.21) | copy-start | bytes 24580
  62.7 8.8 %collective-permute-start.12 = (bf16[2,576,128]{2,1,0:T(8,128)(2,1)S(1)}, bf16[2,576,128]{2,1,0:T(8,128)(2,1)S(1)}, u32[]{:S(2)}, u32[]{:S(2)}) collective-permute-start(bf16[2,576,128]{2,1,0:T(8,128)(2,1)S(1)} %pad_maximum_fusion.1), channel_id=1, source_target_pairs={{0,16},{4,20},{8,24},{12,28},{16,0},{20,4},{24,8},{28,12},{1,17},{... | collective-permute-start | bytes 884744 | tf_op jit(solution)/shard_map/ppermute | solution.py:456
  63.7 7.9 %collective-permute-start.11 = (bf16[32,2048]{1,0:T(8,128)(2,1)S(1)}, bf16[32,2048]{1,0:T(8,128)(2,1)S(1)}, u32[]{:S(2)}, u32[]{:S(2)}) collective-permute-start(bf16[32,2048]{1,0:T(8,128)(2,1)S(1)} %get-tuple-element.87.refs_0_), channel_id=1, source_target_pairs={{0,3},{1,2},{2,1},{3,0},{4,7},{5,6},{6,5},{7,4},{8,11},{9,10},{10,... | collective-permute-start | bytes 393224 | tf_op jit(solution)/shard_map/ppermute | solution.py:462
  66.2 12.7 %collective-permute-start.10 = (bf16[32,2048]{1,0:T(8,128)(2,1)S(1)}, bf16[32,2048]{1,0:T(8,128)(2,1)S(1)}, u32[]{:S(2)}, u32[]{:S(2)}) collective-permute-start(bf16[32,2048]{1,0:T(8,128)(2,1)S(1)} %get-tuple-element.87.refs_0_), channel_id=1, source_target_pairs={{0,2},{1,3},{2,0},{3,1},{4,6},{5,7},{6,4},{7,5},{8,10},{9,11},{10,... | collective-permute-start | bytes 393224 | tf_op jit(solution)/shard_map/ppermute | solution.py:462
  71.4 7.5 %collective-permute-start.9 = (bf16[32,2048]{1,0:T(8,128)(2,1)S(1)}, bf16[32,2048]{1,0:T(8,128)(2,1)S(1)}, u32[]{:S(2)}, u32[]{:S(2)}) collective-permute-start(bf16[32,2048]{1,0:T(8,128)(2,1)S(1)} %get-tuple-element.87.refs_0_), channel_id=1, source_target_pairs={{0,1},{1,0},{2,3},{3,2},{4,5},{5,4},{6,7},{7,6},{8,9},{9,8},{10,11... | collective-permute-start | bytes 393224 | tf_op jit(solution)/shard_map/ppermute | solution.py:462
  79.5 14.0 %collective-permute-start.14 = (bf16[128,2048]{1,0:T(8,128)(2,1)S(1)}, bf16[128,2048]{1,0:T(8,128)(2,1)S(1)}, u32[]{:S(2)}, u32[]{:S(2)}) collective-permute-start(bf16[128,2048]{1,0:T(8,128)(2,1)S(1)} %join_rows.2.refs_0_), channel_id=1, source_target_pairs={{0,16},{4,20},{8,24},{12,28},{16,0},{20,4},{24,8},{28,12},{1,17},{... | collective-permute-start | bytes 1572872 | tf_op jit(solution)/shard_map/ppermute | solution.py:456
  80.7 12.8 %collective-permute-start.13 = (bf16[128,2048]{1,0:T(8,128)(2,1)S(1)}, bf16[128,2048]{1,0:T(8,128)(2,1)S(1)}, u32[]{:S(2)}, u32[]{:S(2)}) collective-permute-start(bf16[128,2048]{1,0:T(8,128)(2,1)S(1)} %join_rows.2.refs_0_), channel_id=1, source_target_pairs={{0,8},{4,12},{8,0},{12,4},{16,24},{20,28},{24,16},{28,20},{1,9},{5... | collective-permute-start | bytes 1572872 | tf_op jit(solution)/shard_map/ppermute | solution.py:456
  81.1 8.1 %collective-permute-start.17 = (bf16[32,2048]{1,0:T(8,128)(2,1)S(1)}, bf16[32,2048]{1,0:T(8,128)(2,1)S(1)}, u32[]{:S(2)}, u32[]{:S(2)}) collective-permute-start(bf16[32,2048]{1,0:T(8,128)(2,1)S(1)} %get-tuple-element.91.refs_0_), channel_id=1, source_target_pairs={{0,3},{1,2},{2,1},{3,0},{4,7},{5,6},{6,5},{7,4},{8,11},{9,10},{10,... | collective-permute-start | bytes 393224 | tf_op jit(solution)/shard_map/ppermute | solution.py:462
  83.7 9.1 %collective-permute-start.16 = (bf16[32,2048]{1,0:T(8,128)(2,1)S(1)}, bf16[32,2048]{1,0:T(8,128)(2,1)S(1)}, u32[]{:S(2)}, u32[]{:S(2)}) collective-permute-start(bf16[32,2048]{1,0:T(8,128)(2,1)S(1)} %get-tuple-element.91.refs_0_), channel_id=1, source_target_pairs={{0,2},{1,3},{2,0},{3,1},{4,6},{5,7},{6,4},{7,5},{8,10},{9,11},{10,... | collective-permute-start | bytes 393224 | tf_op jit(solution)/shard_map/ppermute | solution.py:462
  83.7 9.1 %collective-permute-start.15 = (bf16[32,2048]{1,0:T(8,128)(2,1)S(1)}, bf16[32,2048]{1,0:T(8,128)(2,1)S(1)}, u32[]{:S(2)}, u32[]{:S(2)}) collective-permute-start(bf16[32,2048]{1,0:T(8,128)(2,1)S(1)} %get-tuple-element.91.refs_0_), channel_id=1, source_target_pairs={{0,1},{1,0},{2,3},{3,2},{4,5},{5,4},{6,7},{7,6},{8,9},{9,8},{10,11... | collective-permute-start | bytes 393224 | tf_op jit(solution)/shard_map/ppermute | solution.py:462
  93.5 7.1 %collective-permute-start.18 = (bf16[64,2048]{1,0:T(8,128)(2,1)S(1)}, bf16[64,2048]{1,0:T(8,128)(2,1)S(1)}, u32[]{:S(2)}, u32[]{:S(2)}) collective-permute-start(bf16[64,2048]{1,0:T(8,128)(2,1)S(1)} %slice.84), channel_id=1, source_target_pairs={{0,16},{4,20},{8,24},{12,28},{16,0},{20,4},{24,8},{28,12},{1,17},{... | collective-permute-start | bytes 786440 | tf_op jit(solution)/shard_map/ppermute | solution.py:456
  95.2 6.8 %collective-permute-start.19 = (bf16[64,2048]{1,0:T(8,128)(2,1)S(1)}, bf16[64,2048]{1,0:T(8,128)(2,1)S(1)}, u32[]{:S(2)}, u32[]{:S(2)}) collective-permute-start(bf16[64,2048]{1,0:T(8,128)(2,1)S(1)} %slice.85), channel_id=1, source_target_pairs={{0,8},{4,12},{8,0},{12,4},{16,24},{20,28},{24,16},{28,20},{1,9},{5... | collective-permute-start | bytes 786440 | tf_op jit(solution)/shard_map/ppermute | solution.py:456
  96.0 6.6 %collective-permute-start.20 = (bf16[128,2048]{1,0:T(8,128)(2,1)S(1)}, bf16[128,2048]{1,0:T(8,128)(2,1)S(1)}, u32[]{:S(2)}, u32[]{:S(2)}) collective-permute-start(bf16[128,2048]{1,0:T(8,128)(2,1)S(1)} %join_rows.2.refs_0_), channel_id=1, source_target_pairs={{0,4},{4,0},{8,12},{12,8},{16,20},{20,16},{24,28},{28,24},{1,5},{5... | collective-permute-start | bytes 1572872 | tf_op jit(solution)/shard_map/ppermute | solution.py:456
  96.0 8.1 %collective-permute-start.21 = (bf16[128,2048]{1,0:T(8,128)(2,1)S(1)}, bf16[128,2048]{1,0:T(8,128)(2,1)S(1)}, u32[]{:S(2)}, u32[]{:S(2)}) collective-permute-start(bf16[128,2048]{1,0:T(8,128)(2,1)S(1)} %collective-permute-done.13.refs_1_), channel_id=1, source_target_pairs={{0,4},{4,0},{8,12},{12,8},{16,20},{20,16},{24,28},{28,24},{1,5},{5... | collective-permute-start | bytes 1572872 | tf_op jit(solution)/shard_map/ppermute | solution.py:456
  96.5 7.6 %collective-permute-start.22 = (bf16[128,2048]{1,0:T(8,128)(2,1)S(1)}, bf16[128,2048]{1,0:T(8,128)(2,1)S(1)}, u32[]{:S(2)}, u32[]{:S(2)}) collective-permute-start(bf16[128,2048]{1,0:T(8,128)(2,1)S(1)} %collective-permute-done.14.refs_2_), channel_id=1, source_target_pairs={{0,4},{4,0},{8,12},{12,8},{16,20},{20,16},{24,28},{28,24},{1,5},{5... | collective-permute-start | bytes 1572872 | tf_op jit(solution)/shard_map/ppermute | solution.py:456
  102.1 2.0 %collective-permute-start.23 = (bf16[128,2048]{1,0:T(8,128)(2,1)S(1)}, bf16[128,2048]{1,0:T(8,128)(2,1)S(1)}, u32[]{:S(2)}, u32[]{:S(2)}) collective-permute-start(bf16[128,2048]{1,0:T(8,128)(2,1)S(1)} %constant_dynamic-update-slice_fusion.2.refs_3_), channel_id=1, source_target_pairs={{0,4},{4,0},{8,12},{12,8},{16,20},{20,16},{24,28},{28,24},{1,5},{5... | collective-permute-start | bytes 1572872 | tf_op jit(solution)/shard_map/ppermute | solution.py:456
  102.1 14.3 %collective-permute-start.25 = (bf16[128,2048]{1,0:T(8,128)(2,1)S(1)}, bf16[128,2048]{1,0:T(8,128)(2,1)S(1)}, u32[]{:S(2)}, u32[]{:S(2)}) collective-permute-start(bf16[128,2048]{1,0:T(8,128)(2,1)S(1)} %join_rows.3.refs_0_), channel_id=1, source_target_pairs={{0,16},{4,20},{8,24},{12,28},{16,0},{20,4},{24,8},{28,12},{1,17},{... | collective-permute-start | bytes 1572872 | tf_op jit(solution)/shard_map/ppermute | solution.py:456
  102.6 14.0 %collective-permute-start.24 = (bf16[128,2048]{1,0:T(8,128)(2,1)S(1)}, bf16[128,2048]{1,0:T(8,128)(2,1)S(1)}, u32[]{:S(2)}, u32[]{:S(2)}) collective-permute-start(bf16[128,2048]{1,0:T(8,128)(2,1)S(1)} %join_rows.3.refs_0_), channel_id=1, source_target_pairs={{0,8},{4,12},{8,0},{12,4},{16,24},{20,28},{24,16},{28,20},{1,9},{5... | collective-permute-start | bytes 1572872 | tf_op jit(solution)/shard_map/ppermute | solution.py:456
  116.6 4.2 %collective-permute-start.26 = (bf16[4,128,2048]{2,1,0:T(8,128)(2,1)S(1)}, bf16[4,128,2048]{2,1,0:T(8,128)(2,1)S(1)}, u32[]{:S(2)}, u32[]{:S(2)}) collective-permute-start(bf16[4,128,2048]{2,1,0:T(8,128)(2,1)S(1)} %get-tuple-element.96), channel_id=1, source_target_pairs={{0,4},{4,0},{8,12},{12,8},{16,20},{20,16},{24,28},{28,24},{1,5},{5... | collective-permute-start | bytes 6291464 | tf_op jit(solution)/shard_map/ppermute | solution.py:456
  116.6 11.2 %collective-permute-start.33 = (bf16[128,2048]{1,0:T(8,128)(2,1)S(1)}, bf16[128,2048]{1,0:T(8,128)(2,1)S(1)}, u32[]{:S(2)}, u32[]{:S(2)}) collective-permute-start(bf16[128,2048]{1,0:T(8,128)(2,1)S(1)} %join_rows.3.refs_0_), channel_id=1, source_target_pairs={{0,4},{4,0},{8,12},{12,8},{16,20},{20,16},{24,28},{28,24},{1,5},{5... | collective-permute-start | bytes 1572872 | tf_op jit(solution)/shard_map/ppermute | solution.py:456
  117.1 8.3 %collective-permute-start.37 = (bf16[64,2048]{1,0:T(8,128)(2,1)S(1)}, bf16[64,2048]{1,0:T(8,128)(2,1)S(1)}, u32[]{:S(2)}, u32[]{:S(2)}) collective-permute-start(bf16[64,2048]{1,0:T(8,128)(2,1)S(1)} %slice.119), channel_id=1, source_target_pairs={{0,8},{4,12},{8,0},{12,4},{16,24},{20,28},{24,16},{28,20},{1,9},{5... | collective-permute-start | bytes 786440 | tf_op jit(solution)/shard_map/ppermute | solution.py:456
  118.7 8.0 %collective-permute-start.36 = (bf16[64,2048]{1,0:T(8,128)(2,1)S(1)}, bf16[64,2048]{1,0:T(8,128)(2,1)S(1)}, u32[]{:S(2)}, u32[]{:S(2)}) collective-permute-start(bf16[64,2048]{1,0:T(8,128)(2,1)S(1)} %slice.118), channel_id=1, source_target_pairs={{0,16},{4,20},{8,24},{12,28},{16,0},{20,4},{24,8},{28,12},{1,17},{... | collective-permute-start | bytes 786440 | tf_op jit(solution)/shard_map/ppermute | solution.py:456
  119.6 9.5 %collective-permute-start.35 = (bf16[128,2048]{1,0:T(8,128)(2,1)S(1)}, bf16[128,2048]{1,0:T(8,128)(2,1)S(1)}, u32[]{:S(2)}, u32[]{:S(2)}) collective-permute-start(bf16[128,2048]{1,0:T(8,128)(2,1)S(1)} %collective-permute-done.25.refs_2_), channel_id=1, source_target_pairs={{0,4},{4,0},{8,12},{12,8},{16,20},{20,16},{24,28},{28,24},{1,5},{5... | collective-permute-start | bytes 1572872 | tf_op jit(solution)/shard_map/ppermute | solution.py:456
  120.7 8.7 %collective-permute-start.34 = (bf16[128,2048]{1,0:T(8,128)(2,1)S(1)}, bf16[128,2048]{1,0:T(8,128)(2,1)S(1)}, u32[]{:S(2)}, u32[]{:S(2)}) collective-permute-start(bf16[128,2048]{1,0:T(8,128)(2,1)S(1)} %collective-permute-done.24.refs_1_), channel_id=1, source_target_pairs={{0,4},{4,0},{8,12},{12,8},{16,20},{20,16},{24,28},{28,24},{1,5},{5... | collective-permute-start | bytes 1572872 | tf_op jit(solution)/shard_map/ppermute | solution.py:456
  126.7 4.2 %collective-permute-start.38 = (bf16[128,2048]{1,0:T(8,128)(2,1)S(1)}, bf16[128,2048]{1,0:T(8,128)(2,1)S(1)}, u32[]{:S(2)}, u32[]{:S(2)}) collective-permute-start(bf16[128,2048]{1,0:T(8,128)(2,1)S(1)} %constant_dynamic-update-slice_fusion.4.refs_3_), channel_id=1, source_target_pairs={{0,4},{4,0},{8,12},{12,8},{16,20},{20,16},{24,28},{28,24},{1,5},{5... | collective-permute-start | bytes 1572872 | tf_op jit(solution)/shard_map/ppermute | solution.py:456
  126.8 10.2 %collective-permute-start.31 = (bf16[64,2048]{1,0:T(8,128)(2,1)S(1)}, bf16[64,2048]{1,0:T(8,128)(2,1)S(1)}, u32[]{:S(2)}, u32[]{:S(2)}) collective-permute-start(bf16[64,2048]{1,0:T(8,128)(2,1)S(1)} %get-tuple-element.138), channel_id=1, source_target_pairs={{0,16},{4,20},{8,24},{12,28},{16,0},{20,4},{24,8},{28,12},{1,17},{... | collective-permute-start | bytes 786440 | tf_op jit(solution)/shard_map/ppermute | solution.py:456
  127.7 9.3 %collective-permute-start.29 = (bf16[64,2048]{1,0:T(8,128)(2,1)S(1)}, bf16[64,2048]{1,0:T(8,128)(2,1)S(1)}, u32[]{:S(2)}, u32[]{:S(2)}) collective-permute-start(bf16[64,2048]{1,0:T(8,128)(2,1)S(1)} %get-tuple-element.139), channel_id=1, source_target_pairs={{0,8},{4,12},{8,0},{12,4},{16,24},{20,28},{24,16},{28,20},{1,9},{5... | collective-permute-start | bytes 786440 | tf_op jit(solution)/shard_map/ppermute | solution.py:456
  129.1 12.1 %collective-permute-start.28 = (bf16[64,2048]{1,0:T(8,128)(2,1)S(1)}, bf16[64,2048]{1,0:T(8,128)(2,1)S(1)}, u32[]{:S(2)}, u32[]{:S(2)}) collective-permute-start(bf16[64,2048]{1,0:T(8,128)(2,1)S(1)} %get-tuple-element.140), channel_id=1, source_target_pairs={{0,16},{4,20},{8,24},{12,28},{16,0},{20,4},{24,8},{28,12},{1,17},{... | collective-permute-start | bytes 786440 | tf_op jit(solution)/shard_map/ppermute | solution.py:456
  129.4 12.3 %collective-permute-start.27 = (bf16[64,2048]{1,0:T(8,128)(2,1)S(1)}, bf16[64,2048]{1,0:T(8,128)(2,1)S(1)}, u32[]{:S(2)}, u32[]{:S(2)}) collective-permute-start(bf16[64,2048]{1,0:T(8,128)(2,1)S(1)} %get-tuple-element.141), channel_id=1, source_target_pairs={{0,8},{4,12},{8,0},{12,4},{16,24},{20,28},{24,16},{28,20},{1,9},{5... | collective-permute-start | bytes 786440 | tf_op jit(solution)/shard_map/ppermute | solution.py:456
  141.7 10.1 %collective-permute-start.39 = (bf16[4,128,2048]{2,1,0:T(8,128)(2,1)S(1)}, bf16[4,128,2048]{2,1,0:T(8,128)(2,1)S(1)}, u32[]{:S(2)}, u32[]{:S(2)}) collective-permute-start(bf16[4,128,2048]{2,1,0:T(8,128)(2,1)S(1)} %expert_pieces.4), channel_id=1, source_target_pairs={{0,4},{4,0},{8,12},{12,8},{16,20},{20,16},{24,28},{28,24},{1,5},{5... | collective-permute-start | bytes 6291464 | tf_op jit(solution)/shard_map/ppermute | solution.py:456
  142.0 8.8 %collective-permute-start.32 = (bf16[64,2048]{1,0:T(8,128)(2,1)S(1)}, bf16[64,2048]{1,0:T(8,128)(2,1)S(1)}, u32[]{:S(2)}, u32[]{:S(2)}) collective-permute-start(bf16[64,2048]{1,0:T(8,128)(2,1)S(1)} %get-tuple-element.136), channel_id=1, source_target_pairs={{0,8},{4,12},{8,0},{12,4},{16,24},{20,28},{24,16},{28,20},{1,9},{5... | collective-permute-start | bytes 786440 | tf_op jit(solution)/shard_map/ppermute | solution.py:456
  143.4 8.4 %collective-permute-start.30 = (bf16[64,2048]{1,0:T(8,128)(2,1)S(1)}, bf16[64,2048]{1,0:T(8,128)(2,1)S(1)}, u32[]{:S(2)}, u32[]{:S(2)}) collective-permute-start(bf16[64,2048]{1,0:T(8,128)(2,1)S(1)} %get-tuple-element.137), channel_id=1, source_target_pairs={{0,16},{4,20},{8,24},{12,28},{16,0},{20,4},{24,8},{28,12},{1,17},{... | collective-permute-start | bytes 786440 | tf_op jit(solution)/shard_map/ppermute | solution.py:456
  152.2 9.3 %collective-permute-start.47 = (bf16[64,2048]{1,0:T(8,128)(2,1)S(1)}, bf16[64,2048]{1,0:T(8,128)(2,1)S(1)}, u32[]{:S(2)}, u32[]{:S(2)}) collective-permute-start(bf16[64,2048]{1,0:T(8,128)(2,1)S(1)} %get-tuple-element.134), channel_id=1, source_target_pairs={{0,16},{4,20},{8,24},{12,28},{16,0},{20,4},{24,8},{28,12},{1,17},{... | collective-permute-start | bytes 786440 | tf_op jit(solution)/shard_map/ppermute | solution.py:456
  152.6 9.2 %collective-permute-start.45 = (bf16[64,2048]{1,0:T(8,128)(2,1)S(1)}, bf16[64,2048]{1,0:T(8,128)(2,1)S(1)}, u32[]{:S(2)}, u32[]{:S(2)}) collective-permute-start(bf16[64,2048]{1,0:T(8,128)(2,1)S(1)} %get-tuple-element.135), channel_id=1, source_target_pairs={{0,8},{4,12},{8,0},{12,4},{16,24},{20,28},{24,16},{28,20},{1,9},{5... | collective-permute-start | bytes 786440 | tf_op jit(solution)/shard_map/ppermute | solution.py:456
  154.1 20.5 %collective-permute-start.52 = (bf16[4,576,128]{2,1,0:T(8,128)(2,1)S(1)}, bf16[4,576,128]{2,1,0:T(8,128)(2,1)S(1)}, u32[]{:S(2)}, u32[]{:S(2)}) collective-permute-start(bf16[4,576,128]{2,1,0:T(8,128)(2,1)S(1)} %constant_dynamic-update-slice_fusion.bwd_near), channel_id=1, source_target_pairs={{0,4},{4,0},{8,12},{12,8},{16,20},{20,16},{24,28},{28,24},{1,5},{5... | collective-permute-start | bytes 1769480 | tf_op jit(solution)/shard_map/ppermute | solution.py:456
  154.2 13.0 %collective-permute-start.44 = (bf16[64,2048]{1,0:T(8,128)(2,1)S(1)}, bf16[64,2048]{1,0:T(8,128)(2,1)S(1)}, u32[]{:S(2)}, u32[]{:S(2)}) collective-permute-start(bf16[64,2048]{1,0:T(8,128)(2,1)S(1)} %get-tuple-element.132), channel_id=1, source_target_pairs={{0,16},{4,20},{8,24},{12,28},{16,0},{20,4},{24,8},{28,12},{1,17},{... | collective-permute-start | bytes 786440 | tf_op jit(solution)/shard_map/ppermute | solution.py:456
  155.0 12.5 %collective-permute-start.43 = (bf16[64,2048]{1,0:T(8,128)(2,1)S(1)}, bf16[64,2048]{1,0:T(8,128)(2,1)S(1)}, u32[]{:S(2)}, u32[]{:S(2)}) collective-permute-start(bf16[64,2048]{1,0:T(8,128)(2,1)S(1)} %get-tuple-element.133), channel_id=1, source_target_pairs={{0,8},{4,12},{8,0},{12,4},{16,24},{20,28},{24,16},{28,20},{1,9},{5... | collective-permute-start | bytes 786440 | tf_op jit(solution)/shard_map/ppermute | solution.py:456
  162.1 9.2 %collective-permute-start.48 = (bf16[64,2048]{1,0:T(8,128)(2,1)S(1)}, bf16[64,2048]{1,0:T(8,128)(2,1)S(1)}, u32[]{:S(2)}, u32[]{:S(2)}) collective-permute-start(bf16[64,2048]{1,0:T(8,128)(2,1)S(1)} %get-tuple-element.130), channel_id=1, source_target_pairs={{0,8},{4,12},{8,0},{12,4},{16,24},{20,28},{24,16},{28,20},{1,9},{5... | collective-permute-start | bytes 786440 | tf_op jit(solution)/shard_map/ppermute | solution.py:456
  163.7 9.9 %collective-permute-start.46 = (bf16[64,2048]{1,0:T(8,128)(2,1)S(1)}, bf16[64,2048]{1,0:T(8,128)(2,1)S(1)}, u32[]{:S(2)}, u32[]{:S(2)}) collective-permute-start(bf16[64,2048]{1,0:T(8,128)(2,1)S(1)} %get-tuple-element.131), channel_id=1, source_target_pairs={{0,16},{4,20},{8,24},{12,28},{16,0},{20,4},{24,8},{28,12},{1,17},{... | collective-permute-start | bytes 786440 | tf_op jit(solution)/shard_map/ppermute | solution.py:456
  167.1 9.6 %collective-permute-start.40 = (bf16[128,512]{1,0:T(8,128)(2,1)S(1)}, bf16[128,512]{1,0:T(8,128)(2,1)S(1)}, u32[]{:S(2)}, u32[]{:S(2)}) collective-permute-start(bf16[128,512]{1,0:T(8,128)(2,1)S(1)} %get-tuple-element.118), channel_id=1, source_target_pairs={{0,1},{1,0},{2,3},{3,2},{4,5},{5,4},{6,7},{7,6},{8,9},{9,8},{10,11... | collective-permute-start | bytes 393224 | tf_op jit(solution)/shard_map/ppermute | solution.py:462
  167.5 16.2 %collective-permute-start.41 = (bf16[128,512]{1,0:T(8,128)(2,1)S(1)}, bf16[128,512]{1,0:T(8,128)(2,1)S(1)}, u32[]{:S(2)}, u32[]{:S(2)}) collective-permute-start(bf16[128,512]{1,0:T(8,128)(2,1)S(1)} %get-tuple-element.119), channel_id=1, source_target_pairs={{0,2},{1,3},{2,0},{3,1},{4,6},{5,7},{6,4},{7,5},{8,10},{9,11},{10,... | collective-permute-start | bytes 393224 | tf_op jit(solution)/shard_map/ppermute | solution.py:462
  171.3 12.4 %collective-permute-start.42 = (bf16[128,512]{1,0:T(8,128)(2,1)S(1)}, bf16[128,512]{1,0:T(8,128)(2,1)S(1)}, u32[]{:S(2)}, u32[]{:S(2)}) collective-permute-start(bf16[128,512]{1,0:T(8,128)(2,1)S(1)} %get-tuple-element.120), channel_id=1, source_target_pairs={{0,3},{1,2},{2,1},{3,0},{4,7},{5,6},{6,5},{7,4},{8,11},{9,10},{10,... | collective-permute-start | bytes 393224 | tf_op jit(solution)/shard_map/ppermute | solution.py:462
  174.6 9.2 %collective-permute-start.49 = (bf16[128,512]{1,0:T(8,128)(2,1)S(1)}, bf16[128,512]{1,0:T(8,128)(2,1)S(1)}, u32[]{:S(2)}, u32[]{:S(2)}) collective-permute-start(bf16[128,512]{1,0:T(8,128)(2,1)S(1)} %get-tuple-element.123), channel_id=1, source_target_pairs={{0,1},{1,0},{2,3},{3,2},{4,5},{5,4},{6,7},{7,6},{8,9},{9,8},{10,11... | collective-permute-start | bytes 393224 | tf_op jit(solution)/shard_map/ppermute | solution.py:462
  174.7 15.2 %collective-permute-start.50 = (bf16[128,512]{1,0:T(8,128)(2,1)S(1)}, bf16[128,512]{1,0:T(8,128)(2,1)S(1)}, u32[]{:S(2)}, u32[]{:S(2)}) collective-permute-start(bf16[128,512]{1,0:T(8,128)(2,1)S(1)} %get-tuple-element.124), channel_id=1, source_target_pairs={{0,2},{1,3},{2,0},{3,1},{4,6},{5,7},{6,4},{7,5},{8,10},{9,11},{10,... | collective-permute-start | bytes 393224 | tf_op jit(solution)/shard_map/ppermute | solution.py:462
  176.7 13.2 %collective-permute-start.51 = (bf16[128,512]{1,0:T(8,128)(2,1)S(1)}, bf16[128,512]{1,0:T(8,128)(2,1)S(1)}, u32[]{:S(2)}, u32[]{:S(2)}) collective-permute-start(bf16[128,512]{1,0:T(8,128)(2,1)S(1)} %get-tuple-element.125), channel_id=1, source_target_pairs={{0,3},{1,2},{2,1},{3,0},{4,7},{5,6},{6,5},{7,4},{8,11},{9,10},{10,... | collective-permute-start | bytes 393224 | tf_op jit(solution)/shard_map/ppermute | solution.py:462
  (8 other events, 24.3 us)

commit v9 on v8

--- a/solution.py
+++ b/solution.py
@@ -484,27 +484,24 @@
     return {mask: swap(own, mask) for mask in masks}
 
 
-def forward(own, came, leaving=None):
-    came = {0: own} | came
-    if lax.axis_size("ctx") == PLANE:
-        half = own.shape[0] // 2
-        halves = [swap(came[ROW][:half], COL), swap(came[COL][half:], ROW)]
-        came[ROW | COL] = jnp.concatenate(halves if leaving is None else after(halves, leaving))
-    return [came[mask] for mask in range(0, lax.axis_size("ctx"), 2)]
+def forward(came):
+    if lax.axis_size("ctx") != PLANE:
+        return []
+    half = came[ROW].shape[0] // 2
+    return [swap(came[ROW][:half], COL), swap(came[COL][half:], ROW)]
 
 
 def first_sums(here, arrived):
+    tok = here.shape[1]
     if lax.axis_size("ctx") != PLANE:
-        return [(2 * at, 0, plus(here[at], arrived[at])) for at in range(1, here.shape[0])]
-    half = here.shape[1] // 2
-    row, col, across = ROW // 2, COL // 2, (ROW | COL) // 2
-    upper, lower = slice(0, half), slice(half, 2 * half)
-    return [
-        (ROW, 0, plus(here[across, upper], arrived[across, upper])),
-        (COL, half, plus(here[across, lower], arrived[across, lower])),
-        (ROW, 0, plus(here[row, upper], arrived[row, upper])),
-        (COL, half, plus(here[col, lower], arrived[col, lower])),
-    ]
+        return [(2 * at, plus(here[at], arrived[at]), [(0, 0, tok)]) for at in range(1, here.shape[0])]
+    half, across = tok // 2, (ROW | COL) // 2
+    sums = []
+    for mask, start in ((ROW, 0), (COL, half)):
+        part = slice(start, start + half)
+        pieces = [plus(here[at, part], arrived[at, part]) for at in (across, mask // 2)]
+        sums.append((mask, jnp.concatenate(pieces), [(half, start, half)]))
+    return sums
 
 
 def last_sums(here, arrived, came):
@@ -513,16 +510,24 @@
     half = here.shape[1] // 2
     row, col = ROW // 2, COL // 2
     return [
-        (COL, 0, plus(here[col, :half], arrived[col, :half], came[0])),
-        (ROW, half, plus(here[row, half:], arrived[row, half:], came[1])),
+        (COL, plus(here[col, :half], arrived[col, :half], came[0][:half]), [(0, 0, half)]),
+        (ROW, plus(here[row, half:], arrived[row, half:], came[1][:half]), [(0, half, half)]),
     ]
 
 
 def send_sums(sums):
-    return [swap(rows, mask) for mask, _, rows in sums]
-
-
-def sum_kernel(starts, where_ref, attn_ref, near_ref, arrived_ref, *refs):
+    return [swap(rows, mask) for mask, rows, _ in sums]
+
+
+def arrays(sums):
+    return [rows for _, rows, _ in sums]
+
+
+def terms_of(sums, received):
+    return [(rows, places) for (_, _, places), rows in zip(sums, received) if places]
+
+
+def sum_kernel(places, where_ref, attn_ref, near_ref, arrived_ref, *refs):
     parts = attn_ref.shape[1] // refs[-1].shape[1]
     others, outs, total_ref = refs[: -parts - 1], refs[-parts - 1 : -1], refs[-1]
     part, width = attn_ref.shape
@@ -532,19 +537,21 @@
         at = pl.ds(pl.multiple_of((where_ref[2] ^ mask) * cols, cols), cols)
         total = near_ref[0, :, at].astype(F32) + arrived_ref[0, :, at].astype(F32)
         total_ref[...] = total
-        for start, ref in zip(starts, others):
-            total_ref[start : start + ref.shape[0]] += ref[:, at].astype(F32)
+        for spots, ref in zip(places, others):
+            for source, target, count in spots:
+                total_ref[target : target + count] += ref[source : source + count, at].astype(F32)
         total_ref[own, :] += attn_ref[:, at]
         out_ref[...] = total_ref[...].astype(BF)
 
 
-def sum_terms(where, attn, near, arrived, others, starts, parts):
+def sum_terms(where, attn, near, arrived, terms, parts):
+    others, places = [rows for rows, _ in terms], tuple(tuple(spots) for _, spots in terms)
     _, tok, width = near.shape
     part = attn.shape[0]
     cols = width // parts
     first = pl.BlockSpec((1, tok, width), lambda i: (0, 0, 0))
     return pl.pallas_call(
-        functools.partial(sum_kernel, tuple(starts)),
+        functools.partial(sum_kernel, places),
         grid=(1,),
         in_specs=[
             pl.BlockSpec(memory_space=pltpu.SMEM),
@@ -633,54 +640,61 @@
     while bwd.shape[0] < n_ctx // 2:
         bwd = double(bwd, 2 * bwd.shape[0])
 
-    came, owns = [], []
+    evens = list(range(0, n_ctx, 2))
+    odds = [mask | CORE for mask in evens]
     own = join_rows(where, after(send_heads([normed[0]] * n_head), bwd))
     bwd = (bwd, swap(after(bwd, own), CORE))
+    rows = []
     for chunk in range(CHUNKS):
-        owns.append(own)
-        came.append(depart(own))
+        rows.append({0: own, CORE: swap(own, CORE)} | depart(own))
         if chunk + 1 < CHUNKS:
-            own = join_rows(where, send_heads([after(normed[chunk + 1], own)] * n_head))
-            came[chunk] = after(came[chunk], own)
-    evens = list(range(0, n_ctx, 2))
-    odds = [mask | CORE for mask in evens]
-    pending, sums, first = [], [], None
+            parts = send_heads([after(normed[chunk + 1], own)] * n_head)
+            own = join_rows(where, after(parts, rows[chunk][CORE]))
+            rows[chunk] = after(rows[chunk], own)
+
+    pending, sums, first, arrived = [], [], None, None
     for chunk in range(CHUNKS):
-        near = forward(owns[chunk], came[chunk], first and [part for _, _, part in first])
-        rows = {mask: part for mask, part in zip(evens, near)}
-        rows |= {mask | CORE: swap(part, CORE) for mask, part in rows.items()}
+        here_rows = rows[chunk]
+        halves = forward(here_rows)
+        here_rows |= {mask | CORE: swap(part, CORE) for mask, part in here_rows.items() if mask and not mask & CORE}
         if pending:
-            rows = after(rows, [part for _, _, part in first])
+            arrived = after(arrived, [part for mask, part in here_rows.items() if mask & CORE])
+            first = first_sums(pending[-1][0], arrived)
+            pending[-1] += (arrived, first, send_sums(first))
+            halves = after(halves, arrays(first))
+        if halves:
+            across = jnp.concatenate(halves)
+            here_rows |= {ROW | COL: across, ROW | COL | CORE: swap(across, CORE)}
+        if pending:
+            here_rows = after(here_rows, arrays(first))
         experts_of = functools.partial(
             expert_pieces, chunk * chunk_rows, where, gate=w_gate, up=w_up, down=w_down, routes=fwd
         )
         if chunk + 1 < CHUNKS:
-            here, far = experts_of(rows=rows, groups=[evens, odds])
-            arrived = swap(after(far, came[chunk + 1]), CORE)
+            here, far = experts_of(rows=here_rows, groups=[evens, odds])
+            arrived = swap(after(far, (rows[chunk + 1], bwd)), CORE)
+            pending.append((here,))
         else:
-            (far,) = experts_of(rows=rows, groups=[odds])
-            ready = [far]
-            arrived = swap(after(far, pending[-1][3]) if pending else far, CORE)
-            if pending:
-                last = last_sums(*pending[-1][:2], pending[-1][3])
-                ready += [part for _, _, part in last]
-                last = [(mask, start, swap(part, mask)) for mask, start, part in last]
-                pending[-1] += (last,)
-                arrived = after(arrived, [part for _, _, part in last])
-            (here,) = experts_of(rows=after(rows, ready), groups=[evens])
-        first = first_sums(here, arrived)
-        pending.append((here, arrived, first, send_sums(first)))
-    last = last_sums(*pending[-1][:2], pending[-1][3])
-    pending[-1] += ([(mask, start, swap(part, mask)) for mask, start, part in last],)
+            (far,) = experts_of(rows=here_rows, groups=[odds])
+            arrived = swap(after(far, pending[-1][3]), CORE)
+            last = last_sums(*pending[-1][:2], pending[-1][3])
+            received = send_sums(last)
+            pending[-1] += (terms_of(first, pending[-1][3]) + terms_of(last, received),)
+            (here,) = experts_of(rows=after(here_rows, [far] + arrays(last)), groups=[evens])
+            arrived = after(arrived, received)
+            first = first_sums(here, arrived)
+            pending.append((here, arrived, first, send_sums(first)))
+
     for chunk in range(CHUNKS):
-        here, arrived, first, received, last = pending[chunk]
-        terms = [(start, part) for (_, start, _), part in zip(first, received)]
-        if last:
-            terms = terms[2:] + [(start, part) for _, start, part in last]
-        starts, others = zip(*terms)
+        here, arrived, first, received = pending[chunk][:4]
         if chunk + 1 < CHUNKS:
-            others = after(others, [part for _, _, part in pending[chunk + 1][2]])
-        sums.append(send_heads(sum_terms(where, attn[chunk], here, arrived, others, starts, n_head)))
+            terms = pending[chunk][4]
+            held = after([rows for rows, _ in terms], arrays(pending[chunk + 1][2]))
+            terms = list(zip(held, [places for _, places in terms]))
+        else:
+            last = last_sums(here, arrived, after(received, sums[-1][0]))
+            terms = terms_of(first, received) + terms_of(last, send_sums(last))
+        sums.append(send_heads(sum_terms(where, attn[chunk], here, arrived, terms, n_head)))
     grads = core_grads(where, qkv, grad_core, steps, fwd, bwd)
     return (final_sum(where, hidden_in, sums), *grads)
 

time: 192 us -> 196 us (1.021)
  waiting for transfers between devices: 73.1 us -> 79.2 us
  starting transfers between devices: 60.8 us -> 58.8 us
    ppermute x37 -> x33, waiting for transfers between devices: 35.4 us -> 38.8 us  [swap(): lax.ppermute(value, 'ctx', [(at, at ^ mask) for at in range(lax.axis_size...]
    ppermute x15, waiting for transfers between devices: 36.6 us -> 39.3 us  [send_heads(): lax.ppermute(parts[mask], 'head', [(at, at ^ mask) for at in range(count)])]
    ppermute x37 -> x33, starting transfers between devices: 32.5 us -> 30.1 us  [swap(): lax.ppermute(value, 'ctx', [(at, at ^ mask) for at in range(lax.axis_size...]
  transfers between devices with their start and end apart: 53 -> 49, of which waited for: 27 -> 27; matrix products, arithmetic and copies ran while one was open for 1% -> 1% of each run, Pallas kernels for 18% -> 17%
where the time goes in v9:
time: 196 us
  waiting for transfers between devices  79.2 us (40%)
  starting transfers between devices  58.8 us (30%)
  Pallas kernels  50.4 us (26%)
  local copies, waits for them, and re-layouts  4.58 us (2%)
    ppermute x15, waiting for transfers between devices, send_heads(): lax.ppermute(parts[mask], 'head', [(at, at ^ mask) for at in range(count)])  39.3 us
    ppermute x33, waiting for transfers between devices, swap(): lax.ppermute(value, 'ctx', [(at, at ^ mask) for at in range(lax.axis_size...  38.8 us
    ppermute x33, starting transfers between devices, swap(): lax.ppermute(value, 'ctx', [(at, at ^ mask) for at in range(lax.axis_size...  30.1 us
    ppermute x15, starting transfers between devices, send_heads(): lax.ppermute(parts[mask], 'head', [(at, at ^ mask) for at in range(count)])  26.2 us
    pallas_call x3, Pallas kernels, expert_pieces(): pl.pallas_call(functools.partial(expert_kernel, tuple(map(tuple, groups))...  24.1 us
    pallas_call x1, Pallas kernels, project(): pl.pallas_call(qkv_kernel, in_specs=[hbm, vmem, hbm], out_specs=[vmem, vm...  7.28 us
    pallas_call x1, Pallas kernels, core_grads(): pl.pallas_call(grad_kernel, in_specs=[pl.BlockSpec(memory_space=pltpu.SME...  4.7 us
    unnamed x41, local copies, waits for them, and re-layouts  4.43 us
  transfers between devices with their start and end apart: 49, of which 27 were waited for; matrix products, arithmetic and copies ran while one was open for 1% of the time, Pallas kernels for 17%

profile of v9, /device:TPU:0, one launch (start us, length us, event | category | flops | bytes accessed | tf_op | source)
XLA Modules:
  0.0 195.8 jit_solution(4128432073411419891)
XLA Ops:
  0.7 7.3 %qkv_projection.1 = (bf16[3,256,512]{2,1,0:T(8,128)(2,1)}, bf16[3,16,512]{2,1,0:T(8,128)(2,1)}) custom-call(bf16[256,2048]{1,0:T(8,128)(2,1)} %x_ref.3, f32[1,2048]{1,0:T(1,128)} %bitcast.63, bf16[3,2048,512]{2,1,0:T(8,128)(2,1)} %bitcast.59), custom_call_target="tpu_custom_call" | custom-call | tf_op jit(solution)/shard_map/qkv_projection/pallas_call | solution.py:68
  8.0 2.5 %collective-permute-start = (bf16[3,16,512]{2,1,0:T(8,128)(2,1)}, bf16[3,16,512]{2,1,0:T(8,128)(2,1)S(1)}, u32[]{:S(2)}, u32[]{:S(2)}) collective-permute-start(bf16[3,16,512]{2,1,0:T(8,128)(2,1)} %get-tuple-element.77), channel_id=1, source_target_pairs={{0,4},{4,8},{8,12},{12,16},{16,20},{20,24},{24,28},{1,5},{5,9},{9,... | collective-permute-start | bytes 147464 | tf_op jit(solution)/shard_map/ppermute | solution.py:628
  10.5 1.1 collective-permute-done.rim_ref
  11.6 1.1 copy-done.10
  12.7 3.0 %conv_states.1 = (bf16[3,256,512]{2,1,0:T(8,128)(2,1)S(1)}, bf16[672,128]{1,0:T(8,128)(2,1)S(1)}, bf16[576,128]{1,0:T(8,128)(2,1)S(1)}) custom-call(bf16[3,256,512]{2,1,0:T(8,128)(2,1)S(1)} %copy-done.10, bf16[3,16,512]{2,1,0:T(8,128)(2,1)S(1)} %collective-permute-done.rim_ref, f32[3,4,512]{2,1,0:T(4,128)S(1)} %bitcast.54, f32[4,256]{1,0:T(4,128)S(1)} %bitcast.51, ...), custom_call_target="tpu_custom_call" | custom-call | tf_op jit(solution)/shard_map/conv_states/pallas_call | solution.py:166
  15.7 0.9 copy-done.2
  17.3 6.1 %collective-permute-start.3 = (bf16[672,128]{1,0:T(8,128)(2,1)S(1)}, bf16[672,128]{1,0:T(8,128)(2,1)S(1)}, u32[]{:S(2)}, u32[]{:S(2)}) collective-permute-start(bf16[672,128]{1,0:T(8,128)(2,1)S(1)} %get-tuple-element.80), channel_id=1, source_target_pairs={{0,24},{4,28},{8,16},{12,20},{16,8},{20,12},{24,0},{28,4},{1,25},{... | collective-permute-start | bytes 516104 | tf_op jit(solution)/shard_map/ppermute | solution.py:456
  23.9 0.9 collective-permute-start.1
  24.9 3.8 %collective-permute-done.3 = bf16[672,128]{1,0:T(8,128)(2,1)S(1)} collective-permute-done((bf16[672,128]{1,0:T(8,128)(2,1)S(1)}, bf16[672,128]{1,0:T(8,128)(2,1)S(1)}, u32[]{:S(2)}, u32[]{:S(2)}) %collective-permute-start.3) | collective-permute-done | bytes 172064 | tf_op jit(solution)/shard_map/ppermute | solution.py:456
  28.7 2.5 %collective-permute-done.2 = bf16[672,128]{1,0:T(8,128)(2,1)S(1)} collective-permute-done((bf16[672,128]{1,0:T(8,128)(2,1)S(1)}, bf16[672,128]{1,0:T(8,128)(2,1)S(1)}, u32[]{:S(2)}, u32[]{:S(2)}) %collective-permute-start.2) | collective-permute-done | bytes 172064 | tf_op jit(solution)/shard_map/ppermute | solution.py:456
  31.5 1.1 stage_weights.2.me_ref.where_ref
  32.7 0.9 collective-permute-done.4.far_ref.far_routes.fwd_far
  33.6 3.7 %core_out.1 = (bf16[64,2048]{1,0:T(8,128)(2,1)S(1)}, bf16[64,2048]{1,0:T(8,128)(2,1)S(1)}, bf16[64,2048]{1,0:T(8,128)(2,1)S(1)}, bf16[64,2048]{1,0:T(8,128)(2,1)S(1)}) custom-call(s32[3]{0:T(128)S(1)} %stage_weights.2.me_ref.where_ref, bf16[3,256,512]{2,1,0:T(8,128)(2,1)S(1)} %copy-done.3, f32[4,256]{1,0:T(4,128)S(1)} %bitcast.52, f32[1,512]{1,0:T(1,128)S(1)} %bitcast.58, ...), custom_call_target="tpu_custom_call" | custom-call | tf_op jit(solution)/shard_map/core_out/pallas_call | solution.py:233
  37.3 1.7 collective-permute-start.8
  39.0 1.6 collective-permute-start.5
  40.5 2.6 %collective-permute-start.6 = (bf16[64,2048]{1,0:T(8,128)(2,1)S(1)}, bf16[64,2048]{1,0:T(8,128)(2,1)S(1)}, u32[]{:S(2)}, u32[]{:S(2)}) collective-permute-start(bf16[64,2048]{1,0:T(8,128)(2,1)S(1)} %get-tuple-element.83), channel_id=1, source_target_pairs={{0,2},{1,3},{2,0},{3,1},{4,6},{5,7},{6,4},{7,5},{8,10},{9,11},{10,... | collective-permute-start | bytes 786440 | tf_op jit(solution)/shard_map/ppermute | solution.py:462
  43.4 1.6 copy-done.6
  44.9 1.1 stage_weights.3.where_ref.me_ref
  46.1 5.9 %collective-permute-done.5.refs_1_ = bf16[64,2048]{1,0:T(8,128)(2,1)S(1)} collective-permute-done((bf16[64,2048]{1,0:T(8,128)(2,1)S(1)}, bf16[64,2048]{1,0:T(8,128)(2,1)S(1)}, u32[]{:S(2)}, u32[]{:S(2)}) %collective-permute-start.5) | collective-permute-done | bytes 262176 | tf_op jit(solution)/shard_map/ppermute | solution.py:462
  52.0 9.9 %collective-permute-done.6.refs_2_ = bf16[64,2048]{1,0:T(8,128)(2,1)S(1)} collective-permute-done((bf16[64,2048]{1,0:T(8,128)(2,1)S(1)}, bf16[64,2048]{1,0:T(8,128)(2,1)S(1)}, u32[]{:S(2)}, u32[]{:S(2)}) %collective-permute-start.6) | collective-permute-done | bytes 262176 | tf_op jit(solution)/shard_map/ppermute | solution.py:462
  61.9 0.9 moe_norm.1
  62.8 1.0 collective-permute-start.12
  63.7 2.5 %collective-permute-start.11 = (bf16[32,2048]{1,0:T(8,128)(2,1)S(1)}, bf16[32,2048]{1,0:T(8,128)(2,1)S(1)}, u32[]{:S(2)}, u32[]{:S(2)}) collective-permute-start(bf16[32,2048]{1,0:T(8,128)(2,1)S(1)} %get-tuple-element.96.refs_0_), channel_id=1, source_target_pairs={{0,3},{1,2},{2,1},{3,0},{4,7},{5,6},{6,5},{7,4},{8,11},{9,10},{10,... | collective-permute-start | bytes 393224 | tf_op jit(solution)/shard_map/ppermute | solution.py:462
  66.2 5.2 %collective-permute-start.10 = (bf16[32,2048]{1,0:T(8,128)(2,1)S(1)}, bf16[32,2048]{1,0:T(8,128)(2,1)S(1)}, u32[]{:S(2)}, u32[]{:S(2)}) collective-permute-start(bf16[32,2048]{1,0:T(8,128)(2,1)S(1)} %get-tuple-element.96.refs_0_), channel_id=1, source_target_pairs={{0,2},{1,3},{2,0},{3,1},{4,6},{5,7},{6,4},{7,5},{8,10},{9,11},{10,... | collective-permute-start | bytes 393224 | tf_op jit(solution)/shard_map/ppermute | solution.py:462
  71.7 7.3 %collective-permute-done.10.refs_2_ = bf16[32,2048]{1,0:T(8,128)(2,1)S(1)} collective-permute-done((bf16[32,2048]{1,0:T(8,128)(2,1)S(1)}, bf16[32,2048]{1,0:T(8,128)(2,1)S(1)}, u32[]{:S(2)}, u32[]{:S(2)}) %collective-permute-start.10) | collective-permute-done | bytes 131104 | tf_op jit(solution)/shard_map/ppermute | solution.py:462
  79.6 1.2 collective-permute-start.15
  81.2 2.6 %collective-permute-start.18 = (bf16[32,2048]{1,0:T(8,128)(2,1)S(1)}, bf16[32,2048]{1,0:T(8,128)(2,1)S(1)}, u32[]{:S(2)}, u32[]{:S(2)}) collective-permute-start(bf16[32,2048]{1,0:T(8,128)(2,1)S(1)} %get-tuple-element.101.refs_0_), channel_id=1, source_target_pairs={{0,3},{1,2},{2,1},{3,0},{4,7},{5,6},{6,5},{7,4},{8,11},{9,10},{10,... | collective-permute-start | bytes 393224 | tf_op jit(solution)/shard_map/ppermute | solution.py:462
  83.9 5.6 %collective-permute-done.18.refs_3_ = bf16[32,2048]{1,0:T(8,128)(2,1)S(1)} collective-permute-done((bf16[32,2048]{1,0:T(8,128)(2,1)S(1)}, bf16[32,2048]{1,0:T(8,128)(2,1)S(1)}, u32[]{:S(2)}, u32[]{:S(2)}) %collective-permute-start.18) | collective-permute-done | bytes 131104 | tf_op jit(solution)/shard_map/ppermute | solution.py:462
  89.4 2.5 %collective-permute-start.16 = (bf16[32,2048]{1,0:T(8,128)(2,1)S(1)}, bf16[32,2048]{1,0:T(8,128)(2,1)S(1)}, u32[]{:S(2)}, u32[]{:S(2)}) collective-permute-start(bf16[32,2048]{1,0:T(8,128)(2,1)S(1)} %get-tuple-element.101.refs_0_), channel_id=1, source_target_pairs={{0,1},{1,0},{2,3},{3,2},{4,5},{5,4},{6,7},{7,6},{8,9},{9,8},{10,11... | collective-permute-start | bytes 393224 | tf_op jit(solution)/shard_map/ppermute | solution.py:462
  92.0 2.3 %collective-permute-done.17.refs_2_ = bf16[32,2048]{1,0:T(8,128)(2,1)S(1)} collective-permute-done((bf16[32,2048]{1,0:T(8,128)(2,1)S(1)}, bf16[32,2048]{1,0:T(8,128)(2,1)S(1)}, u32[]{:S(2)}, u32[]{:S(2)}) %collective-permute-start.17) | collective-permute-done | bytes 131104 | tf_op jit(solution)/shard_map/ppermute | solution.py:462
  94.3 1.4 collective-permute-done.16.refs_1_
  96.3 1.8 collective-permute-start.19
  98.1 0.8 collective-permute-start.20
  99.4 3.9 %collective-permute-done.19 = bf16[64,2048]{1,0:T(8,128)(2,1)S(1)} collective-permute-done((bf16[64,2048]{1,0:T(8,128)(2,1)S(1)}, bf16[64,2048]{1,0:T(8,128)(2,1)S(1)}, u32[]{:S(2)}, u32[]{:S(2)}) %collective-permute-start.19) | collective-permute-done | bytes 262176 | tf_op jit(solution)/shard_map/ppermute | solution.py:456
  103.3 1.4 collective-permute-done.20
  105.8 1.4 collective-permute-start.25
  107.2 11.9 %expert_pieces.3 = (bf16[4,128,2048]{2,1,0:T(8,128)(2,1)S(1)}, bf16[4,128,2048]{2,1,0:T(8,128)(2,1)S(1)}) custom-call(s32[3]{0:T(128)S(1)} %stage_weights.3.where_ref.me_ref, bf16[4,672,128]{2,1,0:T(8,128)(2,1)S(1)} %pad_maximum_fusion.near_ref.near_routes.fwd_near, bf16[4,672,128]{2,1,0:T(8,128)(2,1)S(1)} %collective-permute-done.4.far_ref.far_routes.fwd_far, ...), custom_call_target="tpu_custom_call" | custom-call | flops 6442450944 | bytes 8388608 | tf_op jit(solution)/shard_map/expert_pieces/pallas_call | solution.py:429
  120.1 1.4 collective-permute-start.36
  121.5 1.1 collective-permute-start.35
  122.5 1.8 collective-permute-done.30.refs_2_
  125.5 3.2 %collective-permute-done.36 = bf16[64,2048]{1,0:T(8,128)(2,1)S(1)} collective-permute-done((bf16[64,2048]{1,0:T(8,128)(2,1)S(1)}, bf16[64,2048]{1,0:T(8,128)(2,1)S(1)}, u32[]{:S(2)}, u32[]{:S(2)}) %collective-permute-start.36) | collective-permute-done | bytes 262176 | tf_op jit(solution)/shard_map/ppermute | solution.py:456
  128.7 1.2 collective-permute-done.35
  130.7 1.6 collective-permute-start.32
  132.3 6.1 %expert_pieces.4 = bf16[4,128,2048]{2,1,0:T(8,128)(2,1)S(1)} custom-call(s32[3]{0:T(128)S(1)} %stage_weights.3.where_ref.me_ref, bf16[4,672,128]{2,1,0:T(8,128)(2,1)S(1)} %pad_maximum_fusion.near_ref.near_routes.fwd_near, bf16[4,672,128]{2,1,0:T(8,128)(2,1)S(1)} %collective-permute-done.4.far_ref.far_routes.fwd_far, bf16[1,2048,512]{2,1,0:T(8,128)(2,1)S(1)} %copy-done.4, ...), custom_call_target="tpu_custom_call" | custom-call | flops 3221225472 | bytes 4194304 | tf_op jit(solution)/shard_map/expert_pieces/pallas_call | solution.py:429
  138.4 6.0 %collective-permute-done.31.refs_0_ = bf16[128,2048]{1,0:T(8,128)(2,1)S(1)} collective-permute-done((bf16[128,2048]{1,0:T(8,128)(2,1)S(1)}, bf16[128,2048]{1,0:T(8,128)(2,1)S(1)}, u32[]{:S(2)}, u32[]{:S(2)}) %collective-permute-start.31) | collective-permute-done | bytes 524320 | tf_op jit(solution)/shard_map/ppermute | solution.py:456
  145.0 1.5 collective-permute-start.34
  146.5 1.0 collective-permute-start.33
  147.5 6.1 %expert_pieces.5.near_ref = bf16[4,128,2048]{2,1,0:T(8,128)(2,1)S(1)} custom-call(s32[3]{0:T(128)S(1)} %stage_weights.3.where_ref.me_ref, bf16[4,672,128]{2,1,0:T(8,128)(2,1)S(1)} %pad_maximum_fusion.near_ref.near_routes.fwd_near, bf16[4,672,128]{2,1,0:T(8,128)(2,1)S(1)} %collective-permute-done.4.far_ref.far_routes.fwd_far, ...), custom_call_target="tpu_custom_call" | custom-call | flops 3221225472 | bytes 4194304 | tf_op jit(solution)/shard_map/expert_pieces/pallas_call | solution.py:429
  153.8 1.2 collective-permute-done.33.refs_2_
  156.1 1.7 collective-permute-start.43
  157.7 1.0 sum_terms.2
  158.7 10.0 %collective-permute-done.42.refs_0_ = bf16[128,2048]{1,0:T(8,128)(2,1)S(1)} collective-permute-done((bf16[128,2048]{1,0:T(8,128)(2,1)S(1)}, bf16[128,2048]{1,0:T(8,128)(2,1)S(1)}, u32[]{:S(2)}, u32[]{:S(2)}) %collective-permute-start.42) | collective-permute-done | bytes 524320 | tf_op jit(solution)/shard_map/ppermute | solution.py:456
  169.4 1.5 collective-permute-start.45
  170.8 1.0 collective-permute-start.44
  172.4 2.3 %collective-permute-start.40 = (bf16[128,512]{1,0:T(8,128)(2,1)S(1)}, bf16[128,512]{1,0:T(8,128)(2,1)S(1)}, u32[]{:S(2)}, u32[]{:S(2)}) collective-permute-start(bf16[128,512]{1,0:T(8,128)(2,1)S(1)} %get-tuple-element.136), channel_id=1, source_target_pairs={{0,2},{1,3},{2,0},{3,1},{4,6},{5,7},{6,4},{7,5},{8,10},{9,11},{10,... | collective-permute-start | bytes 393224 | tf_op jit(solution)/shard_map/ppermute | solution.py:462
  174.7 1.5 collective-permute-start.41
  176.2 1.0 collective-permute-done.44.refs_2_
  177.2 1.0 sum_terms.3
  178.2 0.8 collective-permute-start.46
  179.0 2.2 %collective-permute-start.47 = (bf16[128,512]{1,0:T(8,128)(2,1)S(1)}, bf16[128,512]{1,0:T(8,128)(2,1)S(1)}, u32[]{:S(2)}, u32[]{:S(2)}) collective-permute-start(bf16[128,512]{1,0:T(8,128)(2,1)S(1)} %get-tuple-element.143), channel_id=1, source_target_pairs={{0,2},{1,3},{2,0},{3,1},{4,6},{5,7},{6,4},{7,5},{8,10},{9,11},{10,... | collective-permute-start | bytes 393224 | tf_op jit(solution)/shard_map/ppermute | solution.py:462
  181.2 1.5 collective-permute-start.48
  182.7 4.7 %core_grads.1 = (bf16[256,512]{1,0:T(8,128)(2,1)}, bf16[256,512]{1,0:T(8,128)(2,1)}, bf16[256,512]{1,0:T(8,128)(2,1)}) custom-call(s32[3]{0:T(128)S(1)} %stage_weights.3.where_ref.me_ref, bf16[3,256,512]{2,1,0:T(8,128)(2,1)S(1)} %copy-done.3, bf16[256,512]{1,0:T(8,128)(2,1)S(1)} %copy-done.9, f32[4,256]{1,0:T(4,128)S(1)} %bitcast.53, ...), custom_call_target="tpu_custom_call" | custom-call | tf_op jit(solution)/shard_map/core_grads/pallas_call | solution.py:278
  187.4 7.0 %collective-permute-done.47.refs_6_ = bf16[128,512]{1,0:T(8,128)(2,1)S(1)} collective-permute-done((bf16[128,512]{1,0:T(8,128)(2,1)S(1)}, bf16[128,512]{1,0:T(8,128)(2,1)S(1)}, u32[]{:S(2)}, u32[]{:S(2)}) %collective-permute-start.47) | collective-permute-done | bytes 131104 | tf_op jit(solution)/shard_map/ppermute | solution.py:462
  194.3 1.4 layer_out.1
  (108 shorter events, 11.3 us)
Async XLA Ops:
  0.6 10.9 %copy-start.8 = (bf16[256,512]{1,0:T(8,128)(2,1)S(1)}, bf16[256,512]{1,0:T(8,128)(2,1)}, u32[]{:S(2)}) copy-start(bf16[256,512]{1,0:T(8,128)(2,1)} %cot_ref.3) | copy-start | bytes 786436
  0.6 10.9 %copy-start.13 = (f32[256,4]{0,1:T(4,128)S(1)}, f32[256,4]{0,1:T(4,128)}, u32[]{:S(2)}) copy-start(f32[256,4]{0,1:T(4,128)} %param.18) | copy-start | bytes 12292
  0.7 10.9 %copy-start.14 = (f32[4,3,512]{2,0,1:T(4,128)S(1)}, f32[4,3,512]{2,0,1:T(4,128)}, u32[]{:S(2)}) copy-start(f32[4,3,512]{2,0,1:T(4,128)} %param.17) | copy-start | bytes 73732
  0.7 10.9 %copy-start.15 = (s32[256,8]{0,1:T(8,128)S(1)}, s32[256,8]{0,1:T(8,128)}, u32[]{:S(2)}) copy-start(s32[256,8]{0,1:T(8,128)} %param.22) | copy-start | bytes 24580
  0.7 10.9 %copy-start.16 = (f32[256,8]{0,1:T(8,128)S(1)}, f32[256,8]{0,1:T(8,128)}, u32[]{:S(2)}) copy-start(f32[256,8]{0,1:T(8,128)} %param.23) | copy-start | bytes 24580
  8.0 23.6 %copy-start.1 = (bf16[512,2048]{1,0:T(8,128)(2,1)S(1)}, bf16[512,2048]{1,0:T(8,128)(2,1)}, u32[]{:S(2)}) copy-start(bf16[512,2048]{1,0:T(8,128)(2,1)} %w_ref.1) | copy-start | bytes 6291460
  8.0 3.6 %collective-permute-start = (bf16[3,16,512]{2,1,0:T(8,128)(2,1)}, bf16[3,16,512]{2,1,0:T(8,128)(2,1)S(1)}, u32[]{:S(2)}, u32[]{:S(2)}) collective-permute-start(bf16[3,16,512]{2,1,0:T(8,128)(2,1)} %get-tuple-element.77), channel_id=1, source_target_pairs={{0,4},{4,8},{8,12},{12,16},{16,20},{20,24},{24,28},{1,5},{5,9},{9,... | collective-permute-start | bytes 147464 | tf_op jit(solution)/shard_map/ppermute | solution.py:628
  12.7 20.9 %copy-start.18 = (f32[512]{0:T(512)S(1)}, f32[512]{0:T(512)}, u32[]{:S(2)}) copy-start(f32[512]{0:T(512)} %param.19) | copy-start | bytes 6148
  17.3 11.4 %collective-permute-start.3 = (bf16[672,128]{1,0:T(8,128)(2,1)S(1)}, bf16[672,128]{1,0:T(8,128)(2,1)S(1)}, u32[]{:S(2)}, u32[]{:S(2)}) collective-permute-start(bf16[672,128]{1,0:T(8,128)(2,1)S(1)} %get-tuple-element.80), channel_id=1, source_target_pairs={{0,24},{4,28},{8,16},{12,20},{16,8},{20,12},{24,0},{28,4},{1,25},{... | collective-permute-start | bytes 516104 | tf_op jit(solution)/shard_map/ppermute | solution.py:456
  23.4 7.8 %collective-permute-start.2 = (bf16[672,128]{1,0:T(8,128)(2,1)S(1)}, bf16[672,128]{1,0:T(8,128)(2,1)S(1)}, u32[]{:S(2)}, u32[]{:S(2)}) collective-permute-start(bf16[672,128]{1,0:T(8,128)(2,1)S(1)} %get-tuple-element.80), channel_id=1, source_target_pairs={{0,16},{4,20},{8,24},{12,28},{16,0},{20,4},{24,8},{28,12},{1,17},{... | collective-permute-start | bytes 516104 | tf_op jit(solution)/shard_map/ppermute | solution.py:456
  23.9 7.3 %collective-permute-start.1 = (bf16[672,128]{1,0:T(8,128)(2,1)S(1)}, bf16[672,128]{1,0:T(8,128)(2,1)S(1)}, u32[]{:S(2)}, u32[]{:S(2)}) collective-permute-start(bf16[672,128]{1,0:T(8,128)(2,1)S(1)} %get-tuple-element.80), channel_id=1, source_target_pairs={{0,8},{4,12},{8,0},{12,4},{16,24},{20,28},{24,16},{28,20},{1,9},{5... | collective-permute-start | bytes 516104 | tf_op jit(solution)/shard_map/ppermute | solution.py:456
  31.4 2.2 %collective-permute-start.4 = (bf16[4,672,128]{2,1,0:T(8,128)(2,1)S(1)}, bf16[4,672,128]{2,1,0:T(8,128)(2,1)S(1)}, u32[]{:S(2)}, u32[]{:S(2)}) collective-permute-start(bf16[4,672,128]{2,1,0:T(8,128)(2,1)S(1)} %pad_maximum_fusion.near_ref.near_routes.fwd_near), channel_id=1, source_target_pairs={{0,4},{4,0},{8,12},{12,8},{16,20},{20,16},{24,28},{28,24},{1,5},{5... | collective-permute-start | bytes 2064392 | tf_op jit(solution)/shard_map/ppermute | solution.py:456
  31.5 2.1 %copy-start.3 = (bf16[3,256,512]{2,1,0:T(8,128)(2,1)S(1)}, bf16[3,256,512]{2,1,0:T(8,128)(2,1)}, u32[]{:S(2)}) copy-start(bf16[3,256,512]{2,1,0:T(8,128)(2,1)} %copy-done.2) | copy-start | bytes 2359300
  31.5 5.7 %copy-start.12 = (bf16[576,128]{1,0:T(8,128)(2,1)S(1)}, bf16[576,128]{1,0:T(8,128)(2,1)}, u32[]{:S(2)}) copy-start(bf16[576,128]{1,0:T(8,128)(2,1)} %copy-done.11) | copy-start | bytes 442372
  33.6 9.8 %copy-start.4 = (bf16[1,2048,512]{2,1,0:T(8,128)(2,1)S(1)}, bf16[1,2048,512]{2,1,0:T(8,128)(2,1)}, u32[]{:S(2)}) copy-start(bf16[1,2048,512]{2,1,0:T(8,128)(2,1)} %gate_ref.5) | copy-start | bytes 6291460
  33.6 9.8 %copy-start.5 = (bf16[1,2048,512]{2,1,0:T(8,128)(2,1)S(1)}, bf16[1,2048,512]{2,1,0:T(8,128)(2,1)}, u32[]{:S(2)}) copy-start(bf16[1,2048,512]{2,1,0:T(8,128)(2,1)} %up_ref.5) | copy-start | bytes 6291460
  37.3 24.6 %copy-start = (bf16[256,2048]{1,0:T(8,128)(2,1)S(1)}, bf16[256,2048]{1,0:T(8,128)(2,1)}, u32[]{:S(2)}) copy-start(bf16[256,2048]{1,0:T(8,128)(2,1)} %x_ref.3) | copy-start | bytes 3145732
  37.3 8.8 %collective-permute-start.8 = (bf16[1,576,128]{2,1,0:T(8,128)(2,1)S(1)}, bf16[1,576,128]{2,1,0:T(8,128)(2,1)S(1)}, u32[]{:S(2)}, u32[]{:S(2)}) collective-permute-start(bf16[1,576,128]{2,1,0:T(8,128)(2,1)S(1)} %bitcast.49), channel_id=1, source_target_pairs={{0,8},{4,12},{8,0},{12,4},{16,24},{20,28},{24,16},{28,20},{1,9},{5... | collective-permute-start | bytes 442376 | tf_op jit(solution)/shard_map/ppermute | solution.py:456
  39.0 13.1 %collective-permute-start.5 = (bf16[64,2048]{1,0:T(8,128)(2,1)S(1)}, bf16[64,2048]{1,0:T(8,128)(2,1)S(1)}, u32[]{:S(2)}, u32[]{:S(2)}) collective-permute-start(bf16[64,2048]{1,0:T(8,128)(2,1)S(1)} %get-tuple-element.82), channel_id=1, source_target_pairs={{0,1},{1,0},{2,3},{3,2},{4,5},{5,4},{6,7},{7,6},{8,9},{9,8},{10,11... | collective-permute-start | bytes 786440 | tf_op jit(solution)/shard_map/ppermute | solution.py:462
  40.5 21.4 %collective-permute-start.6 = (bf16[64,2048]{1,0:T(8,128)(2,1)S(1)}, bf16[64,2048]{1,0:T(8,128)(2,1)S(1)}, u32[]{:S(2)}, u32[]{:S(2)}) collective-permute-start(bf16[64,2048]{1,0:T(8,128)(2,1)S(1)} %get-tuple-element.83), channel_id=1, source_target_pairs={{0,2},{1,3},{2,0},{3,1},{4,6},{5,7},{6,4},{7,5},{8,10},{9,11},{10,... | collective-permute-start | bytes 786440 | tf_op jit(solution)/shard_map/ppermute | solution.py:462
  43.1 18.8 %collective-permute-start.7 = (bf16[64,2048]{1,0:T(8,128)(2,1)S(1)}, bf16[64,2048]{1,0:T(8,128)(2,1)S(1)}, u32[]{:S(2)}, u32[]{:S(2)}) collective-permute-start(bf16[64,2048]{1,0:T(8,128)(2,1)S(1)} %get-tuple-element.84), channel_id=1, source_target_pairs={{0,3},{1,2},{2,1},{3,0},{4,7},{5,6},{6,5},{7,4},{8,11},{9,10},{10,... | collective-permute-start | bytes 786440 | tf_op jit(solution)/shard_map/ppermute | solution.py:462
  44.9 17.0 %copy-start.17 = (f32[2048]{0:T(1024)S(1)}, f32[2048]{0:T(1024)}, u32[]{:S(2)}) copy-start(f32[2048]{0:T(1024)} %param.21) | copy-start | bytes 24580
  62.8 8.8 %collective-permute-start.12 = (bf16[2,576,128]{2,1,0:T(8,128)(2,1)S(1)}, bf16[2,576,128]{2,1,0:T(8,128)(2,1)S(1)}, u32[]{:S(2)}, u32[]{:S(2)}) collective-permute-start(bf16[2,576,128]{2,1,0:T(8,128)(2,1)S(1)} %pad_maximum_fusion.5), channel_id=1, source_target_pairs={{0,16},{4,20},{8,24},{12,28},{16,0},{20,4},{24,8},{28,12},{1,17},{... | collective-permute-start | bytes 884744 | tf_op jit(solution)/shard_map/ppermute | solution.py:456
  63.7 7.9 %collective-permute-start.11 = (bf16[32,2048]{1,0:T(8,128)(2,1)S(1)}, bf16[32,2048]{1,0:T(8,128)(2,1)S(1)}, u32[]{:S(2)}, u32[]{:S(2)}) collective-permute-start(bf16[32,2048]{1,0:T(8,128)(2,1)S(1)} %get-tuple-element.96.refs_0_), channel_id=1, source_target_pairs={{0,3},{1,2},{2,1},{3,0},{4,7},{5,6},{6,5},{7,4},{8,11},{9,10},{10,... | collective-permute-start | bytes 393224 | tf_op jit(solution)/shard_map/ppermute | solution.py:462
  66.2 12.7 %collective-permute-start.10 = (bf16[32,2048]{1,0:T(8,128)(2,1)S(1)}, bf16[32,2048]{1,0:T(8,128)(2,1)S(1)}, u32[]{:S(2)}, u32[]{:S(2)}) collective-permute-start(bf16[32,2048]{1,0:T(8,128)(2,1)S(1)} %get-tuple-element.96.refs_0_), channel_id=1, source_target_pairs={{0,2},{1,3},{2,0},{3,1},{4,6},{5,7},{6,4},{7,5},{8,10},{9,11},{10,... | collective-permute-start | bytes 393224 | tf_op jit(solution)/shard_map/ppermute | solution.py:462
  71.5 7.5 %collective-permute-start.9 = (bf16[32,2048]{1,0:T(8,128)(2,1)S(1)}, bf16[32,2048]{1,0:T(8,128)(2,1)S(1)}, u32[]{:S(2)}, u32[]{:S(2)}) collective-permute-start(bf16[32,2048]{1,0:T(8,128)(2,1)S(1)} %get-tuple-element.96.refs_0_), channel_id=1, source_target_pairs={{0,1},{1,0},{2,3},{3,2},{4,5},{5,4},{6,7},{7,6},{8,9},{9,8},{10,11... | collective-permute-start | bytes 393224 | tf_op jit(solution)/shard_map/ppermute | solution.py:462
  79.5 16.2 %collective-permute-start.13 = (bf16[128,2048]{1,0:T(8,128)(2,1)S(1)}, bf16[128,2048]{1,0:T(8,128)(2,1)S(1)}, u32[]{:S(2)}, u32[]{:S(2)}) collective-permute-start(bf16[128,2048]{1,0:T(8,128)(2,1)S(1)} %join_rows.2.refs_0_), channel_id=1, source_target_pairs={{0,4},{4,0},{8,12},{12,8},{16,20},{20,16},{24,28},{28,24},{1,5},{5... | collective-permute-start | bytes 1572872 | tf_op jit(solution)/shard_map/ppermute | solution.py:456
  79.6 16.7 %collective-permute-start.15 = (bf16[128,2048]{1,0:T(8,128)(2,1)S(1)}, bf16[128,2048]{1,0:T(8,128)(2,1)S(1)}, u32[]{:S(2)}, u32[]{:S(2)}) collective-permute-start(bf16[128,2048]{1,0:T(8,128)(2,1)S(1)} %join_rows.2.refs_0_), channel_id=1, source_target_pairs={{0,16},{4,20},{8,24},{12,28},{16,0},{20,4},{24,8},{28,12},{1,17},{... | collective-permute-start | bytes 1572872 | tf_op jit(solution)/shard_map/ppermute | solution.py:456
  80.8 15.5 %collective-permute-start.14 = (bf16[128,2048]{1,0:T(8,128)(2,1)S(1)}, bf16[128,2048]{1,0:T(8,128)(2,1)S(1)}, u32[]{:S(2)}, u32[]{:S(2)}) collective-permute-start(bf16[128,2048]{1,0:T(8,128)(2,1)S(1)} %join_rows.2.refs_0_), channel_id=1, source_target_pairs={{0,8},{4,12},{8,0},{12,4},{16,24},{20,28},{24,16},{28,20},{1,9},{5... | collective-permute-start | bytes 1572872 | tf_op jit(solution)/shard_map/ppermute | solution.py:456
  81.2 8.2 %collective-permute-start.18 = (bf16[32,2048]{1,0:T(8,128)(2,1)S(1)}, bf16[32,2048]{1,0:T(8,128)(2,1)S(1)}, u32[]{:S(2)}, u32[]{:S(2)}) collective-permute-start(bf16[32,2048]{1,0:T(8,128)(2,1)S(1)} %get-tuple-element.101.refs_0_), channel_id=1, source_target_pairs={{0,3},{1,2},{2,1},{3,0},{4,7},{5,6},{6,5},{7,4},{8,11},{9,10},{10,... | collective-permute-start | bytes 393224 | tf_op jit(solution)/shard_map/ppermute | solution.py:462
  83.9 10.4 %collective-permute-start.17 = (bf16[32,2048]{1,0:T(8,128)(2,1)S(1)}, bf16[32,2048]{1,0:T(8,128)(2,1)S(1)}, u32[]{:S(2)}, u32[]{:S(2)}) collective-permute-start(bf16[32,2048]{1,0:T(8,128)(2,1)S(1)} %get-tuple-element.101.refs_0_), channel_id=1, source_target_pairs={{0,2},{1,3},{2,0},{3,1},{4,6},{5,7},{6,4},{7,5},{8,10},{9,11},{10,... | collective-permute-start | bytes 393224 | tf_op jit(solution)/shard_map/ppermute | solution.py:462
  89.4 6.3 %collective-permute-start.16 = (bf16[32,2048]{1,0:T(8,128)(2,1)S(1)}, bf16[32,2048]{1,0:T(8,128)(2,1)S(1)}, u32[]{:S(2)}, u32[]{:S(2)}) collective-permute-start(bf16[32,2048]{1,0:T(8,128)(2,1)S(1)} %get-tuple-element.101.refs_0_), channel_id=1, source_target_pairs={{0,1},{1,0},{2,3},{3,2},{4,5},{5,4},{6,7},{7,6},{8,9},{9,8},{10,11... | collective-permute-start | bytes 393224 | tf_op jit(solution)/shard_map/ppermute | solution.py:462
  96.3 7.0 %collective-permute-start.19 = (bf16[64,2048]{1,0:T(8,128)(2,1)S(1)}, bf16[64,2048]{1,0:T(8,128)(2,1)S(1)}, u32[]{:S(2)}, u32[]{:S(2)}) collective-permute-start(bf16[64,2048]{1,0:T(8,128)(2,1)S(1)} %slice.96), channel_id=1, source_target_pairs={{0,16},{4,20},{8,24},{12,28},{16,0},{20,4},{24,8},{28,12},{1,17},{... | collective-permute-start | bytes 786440 | tf_op jit(solution)/shard_map/ppermute | solution.py:456
  98.1 6.6 %collective-permute-start.20 = (bf16[64,2048]{1,0:T(8,128)(2,1)S(1)}, bf16[64,2048]{1,0:T(8,128)(2,1)S(1)}, u32[]{:S(2)}, u32[]{:S(2)}) collective-permute-start(bf16[64,2048]{1,0:T(8,128)(2,1)S(1)} %slice.97), channel_id=1, source_target_pairs={{0,8},{4,12},{8,0},{12,4},{16,24},{20,28},{24,16},{28,20},{1,9},{5... | collective-permute-start | bytes 786440 | tf_op jit(solution)/shard_map/ppermute | solution.py:456
  98.9 6.8 %collective-permute-start.21 = (bf16[128,2048]{1,0:T(8,128)(2,1)S(1)}, bf16[128,2048]{1,0:T(8,128)(2,1)S(1)}, u32[]{:S(2)}, u32[]{:S(2)}) collective-permute-start(bf16[128,2048]{1,0:T(8,128)(2,1)S(1)} %collective-permute-done.14.refs_1_), channel_id=1, source_target_pairs={{0,4},{4,0},{8,12},{12,8},{16,20},{20,16},{24,28},{28,24},{1,5},{5... | collective-permute-start | bytes 1572872 | tf_op jit(solution)/shard_map/ppermute | solution.py:456
  98.9 8.3 %collective-permute-start.22 = (bf16[128,2048]{1,0:T(8,128)(2,1)S(1)}, bf16[128,2048]{1,0:T(8,128)(2,1)S(1)}, u32[]{:S(2)}, u32[]{:S(2)}) collective-permute-start(bf16[128,2048]{1,0:T(8,128)(2,1)S(1)} %collective-permute-done.15.refs_2_), channel_id=1, source_target_pairs={{0,4},{4,0},{8,12},{12,8},{16,20},{20,16},{24,28},{28,24},{1,5},{5... | collective-permute-start | bytes 1572872 | tf_op jit(solution)/shard_map/ppermute | solution.py:456
  104.7 2.5 %collective-permute-start.23 = (bf16[128,2048]{1,0:T(8,128)(2,1)S(1)}, bf16[128,2048]{1,0:T(8,128)(2,1)S(1)}, u32[]{:S(2)}, u32[]{:S(2)}) collective-permute-start(bf16[128,2048]{1,0:T(8,128)(2,1)S(1)} %constant_dynamic-update-slice_fusion.2.refs_3_), channel_id=1, source_target_pairs={{0,4},{4,0},{8,12},{12,8},{16,20},{20,16},{24,28},{28,24},{1,5},{5... | collective-permute-start | bytes 1572872 | tf_op jit(solution)/shard_map/ppermute | solution.py:456
  104.8 14.3 %collective-permute-start.27 = (bf16[4,576,128]{2,1,0:T(8,128)(2,1)S(1)}, bf16[4,576,128]{2,1,0:T(8,128)(2,1)S(1)}, u32[]{:S(2)}, u32[]{:S(2)}) collective-permute-start(bf16[4,576,128]{2,1,0:T(8,128)(2,1)S(1)} %constant_dynamic-update-slice_fusion.bwd_near), channel_id=1, source_target_pairs={{0,4},{4,0},{8,12},{12,8},{16,20},{20,16},{24,28},{28,24},{1,5},{5... | collective-permute-start | bytes 1769480 | tf_op jit(solution)/shard_map/ppermute | solution.py:456
  105.3 13.9 %collective-permute-start.26 = (bf16[128,2048]{1,0:T(8,128)(2,1)S(1)}, bf16[128,2048]{1,0:T(8,128)(2,1)S(1)}, u32[]{:S(2)}, u32[]{:S(2)}) collective-permute-start(bf16[128,2048]{1,0:T(8,128)(2,1)S(1)} %join_rows.3.refs_0_), channel_id=1, source_target_pairs={{0,16},{4,20},{8,24},{12,28},{16,0},{20,4},{24,8},{28,12},{1,17},{... | collective-permute-start | bytes 1572872 | tf_op jit(solution)/shard_map/ppermute | solution.py:456
  105.8 13.6 %collective-permute-start.25 = (bf16[128,2048]{1,0:T(8,128)(2,1)S(1)}, bf16[128,2048]{1,0:T(8,128)(2,1)S(1)}, u32[]{:S(2)}, u32[]{:S(2)}) collective-permute-start(bf16[128,2048]{1,0:T(8,128)(2,1)S(1)} %join_rows.3.refs_0_), channel_id=1, source_target_pairs={{0,8},{4,12},{8,0},{12,4},{16,24},{20,28},{24,16},{28,20},{1,9},{5... | collective-permute-start | bytes 1572872 | tf_op jit(solution)/shard_map/ppermute | solution.py:456
  107.2 12.2 %collective-permute-start.24 = (bf16[128,2048]{1,0:T(8,128)(2,1)S(1)}, bf16[128,2048]{1,0:T(8,128)(2,1)S(1)}, u32[]{:S(2)}, u32[]{:S(2)}) collective-permute-start(bf16[128,2048]{1,0:T(8,128)(2,1)S(1)} %join_rows.3.refs_0_), channel_id=1, source_target_pairs={{0,4},{4,0},{8,12},{12,8},{16,20},{20,16},{24,28},{28,24},{1,5},{5... | collective-permute-start | bytes 1572872 | tf_op jit(solution)/shard_map/ppermute | solution.py:456
  119.4 5.7 %collective-permute-start.28 = (bf16[4,128,2048]{2,1,0:T(8,128)(2,1)S(1)}, bf16[4,128,2048]{2,1,0:T(8,128)(2,1)S(1)}, u32[]{:S(2)}, u32[]{:S(2)}) collective-permute-start(bf16[4,128,2048]{2,1,0:T(8,128)(2,1)S(1)} %get-tuple-element.112), channel_id=1, source_target_pairs={{0,4},{4,0},{8,12},{12,8},{16,20},{20,16},{24,28},{28,24},{1,5},{5... | collective-permute-start | bytes 6291464 | tf_op jit(solution)/shard_map/ppermute | solution.py:456
  119.5 4.8 %collective-permute-start.30 = (bf16[128,2048]{1,0:T(8,128)(2,1)S(1)}, bf16[128,2048]{1,0:T(8,128)(2,1)S(1)}, u32[]{:S(2)}, u32[]{:S(2)}) collective-permute-start(bf16[128,2048]{1,0:T(8,128)(2,1)S(1)} %collective-permute-done.26.refs_2_), channel_id=1, source_target_pairs={{0,4},{4,0},{8,12},{12,8},{16,20},{20,16},{24,28},{28,24},{1,5},{5... | collective-permute-start | bytes 1572872 | tf_op jit(solution)/shard_map/ppermute | solution.py:456
  119.9 5.1 %collective-permute-start.29 = (bf16[128,2048]{1,0:T(8,128)(2,1)S(1)}, bf16[128,2048]{1,0:T(8,128)(2,1)S(1)}, u32[]{:S(2)}, u32[]{:S(2)}) collective-permute-start(bf16[128,2048]{1,0:T(8,128)(2,1)S(1)} %collective-permute-done.25.refs_1_), channel_id=1, source_target_pairs={{0,4},{4,0},{8,12},{12,8},{16,20},{20,16},{24,28},{28,24},{1,5},{5... | collective-permute-start | bytes 1572872 | tf_op jit(solution)/shard_map/ppermute | solution.py:456
  120.1 8.6 %collective-permute-start.36 = (bf16[64,2048]{1,0:T(8,128)(2,1)S(1)}, bf16[64,2048]{1,0:T(8,128)(2,1)S(1)}, u32[]{:S(2)}, u32[]{:S(2)}) collective-permute-start(bf16[64,2048]{1,0:T(8,128)(2,1)S(1)} %slice.131), channel_id=1, source_target_pairs={{0,8},{4,12},{8,0},{12,4},{16,24},{20,28},{24,16},{28,20},{1,9},{5... | collective-permute-start | bytes 786440 | tf_op jit(solution)/shard_map/ppermute | solution.py:456
  121.5 8.5 %collective-permute-start.35 = (bf16[64,2048]{1,0:T(8,128)(2,1)S(1)}, bf16[64,2048]{1,0:T(8,128)(2,1)S(1)}, u32[]{:S(2)}, u32[]{:S(2)}) collective-permute-start(bf16[64,2048]{1,0:T(8,128)(2,1)S(1)} %slice.130), channel_id=1, source_target_pairs={{0,16},{4,20},{8,24},{12,28},{16,0},{20,4},{24,8},{28,12},{1,17},{... | collective-permute-start | bytes 786440 | tf_op jit(solution)/shard_map/ppermute | solution.py:456
  130.0 2.3 %collective-permute-start.37 = (bf16[128,2048]{1,0:T(8,128)(2,1)S(1)}, bf16[128,2048]{1,0:T(8,128)(2,1)S(1)}, u32[]{:S(2)}, u32[]{:S(2)}) collective-permute-start(bf16[128,2048]{1,0:T(8,128)(2,1)S(1)} %constant_dynamic-update-slice_fusion.4.refs_3_), channel_id=1, source_target_pairs={{0,4},{4,0},{8,12},{12,8},{16,20},{20,16},{24,28},{28,24},{1,5},{5... | collective-permute-start | bytes 1572872 | tf_op jit(solution)/shard_map/ppermute | solution.py:456
  130.1 14.3 %collective-permute-start.31 = (bf16[128,2048]{1,0:T(8,128)(2,1)S(1)}, bf16[128,2048]{1,0:T(8,128)(2,1)S(1)}, u32[]{:S(2)}, u32[]{:S(2)}) collective-permute-start(bf16[128,2048]{1,0:T(8,128)(2,1)S(1)} %pad_maximum_fusion.1), channel_id=1, source_target_pairs={{0,8},{4,12},{8,0},{12,4},{16,24},{20,28},{24,16},{28,20},{1,9},{5... | collective-permute-start | bytes 1572872 | tf_op jit(solution)/shard_map/ppermute | solution.py:456
  130.7 14.0 %collective-permute-start.32 = (bf16[128,2048]{1,0:T(8,128)(2,1)S(1)}, bf16[128,2048]{1,0:T(8,128)(2,1)S(1)}, u32[]{:S(2)}, u32[]{:S(2)}) collective-permute-start(bf16[128,2048]{1,0:T(8,128)(2,1)S(1)} %pad_maximum_fusion.2), channel_id=1, source_target_pairs={{0,16},{4,20},{8,24},{12,28},{16,0},{20,4},{24,8},{28,12},{1,17},{... | collective-permute-start | bytes 1572872 | tf_op jit(solution)/shard_map/ppermute | solution.py:456
  138.4 9.1 %copy-start.7 = (bf16[1,512,2048]{2,1,0:T(8,128)(2,1)S(1)}, bf16[1,512,2048]{2,1,0:T(8,128)(2,1)}, u32[]{:S(2)}) copy-start(bf16[1,512,2048]{2,1,0:T(8,128)(2,1)} %down_ref.5) | copy-start | bytes 6291460
  144.7 10.2 %collective-permute-start.38 = (bf16[4,128,2048]{2,1,0:T(8,128)(2,1)S(1)}, bf16[4,128,2048]{2,1,0:T(8,128)(2,1)S(1)}, u32[]{:S(2)}, u32[]{:S(2)}) collective-permute-start(bf16[4,128,2048]{2,1,0:T(8,128)(2,1)S(1)} %expert_pieces.4), channel_id=1, source_target_pairs={{0,4},{4,0},{8,12},{12,8},{16,20},{20,16},{24,28},{28,24},{1,5},{5... | collective-permute-start | bytes 6291464 | tf_op jit(solution)/shard_map/ppermute | solution.py:456
  145.0 8.8 %collective-permute-start.34 = (bf16[64,2048]{1,0:T(8,128)(2,1)S(1)}, bf16[64,2048]{1,0:T(8,128)(2,1)S(1)}, u32[]{:S(2)}, u32[]{:S(2)}) collective-permute-start(bf16[64,2048]{1,0:T(8,128)(2,1)S(1)} %get-tuple-element.154), channel_id=1, source_target_pairs={{0,8},{4,12},{8,0},{12,4},{16,24},{20,28},{24,16},{28,20},{1,9},{5... | collective-permute-start | bytes 786440 | tf_op jit(solution)/shard_map/ppermute | solution.py:456
  146.5 8.4 %collective-permute-start.33 = (bf16[64,2048]{1,0:T(8,128)(2,1)S(1)}, bf16[64,2048]{1,0:T(8,128)(2,1)S(1)}, u32[]{:S(2)}, u32[]{:S(2)}) collective-permute-start(bf16[64,2048]{1,0:T(8,128)(2,1)S(1)} %get-tuple-element.155), channel_id=1, source_target_pairs={{0,16},{4,20},{8,24},{12,28},{16,0},{20,4},{24,8},{28,12},{1,17},{... | collective-permute-start | bytes 786440 | tf_op jit(solution)/shard_map/ppermute | solution.py:456
  155.4 13.3 %collective-permute-start.42 = (bf16[128,2048]{1,0:T(8,128)(2,1)S(1)}, bf16[128,2048]{1,0:T(8,128)(2,1)S(1)}, u32[]{:S(2)}, u32[]{:S(2)}) collective-permute-start(bf16[128,2048]{1,0:T(8,128)(2,1)S(1)} %pad_maximum_fusion.3), channel_id=1, source_target_pairs={{0,8},{4,12},{8,0},{12,4},{16,24},{20,28},{24,16},{28,20},{1,9},{5... | collective-permute-start | bytes 1572872 | tf_op jit(solution)/shard_map/ppermute | solution.py:456
  156.1 13.0 %collective-permute-start.43 = (bf16[128,2048]{1,0:T(8,128)(2,1)S(1)}, bf16[128,2048]{1,0:T(8,128)(2,1)S(1)}, u32[]{:S(2)}, u32[]{:S(2)}) collective-permute-start(bf16[128,2048]{1,0:T(8,128)(2,1)S(1)} %pad_maximum_fusion.4), channel_id=1, source_target_pairs={{0,16},{4,20},{8,24},{12,28},{16,0},{20,4},{24,8},{28,12},{1,17},{... | collective-permute-start | bytes 1572872 | tf_op jit(solution)/shard_map/ppermute | solution.py:456
  169.4 6.9 %collective-permute-start.45 = (bf16[64,2048]{1,0:T(8,128)(2,1)S(1)}, bf16[64,2048]{1,0:T(8,128)(2,1)S(1)}, u32[]{:S(2)}, u32[]{:S(2)}) collective-permute-start(bf16[64,2048]{1,0:T(8,128)(2,1)S(1)} %get-tuple-element.148), channel_id=1, source_target_pairs={{0,8},{4,12},{8,0},{12,4},{16,24},{20,28},{24,16},{28,20},{1,9},{5... | collective-permute-start | bytes 786440 | tf_op jit(solution)/shard_map/ppermute | solution.py:456
  170.8 6.4 %collective-permute-start.44 = (bf16[64,2048]{1,0:T(8,128)(2,1)S(1)}, bf16[64,2048]{1,0:T(8,128)(2,1)S(1)}, u32[]{:S(2)}, u32[]{:S(2)}) collective-permute-start(bf16[64,2048]{1,0:T(8,128)(2,1)S(1)} %get-tuple-element.149), channel_id=1, source_target_pairs={{0,16},{4,20},{8,24},{12,28},{16,0},{20,4},{24,8},{28,12},{1,17},{... | collective-permute-start | bytes 786440 | tf_op jit(solution)/shard_map/ppermute | solution.py:456
  171.8 9.4 %collective-permute-start.39 = (bf16[128,512]{1,0:T(8,128)(2,1)S(1)}, bf16[128,512]{1,0:T(8,128)(2,1)S(1)}, u32[]{:S(2)}, u32[]{:S(2)}) collective-permute-start(bf16[128,512]{1,0:T(8,128)(2,1)S(1)} %get-tuple-element.135), channel_id=1, source_target_pairs={{0,1},{1,0},{2,3},{3,2},{4,5},{5,4},{6,7},{7,6},{8,9},{9,8},{10,11... | collective-permute-start | bytes 393224 | tf_op jit(solution)/shard_map/ppermute | solution.py:462
  172.4 14.9 %collective-permute-start.40 = (bf16[128,512]{1,0:T(8,128)(2,1)S(1)}, bf16[128,512]{1,0:T(8,128)(2,1)S(1)}, u32[]{:S(2)}, u32[]{:S(2)}) collective-permute-start(bf16[128,512]{1,0:T(8,128)(2,1)S(1)} %get-tuple-element.136), channel_id=1, source_target_pairs={{0,2},{1,3},{2,0},{3,1},{4,6},{5,7},{6,4},{7,5},{8,10},{9,11},{10,... | collective-permute-start | bytes 393224 | tf_op jit(solution)/shard_map/ppermute | solution.py:462
  174.7 12.6 %collective-permute-start.41 = (bf16[128,512]{1,0:T(8,128)(2,1)S(1)}, bf16[128,512]{1,0:T(8,128)(2,1)S(1)}, u32[]{:S(2)}, u32[]{:S(2)}) collective-permute-start(bf16[128,512]{1,0:T(8,128)(2,1)S(1)} %get-tuple-element.137), channel_id=1, source_target_pairs={{0,3},{1,2},{2,1},{3,0},{4,7},{5,6},{6,5},{7,4},{8,11},{9,10},{10,... | collective-permute-start | bytes 393224 | tf_op jit(solution)/shard_map/ppermute | solution.py:462
  177.2 5.4 %copy-start.9 = (bf16[256,512]{1,0:T(8,128)(2,1)S(1)}, bf16[256,512]{1,0:T(8,128)(2,1)}, u32[]{:S(2)}) copy-start(bf16[256,512]{1,0:T(8,128)(2,1)} %cot_ref.3) | copy-start | bytes 786436
  178.2 9.2 %collective-permute-start.46 = (bf16[128,512]{1,0:T(8,128)(2,1)S(1)}, bf16[128,512]{1,0:T(8,128)(2,1)S(1)}, u32[]{:S(2)}, u32[]{:S(2)}) collective-permute-start(bf16[128,512]{1,0:T(8,128)(2,1)S(1)} %get-tuple-element.142), channel_id=1, source_target_pairs={{0,1},{1,0},{2,3},{3,2},{4,5},{5,4},{6,7},{7,6},{8,9},{9,8},{10,11... | collective-permute-start | bytes 393224 | tf_op jit(solution)/shard_map/ppermute | solution.py:462
  179.0 15.3 %collective-permute-start.47 = (bf16[128,512]{1,0:T(8,128)(2,1)S(1)}, bf16[128,512]{1,0:T(8,128)(2,1)S(1)}, u32[]{:S(2)}, u32[]{:S(2)}) collective-permute-start(bf16[128,512]{1,0:T(8,128)(2,1)S(1)} %get-tuple-element.143), channel_id=1, source_target_pairs={{0,2},{1,3},{2,0},{3,1},{4,6},{5,7},{6,4},{7,5},{8,10},{9,11},{10,... | collective-permute-start | bytes 393224 | tf_op jit(solution)/shard_map/ppermute | solution.py:462
  181.2 13.1 %collective-permute-start.48 = (bf16[128,512]{1,0:T(8,128)(2,1)S(1)}, bf16[128,512]{1,0:T(8,128)(2,1)S(1)}, u32[]{:S(2)}, u32[]{:S(2)}) collective-permute-start(bf16[128,512]{1,0:T(8,128)(2,1)S(1)} %get-tuple-element.144), channel_id=1, source_target_pairs={{0,3},{1,2},{2,1},{3,0},{4,7},{5,6},{6,5},{7,4},{8,11},{9,10},{10,... | collective-permute-start | bytes 393224 | tf_op jit(solution)/shard_map/ppermute | solution.py:462
  (4 other events, 4.3 us)

commit v10 on v9

--- a/solution.py
+++ b/solution.py
@@ -335,11 +335,10 @@
 PAIR = 2
 
 
-def expert_kernel(groups, chunk, experts, where_ref, near_routes, far_routes, gate_ref, up_ref, down_ref, *refs):
-    masks = [mask for group in groups for mask in group]
-    row_refs, outs, (rows_ref, sems) = refs[: len(masks)], refs[len(masks) : -2], refs[-2:]
-    _, tok, width = outs[0].shape
-    steps = len(masks) // PAIR
+def expert_kernel(masks, chunk, experts, where_ref, near_routes, far_routes, gate_ref, up_ref, down_ref, *refs):
+    row_refs, (near_ref, far_ref, rows_ref, sems) = refs[: PAIR * len(masks)], refs[PAIR * len(masks) :]
+    _, tok, width = near_ref.shape
+    steps = len(masks)
     step = pl.program_id(0)
     slot = lax.rem(step, 2)
 
@@ -362,17 +361,14 @@
     mine = (here == where_ref[1]) | (here == where_ref[1] + experts) | (here == where_ref[1] + 2 * experts)
     square = (LANES, LANES)
     diagonal = lax.broadcasted_iota(jnp.int32, square, 0) == lax.broadcasted_iota(jnp.int32, square, 1)
+    index = jnp.int32(masks[0] // 2)
+    for at in range(1, steps):
+        index = jnp.where(step == at, masks[at] // 2, index)
     weights = []
-    for part in range(PAIR):
-        mask = jnp.int32(masks[part])
-        for at in range(1, steps):
-            mask = jnp.where(step == at, masks[PAIR * at + part], mask)
-        index = lax.shift_right_logical(mask, 1)
+    for routes_ref in (near_routes, far_routes):
         for block in range(tok // LANES):
             base = (chunk // LANES + block) * 3 * experts
-            at = slice(base, base + 3 * experts)
-            near, far = near_routes[index, at, :].astype(F32), far_routes[index, at, :].astype(F32)
-            table = jnp.where((mask & CORE) == 0, near, far)
+            table = routes_ref[index, base : base + 3 * experts, :].astype(F32)
             row = jnp.sum(jnp.where(mine, table, 0.0), axis=0, keepdims=True)
             weights.append(jnp.sum(jnp.where(diagonal, jnp.broadcast_to(row, square), 0.0), axis=1, keepdims=True))
 
@@ -381,17 +377,12 @@
     gate = mm(tokens, gate_ref[0])
     inner = (gate * jax.nn.sigmoid(gate) * mm(tokens, up_ref[0])).astype(BF)
     cols = pick_block(width, 512)
-    per = steps // len(outs)
     for begin in range(0, width, cols):
         piece = mm(inner, down_ref[0, :, begin : begin + cols])
         for at, weight in enumerate(weights):
             part, row = divmod(at * LANES, tok)
             scaled = (piece[at * LANES : (at + 1) * LANES] * weight).astype(BF)
-            for group, out_ref in enumerate(outs):
-
-                @pl.when((step >= group * per) & (step < (group + 1) * per))
-                def _(scaled=scaled, part=part, row=row, out_ref=out_ref):
-                    out_ref[part, row : row + LANES, begin : begin + cols] = scaled
+            (near_ref, far_ref)[part][0, row : row + LANES, begin : begin + cols] = scaled
 
 
 def stage_kernel(where_ref, *refs):
@@ -412,37 +403,32 @@
     )(where, *weights)
 
 
-def expert_pieces(chunk, where, rows, groups, gate, up, down, routes):
-    blocks = [rows[mask] for group in groups for mask in group]
+def expert_pieces(chunk, where, rows, masks, gate, up, down, routes):
+    blocks = [rows[mask | core] for mask in masks for core in (0, CORE)]
     tok, width = blocks[0].shape
     hidden = gate.shape[2]
-    count, each = len(blocks), len(groups[0])
-    per = each // PAIR
+    count = len(masks)
     experts = EXP_CTX * 2 * routes[0].shape[0]
     route_rows = CHUNKS * tok // LANES * 3 * experts
     vmem = pl.BlockSpec(memory_space=pltpu.VMEM)
     table = pl.BlockSpec((routes[0].shape[0], route_rows, LANES), lambda i: (0, 0, 0))
-
-    def out_spec(group):
-        return pl.BlockSpec((PAIR, tok, width), lambda i: (jnp.clip(i - group * per, 0, per - 1), 0, 0))
-
-    return pl.pallas_call(
-        functools.partial(expert_kernel, tuple(map(tuple, groups)), chunk, experts),
-        grid=(count // PAIR,),
+    return pl.pallas_call(
+        functools.partial(expert_kernel, tuple(masks), chunk, experts),
+        grid=(count,),
         in_specs=[pl.BlockSpec(memory_space=pltpu.SMEM), table, table]
         + [vmem] * 3
-        + [pl.BlockSpec(memory_space=pl.ANY)] * count,
-        out_specs=[out_spec(group) for group in range(len(groups))],
-        out_shape=[jax.ShapeDtypeStruct((each, tok, width), BF)] * len(groups),
+        + [pl.BlockSpec(memory_space=pl.ANY)] * (PAIR * count),
+        out_specs=[pl.BlockSpec((1, tok, width), lambda i: (i, 0, 0))] * PAIR,
+        out_shape=[jax.ShapeDtypeStruct((count, tok, width), BF)] * PAIR,
         scratch_shapes=[
             pltpu.VMEM((2, PAIR * tok, width), BF),
             pltpu.SemaphoreType.DMA((2,)),
         ],
         compiler_params=params(20),
         cost_estimate=pl.CostEstimate(
-            flops=6 * count * tok * width * hidden,
-            bytes_accessed=4 * count * tok * width,
-            transcendentals=count * tok * hidden,
+            flops=6 * PAIR * count * tok * width * hidden,
+            bytes_accessed=4 * PAIR * count * tok * width,
+            transcendentals=PAIR * count * tok * hidden,
         ),
         name="expert_pieces",
     )(where, *routes, gate, up, down, *blocks)
@@ -491,27 +477,25 @@
     return [swap(came[ROW][:half], COL), swap(came[COL][half:], ROW)]
 
 
-def first_sums(here, arrived):
-    tok = here.shape[1]
+def first_sums(pieces):
+    tok = pieces[0][0].shape[0]
     if lax.axis_size("ctx") != PLANE:
-        return [(2 * at, plus(here[at], arrived[at]), [(0, 0, tok)]) for at in range(1, here.shape[0])]
-    half, across = tok // 2, (ROW | COL) // 2
+        return [(mask, plus(*parts), [(0, 0, tok)]) for mask, parts in pieces.items() if mask]
+    half = tok // 2
     sums = []
     for mask, start in ((ROW, 0), (COL, half)):
-        part = slice(start, start + half)
-        pieces = [plus(here[at, part], arrived[at, part]) for at in (across, mask // 2)]
-        sums.append((mask, jnp.concatenate(pieces), [(half, start, half)]))
+        both = [plus(*[part[start : start + half] for part in pieces[at]]) for at in (ROW | COL, mask)]
+        sums.append((mask, jnp.concatenate(both), [(half, start, half)]))
     return sums
 
 
-def last_sums(here, arrived, came):
+def last_sums(pieces, came):
     if lax.axis_size("ctx") != PLANE:
         return []
-    half = here.shape[1] // 2
-    row, col = ROW // 2, COL // 2
+    half = pieces[0][0].shape[0] // 2
     return [
-        (COL, plus(here[col, :half], arrived[col, :half], came[0][:half]), [(0, 0, half)]),
-        (ROW, plus(here[row, half:], arrived[row, half:], came[1][:half]), [(0, half, half)]),
+        (mask, plus(*[part[start : start + half] for part in pieces[mask]], rows[:half]), [(0, start, half)])
+        for mask, start, rows in ((COL, 0, came[0]), (ROW, half, came[1]))
     ]
 
 
@@ -640,61 +624,63 @@
     while bwd.shape[0] < n_ctx // 2:
         bwd = double(bwd, 2 * bwd.shape[0])
 
-    evens = list(range(0, n_ctx, 2))
-    odds = [mask | CORE for mask in evens]
     own = join_rows(where, after(send_heads([normed[0]] * n_head), bwd))
     bwd = (bwd, swap(after(bwd, own), CORE))
     rows = []
     for chunk in range(CHUNKS):
-        rows.append({0: own, CORE: swap(own, CORE)} | depart(own))
+        rows.append({0: own} | depart(own))
         if chunk + 1 < CHUNKS:
-            parts = send_heads([after(normed[chunk + 1], own)] * n_head)
-            own = join_rows(where, after(parts, rows[chunk][CORE]))
+            own = join_rows(where, send_heads([after(normed[chunk + 1], own)] * n_head))
             rows[chunk] = after(rows[chunk], own)
 
-    pending, sums, first, arrived = [], [], None, None
+    state = []
     for chunk in range(CHUNKS):
-        here_rows = rows[chunk]
-        halves = forward(here_rows)
-        here_rows |= {mask | CORE: swap(part, CORE) for mask, part in here_rows.items() if mask and not mask & CORE}
-        if pending:
-            arrived = after(arrived, [part for mask, part in here_rows.items() if mask & CORE])
-            first = first_sums(pending[-1][0], arrived)
-            pending[-1] += (arrived, first, send_sums(first))
-            halves = after(halves, arrays(first))
-        if halves:
-            across = jnp.concatenate(halves)
-            here_rows |= {ROW | COL: across, ROW | COL | CORE: swap(across, CORE)}
-        if pending:
-            here_rows = after(here_rows, arrays(first))
         experts_of = functools.partial(
             expert_pieces, chunk * chunk_rows, where, gate=w_gate, up=w_up, down=w_down, routes=fwd
         )
+        halves = forward(rows[chunk]) if chunk == 0 else halves
+        masks = list(rows[chunk])
+        here = rows[chunk] | {mask | CORE: swap(part, CORE) for mask, part in rows[chunk].items()}
+        if state:
+            if halves:
+                across = jnp.concatenate(halves)
+                pair = {ROW | COL: across, ROW | COL | CORE: swap(across, CORE)}
+                here = after(here, pair)
+            here = after(here, arrays(state[-1]["first"]))
+        near, far = experts_of(rows=here, masks=masks)
+        if state:
+            before = state[-1]
+            far = after(far, (before["came"], bwd))
+            before["last"] = last_sums(before["pieces"], before["came"])
+            before["came_last"] = send_sums(before["last"])
+        arrived = swap(far, CORE)
+        pieces = {mask: (near[at], arrived[at]) for at, mask in enumerate(masks)}
+        if halves:
+            if not state:
+                across = jnp.concatenate(after(halves, near))
+                pair = {ROW | COL: across, ROW | COL | CORE: swap(across, CORE)}
+            pair = after(pair, [far] + arrays(before["last"]) if state else rows[chunk + 1])
+            near_across, far_across = experts_of(rows=pair, masks=[ROW | COL])
+            arrived_across = swap(after(far_across, before["came_last"]) if state else far_across, CORE)
+            if chunk + 1 < CHUNKS:
+                halves = forward(rows[chunk + 1])
+                arrived_across = after(arrived_across, halves)
+            pieces[ROW | COL] = (near_across[0], arrived_across[0])
+        first = first_sums(pieces)
+        state.append(
+            {"first": first, "came": send_sums(first), "pieces": pieces, "own": (near, arrived), "came_last": []}
+        )
+
+    sums = []
+    for chunk, made in enumerate(state):
+        if chunk + 1 == CHUNKS:
+            made["last"] = last_sums(made["pieces"], after(made["came"], sums[-1][0]))
+            made["came_last"] = send_sums(made["last"])
+        terms = terms_of(made["first"], made["came"]) + terms_of(made["last"], made["came_last"])
         if chunk + 1 < CHUNKS:
-            here, far = experts_of(rows=here_rows, groups=[evens, odds])
-            arrived = swap(after(far, (rows[chunk + 1], bwd)), CORE)
-            pending.append((here,))
-        else:
-            (far,) = experts_of(rows=here_rows, groups=[odds])
-            arrived = swap(after(far, pending[-1][3]), CORE)
-            last = last_sums(*pending[-1][:2], pending[-1][3])
-            received = send_sums(last)
-            pending[-1] += (terms_of(first, pending[-1][3]) + terms_of(last, received),)
-            (here,) = experts_of(rows=after(here_rows, [far] + arrays(last)), groups=[evens])
-            arrived = after(arrived, received)
-            first = first_sums(here, arrived)
-            pending.append((here, arrived, first, send_sums(first)))
-
-    for chunk in range(CHUNKS):
-        here, arrived, first, received = pending[chunk][:4]
-        if chunk + 1 < CHUNKS:
-            terms = pending[chunk][4]
-            held = after([rows for rows, _ in terms], arrays(pending[chunk + 1][2]))
+            held = after([part for part, _ in terms], arrays(state[chunk + 1]["first"]))
             terms = list(zip(held, [places for _, places in terms]))
-        else:
-            last = last_sums(here, arrived, after(received, sums[-1][0]))
-            terms = terms_of(first, received) + terms_of(last, send_sums(last))
-        sums.append(send_heads(sum_terms(where, attn[chunk], here, arrived, terms, n_head)))
+        sums.append(send_heads(sum_terms(where, attn[chunk], *made["own"], terms, n_head)))
     grads = core_grads(where, qkv, grad_core, steps, fwd, bwd)
     return (final_sum(where, hidden_in, sums), *grads)
 

time: 196 us -> 203 us (1.036)
  waiting for transfers between devices: 79.2 us -> 93.8 us
  Pallas kernels: 50.4 us -> 45.6 us
  starting transfers between devices: 58.8 us -> 56.3 us
    ppermute x33 -> x35, waiting for transfers between devices: 38.8 us -> 51.7 us  [swap(): lax.ppermute(value, 'ctx', [(at, at ^ mask) for at in range(lax.axis_size...]
    pallas_call x3 -> x4, Pallas kernels: 24.1 us -> 19.3 us  [expert_pieces(): pl.pallas_call(functools.partial(expert_kernel, tuple(masks), chunk, expe...]
    ppermute x33 -> x35, starting transfers between devices: 30.1 us -> 27.7 us  [swap(): lax.ppermute(value, 'ctx', [(at, at ^ mask) for at in range(lax.axis_size...]
  transfers between devices with their start and end apart: 49 -> 51, of which waited for: 27 -> 24; matrix products, arithmetic and copies ran while one was open for 1% -> 1% of each run, Pallas kernels for 17% -> 14%
where the time goes in v10:
time: 203 us; the launch traced here: 202 us
  waiting for transfers between devices  93.8 us (46%)
  starting transfers between devices  56.3 us (28%)
  Pallas kernels  45.6 us (22%)
  local copies, waits for them, and re-layouts  4.1 us (2%)
    ppermute x35, waiting for transfers between devices, swap(): lax.ppermute(value, 'ctx', [(at, at ^ mask) for at in range(lax.axis_size...  51.7 us
    ppermute x15, waiting for transfers between devices, send_heads(): lax.ppermute(parts[mask], 'head', [(at, at ^ mask) for at in range(count)])  41 us
    ppermute x35, starting transfers between devices, swap(): lax.ppermute(value, 'ctx', [(at, at ^ mask) for at in range(lax.axis_size...  27.7 us
    ppermute x15, starting transfers between devices, send_heads(): lax.ppermute(parts[mask], 'head', [(at, at ^ mask) for at in range(count)])  26.1 us
    pallas_call x4, Pallas kernels, expert_pieces(): pl.pallas_call(functools.partial(expert_kernel, tuple(masks), chunk, expe...  19.3 us
    pallas_call x1, Pallas kernels, project(): pl.pallas_call(qkv_kernel, in_specs=[hbm, vmem, hbm], out_specs=[vmem, vm...  7.26 us
    pallas_call x1, Pallas kernels, core_grads(): pl.pallas_call(grad_kernel, in_specs=[pl.BlockSpec(memory_space=pltpu.SME...  4.7 us
  transfers between devices with their start and end apart: 51, of which 24 were waited for; matrix products, arithmetic and copies ran while one was open for 1% of the time, Pallas kernels for 14%

profile of v10, /device:TPU:0, one launch (start us, length us, event | category | flops | bytes accessed | tf_op | source)
XLA Modules:
  0.0 202.3 jit_solution(9755112932126799532)
XLA Ops:
  0.7 7.3 %qkv_projection.1 = (bf16[3,256,512]{2,1,0:T(8,128)(2,1)}, bf16[3,16,512]{2,1,0:T(8,128)(2,1)}) custom-call(bf16[256,2048]{1,0:T(8,128)(2,1)} %x_ref.3, f32[1,2048]{1,0:T(1,128)} %bitcast.63, bf16[3,2048,512]{2,1,0:T(8,128)(2,1)} %bitcast.59), custom_call_target="tpu_custom_call" | custom-call | tf_op jit(solution)/shard_map/qkv_projection/pallas_call | solution.py:68
  8.0 2.5 %collective-permute-start = (bf16[3,16,512]{2,1,0:T(8,128)(2,1)}, bf16[3,16,512]{2,1,0:T(8,128)(2,1)S(1)}, u32[]{:S(2)}, u32[]{:S(2)}) collective-permute-start(bf16[3,16,512]{2,1,0:T(8,128)(2,1)} %get-tuple-element.81), channel_id=1, source_target_pairs={{0,4},{4,8},{8,12},{12,16},{16,20},{20,24},{24,28},{1,5},{5,9},{9,... | collective-permute-start | bytes 147464 | tf_op jit(solution)/shard_map/ppermute | solution.py:612
  10.5 1.1 collective-permute-done.rim_ref
  11.6 1.1 copy-done.10
  12.7 3.0 %conv_states.1 = (bf16[3,256,512]{2,1,0:T(8,128)(2,1)S(1)}, bf16[672,128]{1,0:T(8,128)(2,1)S(1)}, bf16[576,128]{1,0:T(8,128)(2,1)S(1)}) custom-call(bf16[3,256,512]{2,1,0:T(8,128)(2,1)S(1)} %copy-done.10, bf16[3,16,512]{2,1,0:T(8,128)(2,1)S(1)} %collective-permute-done.rim_ref, f32[3,4,512]{2,1,0:T(4,128)S(1)} %bitcast.54, f32[4,256]{1,0:T(4,128)S(1)} %bitcast.51, ...), custom_call_target="tpu_custom_call" | custom-call | tf_op jit(solution)/shard_map/conv_states/pallas_call | solution.py:166
  15.7 0.9 copy-done.5
  17.3 5.1 %collective-permute-start.1 = (bf16[672,128]{1,0:T(8,128)(2,1)S(1)}, bf16[672,128]{1,0:T(8,128)(2,1)S(1)}, u32[]{:S(2)}, u32[]{:S(2)}) collective-permute-start(bf16[672,128]{1,0:T(8,128)(2,1)S(1)} %get-tuple-element.84), channel_id=1, source_target_pairs={{0,8},{4,12},{8,0},{12,4},{16,24},{20,28},{24,16},{28,20},{1,9},{5... | collective-permute-start | bytes 516104 | tf_op jit(solution)/shard_map/ppermute | solution.py:442
  22.4 1.5 collective-permute-start.2
  23.9 0.9 collective-permute-start.3
  24.8 2.8 %collective-permute-done.1 = bf16[672,128]{1,0:T(8,128)(2,1)S(1)} collective-permute-done((bf16[672,128]{1,0:T(8,128)(2,1)S(1)}, bf16[672,128]{1,0:T(8,128)(2,1)S(1)}, u32[]{:S(2)}, u32[]{:S(2)}) %collective-permute-start.1) | collective-permute-done | bytes 172064 | tf_op jit(solution)/shard_map/ppermute | solution.py:442
  27.6 3.8 %collective-permute-done.2 = bf16[672,128]{1,0:T(8,128)(2,1)S(1)} collective-permute-done((bf16[672,128]{1,0:T(8,128)(2,1)S(1)}, bf16[672,128]{1,0:T(8,128)(2,1)S(1)}, u32[]{:S(2)}, u32[]{:S(2)}) %collective-permute-start.2) | collective-permute-done | bytes 172064 | tf_op jit(solution)/shard_map/ppermute | solution.py:442
  31.7 1.1 stage_weights.2.me_ref.where_ref
  32.9 0.9 collective-permute-done.4.far_ref.far_routes.fwd_far
  33.8 1.1 copy-done.6
  34.9 3.6 %core_out.1 = (bf16[64,2048]{1,0:T(8,128)(2,1)S(1)}, bf16[64,2048]{1,0:T(8,128)(2,1)S(1)}, bf16[64,2048]{1,0:T(8,128)(2,1)S(1)}, bf16[64,2048]{1,0:T(8,128)(2,1)S(1)}) custom-call(s32[3]{0:T(128)S(1)} %stage_weights.2.me_ref.where_ref, bf16[3,256,512]{2,1,0:T(8,128)(2,1)S(1)} %copy-done.6, f32[4,256]{1,0:T(4,128)S(1)} %bitcast.52, f32[1,512]{1,0:T(1,128)S(1)} %bitcast.58, ...), custom_call_target="tpu_custom_call" | custom-call | tf_op jit(solution)/shard_map/core_out/pallas_call | solution.py:233
  38.6 1.1 collective-permute-start.8
  39.7 1.6 collective-permute-start.5
  41.2 2.6 %collective-permute-start.6 = (bf16[64,2048]{1,0:T(8,128)(2,1)S(1)}, bf16[64,2048]{1,0:T(8,128)(2,1)S(1)}, u32[]{:S(2)}, u32[]{:S(2)}) collective-permute-start(bf16[64,2048]{1,0:T(8,128)(2,1)S(1)} %get-tuple-element.87), channel_id=1, source_target_pairs={{0,2},{1,3},{2,0},{3,1},{4,6},{5,7},{6,4},{7,5},{8,10},{9,11},{10,... | collective-permute-start | bytes 786440 | tf_op jit(solution)/shard_map/ppermute | solution.py:448
  44.1 1.1 stage_weights.3.where_ref.me_ref
  45.3 7.5 %collective-permute-done.5.refs_1_ = bf16[64,2048]{1,0:T(8,128)(2,1)S(1)} collective-permute-done((bf16[64,2048]{1,0:T(8,128)(2,1)S(1)}, bf16[64,2048]{1,0:T(8,128)(2,1)S(1)}, u32[]{:S(2)}, u32[]{:S(2)}) %collective-permute-start.5) | collective-permute-done | bytes 262176 | tf_op jit(solution)/shard_map/ppermute | solution.py:448
  52.7 9.9 %collective-permute-done.6.refs_2_ = bf16[64,2048]{1,0:T(8,128)(2,1)S(1)} collective-permute-done((bf16[64,2048]{1,0:T(8,128)(2,1)S(1)}, bf16[64,2048]{1,0:T(8,128)(2,1)S(1)}, u32[]{:S(2)}, u32[]{:S(2)}) %collective-permute-start.6) | collective-permute-done | bytes 262176 | tf_op jit(solution)/shard_map/ppermute | solution.py:448
  62.6 0.8 moe_norm.1
  63.5 2.0 collective-permute-start.12
  65.5 5.9 %collective-permute-start.10 = (bf16[32,2048]{1,0:T(8,128)(2,1)S(1)}, bf16[32,2048]{1,0:T(8,128)(2,1)S(1)}, u32[]{:S(2)}, u32[]{:S(2)}) collective-permute-start(bf16[32,2048]{1,0:T(8,128)(2,1)S(1)} %get-tuple-element.100.refs_0_), channel_id=1, source_target_pairs={{0,2},{1,3},{2,0},{3,1},{4,6},{5,7},{6,4},{7,5},{8,10},{9,11},{10,... | collective-permute-start | bytes 393224 | tf_op jit(solution)/shard_map/ppermute | solution.py:448
  71.4 1.3 collective-permute-start.11
  72.8 7.6 %collective-permute-done.10.refs_2_ = bf16[32,2048]{1,0:T(8,128)(2,1)S(1)} collective-permute-done((bf16[32,2048]{1,0:T(8,128)(2,1)S(1)}, bf16[32,2048]{1,0:T(8,128)(2,1)S(1)}, u32[]{:S(2)}, u32[]{:S(2)}) %collective-permute-start.10) | collective-permute-done | bytes 131104 | tf_op jit(solution)/shard_map/ppermute | solution.py:448
  81.1 0.7 collective-permute-start.13
  82.3 2.0 collective-permute-start.15
  84.3 0.7 collective-permute-start.16
  85.1 1.6 collective-permute-start.17
  86.7 3.3 %collective-permute-done.15.refs_1_ = bf16[32,2048]{1,0:T(8,128)(2,1)S(1)} collective-permute-done((bf16[32,2048]{1,0:T(8,128)(2,1)S(1)}, bf16[32,2048]{1,0:T(8,128)(2,1)S(1)}, u32[]{:S(2)}, u32[]{:S(2)}) %collective-permute-start.15) | collective-permute-done | bytes 131104 | tf_op jit(solution)/shard_map/ppermute | solution.py:448
  90.1 4.7 %collective-permute-done.16.refs_2_ = bf16[32,2048]{1,0:T(8,128)(2,1)S(1)} collective-permute-done((bf16[32,2048]{1,0:T(8,128)(2,1)S(1)}, bf16[32,2048]{1,0:T(8,128)(2,1)S(1)}, u32[]{:S(2)}, u32[]{:S(2)}) %collective-permute-start.16) | collective-permute-done | bytes 131104 | tf_op jit(solution)/shard_map/ppermute | solution.py:448
  96.1 1.3 collective-permute-start.25
  97.4 1.6 collective-permute-start.26
  99.5 0.8 collective-permute-start.23
  100.3 7.0 %expert_pieces.4 = (bf16[3,128,2048]{2,1,0:T(8,128)(2,1)S(1)}, bf16[3,128,2048]{2,1,0:T(8,128)(2,1)S(1)}) custom-call(s32[3]{0:T(128)S(1)} %stage_weights.3.where_ref.me_ref, bf16[4,672,128]{2,1,0:T(8,128)(2,1)S(1)} %pad_maximum_fusion.near_ref.near_routes.fwd_near, bf16[4,672,128]{2,1,0:T(8,128)(2,1)S(1)} %collective-permute-done.4.far_ref.far_routes.fwd_far, ...), custom_call_target="tpu_custom_call" | custom-call | flops 4831838208 | bytes 6291456 | tf_op jit(solution)/shard_map/expert_pieces/pallas_call | solution.py:415
  107.3 9.6 %collective-permute-done.22 = bf16[64,2048]{1,0:T(8,128)(2,1)S(1)} collective-permute-done((bf16[64,2048]{1,0:T(8,128)(2,1)S(1)}, bf16[64,2048]{1,0:T(8,128)(2,1)S(1)}, u32[]{:S(2)}, u32[]{:S(2)}) %collective-permute-start.22) | collective-permute-done | bytes 262176 | tf_op jit(solution)/shard_map/ppermute | solution.py:442
  117.6 1.7 collective-permute-start.28
  119.3 2.7 %expert_pieces.5 = (bf16[1,128,2048]{2,1,0:T(8,128)(2,1)S(1)}, bf16[1,128,2048]{2,1,0:T(8,128)(2,1)S(1)}) custom-call(s32[3]{0:T(128)S(1)} %stage_weights.3.where_ref.me_ref, bf16[4,672,128]{2,1,0:T(8,128)(2,1)S(1)} %pad_maximum_fusion.near_ref.near_routes.fwd_near, bf16[4,672,128]{2,1,0:T(8,128)(2,1)S(1)} %collective-permute-done.4.far_ref.far_routes.fwd_far, ...), custom_call_target="tpu_custom_call" | custom-call | flops 1610612736 | bytes 2097152 | tf_op jit(solution)/shard_map/expert_pieces/pallas_call | solution.py:415
  122.1 0.7 collective-permute-start.29
  123.1 2.9 %collective-permute-done.28 = bf16[64,2048]{1,0:T(8,128)(2,1)S(1)} collective-permute-done((bf16[64,2048]{1,0:T(8,128)(2,1)S(1)}, bf16[64,2048]{1,0:T(8,128)(2,1)S(1)}, u32[]{:S(2)}, u32[]{:S(2)}) %collective-permute-start.28) | collective-permute-done | bytes 262176 | tf_op jit(solution)/shard_map/ppermute | solution.py:442
  126.0 4.9 %collective-permute-done.29 = bf16[64,2048]{1,0:T(8,128)(2,1)S(1)} collective-permute-done((bf16[64,2048]{1,0:T(8,128)(2,1)S(1)}, bf16[64,2048]{1,0:T(8,128)(2,1)S(1)}, u32[]{:S(2)}, u32[]{:S(2)}) %collective-permute-start.29) | collective-permute-done | bytes 262176 | tf_op jit(solution)/shard_map/ppermute | solution.py:442
  132.0 1.4 collective-permute-start.31
  134.3 7.0 %expert_pieces.6 = (bf16[3,128,2048]{2,1,0:T(8,128)(2,1)S(1)}, bf16[3,128,2048]{2,1,0:T(8,128)(2,1)S(1)}) custom-call(s32[3]{0:T(128)S(1)} %stage_weights.3.where_ref.me_ref, bf16[4,672,128]{2,1,0:T(8,128)(2,1)S(1)} %pad_maximum_fusion.near_ref.near_routes.fwd_near, bf16[4,672,128]{2,1,0:T(8,128)(2,1)S(1)} %collective-permute-done.4.far_ref.far_routes.fwd_far, ...), custom_call_target="tpu_custom_call" | custom-call | flops 4831838208 | bytes 6291456 | tf_op jit(solution)/shard_map/expert_pieces/pallas_call | solution.py:415
  141.3 5.0 %collective-permute-done.31.refs_1_ = bf16[128,2048]{1,0:T(8,128)(2,1)S(1)} collective-permute-done((bf16[128,2048]{1,0:T(8,128)(2,1)S(1)}, bf16[128,2048]{1,0:T(8,128)(2,1)S(1)}, u32[]{:S(2)}, u32[]{:S(2)}) %collective-permute-start.31) | collective-permute-done | bytes 524320 | tf_op jit(solution)/shard_map/ppermute | solution.py:442
  146.4 1.0 collective-permute-done.30.refs_0_
  147.6 0.8 collective-permute-start.32
  149.1 2.7 %expert_pieces.7 = (bf16[1,128,2048]{2,1,0:T(8,128)(2,1)S(1)}, bf16[1,128,2048]{2,1,0:T(8,128)(2,1)S(1)}) custom-call(s32[3]{0:T(128)S(1)} %stage_weights.3.where_ref.me_ref, bf16[4,672,128]{2,1,0:T(8,128)(2,1)S(1)} %pad_maximum_fusion.near_ref.near_routes.fwd_near, bf16[4,672,128]{2,1,0:T(8,128)(2,1)S(1)} %collective-permute-done.4.far_ref.far_routes.fwd_far, ...), custom_call_target="tpu_custom_call" | custom-call | flops 1610612736 | bytes 2097152 | tf_op jit(solution)/shard_map/expert_pieces/pallas_call | solution.py:415
  151.8 4.6 %collective-permute-done.32.refs_2_ = bf16[64,2048]{1,0:T(8,128)(2,1)S(1)} collective-permute-done((bf16[64,2048]{1,0:T(8,128)(2,1)S(1)}, bf16[64,2048]{1,0:T(8,128)(2,1)S(1)}, u32[]{:S(2)}, u32[]{:S(2)}) %collective-permute-start.32) | collective-permute-done | bytes 262176 | tf_op jit(solution)/shard_map/ppermute | solution.py:442
  156.9 1.9 collective-permute-done.39
  159.1 1.4 collective-permute-start.45
  161.3 1.0 sum_terms.2
  162.2 10.9 %collective-permute-done.45.refs_1_ = bf16[128,2048]{1,0:T(8,128)(2,1)S(1)} collective-permute-done((bf16[128,2048]{1,0:T(8,128)(2,1)S(1)}, bf16[128,2048]{1,0:T(8,128)(2,1)S(1)}, u32[]{:S(2)}, u32[]{:S(2)}) %collective-permute-start.45) | collective-permute-done | bytes 524320 | tf_op jit(solution)/shard_map/ppermute | solution.py:442
  173.1 1.1 collective-permute-done.44.refs_0_
  174.5 0.8 collective-permute-start.46
  176.0 2.6 %collective-permute-start.41 = (bf16[128,512]{1,0:T(8,128)(2,1)S(1)}, bf16[128,512]{1,0:T(8,128)(2,1)S(1)}, u32[]{:S(2)}, u32[]{:S(2)}) collective-permute-start(bf16[128,512]{1,0:T(8,128)(2,1)S(1)} %get-tuple-element.143), channel_id=1, source_target_pairs={{0,1},{1,0},{2,3},{3,2},{4,5},{5,4},{6,7},{7,6},{8,9},{9,8},{10,11... | collective-permute-start | bytes 393224 | tf_op jit(solution)/shard_map/ppermute | solution.py:448
  178.6 2.4 %collective-permute-start.43 = (bf16[128,512]{1,0:T(8,128)(2,1)S(1)}, bf16[128,512]{1,0:T(8,128)(2,1)S(1)}, u32[]{:S(2)}, u32[]{:S(2)}) collective-permute-start(bf16[128,512]{1,0:T(8,128)(2,1)S(1)} %get-tuple-element.145), channel_id=1, source_target_pairs={{0,3},{1,2},{2,1},{3,0},{4,7},{5,6},{6,5},{7,4},{8,11},{9,10},{10,... | collective-permute-start | bytes 393224 | tf_op jit(solution)/shard_map/ppermute | solution.py:448
  181.0 0.8 collective-permute-done.46.refs_2_
  182.2 1.0 sum_terms.3
  183.2 2.7 %collective-permute-start.48 = (bf16[128,512]{1,0:T(8,128)(2,1)S(1)}, bf16[128,512]{1,0:T(8,128)(2,1)S(1)}, u32[]{:S(2)}, u32[]{:S(2)}) collective-permute-start(bf16[128,512]{1,0:T(8,128)(2,1)S(1)} %get-tuple-element.150), channel_id=1, source_target_pairs={{0,1},{1,0},{2,3},{3,2},{4,5},{5,4},{6,7},{7,6},{8,9},{9,8},{10,11... | collective-permute-start | bytes 393224 | tf_op jit(solution)/shard_map/ppermute | solution.py:448
  185.9 2.4 %collective-permute-start.50 = (bf16[128,512]{1,0:T(8,128)(2,1)S(1)}, bf16[128,512]{1,0:T(8,128)(2,1)S(1)}, u32[]{:S(2)}, u32[]{:S(2)}) collective-permute-start(bf16[128,512]{1,0:T(8,128)(2,1)S(1)} %get-tuple-element.152), channel_id=1, source_target_pairs={{0,3},{1,2},{2,1},{3,0},{4,7},{5,6},{6,5},{7,4},{8,11},{9,10},{10,... | collective-permute-start | bytes 393224 | tf_op jit(solution)/shard_map/ppermute | solution.py:448
  188.3 4.7 %core_grads.1 = (bf16[256,512]{1,0:T(8,128)(2,1)}, bf16[256,512]{1,0:T(8,128)(2,1)}, bf16[256,512]{1,0:T(8,128)(2,1)}) custom-call(s32[3]{0:T(128)S(1)} %stage_weights.3.where_ref.me_ref, bf16[3,256,512]{2,1,0:T(8,128)(2,1)S(1)} %copy-done.7, bf16[256,512]{1,0:T(8,128)(2,1)S(1)} %copy-done.9, f32[4,256]{1,0:T(4,128)S(1)} %bitcast.53, ...), custom_call_target="tpu_custom_call" | custom-call | tf_op jit(solution)/shard_map/core_grads/pallas_call | solution.py:278
  193.1 7.9 %collective-permute-done.49.refs_6_ = bf16[128,512]{1,0:T(8,128)(2,1)S(1)} collective-permute-done((bf16[128,512]{1,0:T(8,128)(2,1)S(1)}, bf16[128,512]{1,0:T(8,128)(2,1)S(1)}, u32[]{:S(2)}, u32[]{:S(2)}) %collective-permute-start.49) | collective-permute-done | bytes 131104 | tf_op jit(solution)/shard_map/ppermute | solution.py:448
  200.9 1.4 layer_out.1
  (115 shorter events, 11.0 us)
Async XLA Ops:
  0.6 10.9 %copy-start.8 = (bf16[256,512]{1,0:T(8,128)(2,1)S(1)}, bf16[256,512]{1,0:T(8,128)(2,1)}, u32[]{:S(2)}) copy-start(bf16[256,512]{1,0:T(8,128)(2,1)} %cot_ref.3) | copy-start | bytes 786436
  0.6 10.9 %copy-start.13 = (f32[256,4]{0,1:T(4,128)S(1)}, f32[256,4]{0,1:T(4,128)}, u32[]{:S(2)}) copy-start(f32[256,4]{0,1:T(4,128)} %param.18) | copy-start | bytes 12292
  0.7 10.9 %copy-start.14 = (f32[4,3,512]{2,0,1:T(4,128)S(1)}, f32[4,3,512]{2,0,1:T(4,128)}, u32[]{:S(2)}) copy-start(f32[4,3,512]{2,0,1:T(4,128)} %param.17) | copy-start | bytes 73732
  0.7 10.9 %copy-start.15 = (s32[256,8]{0,1:T(8,128)S(1)}, s32[256,8]{0,1:T(8,128)}, u32[]{:S(2)}) copy-start(s32[256,8]{0,1:T(8,128)} %param.22) | copy-start | bytes 24580
  0.7 10.9 %copy-start.16 = (f32[256,8]{0,1:T(8,128)S(1)}, f32[256,8]{0,1:T(8,128)}, u32[]{:S(2)}) copy-start(f32[256,8]{0,1:T(8,128)} %param.23) | copy-start | bytes 24580
  7.9 23.8 %copy-start.4 = (bf16[512,2048]{1,0:T(8,128)(2,1)S(1)}, bf16[512,2048]{1,0:T(8,128)(2,1)}, u32[]{:S(2)}) copy-start(bf16[512,2048]{1,0:T(8,128)(2,1)} %w_ref.1) | copy-start | bytes 6291460
  8.0 3.6 %collective-permute-start = (bf16[3,16,512]{2,1,0:T(8,128)(2,1)}, bf16[3,16,512]{2,1,0:T(8,128)(2,1)S(1)}, u32[]{:S(2)}, u32[]{:S(2)}) collective-permute-start(bf16[3,16,512]{2,1,0:T(8,128)(2,1)} %get-tuple-element.81), channel_id=1, source_target_pairs={{0,4},{4,8},{8,12},{12,16},{16,20},{20,24},{24,28},{1,5},{5,9},{9,... | collective-permute-start | bytes 147464 | tf_op jit(solution)/shard_map/ppermute | solution.py:612
  17.3 10.4 %collective-permute-start.1 = (bf16[672,128]{1,0:T(8,128)(2,1)S(1)}, bf16[672,128]{1,0:T(8,128)(2,1)S(1)}, u32[]{:S(2)}, u32[]{:S(2)}) collective-permute-start(bf16[672,128]{1,0:T(8,128)(2,1)S(1)} %get-tuple-element.84), channel_id=1, source_target_pairs={{0,8},{4,12},{8,0},{12,4},{16,24},{20,28},{24,16},{28,20},{1,9},{5... | collective-permute-start | bytes 516104 | tf_op jit(solution)/shard_map/ppermute | solution.py:442
  22.4 9.1 %collective-permute-start.2 = (bf16[672,128]{1,0:T(8,128)(2,1)S(1)}, bf16[672,128]{1,0:T(8,128)(2,1)S(1)}, u32[]{:S(2)}, u32[]{:S(2)}) collective-permute-start(bf16[672,128]{1,0:T(8,128)(2,1)S(1)} %get-tuple-element.84), channel_id=1, source_target_pairs={{0,16},{4,20},{8,24},{12,28},{16,0},{20,4},{24,8},{28,12},{1,17},{... | collective-permute-start | bytes 516104 | tf_op jit(solution)/shard_map/ppermute | solution.py:442
  23.9 7.5 %collective-permute-start.3 = (bf16[672,128]{1,0:T(8,128)(2,1)S(1)}, bf16[672,128]{1,0:T(8,128)(2,1)S(1)}, u32[]{:S(2)}, u32[]{:S(2)}) collective-permute-start(bf16[672,128]{1,0:T(8,128)(2,1)S(1)} %get-tuple-element.84), channel_id=1, source_target_pairs={{0,24},{4,28},{8,16},{12,20},{16,8},{20,12},{24,0},{28,4},{1,25},{... | collective-permute-start | bytes 516104 | tf_op jit(solution)/shard_map/ppermute | solution.py:442
  31.6 2.2 %collective-permute-start.4 = (bf16[4,672,128]{2,1,0:T(8,128)(2,1)S(1)}, bf16[4,672,128]{2,1,0:T(8,128)(2,1)S(1)}, u32[]{:S(2)}, u32[]{:S(2)}) collective-permute-start(bf16[4,672,128]{2,1,0:T(8,128)(2,1)S(1)} %pad_maximum_fusion.near_ref.near_routes.fwd_near), channel_id=1, source_target_pairs={{0,4},{4,0},{8,12},{12,8},{16,20},{20,16},{24,28},{28,24},{1,5},{5... | collective-permute-start | bytes 2064392 | tf_op jit(solution)/shard_map/ppermute | solution.py:442
  31.7 12.3 %copy-start.2 = (bf16[1,512,2048]{2,1,0:T(8,128)(2,1)S(1)}, bf16[1,512,2048]{2,1,0:T(8,128)(2,1)}, u32[]{:S(2)}) copy-start(bf16[1,512,2048]{2,1,0:T(8,128)(2,1)} %down_ref.7) | copy-start | bytes 6291460
  34.9 9.2 %copy-start = (bf16[1,2048,512]{2,1,0:T(8,128)(2,1)S(1)}, bf16[1,2048,512]{2,1,0:T(8,128)(2,1)}, u32[]{:S(2)}) copy-start(bf16[1,2048,512]{2,1,0:T(8,128)(2,1)} %gate_ref.7) | copy-start | bytes 6291460
  34.9 9.2 %copy-start.1 = (bf16[1,2048,512]{2,1,0:T(8,128)(2,1)S(1)}, bf16[1,2048,512]{2,1,0:T(8,128)(2,1)}, u32[]{:S(2)}) copy-start(bf16[1,2048,512]{2,1,0:T(8,128)(2,1)} %up_ref.7) | copy-start | bytes 6291460
  38.6 6.7 %copy-start.12 = (bf16[576,128]{1,0:T(8,128)(2,1)S(1)}, bf16[576,128]{1,0:T(8,128)(2,1)}, u32[]{:S(2)}) copy-start(bf16[576,128]{1,0:T(8,128)(2,1)} %copy-done.11) | copy-start | bytes 442372
  38.6 24.0 %copy-start.3 = (bf16[256,2048]{1,0:T(8,128)(2,1)S(1)}, bf16[256,2048]{1,0:T(8,128)(2,1)}, u32[]{:S(2)}) copy-start(bf16[256,2048]{1,0:T(8,128)(2,1)} %x_ref.3) | copy-start | bytes 3145732
  38.6 24.0 %copy-start.17 = (f32[2048]{0:T(1024)S(1)}, f32[2048]{0:T(1024)}, u32[]{:S(2)}) copy-start(f32[2048]{0:T(1024)} %param.21) | copy-start | bytes 24580
  38.6 6.6 %collective-permute-start.8 = (bf16[1,576,128]{2,1,0:T(8,128)(2,1)}, bf16[1,576,128]{2,1,0:T(8,128)(2,1)S(1)}, u32[]{:S(2)}, u32[]{:S(2)}) collective-permute-start(bf16[1,576,128]{2,1,0:T(8,128)(2,1)} %bitcast.49), channel_id=1, source_target_pairs={{0,8},{4,12},{8,0},{12,4},{16,24},{20,28},{24,16},{28,20},{1,9},{5... | collective-permute-start | bytes 442376 | tf_op jit(solution)/shard_map/ppermute | solution.py:442
  39.7 13.1 %collective-permute-start.5 = (bf16[64,2048]{1,0:T(8,128)(2,1)S(1)}, bf16[64,2048]{1,0:T(8,128)(2,1)S(1)}, u32[]{:S(2)}, u32[]{:S(2)}) collective-permute-start(bf16[64,2048]{1,0:T(8,128)(2,1)S(1)} %get-tuple-element.86), channel_id=1, source_target_pairs={{0,1},{1,0},{2,3},{3,2},{4,5},{5,4},{6,7},{7,6},{8,9},{9,8},{10,11... | collective-permute-start | bytes 786440 | tf_op jit(solution)/shard_map/ppermute | solution.py:448
  41.2 21.4 %collective-permute-start.6 = (bf16[64,2048]{1,0:T(8,128)(2,1)S(1)}, bf16[64,2048]{1,0:T(8,128)(2,1)S(1)}, u32[]{:S(2)}, u32[]{:S(2)}) collective-permute-start(bf16[64,2048]{1,0:T(8,128)(2,1)S(1)} %get-tuple-element.87), channel_id=1, source_target_pairs={{0,2},{1,3},{2,0},{3,1},{4,6},{5,7},{6,4},{7,5},{8,10},{9,11},{10,... | collective-permute-start | bytes 786440 | tf_op jit(solution)/shard_map/ppermute | solution.py:448
  43.8 18.8 %collective-permute-start.7 = (bf16[64,2048]{1,0:T(8,128)(2,1)S(1)}, bf16[64,2048]{1,0:T(8,128)(2,1)S(1)}, u32[]{:S(2)}, u32[]{:S(2)}) collective-permute-start(bf16[64,2048]{1,0:T(8,128)(2,1)S(1)} %get-tuple-element.88), channel_id=1, source_target_pairs={{0,3},{1,2},{2,1},{3,0},{4,7},{5,6},{6,5},{7,4},{8,11},{9,10},{10,... | collective-permute-start | bytes 786440 | tf_op jit(solution)/shard_map/ppermute | solution.py:448
  63.5 9.3 %collective-permute-start.12 = (bf16[2,576,128]{2,1,0:T(8,128)(2,1)S(1)}, bf16[2,576,128]{2,1,0:T(8,128)(2,1)S(1)}, u32[]{:S(2)}, u32[]{:S(2)}) collective-permute-start(bf16[2,576,128]{2,1,0:T(8,128)(2,1)S(1)} %pad_maximum_fusion.5), channel_id=1, source_target_pairs={{0,16},{4,20},{8,24},{12,28},{16,0},{20,4},{24,8},{28,12},{1,17},{... | collective-permute-start | bytes 884744 | tf_op jit(solution)/shard_map/ppermute | solution.py:442
  65.5 14.9 %collective-permute-start.10 = (bf16[32,2048]{1,0:T(8,128)(2,1)S(1)}, bf16[32,2048]{1,0:T(8,128)(2,1)S(1)}, u32[]{:S(2)}, u32[]{:S(2)}) collective-permute-start(bf16[32,2048]{1,0:T(8,128)(2,1)S(1)} %get-tuple-element.100.refs_0_), channel_id=1, source_target_pairs={{0,2},{1,3},{2,0},{3,1},{4,6},{5,7},{6,4},{7,5},{8,10},{9,11},{10,... | collective-permute-start | bytes 393224 | tf_op jit(solution)/shard_map/ppermute | solution.py:448
  71.4 9.0 %collective-permute-start.11 = (bf16[32,2048]{1,0:T(8,128)(2,1)S(1)}, bf16[32,2048]{1,0:T(8,128)(2,1)S(1)}, u32[]{:S(2)}, u32[]{:S(2)}) collective-permute-start(bf16[32,2048]{1,0:T(8,128)(2,1)S(1)} %get-tuple-element.100.refs_0_), channel_id=1, source_target_pairs={{0,3},{1,2},{2,1},{3,0},{4,7},{5,6},{6,5},{7,4},{8,11},{9,10},{10,... | collective-permute-start | bytes 393224 | tf_op jit(solution)/shard_map/ppermute | solution.py:448
  72.7 7.8 %collective-permute-start.9 = (bf16[32,2048]{1,0:T(8,128)(2,1)S(1)}, bf16[32,2048]{1,0:T(8,128)(2,1)S(1)}, u32[]{:S(2)}, u32[]{:S(2)}) collective-permute-start(bf16[32,2048]{1,0:T(8,128)(2,1)S(1)} %get-tuple-element.100.refs_0_), channel_id=1, source_target_pairs={{0,1},{1,0},{2,3},{3,2},{4,5},{5,4},{6,7},{7,6},{8,9},{9,8},{10,11... | collective-permute-start | bytes 393224 | tf_op jit(solution)/shard_map/ppermute | solution.py:448
  81.1 14.3 %collective-permute-start.13 = (bf16[128,2048]{1,0:T(8,128)(2,1)S(1)}, bf16[128,2048]{1,0:T(8,128)(2,1)S(1)}, u32[]{:S(2)}, u32[]{:S(2)}) collective-permute-start(bf16[128,2048]{1,0:T(8,128)(2,1)S(1)} %join_rows.2.refs_0_), channel_id=1, source_target_pairs={{0,8},{4,12},{8,0},{12,4},{16,24},{20,28},{24,16},{28,20},{1,9},{5... | collective-permute-start | bytes 1572872 | tf_op jit(solution)/shard_map/ppermute | solution.py:442
  81.9 13.5 %collective-permute-start.14 = (bf16[128,2048]{1,0:T(8,128)(2,1)S(1)}, bf16[128,2048]{1,0:T(8,128)(2,1)S(1)}, u32[]{:S(2)}, u32[]{:S(2)}) collective-permute-start(bf16[128,2048]{1,0:T(8,128)(2,1)S(1)} %join_rows.2.refs_0_), channel_id=1, source_target_pairs={{0,16},{4,20},{8,24},{12,28},{16,0},{20,4},{24,8},{28,12},{1,17},{... | collective-permute-start | bytes 1572872 | tf_op jit(solution)/shard_map/ppermute | solution.py:442
  82.3 7.7 %collective-permute-start.15 = (bf16[32,2048]{1,0:T(8,128)(2,1)S(1)}, bf16[32,2048]{1,0:T(8,128)(2,1)S(1)}, u32[]{:S(2)}, u32[]{:S(2)}) collective-permute-start(bf16[32,2048]{1,0:T(8,128)(2,1)S(1)} %get-tuple-element.104.refs_0_), channel_id=1, source_target_pairs={{0,1},{1,0},{2,3},{3,2},{4,5},{5,4},{6,7},{7,6},{8,9},{9,8},{10,11... | collective-permute-start | bytes 393224 | tf_op jit(solution)/shard_map/ppermute | solution.py:448
  84.3 10.5 %collective-permute-start.16 = (bf16[32,2048]{1,0:T(8,128)(2,1)S(1)}, bf16[32,2048]{1,0:T(8,128)(2,1)S(1)}, u32[]{:S(2)}, u32[]{:S(2)}) collective-permute-start(bf16[32,2048]{1,0:T(8,128)(2,1)S(1)} %get-tuple-element.104.refs_0_), channel_id=1, source_target_pairs={{0,2},{1,3},{2,0},{3,1},{4,6},{5,7},{6,4},{7,5},{8,10},{9,11},{10,... | collective-permute-start | bytes 393224 | tf_op jit(solution)/shard_map/ppermute | solution.py:448
  85.1 9.7 %collective-permute-start.17 = (bf16[32,2048]{1,0:T(8,128)(2,1)S(1)}, bf16[32,2048]{1,0:T(8,128)(2,1)S(1)}, u32[]{:S(2)}, u32[]{:S(2)}) collective-permute-start(bf16[32,2048]{1,0:T(8,128)(2,1)S(1)} %get-tuple-element.104.refs_0_), channel_id=1, source_target_pairs={{0,3},{1,2},{2,1},{3,0},{4,7},{5,6},{6,5},{7,4},{8,11},{9,10},{10,... | collective-permute-start | bytes 393224 | tf_op jit(solution)/shard_map/ppermute | solution.py:448
  95.4 3.6 %collective-permute-start.18 = (bf16[128,2048]{1,0:T(8,128)(2,1)S(1)}, bf16[128,2048]{1,0:T(8,128)(2,1)S(1)}, u32[]{:S(2)}, u32[]{:S(2)}) collective-permute-start(bf16[128,2048]{1,0:T(8,128)(2,1)S(1)} %join_rows.2.refs_0_), channel_id=1, source_target_pairs={{0,4},{4,0},{8,12},{12,8},{16,20},{20,16},{24,28},{28,24},{1,5},{5... | collective-permute-start | bytes 1572872 | tf_op jit(solution)/shard_map/ppermute | solution.py:442
  95.5 4.0 %collective-permute-start.19 = (bf16[128,2048]{1,0:T(8,128)(2,1)S(1)}, bf16[128,2048]{1,0:T(8,128)(2,1)S(1)}, u32[]{:S(2)}, u32[]{:S(2)}) collective-permute-start(bf16[128,2048]{1,0:T(8,128)(2,1)S(1)} %collective-permute-done.13.refs_2_), channel_id=1, source_target_pairs={{0,4},{4,0},{8,12},{12,8},{16,20},{20,16},{24,28},{28,24},{1,5},{5... | collective-permute-start | bytes 1572872 | tf_op jit(solution)/shard_map/ppermute | solution.py:442
  96.0 4.3 %collective-permute-start.20 = (bf16[128,2048]{1,0:T(8,128)(2,1)S(1)}, bf16[128,2048]{1,0:T(8,128)(2,1)S(1)}, u32[]{:S(2)}, u32[]{:S(2)}) collective-permute-start(bf16[128,2048]{1,0:T(8,128)(2,1)S(1)} %collective-permute-done.14.refs_4_), channel_id=1, source_target_pairs={{0,4},{4,0},{8,12},{12,8},{16,20},{20,16},{24,28},{28,24},{1,5},{5... | collective-permute-start | bytes 1572872 | tf_op jit(solution)/shard_map/ppermute | solution.py:442
  96.1 21.5 %collective-permute-start.25 = (bf16[128,2048]{1,0:T(8,128)(2,1)S(1)}, bf16[128,2048]{1,0:T(8,128)(2,1)S(1)}, u32[]{:S(2)}, u32[]{:S(2)}) collective-permute-start(bf16[128,2048]{1,0:T(8,128)(2,1)S(1)} %join_rows.3.refs_0_), channel_id=1, source_target_pairs={{0,8},{4,12},{8,0},{12,4},{16,24},{20,28},{24,16},{28,20},{1,9},{5... | collective-permute-start | bytes 1572872 | tf_op jit(solution)/shard_map/ppermute | solution.py:442
  97.4 22.0 %collective-permute-start.26 = (bf16[128,2048]{1,0:T(8,128)(2,1)S(1)}, bf16[128,2048]{1,0:T(8,128)(2,1)S(1)}, u32[]{:S(2)}, u32[]{:S(2)}) collective-permute-start(bf16[128,2048]{1,0:T(8,128)(2,1)S(1)} %join_rows.3.refs_0_), channel_id=1, source_target_pairs={{0,16},{4,20},{8,24},{12,28},{16,0},{20,4},{24,8},{28,12},{1,17},{... | collective-permute-start | bytes 1572872 | tf_op jit(solution)/shard_map/ppermute | solution.py:442
  99.1 17.9 %collective-permute-start.22 = (bf16[64,2048]{1,0:T(8,128)(2,1)S(1)}, bf16[64,2048]{1,0:T(8,128)(2,1)S(1)}, u32[]{:S(2)}, u32[]{:S(2)}) collective-permute-start(bf16[64,2048]{1,0:T(8,128)(2,1)S(1)} %slice.144), channel_id=1, source_target_pairs={{0,16},{4,20},{8,24},{12,28},{16,0},{20,4},{24,8},{28,12},{1,17},{... | collective-permute-start | bytes 786440 | tf_op jit(solution)/shard_map/ppermute | solution.py:442
  99.5 17.5 %collective-permute-start.23 = (bf16[64,2048]{1,0:T(8,128)(2,1)S(1)}, bf16[64,2048]{1,0:T(8,128)(2,1)S(1)}, u32[]{:S(2)}, u32[]{:S(2)}) collective-permute-start(bf16[64,2048]{1,0:T(8,128)(2,1)S(1)} %slice.145), channel_id=1, source_target_pairs={{0,8},{4,12},{8,0},{12,4},{16,24},{20,28},{24,16},{28,20},{1,9},{5... | collective-permute-start | bytes 786440 | tf_op jit(solution)/shard_map/ppermute | solution.py:442
  117.0 2.3 %collective-permute-start.24 = (bf16[128,2048]{1,0:T(8,128)(2,1)S(1)}, bf16[128,2048]{1,0:T(8,128)(2,1)S(1)}, u32[]{:S(2)}, u32[]{:S(2)}) collective-permute-start(bf16[128,2048]{1,0:T(8,128)(2,1)S(1)} %constant_dynamic-update-slice_fusion.2.refs_0_), channel_id=1, source_target_pairs={{0,4},{4,0},{8,12},{12,8},{16,20},{20,16},{24,28},{28,24},{1,5},{5... | collective-permute-start | bytes 1572872 | tf_op jit(solution)/shard_map/ppermute | solution.py:442
  117.1 14.5 %collective-permute-start.21 = (bf16[3,128,2048]{2,1,0:T(8,128)(2,1)S(1)}, bf16[3,128,2048]{2,1,0:T(8,128)(2,1)S(1)}, u32[]{:S(2)}, u32[]{:S(2)}) collective-permute-start(bf16[3,128,2048]{2,1,0:T(8,128)(2,1)S(1)} %get-tuple-element.109), channel_id=1, source_target_pairs={{0,4},{4,0},{8,12},{12,8},{16,20},{20,16},{24,28},{28,24},{1,5},{5... | collective-permute-start | bytes 4718600 | tf_op jit(solution)/shard_map/ppermute | solution.py:442
  117.6 8.4 %collective-permute-start.28 = (bf16[64,2048]{1,0:T(8,128)(2,1)S(1)}, bf16[64,2048]{1,0:T(8,128)(2,1)S(1)}, u32[]{:S(2)}, u32[]{:S(2)}) collective-permute-start(bf16[64,2048]{1,0:T(8,128)(2,1)S(1)} %slice.176), channel_id=1, source_target_pairs={{0,16},{4,20},{8,24},{12,28},{16,0},{20,4},{24,8},{28,12},{1,17},{... | collective-permute-start | bytes 786440 | tf_op jit(solution)/shard_map/ppermute | solution.py:442
  122.0 8.9 %collective-permute-start.27 = (bf16[1,128,2048]{2,1,0:T(8,128)(2,1)S(1)}, bf16[1,128,2048]{2,1,0:T(8,128)(2,1)S(1)}, u32[]{:S(2)}, u32[]{:S(2)}) collective-permute-start(bf16[1,128,2048]{2,1,0:T(8,128)(2,1)S(1)} %get-tuple-element.115), channel_id=1, source_target_pairs={{0,4},{4,0},{8,12},{12,8},{16,20},{20,16},{24,28},{28,24},{1,5},{5... | collective-permute-start | bytes 1572872 | tf_op jit(solution)/shard_map/ppermute | solution.py:442
  122.1 8.8 %collective-permute-start.29 = (bf16[64,2048]{1,0:T(8,128)(2,1)S(1)}, bf16[64,2048]{1,0:T(8,128)(2,1)S(1)}, u32[]{:S(2)}, u32[]{:S(2)}) collective-permute-start(bf16[64,2048]{1,0:T(8,128)(2,1)S(1)} %slice.177), channel_id=1, source_target_pairs={{0,8},{4,12},{8,0},{12,4},{16,24},{20,28},{24,16},{28,20},{1,9},{5... | collective-permute-start | bytes 786440 | tf_op jit(solution)/shard_map/ppermute | solution.py:442
  122.9 18.5 %collective-permute-start.38 = (bf16[4,576,128]{2,1,0:T(8,128)(2,1)S(1)}, bf16[4,576,128]{2,1,0:T(8,128)(2,1)S(1)}, u32[]{:S(2)}, u32[]{:S(2)}) collective-permute-start(bf16[4,576,128]{2,1,0:T(8,128)(2,1)S(1)} %constant_dynamic-update-slice_fusion.bwd_near), channel_id=1, source_target_pairs={{0,4},{4,0},{8,12},{12,8},{16,20},{20,16},{24,28},{28,24},{1,5},{5... | collective-permute-start | bytes 1769480 | tf_op jit(solution)/shard_map/ppermute | solution.py:442
  126.0 6.0 %collective-permute-start.35 = (bf16[128,2048]{1,0:T(8,128)(2,1)S(1)}, bf16[128,2048]{1,0:T(8,128)(2,1)S(1)}, u32[]{:S(2)}, u32[]{:S(2)}) collective-permute-start(bf16[128,2048]{1,0:T(8,128)(2,1)S(1)} %join_rows.3.refs_0_), channel_id=1, source_target_pairs={{0,4},{4,0},{8,12},{12,8},{16,20},{20,16},{24,28},{28,24},{1,5},{5... | collective-permute-start | bytes 1572872 | tf_op jit(solution)/shard_map/ppermute | solution.py:442
  130.9 2.4 %collective-permute-start.36 = (bf16[128,2048]{1,0:T(8,128)(2,1)S(1)}, bf16[128,2048]{1,0:T(8,128)(2,1)S(1)}, u32[]{:S(2)}, u32[]{:S(2)}) collective-permute-start(bf16[128,2048]{1,0:T(8,128)(2,1)S(1)} %collective-permute-done.25.refs_2_), channel_id=1, source_target_pairs={{0,4},{4,0},{8,12},{12,8},{16,20},{20,16},{24,28},{28,24},{1,5},{5... | collective-permute-start | bytes 1572872 | tf_op jit(solution)/shard_map/ppermute | solution.py:442
  130.9 3.1 %collective-permute-start.37 = (bf16[128,2048]{1,0:T(8,128)(2,1)S(1)}, bf16[128,2048]{1,0:T(8,128)(2,1)S(1)}, u32[]{:S(2)}, u32[]{:S(2)}) collective-permute-start(bf16[128,2048]{1,0:T(8,128)(2,1)S(1)} %collective-permute-done.26.refs_4_), channel_id=1, source_target_pairs={{0,4},{4,0},{8,12},{12,8},{16,20},{20,16},{24,28},{28,24},{1,5},{5... | collective-permute-start | bytes 1572872 | tf_op jit(solution)/shard_map/ppermute | solution.py:442
  131.7 2.7 %collective-permute-start.34 = (bf16[128,2048]{1,0:T(8,128)(2,1)S(1)}, bf16[128,2048]{1,0:T(8,128)(2,1)S(1)}, u32[]{:S(2)}, u32[]{:S(2)}) collective-permute-start(bf16[128,2048]{1,0:T(8,128)(2,1)S(1)} %constant_dynamic-update-slice_fusion.4.refs_0_), channel_id=1, source_target_pairs={{0,4},{4,0},{8,12},{12,8},{16,20},{20,16},{24,28},{28,24},{1,5},{5... | collective-permute-start | bytes 1572872 | tf_op jit(solution)/shard_map/ppermute | solution.py:442
  132.0 14.4 %collective-permute-start.31 = (bf16[128,2048]{1,0:T(8,128)(2,1)S(1)}, bf16[128,2048]{1,0:T(8,128)(2,1)S(1)}, u32[]{:S(2)}, u32[]{:S(2)}) collective-permute-start(bf16[128,2048]{1,0:T(8,128)(2,1)S(1)} %pad_maximum_fusion.2), channel_id=1, source_target_pairs={{0,16},{4,20},{8,24},{12,28},{16,0},{20,4},{24,8},{28,12},{1,17},{... | collective-permute-start | bytes 1572872 | tf_op jit(solution)/shard_map/ppermute | solution.py:442
  133.3 14.0 %collective-permute-start.30 = (bf16[128,2048]{1,0:T(8,128)(2,1)S(1)}, bf16[128,2048]{1,0:T(8,128)(2,1)S(1)}, u32[]{:S(2)}, u32[]{:S(2)}) collective-permute-start(bf16[128,2048]{1,0:T(8,128)(2,1)S(1)} %pad_maximum_fusion.1), channel_id=1, source_target_pairs={{0,8},{4,12},{8,0},{12,4},{16,24},{20,28},{24,16},{28,20},{1,9},{5... | collective-permute-start | bytes 1572872 | tf_op jit(solution)/shard_map/ppermute | solution.py:442
  147.4 11.5 %collective-permute-start.40 = (bf16[3,128,2048]{2,1,0:T(8,128)(2,1)S(1)}, bf16[3,128,2048]{2,1,0:T(8,128)(2,1)S(1)}, u32[]{:S(2)}, u32[]{:S(2)}) collective-permute-start(bf16[3,128,2048]{2,1,0:T(8,128)(2,1)S(1)} %get-tuple-element.131), channel_id=1, source_target_pairs={{0,4},{4,0},{8,12},{12,8},{16,20},{20,16},{24,28},{28,24},{1,5},{5... | collective-permute-start | bytes 4718600 | tf_op jit(solution)/shard_map/ppermute | solution.py:442
  147.6 8.8 %collective-permute-start.32 = (bf16[64,2048]{1,0:T(8,128)(2,1)S(1)}, bf16[64,2048]{1,0:T(8,128)(2,1)S(1)}, u32[]{:S(2)}, u32[]{:S(2)}) collective-permute-start(bf16[64,2048]{1,0:T(8,128)(2,1)S(1)} %get-tuple-element.161), channel_id=1, source_target_pairs={{0,16},{4,20},{8,24},{12,28},{16,0},{20,4},{24,8},{28,12},{1,17},{... | collective-permute-start | bytes 786440 | tf_op jit(solution)/shard_map/ppermute | solution.py:442
  148.4 8.4 %collective-permute-start.33 = (bf16[64,2048]{1,0:T(8,128)(2,1)S(1)}, bf16[64,2048]{1,0:T(8,128)(2,1)S(1)}, u32[]{:S(2)}, u32[]{:S(2)}) collective-permute-start(bf16[64,2048]{1,0:T(8,128)(2,1)S(1)} %get-tuple-element.160), channel_id=1, source_target_pairs={{0,8},{4,12},{8,0},{12,4},{16,24},{20,28},{24,16},{28,20},{1,9},{5... | collective-permute-start | bytes 786440 | tf_op jit(solution)/shard_map/ppermute | solution.py:442
  156.9 1.9 collective-permute-start.39
  159.1 14.0 %collective-permute-start.45 = (bf16[128,2048]{1,0:T(8,128)(2,1)S(1)}, bf16[128,2048]{1,0:T(8,128)(2,1)S(1)}, u32[]{:S(2)}, u32[]{:S(2)}) collective-permute-start(bf16[128,2048]{1,0:T(8,128)(2,1)S(1)} %pad_maximum_fusion.4), channel_id=1, source_target_pairs={{0,16},{4,20},{8,24},{12,28},{16,0},{20,4},{24,8},{28,12},{1,17},{... | collective-permute-start | bytes 1572872 | tf_op jit(solution)/shard_map/ppermute | solution.py:442
  160.5 13.8 %collective-permute-start.44 = (bf16[128,2048]{1,0:T(8,128)(2,1)S(1)}, bf16[128,2048]{1,0:T(8,128)(2,1)S(1)}, u32[]{:S(2)}, u32[]{:S(2)}) collective-permute-start(bf16[128,2048]{1,0:T(8,128)(2,1)S(1)} %pad_maximum_fusion.3), channel_id=1, source_target_pairs={{0,8},{4,12},{8,0},{12,4},{16,24},{20,28},{24,16},{28,20},{1,9},{5... | collective-permute-start | bytes 1572872 | tf_op jit(solution)/shard_map/ppermute | solution.py:442
  174.5 7.3 %collective-permute-start.46 = (bf16[64,2048]{1,0:T(8,128)(2,1)S(1)}, bf16[64,2048]{1,0:T(8,128)(2,1)S(1)}, u32[]{:S(2)}, u32[]{:S(2)}) collective-permute-start(bf16[64,2048]{1,0:T(8,128)(2,1)S(1)} %get-tuple-element.157), channel_id=1, source_target_pairs={{0,16},{4,20},{8,24},{12,28},{16,0},{20,4},{24,8},{28,12},{1,17},{... | collective-permute-start | bytes 786440 | tf_op jit(solution)/shard_map/ppermute | solution.py:442
  175.3 6.9 %collective-permute-start.47 = (bf16[64,2048]{1,0:T(8,128)(2,1)S(1)}, bf16[64,2048]{1,0:T(8,128)(2,1)S(1)}, u32[]{:S(2)}, u32[]{:S(2)}) collective-permute-start(bf16[64,2048]{1,0:T(8,128)(2,1)S(1)} %get-tuple-element.156), channel_id=1, source_target_pairs={{0,8},{4,12},{8,0},{12,4},{16,24},{20,28},{24,16},{28,20},{1,9},{5... | collective-permute-start | bytes 786440 | tf_op jit(solution)/shard_map/ppermute | solution.py:442
  176.0 9.9 %collective-permute-start.41 = (bf16[128,512]{1,0:T(8,128)(2,1)S(1)}, bf16[128,512]{1,0:T(8,128)(2,1)S(1)}, u32[]{:S(2)}, u32[]{:S(2)}) collective-permute-start(bf16[128,512]{1,0:T(8,128)(2,1)S(1)} %get-tuple-element.143), channel_id=1, source_target_pairs={{0,1},{1,0},{2,3},{3,2},{4,5},{5,4},{6,7},{7,6},{8,9},{9,8},{10,11... | collective-permute-start | bytes 393224 | tf_op jit(solution)/shard_map/ppermute | solution.py:448
  178.6 14.4 %collective-permute-start.42 = (bf16[128,512]{1,0:T(8,128)(2,1)S(1)}, bf16[128,512]{1,0:T(8,128)(2,1)S(1)}, u32[]{:S(2)}, u32[]{:S(2)}) collective-permute-start(bf16[128,512]{1,0:T(8,128)(2,1)S(1)} %get-tuple-element.144), channel_id=1, source_target_pairs={{0,2},{1,3},{2,0},{3,1},{4,6},{5,7},{6,4},{7,5},{8,10},{9,11},{10,... | collective-permute-start | bytes 393224 | tf_op jit(solution)/shard_map/ppermute | solution.py:448
  178.6 14.4 %collective-permute-start.43 = (bf16[128,512]{1,0:T(8,128)(2,1)S(1)}, bf16[128,512]{1,0:T(8,128)(2,1)S(1)}, u32[]{:S(2)}, u32[]{:S(2)}) collective-permute-start(bf16[128,512]{1,0:T(8,128)(2,1)S(1)} %get-tuple-element.145), channel_id=1, source_target_pairs={{0,3},{1,2},{2,1},{3,0},{4,7},{5,6},{6,5},{7,4},{8,11},{9,10},{10,... | collective-permute-start | bytes 393224 | tf_op jit(solution)/shard_map/ppermute | solution.py:448
  182.2 6.1 %copy-start.9 = (bf16[256,512]{1,0:T(8,128)(2,1)S(1)}, bf16[256,512]{1,0:T(8,128)(2,1)}, u32[]{:S(2)}) copy-start(bf16[256,512]{1,0:T(8,128)(2,1)} %cot_ref.3) | copy-start | bytes 786436
  183.2 9.8 %collective-permute-start.48 = (bf16[128,512]{1,0:T(8,128)(2,1)S(1)}, bf16[128,512]{1,0:T(8,128)(2,1)S(1)}, u32[]{:S(2)}, u32[]{:S(2)}) collective-permute-start(bf16[128,512]{1,0:T(8,128)(2,1)S(1)} %get-tuple-element.150), channel_id=1, source_target_pairs={{0,1},{1,0},{2,3},{3,2},{4,5},{5,4},{6,7},{7,6},{8,9},{9,8},{10,11... | collective-permute-start | bytes 393224 | tf_op jit(solution)/shard_map/ppermute | solution.py:448
  185.9 15.0 %collective-permute-start.49 = (bf16[128,512]{1,0:T(8,128)(2,1)S(1)}, bf16[128,512]{1,0:T(8,128)(2,1)S(1)}, u32[]{:S(2)}, u32[]{:S(2)}) collective-permute-start(bf16[128,512]{1,0:T(8,128)(2,1)S(1)} %get-tuple-element.151), channel_id=1, source_target_pairs={{0,2},{1,3},{2,0},{3,1},{4,6},{5,7},{6,4},{7,5},{8,10},{9,11},{10,... | collective-permute-start | bytes 393224 | tf_op jit(solution)/shard_map/ppermute | solution.py:448
  185.9 15.0 %collective-permute-start.50 = (bf16[128,512]{1,0:T(8,128)(2,1)S(1)}, bf16[128,512]{1,0:T(8,128)(2,1)S(1)}, u32[]{:S(2)}, u32[]{:S(2)}) collective-permute-start(bf16[128,512]{1,0:T(8,128)(2,1)S(1)} %get-tuple-element.152), channel_id=1, source_target_pairs={{0,3},{1,2},{2,1},{3,0},{4,7},{5,6},{6,5},{7,4},{8,11},{9,10},{10,... | collective-permute-start | bytes 393224 | tf_op jit(solution)/shard_map/ppermute | solution.py:448
  (6 other events, 12.3 us)

commit v11 on v10

--- a/solution.py
+++ b/solution.py
@@ -633,54 +633,40 @@
             own = join_rows(where, send_heads([after(normed[chunk + 1], own)] * n_head))
             rows[chunk] = after(rows[chunk], own)
 
-    state = []
+    def experts_of(chunk, rows):
+        masks = [mask for mask in rows if not mask & CORE]
+        return expert_pieces(chunk * chunk_rows, where, rows, masks, w_gate, w_up, w_down, fwd)
+
+    def with_cores(rows):
+        return rows | {mask | CORE: swap(part, CORE) for mask, part in rows.items()}
+
+    halves, pieces, owns = [], [], []
     for chunk in range(CHUNKS):
-        experts_of = functools.partial(
-            expert_pieces, chunk * chunk_rows, where, gate=w_gate, up=w_up, down=w_down, routes=fwd
-        )
-        halves = forward(rows[chunk]) if chunk == 0 else halves
-        masks = list(rows[chunk])
-        here = rows[chunk] | {mask | CORE: swap(part, CORE) for mask, part in rows[chunk].items()}
-        if state:
-            if halves:
-                across = jnp.concatenate(halves)
-                pair = {ROW | COL: across, ROW | COL | CORE: swap(across, CORE)}
-                here = after(here, pair)
-            here = after(here, arrays(state[-1]["first"]))
-        near, far = experts_of(rows=here, masks=masks)
-        if state:
-            before = state[-1]
-            far = after(far, (before["came"], bwd))
-            before["last"] = last_sums(before["pieces"], before["came"])
-            before["came_last"] = send_sums(before["last"])
-        arrived = swap(far, CORE)
-        pieces = {mask: (near[at], arrived[at]) for at, mask in enumerate(masks)}
-        if halves:
-            if not state:
-                across = jnp.concatenate(after(halves, near))
-                pair = {ROW | COL: across, ROW | COL | CORE: swap(across, CORE)}
-            pair = after(pair, [far] + arrays(before["last"]) if state else rows[chunk + 1])
-            near_across, far_across = experts_of(rows=pair, masks=[ROW | COL])
-            arrived_across = swap(after(far_across, before["came_last"]) if state else far_across, CORE)
-            if chunk + 1 < CHUNKS:
-                halves = forward(rows[chunk + 1])
-                arrived_across = after(arrived_across, halves)
-            pieces[ROW | COL] = (near_across[0], arrived_across[0])
-        first = first_sums(pieces)
-        state.append(
-            {"first": first, "came": send_sums(first), "pieces": pieces, "own": (near, arrived), "came_last": []}
-        )
-
+        here = rows[chunk] if chunk == 0 else after(rows[chunk], near)
+        halves.append(forward(here))
+        near, far = experts_of(chunk, with_cores(here))
+        arrived = swap(far if chunk == 0 else after(far, bwd), CORE)
+        pieces.append({mask: (near[at], arrived[at]) for at, mask in enumerate(here)})
+        owns.append((near, arrived))
+    halves = after(halves, near)
+    for chunk in range(CHUNKS):
+        if halves[chunk]:
+            across = with_cores({ROW | COL: jnp.concatenate(halves[chunk])})
+            if chunk:
+                across = after(across, near)
+            near, far = experts_of(chunk, across)
+            pieces[chunk][ROW | COL] = (near[0], swap(far, CORE)[0])
+    firsts = [first_sums(part) for part in pieces]
+    came = [send_sums(first) for first in firsts]
+    lasts = [last_sums(*both) for both in zip(pieces, came)]
+    came_last = [send_sums(last) for last in lasts]
     sums = []
-    for chunk, made in enumerate(state):
-        if chunk + 1 == CHUNKS:
-            made["last"] = last_sums(made["pieces"], after(made["came"], sums[-1][0]))
-            made["came_last"] = send_sums(made["last"])
-        terms = terms_of(made["first"], made["came"]) + terms_of(made["last"], made["came_last"])
+    for chunk in range(CHUNKS):
+        terms = terms_of(firsts[chunk], came[chunk]) + terms_of(lasts[chunk], came_last[chunk])
         if chunk + 1 < CHUNKS:
-            held = after([part for part, _ in terms], arrays(state[chunk + 1]["first"]))
+            held = after([part for part, _ in terms], arrays(firsts[chunk + 1]))
             terms = list(zip(held, [places for _, places in terms]))
-        sums.append(send_heads(sum_terms(where, attn[chunk], *made["own"], terms, n_head)))
+        sums.append(send_heads(sum_terms(where, attn[chunk], *owns[chunk], terms, n_head)))
     grads = core_grads(where, qkv, grad_core, steps, fwd, bwd)
     return (final_sum(where, hidden_in, sums), *grads)
 

time: 203 us -> 194 us (0.956)
  waiting for transfers between devices: 93.8 us -> 84.3 us
    ppermute x35, waiting for transfers between devices: 51.7 us -> 42.6 us  [swap(): lax.ppermute(value, 'ctx', [(at, at ^ mask) for at in range(lax.axis_size...]
  transfers between devices with their start and end apart: 51 -> 51, of which waited for: 24 -> 24; matrix products, arithmetic and copies ran while one was open for 1% -> 1% of each run, Pallas kernels for 14% -> 15%
where the time goes in v11:
time: 194 us
  waiting for transfers between devices  84.3 us (43%)
  starting transfers between devices  57.7 us (30%)
  Pallas kernels  45.6 us (24%)
  local copies, waits for them, and re-layouts  4.11 us (2%)
    ppermute x35, waiting for transfers between devices, swap(): lax.ppermute(value, 'ctx', [(at, at ^ mask) for at in range(lax.axis_size...  42.6 us
    ppermute x15, waiting for transfers between devices, send_heads(): lax.ppermute(parts[mask], 'head', [(at, at ^ mask) for at in range(count)])  40.6 us
    ppermute x35, starting transfers between devices, swap(): lax.ppermute(value, 'ctx', [(at, at ^ mask) for at in range(lax.axis_size...  29.7 us
    ppermute x15, starting transfers between devices, send_heads(): lax.ppermute(parts[mask], 'head', [(at, at ^ mask) for at in range(count)])  25.5 us
    pallas_call x4, Pallas kernels, expert_pieces(): pl.pallas_call(functools.partial(expert_kernel, tuple(masks), chunk, expe...  19.3 us
    pallas_call x1, Pallas kernels, project(): pl.pallas_call(qkv_kernel, in_specs=[hbm, vmem, hbm], out_specs=[vmem, vm...  7.26 us
    pallas_call x1, Pallas kernels, core_grads(): pl.pallas_call(grad_kernel, in_specs=[pl.BlockSpec(memory_space=pltpu.SME...  4.71 us
    unnamed x41, local copies, waits for them, and re-layouts  3.95 us
  transfers between devices with their start and end apart: 51, of which 24 were waited for; matrix products, arithmetic and copies ran while one was open for 1% of the time, Pallas kernels for 15%

profile of v11, /device:TPU:0, one launch (start us, length us, event | category | flops | bytes accessed | tf_op | source)
XLA Modules:
  0.0 194.2 jit_solution(10366629724885562998)
XLA Ops:
  0.7 7.3 %qkv_projection.1 = (bf16[3,256,512]{2,1,0:T(8,128)(2,1)}, bf16[3,16,512]{2,1,0:T(8,128)(2,1)}) custom-call(bf16[256,2048]{1,0:T(8,128)(2,1)} %x_ref.3, f32[1,2048]{1,0:T(1,128)} %bitcast.63, bf16[3,2048,512]{2,1,0:T(8,128)(2,1)} %bitcast.59), custom_call_target="tpu_custom_call" | custom-call | tf_op jit(solution)/shard_map/qkv_projection/pallas_call | solution.py:68
  8.0 2.5 %collective-permute-start = (bf16[3,16,512]{2,1,0:T(8,128)(2,1)}, bf16[3,16,512]{2,1,0:T(8,128)(2,1)S(1)}, u32[]{:S(2)}, u32[]{:S(2)}) collective-permute-start(bf16[3,16,512]{2,1,0:T(8,128)(2,1)} %get-tuple-element.68), channel_id=1, source_target_pairs={{0,4},{4,8},{8,12},{12,16},{16,20},{20,24},{24,28},{1,5},{5,9},{9,... | collective-permute-start | bytes 147464 | tf_op jit(solution)/shard_map/ppermute | solution.py:612
  10.5 1.1 collective-permute-done.rim_ref
  11.6 1.1 copy-done.10
  12.7 3.0 %conv_states.1 = (bf16[3,256,512]{2,1,0:T(8,128)(2,1)S(1)}, bf16[672,128]{1,0:T(8,128)(2,1)S(1)}, bf16[576,128]{1,0:T(8,128)(2,1)S(1)}) custom-call(bf16[3,256,512]{2,1,0:T(8,128)(2,1)S(1)} %copy-done.10, bf16[3,16,512]{2,1,0:T(8,128)(2,1)S(1)} %collective-permute-done.rim_ref, f32[3,4,512]{2,1,0:T(4,128)S(1)} %bitcast.54, f32[4,256]{1,0:T(4,128)S(1)} %bitcast.51, ...), custom_call_target="tpu_custom_call" | custom-call | tf_op jit(solution)/shard_map/conv_states/pallas_call | solution.py:166
  15.7 0.9 copy-done.5
  17.3 6.1 %collective-permute-start.3 = (bf16[672,128]{1,0:T(8,128)(2,1)S(1)}, bf16[672,128]{1,0:T(8,128)(2,1)S(1)}, u32[]{:S(2)}, u32[]{:S(2)}) collective-permute-start(bf16[672,128]{1,0:T(8,128)(2,1)S(1)} %get-tuple-element.71), channel_id=1, source_target_pairs={{0,24},{4,28},{8,16},{12,20},{16,8},{20,12},{24,0},{28,4},{1,25},{... | collective-permute-start | bytes 516104 | tf_op jit(solution)/shard_map/ppermute | solution.py:442
  23.9 0.9 collective-permute-start.1
  24.8 3.8 %collective-permute-done.3 = bf16[672,128]{1,0:T(8,128)(2,1)S(1)} collective-permute-done((bf16[672,128]{1,0:T(8,128)(2,1)S(1)}, bf16[672,128]{1,0:T(8,128)(2,1)S(1)}, u32[]{:S(2)}, u32[]{:S(2)}) %collective-permute-start.3) | collective-permute-done | bytes 172064 | tf_op jit(solution)/shard_map/ppermute | solution.py:442
  28.6 2.5 %collective-permute-done.2 = bf16[672,128]{1,0:T(8,128)(2,1)S(1)} collective-permute-done((bf16[672,128]{1,0:T(8,128)(2,1)S(1)}, bf16[672,128]{1,0:T(8,128)(2,1)S(1)}, u32[]{:S(2)}, u32[]{:S(2)}) %collective-permute-start.2) | collective-permute-done | bytes 172064 | tf_op jit(solution)/shard_map/ppermute | solution.py:442
  31.5 1.1 stage_weights.2.me_ref.where_ref
  32.6 0.9 collective-permute-done.4.far_ref.far_routes.fwd_far
  33.5 1.1 copy-done.6
  34.7 3.6 %core_out.1 = (bf16[64,2048]{1,0:T(8,128)(2,1)S(1)}, bf16[64,2048]{1,0:T(8,128)(2,1)S(1)}, bf16[64,2048]{1,0:T(8,128)(2,1)S(1)}, bf16[64,2048]{1,0:T(8,128)(2,1)S(1)}) custom-call(s32[3]{0:T(128)S(1)} %stage_weights.2.me_ref.where_ref, bf16[3,256,512]{2,1,0:T(8,128)(2,1)S(1)} %copy-done.6, f32[4,256]{1,0:T(4,128)S(1)} %bitcast.52, f32[1,512]{1,0:T(1,128)S(1)} %bitcast.58, ...), custom_call_target="tpu_custom_call" | custom-call | tf_op jit(solution)/shard_map/core_out/pallas_call | solution.py:233
  38.4 1.7 collective-permute-start.8
  40.0 1.6 collective-permute-start.5
  41.6 2.6 %collective-permute-start.6 = (bf16[64,2048]{1,0:T(8,128)(2,1)S(1)}, bf16[64,2048]{1,0:T(8,128)(2,1)S(1)}, u32[]{:S(2)}, u32[]{:S(2)}) collective-permute-start(bf16[64,2048]{1,0:T(8,128)(2,1)S(1)} %get-tuple-element.74), channel_id=1, source_target_pairs={{0,2},{1,3},{2,0},{3,1},{4,6},{5,7},{6,4},{7,5},{8,10},{9,11},{10,... | collective-permute-start | bytes 786440 | tf_op jit(solution)/shard_map/ppermute | solution.py:448
  44.4 1.1 stage_weights.3.where_ref.me_ref
  45.6 7.5 %collective-permute-done.5.refs_1_ = bf16[64,2048]{1,0:T(8,128)(2,1)S(1)} collective-permute-done((bf16[64,2048]{1,0:T(8,128)(2,1)S(1)}, bf16[64,2048]{1,0:T(8,128)(2,1)S(1)}, u32[]{:S(2)}, u32[]{:S(2)}) %collective-permute-start.5) | collective-permute-done | bytes 262176 | tf_op jit(solution)/shard_map/ppermute | solution.py:448
  53.1 9.9 %collective-permute-done.6.refs_2_ = bf16[64,2048]{1,0:T(8,128)(2,1)S(1)} collective-permute-done((bf16[64,2048]{1,0:T(8,128)(2,1)S(1)}, bf16[64,2048]{1,0:T(8,128)(2,1)S(1)}, u32[]{:S(2)}, u32[]{:S(2)}) %collective-permute-start.6) | collective-permute-done | bytes 262176 | tf_op jit(solution)/shard_map/ppermute | solution.py:448
  63.0 0.8 moe_norm.1
  63.8 1.0 collective-permute-start.12
  64.8 2.5 %collective-permute-start.11 = (bf16[32,2048]{1,0:T(8,128)(2,1)S(1)}, bf16[32,2048]{1,0:T(8,128)(2,1)S(1)}, u32[]{:S(2)}, u32[]{:S(2)}) collective-permute-start(bf16[32,2048]{1,0:T(8,128)(2,1)S(1)} %get-tuple-element.87.refs_0_), channel_id=1, source_target_pairs={{0,3},{1,2},{2,1},{3,0},{4,7},{5,6},{6,5},{7,4},{8,11},{9,10},{10,... | collective-permute-start | bytes 393224 | tf_op jit(solution)/shard_map/ppermute | solution.py:448
  67.3 5.3 %collective-permute-start.10 = (bf16[32,2048]{1,0:T(8,128)(2,1)S(1)}, bf16[32,2048]{1,0:T(8,128)(2,1)S(1)}, u32[]{:S(2)}, u32[]{:S(2)}) collective-permute-start(bf16[32,2048]{1,0:T(8,128)(2,1)S(1)} %get-tuple-element.87.refs_0_), channel_id=1, source_target_pairs={{0,2},{1,3},{2,0},{3,1},{4,6},{5,7},{6,4},{7,5},{8,10},{9,11},{10,... | collective-permute-start | bytes 393224 | tf_op jit(solution)/shard_map/ppermute | solution.py:448
  72.7 7.3 %collective-permute-done.10.refs_2_ = bf16[32,2048]{1,0:T(8,128)(2,1)S(1)} collective-permute-done((bf16[32,2048]{1,0:T(8,128)(2,1)S(1)}, bf16[32,2048]{1,0:T(8,128)(2,1)S(1)}, u32[]{:S(2)}, u32[]{:S(2)}) %collective-permute-start.10) | collective-permute-done | bytes 131104 | tf_op jit(solution)/shard_map/ppermute | solution.py:448
  80.6 1.2 collective-permute-start.14
  82.2 2.6 %collective-permute-start.17 = (bf16[32,2048]{1,0:T(8,128)(2,1)S(1)}, bf16[32,2048]{1,0:T(8,128)(2,1)S(1)}, u32[]{:S(2)}, u32[]{:S(2)}) collective-permute-start(bf16[32,2048]{1,0:T(8,128)(2,1)S(1)} %get-tuple-element.91.refs_0_), channel_id=1, source_target_pairs={{0,3},{1,2},{2,1},{3,0},{4,7},{5,6},{6,5},{7,4},{8,11},{9,10},{10,... | collective-permute-start | bytes 393224 | tf_op jit(solution)/shard_map/ppermute | solution.py:448
  84.8 1.7 collective-permute-start.15
  86.6 3.7 %collective-permute-done.17.refs_3_ = bf16[32,2048]{1,0:T(8,128)(2,1)S(1)} collective-permute-done((bf16[32,2048]{1,0:T(8,128)(2,1)S(1)}, bf16[32,2048]{1,0:T(8,128)(2,1)S(1)}, u32[]{:S(2)}, u32[]{:S(2)}) %collective-permute-start.17) | collective-permute-done | bytes 131104 | tf_op jit(solution)/shard_map/ppermute | solution.py:448
  90.3 3.7 %collective-permute-done.16.refs_2_ = bf16[32,2048]{1,0:T(8,128)(2,1)S(1)} collective-permute-done((bf16[32,2048]{1,0:T(8,128)(2,1)S(1)}, bf16[32,2048]{1,0:T(8,128)(2,1)S(1)}, u32[]{:S(2)}, u32[]{:S(2)}) %collective-permute-start.16) | collective-permute-done | bytes 131104 | tf_op jit(solution)/shard_map/ppermute | solution.py:448
  95.2 1.7 collective-permute-start.25
  98.0 7.0 %expert_pieces.4 = (bf16[3,128,2048]{2,1,0:T(8,128)(2,1)S(1)}, bf16[3,128,2048]{2,1,0:T(8,128)(2,1)S(1)}) custom-call(s32[3]{0:T(128)S(1)} %stage_weights.3.where_ref.me_ref, bf16[4,672,128]{2,1,0:T(8,128)(2,1)S(1)} %pad_maximum_fusion.near_ref.near_routes.fwd_near, bf16[4,672,128]{2,1,0:T(8,128)(2,1)S(1)} %collective-permute-done.4.far_ref.far_routes.fwd_far, ...), custom_call_target="tpu_custom_call" | custom-call | flops 4831838208 | bytes 6291456 | tf_op jit(solution)/shard_map/expert_pieces/pallas_call | solution.py:415
  105.1 4.4 %collective-permute-done.25.refs_4_ = bf16[128,2048]{1,0:T(8,128)(2,1)S(1)} collective-permute-done((bf16[128,2048]{1,0:T(8,128)(2,1)S(1)}, bf16[128,2048]{1,0:T(8,128)(2,1)S(1)}, u32[]{:S(2)}, u32[]{:S(2)}) %collective-permute-start.25) | collective-permute-done | bytes 524320 | tf_op jit(solution)/shard_map/ppermute | solution.py:442
  109.5 1.4 collective-permute-done.24.refs_2_
  111.5 0.8 collective-permute-start.23
  112.3 1.1 collective-permute-start.22
  114.0 1.7 collective-permute-start.26
  115.7 7.0 %expert_pieces.5 = (bf16[3,128,2048]{2,1,0:T(8,128)(2,1)S(1)}, bf16[3,128,2048]{2,1,0:T(8,128)(2,1)S(1)}) custom-call(s32[3]{0:T(128)S(1)} %stage_weights.3.where_ref.me_ref, bf16[4,672,128]{2,1,0:T(8,128)(2,1)S(1)} %pad_maximum_fusion.near_ref.near_routes.fwd_near, bf16[4,672,128]{2,1,0:T(8,128)(2,1)S(1)} %collective-permute-done.4.far_ref.far_routes.fwd_far, ...), custom_call_target="tpu_custom_call" | custom-call | flops 4831838208 | bytes 6291456 | tf_op jit(solution)/shard_map/expert_pieces/pallas_call | solution.py:415
  122.7 3.1 %collective-permute-done.27 = bf16[64,2048]{1,0:T(8,128)(2,1)S(1)} collective-permute-done((bf16[64,2048]{1,0:T(8,128)(2,1)S(1)}, bf16[64,2048]{1,0:T(8,128)(2,1)S(1)}, u32[]{:S(2)}, u32[]{:S(2)}) %collective-permute-start.27) | collective-permute-done | bytes 262176 | tf_op jit(solution)/shard_map/ppermute | solution.py:442
  127.6 0.8 collective-permute-done.31.refs_1_
  128.3 2.7 %expert_pieces.6 = (bf16[1,128,2048]{2,1,0:T(8,128)(2,1)S(1)}, bf16[1,128,2048]{2,1,0:T(8,128)(2,1)S(1)}) custom-call(s32[3]{0:T(128)S(1)} %stage_weights.3.where_ref.me_ref, bf16[4,672,128]{2,1,0:T(8,128)(2,1)S(1)} %pad_maximum_fusion.near_ref.near_routes.fwd_near, bf16[4,672,128]{2,1,0:T(8,128)(2,1)S(1)} %collective-permute-done.4.far_ref.far_routes.fwd_far, ...), custom_call_target="tpu_custom_call" | custom-call | flops 1610612736 | bytes 2097152 | tf_op jit(solution)/shard_map/expert_pieces/pallas_call | solution.py:415
  132.2 2.7 %expert_pieces.7 = (bf16[1,128,2048]{2,1,0:T(8,128)(2,1)S(1)}, bf16[1,128,2048]{2,1,0:T(8,128)(2,1)S(1)}) custom-call(s32[3]{0:T(128)S(1)} %stage_weights.3.where_ref.me_ref, bf16[4,672,128]{2,1,0:T(8,128)(2,1)S(1)} %pad_maximum_fusion.near_ref.near_routes.fwd_near, bf16[4,672,128]{2,1,0:T(8,128)(2,1)S(1)} %collective-permute-done.4.far_ref.far_routes.fwd_far, ...), custom_call_target="tpu_custom_call" | custom-call | flops 1610612736 | bytes 2097152 | tf_op jit(solution)/shard_map/expert_pieces/pallas_call | solution.py:415
  135.4 1.4 collective-permute-start.33
  137.6 1.6 collective-permute-start.44
  139.2 1.0 collective-permute-start.45
  140.1 10.1 %collective-permute-done.33.refs_0_ = bf16[128,2048]{1,0:T(8,128)(2,1)S(1)} collective-permute-done((bf16[128,2048]{1,0:T(8,128)(2,1)S(1)}, bf16[128,2048]{1,0:T(8,128)(2,1)S(1)}, u32[]{:S(2)}, u32[]{:S(2)}) %collective-permute-start.33) | collective-permute-done | bytes 524320 | tf_op jit(solution)/shard_map/ppermute | solution.py:442
  150.2 1.4 collective-permute-done.34.refs_1_
  151.9 0.8 collective-permute-start.36
  152.7 1.1 collective-permute-start.35
  153.8 7.6 %collective-permute-done.44.refs_0_ = bf16[128,2048]{1,0:T(8,128)(2,1)S(1)} collective-permute-done((bf16[128,2048]{1,0:T(8,128)(2,1)S(1)}, bf16[128,2048]{1,0:T(8,128)(2,1)S(1)}, u32[]{:S(2)}, u32[]{:S(2)}) %collective-permute-start.44) | collective-permute-done | bytes 524320 | tf_op jit(solution)/shard_map/ppermute | solution.py:442
  161.4 1.4 collective-permute-done.45.refs_1_
  163.1 0.8 collective-permute-start.47
  163.9 1.1 collective-permute-start.46
  165.1 2.0 %collective-permute-done.36.refs_3_ = bf16[64,2048]{1,0:T(8,128)(2,1)S(1)} collective-permute-done((bf16[64,2048]{1,0:T(8,128)(2,1)S(1)}, bf16[64,2048]{1,0:T(8,128)(2,1)S(1)}, u32[]{:S(2)}, u32[]{:S(2)}) %collective-permute-start.36) | collective-permute-done | bytes 262176 | tf_op jit(solution)/shard_map/ppermute | solution.py:442
  167.1 1.4 collective-permute-done.35.refs_2_
  168.5 1.0 sum_terms.2
  169.9 2.8 %collective-permute-start.42 = (bf16[128,512]{1,0:T(8,128)(2,1)S(1)}, bf16[128,512]{1,0:T(8,128)(2,1)S(1)}, u32[]{:S(2)}, u32[]{:S(2)}) collective-permute-start(bf16[128,512]{1,0:T(8,128)(2,1)S(1)} %get-tuple-element.120), channel_id=1, source_target_pairs={{0,2},{1,3},{2,0},{3,1},{4,6},{5,7},{6,4},{7,5},{8,10},{9,11},{10,... | collective-permute-start | bytes 393224 | tf_op jit(solution)/shard_map/ppermute | solution.py:448
  172.8 1.2 collective-permute-start.43
  174.0 1.0 sum_terms.3
  175.0 3.2 %collective-permute-start.49 = (bf16[128,512]{1,0:T(8,128)(2,1)S(1)}, bf16[128,512]{1,0:T(8,128)(2,1)S(1)}, u32[]{:S(2)}, u32[]{:S(2)}) collective-permute-start(bf16[128,512]{1,0:T(8,128)(2,1)S(1)} %get-tuple-element.125), channel_id=1, source_target_pairs={{0,2},{1,3},{2,0},{3,1},{4,6},{5,7},{6,4},{7,5},{8,10},{9,11},{10,... | collective-permute-start | bytes 393224 | tf_op jit(solution)/shard_map/ppermute | solution.py:448
  178.2 1.2 collective-permute-start.50
  179.4 4.7 %core_grads.1 = (bf16[256,512]{1,0:T(8,128)(2,1)}, bf16[256,512]{1,0:T(8,128)(2,1)}, bf16[256,512]{1,0:T(8,128)(2,1)}) custom-call(s32[3]{0:T(128)S(1)} %stage_weights.3.where_ref.me_ref, bf16[3,256,512]{2,1,0:T(8,128)(2,1)S(1)} %copy-done.7, bf16[256,512]{1,0:T(8,128)(2,1)S(1)} %copy-done.9, f32[4,256]{1,0:T(4,128)S(1)} %bitcast.53, ...), custom_call_target="tpu_custom_call" | custom-call | tf_op jit(solution)/shard_map/core_grads/pallas_call | solution.py:278
  184.1 8.7 %collective-permute-done.49.refs_6_ = bf16[128,512]{1,0:T(8,128)(2,1)S(1)} collective-permute-done((bf16[128,512]{1,0:T(8,128)(2,1)S(1)}, bf16[128,512]{1,0:T(8,128)(2,1)S(1)}, u32[]{:S(2)}, u32[]{:S(2)}) %collective-permute-start.49) | collective-permute-done | bytes 131104 | tf_op jit(solution)/shard_map/ppermute | solution.py:448
  192.8 1.4 layer_out.1
  (115 shorter events, 11.7 us)
Async XLA Ops:
  0.6 10.9 %copy-start.8 = (bf16[256,512]{1,0:T(8,128)(2,1)S(1)}, bf16[256,512]{1,0:T(8,128)(2,1)}, u32[]{:S(2)}) copy-start(bf16[256,512]{1,0:T(8,128)(2,1)} %cot_ref.3) | copy-start | bytes 786436
  0.6 10.9 %copy-start.13 = (f32[256,4]{0,1:T(4,128)S(1)}, f32[256,4]{0,1:T(4,128)}, u32[]{:S(2)}) copy-start(f32[256,4]{0,1:T(4,128)} %param.18) | copy-start | bytes 12292
  0.7 10.9 %copy-start.14 = (f32[4,3,512]{2,0,1:T(4,128)S(1)}, f32[4,3,512]{2,0,1:T(4,128)}, u32[]{:S(2)}) copy-start(f32[4,3,512]{2,0,1:T(4,128)} %param.17) | copy-start | bytes 73732
  0.7 10.9 %copy-start.15 = (s32[256,8]{0,1:T(8,128)S(1)}, s32[256,8]{0,1:T(8,128)}, u32[]{:S(2)}) copy-start(s32[256,8]{0,1:T(8,128)} %param.22) | copy-start | bytes 24580
  0.7 10.9 %copy-start.16 = (f32[256,8]{0,1:T(8,128)S(1)}, f32[256,8]{0,1:T(8,128)}, u32[]{:S(2)}) copy-start(f32[256,8]{0,1:T(8,128)} %param.23) | copy-start | bytes 24580
  7.9 23.5 %copy-start.4 = (bf16[512,2048]{1,0:T(8,128)(2,1)S(1)}, bf16[512,2048]{1,0:T(8,128)(2,1)}, u32[]{:S(2)}) copy-start(bf16[512,2048]{1,0:T(8,128)(2,1)} %w_ref.1) | copy-start | bytes 6291460
  8.0 3.6 %collective-permute-start = (bf16[3,16,512]{2,1,0:T(8,128)(2,1)}, bf16[3,16,512]{2,1,0:T(8,128)(2,1)S(1)}, u32[]{:S(2)}, u32[]{:S(2)}) collective-permute-start(bf16[3,16,512]{2,1,0:T(8,128)(2,1)} %get-tuple-element.68), channel_id=1, source_target_pairs={{0,4},{4,8},{8,12},{12,16},{16,20},{20,24},{24,28},{1,5},{5,9},{9,... | collective-permute-start | bytes 147464 | tf_op jit(solution)/shard_map/ppermute | solution.py:612
  17.3 11.4 %collective-permute-start.3 = (bf16[672,128]{1,0:T(8,128)(2,1)S(1)}, bf16[672,128]{1,0:T(8,128)(2,1)S(1)}, u32[]{:S(2)}, u32[]{:S(2)}) collective-permute-start(bf16[672,128]{1,0:T(8,128)(2,1)S(1)} %get-tuple-element.71), channel_id=1, source_target_pairs={{0,24},{4,28},{8,16},{12,20},{16,8},{20,12},{24,0},{28,4},{1,25},{... | collective-permute-start | bytes 516104 | tf_op jit(solution)/shard_map/ppermute | solution.py:442
  23.4 7.8 %collective-permute-start.2 = (bf16[672,128]{1,0:T(8,128)(2,1)S(1)}, bf16[672,128]{1,0:T(8,128)(2,1)S(1)}, u32[]{:S(2)}, u32[]{:S(2)}) collective-permute-start(bf16[672,128]{1,0:T(8,128)(2,1)S(1)} %get-tuple-element.71), channel_id=1, source_target_pairs={{0,16},{4,20},{8,24},{12,28},{16,0},{20,4},{24,8},{28,12},{1,17},{... | collective-permute-start | bytes 516104 | tf_op jit(solution)/shard_map/ppermute | solution.py:442
  23.9 7.3 %collective-permute-start.1 = (bf16[672,128]{1,0:T(8,128)(2,1)S(1)}, bf16[672,128]{1,0:T(8,128)(2,1)S(1)}, u32[]{:S(2)}, u32[]{:S(2)}) collective-permute-start(bf16[672,128]{1,0:T(8,128)(2,1)S(1)} %get-tuple-element.71), channel_id=1, source_target_pairs={{0,8},{4,12},{8,0},{12,4},{16,24},{20,28},{24,16},{28,20},{1,9},{5... | collective-permute-start | bytes 516104 | tf_op jit(solution)/shard_map/ppermute | solution.py:442
  31.3 2.2 %collective-permute-start.4 = (bf16[4,672,128]{2,1,0:T(8,128)(2,1)S(1)}, bf16[4,672,128]{2,1,0:T(8,128)(2,1)S(1)}, u32[]{:S(2)}, u32[]{:S(2)}) collective-permute-start(bf16[4,672,128]{2,1,0:T(8,128)(2,1)S(1)} %pad_maximum_fusion.near_ref.near_routes.fwd_near), channel_id=1, source_target_pairs={{0,4},{4,0},{8,12},{12,8},{16,20},{20,16},{24,28},{28,24},{1,5},{5... | collective-permute-start | bytes 2064392 | tf_op jit(solution)/shard_map/ppermute | solution.py:442
  31.5 12.9 %copy-start.2 = (bf16[1,512,2048]{2,1,0:T(8,128)(2,1)S(1)}, bf16[1,512,2048]{2,1,0:T(8,128)(2,1)}, u32[]{:S(2)}) copy-start(bf16[1,512,2048]{2,1,0:T(8,128)(2,1)} %down_ref.7) | copy-start | bytes 6291460
  34.7 9.8 %copy-start = (bf16[1,2048,512]{2,1,0:T(8,128)(2,1)S(1)}, bf16[1,2048,512]{2,1,0:T(8,128)(2,1)}, u32[]{:S(2)}) copy-start(bf16[1,2048,512]{2,1,0:T(8,128)(2,1)} %gate_ref.7) | copy-start | bytes 6291460
  34.7 9.8 %copy-start.1 = (bf16[1,2048,512]{2,1,0:T(8,128)(2,1)S(1)}, bf16[1,2048,512]{2,1,0:T(8,128)(2,1)}, u32[]{:S(2)}) copy-start(bf16[1,2048,512]{2,1,0:T(8,128)(2,1)} %up_ref.7) | copy-start | bytes 6291460
  38.3 7.3 %copy-start.12 = (bf16[576,128]{1,0:T(8,128)(2,1)S(1)}, bf16[576,128]{1,0:T(8,128)(2,1)}, u32[]{:S(2)}) copy-start(bf16[576,128]{1,0:T(8,128)(2,1)} %copy-done.11) | copy-start | bytes 442372
  38.3 24.6 %copy-start.3 = (bf16[256,2048]{1,0:T(8,128)(2,1)S(1)}, bf16[256,2048]{1,0:T(8,128)(2,1)}, u32[]{:S(2)}) copy-start(bf16[256,2048]{1,0:T(8,128)(2,1)} %x_ref.3) | copy-start | bytes 3145732
  38.3 24.6 %copy-start.17 = (f32[2048]{0:T(1024)S(1)}, f32[2048]{0:T(1024)}, u32[]{:S(2)}) copy-start(f32[2048]{0:T(1024)} %param.21) | copy-start | bytes 24580
  38.4 7.2 %collective-permute-start.8 = (bf16[1,576,128]{2,1,0:T(8,128)(2,1)}, bf16[1,576,128]{2,1,0:T(8,128)(2,1)S(1)}, u32[]{:S(2)}, u32[]{:S(2)}) collective-permute-start(bf16[1,576,128]{2,1,0:T(8,128)(2,1)} %bitcast.49), channel_id=1, source_target_pairs={{0,8},{4,12},{8,0},{12,4},{16,24},{20,28},{24,16},{28,20},{1,9},{5... | collective-permute-start | bytes 442376 | tf_op jit(solution)/shard_map/ppermute | solution.py:442
  40.0 13.1 %collective-permute-start.5 = (bf16[64,2048]{1,0:T(8,128)(2,1)S(1)}, bf16[64,2048]{1,0:T(8,128)(2,1)S(1)}, u32[]{:S(2)}, u32[]{:S(2)}) collective-permute-start(bf16[64,2048]{1,0:T(8,128)(2,1)S(1)} %get-tuple-element.73), channel_id=1, source_target_pairs={{0,1},{1,0},{2,3},{3,2},{4,5},{5,4},{6,7},{7,6},{8,9},{9,8},{10,11... | collective-permute-start | bytes 786440 | tf_op jit(solution)/shard_map/ppermute | solution.py:448
  41.6 21.4 %collective-permute-start.6 = (bf16[64,2048]{1,0:T(8,128)(2,1)S(1)}, bf16[64,2048]{1,0:T(8,128)(2,1)S(1)}, u32[]{:S(2)}, u32[]{:S(2)}) collective-permute-start(bf16[64,2048]{1,0:T(8,128)(2,1)S(1)} %get-tuple-element.74), channel_id=1, source_target_pairs={{0,2},{1,3},{2,0},{3,1},{4,6},{5,7},{6,4},{7,5},{8,10},{9,11},{10,... | collective-permute-start | bytes 786440 | tf_op jit(solution)/shard_map/ppermute | solution.py:448
  44.2 18.8 %collective-permute-start.7 = (bf16[64,2048]{1,0:T(8,128)(2,1)S(1)}, bf16[64,2048]{1,0:T(8,128)(2,1)S(1)}, u32[]{:S(2)}, u32[]{:S(2)}) collective-permute-start(bf16[64,2048]{1,0:T(8,128)(2,1)S(1)} %get-tuple-element.75), channel_id=1, source_target_pairs={{0,3},{1,2},{2,1},{3,0},{4,7},{5,6},{6,5},{7,4},{8,11},{9,10},{10,... | collective-permute-start | bytes 786440 | tf_op jit(solution)/shard_map/ppermute | solution.py:448
  63.8 8.8 %collective-permute-start.12 = (bf16[2,576,128]{2,1,0:T(8,128)(2,1)S(1)}, bf16[2,576,128]{2,1,0:T(8,128)(2,1)S(1)}, u32[]{:S(2)}, u32[]{:S(2)}) collective-permute-start(bf16[2,576,128]{2,1,0:T(8,128)(2,1)S(1)} %pad_maximum_fusion.5), channel_id=1, source_target_pairs={{0,16},{4,20},{8,24},{12,28},{16,0},{20,4},{24,8},{28,12},{1,17},{... | collective-permute-start | bytes 884744 | tf_op jit(solution)/shard_map/ppermute | solution.py:442
  64.8 7.9 %collective-permute-start.11 = (bf16[32,2048]{1,0:T(8,128)(2,1)S(1)}, bf16[32,2048]{1,0:T(8,128)(2,1)S(1)}, u32[]{:S(2)}, u32[]{:S(2)}) collective-permute-start(bf16[32,2048]{1,0:T(8,128)(2,1)S(1)} %get-tuple-element.87.refs_0_), channel_id=1, source_target_pairs={{0,3},{1,2},{2,1},{3,0},{4,7},{5,6},{6,5},{7,4},{8,11},{9,10},{10,... | collective-permute-start | bytes 393224 | tf_op jit(solution)/shard_map/ppermute | solution.py:448
  67.3 12.7 %collective-permute-start.10 = (bf16[32,2048]{1,0:T(8,128)(2,1)S(1)}, bf16[32,2048]{1,0:T(8,128)(2,1)S(1)}, u32[]{:S(2)}, u32[]{:S(2)}) collective-permute-start(bf16[32,2048]{1,0:T(8,128)(2,1)S(1)} %get-tuple-element.87.refs_0_), channel_id=1, source_target_pairs={{0,2},{1,3},{2,0},{3,1},{4,6},{5,7},{6,4},{7,5},{8,10},{9,11},{10,... | collective-permute-start | bytes 393224 | tf_op jit(solution)/shard_map/ppermute | solution.py:448
  72.5 7.5 %collective-permute-start.9 = (bf16[32,2048]{1,0:T(8,128)(2,1)S(1)}, bf16[32,2048]{1,0:T(8,128)(2,1)S(1)}, u32[]{:S(2)}, u32[]{:S(2)}) collective-permute-start(bf16[32,2048]{1,0:T(8,128)(2,1)S(1)} %get-tuple-element.87.refs_0_), channel_id=1, source_target_pairs={{0,1},{1,0},{2,3},{3,2},{4,5},{5,4},{6,7},{7,6},{8,9},{9,8},{10,11... | collective-permute-start | bytes 393224 | tf_op jit(solution)/shard_map/ppermute | solution.py:448
  80.6 14.0 %collective-permute-start.14 = (bf16[128,2048]{1,0:T(8,128)(2,1)S(1)}, bf16[128,2048]{1,0:T(8,128)(2,1)S(1)}, u32[]{:S(2)}, u32[]{:S(2)}) collective-permute-start(bf16[128,2048]{1,0:T(8,128)(2,1)S(1)} %join_rows.2.refs_0_), channel_id=1, source_target_pairs={{0,16},{4,20},{8,24},{12,28},{16,0},{20,4},{24,8},{28,12},{1,17},{... | collective-permute-start | bytes 1572872 | tf_op jit(solution)/shard_map/ppermute | solution.py:442
  81.8 12.8 %collective-permute-start.13 = (bf16[128,2048]{1,0:T(8,128)(2,1)S(1)}, bf16[128,2048]{1,0:T(8,128)(2,1)S(1)}, u32[]{:S(2)}, u32[]{:S(2)}) collective-permute-start(bf16[128,2048]{1,0:T(8,128)(2,1)S(1)} %join_rows.2.refs_0_), channel_id=1, source_target_pairs={{0,8},{4,12},{8,0},{12,4},{16,24},{20,28},{24,16},{28,20},{1,9},{5... | collective-permute-start | bytes 1572872 | tf_op jit(solution)/shard_map/ppermute | solution.py:442
  82.2 8.1 %collective-permute-start.17 = (bf16[32,2048]{1,0:T(8,128)(2,1)S(1)}, bf16[32,2048]{1,0:T(8,128)(2,1)S(1)}, u32[]{:S(2)}, u32[]{:S(2)}) collective-permute-start(bf16[32,2048]{1,0:T(8,128)(2,1)S(1)} %get-tuple-element.91.refs_0_), channel_id=1, source_target_pairs={{0,3},{1,2},{2,1},{3,0},{4,7},{5,6},{6,5},{7,4},{8,11},{9,10},{10,... | collective-permute-start | bytes 393224 | tf_op jit(solution)/shard_map/ppermute | solution.py:448
  84.8 9.1 %collective-permute-start.16 = (bf16[32,2048]{1,0:T(8,128)(2,1)S(1)}, bf16[32,2048]{1,0:T(8,128)(2,1)S(1)}, u32[]{:S(2)}, u32[]{:S(2)}) collective-permute-start(bf16[32,2048]{1,0:T(8,128)(2,1)S(1)} %get-tuple-element.91.refs_0_), channel_id=1, source_target_pairs={{0,2},{1,3},{2,0},{3,1},{4,6},{5,7},{6,4},{7,5},{8,10},{9,11},{10,... | collective-permute-start | bytes 393224 | tf_op jit(solution)/shard_map/ppermute | solution.py:448
  84.8 9.1 %collective-permute-start.15 = (bf16[32,2048]{1,0:T(8,128)(2,1)S(1)}, bf16[32,2048]{1,0:T(8,128)(2,1)S(1)}, u32[]{:S(2)}, u32[]{:S(2)}) collective-permute-start(bf16[32,2048]{1,0:T(8,128)(2,1)S(1)} %get-tuple-element.91.refs_0_), channel_id=1, source_target_pairs={{0,1},{1,0},{2,3},{3,2},{4,5},{5,4},{6,7},{7,6},{8,9},{9,8},{10,11... | collective-permute-start | bytes 393224 | tf_op jit(solution)/shard_map/ppermute | solution.py:448
  94.6 3.1 %collective-permute-start.18 = (bf16[128,2048]{1,0:T(8,128)(2,1)S(1)}, bf16[128,2048]{1,0:T(8,128)(2,1)S(1)}, u32[]{:S(2)}, u32[]{:S(2)}) collective-permute-start(bf16[128,2048]{1,0:T(8,128)(2,1)S(1)} %join_rows.2.refs_0_), channel_id=1, source_target_pairs={{0,4},{4,0},{8,12},{12,8},{16,20},{20,16},{24,28},{28,24},{1,5},{5... | collective-permute-start | bytes 1572872 | tf_op jit(solution)/shard_map/ppermute | solution.py:442
  94.6 3.0 %collective-permute-start.19 = (bf16[128,2048]{1,0:T(8,128)(2,1)S(1)}, bf16[128,2048]{1,0:T(8,128)(2,1)S(1)}, u32[]{:S(2)}, u32[]{:S(2)}) collective-permute-start(bf16[128,2048]{1,0:T(8,128)(2,1)S(1)} %collective-permute-done.13.refs_2_), channel_id=1, source_target_pairs={{0,4},{4,0},{8,12},{12,8},{16,20},{20,16},{24,28},{28,24},{1,5},{5... | collective-permute-start | bytes 1572872 | tf_op jit(solution)/shard_map/ppermute | solution.py:442
  95.1 2.9 %collective-permute-start.20 = (bf16[128,2048]{1,0:T(8,128)(2,1)S(1)}, bf16[128,2048]{1,0:T(8,128)(2,1)S(1)}, u32[]{:S(2)}, u32[]{:S(2)}) collective-permute-start(bf16[128,2048]{1,0:T(8,128)(2,1)S(1)} %collective-permute-done.14.refs_4_), channel_id=1, source_target_pairs={{0,4},{4,0},{8,12},{12,8},{16,20},{20,16},{24,28},{28,24},{1,5},{5... | collective-permute-start | bytes 1572872 | tf_op jit(solution)/shard_map/ppermute | solution.py:442
  95.2 14.3 %collective-permute-start.25 = (bf16[128,2048]{1,0:T(8,128)(2,1)S(1)}, bf16[128,2048]{1,0:T(8,128)(2,1)S(1)}, u32[]{:S(2)}, u32[]{:S(2)}) collective-permute-start(bf16[128,2048]{1,0:T(8,128)(2,1)S(1)} %join_rows.3.refs_0_), channel_id=1, source_target_pairs={{0,16},{4,20},{8,24},{12,28},{16,0},{20,4},{24,8},{28,12},{1,17},{... | collective-permute-start | bytes 1572872 | tf_op jit(solution)/shard_map/ppermute | solution.py:442
  96.9 14.0 %collective-permute-start.24 = (bf16[128,2048]{1,0:T(8,128)(2,1)S(1)}, bf16[128,2048]{1,0:T(8,128)(2,1)S(1)}, u32[]{:S(2)}, u32[]{:S(2)}) collective-permute-start(bf16[128,2048]{1,0:T(8,128)(2,1)S(1)} %join_rows.3.refs_0_), channel_id=1, source_target_pairs={{0,8},{4,12},{8,0},{12,4},{16,24},{20,28},{24,16},{28,20},{1,9},{5... | collective-permute-start | bytes 1572872 | tf_op jit(solution)/shard_map/ppermute | solution.py:442
  110.9 2.5 %collective-permute-start.28 = (bf16[128,2048]{1,0:T(8,128)(2,1)S(1)}, bf16[128,2048]{1,0:T(8,128)(2,1)S(1)}, u32[]{:S(2)}, u32[]{:S(2)}) collective-permute-start(bf16[128,2048]{1,0:T(8,128)(2,1)S(1)} %join_rows.3.refs_0_), channel_id=1, source_target_pairs={{0,4},{4,0},{8,12},{12,8},{16,20},{20,16},{24,28},{28,24},{1,5},{5... | collective-permute-start | bytes 1572872 | tf_op jit(solution)/shard_map/ppermute | solution.py:442
  110.9 3.1 %collective-permute-start.29 = (bf16[128,2048]{1,0:T(8,128)(2,1)S(1)}, bf16[128,2048]{1,0:T(8,128)(2,1)S(1)}, u32[]{:S(2)}, u32[]{:S(2)}) collective-permute-start(bf16[128,2048]{1,0:T(8,128)(2,1)S(1)} %collective-permute-done.24.refs_2_), channel_id=1, source_target_pairs={{0,4},{4,0},{8,12},{12,8},{16,20},{20,16},{24,28},{28,24},{1,5},{5... | collective-permute-start | bytes 1572872 | tf_op jit(solution)/shard_map/ppermute | solution.py:442
  111.4 4.3 %collective-permute-start.30 = (bf16[128,2048]{1,0:T(8,128)(2,1)S(1)}, bf16[128,2048]{1,0:T(8,128)(2,1)S(1)}, u32[]{:S(2)}, u32[]{:S(2)}) collective-permute-start(bf16[128,2048]{1,0:T(8,128)(2,1)S(1)} %collective-permute-done.25.refs_4_), channel_id=1, source_target_pairs={{0,4},{4,0},{8,12},{12,8},{16,20},{20,16},{24,28},{28,24},{1,5},{5... | collective-permute-start | bytes 1572872 | tf_op jit(solution)/shard_map/ppermute | solution.py:442
  111.5 11.3 %collective-permute-start.23 = (bf16[64,2048]{1,0:T(8,128)(2,1)S(1)}, bf16[64,2048]{1,0:T(8,128)(2,1)S(1)}, u32[]{:S(2)}, u32[]{:S(2)}) collective-permute-start(bf16[64,2048]{1,0:T(8,128)(2,1)S(1)} %slice.145), channel_id=1, source_target_pairs={{0,8},{4,12},{8,0},{12,4},{16,24},{20,28},{24,16},{28,20},{1,9},{5... | collective-permute-start | bytes 786440 | tf_op jit(solution)/shard_map/ppermute | solution.py:442
  112.3 10.5 %collective-permute-start.22 = (bf16[64,2048]{1,0:T(8,128)(2,1)S(1)}, bf16[64,2048]{1,0:T(8,128)(2,1)S(1)}, u32[]{:S(2)}, u32[]{:S(2)}) collective-permute-start(bf16[64,2048]{1,0:T(8,128)(2,1)S(1)} %slice.144), channel_id=1, source_target_pairs={{0,16},{4,20},{8,24},{12,28},{16,0},{20,4},{24,8},{28,12},{1,17},{... | collective-permute-start | bytes 786440 | tf_op jit(solution)/shard_map/ppermute | solution.py:442
  113.4 12.4 %collective-permute-start.27 = (bf16[64,2048]{1,0:T(8,128)(2,1)S(1)}, bf16[64,2048]{1,0:T(8,128)(2,1)S(1)}, u32[]{:S(2)}, u32[]{:S(2)}) collective-permute-start(bf16[64,2048]{1,0:T(8,128)(2,1)S(1)} %slice.147), channel_id=1, source_target_pairs={{0,8},{4,12},{8,0},{12,4},{16,24},{20,28},{24,16},{28,20},{1,9},{5... | collective-permute-start | bytes 786440 | tf_op jit(solution)/shard_map/ppermute | solution.py:442
  114.0 12.3 %collective-permute-start.26 = (bf16[64,2048]{1,0:T(8,128)(2,1)S(1)}, bf16[64,2048]{1,0:T(8,128)(2,1)S(1)}, u32[]{:S(2)}, u32[]{:S(2)}) collective-permute-start(bf16[64,2048]{1,0:T(8,128)(2,1)S(1)} %slice.146), channel_id=1, source_target_pairs={{0,16},{4,20},{8,24},{12,28},{16,0},{20,4},{24,8},{28,12},{1,17},{... | collective-permute-start | bytes 786440 | tf_op jit(solution)/shard_map/ppermute | solution.py:442
  126.4 2.0 %collective-permute-start.31 = (bf16[128,2048]{1,0:T(8,128)(2,1)S(1)}, bf16[128,2048]{1,0:T(8,128)(2,1)S(1)}, u32[]{:S(2)}, u32[]{:S(2)}) collective-permute-start(bf16[128,2048]{1,0:T(8,128)(2,1)S(1)} %constant_dynamic-update-slice_fusion.2.refs_0_), channel_id=1, source_target_pairs={{0,4},{4,0},{8,12},{12,8},{16,20},{20,16},{24,28},{28,24},{1,5},{5... | collective-permute-start | bytes 1572872 | tf_op jit(solution)/shard_map/ppermute | solution.py:442
  126.4 4.8 %collective-permute-start.39 = (bf16[4,576,128]{2,1,0:T(8,128)(2,1)S(1)}, bf16[4,576,128]{2,1,0:T(8,128)(2,1)S(1)}, u32[]{:S(2)}, u32[]{:S(2)}) collective-permute-start(bf16[4,576,128]{2,1,0:T(8,128)(2,1)S(1)} %constant_dynamic-update-slice_fusion.bwd_near), channel_id=1, source_target_pairs={{0,4},{4,0},{8,12},{12,8},{16,20},{20,16},{24,28},{28,24},{1,5},{5... | collective-permute-start | bytes 1769480 | tf_op jit(solution)/shard_map/ppermute | solution.py:442
  126.9 8.3 %collective-permute-start.21 = (bf16[3,128,2048]{2,1,0:T(8,128)(2,1)S(1)}, bf16[3,128,2048]{2,1,0:T(8,128)(2,1)S(1)}, u32[]{:S(2)}, u32[]{:S(2)}) collective-permute-start(bf16[3,128,2048]{2,1,0:T(8,128)(2,1)S(1)} %get-tuple-element.96), channel_id=1, source_target_pairs={{0,4},{4,0},{8,12},{12,8},{16,20},{20,16},{24,28},{28,24},{1,5},{5... | collective-permute-start | bytes 4718600 | tf_op jit(solution)/shard_map/ppermute | solution.py:442
  127.1 5.1 %collective-permute-start.37 = (bf16[128,2048]{1,0:T(8,128)(2,1)S(1)}, bf16[128,2048]{1,0:T(8,128)(2,1)S(1)}, u32[]{:S(2)}, u32[]{:S(2)}) collective-permute-start(bf16[128,2048]{1,0:T(8,128)(2,1)S(1)} %constant_dynamic-update-slice_fusion.4.refs_0_), channel_id=1, source_target_pairs={{0,4},{4,0},{8,12},{12,8},{16,20},{20,16},{24,28},{28,24},{1,5},{5... | collective-permute-start | bytes 1572872 | tf_op jit(solution)/shard_map/ppermute | solution.py:442
  131.0 4.0 %collective-permute-start.32 = (bf16[1,128,2048]{2,1,0:T(8,128)(2,1)S(1)}, bf16[1,128,2048]{2,1,0:T(8,128)(2,1)S(1)}, u32[]{:S(2)}, u32[]{:S(2)}) collective-permute-start(bf16[1,128,2048]{2,1,0:T(8,128)(2,1)S(1)} %get-tuple-element.104), channel_id=1, source_target_pairs={{0,4},{4,0},{8,12},{12,8},{16,20},{20,16},{24,28},{28,24},{1,5},{5... | collective-permute-start | bytes 1572872 | tf_op jit(solution)/shard_map/ppermute | solution.py:442
  131.2 6.2 %collective-permute-start.40 = (bf16[3,128,2048]{2,1,0:T(8,128)(2,1)S(1)}, bf16[3,128,2048]{2,1,0:T(8,128)(2,1)S(1)}, u32[]{:S(2)}, u32[]{:S(2)}) collective-permute-start(bf16[3,128,2048]{2,1,0:T(8,128)(2,1)S(1)} %get-tuple-element.113), channel_id=1, source_target_pairs={{0,4},{4,0},{8,12},{12,8},{16,20},{20,16},{24,28},{28,24},{1,5},{5... | collective-permute-start | bytes 4718600 | tf_op jit(solution)/shard_map/ppermute | solution.py:442
  134.9 2.4 %collective-permute-start.38 = (bf16[1,128,2048]{2,1,0:T(8,128)(2,1)S(1)}, bf16[1,128,2048]{2,1,0:T(8,128)(2,1)S(1)}, u32[]{:S(2)}, u32[]{:S(2)}) collective-permute-start(bf16[1,128,2048]{2,1,0:T(8,128)(2,1)S(1)} %get-tuple-element.110), channel_id=1, source_target_pairs={{0,4},{4,0},{8,12},{12,8},{16,20},{20,16},{24,28},{28,24},{1,5},{5... | collective-permute-start | bytes 1572872 | tf_op jit(solution)/shard_map/ppermute | solution.py:442
  135.4 14.8 %collective-permute-start.33 = (bf16[128,2048]{1,0:T(8,128)(2,1)S(1)}, bf16[128,2048]{1,0:T(8,128)(2,1)S(1)}, u32[]{:S(2)}, u32[]{:S(2)}) collective-permute-start(bf16[128,2048]{1,0:T(8,128)(2,1)S(1)} %pad_maximum_fusion.1), channel_id=1, source_target_pairs={{0,8},{4,12},{8,0},{12,4},{16,24},{20,28},{24,16},{28,20},{1,9},{5... | collective-permute-start | bytes 1572872 | tf_op jit(solution)/shard_map/ppermute | solution.py:442
  136.8 14.8 %collective-permute-start.34 = (bf16[128,2048]{1,0:T(8,128)(2,1)S(1)}, bf16[128,2048]{1,0:T(8,128)(2,1)S(1)}, u32[]{:S(2)}, u32[]{:S(2)}) collective-permute-start(bf16[128,2048]{1,0:T(8,128)(2,1)S(1)} %pad_maximum_fusion.2), channel_id=1, source_target_pairs={{0,16},{4,20},{8,24},{12,28},{16,0},{20,4},{24,8},{28,12},{1,17},{... | collective-permute-start | bytes 1572872 | tf_op jit(solution)/shard_map/ppermute | solution.py:442
  137.6 23.9 %collective-permute-start.44 = (bf16[128,2048]{1,0:T(8,128)(2,1)S(1)}, bf16[128,2048]{1,0:T(8,128)(2,1)S(1)}, u32[]{:S(2)}, u32[]{:S(2)}) collective-permute-start(bf16[128,2048]{1,0:T(8,128)(2,1)S(1)} %pad_maximum_fusion.3), channel_id=1, source_target_pairs={{0,8},{4,12},{8,0},{12,4},{16,24},{20,28},{24,16},{28,20},{1,9},{5... | collective-permute-start | bytes 1572872 | tf_op jit(solution)/shard_map/ppermute | solution.py:442
  139.2 23.7 %collective-permute-start.45 = (bf16[128,2048]{1,0:T(8,128)(2,1)S(1)}, bf16[128,2048]{1,0:T(8,128)(2,1)S(1)}, u32[]{:S(2)}, u32[]{:S(2)}) collective-permute-start(bf16[128,2048]{1,0:T(8,128)(2,1)S(1)} %pad_maximum_fusion.4), channel_id=1, source_target_pairs={{0,16},{4,20},{8,24},{12,28},{16,0},{20,4},{24,8},{28,12},{1,17},{... | collective-permute-start | bytes 1572872 | tf_op jit(solution)/shard_map/ppermute | solution.py:442
  151.9 15.2 %collective-permute-start.36 = (bf16[64,2048]{1,0:T(8,128)(2,1)S(1)}, bf16[64,2048]{1,0:T(8,128)(2,1)S(1)}, u32[]{:S(2)}, u32[]{:S(2)}) collective-permute-start(bf16[64,2048]{1,0:T(8,128)(2,1)S(1)} %get-tuple-element.134), channel_id=1, source_target_pairs={{0,8},{4,12},{8,0},{12,4},{16,24},{20,28},{24,16},{28,20},{1,9},{5... | collective-permute-start | bytes 786440 | tf_op jit(solution)/shard_map/ppermute | solution.py:442
  152.7 15.8 %collective-permute-start.35 = (bf16[64,2048]{1,0:T(8,128)(2,1)S(1)}, bf16[64,2048]{1,0:T(8,128)(2,1)S(1)}, u32[]{:S(2)}, u32[]{:S(2)}) collective-permute-start(bf16[64,2048]{1,0:T(8,128)(2,1)S(1)} %get-tuple-element.135), channel_id=1, source_target_pairs={{0,16},{4,20},{8,24},{12,28},{16,0},{20,4},{24,8},{28,12},{1,17},{... | collective-permute-start | bytes 786440 | tf_op jit(solution)/shard_map/ppermute | solution.py:442
  163.1 10.8 %collective-permute-start.47 = (bf16[64,2048]{1,0:T(8,128)(2,1)S(1)}, bf16[64,2048]{1,0:T(8,128)(2,1)S(1)}, u32[]{:S(2)}, u32[]{:S(2)}) collective-permute-start(bf16[64,2048]{1,0:T(8,128)(2,1)S(1)} %get-tuple-element.130), channel_id=1, source_target_pairs={{0,8},{4,12},{8,0},{12,4},{16,24},{20,28},{24,16},{28,20},{1,9},{5... | collective-permute-start | bytes 786440 | tf_op jit(solution)/shard_map/ppermute | solution.py:442
  163.9 10.0 %collective-permute-start.46 = (bf16[64,2048]{1,0:T(8,128)(2,1)S(1)}, bf16[64,2048]{1,0:T(8,128)(2,1)S(1)}, u32[]{:S(2)}, u32[]{:S(2)}) collective-permute-start(bf16[64,2048]{1,0:T(8,128)(2,1)S(1)} %get-tuple-element.131), channel_id=1, source_target_pairs={{0,16},{4,20},{8,24},{12,28},{16,0},{20,4},{24,8},{28,12},{1,17},{... | collective-permute-start | bytes 786440 | tf_op jit(solution)/shard_map/ppermute | solution.py:442
  169.5 8.7 %collective-permute-start.41 = (bf16[128,512]{1,0:T(8,128)(2,1)S(1)}, bf16[128,512]{1,0:T(8,128)(2,1)S(1)}, u32[]{:S(2)}, u32[]{:S(2)}) collective-permute-start(bf16[128,512]{1,0:T(8,128)(2,1)S(1)} %get-tuple-element.119), channel_id=1, source_target_pairs={{0,1},{1,0},{2,3},{3,2},{4,5},{5,4},{6,7},{7,6},{8,9},{9,8},{10,11... | collective-permute-start | bytes 393224 | tf_op jit(solution)/shard_map/ppermute | solution.py:448
  169.9 14.2 %collective-permute-start.42 = (bf16[128,512]{1,0:T(8,128)(2,1)S(1)}, bf16[128,512]{1,0:T(8,128)(2,1)S(1)}, u32[]{:S(2)}, u32[]{:S(2)}) collective-permute-start(bf16[128,512]{1,0:T(8,128)(2,1)S(1)} %get-tuple-element.120), channel_id=1, source_target_pairs={{0,2},{1,3},{2,0},{3,1},{4,6},{5,7},{6,4},{7,5},{8,10},{9,11},{10,... | collective-permute-start | bytes 393224 | tf_op jit(solution)/shard_map/ppermute | solution.py:448
  172.8 11.4 %collective-permute-start.43 = (bf16[128,512]{1,0:T(8,128)(2,1)S(1)}, bf16[128,512]{1,0:T(8,128)(2,1)S(1)}, u32[]{:S(2)}, u32[]{:S(2)}) collective-permute-start(bf16[128,512]{1,0:T(8,128)(2,1)S(1)} %get-tuple-element.121), channel_id=1, source_target_pairs={{0,3},{1,2},{2,1},{3,0},{4,7},{5,6},{6,5},{7,4},{8,11},{9,10},{10,... | collective-permute-start | bytes 393224 | tf_op jit(solution)/shard_map/ppermute | solution.py:448
  174.0 5.5 %copy-start.7 = (bf16[3,256,512]{2,1,0:T(8,128)(2,1)S(1)}, bf16[3,256,512]{2,1,0:T(8,128)(2,1)}, u32[]{:S(2)}) copy-start(bf16[3,256,512]{2,1,0:T(8,128)(2,1)} %copy-done.5) | copy-start | bytes 2359300
  175.0 9.2 %collective-permute-start.48 = (bf16[128,512]{1,0:T(8,128)(2,1)S(1)}, bf16[128,512]{1,0:T(8,128)(2,1)S(1)}, u32[]{:S(2)}, u32[]{:S(2)}) collective-permute-start(bf16[128,512]{1,0:T(8,128)(2,1)S(1)} %get-tuple-element.124), channel_id=1, source_target_pairs={{0,1},{1,0},{2,3},{3,2},{4,5},{5,4},{6,7},{7,6},{8,9},{9,8},{10,11... | collective-permute-start | bytes 393224 | tf_op jit(solution)/shard_map/ppermute | solution.py:448
  175.0 17.8 %collective-permute-start.49 = (bf16[128,512]{1,0:T(8,128)(2,1)S(1)}, bf16[128,512]{1,0:T(8,128)(2,1)S(1)}, u32[]{:S(2)}, u32[]{:S(2)}) collective-permute-start(bf16[128,512]{1,0:T(8,128)(2,1)S(1)} %get-tuple-element.125), channel_id=1, source_target_pairs={{0,2},{1,3},{2,0},{3,1},{4,6},{5,7},{6,4},{7,5},{8,10},{9,11},{10,... | collective-permute-start | bytes 393224 | tf_op jit(solution)/shard_map/ppermute | solution.py:448
  178.2 14.6 %collective-permute-start.50 = (bf16[128,512]{1,0:T(8,128)(2,1)S(1)}, bf16[128,512]{1,0:T(8,128)(2,1)S(1)}, u32[]{:S(2)}, u32[]{:S(2)}) collective-permute-start(bf16[128,512]{1,0:T(8,128)(2,1)S(1)} %get-tuple-element.126), channel_id=1, source_target_pairs={{0,3},{1,2},{2,1},{3,0},{4,7},{5,6},{6,5},{7,4},{8,11},{9,10},{10,... | collective-permute-start | bytes 393224 | tf_op jit(solution)/shard_map/ppermute | solution.py:448
  (6 other events, 11.6 us)

commit v12 on v11

--- a/solution.py
+++ b/solution.py
@@ -477,16 +477,25 @@
     return [swap(came[ROW][:half], COL), swap(came[COL][half:], ROW)]
 
 
-def first_sums(pieces):
+def direct_sums(pieces):
     tok = pieces[0][0].shape[0]
     if lax.axis_size("ctx") != PLANE:
         return [(mask, plus(*parts), [(0, 0, tok)]) for mask, parts in pieces.items() if mask]
     half = tok // 2
-    sums = []
-    for mask, start in ((ROW, 0), (COL, half)):
-        both = [plus(*[part[start : start + half] for part in pieces[at]]) for at in (ROW | COL, mask)]
-        sums.append((mask, jnp.concatenate(both), [(half, start, half)]))
-    return sums
+    return [
+        (mask, plus(*[part[start : start + half] for part in pieces[mask]]), [(0, start, half)])
+        for mask, start in ((ROW, 0), (COL, half))
+    ]
+
+
+def through_sums(pieces):
+    if lax.axis_size("ctx") != PLANE:
+        return []
+    half = pieces[0][0].shape[0] // 2
+    return [
+        (mask, plus(*[part[start : start + half] for part in pieces[ROW | COL]]), [])
+        for mask, start in ((ROW, 0), (COL, half))
+    ]
 
 
 def last_sums(pieces, came):
@@ -494,7 +503,7 @@
         return []
     half = pieces[0][0].shape[0] // 2
     return [
-        (mask, plus(*[part[start : start + half] for part in pieces[mask]], rows[:half]), [(0, start, half)])
+        (mask, plus(*[part[start : start + half] for part in pieces[mask]], rows), [(0, start, half)])
         for mask, start, rows in ((COL, 0, came[0]), (ROW, half, came[1]))
     ]
 
@@ -649,22 +658,25 @@
         pieces.append({mask: (near[at], arrived[at]) for at, mask in enumerate(here)})
         owns.append((near, arrived))
     halves = after(halves, near)
+    direct = [direct_sums(part) for part in pieces]
+    came = [send_sums(part) for part in direct]
+    through, came_through = [], []
+    ahead = [rows for part in direct for rows in arrays(part)]
     for chunk in range(CHUNKS):
         if halves[chunk]:
-            across = with_cores({ROW | COL: jnp.concatenate(halves[chunk])})
-            if chunk:
-                across = after(across, near)
+            across = after(with_cores({ROW | COL: jnp.concatenate(halves[chunk])}), near if chunk else ahead)
             near, far = experts_of(chunk, across)
-            pieces[chunk][ROW | COL] = (near[0], swap(far, CORE)[0])
-    firsts = [first_sums(part) for part in pieces]
-    came = [send_sums(first) for first in firsts]
-    lasts = [last_sums(*both) for both in zip(pieces, came)]
-    came_last = [send_sums(last) for last in lasts]
+            pieces[chunk][ROW | COL] = (near[0], swap(after(far, came[chunk]), CORE)[0])
+    for chunk in range(CHUNKS):
+        through.append(through_sums(pieces[chunk]))
+        came_through.append(send_sums(through[chunk]))
+    last = [last_sums(*both) for both in zip(pieces, came_through)]
+    came_last = [send_sums(part) for part in last]
     sums = []
     for chunk in range(CHUNKS):
-        terms = terms_of(firsts[chunk], came[chunk]) + terms_of(lasts[chunk], came_last[chunk])
-        if chunk + 1 < CHUNKS:
-            held = after([part for part, _ in terms], arrays(firsts[chunk + 1]))
+        terms = terms_of(direct[chunk], came[chunk]) + terms_of(last[chunk], came_last[chunk])
+        if chunk + 1 < CHUNKS and through[chunk + 1]:
+            held = after([part for part, _ in terms], arrays(through[chunk + 1]))
             terms = list(zip(held, [places for _, places in terms]))
         sums.append(send_heads(sum_terms(where, attn[chunk], *owns[chunk], terms, n_head)))
     grads = core_grads(where, qkv, grad_core, steps, fwd, bwd)

time: 194 us -> 194 us (level)
  waiting for transfers between devices: 84.3 us -> 79.8 us
  starting transfers between devices: 57.7 us -> 61.6 us
    ppermute x35 -> x39, waiting for transfers between devices: 42.6 us -> 37.8 us  [swap(): lax.ppermute(value, 'ctx', [(at, at ^ mask) for at in range(lax.axis_size...]
    ppermute x35 -> x39, starting transfers between devices: 29.7 us -> 33.6 us  [swap(): lax.ppermute(value, 'ctx', [(at, at ^ mask) for at in range(lax.axis_size...]
  transfers between devices with their start and end apart: 51 -> 55, of which waited for: 24 -> 25; matrix products, arithmetic and copies ran while one was open for 1% -> 1% of each run, Pallas kernels for 15% -> 15%
where the time goes in v12:
time: 194 us; the launch traced here: 193 us
  waiting for transfers between devices  79.8 us (41%)
  starting transfers between devices  61.6 us (32%)
  Pallas kernels  45.6 us (24%)
  local copies, waits for them, and re-layouts  4.09 us (2%)
    ppermute x15, waiting for transfers between devices, send_heads(): lax.ppermute(parts[mask], 'head', [(at, at ^ mask) for at in range(count)])  41 us
    ppermute x39, waiting for transfers between devices, swap(): lax.ppermute(value, 'ctx', [(at, at ^ mask) for at in range(lax.axis_size...  37.8 us
    ppermute x39, starting transfers between devices, swap(): lax.ppermute(value, 'ctx', [(at, at ^ mask) for at in range(lax.axis_size...  33.6 us
    ppermute x15, starting transfers between devices, send_heads(): lax.ppermute(parts[mask], 'head', [(at, at ^ mask) for at in range(count)])  25.5 us
    pallas_call x4, Pallas kernels, expert_pieces(): pl.pallas_call(functools.partial(expert_kernel, tuple(masks), chunk, expe...  19.3 us
    pallas_call x1, Pallas kernels, project(): pl.pallas_call(qkv_kernel, in_specs=[hbm, vmem, hbm], out_specs=[vmem, vm...  7.24 us
    pallas_call x1, Pallas kernels, core_grads(): pl.pallas_call(grad_kernel, in_specs=[pl.BlockSpec(memory_space=pltpu.SME...  4.71 us
    unnamed x41, local copies, waits for them, and re-layouts  3.94 us
  transfers between devices with their start and end apart: 55, of which 25 were waited for; matrix products, arithmetic and copies ran while one was open for 1% of the time, Pallas kernels for 15%

profile of v12, /device:TPU:0, one launch (start us, length us, event | category | flops | bytes accessed | tf_op | source)
XLA Modules:
  0.0 193.4 jit_solution(15213516931442816909)
XLA Ops:
  0.7 7.2 %qkv_projection.1 = (bf16[3,256,512]{2,1,0:T(8,128)(2,1)}, bf16[3,16,512]{2,1,0:T(8,128)(2,1)}) custom-call(bf16[256,2048]{1,0:T(8,128)(2,1)} %x_ref.3, f32[1,2048]{1,0:T(1,128)} %bitcast.63, bf16[3,2048,512]{2,1,0:T(8,128)(2,1)} %bitcast.59), custom_call_target="tpu_custom_call" | custom-call | tf_op jit(solution)/shard_map/qkv_projection/pallas_call | solution.py:68
  7.9 2.5 %collective-permute-start = (bf16[3,16,512]{2,1,0:T(8,128)(2,1)}, bf16[3,16,512]{2,1,0:T(8,128)(2,1)S(1)}, u32[]{:S(2)}, u32[]{:S(2)}) collective-permute-start(bf16[3,16,512]{2,1,0:T(8,128)(2,1)} %get-tuple-element.72), channel_id=1, source_target_pairs={{0,4},{4,8},{8,12},{12,16},{16,20},{20,24},{24,28},{1,5},{5,9},{9,... | collective-permute-start | bytes 147464 | tf_op jit(solution)/shard_map/ppermute | solution.py:621
  10.4 1.1 collective-permute-done.rim_ref
  11.5 1.1 copy-done.10
  12.7 3.0 %conv_states.1 = (bf16[3,256,512]{2,1,0:T(8,128)(2,1)S(1)}, bf16[672,128]{1,0:T(8,128)(2,1)S(1)}, bf16[576,128]{1,0:T(8,128)(2,1)S(1)}) custom-call(bf16[3,256,512]{2,1,0:T(8,128)(2,1)S(1)} %copy-done.10, bf16[3,16,512]{2,1,0:T(8,128)(2,1)S(1)} %collective-permute-done.rim_ref, f32[3,4,512]{2,1,0:T(4,128)S(1)} %bitcast.54, f32[4,256]{1,0:T(4,128)S(1)} %bitcast.51, ...), custom_call_target="tpu_custom_call" | custom-call | tf_op jit(solution)/shard_map/conv_states/pallas_call | solution.py:166
  15.7 0.9 copy-done.5
  17.2 6.1 %collective-permute-start.3 = (bf16[672,128]{1,0:T(8,128)(2,1)S(1)}, bf16[672,128]{1,0:T(8,128)(2,1)S(1)}, u32[]{:S(2)}, u32[]{:S(2)}) collective-permute-start(bf16[672,128]{1,0:T(8,128)(2,1)S(1)} %get-tuple-element.75), channel_id=1, source_target_pairs={{0,24},{4,28},{8,16},{12,20},{16,8},{20,12},{24,0},{28,4},{1,25},{... | collective-permute-start | bytes 516104 | tf_op jit(solution)/shard_map/ppermute | solution.py:442
  23.8 0.9 collective-permute-start.1
  24.8 3.8 %collective-permute-done.3 = bf16[672,128]{1,0:T(8,128)(2,1)S(1)} collective-permute-done((bf16[672,128]{1,0:T(8,128)(2,1)S(1)}, bf16[672,128]{1,0:T(8,128)(2,1)S(1)}, u32[]{:S(2)}, u32[]{:S(2)}) %collective-permute-start.3) | collective-permute-done | bytes 172064 | tf_op jit(solution)/shard_map/ppermute | solution.py:442
  28.6 2.5 %collective-permute-done.2 = bf16[672,128]{1,0:T(8,128)(2,1)S(1)} collective-permute-done((bf16[672,128]{1,0:T(8,128)(2,1)S(1)}, bf16[672,128]{1,0:T(8,128)(2,1)S(1)}, u32[]{:S(2)}, u32[]{:S(2)}) %collective-permute-start.2) | collective-permute-done | bytes 172064 | tf_op jit(solution)/shard_map/ppermute | solution.py:442
  31.4 1.1 stage_weights.2.me_ref.where_ref
  32.6 0.9 collective-permute-done.4.far_ref.far_routes.fwd_far
  33.5 1.1 copy-done.6
  34.6 3.6 %core_out.1 = (bf16[64,2048]{1,0:T(8,128)(2,1)S(1)}, bf16[64,2048]{1,0:T(8,128)(2,1)S(1)}, bf16[64,2048]{1,0:T(8,128)(2,1)S(1)}, bf16[64,2048]{1,0:T(8,128)(2,1)S(1)}) custom-call(s32[3]{0:T(128)S(1)} %stage_weights.2.me_ref.where_ref, bf16[3,256,512]{2,1,0:T(8,128)(2,1)S(1)} %copy-done.6, f32[4,256]{1,0:T(4,128)S(1)} %bitcast.52, f32[1,512]{1,0:T(1,128)S(1)} %bitcast.58, ...), custom_call_target="tpu_custom_call" | custom-call | tf_op jit(solution)/shard_map/core_out/pallas_call | solution.py:233
  38.3 1.7 collective-permute-start.8
  40.0 1.6 collective-permute-start.5
  41.6 2.6 %collective-permute-start.6 = (bf16[64,2048]{1,0:T(8,128)(2,1)S(1)}, bf16[64,2048]{1,0:T(8,128)(2,1)S(1)}, u32[]{:S(2)}, u32[]{:S(2)}) collective-permute-start(bf16[64,2048]{1,0:T(8,128)(2,1)S(1)} %get-tuple-element.78), channel_id=1, source_target_pairs={{0,2},{1,3},{2,0},{3,1},{4,6},{5,7},{6,4},{7,5},{8,10},{9,11},{10,... | collective-permute-start | bytes 786440 | tf_op jit(solution)/shard_map/ppermute | solution.py:448
  44.4 1.1 stage_weights.3.where_ref.me_ref
  45.6 7.5 %collective-permute-done.5.refs_1_ = bf16[64,2048]{1,0:T(8,128)(2,1)S(1)} collective-permute-done((bf16[64,2048]{1,0:T(8,128)(2,1)S(1)}, bf16[64,2048]{1,0:T(8,128)(2,1)S(1)}, u32[]{:S(2)}, u32[]{:S(2)}) %collective-permute-start.5) | collective-permute-done | bytes 262176 | tf_op jit(solution)/shard_map/ppermute | solution.py:448
  53.0 9.9 %collective-permute-done.6.refs_2_ = bf16[64,2048]{1,0:T(8,128)(2,1)S(1)} collective-permute-done((bf16[64,2048]{1,0:T(8,128)(2,1)S(1)}, bf16[64,2048]{1,0:T(8,128)(2,1)S(1)}, u32[]{:S(2)}, u32[]{:S(2)}) %collective-permute-start.6) | collective-permute-done | bytes 262176 | tf_op jit(solution)/shard_map/ppermute | solution.py:448
  63.8 1.0 collective-permute-start.12
  64.7 2.5 %collective-permute-start.11 = (bf16[32,2048]{1,0:T(8,128)(2,1)S(1)}, bf16[32,2048]{1,0:T(8,128)(2,1)S(1)}, u32[]{:S(2)}, u32[]{:S(2)}) collective-permute-start(bf16[32,2048]{1,0:T(8,128)(2,1)S(1)} %get-tuple-element.91.refs_0_), channel_id=1, source_target_pairs={{0,3},{1,2},{2,1},{3,0},{4,7},{5,6},{6,5},{7,4},{8,11},{9,10},{10,... | collective-permute-start | bytes 393224 | tf_op jit(solution)/shard_map/ppermute | solution.py:448
  67.2 5.2 %collective-permute-start.10 = (bf16[32,2048]{1,0:T(8,128)(2,1)S(1)}, bf16[32,2048]{1,0:T(8,128)(2,1)S(1)}, u32[]{:S(2)}, u32[]{:S(2)}) collective-permute-start(bf16[32,2048]{1,0:T(8,128)(2,1)S(1)} %get-tuple-element.91.refs_0_), channel_id=1, source_target_pairs={{0,2},{1,3},{2,0},{3,1},{4,6},{5,7},{6,4},{7,5},{8,10},{9,11},{10,... | collective-permute-start | bytes 393224 | tf_op jit(solution)/shard_map/ppermute | solution.py:448
  72.7 7.2 %collective-permute-done.10.refs_2_ = bf16[32,2048]{1,0:T(8,128)(2,1)S(1)} collective-permute-done((bf16[32,2048]{1,0:T(8,128)(2,1)S(1)}, bf16[32,2048]{1,0:T(8,128)(2,1)S(1)}, u32[]{:S(2)}, u32[]{:S(2)}) %collective-permute-start.10) | collective-permute-done | bytes 131104 | tf_op jit(solution)/shard_map/ppermute | solution.py:448
  80.5 1.2 collective-permute-start.14
  82.2 2.6 %collective-permute-start.17 = (bf16[32,2048]{1,0:T(8,128)(2,1)S(1)}, bf16[32,2048]{1,0:T(8,128)(2,1)S(1)}, u32[]{:S(2)}, u32[]{:S(2)}) collective-permute-start(bf16[32,2048]{1,0:T(8,128)(2,1)S(1)} %get-tuple-element.95.refs_0_), channel_id=1, source_target_pairs={{0,3},{1,2},{2,1},{3,0},{4,7},{5,6},{6,5},{7,4},{8,11},{9,10},{10,... | collective-permute-start | bytes 393224 | tf_op jit(solution)/shard_map/ppermute | solution.py:448
  84.8 1.7 collective-permute-start.15
  86.5 3.7 %collective-permute-done.17.refs_3_ = bf16[32,2048]{1,0:T(8,128)(2,1)S(1)} collective-permute-done((bf16[32,2048]{1,0:T(8,128)(2,1)S(1)}, bf16[32,2048]{1,0:T(8,128)(2,1)S(1)}, u32[]{:S(2)}, u32[]{:S(2)}) %collective-permute-start.17) | collective-permute-done | bytes 131104 | tf_op jit(solution)/shard_map/ppermute | solution.py:448
  90.2 3.7 %collective-permute-done.16.refs_2_ = bf16[32,2048]{1,0:T(8,128)(2,1)S(1)} collective-permute-done((bf16[32,2048]{1,0:T(8,128)(2,1)S(1)}, bf16[32,2048]{1,0:T(8,128)(2,1)S(1)}, u32[]{:S(2)}, u32[]{:S(2)}) %collective-permute-start.16) | collective-permute-done | bytes 131104 | tf_op jit(solution)/shard_map/ppermute | solution.py:448
  95.2 1.7 collective-permute-start.27
  98.0 7.0 %expert_pieces.4 = (bf16[3,128,2048]{2,1,0:T(8,128)(2,1)S(1)}, bf16[3,128,2048]{2,1,0:T(8,128)(2,1)S(1)}) custom-call(s32[3]{0:T(128)S(1)} %stage_weights.3.where_ref.me_ref, bf16[4,672,128]{2,1,0:T(8,128)(2,1)S(1)} %pad_maximum_fusion.near_ref.near_routes.fwd_near, bf16[4,672,128]{2,1,0:T(8,128)(2,1)S(1)} %collective-permute-done.4.far_ref.far_routes.fwd_far, ...), custom_call_target="tpu_custom_call" | custom-call | flops 4831838208 | bytes 6291456 | tf_op jit(solution)/shard_map/expert_pieces/pallas_call | solution.py:415
  105.0 4.5 %collective-permute-done.27.refs_4_ = bf16[128,2048]{1,0:T(8,128)(2,1)S(1)} collective-permute-done((bf16[128,2048]{1,0:T(8,128)(2,1)S(1)}, bf16[128,2048]{1,0:T(8,128)(2,1)S(1)}, u32[]{:S(2)}, u32[]{:S(2)}) %collective-permute-start.27) | collective-permute-done | bytes 524320 | tf_op jit(solution)/shard_map/ppermute | solution.py:442
  109.5 1.4 collective-permute-done.26.refs_2_
  112.8 1.1 collective-permute-start.24
  114.6 1.5 collective-permute-start.28
  116.1 7.0 %expert_pieces.5 = (bf16[3,128,2048]{2,1,0:T(8,128)(2,1)S(1)}, bf16[3,128,2048]{2,1,0:T(8,128)(2,1)S(1)}) custom-call(s32[3]{0:T(128)S(1)} %stage_weights.3.where_ref.me_ref, bf16[4,672,128]{2,1,0:T(8,128)(2,1)S(1)} %pad_maximum_fusion.near_ref.near_routes.fwd_near, bf16[4,672,128]{2,1,0:T(8,128)(2,1)S(1)} %collective-permute-done.4.far_ref.far_routes.fwd_far, ...), custom_call_target="tpu_custom_call" | custom-call | flops 4831838208 | bytes 6291456 | tf_op jit(solution)/shard_map/expert_pieces/pallas_call | solution.py:415
  123.2 2.7 %collective-permute-done.29 = bf16[64,2048]{1,0:T(8,128)(2,1)S(1)} collective-permute-done((bf16[64,2048]{1,0:T(8,128)(2,1)S(1)}, bf16[64,2048]{1,0:T(8,128)(2,1)S(1)}, u32[]{:S(2)}, u32[]{:S(2)}) %collective-permute-start.29) | collective-permute-done | bytes 262176 | tf_op jit(solution)/shard_map/ppermute | solution.py:442
  128.4 1.1 collective-permute-start.22
  129.7 2.7 %expert_pieces.6 = (bf16[1,128,2048]{2,1,0:T(8,128)(2,1)S(1)}, bf16[1,128,2048]{2,1,0:T(8,128)(2,1)S(1)}) custom-call(s32[3]{0:T(128)S(1)} %stage_weights.3.where_ref.me_ref, bf16[4,672,128]{2,1,0:T(8,128)(2,1)S(1)} %pad_maximum_fusion.near_ref.near_routes.fwd_near, bf16[4,672,128]{2,1,0:T(8,128)(2,1)S(1)} %collective-permute-done.4.far_ref.far_routes.fwd_far, ...), custom_call_target="tpu_custom_call" | custom-call | flops 1610612736 | bytes 2097152 | tf_op jit(solution)/shard_map/expert_pieces/pallas_call | solution.py:415
  132.3 3.6 %collective-permute-done.23.refs_1_ = bf16[64,2048]{1,0:T(8,128)(2,1)S(1)} collective-permute-done((bf16[64,2048]{1,0:T(8,128)(2,1)S(1)}, bf16[64,2048]{1,0:T(8,128)(2,1)S(1)}, u32[]{:S(2)}, u32[]{:S(2)}) %collective-permute-start.23) | collective-permute-done | bytes 262176 | tf_op jit(solution)/shard_map/ppermute | solution.py:442
  136.3 1.3 collective-permute-start.43
  137.7 0.9 collective-permute-start.42
  138.6 2.7 %expert_pieces.7 = (bf16[1,128,2048]{2,1,0:T(8,128)(2,1)S(1)}, bf16[1,128,2048]{2,1,0:T(8,128)(2,1)S(1)}) custom-call(s32[3]{0:T(128)S(1)} %stage_weights.3.where_ref.me_ref, bf16[4,672,128]{2,1,0:T(8,128)(2,1)S(1)} %pad_maximum_fusion.near_ref.near_routes.fwd_near, bf16[4,672,128]{2,1,0:T(8,128)(2,1)S(1)} %collective-permute-done.4.far_ref.far_routes.fwd_far, ...), custom_call_target="tpu_custom_call" | custom-call | flops 1610612736 | bytes 2097152 | tf_op jit(solution)/shard_map/expert_pieces/pallas_call | solution.py:415
  141.2 3.8 %collective-permute-done.43.refs_1_ = bf16[64,2048]{1,0:T(8,128)(2,1)S(1)} collective-permute-done((bf16[64,2048]{1,0:T(8,128)(2,1)S(1)}, bf16[64,2048]{1,0:T(8,128)(2,1)S(1)}, u32[]{:S(2)}, u32[]{:S(2)}) %collective-permute-start.43) | collective-permute-done | bytes 262176 | tf_op jit(solution)/shard_map/ppermute | solution.py:442
  145.1 1.0 collective-permute-done.42.refs_0_
  147.0 1.1 collective-permute-start.37
  148.3 1.2 collective-permute-start.50
  149.4 1.1 collective-permute-start.48
  150.6 4.8 %collective-permute-done.39 = bf16[64,2048]{1,0:T(8,128)(2,1)S(1)} collective-permute-done((bf16[64,2048]{1,0:T(8,128)(2,1)S(1)}, bf16[64,2048]{1,0:T(8,128)(2,1)S(1)}, u32[]{:S(2)}, u32[]{:S(2)}) %collective-permute-start.39) | collective-permute-done | bytes 262176 | tf_op jit(solution)/shard_map/ppermute | solution.py:442
  156.4 1.2 collective-permute-start.40
  157.6 1.1 collective-permute-start.38
  158.7 2.3 %collective-permute-done.50 = bf16[64,2048]{1,0:T(8,128)(2,1)S(1)} collective-permute-done((bf16[64,2048]{1,0:T(8,128)(2,1)S(1)}, bf16[64,2048]{1,0:T(8,128)(2,1)S(1)}, u32[]{:S(2)}, u32[]{:S(2)}) %collective-permute-start.50) | collective-permute-done | bytes 262176 | tf_op jit(solution)/shard_map/ppermute | solution.py:442
  162.0 1.2 collective-permute-start.51
  163.2 1.1 collective-permute-start.49
  164.3 3.1 %collective-permute-done.40.refs_3_ = bf16[64,2048]{1,0:T(8,128)(2,1)S(1)} collective-permute-done((bf16[64,2048]{1,0:T(8,128)(2,1)S(1)}, bf16[64,2048]{1,0:T(8,128)(2,1)S(1)}, u32[]{:S(2)}, u32[]{:S(2)}) %collective-permute-start.40) | collective-permute-done | bytes 262176 | tf_op jit(solution)/shard_map/ppermute | solution.py:442
  167.4 1.0 sum_terms.2
  168.8 2.8 %collective-permute-start.46 = (bf16[128,512]{1,0:T(8,128)(2,1)S(1)}, bf16[128,512]{1,0:T(8,128)(2,1)S(1)}, u32[]{:S(2)}, u32[]{:S(2)}) collective-permute-start(bf16[128,512]{1,0:T(8,128)(2,1)S(1)} %get-tuple-element.128), channel_id=1, source_target_pairs={{0,2},{1,3},{2,0},{3,1},{4,6},{5,7},{6,4},{7,5},{8,10},{9,11},{10,... | collective-permute-start | bytes 393224 | tf_op jit(solution)/shard_map/ppermute | solution.py:448
  171.6 1.2 collective-permute-start.47
  172.9 1.0 sum_terms.3
  173.9 3.2 %collective-permute-start.53 = (bf16[128,512]{1,0:T(8,128)(2,1)S(1)}, bf16[128,512]{1,0:T(8,128)(2,1)S(1)}, u32[]{:S(2)}, u32[]{:S(2)}) collective-permute-start(bf16[128,512]{1,0:T(8,128)(2,1)S(1)} %get-tuple-element.133), channel_id=1, source_target_pairs={{0,2},{1,3},{2,0},{3,1},{4,6},{5,7},{6,4},{7,5},{8,10},{9,11},{10,... | collective-permute-start | bytes 393224 | tf_op jit(solution)/shard_map/ppermute | solution.py:448
  177.1 1.2 collective-permute-start.54
  178.3 4.7 %core_grads.1 = (bf16[256,512]{1,0:T(8,128)(2,1)}, bf16[256,512]{1,0:T(8,128)(2,1)}, bf16[256,512]{1,0:T(8,128)(2,1)}) custom-call(s32[3]{0:T(128)S(1)} %stage_weights.3.where_ref.me_ref, bf16[3,256,512]{2,1,0:T(8,128)(2,1)S(1)} %copy-done.7, bf16[256,512]{1,0:T(8,128)(2,1)S(1)} %copy-done.9, f32[4,256]{1,0:T(4,128)S(1)} %bitcast.53, ...), custom_call_target="tpu_custom_call" | custom-call | tf_op jit(solution)/shard_map/core_grads/pallas_call | solution.py:278
  183.0 9.0 %collective-permute-done.53.refs_6_ = bf16[128,512]{1,0:T(8,128)(2,1)S(1)} collective-permute-done((bf16[128,512]{1,0:T(8,128)(2,1)S(1)}, bf16[128,512]{1,0:T(8,128)(2,1)S(1)}, u32[]{:S(2)}, u32[]{:S(2)}) %collective-permute-start.53) | collective-permute-done | bytes 131104 | tf_op jit(solution)/shard_map/ppermute | solution.py:448
  192.0 1.4 layer_out.1
  (119 shorter events, 15.5 us)
Async XLA Ops:
  0.6 10.9 %copy-start.8 = (bf16[256,512]{1,0:T(8,128)(2,1)S(1)}, bf16[256,512]{1,0:T(8,128)(2,1)}, u32[]{:S(2)}) copy-start(bf16[256,512]{1,0:T(8,128)(2,1)} %cot_ref.3) | copy-start | bytes 786436
  0.6 10.9 %copy-start.13 = (f32[256,4]{0,1:T(4,128)S(1)}, f32[256,4]{0,1:T(4,128)}, u32[]{:S(2)}) copy-start(f32[256,4]{0,1:T(4,128)} %param.18) | copy-start | bytes 12292
  0.7 10.9 %copy-start.14 = (f32[4,3,512]{2,0,1:T(4,128)S(1)}, f32[4,3,512]{2,0,1:T(4,128)}, u32[]{:S(2)}) copy-start(f32[4,3,512]{2,0,1:T(4,128)} %param.17) | copy-start | bytes 73732
  0.7 10.9 %copy-start.15 = (s32[256,8]{0,1:T(8,128)S(1)}, s32[256,8]{0,1:T(8,128)}, u32[]{:S(2)}) copy-start(s32[256,8]{0,1:T(8,128)} %param.22) | copy-start | bytes 24580
  0.7 10.9 %copy-start.16 = (f32[256,8]{0,1:T(8,128)S(1)}, f32[256,8]{0,1:T(8,128)}, u32[]{:S(2)}) copy-start(f32[256,8]{0,1:T(8,128)} %param.23) | copy-start | bytes 24580
  7.9 23.5 %copy-start.4 = (bf16[512,2048]{1,0:T(8,128)(2,1)S(1)}, bf16[512,2048]{1,0:T(8,128)(2,1)}, u32[]{:S(2)}) copy-start(bf16[512,2048]{1,0:T(8,128)(2,1)} %w_ref.1) | copy-start | bytes 6291460
  7.9 3.6 %collective-permute-start = (bf16[3,16,512]{2,1,0:T(8,128)(2,1)}, bf16[3,16,512]{2,1,0:T(8,128)(2,1)S(1)}, u32[]{:S(2)}, u32[]{:S(2)}) collective-permute-start(bf16[3,16,512]{2,1,0:T(8,128)(2,1)} %get-tuple-element.72), channel_id=1, source_target_pairs={{0,4},{4,8},{8,12},{12,16},{16,20},{20,24},{24,28},{1,5},{5,9},{9,... | collective-permute-start | bytes 147464 | tf_op jit(solution)/shard_map/ppermute | solution.py:621
  17.2 11.4 %collective-permute-start.3 = (bf16[672,128]{1,0:T(8,128)(2,1)S(1)}, bf16[672,128]{1,0:T(8,128)(2,1)S(1)}, u32[]{:S(2)}, u32[]{:S(2)}) collective-permute-start(bf16[672,128]{1,0:T(8,128)(2,1)S(1)} %get-tuple-element.75), channel_id=1, source_target_pairs={{0,24},{4,28},{8,16},{12,20},{16,8},{20,12},{24,0},{28,4},{1,25},{... | collective-permute-start | bytes 516104 | tf_op jit(solution)/shard_map/ppermute | solution.py:442
  23.3 7.8 %collective-permute-start.2 = (bf16[672,128]{1,0:T(8,128)(2,1)S(1)}, bf16[672,128]{1,0:T(8,128)(2,1)S(1)}, u32[]{:S(2)}, u32[]{:S(2)}) collective-permute-start(bf16[672,128]{1,0:T(8,128)(2,1)S(1)} %get-tuple-element.75), channel_id=1, source_target_pairs={{0,16},{4,20},{8,24},{12,28},{16,0},{20,4},{24,8},{28,12},{1,17},{... | collective-permute-start | bytes 516104 | tf_op jit(solution)/shard_map/ppermute | solution.py:442
  23.8 7.3 %collective-permute-start.1 = (bf16[672,128]{1,0:T(8,128)(2,1)S(1)}, bf16[672,128]{1,0:T(8,128)(2,1)S(1)}, u32[]{:S(2)}, u32[]{:S(2)}) collective-permute-start(bf16[672,128]{1,0:T(8,128)(2,1)S(1)} %get-tuple-element.75), channel_id=1, source_target_pairs={{0,8},{4,12},{8,0},{12,4},{16,24},{20,28},{24,16},{28,20},{1,9},{5... | collective-permute-start | bytes 516104 | tf_op jit(solution)/shard_map/ppermute | solution.py:442
  31.3 2.2 %collective-permute-start.4 = (bf16[4,672,128]{2,1,0:T(8,128)(2,1)S(1)}, bf16[4,672,128]{2,1,0:T(8,128)(2,1)S(1)}, u32[]{:S(2)}, u32[]{:S(2)}) collective-permute-start(bf16[4,672,128]{2,1,0:T(8,128)(2,1)S(1)} %pad_maximum_fusion.near_ref.near_routes.fwd_near), channel_id=1, source_target_pairs={{0,4},{4,0},{8,12},{12,8},{16,20},{20,16},{24,28},{28,24},{1,5},{5... | collective-permute-start | bytes 2064392 | tf_op jit(solution)/shard_map/ppermute | solution.py:442
  31.4 12.9 %copy-start.2 = (bf16[1,512,2048]{2,1,0:T(8,128)(2,1)S(1)}, bf16[1,512,2048]{2,1,0:T(8,128)(2,1)}, u32[]{:S(2)}) copy-start(bf16[1,512,2048]{2,1,0:T(8,128)(2,1)} %down_ref.7) | copy-start | bytes 6291460
  38.3 24.6 %copy-start.3 = (bf16[256,2048]{1,0:T(8,128)(2,1)S(1)}, bf16[256,2048]{1,0:T(8,128)(2,1)}, u32[]{:S(2)}) copy-start(bf16[256,2048]{1,0:T(8,128)(2,1)} %x_ref.3) | copy-start | bytes 3145732
  38.3 24.6 %copy-start.17 = (f32[2048]{0:T(1024)S(1)}, f32[2048]{0:T(1024)}, u32[]{:S(2)}) copy-start(f32[2048]{0:T(1024)} %param.21) | copy-start | bytes 24580
  38.3 7.2 %collective-permute-start.8 = (bf16[1,576,128]{2,1,0:T(8,128)(2,1)}, bf16[1,576,128]{2,1,0:T(8,128)(2,1)S(1)}, u32[]{:S(2)}, u32[]{:S(2)}) collective-permute-start(bf16[1,576,128]{2,1,0:T(8,128)(2,1)} %bitcast.49), channel_id=1, source_target_pairs={{0,8},{4,12},{8,0},{12,4},{16,24},{20,28},{24,16},{28,20},{1,9},{5... | collective-permute-start | bytes 442376 | tf_op jit(solution)/shard_map/ppermute | solution.py:442
  40.0 13.1 %collective-permute-start.5 = (bf16[64,2048]{1,0:T(8,128)(2,1)S(1)}, bf16[64,2048]{1,0:T(8,128)(2,1)S(1)}, u32[]{:S(2)}, u32[]{:S(2)}) collective-permute-start(bf16[64,2048]{1,0:T(8,128)(2,1)S(1)} %get-tuple-element.77), channel_id=1, source_target_pairs={{0,1},{1,0},{2,3},{3,2},{4,5},{5,4},{6,7},{7,6},{8,9},{9,8},{10,11... | collective-permute-start | bytes 786440 | tf_op jit(solution)/shard_map/ppermute | solution.py:448
  41.6 21.4 %collective-permute-start.6 = (bf16[64,2048]{1,0:T(8,128)(2,1)S(1)}, bf16[64,2048]{1,0:T(8,128)(2,1)S(1)}, u32[]{:S(2)}, u32[]{:S(2)}) collective-permute-start(bf16[64,2048]{1,0:T(8,128)(2,1)S(1)} %get-tuple-element.78), channel_id=1, source_target_pairs={{0,2},{1,3},{2,0},{3,1},{4,6},{5,7},{6,4},{7,5},{8,10},{9,11},{10,... | collective-permute-start | bytes 786440 | tf_op jit(solution)/shard_map/ppermute | solution.py:448
  44.2 18.8 %collective-permute-start.7 = (bf16[64,2048]{1,0:T(8,128)(2,1)S(1)}, bf16[64,2048]{1,0:T(8,128)(2,1)S(1)}, u32[]{:S(2)}, u32[]{:S(2)}) collective-permute-start(bf16[64,2048]{1,0:T(8,128)(2,1)S(1)} %get-tuple-element.79), channel_id=1, source_target_pairs={{0,3},{1,2},{2,1},{3,0},{4,7},{5,6},{6,5},{7,4},{8,11},{9,10},{10,... | collective-permute-start | bytes 786440 | tf_op jit(solution)/shard_map/ppermute | solution.py:448
  63.8 8.8 %collective-permute-start.12 = (bf16[2,576,128]{2,1,0:T(8,128)(2,1)S(1)}, bf16[2,576,128]{2,1,0:T(8,128)(2,1)S(1)}, u32[]{:S(2)}, u32[]{:S(2)}) collective-permute-start(bf16[2,576,128]{2,1,0:T(8,128)(2,1)S(1)} %pad_maximum_fusion.1), channel_id=1, source_target_pairs={{0,16},{4,20},{8,24},{12,28},{16,0},{20,4},{24,8},{28,12},{1,17},{... | collective-permute-start | bytes 884744 | tf_op jit(solution)/shard_map/ppermute | solution.py:442
  64.7 7.9 %collective-permute-start.11 = (bf16[32,2048]{1,0:T(8,128)(2,1)S(1)}, bf16[32,2048]{1,0:T(8,128)(2,1)S(1)}, u32[]{:S(2)}, u32[]{:S(2)}) collective-permute-start(bf16[32,2048]{1,0:T(8,128)(2,1)S(1)} %get-tuple-element.91.refs_0_), channel_id=1, source_target_pairs={{0,3},{1,2},{2,1},{3,0},{4,7},{5,6},{6,5},{7,4},{8,11},{9,10},{10,... | collective-permute-start | bytes 393224 | tf_op jit(solution)/shard_map/ppermute | solution.py:448
  67.2 12.7 %collective-permute-start.10 = (bf16[32,2048]{1,0:T(8,128)(2,1)S(1)}, bf16[32,2048]{1,0:T(8,128)(2,1)S(1)}, u32[]{:S(2)}, u32[]{:S(2)}) collective-permute-start(bf16[32,2048]{1,0:T(8,128)(2,1)S(1)} %get-tuple-element.91.refs_0_), channel_id=1, source_target_pairs={{0,2},{1,3},{2,0},{3,1},{4,6},{5,7},{6,4},{7,5},{8,10},{9,11},{10,... | collective-permute-start | bytes 393224 | tf_op jit(solution)/shard_map/ppermute | solution.py:448
  72.5 7.5 %collective-permute-start.9 = (bf16[32,2048]{1,0:T(8,128)(2,1)S(1)}, bf16[32,2048]{1,0:T(8,128)(2,1)S(1)}, u32[]{:S(2)}, u32[]{:S(2)}) collective-permute-start(bf16[32,2048]{1,0:T(8,128)(2,1)S(1)} %get-tuple-element.91.refs_0_), channel_id=1, source_target_pairs={{0,1},{1,0},{2,3},{3,2},{4,5},{5,4},{6,7},{7,6},{8,9},{9,8},{10,11... | collective-permute-start | bytes 393224 | tf_op jit(solution)/shard_map/ppermute | solution.py:448
  80.5 14.0 %collective-permute-start.14 = (bf16[128,2048]{1,0:T(8,128)(2,1)S(1)}, bf16[128,2048]{1,0:T(8,128)(2,1)S(1)}, u32[]{:S(2)}, u32[]{:S(2)}) collective-permute-start(bf16[128,2048]{1,0:T(8,128)(2,1)S(1)} %join_rows.2.refs_0_), channel_id=1, source_target_pairs={{0,16},{4,20},{8,24},{12,28},{16,0},{20,4},{24,8},{28,12},{1,17},{... | collective-permute-start | bytes 1572872 | tf_op jit(solution)/shard_map/ppermute | solution.py:442
  81.7 12.8 %collective-permute-start.13 = (bf16[128,2048]{1,0:T(8,128)(2,1)S(1)}, bf16[128,2048]{1,0:T(8,128)(2,1)S(1)}, u32[]{:S(2)}, u32[]{:S(2)}) collective-permute-start(bf16[128,2048]{1,0:T(8,128)(2,1)S(1)} %join_rows.2.refs_0_), channel_id=1, source_target_pairs={{0,8},{4,12},{8,0},{12,4},{16,24},{20,28},{24,16},{28,20},{1,9},{5... | collective-permute-start | bytes 1572872 | tf_op jit(solution)/shard_map/ppermute | solution.py:442
  82.2 8.1 %collective-permute-start.17 = (bf16[32,2048]{1,0:T(8,128)(2,1)S(1)}, bf16[32,2048]{1,0:T(8,128)(2,1)S(1)}, u32[]{:S(2)}, u32[]{:S(2)}) collective-permute-start(bf16[32,2048]{1,0:T(8,128)(2,1)S(1)} %get-tuple-element.95.refs_0_), channel_id=1, source_target_pairs={{0,3},{1,2},{2,1},{3,0},{4,7},{5,6},{6,5},{7,4},{8,11},{9,10},{10,... | collective-permute-start | bytes 393224 | tf_op jit(solution)/shard_map/ppermute | solution.py:448
  84.8 9.1 %collective-permute-start.16 = (bf16[32,2048]{1,0:T(8,128)(2,1)S(1)}, bf16[32,2048]{1,0:T(8,128)(2,1)S(1)}, u32[]{:S(2)}, u32[]{:S(2)}) collective-permute-start(bf16[32,2048]{1,0:T(8,128)(2,1)S(1)} %get-tuple-element.95.refs_0_), channel_id=1, source_target_pairs={{0,2},{1,3},{2,0},{3,1},{4,6},{5,7},{6,4},{7,5},{8,10},{9,11},{10,... | collective-permute-start | bytes 393224 | tf_op jit(solution)/shard_map/ppermute | solution.py:448
  84.8 9.1 %collective-permute-start.15 = (bf16[32,2048]{1,0:T(8,128)(2,1)S(1)}, bf16[32,2048]{1,0:T(8,128)(2,1)S(1)}, u32[]{:S(2)}, u32[]{:S(2)}) collective-permute-start(bf16[32,2048]{1,0:T(8,128)(2,1)S(1)} %get-tuple-element.95.refs_0_), channel_id=1, source_target_pairs={{0,1},{1,0},{2,3},{3,2},{4,5},{5,4},{6,7},{7,6},{8,9},{9,8},{10,11... | collective-permute-start | bytes 393224 | tf_op jit(solution)/shard_map/ppermute | solution.py:448
  94.5 3.0 %collective-permute-start.18 = (bf16[128,2048]{1,0:T(8,128)(2,1)S(1)}, bf16[128,2048]{1,0:T(8,128)(2,1)S(1)}, u32[]{:S(2)}, u32[]{:S(2)}) collective-permute-start(bf16[128,2048]{1,0:T(8,128)(2,1)S(1)} %join_rows.2.refs_0_), channel_id=1, source_target_pairs={{0,4},{4,0},{8,12},{12,8},{16,20},{20,16},{24,28},{28,24},{1,5},{5... | collective-permute-start | bytes 1572872 | tf_op jit(solution)/shard_map/ppermute | solution.py:442
  94.6 3.0 %collective-permute-start.19 = (bf16[128,2048]{1,0:T(8,128)(2,1)S(1)}, bf16[128,2048]{1,0:T(8,128)(2,1)S(1)}, u32[]{:S(2)}, u32[]{:S(2)}) collective-permute-start(bf16[128,2048]{1,0:T(8,128)(2,1)S(1)} %collective-permute-done.13.refs_2_), channel_id=1, source_target_pairs={{0,4},{4,0},{8,12},{12,8},{16,20},{20,16},{24,28},{28,24},{1,5},{5... | collective-permute-start | bytes 1572872 | tf_op jit(solution)/shard_map/ppermute | solution.py:442
  95.1 2.9 %collective-permute-start.20 = (bf16[128,2048]{1,0:T(8,128)(2,1)S(1)}, bf16[128,2048]{1,0:T(8,128)(2,1)S(1)}, u32[]{:S(2)}, u32[]{:S(2)}) collective-permute-start(bf16[128,2048]{1,0:T(8,128)(2,1)S(1)} %collective-permute-done.14.refs_4_), channel_id=1, source_target_pairs={{0,4},{4,0},{8,12},{12,8},{16,20},{20,16},{24,28},{28,24},{1,5},{5... | collective-permute-start | bytes 1572872 | tf_op jit(solution)/shard_map/ppermute | solution.py:442
  95.2 14.3 %collective-permute-start.27 = (bf16[128,2048]{1,0:T(8,128)(2,1)S(1)}, bf16[128,2048]{1,0:T(8,128)(2,1)S(1)}, u32[]{:S(2)}, u32[]{:S(2)}) collective-permute-start(bf16[128,2048]{1,0:T(8,128)(2,1)S(1)} %join_rows.3.refs_0_), channel_id=1, source_target_pairs={{0,16},{4,20},{8,24},{12,28},{16,0},{20,4},{24,8},{28,12},{1,17},{... | collective-permute-start | bytes 1572872 | tf_op jit(solution)/shard_map/ppermute | solution.py:442
  96.9 14.0 %collective-permute-start.26 = (bf16[128,2048]{1,0:T(8,128)(2,1)S(1)}, bf16[128,2048]{1,0:T(8,128)(2,1)S(1)}, u32[]{:S(2)}, u32[]{:S(2)}) collective-permute-start(bf16[128,2048]{1,0:T(8,128)(2,1)S(1)} %join_rows.3.refs_0_), channel_id=1, source_target_pairs={{0,8},{4,12},{8,0},{12,4},{16,24},{20,28},{24,16},{28,20},{1,9},{5... | collective-permute-start | bytes 1572872 | tf_op jit(solution)/shard_map/ppermute | solution.py:442
  97.6 14.4 %collective-permute-start.34 = (bf16[4,576,128]{2,1,0:T(8,128)(2,1)S(1)}, bf16[4,576,128]{2,1,0:T(8,128)(2,1)S(1)}, u32[]{:S(2)}, u32[]{:S(2)}) collective-permute-start(bf16[4,576,128]{2,1,0:T(8,128)(2,1)S(1)} %constant_dynamic-update-slice_fusion.bwd_near), channel_id=1, source_target_pairs={{0,4},{4,0},{8,12},{12,8},{16,20},{20,16},{24,28},{28,24},{1,5},{5... | collective-permute-start | bytes 1769480 | tf_op jit(solution)/shard_map/ppermute | solution.py:442
  110.9 1.9 collective-permute-start.30
  110.9 3.0 %collective-permute-start.31 = (bf16[128,2048]{1,0:T(8,128)(2,1)S(1)}, bf16[128,2048]{1,0:T(8,128)(2,1)S(1)}, u32[]{:S(2)}, u32[]{:S(2)}) collective-permute-start(bf16[128,2048]{1,0:T(8,128)(2,1)S(1)} %collective-permute-done.26.refs_2_), channel_id=1, source_target_pairs={{0,4},{4,0},{8,12},{12,8},{16,20},{20,16},{24,28},{28,24},{1,5},{5... | collective-permute-start | bytes 1572872 | tf_op jit(solution)/shard_map/ppermute | solution.py:442
  111.4 3.2 %collective-permute-start.32 = (bf16[128,2048]{1,0:T(8,128)(2,1)S(1)}, bf16[128,2048]{1,0:T(8,128)(2,1)S(1)}, u32[]{:S(2)}, u32[]{:S(2)}) collective-permute-start(bf16[128,2048]{1,0:T(8,128)(2,1)S(1)} %collective-permute-done.27.refs_4_), channel_id=1, source_target_pairs={{0,4},{4,0},{8,12},{12,8},{16,20},{20,16},{24,28},{28,24},{1,5},{5... | collective-permute-start | bytes 1572872 | tf_op jit(solution)/shard_map/ppermute | solution.py:442
  111.4 16.1 %collective-permute-start.21 = (bf16[3,128,2048]{2,1,0:T(8,128)(2,1)S(1)}, bf16[3,128,2048]{2,1,0:T(8,128)(2,1)S(1)}, u32[]{:S(2)}, u32[]{:S(2)}) collective-permute-start(bf16[3,128,2048]{2,1,0:T(8,128)(2,1)S(1)} %get-tuple-element.100), channel_id=1, source_target_pairs={{0,4},{4,0},{8,12},{12,8},{16,20},{20,16},{24,28},{28,24},{1,5},{5... | collective-permute-start | bytes 4718600 | tf_op jit(solution)/shard_map/ppermute | solution.py:442
  112.0 11.1 %collective-permute-start.25 = (bf16[64,2048]{1,0:T(8,128)(2,1)S(1)}, bf16[64,2048]{1,0:T(8,128)(2,1)S(1)}, u32[]{:S(2)}, u32[]{:S(2)}) collective-permute-start(bf16[64,2048]{1,0:T(8,128)(2,1)S(1)} %slice.139), channel_id=1, source_target_pairs={{0,8},{4,12},{8,0},{12,4},{16,24},{20,28},{24,16},{28,20},{1,9},{5... | collective-permute-start | bytes 786440 | tf_op jit(solution)/shard_map/ppermute | solution.py:442
  112.8 10.4 %collective-permute-start.24 = (bf16[64,2048]{1,0:T(8,128)(2,1)S(1)}, bf16[64,2048]{1,0:T(8,128)(2,1)S(1)}, u32[]{:S(2)}, u32[]{:S(2)}) collective-permute-start(bf16[64,2048]{1,0:T(8,128)(2,1)S(1)} %slice.138), channel_id=1, source_target_pairs={{0,16},{4,20},{8,24},{12,28},{16,0},{20,4},{24,8},{28,12},{1,17},{... | collective-permute-start | bytes 786440 | tf_op jit(solution)/shard_map/ppermute | solution.py:442
  113.9 12.0 %collective-permute-start.29 = (bf16[64,2048]{1,0:T(8,128)(2,1)S(1)}, bf16[64,2048]{1,0:T(8,128)(2,1)S(1)}, u32[]{:S(2)}, u32[]{:S(2)}) collective-permute-start(bf16[64,2048]{1,0:T(8,128)(2,1)S(1)} %slice.141), channel_id=1, source_target_pairs={{0,8},{4,12},{8,0},{12,4},{16,24},{20,28},{24,16},{28,20},{1,9},{5... | collective-permute-start | bytes 786440 | tf_op jit(solution)/shard_map/ppermute | solution.py:442
  114.6 12.1 %collective-permute-start.28 = (bf16[64,2048]{1,0:T(8,128)(2,1)S(1)}, bf16[64,2048]{1,0:T(8,128)(2,1)S(1)}, u32[]{:S(2)}, u32[]{:S(2)}) collective-permute-start(bf16[64,2048]{1,0:T(8,128)(2,1)S(1)} %slice.140), channel_id=1, source_target_pairs={{0,16},{4,20},{8,24},{12,28},{16,0},{20,4},{24,8},{28,12},{1,17},{... | collective-permute-start | bytes 786440 | tf_op jit(solution)/shard_map/ppermute | solution.py:442
  123.1 6.4 %collective-permute-start.35 = (bf16[3,128,2048]{2,1,0:T(8,128)(2,1)S(1)}, bf16[3,128,2048]{2,1,0:T(8,128)(2,1)S(1)}, u32[]{:S(2)}, u32[]{:S(2)}) collective-permute-start(bf16[3,128,2048]{2,1,0:T(8,128)(2,1)S(1)} %get-tuple-element.109), channel_id=1, source_target_pairs={{0,4},{4,0},{8,12},{12,8},{16,20},{20,16},{24,28},{28,24},{1,5},{5... | collective-permute-start | bytes 4718600 | tf_op jit(solution)/shard_map/ppermute | solution.py:442
  126.8 11.8 %collective-permute-start.41 = (bf16[128,2048]{1,0:T(8,128)(2,1)S(1)}, bf16[128,2048]{1,0:T(8,128)(2,1)S(1)}, u32[]{:S(2)}, u32[]{:S(2)}) collective-permute-start(bf16[128,2048]{1,0:T(8,128)(2,1)S(1)} %constant_dynamic-update-slice_fusion.4.refs_0_), channel_id=1, source_target_pairs={{0,4},{4,0},{8,12},{12,8},{16,20},{20,16},{24,28},{28,24},{1,5},{5... | collective-permute-start | bytes 1572872 | tf_op jit(solution)/shard_map/ppermute | solution.py:442
  126.9 2.7 %collective-permute-start.33 = (bf16[128,2048]{1,0:T(8,128)(2,1)S(1)}, bf16[128,2048]{1,0:T(8,128)(2,1)S(1)}, u32[]{:S(2)}, u32[]{:S(2)}) collective-permute-start(bf16[128,2048]{1,0:T(8,128)(2,1)S(1)} %constant_dynamic-update-slice_fusion.2.refs_0_), channel_id=1, source_target_pairs={{0,4},{4,0},{8,12},{12,8},{16,20},{20,16},{24,28},{28,24},{1,5},{5... | collective-permute-start | bytes 1572872 | tf_op jit(solution)/shard_map/ppermute | solution.py:442
  127.6 8.3 %collective-permute-start.23 = (bf16[64,2048]{1,0:T(8,128)(2,1)S(1)}, bf16[64,2048]{1,0:T(8,128)(2,1)S(1)}, u32[]{:S(2)}, u32[]{:S(2)}) collective-permute-start(bf16[64,2048]{1,0:T(8,128)(2,1)S(1)} %get-tuple-element.144), channel_id=1, source_target_pairs={{0,16},{4,20},{8,24},{12,28},{16,0},{20,4},{24,8},{28,12},{1,17},{... | collective-permute-start | bytes 786440 | tf_op jit(solution)/shard_map/ppermute | solution.py:442
  128.4 8.0 %collective-permute-start.22 = (bf16[64,2048]{1,0:T(8,128)(2,1)S(1)}, bf16[64,2048]{1,0:T(8,128)(2,1)S(1)}, u32[]{:S(2)}, u32[]{:S(2)}) collective-permute-start(bf16[64,2048]{1,0:T(8,128)(2,1)S(1)} %get-tuple-element.145), channel_id=1, source_target_pairs={{0,8},{4,12},{8,0},{12,4},{16,24},{20,28},{24,16},{28,20},{1,9},{5... | collective-permute-start | bytes 786440 | tf_op jit(solution)/shard_map/ppermute | solution.py:442
  136.3 9.8 %collective-permute-start.36 = (bf16[1,128,2048]{2,1,0:T(8,128)(2,1)S(1)}, bf16[1,128,2048]{2,1,0:T(8,128)(2,1)S(1)}, u32[]{:S(2)}, u32[]{:S(2)}) collective-permute-start(bf16[1,128,2048]{2,1,0:T(8,128)(2,1)S(1)} %get-tuple-element.114), channel_id=1, source_target_pairs={{0,4},{4,0},{8,12},{12,8},{16,20},{20,16},{24,28},{28,24},{1,5},{5... | collective-permute-start | bytes 1572872 | tf_op jit(solution)/shard_map/ppermute | solution.py:442
  136.3 8.7 %collective-permute-start.43 = (bf16[64,2048]{1,0:T(8,128)(2,1)S(1)}, bf16[64,2048]{1,0:T(8,128)(2,1)S(1)}, u32[]{:S(2)}, u32[]{:S(2)}) collective-permute-start(bf16[64,2048]{1,0:T(8,128)(2,1)S(1)} %get-tuple-element.142), channel_id=1, source_target_pairs={{0,16},{4,20},{8,24},{12,28},{16,0},{20,4},{24,8},{28,12},{1,17},{... | collective-permute-start | bytes 786440 | tf_op jit(solution)/shard_map/ppermute | solution.py:442
  137.7 8.4 %collective-permute-start.42 = (bf16[64,2048]{1,0:T(8,128)(2,1)S(1)}, bf16[64,2048]{1,0:T(8,128)(2,1)S(1)}, u32[]{:S(2)}, u32[]{:S(2)}) collective-permute-start(bf16[64,2048]{1,0:T(8,128)(2,1)S(1)} %get-tuple-element.143), channel_id=1, source_target_pairs={{0,8},{4,12},{8,0},{12,4},{16,24},{20,28},{24,16},{28,20},{1,9},{5... | collective-permute-start | bytes 786440 | tf_op jit(solution)/shard_map/ppermute | solution.py:442
  146.1 2.0 %collective-permute-start.44 = (bf16[1,128,2048]{2,1,0:T(8,128)(2,1)S(1)}, bf16[1,128,2048]{2,1,0:T(8,128)(2,1)S(1)}, u32[]{:S(2)}, u32[]{:S(2)}) collective-permute-start(bf16[1,128,2048]{2,1,0:T(8,128)(2,1)S(1)} %get-tuple-element.121), channel_id=1, source_target_pairs={{0,4},{4,0},{8,12},{12,8},{16,20},{20,16},{24,28},{28,24},{1,5},{5... | collective-permute-start | bytes 1572872 | tf_op jit(solution)/shard_map/ppermute | solution.py:442
  146.2 9.2 %collective-permute-start.39 = (bf16[64,2048]{1,0:T(8,128)(2,1)S(1)}, bf16[64,2048]{1,0:T(8,128)(2,1)S(1)}, u32[]{:S(2)}, u32[]{:S(2)}) collective-permute-start(bf16[64,2048]{1,0:T(8,128)(2,1)S(1)} %get-tuple-element.148), channel_id=1, source_target_pairs={{0,16},{4,20},{8,24},{12,28},{16,0},{20,4},{24,8},{28,12},{1,17},{... | collective-permute-start | bytes 786440 | tf_op jit(solution)/shard_map/ppermute | solution.py:442
  147.0 9.1 %collective-permute-start.37 = (bf16[64,2048]{1,0:T(8,128)(2,1)S(1)}, bf16[64,2048]{1,0:T(8,128)(2,1)S(1)}, u32[]{:S(2)}, u32[]{:S(2)}) collective-permute-start(bf16[64,2048]{1,0:T(8,128)(2,1)S(1)} %get-tuple-element.149), channel_id=1, source_target_pairs={{0,8},{4,12},{8,0},{12,4},{16,24},{20,28},{24,16},{28,20},{1,9},{5... | collective-permute-start | bytes 786440 | tf_op jit(solution)/shard_map/ppermute | solution.py:442
  148.3 12.7 %collective-permute-start.50 = (bf16[64,2048]{1,0:T(8,128)(2,1)S(1)}, bf16[64,2048]{1,0:T(8,128)(2,1)S(1)}, u32[]{:S(2)}, u32[]{:S(2)}) collective-permute-start(bf16[64,2048]{1,0:T(8,128)(2,1)S(1)} %get-tuple-element.146), channel_id=1, source_target_pairs={{0,16},{4,20},{8,24},{12,28},{16,0},{20,4},{24,8},{28,12},{1,17},{... | collective-permute-start | bytes 786440 | tf_op jit(solution)/shard_map/ppermute | solution.py:442
  149.4 12.3 %collective-permute-start.48 = (bf16[64,2048]{1,0:T(8,128)(2,1)S(1)}, bf16[64,2048]{1,0:T(8,128)(2,1)S(1)}, u32[]{:S(2)}, u32[]{:S(2)}) collective-permute-start(bf16[64,2048]{1,0:T(8,128)(2,1)S(1)} %get-tuple-element.147), channel_id=1, source_target_pairs={{0,8},{4,12},{8,0},{12,4},{16,24},{20,28},{24,16},{28,20},{1,9},{5... | collective-permute-start | bytes 786440 | tf_op jit(solution)/shard_map/ppermute | solution.py:442
  156.4 11.0 %collective-permute-start.40 = (bf16[64,2048]{1,0:T(8,128)(2,1)S(1)}, bf16[64,2048]{1,0:T(8,128)(2,1)S(1)}, u32[]{:S(2)}, u32[]{:S(2)}) collective-permute-start(bf16[64,2048]{1,0:T(8,128)(2,1)S(1)} %get-tuple-element.140), channel_id=1, source_target_pairs={{0,8},{4,12},{8,0},{12,4},{16,24},{20,28},{24,16},{28,20},{1,9},{5... | collective-permute-start | bytes 786440 | tf_op jit(solution)/shard_map/ppermute | solution.py:442
  157.6 9.8 %collective-permute-start.38 = (bf16[64,2048]{1,0:T(8,128)(2,1)S(1)}, bf16[64,2048]{1,0:T(8,128)(2,1)S(1)}, u32[]{:S(2)}, u32[]{:S(2)}) collective-permute-start(bf16[64,2048]{1,0:T(8,128)(2,1)S(1)} %get-tuple-element.141), channel_id=1, source_target_pairs={{0,16},{4,20},{8,24},{12,28},{16,0},{20,4},{24,8},{28,12},{1,17},{... | collective-permute-start | bytes 786440 | tf_op jit(solution)/shard_map/ppermute | solution.py:442
  162.0 10.8 %collective-permute-start.51 = (bf16[64,2048]{1,0:T(8,128)(2,1)S(1)}, bf16[64,2048]{1,0:T(8,128)(2,1)S(1)}, u32[]{:S(2)}, u32[]{:S(2)}) collective-permute-start(bf16[64,2048]{1,0:T(8,128)(2,1)S(1)} %get-tuple-element.138), channel_id=1, source_target_pairs={{0,8},{4,12},{8,0},{12,4},{16,24},{20,28},{24,16},{28,20},{1,9},{5... | collective-permute-start | bytes 786440 | tf_op jit(solution)/shard_map/ppermute | solution.py:442
  163.2 9.6 %collective-permute-start.49 = (bf16[64,2048]{1,0:T(8,128)(2,1)S(1)}, bf16[64,2048]{1,0:T(8,128)(2,1)S(1)}, u32[]{:S(2)}, u32[]{:S(2)}) collective-permute-start(bf16[64,2048]{1,0:T(8,128)(2,1)S(1)} %get-tuple-element.139), channel_id=1, source_target_pairs={{0,16},{4,20},{8,24},{12,28},{16,0},{20,4},{24,8},{28,12},{1,17},{... | collective-permute-start | bytes 786440 | tf_op jit(solution)/shard_map/ppermute | solution.py:442
  168.4 8.7 %collective-permute-start.45 = (bf16[128,512]{1,0:T(8,128)(2,1)S(1)}, bf16[128,512]{1,0:T(8,128)(2,1)S(1)}, u32[]{:S(2)}, u32[]{:S(2)}) collective-permute-start(bf16[128,512]{1,0:T(8,128)(2,1)S(1)} %get-tuple-element.127), channel_id=1, source_target_pairs={{0,1},{1,0},{2,3},{3,2},{4,5},{5,4},{6,7},{7,6},{8,9},{9,8},{10,11... | collective-permute-start | bytes 393224 | tf_op jit(solution)/shard_map/ppermute | solution.py:448
  168.8 14.2 %collective-permute-start.46 = (bf16[128,512]{1,0:T(8,128)(2,1)S(1)}, bf16[128,512]{1,0:T(8,128)(2,1)S(1)}, u32[]{:S(2)}, u32[]{:S(2)}) collective-permute-start(bf16[128,512]{1,0:T(8,128)(2,1)S(1)} %get-tuple-element.128), channel_id=1, source_target_pairs={{0,2},{1,3},{2,0},{3,1},{4,6},{5,7},{6,4},{7,5},{8,10},{9,11},{10,... | collective-permute-start | bytes 393224 | tf_op jit(solution)/shard_map/ppermute | solution.py:448
  171.6 11.4 %collective-permute-start.47 = (bf16[128,512]{1,0:T(8,128)(2,1)S(1)}, bf16[128,512]{1,0:T(8,128)(2,1)S(1)}, u32[]{:S(2)}, u32[]{:S(2)}) collective-permute-start(bf16[128,512]{1,0:T(8,128)(2,1)S(1)} %get-tuple-element.129), channel_id=1, source_target_pairs={{0,3},{1,2},{2,1},{3,0},{4,7},{5,6},{6,5},{7,4},{8,11},{9,10},{10,... | collective-permute-start | bytes 393224 | tf_op jit(solution)/shard_map/ppermute | solution.py:448
  173.8 9.2 %collective-permute-start.52 = (bf16[128,512]{1,0:T(8,128)(2,1)S(1)}, bf16[128,512]{1,0:T(8,128)(2,1)S(1)}, u32[]{:S(2)}, u32[]{:S(2)}) collective-permute-start(bf16[128,512]{1,0:T(8,128)(2,1)S(1)} %get-tuple-element.132), channel_id=1, source_target_pairs={{0,1},{1,0},{2,3},{3,2},{4,5},{5,4},{6,7},{7,6},{8,9},{9,8},{10,11... | collective-permute-start | bytes 393224 | tf_op jit(solution)/shard_map/ppermute | solution.py:448
  173.9 18.1 %collective-permute-start.53 = (bf16[128,512]{1,0:T(8,128)(2,1)S(1)}, bf16[128,512]{1,0:T(8,128)(2,1)S(1)}, u32[]{:S(2)}, u32[]{:S(2)}) collective-permute-start(bf16[128,512]{1,0:T(8,128)(2,1)S(1)} %get-tuple-element.133), channel_id=1, source_target_pairs={{0,2},{1,3},{2,0},{3,1},{4,6},{5,7},{6,4},{7,5},{8,10},{9,11},{10,... | collective-permute-start | bytes 393224 | tf_op jit(solution)/shard_map/ppermute | solution.py:448
  177.1 14.9 %collective-permute-start.54 = (bf16[128,512]{1,0:T(8,128)(2,1)S(1)}, bf16[128,512]{1,0:T(8,128)(2,1)S(1)}, u32[]{:S(2)}, u32[]{:S(2)}) collective-permute-start(bf16[128,512]{1,0:T(8,128)(2,1)S(1)} %get-tuple-element.134), channel_id=1, source_target_pairs={{0,3},{1,2},{2,1},{3,0},{4,7},{5,6},{6,5},{7,4},{8,11},{9,10},{10,... | collective-permute-start | bytes 393224 | tf_op jit(solution)/shard_map/ppermute | solution.py:448
  (10 other events, 43.8 us)

commit v13 on v9

--- a/solution.py
+++ b/solution.py
@@ -117,18 +117,13 @@
 
 
 def conv_kernel(
-    experts, mixed_any, rim_ref, taps_ref, steps_ref, cot_ref, ids_ref, weights_ref, qkv_ref, fwd_ref, bwd_ref,
-    pad_ref, mixed_ref, sems,
+    experts, mixed_ref, rim_ref, taps_ref, steps_ref, cot_ref, ids_ref, weights_ref, qkv_ref, fwd_ref, bwd_ref, pad_ref
 ):
     kinds, rows, chans = mixed_ref.shape
-    copies = [pltpu.make_async_copy(mixed_any.at[kind], mixed_ref.at[kind], sems.at[kind]) for kind in range(kinds)]
-    for copy in copies:
-        copy.start()
     heads = steps_ref.shape[0]
     size = chans // heads
     along, down, _ = decay_sums(steps_ref[...])
     for kind in range(kinds):
-        copies[kind].wait()
         pad_ref[:RIM] = rim_ref[kind].astype(F32)
         pad_ref[RIM:] = mixed_ref[kind].astype(F32)
         total = taps_ref[kind, 0:1, :] * pad_ref[RIM:]
@@ -165,18 +160,13 @@
     states = heads * (size + RIM)
     return pl.pallas_call(
         functools.partial(conv_kernel, experts),
-        in_specs=[pl.BlockSpec(memory_space=pl.ANY)] + [pl.BlockSpec(memory_space=pltpu.VMEM)] * 6,
         out_specs=[pl.BlockSpec(memory_space=pltpu.VMEM)] * 3,
         out_shape=[
             jax.ShapeDtypeStruct((kinds, rows, chans), BF),
             jax.ShapeDtypeStruct((states + rows // LANES * 3 * experts, size), BF),
             jax.ShapeDtypeStruct((states, size), BF),
         ],
-        scratch_shapes=[
-            pltpu.VMEM((rows + RIM, chans), F32),
-            pltpu.VMEM(mixed.shape, BF),
-            pltpu.SemaphoreType.DMA((kinds,)),
-        ],
+        scratch_shapes=[pltpu.VMEM((rows + RIM, chans), F32)],
         compiler_params=params(12),
         name="conv_states",
     )(mixed, rim, taps, steps, cot, ids, weights)
@@ -335,8 +325,7 @@
 PAIR = 2
 
 
-def expert_kernel(groups, chunk, experts, where_ref, near_routes, far_routes, gate_ref, up_ref, down_ref, *refs):
-    masks = [mask for group in groups for mask in group]
+def expert_kernel(masks, chunk, experts, where_ref, near_routes, far_routes, gate_ref, up_ref, down_ref, *refs):
     row_refs, outs, (rows_ref, sems) = refs[: len(masks)], refs[len(masks) : -2], refs[-2:]
     _, tok, width = outs[0].shape
     steps = len(masks) // PAIR
@@ -364,15 +353,13 @@
     diagonal = lax.broadcasted_iota(jnp.int32, square, 0) == lax.broadcasted_iota(jnp.int32, square, 1)
     weights = []
     for part in range(PAIR):
-        mask = jnp.int32(masks[part])
+        index = jnp.int32(masks[part] // 2)
         for at in range(1, steps):
-            mask = jnp.where(step == at, masks[PAIR * at + part], mask)
-        index = lax.shift_right_logical(mask, 1)
+            index = jnp.where(step == at, masks[PAIR * at + part] // 2, index)
+        routes_ref = far_routes if masks[part] & CORE else near_routes
         for block in range(tok // LANES):
             base = (chunk // LANES + block) * 3 * experts
-            at = slice(base, base + 3 * experts)
-            near, far = near_routes[index, at, :].astype(F32), far_routes[index, at, :].astype(F32)
-            table = jnp.where((mask & CORE) == 0, near, far)
+            table = routes_ref[index, base : base + 3 * experts, :].astype(F32)
             row = jnp.sum(jnp.where(mine, table, 0.0), axis=0, keepdims=True)
             weights.append(jnp.sum(jnp.where(diagonal, jnp.broadcast_to(row, square), 0.0), axis=1, keepdims=True))
 
@@ -381,17 +368,15 @@
     gate = mm(tokens, gate_ref[0])
     inner = (gate * jax.nn.sigmoid(gate) * mm(tokens, up_ref[0])).astype(BF)
     cols = pick_block(width, 512)
-    per = steps // len(outs)
     for begin in range(0, width, cols):
         piece = mm(inner, down_ref[0, :, begin : begin + cols])
         for at, weight in enumerate(weights):
             part, row = divmod(at * LANES, tok)
             scaled = (piece[at * LANES : (at + 1) * LANES] * weight).astype(BF)
-            for group, out_ref in enumerate(outs):
-
-                @pl.when((step >= group * per) & (step < (group + 1) * per))
-                def _(scaled=scaled, part=part, row=row, out_ref=out_ref):
-                    out_ref[part, row : row + LANES, begin : begin + cols] = scaled
+            if len(outs) > 1:
+                outs[part][0, row : row + LANES, begin : begin + cols] = scaled
+            else:
+                outs[0][part, row : row + LANES, begin : begin + cols] = scaled
 
 
 def stage_kernel(where_ref, *refs):
@@ -413,27 +398,24 @@
 
 
 def expert_pieces(chunk, where, rows, groups, gate, up, down, routes):
-    blocks = [rows[mask] for group in groups for mask in group]
+    split = len(groups)
+    masks = groups[0] if split == 1 else [mask for pair in zip(*groups) for mask in pair]
+    blocks = [rows[mask] for mask in masks]
     tok, width = blocks[0].shape
     hidden = gate.shape[2]
-    count, each = len(blocks), len(groups[0])
-    per = each // PAIR
+    count, each, per = len(blocks), len(groups[0]), PAIR // split
     experts = EXP_CTX * 2 * routes[0].shape[0]
     route_rows = CHUNKS * tok // LANES * 3 * experts
     vmem = pl.BlockSpec(memory_space=pltpu.VMEM)
     table = pl.BlockSpec((routes[0].shape[0], route_rows, LANES), lambda i: (0, 0, 0))
-
-    def out_spec(group):
-        return pl.BlockSpec((PAIR, tok, width), lambda i: (jnp.clip(i - group * per, 0, per - 1), 0, 0))
-
-    return pl.pallas_call(
-        functools.partial(expert_kernel, tuple(map(tuple, groups)), chunk, experts),
+    return pl.pallas_call(
+        functools.partial(expert_kernel, tuple(masks), chunk, experts),
         grid=(count // PAIR,),
         in_specs=[pl.BlockSpec(memory_space=pltpu.SMEM), table, table]
         + [vmem] * 3
         + [pl.BlockSpec(memory_space=pl.ANY)] * count,
-        out_specs=[out_spec(group) for group in range(len(groups))],
-        out_shape=[jax.ShapeDtypeStruct((each, tok, width), BF)] * len(groups),
+        out_specs=[pl.BlockSpec((per, tok, width), lambda i: (i, 0, 0))] * split,
+        out_shape=[jax.ShapeDtypeStruct((each, tok, width), BF)] * split,
         scratch_shapes=[
             pltpu.VMEM((2, PAIR * tok, width), BF),
             pltpu.SemaphoreType.DMA((2,)),
@@ -646,17 +628,18 @@
     bwd = (bwd, swap(after(bwd, own), CORE))
     rows = []
     for chunk in range(CHUNKS):
-        rows.append({0: own, CORE: swap(own, CORE)} | depart(own))
+        rows.append({0: own} | ({CORE: swap(own, CORE)} if chunk else {}) | depart(own))
         if chunk + 1 < CHUNKS:
             parts = send_heads([after(normed[chunk + 1], own)] * n_head)
-            own = join_rows(where, after(parts, rows[chunk][CORE]))
+            own = join_rows(where, parts)
             rows[chunk] = after(rows[chunk], own)
 
     pending, sums, first, arrived = [], [], None, None
     for chunk in range(CHUNKS):
         here_rows = rows[chunk]
         halves = forward(here_rows)
-        here_rows |= {mask | CORE: swap(part, CORE) for mask, part in here_rows.items() if mask and not mask & CORE}
+        lacking = [mask for mask in here_rows if mask | CORE not in here_rows]
+        here_rows |= {mask | CORE: swap(here_rows[mask], CORE) for mask in lacking}
         if pending:
             arrived = after(arrived, [part for mask, part in here_rows.items() if mask & CORE])
             first = first_sums(pending[-1][0], arrived)

time: 196 us -> 192 us (0.980)
  Pallas kernels: 50.4 us -> 44.5 us
  waiting for transfers between devices: 79.2 us -> 82.2 us
    pallas_call x4, Pallas kernels: 27.1 us -> 21.2 us  [the longest x3 19.1 us: expert_pieces(): pl.pallas_call(functools.partial(expert_kernel, tuple(masks), chunk, expe...]
    ppermute x33, waiting for transfers between devices: 38.8 us -> 44.1 us  [swap(): lax.ppermute(value, 'ctx', [(at, at ^ mask) for at in range(lax.axis_size...]
    ppermute x15, waiting for transfers between devices: 39.3 us -> 37 us  [send_heads(): lax.ppermute(parts[mask], 'head', [(at, at ^ mask) for at in range(count)])]
  transfers between devices with their start and end apart: 49 -> 49, of which waited for: 27 -> 26; matrix products, arithmetic and copies ran while one was open for 1% -> 1% of each run, Pallas kernels for 17% -> 15%
where the time goes in v13:
time: 192 us
  waiting for transfers between devices  82.2 us (43%)
  starting transfers between devices  57.9 us (30%)
  Pallas kernels  44.5 us (23%)
  local copies, waits for them, and re-layouts  4.58 us (2%)
    ppermute x33, waiting for transfers between devices, swap(): lax.ppermute(value, 'ctx', [(at, at ^ mask) for at in range(lax.axis_size...  44.1 us
    ppermute x15, waiting for transfers between devices, send_heads(): lax.ppermute(parts[mask], 'head', [(at, at ^ mask) for at in range(count)])  37 us
    ppermute x33, starting transfers between devices, swap(): lax.ppermute(value, 'ctx', [(at, at ^ mask) for at in range(lax.axis_size...  29.9 us
    ppermute x15, starting transfers between devices, send_heads(): lax.ppermute(parts[mask], 'head', [(at, at ^ mask) for at in range(count)])  25.5 us
    pallas_call x3, Pallas kernels, expert_pieces(): pl.pallas_call(functools.partial(expert_kernel, tuple(masks), chunk, expe...  19.1 us
    pallas_call x1, Pallas kernels, project(): pl.pallas_call(qkv_kernel, in_specs=[hbm, vmem, hbm], out_specs=[vmem, vm...  7.28 us
    pallas_call x1, Pallas kernels, core_grads(): pl.pallas_call(grad_kernel, in_specs=[pl.BlockSpec(memory_space=pltpu.SME...  4.7 us
    unnamed x41, local copies, waits for them, and re-layouts  4.43 us
  transfers between devices with their start and end apart: 49, of which 26 were waited for; matrix products, arithmetic and copies ran while one was open for 1% of the time, Pallas kernels for 15%

profile of v13, /device:TPU:0, one launch (start us, length us, event | category | flops | bytes accessed | tf_op | source)
XLA Modules:
  0.0 191.9 jit_solution(2526459516919666455)
XLA Ops:
  0.7 7.3 %qkv_projection.1 = (bf16[3,256,512]{2,1,0:T(8,128)(2,1)}, bf16[3,16,512]{2,1,0:T(8,128)(2,1)}) custom-call(bf16[256,2048]{1,0:T(8,128)(2,1)} %x_ref.3, f32[1,2048]{1,0:T(1,128)} %bitcast.63, bf16[3,2048,512]{2,1,0:T(8,128)(2,1)} %bitcast.59), custom_call_target="tpu_custom_call" | custom-call | tf_op jit(solution)/shard_map/qkv_projection/pallas_call | solution.py:68
  8.0 2.5 %collective-permute-start = (bf16[3,16,512]{2,1,0:T(8,128)(2,1)}, bf16[3,16,512]{2,1,0:T(8,128)(2,1)S(1)}, u32[]{:S(2)}, u32[]{:S(2)}) collective-permute-start(bf16[3,16,512]{2,1,0:T(8,128)(2,1)} %get-tuple-element.72), channel_id=1, source_target_pairs={{0,4},{4,8},{8,12},{12,16},{16,20},{20,24},{24,28},{1,5},{5,9},{9,... | collective-permute-start | bytes 147464 | tf_op jit(solution)/shard_map/ppermute | solution.py:610
  10.5 1.1 collective-permute-done.rim_ref
  11.6 1.1 copy-done.10
  12.7 2.2 %conv_states.1 = (bf16[3,256,512]{2,1,0:T(8,128)(2,1)S(1)}, bf16[672,128]{1,0:T(8,128)(2,1)S(1)}, bf16[576,128]{1,0:T(8,128)(2,1)S(1)}) custom-call(bf16[3,256,512]{2,1,0:T(8,128)(2,1)S(1)} %copy-done.10, bf16[3,16,512]{2,1,0:T(8,128)(2,1)S(1)} %collective-permute-done.rim_ref, f32[3,4,512]{2,1,0:T(4,128)S(1)} %bitcast.54, f32[4,256]{1,0:T(4,128)S(1)} %bitcast.51, ...), custom_call_target="tpu_custom_call" | custom-call | tf_op jit(solution)/shard_map/conv_states/pallas_call | solution.py:161
  14.9 0.9 copy-done.2
  16.5 6.1 %collective-permute-start.3 = (bf16[672,128]{1,0:T(8,128)(2,1)S(1)}, bf16[672,128]{1,0:T(8,128)(2,1)S(1)}, u32[]{:S(2)}, u32[]{:S(2)}) collective-permute-start(bf16[672,128]{1,0:T(8,128)(2,1)S(1)} %get-tuple-element.75), channel_id=1, source_target_pairs={{0,24},{4,28},{8,16},{12,20},{16,8},{20,12},{24,0},{28,4},{1,25},{... | collective-permute-start | bytes 516104 | tf_op jit(solution)/shard_map/ppermute | solution.py:438
  23.1 0.9 collective-permute-start.1
  24.0 3.8 %collective-permute-done.3 = bf16[672,128]{1,0:T(8,128)(2,1)S(1)} collective-permute-done((bf16[672,128]{1,0:T(8,128)(2,1)S(1)}, bf16[672,128]{1,0:T(8,128)(2,1)S(1)}, u32[]{:S(2)}, u32[]{:S(2)}) %collective-permute-start.3) | collective-permute-done | bytes 172064 | tf_op jit(solution)/shard_map/ppermute | solution.py:438
  27.8 2.5 %collective-permute-done.2 = bf16[672,128]{1,0:T(8,128)(2,1)S(1)} collective-permute-done((bf16[672,128]{1,0:T(8,128)(2,1)S(1)}, bf16[672,128]{1,0:T(8,128)(2,1)S(1)}, u32[]{:S(2)}, u32[]{:S(2)}) %collective-permute-start.2) | collective-permute-done | bytes 172064 | tf_op jit(solution)/shard_map/ppermute | solution.py:438
  30.7 1.1 stage_weights.2.me_ref.where_ref
  31.8 0.9 collective-permute-done.4.far_ref.far_routes.fwd_far
  32.7 3.7 %core_out.1 = (bf16[64,2048]{1,0:T(8,128)(2,1)S(1)}, bf16[64,2048]{1,0:T(8,128)(2,1)S(1)}, bf16[64,2048]{1,0:T(8,128)(2,1)S(1)}, bf16[64,2048]{1,0:T(8,128)(2,1)S(1)}) custom-call(s32[3]{0:T(128)S(1)} %stage_weights.2.me_ref.where_ref, bf16[3,256,512]{2,1,0:T(8,128)(2,1)S(1)} %copy-done.3, f32[4,256]{1,0:T(4,128)S(1)} %bitcast.52, f32[1,512]{1,0:T(1,128)S(1)} %bitcast.58, ...), custom_call_target="tpu_custom_call" | custom-call | tf_op jit(solution)/shard_map/core_out/pallas_call | solution.py:223
  36.4 1.7 collective-permute-start.8
  38.1 1.6 collective-permute-start.5
  39.7 2.6 %collective-permute-start.6 = (bf16[64,2048]{1,0:T(8,128)(2,1)S(1)}, bf16[64,2048]{1,0:T(8,128)(2,1)S(1)}, u32[]{:S(2)}, u32[]{:S(2)}) collective-permute-start(bf16[64,2048]{1,0:T(8,128)(2,1)S(1)} %get-tuple-element.78), channel_id=1, source_target_pairs={{0,2},{1,3},{2,0},{3,1},{4,6},{5,7},{6,4},{7,5},{8,10},{9,11},{10,... | collective-permute-start | bytes 786440 | tf_op jit(solution)/shard_map/ppermute | solution.py:444
  42.5 1.6 copy-done.6
  44.1 1.1 stage_weights.3.where_ref.me_ref
  45.3 5.9 %collective-permute-done.5.refs_1_ = bf16[64,2048]{1,0:T(8,128)(2,1)S(1)} collective-permute-done((bf16[64,2048]{1,0:T(8,128)(2,1)S(1)}, bf16[64,2048]{1,0:T(8,128)(2,1)S(1)}, u32[]{:S(2)}, u32[]{:S(2)}) %collective-permute-start.5) | collective-permute-done | bytes 262176 | tf_op jit(solution)/shard_map/ppermute | solution.py:444
  51.1 9.9 %collective-permute-done.6.refs_2_ = bf16[64,2048]{1,0:T(8,128)(2,1)S(1)} collective-permute-done((bf16[64,2048]{1,0:T(8,128)(2,1)S(1)}, bf16[64,2048]{1,0:T(8,128)(2,1)S(1)}, u32[]{:S(2)}, u32[]{:S(2)}) %collective-permute-start.6) | collective-permute-done | bytes 262176 | tf_op jit(solution)/shard_map/ppermute | solution.py:444
  61.0 0.9 moe_norm.1
  61.9 1.0 collective-permute-start.12
  62.9 2.5 %collective-permute-start.11 = (bf16[32,2048]{1,0:T(8,128)(2,1)S(1)}, bf16[32,2048]{1,0:T(8,128)(2,1)S(1)}, u32[]{:S(2)}, u32[]{:S(2)}) collective-permute-start(bf16[32,2048]{1,0:T(8,128)(2,1)S(1)} %get-tuple-element.91.refs_0_), channel_id=1, source_target_pairs={{0,3},{1,2},{2,1},{3,0},{4,7},{5,6},{6,5},{7,4},{8,11},{9,10},{10,... | collective-permute-start | bytes 393224 | tf_op jit(solution)/shard_map/ppermute | solution.py:444
  65.3 5.3 %collective-permute-start.10 = (bf16[32,2048]{1,0:T(8,128)(2,1)S(1)}, bf16[32,2048]{1,0:T(8,128)(2,1)S(1)}, u32[]{:S(2)}, u32[]{:S(2)}) collective-permute-start(bf16[32,2048]{1,0:T(8,128)(2,1)S(1)} %get-tuple-element.91.refs_0_), channel_id=1, source_target_pairs={{0,2},{1,3},{2,0},{3,1},{4,6},{5,7},{6,4},{7,5},{8,10},{9,11},{10,... | collective-permute-start | bytes 393224 | tf_op jit(solution)/shard_map/ppermute | solution.py:444
  70.8 7.2 %collective-permute-done.10.refs_2_ = bf16[32,2048]{1,0:T(8,128)(2,1)S(1)} collective-permute-done((bf16[32,2048]{1,0:T(8,128)(2,1)S(1)}, bf16[32,2048]{1,0:T(8,128)(2,1)S(1)}, u32[]{:S(2)}, u32[]{:S(2)}) %collective-permute-start.10) | collective-permute-done | bytes 131104 | tf_op jit(solution)/shard_map/ppermute | solution.py:444
  78.7 1.2 collective-permute-start.14
  80.3 2.6 %collective-permute-start.17 = (bf16[32,2048]{1,0:T(8,128)(2,1)S(1)}, bf16[32,2048]{1,0:T(8,128)(2,1)S(1)}, u32[]{:S(2)}, u32[]{:S(2)}) collective-permute-start(bf16[32,2048]{1,0:T(8,128)(2,1)S(1)} %get-tuple-element.95.refs_0_), channel_id=1, source_target_pairs={{0,3},{1,2},{2,1},{3,0},{4,7},{5,6},{6,5},{7,4},{8,11},{9,10},{10,... | collective-permute-start | bytes 393224 | tf_op jit(solution)/shard_map/ppermute | solution.py:444
  82.9 1.7 collective-permute-start.15
  84.7 3.7 %collective-permute-done.17.refs_3_ = bf16[32,2048]{1,0:T(8,128)(2,1)S(1)} collective-permute-done((bf16[32,2048]{1,0:T(8,128)(2,1)S(1)}, bf16[32,2048]{1,0:T(8,128)(2,1)S(1)}, u32[]{:S(2)}, u32[]{:S(2)}) %collective-permute-start.17) | collective-permute-done | bytes 131104 | tf_op jit(solution)/shard_map/ppermute | solution.py:444
  88.3 3.7 %collective-permute-done.16.refs_2_ = bf16[32,2048]{1,0:T(8,128)(2,1)S(1)} collective-permute-done((bf16[32,2048]{1,0:T(8,128)(2,1)S(1)}, bf16[32,2048]{1,0:T(8,128)(2,1)S(1)}, u32[]{:S(2)}, u32[]{:S(2)}) %collective-permute-start.16) | collective-permute-done | bytes 131104 | tf_op jit(solution)/shard_map/ppermute | solution.py:444
  92.7 1.7 collective-permute-start.21
  94.4 0.8 collective-permute-start.22
  95.7 4.0 %collective-permute-done.21 = bf16[64,2048]{1,0:T(8,128)(2,1)S(1)} collective-permute-done((bf16[64,2048]{1,0:T(8,128)(2,1)S(1)}, bf16[64,2048]{1,0:T(8,128)(2,1)S(1)}, u32[]{:S(2)}, u32[]{:S(2)}) %collective-permute-start.21) | collective-permute-done | bytes 262176 | tf_op jit(solution)/shard_map/ppermute | solution.py:438
  99.8 1.5 collective-permute-done.22
  102.2 1.5 collective-permute-start.25
  103.7 9.4 %expert_pieces.3 = (bf16[4,128,2048]{2,1,0:T(8,128)(2,1)S(1)}, bf16[4,128,2048]{2,1,0:T(8,128)(2,1)S(1)}) custom-call(s32[3]{0:T(128)S(1)} %stage_weights.3.where_ref.me_ref, bf16[4,672,128]{2,1,0:T(8,128)(2,1)S(1)} %pad_maximum_fusion.near_ref.near_routes.fwd_near, bf16[4,672,128]{2,1,0:T(8,128)(2,1)S(1)} %collective-permute-done.4.far_ref.far_routes.fwd_far, ...), custom_call_target="tpu_custom_call" | custom-call | flops 6442450944 | bytes 8388608 | tf_op jit(solution)/shard_map/expert_pieces/pallas_call | solution.py:411
  113.1 2.6 %collective-permute-done.26.refs_2_ = bf16[128,2048]{1,0:T(8,128)(2,1)S(1)} collective-permute-done((bf16[128,2048]{1,0:T(8,128)(2,1)S(1)}, bf16[128,2048]{1,0:T(8,128)(2,1)S(1)}, u32[]{:S(2)}, u32[]{:S(2)}) %collective-permute-start.26) | collective-permute-done | bytes 524320 | tf_op jit(solution)/shard_map/ppermute | solution.py:438
  116.4 1.5 collective-permute-start.36
  117.9 1.0 collective-permute-start.35
  118.9 1.8 collective-permute-done.30.refs_2_
  122.0 3.2 %collective-permute-done.36 = bf16[64,2048]{1,0:T(8,128)(2,1)S(1)} collective-permute-done((bf16[64,2048]{1,0:T(8,128)(2,1)S(1)}, bf16[64,2048]{1,0:T(8,128)(2,1)S(1)}, u32[]{:S(2)}, u32[]{:S(2)}) %collective-permute-start.36) | collective-permute-done | bytes 262176 | tf_op jit(solution)/shard_map/ppermute | solution.py:438
  125.1 1.3 collective-permute-done.35
  127.2 1.7 collective-permute-start.32
  128.8 4.8 %expert_pieces.4 = bf16[4,128,2048]{2,1,0:T(8,128)(2,1)S(1)} custom-call(s32[3]{0:T(128)S(1)} %stage_weights.3.where_ref.me_ref, bf16[4,672,128]{2,1,0:T(8,128)(2,1)S(1)} %pad_maximum_fusion.near_ref.near_routes.fwd_near, bf16[4,672,128]{2,1,0:T(8,128)(2,1)S(1)} %collective-permute-done.4.far_ref.far_routes.fwd_far, bf16[1,2048,512]{2,1,0:T(8,128)(2,1)S(1)} %copy-done.4, ...), custom_call_target="tpu_custom_call" | custom-call | flops 3221225472 | bytes 4194304 | tf_op jit(solution)/shard_map/expert_pieces/pallas_call | solution.py:411
  133.7 7.2 %collective-permute-done.31.refs_0_ = bf16[128,2048]{1,0:T(8,128)(2,1)S(1)} collective-permute-done((bf16[128,2048]{1,0:T(8,128)(2,1)S(1)}, bf16[128,2048]{1,0:T(8,128)(2,1)S(1)}, u32[]{:S(2)}, u32[]{:S(2)}) %collective-permute-start.31) | collective-permute-done | bytes 524320 | tf_op jit(solution)/shard_map/ppermute | solution.py:438
  141.4 1.6 collective-permute-start.34
  143.0 0.9 collective-permute-start.33
  143.9 4.8 %expert_pieces.5.near_ref = bf16[4,128,2048]{2,1,0:T(8,128)(2,1)S(1)} custom-call(s32[3]{0:T(128)S(1)} %stage_weights.3.where_ref.me_ref, bf16[4,672,128]{2,1,0:T(8,128)(2,1)S(1)} %pad_maximum_fusion.near_ref.near_routes.fwd_near, bf16[4,672,128]{2,1,0:T(8,128)(2,1)S(1)} %collective-permute-done.4.far_ref.far_routes.fwd_far, ...), custom_call_target="tpu_custom_call" | custom-call | flops 3221225472 | bytes 4194304 | tf_op jit(solution)/shard_map/expert_pieces/pallas_call | solution.py:411
  148.7 1.5 collective-permute-done.34.refs_3_
  150.2 1.2 collective-permute-done.33.refs_2_
  152.5 1.7 collective-permute-start.43
  154.2 1.0 sum_terms.2
  155.2 9.9 %collective-permute-done.42.refs_0_ = bf16[128,2048]{1,0:T(8,128)(2,1)S(1)} collective-permute-done((bf16[128,2048]{1,0:T(8,128)(2,1)S(1)}, bf16[128,2048]{1,0:T(8,128)(2,1)S(1)}, u32[]{:S(2)}, u32[]{:S(2)}) %collective-permute-start.42) | collective-permute-done | bytes 524320 | tf_op jit(solution)/shard_map/ppermute | solution.py:438
  165.8 1.5 collective-permute-start.45
  167.3 0.9 collective-permute-start.44
  168.3 2.8 %collective-permute-start.40 = (bf16[128,512]{1,0:T(8,128)(2,1)S(1)}, bf16[128,512]{1,0:T(8,128)(2,1)S(1)}, u32[]{:S(2)}, u32[]{:S(2)}) collective-permute-start(bf16[128,512]{1,0:T(8,128)(2,1)S(1)} %get-tuple-element.126), channel_id=1, source_target_pairs={{0,2},{1,3},{2,0},{3,1},{4,6},{5,7},{6,4},{7,5},{8,10},{9,11},{10,... | collective-permute-start | bytes 393224 | tf_op jit(solution)/shard_map/ppermute | solution.py:444
  171.1 1.5 collective-permute-start.41
  172.6 1.1 collective-permute-done.44.refs_2_
  173.7 1.0 sum_terms.3
  174.8 2.8 %collective-permute-start.47 = (bf16[128,512]{1,0:T(8,128)(2,1)S(1)}, bf16[128,512]{1,0:T(8,128)(2,1)S(1)}, u32[]{:S(2)}, u32[]{:S(2)}) collective-permute-start(bf16[128,512]{1,0:T(8,128)(2,1)S(1)} %get-tuple-element.133), channel_id=1, source_target_pairs={{0,2},{1,3},{2,0},{3,1},{4,6},{5,7},{6,4},{7,5},{8,10},{9,11},{10,... | collective-permute-start | bytes 393224 | tf_op jit(solution)/shard_map/ppermute | solution.py:444
  177.6 1.6 collective-permute-start.48
  179.2 4.7 %core_grads.1 = (bf16[256,512]{1,0:T(8,128)(2,1)}, bf16[256,512]{1,0:T(8,128)(2,1)}, bf16[256,512]{1,0:T(8,128)(2,1)}) custom-call(s32[3]{0:T(128)S(1)} %stage_weights.3.where_ref.me_ref, bf16[3,256,512]{2,1,0:T(8,128)(2,1)S(1)} %copy-done.3, bf16[256,512]{1,0:T(8,128)(2,1)S(1)} %copy-done.9, f32[4,256]{1,0:T(4,128)S(1)} %bitcast.53, ...), custom_call_target="tpu_custom_call" | custom-call | tf_op jit(solution)/shard_map/core_grads/pallas_call | solution.py:268
  183.9 6.6 %collective-permute-done.47.refs_6_ = bf16[128,512]{1,0:T(8,128)(2,1)S(1)} collective-permute-done((bf16[128,512]{1,0:T(8,128)(2,1)S(1)}, bf16[128,512]{1,0:T(8,128)(2,1)S(1)}, u32[]{:S(2)}, u32[]{:S(2)}) %collective-permute-start.47) | collective-permute-done | bytes 131104 | tf_op jit(solution)/shard_map/ppermute | solution.py:444
  190.5 1.4 layer_out.1
  (108 shorter events, 10.0 us)
Async XLA Ops:
  0.6 10.9 %copy-start.8 = (bf16[256,512]{1,0:T(8,128)(2,1)S(1)}, bf16[256,512]{1,0:T(8,128)(2,1)}, u32[]{:S(2)}) copy-start(bf16[256,512]{1,0:T(8,128)(2,1)} %cot_ref.3) | copy-start | bytes 786436
  0.6 10.9 %copy-start.13 = (f32[256,4]{0,1:T(4,128)S(1)}, f32[256,4]{0,1:T(4,128)}, u32[]{:S(2)}) copy-start(f32[256,4]{0,1:T(4,128)} %param.18) | copy-start | bytes 12292
  0.7 10.9 %copy-start.14 = (f32[4,3,512]{2,0,1:T(4,128)S(1)}, f32[4,3,512]{2,0,1:T(4,128)}, u32[]{:S(2)}) copy-start(f32[4,3,512]{2,0,1:T(4,128)} %param.17) | copy-start | bytes 73732
  0.7 10.9 %copy-start.15 = (s32[256,8]{0,1:T(8,128)S(1)}, s32[256,8]{0,1:T(8,128)}, u32[]{:S(2)}) copy-start(s32[256,8]{0,1:T(8,128)} %param.22) | copy-start | bytes 24580
  0.7 10.9 %copy-start.16 = (f32[256,8]{0,1:T(8,128)S(1)}, f32[256,8]{0,1:T(8,128)}, u32[]{:S(2)}) copy-start(f32[256,8]{0,1:T(8,128)} %param.23) | copy-start | bytes 24580
  8.0 22.7 %copy-start.1 = (bf16[512,2048]{1,0:T(8,128)(2,1)S(1)}, bf16[512,2048]{1,0:T(8,128)(2,1)}, u32[]{:S(2)}) copy-start(bf16[512,2048]{1,0:T(8,128)(2,1)} %w_ref.1) | copy-start | bytes 6291460
  8.0 3.6 %collective-permute-start = (bf16[3,16,512]{2,1,0:T(8,128)(2,1)}, bf16[3,16,512]{2,1,0:T(8,128)(2,1)S(1)}, u32[]{:S(2)}, u32[]{:S(2)}) collective-permute-start(bf16[3,16,512]{2,1,0:T(8,128)(2,1)} %get-tuple-element.72), channel_id=1, source_target_pairs={{0,4},{4,8},{8,12},{12,16},{16,20},{20,24},{24,28},{1,5},{5,9},{9,... | collective-permute-start | bytes 147464 | tf_op jit(solution)/shard_map/ppermute | solution.py:610
  12.7 20.0 %copy-start.18 = (f32[512]{0:T(512)S(1)}, f32[512]{0:T(512)}, u32[]{:S(2)}) copy-start(f32[512]{0:T(512)} %param.19) | copy-start | bytes 6148
  16.5 11.4 %collective-permute-start.3 = (bf16[672,128]{1,0:T(8,128)(2,1)S(1)}, bf16[672,128]{1,0:T(8,128)(2,1)S(1)}, u32[]{:S(2)}, u32[]{:S(2)}) collective-permute-start(bf16[672,128]{1,0:T(8,128)(2,1)S(1)} %get-tuple-element.75), channel_id=1, source_target_pairs={{0,24},{4,28},{8,16},{12,20},{16,8},{20,12},{24,0},{28,4},{1,25},{... | collective-permute-start | bytes 516104 | tf_op jit(solution)/shard_map/ppermute | solution.py:438
  22.6 7.8 %collective-permute-start.2 = (bf16[672,128]{1,0:T(8,128)(2,1)S(1)}, bf16[672,128]{1,0:T(8,128)(2,1)S(1)}, u32[]{:S(2)}, u32[]{:S(2)}) collective-permute-start(bf16[672,128]{1,0:T(8,128)(2,1)S(1)} %get-tuple-element.75), channel_id=1, source_target_pairs={{0,16},{4,20},{8,24},{12,28},{16,0},{20,4},{24,8},{28,12},{1,17},{... | collective-permute-start | bytes 516104 | tf_op jit(solution)/shard_map/ppermute | solution.py:438
  23.1 7.3 %collective-permute-start.1 = (bf16[672,128]{1,0:T(8,128)(2,1)S(1)}, bf16[672,128]{1,0:T(8,128)(2,1)S(1)}, u32[]{:S(2)}, u32[]{:S(2)}) collective-permute-start(bf16[672,128]{1,0:T(8,128)(2,1)S(1)} %get-tuple-element.75), channel_id=1, source_target_pairs={{0,8},{4,12},{8,0},{12,4},{16,24},{20,28},{24,16},{28,20},{1,9},{5... | collective-permute-start | bytes 516104 | tf_op jit(solution)/shard_map/ppermute | solution.py:438
  30.5 2.2 %collective-permute-start.4 = (bf16[4,672,128]{2,1,0:T(8,128)(2,1)S(1)}, bf16[4,672,128]{2,1,0:T(8,128)(2,1)S(1)}, u32[]{:S(2)}, u32[]{:S(2)}) collective-permute-start(bf16[4,672,128]{2,1,0:T(8,128)(2,1)S(1)} %pad_maximum_fusion.near_ref.near_routes.fwd_near), channel_id=1, source_target_pairs={{0,4},{4,0},{8,12},{12,8},{16,20},{20,16},{24,28},{28,24},{1,5},{5... | collective-permute-start | bytes 2064392 | tf_op jit(solution)/shard_map/ppermute | solution.py:438
  30.6 2.1 %copy-start.3 = (bf16[3,256,512]{2,1,0:T(8,128)(2,1)S(1)}, bf16[3,256,512]{2,1,0:T(8,128)(2,1)}, u32[]{:S(2)}) copy-start(bf16[3,256,512]{2,1,0:T(8,128)(2,1)} %copy-done.2) | copy-start | bytes 2359300
  30.7 5.7 %copy-start.12 = (bf16[576,128]{1,0:T(8,128)(2,1)S(1)}, bf16[576,128]{1,0:T(8,128)(2,1)}, u32[]{:S(2)}) copy-start(bf16[576,128]{1,0:T(8,128)(2,1)} %copy-done.11) | copy-start | bytes 442372
  32.7 9.8 %copy-start.4 = (bf16[1,2048,512]{2,1,0:T(8,128)(2,1)S(1)}, bf16[1,2048,512]{2,1,0:T(8,128)(2,1)}, u32[]{:S(2)}) copy-start(bf16[1,2048,512]{2,1,0:T(8,128)(2,1)} %gate_ref.5) | copy-start | bytes 6291460
  32.7 9.8 %copy-start.5 = (bf16[1,2048,512]{2,1,0:T(8,128)(2,1)S(1)}, bf16[1,2048,512]{2,1,0:T(8,128)(2,1)}, u32[]{:S(2)}) copy-start(bf16[1,2048,512]{2,1,0:T(8,128)(2,1)} %up_ref.5) | copy-start | bytes 6291460
  36.4 24.6 %copy-start = (bf16[256,2048]{1,0:T(8,128)(2,1)S(1)}, bf16[256,2048]{1,0:T(8,128)(2,1)}, u32[]{:S(2)}) copy-start(bf16[256,2048]{1,0:T(8,128)(2,1)} %x_ref.3) | copy-start | bytes 3145732
  36.4 8.8 %collective-permute-start.8 = (bf16[1,576,128]{2,1,0:T(8,128)(2,1)S(1)}, bf16[1,576,128]{2,1,0:T(8,128)(2,1)S(1)}, u32[]{:S(2)}, u32[]{:S(2)}) collective-permute-start(bf16[1,576,128]{2,1,0:T(8,128)(2,1)S(1)} %bitcast.49), channel_id=1, source_target_pairs={{0,8},{4,12},{8,0},{12,4},{16,24},{20,28},{24,16},{28,20},{1,9},{5... | collective-permute-start | bytes 442376 | tf_op jit(solution)/shard_map/ppermute | solution.py:438
  38.1 13.0 %collective-permute-start.5 = (bf16[64,2048]{1,0:T(8,128)(2,1)S(1)}, bf16[64,2048]{1,0:T(8,128)(2,1)S(1)}, u32[]{:S(2)}, u32[]{:S(2)}) collective-permute-start(bf16[64,2048]{1,0:T(8,128)(2,1)S(1)} %get-tuple-element.77), channel_id=1, source_target_pairs={{0,1},{1,0},{2,3},{3,2},{4,5},{5,4},{6,7},{7,6},{8,9},{9,8},{10,11... | collective-permute-start | bytes 786440 | tf_op jit(solution)/shard_map/ppermute | solution.py:444
  39.7 21.4 %collective-permute-start.6 = (bf16[64,2048]{1,0:T(8,128)(2,1)S(1)}, bf16[64,2048]{1,0:T(8,128)(2,1)S(1)}, u32[]{:S(2)}, u32[]{:S(2)}) collective-permute-start(bf16[64,2048]{1,0:T(8,128)(2,1)S(1)} %get-tuple-element.78), channel_id=1, source_target_pairs={{0,2},{1,3},{2,0},{3,1},{4,6},{5,7},{6,4},{7,5},{8,10},{9,11},{10,... | collective-permute-start | bytes 786440 | tf_op jit(solution)/shard_map/ppermute | solution.py:444
  42.3 18.8 %collective-permute-start.7 = (bf16[64,2048]{1,0:T(8,128)(2,1)S(1)}, bf16[64,2048]{1,0:T(8,128)(2,1)S(1)}, u32[]{:S(2)}, u32[]{:S(2)}) collective-permute-start(bf16[64,2048]{1,0:T(8,128)(2,1)S(1)} %get-tuple-element.79), channel_id=1, source_target_pairs={{0,3},{1,2},{2,1},{3,0},{4,7},{5,6},{6,5},{7,4},{8,11},{9,10},{10,... | collective-permute-start | bytes 786440 | tf_op jit(solution)/shard_map/ppermute | solution.py:444
  44.1 17.0 %copy-start.17 = (f32[2048]{0:T(1024)S(1)}, f32[2048]{0:T(1024)}, u32[]{:S(2)}) copy-start(f32[2048]{0:T(1024)} %param.21) | copy-start | bytes 24580
  61.9 8.8 %collective-permute-start.12 = (bf16[2,576,128]{2,1,0:T(8,128)(2,1)S(1)}, bf16[2,576,128]{2,1,0:T(8,128)(2,1)S(1)}, u32[]{:S(2)}, u32[]{:S(2)}) collective-permute-start(bf16[2,576,128]{2,1,0:T(8,128)(2,1)S(1)} %pad_maximum_fusion.5), channel_id=1, source_target_pairs={{0,16},{4,20},{8,24},{12,28},{16,0},{20,4},{24,8},{28,12},{1,17},{... | collective-permute-start | bytes 884744 | tf_op jit(solution)/shard_map/ppermute | solution.py:438
  62.9 7.9 %collective-permute-start.11 = (bf16[32,2048]{1,0:T(8,128)(2,1)S(1)}, bf16[32,2048]{1,0:T(8,128)(2,1)S(1)}, u32[]{:S(2)}, u32[]{:S(2)}) collective-permute-start(bf16[32,2048]{1,0:T(8,128)(2,1)S(1)} %get-tuple-element.91.refs_0_), channel_id=1, source_target_pairs={{0,3},{1,2},{2,1},{3,0},{4,7},{5,6},{6,5},{7,4},{8,11},{9,10},{10,... | collective-permute-start | bytes 393224 | tf_op jit(solution)/shard_map/ppermute | solution.py:444
  65.3 12.7 %collective-permute-start.10 = (bf16[32,2048]{1,0:T(8,128)(2,1)S(1)}, bf16[32,2048]{1,0:T(8,128)(2,1)S(1)}, u32[]{:S(2)}, u32[]{:S(2)}) collective-permute-start(bf16[32,2048]{1,0:T(8,128)(2,1)S(1)} %get-tuple-element.91.refs_0_), channel_id=1, source_target_pairs={{0,2},{1,3},{2,0},{3,1},{4,6},{5,7},{6,4},{7,5},{8,10},{9,11},{10,... | collective-permute-start | bytes 393224 | tf_op jit(solution)/shard_map/ppermute | solution.py:444
  70.6 7.5 %collective-permute-start.9 = (bf16[32,2048]{1,0:T(8,128)(2,1)S(1)}, bf16[32,2048]{1,0:T(8,128)(2,1)S(1)}, u32[]{:S(2)}, u32[]{:S(2)}) collective-permute-start(bf16[32,2048]{1,0:T(8,128)(2,1)S(1)} %get-tuple-element.91.refs_0_), channel_id=1, source_target_pairs={{0,1},{1,0},{2,3},{3,2},{4,5},{5,4},{6,7},{7,6},{8,9},{9,8},{10,11... | collective-permute-start | bytes 393224 | tf_op jit(solution)/shard_map/ppermute | solution.py:444
  78.7 14.0 %collective-permute-start.14 = (bf16[128,2048]{1,0:T(8,128)(2,1)S(1)}, bf16[128,2048]{1,0:T(8,128)(2,1)S(1)}, u32[]{:S(2)}, u32[]{:S(2)}) collective-permute-start(bf16[128,2048]{1,0:T(8,128)(2,1)S(1)} %join_rows.2.refs_0_), channel_id=1, source_target_pairs={{0,16},{4,20},{8,24},{12,28},{16,0},{20,4},{24,8},{28,12},{1,17},{... | collective-permute-start | bytes 1572872 | tf_op jit(solution)/shard_map/ppermute | solution.py:438
  79.9 12.8 %collective-permute-start.13 = (bf16[128,2048]{1,0:T(8,128)(2,1)S(1)}, bf16[128,2048]{1,0:T(8,128)(2,1)S(1)}, u32[]{:S(2)}, u32[]{:S(2)}) collective-permute-start(bf16[128,2048]{1,0:T(8,128)(2,1)S(1)} %join_rows.2.refs_0_), channel_id=1, source_target_pairs={{0,8},{4,12},{8,0},{12,4},{16,24},{20,28},{24,16},{28,20},{1,9},{5... | collective-permute-start | bytes 1572872 | tf_op jit(solution)/shard_map/ppermute | solution.py:438
  80.3 8.1 %collective-permute-start.17 = (bf16[32,2048]{1,0:T(8,128)(2,1)S(1)}, bf16[32,2048]{1,0:T(8,128)(2,1)S(1)}, u32[]{:S(2)}, u32[]{:S(2)}) collective-permute-start(bf16[32,2048]{1,0:T(8,128)(2,1)S(1)} %get-tuple-element.95.refs_0_), channel_id=1, source_target_pairs={{0,3},{1,2},{2,1},{3,0},{4,7},{5,6},{6,5},{7,4},{8,11},{9,10},{10,... | collective-permute-start | bytes 393224 | tf_op jit(solution)/shard_map/ppermute | solution.py:444
  82.9 9.1 %collective-permute-start.16 = (bf16[32,2048]{1,0:T(8,128)(2,1)S(1)}, bf16[32,2048]{1,0:T(8,128)(2,1)S(1)}, u32[]{:S(2)}, u32[]{:S(2)}) collective-permute-start(bf16[32,2048]{1,0:T(8,128)(2,1)S(1)} %get-tuple-element.95.refs_0_), channel_id=1, source_target_pairs={{0,2},{1,3},{2,0},{3,1},{4,6},{5,7},{6,4},{7,5},{8,10},{9,11},{10,... | collective-permute-start | bytes 393224 | tf_op jit(solution)/shard_map/ppermute | solution.py:444
  82.9 9.1 %collective-permute-start.15 = (bf16[32,2048]{1,0:T(8,128)(2,1)S(1)}, bf16[32,2048]{1,0:T(8,128)(2,1)S(1)}, u32[]{:S(2)}, u32[]{:S(2)}) collective-permute-start(bf16[32,2048]{1,0:T(8,128)(2,1)S(1)} %get-tuple-element.95.refs_0_), channel_id=1, source_target_pairs={{0,1},{1,0},{2,3},{3,2},{4,5},{5,4},{6,7},{7,6},{8,9},{9,8},{10,11... | collective-permute-start | bytes 393224 | tf_op jit(solution)/shard_map/ppermute | solution.py:444
  92.7 7.1 %collective-permute-start.21 = (bf16[64,2048]{1,0:T(8,128)(2,1)S(1)}, bf16[64,2048]{1,0:T(8,128)(2,1)S(1)}, u32[]{:S(2)}, u32[]{:S(2)}) collective-permute-start(bf16[64,2048]{1,0:T(8,128)(2,1)S(1)} %slice.96), channel_id=1, source_target_pairs={{0,16},{4,20},{8,24},{12,28},{16,0},{20,4},{24,8},{28,12},{1,17},{... | collective-permute-start | bytes 786440 | tf_op jit(solution)/shard_map/ppermute | solution.py:438
  94.4 6.8 %collective-permute-start.22 = (bf16[64,2048]{1,0:T(8,128)(2,1)S(1)}, bf16[64,2048]{1,0:T(8,128)(2,1)S(1)}, u32[]{:S(2)}, u32[]{:S(2)}) collective-permute-start(bf16[64,2048]{1,0:T(8,128)(2,1)S(1)} %slice.97), channel_id=1, source_target_pairs={{0,8},{4,12},{8,0},{12,4},{16,24},{20,28},{24,16},{28,20},{1,9},{5... | collective-permute-start | bytes 786440 | tf_op jit(solution)/shard_map/ppermute | solution.py:438
  95.2 7.0 %collective-permute-start.19 = (bf16[128,2048]{1,0:T(8,128)(2,1)S(1)}, bf16[128,2048]{1,0:T(8,128)(2,1)S(1)}, u32[]{:S(2)}, u32[]{:S(2)}) collective-permute-start(bf16[128,2048]{1,0:T(8,128)(2,1)S(1)} %collective-permute-done.13.refs_2_), channel_id=1, source_target_pairs={{0,4},{4,0},{8,12},{12,8},{16,20},{20,16},{24,28},{28,24},{1,5},{5... | collective-permute-start | bytes 1572872 | tf_op jit(solution)/shard_map/ppermute | solution.py:438
  95.2 8.5 %collective-permute-start.20 = (bf16[128,2048]{1,0:T(8,128)(2,1)S(1)}, bf16[128,2048]{1,0:T(8,128)(2,1)S(1)}, u32[]{:S(2)}, u32[]{:S(2)}) collective-permute-start(bf16[128,2048]{1,0:T(8,128)(2,1)S(1)} %collective-permute-done.14.refs_4_), channel_id=1, source_target_pairs={{0,4},{4,0},{8,12},{12,8},{16,20},{20,16},{24,28},{28,24},{1,5},{5... | collective-permute-start | bytes 1572872 | tf_op jit(solution)/shard_map/ppermute | solution.py:438
  95.7 6.1 %collective-permute-start.18 = (bf16[128,2048]{1,0:T(8,128)(2,1)S(1)}, bf16[128,2048]{1,0:T(8,128)(2,1)S(1)}, u32[]{:S(2)}, u32[]{:S(2)}) collective-permute-start(bf16[128,2048]{1,0:T(8,128)(2,1)S(1)} %join_rows.2.refs_0_), channel_id=1, source_target_pairs={{0,4},{4,0},{8,12},{12,8},{16,20},{20,16},{24,28},{28,24},{1,5},{5... | collective-permute-start | bytes 1572872 | tf_op jit(solution)/shard_map/ppermute | solution.py:438
  101.2 2.4 %collective-permute-start.23 = (bf16[128,2048]{1,0:T(8,128)(2,1)S(1)}, bf16[128,2048]{1,0:T(8,128)(2,1)S(1)}, u32[]{:S(2)}, u32[]{:S(2)}) collective-permute-start(bf16[128,2048]{1,0:T(8,128)(2,1)S(1)} %constant_dynamic-update-slice_fusion.2.refs_6_), channel_id=1, source_target_pairs={{0,4},{4,0},{8,12},{12,8},{16,20},{20,16},{24,28},{28,24},{1,5},{5... | collective-permute-start | bytes 1572872 | tf_op jit(solution)/shard_map/ppermute | solution.py:438
  101.3 11.8 %collective-permute-start.27 = (bf16[4,576,128]{2,1,0:T(8,128)(2,1)S(1)}, bf16[4,576,128]{2,1,0:T(8,128)(2,1)S(1)}, u32[]{:S(2)}, u32[]{:S(2)}) collective-permute-start(bf16[4,576,128]{2,1,0:T(8,128)(2,1)S(1)} %constant_dynamic-update-slice_fusion.bwd_near), channel_id=1, source_target_pairs={{0,4},{4,0},{8,12},{12,8},{16,20},{20,16},{24,28},{28,24},{1,5},{5... | collective-permute-start | bytes 1769480 | tf_op jit(solution)/shard_map/ppermute | solution.py:438
  101.8 13.9 %collective-permute-start.26 = (bf16[128,2048]{1,0:T(8,128)(2,1)S(1)}, bf16[128,2048]{1,0:T(8,128)(2,1)S(1)}, u32[]{:S(2)}, u32[]{:S(2)}) collective-permute-start(bf16[128,2048]{1,0:T(8,128)(2,1)S(1)} %join_rows.3.refs_0_), channel_id=1, source_target_pairs={{0,16},{4,20},{8,24},{12,28},{16,0},{20,4},{24,8},{28,12},{1,17},{... | collective-permute-start | bytes 1572872 | tf_op jit(solution)/shard_map/ppermute | solution.py:438
  102.2 13.6 %collective-permute-start.25 = (bf16[128,2048]{1,0:T(8,128)(2,1)S(1)}, bf16[128,2048]{1,0:T(8,128)(2,1)S(1)}, u32[]{:S(2)}, u32[]{:S(2)}) collective-permute-start(bf16[128,2048]{1,0:T(8,128)(2,1)S(1)} %join_rows.3.refs_0_), channel_id=1, source_target_pairs={{0,8},{4,12},{8,0},{12,4},{16,24},{20,28},{24,16},{28,20},{1,9},{5... | collective-permute-start | bytes 1572872 | tf_op jit(solution)/shard_map/ppermute | solution.py:438
  103.7 12.1 %collective-permute-start.24 = (bf16[128,2048]{1,0:T(8,128)(2,1)S(1)}, bf16[128,2048]{1,0:T(8,128)(2,1)S(1)}, u32[]{:S(2)}, u32[]{:S(2)}) collective-permute-start(bf16[128,2048]{1,0:T(8,128)(2,1)S(1)} %join_rows.3.refs_0_), channel_id=1, source_target_pairs={{0,4},{4,0},{8,12},{12,8},{16,20},{20,16},{24,28},{28,24},{1,5},{5... | collective-permute-start | bytes 1572872 | tf_op jit(solution)/shard_map/ppermute | solution.py:438
  115.8 5.7 %collective-permute-start.28 = (bf16[4,128,2048]{2,1,0:T(8,128)(2,1)S(1)}, bf16[4,128,2048]{2,1,0:T(8,128)(2,1)S(1)}, u32[]{:S(2)}, u32[]{:S(2)}) collective-permute-start(bf16[4,128,2048]{2,1,0:T(8,128)(2,1)S(1)} %get-tuple-element.102), channel_id=1, source_target_pairs={{0,4},{4,0},{8,12},{12,8},{16,20},{20,16},{24,28},{28,24},{1,5},{5... | collective-permute-start | bytes 6291464 | tf_op jit(solution)/shard_map/ppermute | solution.py:438
  115.8 4.9 %collective-permute-start.30 = (bf16[128,2048]{1,0:T(8,128)(2,1)S(1)}, bf16[128,2048]{1,0:T(8,128)(2,1)S(1)}, u32[]{:S(2)}, u32[]{:S(2)}) collective-permute-start(bf16[128,2048]{1,0:T(8,128)(2,1)S(1)} %collective-permute-done.26.refs_2_), channel_id=1, source_target_pairs={{0,4},{4,0},{8,12},{12,8},{16,20},{20,16},{24,28},{28,24},{1,5},{5... | collective-permute-start | bytes 1572872 | tf_op jit(solution)/shard_map/ppermute | solution.py:438
  116.3 5.1 %collective-permute-start.29 = (bf16[128,2048]{1,0:T(8,128)(2,1)S(1)}, bf16[128,2048]{1,0:T(8,128)(2,1)S(1)}, u32[]{:S(2)}, u32[]{:S(2)}) collective-permute-start(bf16[128,2048]{1,0:T(8,128)(2,1)S(1)} %collective-permute-done.25.refs_1_), channel_id=1, source_target_pairs={{0,4},{4,0},{8,12},{12,8},{16,20},{20,16},{24,28},{28,24},{1,5},{5... | collective-permute-start | bytes 1572872 | tf_op jit(solution)/shard_map/ppermute | solution.py:438
  116.4 8.8 %collective-permute-start.36 = (bf16[64,2048]{1,0:T(8,128)(2,1)S(1)}, bf16[64,2048]{1,0:T(8,128)(2,1)S(1)}, u32[]{:S(2)}, u32[]{:S(2)}) collective-permute-start(bf16[64,2048]{1,0:T(8,128)(2,1)S(1)} %slice.131), channel_id=1, source_target_pairs={{0,8},{4,12},{8,0},{12,4},{16,24},{20,28},{24,16},{28,20},{1,9},{5... | collective-permute-start | bytes 786440 | tf_op jit(solution)/shard_map/ppermute | solution.py:438
  117.9 8.5 %collective-permute-start.35 = (bf16[64,2048]{1,0:T(8,128)(2,1)S(1)}, bf16[64,2048]{1,0:T(8,128)(2,1)S(1)}, u32[]{:S(2)}, u32[]{:S(2)}) collective-permute-start(bf16[64,2048]{1,0:T(8,128)(2,1)S(1)} %slice.130), channel_id=1, source_target_pairs={{0,16},{4,20},{8,24},{12,28},{16,0},{20,4},{24,8},{28,12},{1,17},{... | collective-permute-start | bytes 786440 | tf_op jit(solution)/shard_map/ppermute | solution.py:438
  126.5 2.3 %collective-permute-start.37 = (bf16[128,2048]{1,0:T(8,128)(2,1)S(1)}, bf16[128,2048]{1,0:T(8,128)(2,1)S(1)}, u32[]{:S(2)}, u32[]{:S(2)}) collective-permute-start(bf16[128,2048]{1,0:T(8,128)(2,1)S(1)} %constant_dynamic-update-slice_fusion.4.refs_3_), channel_id=1, source_target_pairs={{0,4},{4,0},{8,12},{12,8},{16,20},{20,16},{24,28},{28,24},{1,5},{5... | collective-permute-start | bytes 1572872 | tf_op jit(solution)/shard_map/ppermute | solution.py:438
  126.6 14.3 %collective-permute-start.31 = (bf16[128,2048]{1,0:T(8,128)(2,1)S(1)}, bf16[128,2048]{1,0:T(8,128)(2,1)S(1)}, u32[]{:S(2)}, u32[]{:S(2)}) collective-permute-start(bf16[128,2048]{1,0:T(8,128)(2,1)S(1)} %pad_maximum_fusion.1), channel_id=1, source_target_pairs={{0,8},{4,12},{8,0},{12,4},{16,24},{20,28},{24,16},{28,20},{1,9},{5... | collective-permute-start | bytes 1572872 | tf_op jit(solution)/shard_map/ppermute | solution.py:438
  127.2 14.0 %collective-permute-start.32 = (bf16[128,2048]{1,0:T(8,128)(2,1)S(1)}, bf16[128,2048]{1,0:T(8,128)(2,1)S(1)}, u32[]{:S(2)}, u32[]{:S(2)}) collective-permute-start(bf16[128,2048]{1,0:T(8,128)(2,1)S(1)} %pad_maximum_fusion.2), channel_id=1, source_target_pairs={{0,16},{4,20},{8,24},{12,28},{16,0},{20,4},{24,8},{28,12},{1,17},{... | collective-permute-start | bytes 1572872 | tf_op jit(solution)/shard_map/ppermute | solution.py:438
  133.7 10.2 %copy-start.7 = (bf16[1,512,2048]{2,1,0:T(8,128)(2,1)S(1)}, bf16[1,512,2048]{2,1,0:T(8,128)(2,1)}, u32[]{:S(2)}) copy-start(bf16[1,512,2048]{2,1,0:T(8,128)(2,1)} %down_ref.5) | copy-start | bytes 6291460
  141.2 10.2 %collective-permute-start.38 = (bf16[4,128,2048]{2,1,0:T(8,128)(2,1)S(1)}, bf16[4,128,2048]{2,1,0:T(8,128)(2,1)S(1)}, u32[]{:S(2)}, u32[]{:S(2)}) collective-permute-start(bf16[4,128,2048]{2,1,0:T(8,128)(2,1)S(1)} %expert_pieces.4), channel_id=1, source_target_pairs={{0,4},{4,0},{8,12},{12,8},{16,20},{20,16},{24,28},{28,24},{1,5},{5... | collective-permute-start | bytes 6291464 | tf_op jit(solution)/shard_map/ppermute | solution.py:438
  141.4 8.8 %collective-permute-start.34 = (bf16[64,2048]{1,0:T(8,128)(2,1)S(1)}, bf16[64,2048]{1,0:T(8,128)(2,1)S(1)}, u32[]{:S(2)}, u32[]{:S(2)}) collective-permute-start(bf16[64,2048]{1,0:T(8,128)(2,1)S(1)} %get-tuple-element.144), channel_id=1, source_target_pairs={{0,8},{4,12},{8,0},{12,4},{16,24},{20,28},{24,16},{28,20},{1,9},{5... | collective-permute-start | bytes 786440 | tf_op jit(solution)/shard_map/ppermute | solution.py:438
  143.0 8.4 %collective-permute-start.33 = (bf16[64,2048]{1,0:T(8,128)(2,1)S(1)}, bf16[64,2048]{1,0:T(8,128)(2,1)S(1)}, u32[]{:S(2)}, u32[]{:S(2)}) collective-permute-start(bf16[64,2048]{1,0:T(8,128)(2,1)S(1)} %get-tuple-element.145), channel_id=1, source_target_pairs={{0,16},{4,20},{8,24},{12,28},{16,0},{20,4},{24,8},{28,12},{1,17},{... | collective-permute-start | bytes 786440 | tf_op jit(solution)/shard_map/ppermute | solution.py:438
  151.9 13.3 %collective-permute-start.42 = (bf16[128,2048]{1,0:T(8,128)(2,1)S(1)}, bf16[128,2048]{1,0:T(8,128)(2,1)S(1)}, u32[]{:S(2)}, u32[]{:S(2)}) collective-permute-start(bf16[128,2048]{1,0:T(8,128)(2,1)S(1)} %pad_maximum_fusion.3), channel_id=1, source_target_pairs={{0,8},{4,12},{8,0},{12,4},{16,24},{20,28},{24,16},{28,20},{1,9},{5... | collective-permute-start | bytes 1572872 | tf_op jit(solution)/shard_map/ppermute | solution.py:438
  152.5 13.1 %collective-permute-start.43 = (bf16[128,2048]{1,0:T(8,128)(2,1)S(1)}, bf16[128,2048]{1,0:T(8,128)(2,1)S(1)}, u32[]{:S(2)}, u32[]{:S(2)}) collective-permute-start(bf16[128,2048]{1,0:T(8,128)(2,1)S(1)} %pad_maximum_fusion.4), channel_id=1, source_target_pairs={{0,16},{4,20},{8,24},{12,28},{16,0},{20,4},{24,8},{28,12},{1,17},{... | collective-permute-start | bytes 1572872 | tf_op jit(solution)/shard_map/ppermute | solution.py:438
  165.8 6.8 %collective-permute-start.45 = (bf16[64,2048]{1,0:T(8,128)(2,1)S(1)}, bf16[64,2048]{1,0:T(8,128)(2,1)S(1)}, u32[]{:S(2)}, u32[]{:S(2)}) collective-permute-start(bf16[64,2048]{1,0:T(8,128)(2,1)S(1)} %get-tuple-element.138), channel_id=1, source_target_pairs={{0,8},{4,12},{8,0},{12,4},{16,24},{20,28},{24,16},{28,20},{1,9},{5... | collective-permute-start | bytes 786440 | tf_op jit(solution)/shard_map/ppermute | solution.py:438
  167.3 6.4 %collective-permute-start.44 = (bf16[64,2048]{1,0:T(8,128)(2,1)S(1)}, bf16[64,2048]{1,0:T(8,128)(2,1)S(1)}, u32[]{:S(2)}, u32[]{:S(2)}) collective-permute-start(bf16[64,2048]{1,0:T(8,128)(2,1)S(1)} %get-tuple-element.139), channel_id=1, source_target_pairs={{0,16},{4,20},{8,24},{12,28},{16,0},{20,4},{24,8},{28,12},{1,17},{... | collective-permute-start | bytes 786440 | tf_op jit(solution)/shard_map/ppermute | solution.py:438
  168.2 9.4 %collective-permute-start.39 = (bf16[128,512]{1,0:T(8,128)(2,1)S(1)}, bf16[128,512]{1,0:T(8,128)(2,1)S(1)}, u32[]{:S(2)}, u32[]{:S(2)}) collective-permute-start(bf16[128,512]{1,0:T(8,128)(2,1)S(1)} %get-tuple-element.125), channel_id=1, source_target_pairs={{0,1},{1,0},{2,3},{3,2},{4,5},{5,4},{6,7},{7,6},{8,9},{9,8},{10,11... | collective-permute-start | bytes 393224 | tf_op jit(solution)/shard_map/ppermute | solution.py:444
  168.3 15.6 %collective-permute-start.40 = (bf16[128,512]{1,0:T(8,128)(2,1)S(1)}, bf16[128,512]{1,0:T(8,128)(2,1)S(1)}, u32[]{:S(2)}, u32[]{:S(2)}) collective-permute-start(bf16[128,512]{1,0:T(8,128)(2,1)S(1)} %get-tuple-element.126), channel_id=1, source_target_pairs={{0,2},{1,3},{2,0},{3,1},{4,6},{5,7},{6,4},{7,5},{8,10},{9,11},{10,... | collective-permute-start | bytes 393224 | tf_op jit(solution)/shard_map/ppermute | solution.py:444
  171.1 12.8 %collective-permute-start.41 = (bf16[128,512]{1,0:T(8,128)(2,1)S(1)}, bf16[128,512]{1,0:T(8,128)(2,1)S(1)}, u32[]{:S(2)}, u32[]{:S(2)}) collective-permute-start(bf16[128,512]{1,0:T(8,128)(2,1)S(1)} %get-tuple-element.127), channel_id=1, source_target_pairs={{0,3},{1,2},{2,1},{3,0},{4,7},{5,6},{6,5},{7,4},{8,11},{9,10},{10,... | collective-permute-start | bytes 393224 | tf_op jit(solution)/shard_map/ppermute | solution.py:444
  173.7 5.4 %copy-start.9 = (bf16[256,512]{1,0:T(8,128)(2,1)S(1)}, bf16[256,512]{1,0:T(8,128)(2,1)}, u32[]{:S(2)}) copy-start(bf16[256,512]{1,0:T(8,128)(2,1)} %cot_ref.3) | copy-start | bytes 786436
  174.7 9.2 %collective-permute-start.46 = (bf16[128,512]{1,0:T(8,128)(2,1)S(1)}, bf16[128,512]{1,0:T(8,128)(2,1)S(1)}, u32[]{:S(2)}, u32[]{:S(2)}) collective-permute-start(bf16[128,512]{1,0:T(8,128)(2,1)S(1)} %get-tuple-element.132), channel_id=1, source_target_pairs={{0,1},{1,0},{2,3},{3,2},{4,5},{5,4},{6,7},{7,6},{8,9},{9,8},{10,11... | collective-permute-start | bytes 393224 | tf_op jit(solution)/shard_map/ppermute | solution.py:444
  174.8 15.7 %collective-permute-start.47 = (bf16[128,512]{1,0:T(8,128)(2,1)S(1)}, bf16[128,512]{1,0:T(8,128)(2,1)S(1)}, u32[]{:S(2)}, u32[]{:S(2)}) collective-permute-start(bf16[128,512]{1,0:T(8,128)(2,1)S(1)} %get-tuple-element.133), channel_id=1, source_target_pairs={{0,2},{1,3},{2,0},{3,1},{4,6},{5,7},{6,4},{7,5},{8,10},{9,11},{10,... | collective-permute-start | bytes 393224 | tf_op jit(solution)/shard_map/ppermute | solution.py:444
  177.6 12.9 %collective-permute-start.48 = (bf16[128,512]{1,0:T(8,128)(2,1)S(1)}, bf16[128,512]{1,0:T(8,128)(2,1)S(1)}, u32[]{:S(2)}, u32[]{:S(2)}) collective-permute-start(bf16[128,512]{1,0:T(8,128)(2,1)S(1)} %get-tuple-element.134), channel_id=1, source_target_pairs={{0,3},{1,2},{2,1},{3,0},{4,7},{5,6},{6,5},{7,4},{8,11},{9,10},{10,... | collective-permute-start | bytes 393224 | tf_op jit(solution)/shard_map/ppermute | solution.py:444
  (4 other events, 4.3 us)

commit v14 on v13

--- a/solution.py
+++ b/solution.py
@@ -653,17 +653,15 @@
         experts_of = functools.partial(
             expert_pieces, chunk * chunk_rows, where, gate=w_gate, up=w_up, down=w_down, routes=fwd
         )
+        here, far = experts_of(rows=here_rows, groups=[evens, odds])
+        beside = (rows[chunk + 1], bwd) if chunk + 1 < CHUNKS else pending[-1][3]
+        arrived = swap(after(far, beside), CORE)
         if chunk + 1 < CHUNKS:
-            here, far = experts_of(rows=here_rows, groups=[evens, odds])
-            arrived = swap(after(far, (rows[chunk + 1], bwd)), CORE)
             pending.append((here,))
         else:
-            (far,) = experts_of(rows=here_rows, groups=[odds])
-            arrived = swap(after(far, pending[-1][3]), CORE)
             last = last_sums(*pending[-1][:2], pending[-1][3])
             received = send_sums(last)
             pending[-1] += (terms_of(first, pending[-1][3]) + terms_of(last, received),)
-            (here,) = experts_of(rows=after(here_rows, [far] + arrays(last)), groups=[evens])
             arrived = after(arrived, received)
             first = first_sums(here, arrived)
             pending.append((here, arrived, first, send_sums(first)))
@@ -675,7 +673,7 @@
             held = after([rows for rows, _ in terms], arrays(pending[chunk + 1][2]))
             terms = list(zip(held, [places for _, places in terms]))
         else:
-            last = last_sums(here, arrived, after(received, sums[-1][0]))
+            last = last_sums(here, arrived, after(received, sums[-1][:-1]))
             terms = terms_of(first, received) + terms_of(last, send_sums(last))
         sums.append(send_heads(sum_terms(where, attn[chunk], here, arrived, terms, n_head)))
     grads = core_grads(where, qkv, grad_core, steps, fwd, bwd)

time: 192 us -> 187 us (0.974)
  waiting for transfers between devices: 82.2 us -> 77.1 us
    ppermute x33, waiting for transfers between devices: 44.1 us -> 39.1 us  [swap(): lax.ppermute(value, 'ctx', [(at, at ^ mask) for at in range(lax.axis_size...]
    pallas_call x3 -> x2, Pallas kernels: 19.1 us -> 18.3 us  [expert_pieces(): pl.pallas_call(functools.partial(expert_kernel, tuple(masks), chunk, expe...]
  transfers between devices with their start and end apart: 49 -> 49, of which waited for: 26 -> 29; matrix products, arithmetic and copies ran while one was open for 1% -> 1% of each run, Pallas kernels for 15% -> 15%
where the time goes in v14:
time: 187 us
  waiting for transfers between devices  77.1 us (41%)
  starting transfers between devices  58.5 us (31%)
  Pallas kernels  43.9 us (23%)
  local copies, waits for them, and re-layouts  4.58 us (2%)
    ppermute x33, waiting for transfers between devices, swap(): lax.ppermute(value, 'ctx', [(at, at ^ mask) for at in range(lax.axis_size...  39.1 us
    ppermute x15, waiting for transfers between devices, send_heads(): lax.ppermute(parts[mask], 'head', [(at, at ^ mask) for at in range(count)])  37 us
    ppermute x33, starting transfers between devices, swap(): lax.ppermute(value, 'ctx', [(at, at ^ mask) for at in range(lax.axis_size...  29.7 us
    ppermute x15, starting transfers between devices, send_heads(): lax.ppermute(parts[mask], 'head', [(at, at ^ mask) for at in range(count)])  26.2 us
    pallas_call x2, Pallas kernels, expert_pieces(): pl.pallas_call(functools.partial(expert_kernel, tuple(masks), chunk, expe...  18.3 us
    pallas_call x1, Pallas kernels, project(): pl.pallas_call(qkv_kernel, in_specs=[hbm, vmem, hbm], out_specs=[vmem, vm...  7.28 us
    pallas_call x1, Pallas kernels, core_grads(): pl.pallas_call(grad_kernel, in_specs=[pl.BlockSpec(memory_space=pltpu.SME...  4.7 us
    unnamed x41, local copies, waits for them, and re-layouts  4.43 us
  transfers between devices with their start and end apart: 49, of which 29 were waited for; matrix products, arithmetic and copies ran while one was open for 1% of the time, Pallas kernels for 15%

profile of v14, /device:TPU:0, one launch (start us, length us, event | category | flops | bytes accessed | tf_op | source)
XLA Modules:
  0.0 186.8 jit_solution(4465722503542135606)
XLA Ops:
  0.7 7.3 %qkv_projection.1 = (bf16[3,256,512]{2,1,0:T(8,128)(2,1)}, bf16[3,16,512]{2,1,0:T(8,128)(2,1)}) custom-call(bf16[256,2048]{1,0:T(8,128)(2,1)} %x_ref.3, f32[1,2048]{1,0:T(1,128)} %bitcast.63, bf16[3,2048,512]{2,1,0:T(8,128)(2,1)} %bitcast.59), custom_call_target="tpu_custom_call" | custom-call | tf_op jit(solution)/shard_map/qkv_projection/pallas_call | solution.py:68
  8.0 2.5 %collective-permute-start = (bf16[3,16,512]{2,1,0:T(8,128)(2,1)}, bf16[3,16,512]{2,1,0:T(8,128)(2,1)S(1)}, u32[]{:S(2)}, u32[]{:S(2)}) collective-permute-start(bf16[3,16,512]{2,1,0:T(8,128)(2,1)} %get-tuple-element.70), channel_id=1, source_target_pairs={{0,4},{4,8},{8,12},{12,16},{16,20},{20,24},{24,28},{1,5},{5,9},{9,... | collective-permute-start | bytes 147464 | tf_op jit(solution)/shard_map/ppermute | solution.py:610
  10.5 1.1 collective-permute-done.rim_ref
  11.6 1.1 copy-done.10
  12.7 2.1 %conv_states.1 = (bf16[3,256,512]{2,1,0:T(8,128)(2,1)S(1)}, bf16[672,128]{1,0:T(8,128)(2,1)S(1)}, bf16[576,128]{1,0:T(8,128)(2,1)S(1)}) custom-call(bf16[3,256,512]{2,1,0:T(8,128)(2,1)S(1)} %copy-done.10, bf16[3,16,512]{2,1,0:T(8,128)(2,1)S(1)} %collective-permute-done.rim_ref, f32[3,4,512]{2,1,0:T(4,128)S(1)} %bitcast.54, f32[4,256]{1,0:T(4,128)S(1)} %bitcast.51, ...), custom_call_target="tpu_custom_call" | custom-call | tf_op jit(solution)/shard_map/conv_states/pallas_call | solution.py:161
  14.9 0.9 copy-done.2
  16.5 6.1 %collective-permute-start.3 = (bf16[672,128]{1,0:T(8,128)(2,1)S(1)}, bf16[672,128]{1,0:T(8,128)(2,1)S(1)}, u32[]{:S(2)}, u32[]{:S(2)}) collective-permute-start(bf16[672,128]{1,0:T(8,128)(2,1)S(1)} %get-tuple-element.73), channel_id=1, source_target_pairs={{0,24},{4,28},{8,16},{12,20},{16,8},{20,12},{24,0},{28,4},{1,25},{... | collective-permute-start | bytes 516104 | tf_op jit(solution)/shard_map/ppermute | solution.py:438
  23.1 0.9 collective-permute-start.1
  24.0 3.8 %collective-permute-done.3 = bf16[672,128]{1,0:T(8,128)(2,1)S(1)} collective-permute-done((bf16[672,128]{1,0:T(8,128)(2,1)S(1)}, bf16[672,128]{1,0:T(8,128)(2,1)S(1)}, u32[]{:S(2)}, u32[]{:S(2)}) %collective-permute-start.3) | collective-permute-done | bytes 172064 | tf_op jit(solution)/shard_map/ppermute | solution.py:438
  27.8 2.5 %collective-permute-done.2 = bf16[672,128]{1,0:T(8,128)(2,1)S(1)} collective-permute-done((bf16[672,128]{1,0:T(8,128)(2,1)S(1)}, bf16[672,128]{1,0:T(8,128)(2,1)S(1)}, u32[]{:S(2)}, u32[]{:S(2)}) %collective-permute-start.2) | collective-permute-done | bytes 172064 | tf_op jit(solution)/shard_map/ppermute | solution.py:438
  30.7 1.1 stage_weights.2.me_ref.where_ref
  31.8 0.9 collective-permute-done.4.far_ref.far_routes.fwd_far
  32.7 3.8 %core_out.1 = (bf16[64,2048]{1,0:T(8,128)(2,1)S(1)}, bf16[64,2048]{1,0:T(8,128)(2,1)S(1)}, bf16[64,2048]{1,0:T(8,128)(2,1)S(1)}, bf16[64,2048]{1,0:T(8,128)(2,1)S(1)}) custom-call(s32[3]{0:T(128)S(1)} %stage_weights.2.me_ref.where_ref, bf16[3,256,512]{2,1,0:T(8,128)(2,1)S(1)} %copy-done.3, f32[4,256]{1,0:T(4,128)S(1)} %bitcast.52, f32[1,512]{1,0:T(1,128)S(1)} %bitcast.58, ...), custom_call_target="tpu_custom_call" | custom-call | tf_op jit(solution)/shard_map/core_out/pallas_call | solution.py:223
  36.6 1.7 collective-permute-start.8
  38.3 1.6 collective-permute-start.5
  39.8 2.6 %collective-permute-start.6 = (bf16[64,2048]{1,0:T(8,128)(2,1)S(1)}, bf16[64,2048]{1,0:T(8,128)(2,1)S(1)}, u32[]{:S(2)}, u32[]{:S(2)}) collective-permute-start(bf16[64,2048]{1,0:T(8,128)(2,1)S(1)} %get-tuple-element.76), channel_id=1, source_target_pairs={{0,2},{1,3},{2,0},{3,1},{4,6},{5,7},{6,4},{7,5},{8,10},{9,11},{10,... | collective-permute-start | bytes 786440 | tf_op jit(solution)/shard_map/ppermute | solution.py:444
  42.7 1.6 copy-done.6
  44.2 1.1 stage_weights.3.where_ref.me_ref
  45.4 5.9 %collective-permute-done.5.refs_1_ = bf16[64,2048]{1,0:T(8,128)(2,1)S(1)} collective-permute-done((bf16[64,2048]{1,0:T(8,128)(2,1)S(1)}, bf16[64,2048]{1,0:T(8,128)(2,1)S(1)}, u32[]{:S(2)}, u32[]{:S(2)}) %collective-permute-start.5) | collective-permute-done | bytes 262176 | tf_op jit(solution)/shard_map/ppermute | solution.py:444
  51.3 9.9 %collective-permute-done.6.refs_2_ = bf16[64,2048]{1,0:T(8,128)(2,1)S(1)} collective-permute-done((bf16[64,2048]{1,0:T(8,128)(2,1)S(1)}, bf16[64,2048]{1,0:T(8,128)(2,1)S(1)}, u32[]{:S(2)}, u32[]{:S(2)}) %collective-permute-start.6) | collective-permute-done | bytes 262176 | tf_op jit(solution)/shard_map/ppermute | solution.py:444
  62.1 1.0 collective-permute-start.12
  63.0 2.5 %collective-permute-start.11 = (bf16[32,2048]{1,0:T(8,128)(2,1)S(1)}, bf16[32,2048]{1,0:T(8,128)(2,1)S(1)}, u32[]{:S(2)}, u32[]{:S(2)}) collective-permute-start(bf16[32,2048]{1,0:T(8,128)(2,1)S(1)} %get-tuple-element.89.refs_0_), channel_id=1, source_target_pairs={{0,3},{1,2},{2,1},{3,0},{4,7},{5,6},{6,5},{7,4},{8,11},{9,10},{10,... | collective-permute-start | bytes 393224 | tf_op jit(solution)/shard_map/ppermute | solution.py:444
  65.5 5.2 %collective-permute-start.10 = (bf16[32,2048]{1,0:T(8,128)(2,1)S(1)}, bf16[32,2048]{1,0:T(8,128)(2,1)S(1)}, u32[]{:S(2)}, u32[]{:S(2)}) collective-permute-start(bf16[32,2048]{1,0:T(8,128)(2,1)S(1)} %get-tuple-element.89.refs_0_), channel_id=1, source_target_pairs={{0,2},{1,3},{2,0},{3,1},{4,6},{5,7},{6,4},{7,5},{8,10},{9,11},{10,... | collective-permute-start | bytes 393224 | tf_op jit(solution)/shard_map/ppermute | solution.py:444
  71.0 7.2 %collective-permute-done.10.refs_2_ = bf16[32,2048]{1,0:T(8,128)(2,1)S(1)} collective-permute-done((bf16[32,2048]{1,0:T(8,128)(2,1)S(1)}, bf16[32,2048]{1,0:T(8,128)(2,1)S(1)}, u32[]{:S(2)}, u32[]{:S(2)}) %collective-permute-start.10) | collective-permute-done | bytes 131104 | tf_op jit(solution)/shard_map/ppermute | solution.py:444
  78.8 1.2 collective-permute-start.14
  80.4 2.6 %collective-permute-start.17 = (bf16[32,2048]{1,0:T(8,128)(2,1)S(1)}, bf16[32,2048]{1,0:T(8,128)(2,1)S(1)}, u32[]{:S(2)}, u32[]{:S(2)}) collective-permute-start(bf16[32,2048]{1,0:T(8,128)(2,1)S(1)} %get-tuple-element.93.refs_0_), channel_id=1, source_target_pairs={{0,3},{1,2},{2,1},{3,0},{4,7},{5,6},{6,5},{7,4},{8,11},{9,10},{10,... | collective-permute-start | bytes 393224 | tf_op jit(solution)/shard_map/ppermute | solution.py:444
  83.1 1.7 collective-permute-start.15
  84.8 3.7 %collective-permute-done.17.refs_3_ = bf16[32,2048]{1,0:T(8,128)(2,1)S(1)} collective-permute-done((bf16[32,2048]{1,0:T(8,128)(2,1)S(1)}, bf16[32,2048]{1,0:T(8,128)(2,1)S(1)}, u32[]{:S(2)}, u32[]{:S(2)}) %collective-permute-start.17) | collective-permute-done | bytes 131104 | tf_op jit(solution)/shard_map/ppermute | solution.py:444
  88.5 3.7 %collective-permute-done.16.refs_2_ = bf16[32,2048]{1,0:T(8,128)(2,1)S(1)} collective-permute-done((bf16[32,2048]{1,0:T(8,128)(2,1)S(1)}, bf16[32,2048]{1,0:T(8,128)(2,1)S(1)}, u32[]{:S(2)}, u32[]{:S(2)}) %collective-permute-start.16) | collective-permute-done | bytes 131104 | tf_op jit(solution)/shard_map/ppermute | solution.py:444
  92.8 1.7 collective-permute-start.21
  95.9 4.0 %collective-permute-done.21 = bf16[64,2048]{1,0:T(8,128)(2,1)S(1)} collective-permute-done((bf16[64,2048]{1,0:T(8,128)(2,1)S(1)}, bf16[64,2048]{1,0:T(8,128)(2,1)S(1)}, u32[]{:S(2)}, u32[]{:S(2)}) %collective-permute-start.21) | collective-permute-done | bytes 262176 | tf_op jit(solution)/shard_map/ppermute | solution.py:438
  99.9 1.5 collective-permute-done.22
  102.4 1.5 collective-permute-start.25
  103.9 9.1 %expert_pieces.2 = (bf16[4,128,2048]{2,1,0:T(8,128)(2,1)S(1)}, bf16[4,128,2048]{2,1,0:T(8,128)(2,1)S(1)}) custom-call(s32[3]{0:T(128)S(1)} %stage_weights.3.where_ref.me_ref, bf16[4,672,128]{2,1,0:T(8,128)(2,1)S(1)} %pad_maximum_fusion.near_ref.near_routes.fwd_near, bf16[4,672,128]{2,1,0:T(8,128)(2,1)S(1)} %collective-permute-done.4.far_ref.far_routes.fwd_far, ...), custom_call_target="tpu_custom_call" | custom-call | flops 6442450944 | bytes 8388608 | tf_op jit(solution)/shard_map/expert_pieces/pallas_call | solution.py:411
  113.0 2.9 %collective-permute-done.26.refs_4_ = bf16[128,2048]{1,0:T(8,128)(2,1)S(1)} collective-permute-done((bf16[128,2048]{1,0:T(8,128)(2,1)S(1)}, bf16[128,2048]{1,0:T(8,128)(2,1)S(1)}, u32[]{:S(2)}, u32[]{:S(2)}) %collective-permute-start.26) | collective-permute-done | bytes 524320 | tf_op jit(solution)/shard_map/ppermute | solution.py:438
  116.6 1.5 collective-permute-start.36
  118.1 0.9 collective-permute-start.35
  119.1 1.9 collective-permute-done.30.refs_5_
  122.1 3.2 %collective-permute-done.36 = bf16[64,2048]{1,0:T(8,128)(2,1)S(1)} collective-permute-done((bf16[64,2048]{1,0:T(8,128)(2,1)S(1)}, bf16[64,2048]{1,0:T(8,128)(2,1)S(1)}, u32[]{:S(2)}, u32[]{:S(2)}) %collective-permute-start.36) | collective-permute-done | bytes 262176 | tf_op jit(solution)/shard_map/ppermute | solution.py:438
  125.3 1.3 collective-permute-done.35
  127.3 1.7 collective-permute-start.32
  129.0 9.1 %expert_pieces.3 = (bf16[4,128,2048]{2,1,0:T(8,128)(2,1)S(1)}, bf16[4,128,2048]{2,1,0:T(8,128)(2,1)S(1)}) custom-call(s32[3]{0:T(128)S(1)} %stage_weights.3.where_ref.me_ref, bf16[4,672,128]{2,1,0:T(8,128)(2,1)S(1)} %pad_maximum_fusion.near_ref.near_routes.fwd_near, bf16[4,672,128]{2,1,0:T(8,128)(2,1)S(1)} %collective-permute-done.4.far_ref.far_routes.fwd_far, ...), custom_call_target="tpu_custom_call" | custom-call | flops 6442450944 | bytes 8388608 | tf_op jit(solution)/shard_map/expert_pieces/pallas_call | solution.py:411
  138.1 2.9 %collective-permute-done.31.refs_0_ = bf16[128,2048]{1,0:T(8,128)(2,1)S(1)} collective-permute-done((bf16[128,2048]{1,0:T(8,128)(2,1)S(1)}, bf16[128,2048]{1,0:T(8,128)(2,1)S(1)}, u32[]{:S(2)}, u32[]{:S(2)}) %collective-permute-start.31) | collective-permute-done | bytes 524320 | tf_op jit(solution)/shard_map/ppermute | solution.py:438
  141.6 1.6 collective-permute-start.34
  143.1 0.9 collective-permute-start.33
  144.0 6.4 %collective-permute-done.34.refs_3_ = bf16[64,2048]{1,0:T(8,128)(2,1)S(1)} collective-permute-done((bf16[64,2048]{1,0:T(8,128)(2,1)S(1)}, bf16[64,2048]{1,0:T(8,128)(2,1)S(1)}, u32[]{:S(2)}, u32[]{:S(2)}) %collective-permute-start.34) | collective-permute-done | bytes 262176 | tf_op jit(solution)/shard_map/ppermute | solution.py:438
  150.4 1.2 collective-permute-done.33.refs_2_
  152.7 1.7 collective-permute-start.43
  154.4 1.0 sum_terms.2
  155.5 2.8 %collective-permute-start.40 = (bf16[128,512]{1,0:T(8,128)(2,1)S(1)}, bf16[128,512]{1,0:T(8,128)(2,1)S(1)}, u32[]{:S(2)}, u32[]{:S(2)}) collective-permute-start(bf16[128,512]{1,0:T(8,128)(2,1)S(1)} %get-tuple-element.122), channel_id=1, source_target_pairs={{0,2},{1,3},{2,0},{3,1},{4,6},{5,7},{6,4},{7,5},{8,10},{9,11},{10,... | collective-permute-start | bytes 393224 | tf_op jit(solution)/shard_map/ppermute | solution.py:444
  158.3 3.9 %collective-permute-done.39.refs_1_ = bf16[128,512]{1,0:T(8,128)(2,1)S(1)} collective-permute-done((bf16[128,512]{1,0:T(8,128)(2,1)S(1)}, bf16[128,512]{1,0:T(8,128)(2,1)S(1)}, u32[]{:S(2)}, u32[]{:S(2)}) %collective-permute-start.39) | collective-permute-done | bytes 131104 | tf_op jit(solution)/shard_map/ppermute | solution.py:444
  162.2 1.4 collective-permute-done.40.refs_2_
  163.6 1.8 collective-permute-done.42.refs_0_
  166.0 1.5 collective-permute-start.45
  167.5 0.9 collective-permute-start.44
  168.4 2.3 %collective-permute-start.41 = (bf16[128,512]{1,0:T(8,128)(2,1)S(1)}, bf16[128,512]{1,0:T(8,128)(2,1)S(1)}, u32[]{:S(2)}, u32[]{:S(2)}) collective-permute-start(bf16[128,512]{1,0:T(8,128)(2,1)S(1)} %get-tuple-element.123), channel_id=1, source_target_pairs={{0,3},{1,2},{2,1},{3,0},{4,7},{5,6},{6,5},{7,4},{8,11},{9,10},{10,... | collective-permute-start | bytes 393224 | tf_op jit(solution)/shard_map/ppermute | solution.py:444
  170.7 1.9 %collective-permute-done.45.refs_3_ = bf16[64,2048]{1,0:T(8,128)(2,1)S(1)} collective-permute-done((bf16[64,2048]{1,0:T(8,128)(2,1)S(1)}, bf16[64,2048]{1,0:T(8,128)(2,1)S(1)}, u32[]{:S(2)}, u32[]{:S(2)}) %collective-permute-start.45) | collective-permute-done | bytes 262176 | tf_op jit(solution)/shard_map/ppermute | solution.py:438
  172.6 1.3 collective-permute-done.44.refs_2_
  173.9 1.0 sum_terms.3
  174.9 2.8 %collective-permute-start.47 = (bf16[128,512]{1,0:T(8,128)(2,1)S(1)}, bf16[128,512]{1,0:T(8,128)(2,1)S(1)}, u32[]{:S(2)}, u32[]{:S(2)}) collective-permute-start(bf16[128,512]{1,0:T(8,128)(2,1)S(1)} %get-tuple-element.129), channel_id=1, source_target_pairs={{0,2},{1,3},{2,0},{3,1},{4,6},{5,7},{6,4},{7,5},{8,10},{9,11},{10,... | collective-permute-start | bytes 393224 | tf_op jit(solution)/shard_map/ppermute | solution.py:444
  177.8 1.6 collective-permute-start.48
  179.3 4.7 %core_grads.1 = (bf16[256,512]{1,0:T(8,128)(2,1)}, bf16[256,512]{1,0:T(8,128)(2,1)}, bf16[256,512]{1,0:T(8,128)(2,1)}) custom-call(s32[3]{0:T(128)S(1)} %stage_weights.3.where_ref.me_ref, bf16[3,256,512]{2,1,0:T(8,128)(2,1)S(1)} %copy-done.3, bf16[256,512]{1,0:T(8,128)(2,1)S(1)} %copy-done.9, f32[4,256]{1,0:T(4,128)S(1)} %bitcast.53, ...), custom_call_target="tpu_custom_call" | custom-call | tf_op jit(solution)/shard_map/core_grads/pallas_call | solution.py:268
  184.0 1.4 collective-permute-done.47.refs_6_
  185.4 1.4 layer_out.1
  (107 shorter events, 11.7 us)
Async XLA Ops:
  0.6 10.9 %copy-start.8 = (bf16[256,512]{1,0:T(8,128)(2,1)S(1)}, bf16[256,512]{1,0:T(8,128)(2,1)}, u32[]{:S(2)}) copy-start(bf16[256,512]{1,0:T(8,128)(2,1)} %cot_ref.3) | copy-start | bytes 786436
  0.6 10.9 %copy-start.13 = (f32[256,4]{0,1:T(4,128)S(1)}, f32[256,4]{0,1:T(4,128)}, u32[]{:S(2)}) copy-start(f32[256,4]{0,1:T(4,128)} %param.18) | copy-start | bytes 12292
  0.7 10.9 %copy-start.14 = (f32[4,3,512]{2,0,1:T(4,128)S(1)}, f32[4,3,512]{2,0,1:T(4,128)}, u32[]{:S(2)}) copy-start(f32[4,3,512]{2,0,1:T(4,128)} %param.17) | copy-start | bytes 73732
  0.7 10.9 %copy-start.15 = (s32[256,8]{0,1:T(8,128)S(1)}, s32[256,8]{0,1:T(8,128)}, u32[]{:S(2)}) copy-start(s32[256,8]{0,1:T(8,128)} %param.22) | copy-start | bytes 24580
  0.7 10.9 %copy-start.16 = (f32[256,8]{0,1:T(8,128)S(1)}, f32[256,8]{0,1:T(8,128)}, u32[]{:S(2)}) copy-start(f32[256,8]{0,1:T(8,128)} %param.23) | copy-start | bytes 24580
  8.0 22.7 %copy-start.1 = (bf16[512,2048]{1,0:T(8,128)(2,1)S(1)}, bf16[512,2048]{1,0:T(8,128)(2,1)}, u32[]{:S(2)}) copy-start(bf16[512,2048]{1,0:T(8,128)(2,1)} %w_ref.1) | copy-start | bytes 6291460
  8.0 3.6 %collective-permute-start = (bf16[3,16,512]{2,1,0:T(8,128)(2,1)}, bf16[3,16,512]{2,1,0:T(8,128)(2,1)S(1)}, u32[]{:S(2)}, u32[]{:S(2)}) collective-permute-start(bf16[3,16,512]{2,1,0:T(8,128)(2,1)} %get-tuple-element.70), channel_id=1, source_target_pairs={{0,4},{4,8},{8,12},{12,16},{16,20},{20,24},{24,28},{1,5},{5,9},{9,... | collective-permute-start | bytes 147464 | tf_op jit(solution)/shard_map/ppermute | solution.py:610
  12.7 20.0 %copy-start.18 = (f32[512]{0:T(512)S(1)}, f32[512]{0:T(512)}, u32[]{:S(2)}) copy-start(f32[512]{0:T(512)} %param.19) | copy-start | bytes 6148
  16.5 11.4 %collective-permute-start.3 = (bf16[672,128]{1,0:T(8,128)(2,1)S(1)}, bf16[672,128]{1,0:T(8,128)(2,1)S(1)}, u32[]{:S(2)}, u32[]{:S(2)}) collective-permute-start(bf16[672,128]{1,0:T(8,128)(2,1)S(1)} %get-tuple-element.73), channel_id=1, source_target_pairs={{0,24},{4,28},{8,16},{12,20},{16,8},{20,12},{24,0},{28,4},{1,25},{... | collective-permute-start | bytes 516104 | tf_op jit(solution)/shard_map/ppermute | solution.py:438
  22.5 7.8 %collective-permute-start.2 = (bf16[672,128]{1,0:T(8,128)(2,1)S(1)}, bf16[672,128]{1,0:T(8,128)(2,1)S(1)}, u32[]{:S(2)}, u32[]{:S(2)}) collective-permute-start(bf16[672,128]{1,0:T(8,128)(2,1)S(1)} %get-tuple-element.73), channel_id=1, source_target_pairs={{0,16},{4,20},{8,24},{12,28},{16,0},{20,4},{24,8},{28,12},{1,17},{... | collective-permute-start | bytes 516104 | tf_op jit(solution)/shard_map/ppermute | solution.py:438
  23.1 7.3 %collective-permute-start.1 = (bf16[672,128]{1,0:T(8,128)(2,1)S(1)}, bf16[672,128]{1,0:T(8,128)(2,1)S(1)}, u32[]{:S(2)}, u32[]{:S(2)}) collective-permute-start(bf16[672,128]{1,0:T(8,128)(2,1)S(1)} %get-tuple-element.73), channel_id=1, source_target_pairs={{0,8},{4,12},{8,0},{12,4},{16,24},{20,28},{24,16},{28,20},{1,9},{5... | collective-permute-start | bytes 516104 | tf_op jit(solution)/shard_map/ppermute | solution.py:438
  30.5 2.2 %collective-permute-start.4 = (bf16[4,672,128]{2,1,0:T(8,128)(2,1)S(1)}, bf16[4,672,128]{2,1,0:T(8,128)(2,1)S(1)}, u32[]{:S(2)}, u32[]{:S(2)}) collective-permute-start(bf16[4,672,128]{2,1,0:T(8,128)(2,1)S(1)} %pad_maximum_fusion.near_ref.near_routes.fwd_near), channel_id=1, source_target_pairs={{0,4},{4,0},{8,12},{12,8},{16,20},{20,16},{24,28},{28,24},{1,5},{5... | collective-permute-start | bytes 2064392 | tf_op jit(solution)/shard_map/ppermute | solution.py:438
  30.6 2.1 %copy-start.3 = (bf16[3,256,512]{2,1,0:T(8,128)(2,1)S(1)}, bf16[3,256,512]{2,1,0:T(8,128)(2,1)}, u32[]{:S(2)}) copy-start(bf16[3,256,512]{2,1,0:T(8,128)(2,1)} %copy-done.2) | copy-start | bytes 2359300
  30.7 5.9 %copy-start.12 = (bf16[576,128]{1,0:T(8,128)(2,1)S(1)}, bf16[576,128]{1,0:T(8,128)(2,1)}, u32[]{:S(2)}) copy-start(bf16[576,128]{1,0:T(8,128)(2,1)} %copy-done.11) | copy-start | bytes 442372
  32.7 9.9 %copy-start.4 = (bf16[1,2048,512]{2,1,0:T(8,128)(2,1)S(1)}, bf16[1,2048,512]{2,1,0:T(8,128)(2,1)}, u32[]{:S(2)}) copy-start(bf16[1,2048,512]{2,1,0:T(8,128)(2,1)} %gate_ref.3) | copy-start | bytes 6291460
  32.7 9.9 %copy-start.5 = (bf16[1,2048,512]{2,1,0:T(8,128)(2,1)S(1)}, bf16[1,2048,512]{2,1,0:T(8,128)(2,1)}, u32[]{:S(2)}) copy-start(bf16[1,2048,512]{2,1,0:T(8,128)(2,1)} %up_ref.3) | copy-start | bytes 6291460
  36.6 24.6 %copy-start = (bf16[256,2048]{1,0:T(8,128)(2,1)S(1)}, bf16[256,2048]{1,0:T(8,128)(2,1)}, u32[]{:S(2)}) copy-start(bf16[256,2048]{1,0:T(8,128)(2,1)} %x_ref.3) | copy-start | bytes 3145732
  36.6 8.8 %collective-permute-start.8 = (bf16[1,576,128]{2,1,0:T(8,128)(2,1)S(1)}, bf16[1,576,128]{2,1,0:T(8,128)(2,1)S(1)}, u32[]{:S(2)}, u32[]{:S(2)}) collective-permute-start(bf16[1,576,128]{2,1,0:T(8,128)(2,1)S(1)} %bitcast.49), channel_id=1, source_target_pairs={{0,8},{4,12},{8,0},{12,4},{16,24},{20,28},{24,16},{28,20},{1,9},{5... | collective-permute-start | bytes 442376 | tf_op jit(solution)/shard_map/ppermute | solution.py:438
  38.3 13.1 %collective-permute-start.5 = (bf16[64,2048]{1,0:T(8,128)(2,1)S(1)}, bf16[64,2048]{1,0:T(8,128)(2,1)S(1)}, u32[]{:S(2)}, u32[]{:S(2)}) collective-permute-start(bf16[64,2048]{1,0:T(8,128)(2,1)S(1)} %get-tuple-element.75), channel_id=1, source_target_pairs={{0,1},{1,0},{2,3},{3,2},{4,5},{5,4},{6,7},{7,6},{8,9},{9,8},{10,11... | collective-permute-start | bytes 786440 | tf_op jit(solution)/shard_map/ppermute | solution.py:444
  39.8 21.4 %collective-permute-start.6 = (bf16[64,2048]{1,0:T(8,128)(2,1)S(1)}, bf16[64,2048]{1,0:T(8,128)(2,1)S(1)}, u32[]{:S(2)}, u32[]{:S(2)}) collective-permute-start(bf16[64,2048]{1,0:T(8,128)(2,1)S(1)} %get-tuple-element.76), channel_id=1, source_target_pairs={{0,2},{1,3},{2,0},{3,1},{4,6},{5,7},{6,4},{7,5},{8,10},{9,11},{10,... | collective-permute-start | bytes 786440 | tf_op jit(solution)/shard_map/ppermute | solution.py:444
  42.4 18.8 %collective-permute-start.7 = (bf16[64,2048]{1,0:T(8,128)(2,1)S(1)}, bf16[64,2048]{1,0:T(8,128)(2,1)S(1)}, u32[]{:S(2)}, u32[]{:S(2)}) collective-permute-start(bf16[64,2048]{1,0:T(8,128)(2,1)S(1)} %get-tuple-element.77), channel_id=1, source_target_pairs={{0,3},{1,2},{2,1},{3,0},{4,7},{5,6},{6,5},{7,4},{8,11},{9,10},{10,... | collective-permute-start | bytes 786440 | tf_op jit(solution)/shard_map/ppermute | solution.py:444
  44.2 17.0 %copy-start.17 = (f32[2048]{0:T(1024)S(1)}, f32[2048]{0:T(1024)}, u32[]{:S(2)}) copy-start(f32[2048]{0:T(1024)} %param.21) | copy-start | bytes 24580
  62.1 8.8 %collective-permute-start.12 = (bf16[2,576,128]{2,1,0:T(8,128)(2,1)S(1)}, bf16[2,576,128]{2,1,0:T(8,128)(2,1)S(1)}, u32[]{:S(2)}, u32[]{:S(2)}) collective-permute-start(bf16[2,576,128]{2,1,0:T(8,128)(2,1)S(1)} %pad_maximum_fusion.5), channel_id=1, source_target_pairs={{0,16},{4,20},{8,24},{12,28},{16,0},{20,4},{24,8},{28,12},{1,17},{... | collective-permute-start | bytes 884744 | tf_op jit(solution)/shard_map/ppermute | solution.py:438
  63.0 7.9 %collective-permute-start.11 = (bf16[32,2048]{1,0:T(8,128)(2,1)S(1)}, bf16[32,2048]{1,0:T(8,128)(2,1)S(1)}, u32[]{:S(2)}, u32[]{:S(2)}) collective-permute-start(bf16[32,2048]{1,0:T(8,128)(2,1)S(1)} %get-tuple-element.89.refs_0_), channel_id=1, source_target_pairs={{0,3},{1,2},{2,1},{3,0},{4,7},{5,6},{6,5},{7,4},{8,11},{9,10},{10,... | collective-permute-start | bytes 393224 | tf_op jit(solution)/shard_map/ppermute | solution.py:444
  65.5 12.7 %collective-permute-start.10 = (bf16[32,2048]{1,0:T(8,128)(2,1)S(1)}, bf16[32,2048]{1,0:T(8,128)(2,1)S(1)}, u32[]{:S(2)}, u32[]{:S(2)}) collective-permute-start(bf16[32,2048]{1,0:T(8,128)(2,1)S(1)} %get-tuple-element.89.refs_0_), channel_id=1, source_target_pairs={{0,2},{1,3},{2,0},{3,1},{4,6},{5,7},{6,4},{7,5},{8,10},{9,11},{10,... | collective-permute-start | bytes 393224 | tf_op jit(solution)/shard_map/ppermute | solution.py:444
  70.8 7.5 %collective-permute-start.9 = (bf16[32,2048]{1,0:T(8,128)(2,1)S(1)}, bf16[32,2048]{1,0:T(8,128)(2,1)S(1)}, u32[]{:S(2)}, u32[]{:S(2)}) collective-permute-start(bf16[32,2048]{1,0:T(8,128)(2,1)S(1)} %get-tuple-element.89.refs_0_), channel_id=1, source_target_pairs={{0,1},{1,0},{2,3},{3,2},{4,5},{5,4},{6,7},{7,6},{8,9},{9,8},{10,11... | collective-permute-start | bytes 393224 | tf_op jit(solution)/shard_map/ppermute | solution.py:444
  71.0 32.9 %copy-start.7 = (bf16[1,512,2048]{2,1,0:T(8,128)(2,1)S(1)}, bf16[1,512,2048]{2,1,0:T(8,128)(2,1)}, u32[]{:S(2)}) copy-start(bf16[1,512,2048]{2,1,0:T(8,128)(2,1)} %down_ref.3) | copy-start | bytes 6291460
  78.8 14.0 %collective-permute-start.14 = (bf16[128,2048]{1,0:T(8,128)(2,1)S(1)}, bf16[128,2048]{1,0:T(8,128)(2,1)S(1)}, u32[]{:S(2)}, u32[]{:S(2)}) collective-permute-start(bf16[128,2048]{1,0:T(8,128)(2,1)S(1)} %join_rows.2.refs_0_), channel_id=1, source_target_pairs={{0,16},{4,20},{8,24},{12,28},{16,0},{20,4},{24,8},{28,12},{1,17},{... | collective-permute-start | bytes 1572872 | tf_op jit(solution)/shard_map/ppermute | solution.py:438
  80.0 12.8 %collective-permute-start.13 = (bf16[128,2048]{1,0:T(8,128)(2,1)S(1)}, bf16[128,2048]{1,0:T(8,128)(2,1)S(1)}, u32[]{:S(2)}, u32[]{:S(2)}) collective-permute-start(bf16[128,2048]{1,0:T(8,128)(2,1)S(1)} %join_rows.2.refs_0_), channel_id=1, source_target_pairs={{0,8},{4,12},{8,0},{12,4},{16,24},{20,28},{24,16},{28,20},{1,9},{5... | collective-permute-start | bytes 1572872 | tf_op jit(solution)/shard_map/ppermute | solution.py:438
  80.4 8.1 %collective-permute-start.17 = (bf16[32,2048]{1,0:T(8,128)(2,1)S(1)}, bf16[32,2048]{1,0:T(8,128)(2,1)S(1)}, u32[]{:S(2)}, u32[]{:S(2)}) collective-permute-start(bf16[32,2048]{1,0:T(8,128)(2,1)S(1)} %get-tuple-element.93.refs_0_), channel_id=1, source_target_pairs={{0,3},{1,2},{2,1},{3,0},{4,7},{5,6},{6,5},{7,4},{8,11},{9,10},{10,... | collective-permute-start | bytes 393224 | tf_op jit(solution)/shard_map/ppermute | solution.py:444
  83.1 9.1 %collective-permute-start.16 = (bf16[32,2048]{1,0:T(8,128)(2,1)S(1)}, bf16[32,2048]{1,0:T(8,128)(2,1)S(1)}, u32[]{:S(2)}, u32[]{:S(2)}) collective-permute-start(bf16[32,2048]{1,0:T(8,128)(2,1)S(1)} %get-tuple-element.93.refs_0_), channel_id=1, source_target_pairs={{0,2},{1,3},{2,0},{3,1},{4,6},{5,7},{6,4},{7,5},{8,10},{9,11},{10,... | collective-permute-start | bytes 393224 | tf_op jit(solution)/shard_map/ppermute | solution.py:444
  83.1 9.1 %collective-permute-start.15 = (bf16[32,2048]{1,0:T(8,128)(2,1)S(1)}, bf16[32,2048]{1,0:T(8,128)(2,1)S(1)}, u32[]{:S(2)}, u32[]{:S(2)}) collective-permute-start(bf16[32,2048]{1,0:T(8,128)(2,1)S(1)} %get-tuple-element.93.refs_0_), channel_id=1, source_target_pairs={{0,1},{1,0},{2,3},{3,2},{4,5},{5,4},{6,7},{7,6},{8,9},{9,8},{10,11... | collective-permute-start | bytes 393224 | tf_op jit(solution)/shard_map/ppermute | solution.py:444
  92.8 7.1 %collective-permute-start.21 = (bf16[64,2048]{1,0:T(8,128)(2,1)S(1)}, bf16[64,2048]{1,0:T(8,128)(2,1)S(1)}, u32[]{:S(2)}, u32[]{:S(2)}) collective-permute-start(bf16[64,2048]{1,0:T(8,128)(2,1)S(1)} %slice.96), channel_id=1, source_target_pairs={{0,16},{4,20},{8,24},{12,28},{16,0},{20,4},{24,8},{28,12},{1,17},{... | collective-permute-start | bytes 786440 | tf_op jit(solution)/shard_map/ppermute | solution.py:438
  94.6 6.8 %collective-permute-start.22 = (bf16[64,2048]{1,0:T(8,128)(2,1)S(1)}, bf16[64,2048]{1,0:T(8,128)(2,1)S(1)}, u32[]{:S(2)}, u32[]{:S(2)}) collective-permute-start(bf16[64,2048]{1,0:T(8,128)(2,1)S(1)} %slice.97), channel_id=1, source_target_pairs={{0,8},{4,12},{8,0},{12,4},{16,24},{20,28},{24,16},{28,20},{1,9},{5... | collective-permute-start | bytes 786440 | tf_op jit(solution)/shard_map/ppermute | solution.py:438
  95.4 7.0 %collective-permute-start.19 = (bf16[128,2048]{1,0:T(8,128)(2,1)S(1)}, bf16[128,2048]{1,0:T(8,128)(2,1)S(1)}, u32[]{:S(2)}, u32[]{:S(2)}) collective-permute-start(bf16[128,2048]{1,0:T(8,128)(2,1)S(1)} %collective-permute-done.13.refs_2_), channel_id=1, source_target_pairs={{0,4},{4,0},{8,12},{12,8},{16,20},{20,16},{24,28},{28,24},{1,5},{5... | collective-permute-start | bytes 1572872 | tf_op jit(solution)/shard_map/ppermute | solution.py:438
  95.4 8.5 %collective-permute-start.20 = (bf16[128,2048]{1,0:T(8,128)(2,1)S(1)}, bf16[128,2048]{1,0:T(8,128)(2,1)S(1)}, u32[]{:S(2)}, u32[]{:S(2)}) collective-permute-start(bf16[128,2048]{1,0:T(8,128)(2,1)S(1)} %collective-permute-done.14.refs_4_), channel_id=1, source_target_pairs={{0,4},{4,0},{8,12},{12,8},{16,20},{20,16},{24,28},{28,24},{1,5},{5... | collective-permute-start | bytes 1572872 | tf_op jit(solution)/shard_map/ppermute | solution.py:438
  95.9 6.1 %collective-permute-start.18 = (bf16[128,2048]{1,0:T(8,128)(2,1)S(1)}, bf16[128,2048]{1,0:T(8,128)(2,1)S(1)}, u32[]{:S(2)}, u32[]{:S(2)}) collective-permute-start(bf16[128,2048]{1,0:T(8,128)(2,1)S(1)} %join_rows.2.refs_0_), channel_id=1, source_target_pairs={{0,4},{4,0},{8,12},{12,8},{16,20},{20,16},{24,28},{28,24},{1,5},{5... | collective-permute-start | bytes 1572872 | tf_op jit(solution)/shard_map/ppermute | solution.py:438
  101.4 2.4 %collective-permute-start.23 = (bf16[128,2048]{1,0:T(8,128)(2,1)S(1)}, bf16[128,2048]{1,0:T(8,128)(2,1)S(1)}, u32[]{:S(2)}, u32[]{:S(2)}) collective-permute-start(bf16[128,2048]{1,0:T(8,128)(2,1)S(1)} %constant_dynamic-update-slice_fusion.2.refs_6_), channel_id=1, source_target_pairs={{0,4},{4,0},{8,12},{12,8},{16,20},{20,16},{24,28},{28,24},{1,5},{5... | collective-permute-start | bytes 1572872 | tf_op jit(solution)/shard_map/ppermute | solution.py:438
  101.5 11.5 %collective-permute-start.27 = (bf16[4,576,128]{2,1,0:T(8,128)(2,1)S(1)}, bf16[4,576,128]{2,1,0:T(8,128)(2,1)S(1)}, u32[]{:S(2)}, u32[]{:S(2)}) collective-permute-start(bf16[4,576,128]{2,1,0:T(8,128)(2,1)S(1)} %constant_dynamic-update-slice_fusion.bwd_near), channel_id=1, source_target_pairs={{0,4},{4,0},{8,12},{12,8},{16,20},{20,16},{24,28},{28,24},{1,5},{5... | collective-permute-start | bytes 1769480 | tf_op jit(solution)/shard_map/ppermute | solution.py:438
  102.0 13.9 %collective-permute-start.26 = (bf16[128,2048]{1,0:T(8,128)(2,1)S(1)}, bf16[128,2048]{1,0:T(8,128)(2,1)S(1)}, u32[]{:S(2)}, u32[]{:S(2)}) collective-permute-start(bf16[128,2048]{1,0:T(8,128)(2,1)S(1)} %join_rows.3.refs_0_), channel_id=1, source_target_pairs={{0,16},{4,20},{8,24},{12,28},{16,0},{20,4},{24,8},{28,12},{1,17},{... | collective-permute-start | bytes 1572872 | tf_op jit(solution)/shard_map/ppermute | solution.py:438
  102.4 13.6 %collective-permute-start.25 = (bf16[128,2048]{1,0:T(8,128)(2,1)S(1)}, bf16[128,2048]{1,0:T(8,128)(2,1)S(1)}, u32[]{:S(2)}, u32[]{:S(2)}) collective-permute-start(bf16[128,2048]{1,0:T(8,128)(2,1)S(1)} %join_rows.3.refs_0_), channel_id=1, source_target_pairs={{0,8},{4,12},{8,0},{12,4},{16,24},{20,28},{24,16},{28,20},{1,9},{5... | collective-permute-start | bytes 1572872 | tf_op jit(solution)/shard_map/ppermute | solution.py:438
  103.9 12.1 %collective-permute-start.24 = (bf16[128,2048]{1,0:T(8,128)(2,1)S(1)}, bf16[128,2048]{1,0:T(8,128)(2,1)S(1)}, u32[]{:S(2)}, u32[]{:S(2)}) collective-permute-start(bf16[128,2048]{1,0:T(8,128)(2,1)S(1)} %join_rows.3.refs_0_), channel_id=1, source_target_pairs={{0,4},{4,0},{8,12},{12,8},{16,20},{20,16},{24,28},{28,24},{1,5},{5... | collective-permute-start | bytes 1572872 | tf_op jit(solution)/shard_map/ppermute | solution.py:438
  116.0 5.7 %collective-permute-start.28 = (bf16[4,128,2048]{2,1,0:T(8,128)(2,1)S(1)}, bf16[4,128,2048]{2,1,0:T(8,128)(2,1)S(1)}, u32[]{:S(2)}, u32[]{:S(2)}) collective-permute-start(bf16[4,128,2048]{2,1,0:T(8,128)(2,1)S(1)} %get-tuple-element.100), channel_id=1, source_target_pairs={{0,4},{4,0},{8,12},{12,8},{16,20},{20,16},{24,28},{28,24},{1,5},{5... | collective-permute-start | bytes 6291464 | tf_op jit(solution)/shard_map/ppermute | solution.py:438
  116.0 4.9 %collective-permute-start.30 = (bf16[128,2048]{1,0:T(8,128)(2,1)S(1)}, bf16[128,2048]{1,0:T(8,128)(2,1)S(1)}, u32[]{:S(2)}, u32[]{:S(2)}) collective-permute-start(bf16[128,2048]{1,0:T(8,128)(2,1)S(1)} %collective-permute-done.26.refs_4_), channel_id=1, source_target_pairs={{0,4},{4,0},{8,12},{12,8},{16,20},{20,16},{24,28},{28,24},{1,5},{5... | collective-permute-start | bytes 1572872 | tf_op jit(solution)/shard_map/ppermute | solution.py:438
  116.5 5.1 %collective-permute-start.29 = (bf16[128,2048]{1,0:T(8,128)(2,1)S(1)}, bf16[128,2048]{1,0:T(8,128)(2,1)S(1)}, u32[]{:S(2)}, u32[]{:S(2)}) collective-permute-start(bf16[128,2048]{1,0:T(8,128)(2,1)S(1)} %collective-permute-done.25.refs_2_), channel_id=1, source_target_pairs={{0,4},{4,0},{8,12},{12,8},{16,20},{20,16},{24,28},{28,24},{1,5},{5... | collective-permute-start | bytes 1572872 | tf_op jit(solution)/shard_map/ppermute | solution.py:438
  116.6 8.8 %collective-permute-start.36 = (bf16[64,2048]{1,0:T(8,128)(2,1)S(1)}, bf16[64,2048]{1,0:T(8,128)(2,1)S(1)}, u32[]{:S(2)}, u32[]{:S(2)}) collective-permute-start(bf16[64,2048]{1,0:T(8,128)(2,1)S(1)} %slice.131), channel_id=1, source_target_pairs={{0,8},{4,12},{8,0},{12,4},{16,24},{20,28},{24,16},{28,20},{1,9},{5... | collective-permute-start | bytes 786440 | tf_op jit(solution)/shard_map/ppermute | solution.py:438
  118.1 8.5 %collective-permute-start.35 = (bf16[64,2048]{1,0:T(8,128)(2,1)S(1)}, bf16[64,2048]{1,0:T(8,128)(2,1)S(1)}, u32[]{:S(2)}, u32[]{:S(2)}) collective-permute-start(bf16[64,2048]{1,0:T(8,128)(2,1)S(1)} %slice.130), channel_id=1, source_target_pairs={{0,16},{4,20},{8,24},{12,28},{16,0},{20,4},{24,8},{28,12},{1,17},{... | collective-permute-start | bytes 786440 | tf_op jit(solution)/shard_map/ppermute | solution.py:438
  126.7 2.3 %collective-permute-start.37 = (bf16[128,2048]{1,0:T(8,128)(2,1)S(1)}, bf16[128,2048]{1,0:T(8,128)(2,1)S(1)}, u32[]{:S(2)}, u32[]{:S(2)}) collective-permute-start(bf16[128,2048]{1,0:T(8,128)(2,1)S(1)} %constant_dynamic-update-slice_fusion.4.refs_6_), channel_id=1, source_target_pairs={{0,4},{4,0},{8,12},{12,8},{16,20},{20,16},{24,28},{28,24},{1,5},{5... | collective-permute-start | bytes 1572872 | tf_op jit(solution)/shard_map/ppermute | solution.py:438
  126.7 14.3 %collective-permute-start.31 = (bf16[128,2048]{1,0:T(8,128)(2,1)S(1)}, bf16[128,2048]{1,0:T(8,128)(2,1)S(1)}, u32[]{:S(2)}, u32[]{:S(2)}) collective-permute-start(bf16[128,2048]{1,0:T(8,128)(2,1)S(1)} %pad_maximum_fusion.1), channel_id=1, source_target_pairs={{0,8},{4,12},{8,0},{12,4},{16,24},{20,28},{24,16},{28,20},{1,9},{5... | collective-permute-start | bytes 1572872 | tf_op jit(solution)/shard_map/ppermute | solution.py:438
  127.3 14.0 %collective-permute-start.32 = (bf16[128,2048]{1,0:T(8,128)(2,1)S(1)}, bf16[128,2048]{1,0:T(8,128)(2,1)S(1)}, u32[]{:S(2)}, u32[]{:S(2)}) collective-permute-start(bf16[128,2048]{1,0:T(8,128)(2,1)S(1)} %pad_maximum_fusion.2), channel_id=1, source_target_pairs={{0,16},{4,20},{8,24},{12,28},{16,0},{20,4},{24,8},{28,12},{1,17},{... | collective-permute-start | bytes 1572872 | tf_op jit(solution)/shard_map/ppermute | solution.py:438
  141.3 10.2 %collective-permute-start.38 = (bf16[4,128,2048]{2,1,0:T(8,128)(2,1)S(1)}, bf16[4,128,2048]{2,1,0:T(8,128)(2,1)S(1)}, u32[]{:S(2)}, u32[]{:S(2)}) collective-permute-start(bf16[4,128,2048]{2,1,0:T(8,128)(2,1)S(1)} %get-tuple-element.114), channel_id=1, source_target_pairs={{0,4},{4,0},{8,12},{12,8},{16,20},{20,16},{24,28},{28,24},{1,5},{5... | collective-permute-start | bytes 6291464 | tf_op jit(solution)/shard_map/ppermute | solution.py:438
  141.6 8.8 %collective-permute-start.34 = (bf16[64,2048]{1,0:T(8,128)(2,1)S(1)}, bf16[64,2048]{1,0:T(8,128)(2,1)S(1)}, u32[]{:S(2)}, u32[]{:S(2)}) collective-permute-start(bf16[64,2048]{1,0:T(8,128)(2,1)S(1)} %get-tuple-element.140), channel_id=1, source_target_pairs={{0,8},{4,12},{8,0},{12,4},{16,24},{20,28},{24,16},{28,20},{1,9},{5... | collective-permute-start | bytes 786440 | tf_op jit(solution)/shard_map/ppermute | solution.py:438
  143.1 8.4 %collective-permute-start.33 = (bf16[64,2048]{1,0:T(8,128)(2,1)S(1)}, bf16[64,2048]{1,0:T(8,128)(2,1)S(1)}, u32[]{:S(2)}, u32[]{:S(2)}) collective-permute-start(bf16[64,2048]{1,0:T(8,128)(2,1)S(1)} %get-tuple-element.141), channel_id=1, source_target_pairs={{0,16},{4,20},{8,24},{12,28},{16,0},{20,4},{24,8},{28,12},{1,17},{... | collective-permute-start | bytes 786440 | tf_op jit(solution)/shard_map/ppermute | solution.py:438
  152.0 13.3 %collective-permute-start.42 = (bf16[128,2048]{1,0:T(8,128)(2,1)S(1)}, bf16[128,2048]{1,0:T(8,128)(2,1)S(1)}, u32[]{:S(2)}, u32[]{:S(2)}) collective-permute-start(bf16[128,2048]{1,0:T(8,128)(2,1)S(1)} %pad_maximum_fusion.3), channel_id=1, source_target_pairs={{0,8},{4,12},{8,0},{12,4},{16,24},{20,28},{24,16},{28,20},{1,9},{5... | collective-permute-start | bytes 1572872 | tf_op jit(solution)/shard_map/ppermute | solution.py:438
  152.7 13.1 %collective-permute-start.43 = (bf16[128,2048]{1,0:T(8,128)(2,1)S(1)}, bf16[128,2048]{1,0:T(8,128)(2,1)S(1)}, u32[]{:S(2)}, u32[]{:S(2)}) collective-permute-start(bf16[128,2048]{1,0:T(8,128)(2,1)S(1)} %pad_maximum_fusion.4), channel_id=1, source_target_pairs={{0,16},{4,20},{8,24},{12,28},{16,0},{20,4},{24,8},{28,12},{1,17},{... | collective-permute-start | bytes 1572872 | tf_op jit(solution)/shard_map/ppermute | solution.py:438
  155.4 6.8 %collective-permute-start.39 = (bf16[128,512]{1,0:T(8,128)(2,1)S(1)}, bf16[128,512]{1,0:T(8,128)(2,1)S(1)}, u32[]{:S(2)}, u32[]{:S(2)}) collective-permute-start(bf16[128,512]{1,0:T(8,128)(2,1)S(1)} %get-tuple-element.121), channel_id=1, source_target_pairs={{0,1},{1,0},{2,3},{3,2},{4,5},{5,4},{6,7},{7,6},{8,9},{9,8},{10,11... | collective-permute-start | bytes 393224 | tf_op jit(solution)/shard_map/ppermute | solution.py:444
  155.5 8.1 %collective-permute-start.40 = (bf16[128,512]{1,0:T(8,128)(2,1)S(1)}, bf16[128,512]{1,0:T(8,128)(2,1)S(1)}, u32[]{:S(2)}, u32[]{:S(2)}) collective-permute-start(bf16[128,512]{1,0:T(8,128)(2,1)S(1)} %get-tuple-element.122), channel_id=1, source_target_pairs={{0,2},{1,3},{2,0},{3,1},{4,6},{5,7},{6,4},{7,5},{8,10},{9,11},{10,... | collective-permute-start | bytes 393224 | tf_op jit(solution)/shard_map/ppermute | solution.py:444
  166.0 6.5 %collective-permute-start.45 = (bf16[64,2048]{1,0:T(8,128)(2,1)S(1)}, bf16[64,2048]{1,0:T(8,128)(2,1)S(1)}, u32[]{:S(2)}, u32[]{:S(2)}) collective-permute-start(bf16[64,2048]{1,0:T(8,128)(2,1)S(1)} %get-tuple-element.134), channel_id=1, source_target_pairs={{0,8},{4,12},{8,0},{12,4},{16,24},{20,28},{24,16},{28,20},{1,9},{5... | collective-permute-start | bytes 786440 | tf_op jit(solution)/shard_map/ppermute | solution.py:438
  167.5 6.4 %collective-permute-start.44 = (bf16[64,2048]{1,0:T(8,128)(2,1)S(1)}, bf16[64,2048]{1,0:T(8,128)(2,1)S(1)}, u32[]{:S(2)}, u32[]{:S(2)}) collective-permute-start(bf16[64,2048]{1,0:T(8,128)(2,1)S(1)} %get-tuple-element.135), channel_id=1, source_target_pairs={{0,16},{4,20},{8,24},{12,28},{16,0},{20,4},{24,8},{28,12},{1,17},{... | collective-permute-start | bytes 786440 | tf_op jit(solution)/shard_map/ppermute | solution.py:438
  168.4 15.7 %collective-permute-start.41 = (bf16[128,512]{1,0:T(8,128)(2,1)S(1)}, bf16[128,512]{1,0:T(8,128)(2,1)S(1)}, u32[]{:S(2)}, u32[]{:S(2)}) collective-permute-start(bf16[128,512]{1,0:T(8,128)(2,1)S(1)} %get-tuple-element.123), channel_id=1, source_target_pairs={{0,3},{1,2},{2,1},{3,0},{4,7},{5,6},{6,5},{7,4},{8,11},{9,10},{10,... | collective-permute-start | bytes 393224 | tf_op jit(solution)/shard_map/ppermute | solution.py:444
  173.9 5.4 %copy-start.9 = (bf16[256,512]{1,0:T(8,128)(2,1)S(1)}, bf16[256,512]{1,0:T(8,128)(2,1)}, u32[]{:S(2)}) copy-start(bf16[256,512]{1,0:T(8,128)(2,1)} %cot_ref.3) | copy-start | bytes 786436
  174.9 9.2 %collective-permute-start.46 = (bf16[128,512]{1,0:T(8,128)(2,1)S(1)}, bf16[128,512]{1,0:T(8,128)(2,1)S(1)}, u32[]{:S(2)}, u32[]{:S(2)}) collective-permute-start(bf16[128,512]{1,0:T(8,128)(2,1)S(1)} %get-tuple-element.128), channel_id=1, source_target_pairs={{0,1},{1,0},{2,3},{3,2},{4,5},{5,4},{6,7},{7,6},{8,9},{9,8},{10,11... | collective-permute-start | bytes 393224 | tf_op jit(solution)/shard_map/ppermute | solution.py:444
  174.9 10.5 %collective-permute-start.47 = (bf16[128,512]{1,0:T(8,128)(2,1)S(1)}, bf16[128,512]{1,0:T(8,128)(2,1)S(1)}, u32[]{:S(2)}, u32[]{:S(2)}) collective-permute-start(bf16[128,512]{1,0:T(8,128)(2,1)S(1)} %get-tuple-element.129), channel_id=1, source_target_pairs={{0,2},{1,3},{2,0},{3,1},{4,6},{5,7},{6,4},{7,5},{8,10},{9,11},{10,... | collective-permute-start | bytes 393224 | tf_op jit(solution)/shard_map/ppermute | solution.py:444
  177.8 7.6 %collective-permute-start.48 = (bf16[128,512]{1,0:T(8,128)(2,1)S(1)}, bf16[128,512]{1,0:T(8,128)(2,1)S(1)}, u32[]{:S(2)}, u32[]{:S(2)}) collective-permute-start(bf16[128,512]{1,0:T(8,128)(2,1)S(1)} %get-tuple-element.130), channel_id=1, source_target_pairs={{0,3},{1,2},{2,1},{3,0},{4,7},{5,6},{6,5},{7,4},{8,11},{9,10},{10,... | collective-permute-start | bytes 393224 | tf_op jit(solution)/shard_map/ppermute | solution.py:444
  (4 other events, 4.3 us)

commit v15 on v14

--- a/solution.py
+++ b/solution.py
@@ -210,7 +210,7 @@
         headed_ref[:, at] = (attended * scale * gain_ref[:, at]).astype(BF)
     whole_ref[...] = mm(headed_ref[...], w_ref[...]).astype(BF)
     part = rows // len(out_refs) // chunks
-    for mask, ref in enumerate(out_refs):
+    for mask, ref in enumerate(reversed(out_refs)):
         for chunk in range(chunks):
             start = chunk * len(out_refs) * part + (me_ref[2] ^ mask) * part
             ref[chunk * part : (chunk + 1) * part] = whole_ref[pl.ds(pl.multiple_of(start, part), part), :]
@@ -515,7 +515,7 @@
     part, width = attn_ref.shape
     cols = width // parts
     own = pl.ds(pl.multiple_of(where_ref[2] * part, part), part)
-    for mask, out_ref in enumerate(outs):
+    for mask, out_ref in enumerate(reversed(outs)):
         at = pl.ds(pl.multiple_of((where_ref[2] ^ mask) * cols, cols), cols)
         total = near_ref[0, :, at].astype(F32) + arrived_ref[0, :, at].astype(F32)
         total_ref[...] = total
@@ -617,7 +617,7 @@
     parts = core_out(where, qkv, steps, *fwd, norm_gain, w_out, CHUNKS, n_head)
     where = stage(after(where, parts), w_gate, w_up, w_down)
     bwd = double(after(bwd, parts)[None], ROW)
-    normed, attn = norm_rows(where, hidden_in, after(send_heads(parts), bwd), gain_moe, CHUNKS)
+    normed, attn = norm_rows(where, hidden_in, after(send_heads(parts[::-1]), bwd), gain_moe, CHUNKS)
     bwd = after(bwd, normed)
     while bwd.shape[0] < n_ctx // 2:
         bwd = double(bwd, 2 * bwd.shape[0])
@@ -675,9 +675,9 @@
         else:
             last = last_sums(here, arrived, after(received, sums[-1][:-1]))
             terms = terms_of(first, received) + terms_of(last, send_sums(last))
-        sums.append(send_heads(sum_terms(where, attn[chunk], here, arrived, terms, n_head)))
+        sums.append(send_heads(sum_terms(where, attn[chunk], here, arrived, terms, n_head)[::-1]))
     grads = core_grads(where, qkv, grad_core, steps, fwd, bwd)
-    return (final_sum(where, hidden_in, sums), *grads)
+    return (final_sum(where, hidden_in, [part[::-1] for part in sums]), *grads)
 
 
 def solution(mesh):

time: 187 us -> 190 us (1.016)
  waiting for transfers between devices: 77.1 us -> 83.6 us
  starting transfers between devices: 58.5 us -> 54.9 us
    ppermute x33, waiting for transfers between devices: 39.1 us -> 42.8 us  [swap(): lax.ppermute(value, 'ctx', [(at, at ^ mask) for at in range(lax.axis_size...]
    ppermute x15, starting transfers between devices: 26.2 us -> 22.6 us  [send_heads(): lax.ppermute(parts[mask], 'head', [(at, at ^ mask) for at in range(count)])]
    ppermute x15, waiting for transfers between devices: 37 us -> 39.7 us  [send_heads(): lax.ppermute(parts[mask], 'head', [(at, at ^ mask) for at in range(count)])]
  transfers between devices with their start and end apart: 49 -> 49, of which waited for: 29 -> 31; matrix products, arithmetic and copies ran while one was open for 1% -> 1% of each run, Pallas kernels for 15% -> 15%
where the time goes in v15:
time: 190 us
  waiting for transfers between devices  83.6 us (44%)
  starting transfers between devices  54.9 us (29%)
  Pallas kernels  43.9 us (23%)
  local copies, waits for them, and re-layouts  4.58 us (2%)
    ppermute x33, waiting for transfers between devices, swap(): lax.ppermute(value, 'ctx', [(at, at ^ mask) for at in range(lax.axis_size...  42.8 us
    ppermute x15, waiting for transfers between devices, send_heads(): lax.ppermute(parts[mask], 'head', [(at, at ^ mask) for at in range(count)])  39.7 us
    ppermute x33, starting transfers between devices, swap(): lax.ppermute(value, 'ctx', [(at, at ^ mask) for at in range(lax.axis_size...  29.8 us
    ppermute x15, starting transfers between devices, send_heads(): lax.ppermute(parts[mask], 'head', [(at, at ^ mask) for at in range(count)])  22.6 us
    pallas_call x2, Pallas kernels, expert_pieces(): pl.pallas_call(functools.partial(expert_kernel, tuple(masks), chunk, expe...  18.3 us
    pallas_call x1, Pallas kernels, project(): pl.pallas_call(qkv_kernel, in_specs=[hbm, vmem, hbm], out_specs=[vmem, vm...  7.28 us
    pallas_call x1, Pallas kernels, core_grads(): pl.pallas_call(grad_kernel, in_specs=[pl.BlockSpec(memory_space=pltpu.SME...  4.7 us
    unnamed x41, local copies, waits for them, and re-layouts  4.43 us
  transfers between devices with their start and end apart: 49, of which 31 were waited for; matrix products, arithmetic and copies ran while one was open for 1% of the time, Pallas kernels for 15%

profile of v15, /device:TPU:0, one launch (start us, length us, event | category | flops | bytes accessed | tf_op | source)
XLA Modules:
  0.0 189.6 jit_solution(17914143653282835992)
XLA Ops:
  0.7 7.3 %qkv_projection.1 = (bf16[3,256,512]{2,1,0:T(8,128)(2,1)}, bf16[3,16,512]{2,1,0:T(8,128)(2,1)}) custom-call(bf16[256,2048]{1,0:T(8,128)(2,1)} %x_ref.3, f32[1,2048]{1,0:T(1,128)} %bitcast.63, bf16[3,2048,512]{2,1,0:T(8,128)(2,1)} %bitcast.59), custom_call_target="tpu_custom_call" | custom-call | tf_op jit(solution)/shard_map/qkv_projection/pallas_call | solution.py:68
  8.0 2.5 %collective-permute-start = (bf16[3,16,512]{2,1,0:T(8,128)(2,1)}, bf16[3,16,512]{2,1,0:T(8,128)(2,1)S(1)}, u32[]{:S(2)}, u32[]{:S(2)}) collective-permute-start(bf16[3,16,512]{2,1,0:T(8,128)(2,1)} %get-tuple-element.70), channel_id=1, source_target_pairs={{0,4},{4,8},{8,12},{12,16},{16,20},{20,24},{24,28},{1,5},{5,9},{9,... | collective-permute-start | bytes 147464 | tf_op jit(solution)/shard_map/ppermute | solution.py:610
  10.5 1.1 collective-permute-done.rim_ref
  11.6 1.1 copy-done.10
  12.7 2.1 %conv_states.1 = (bf16[3,256,512]{2,1,0:T(8,128)(2,1)S(1)}, bf16[672,128]{1,0:T(8,128)(2,1)S(1)}, bf16[576,128]{1,0:T(8,128)(2,1)S(1)}) custom-call(bf16[3,256,512]{2,1,0:T(8,128)(2,1)S(1)} %copy-done.10, bf16[3,16,512]{2,1,0:T(8,128)(2,1)S(1)} %collective-permute-done.rim_ref, f32[3,4,512]{2,1,0:T(4,128)S(1)} %bitcast.54, f32[4,256]{1,0:T(4,128)S(1)} %bitcast.51, ...), custom_call_target="tpu_custom_call" | custom-call | tf_op jit(solution)/shard_map/conv_states/pallas_call | solution.py:161
  14.9 0.9 copy-done.2
  16.5 6.1 %collective-permute-start.3 = (bf16[672,128]{1,0:T(8,128)(2,1)S(1)}, bf16[672,128]{1,0:T(8,128)(2,1)S(1)}, u32[]{:S(2)}, u32[]{:S(2)}) collective-permute-start(bf16[672,128]{1,0:T(8,128)(2,1)S(1)} %get-tuple-element.73), channel_id=1, source_target_pairs={{0,24},{4,28},{8,16},{12,20},{16,8},{20,12},{24,0},{28,4},{1,25},{... | collective-permute-start | bytes 516104 | tf_op jit(solution)/shard_map/ppermute | solution.py:438
  23.1 0.9 collective-permute-start.1
  24.0 3.8 %collective-permute-done.3 = bf16[672,128]{1,0:T(8,128)(2,1)S(1)} collective-permute-done((bf16[672,128]{1,0:T(8,128)(2,1)S(1)}, bf16[672,128]{1,0:T(8,128)(2,1)S(1)}, u32[]{:S(2)}, u32[]{:S(2)}) %collective-permute-start.3) | collective-permute-done | bytes 172064 | tf_op jit(solution)/shard_map/ppermute | solution.py:438
  27.8 2.5 %collective-permute-done.2 = bf16[672,128]{1,0:T(8,128)(2,1)S(1)} collective-permute-done((bf16[672,128]{1,0:T(8,128)(2,1)S(1)}, bf16[672,128]{1,0:T(8,128)(2,1)S(1)}, u32[]{:S(2)}, u32[]{:S(2)}) %collective-permute-start.2) | collective-permute-done | bytes 172064 | tf_op jit(solution)/shard_map/ppermute | solution.py:438
  30.7 1.1 stage_weights.2.me_ref.where_ref
  31.8 0.9 collective-permute-done.4.far_ref.far_routes.fwd_far
  32.7 3.8 %core_out.1 = (bf16[64,2048]{1,0:T(8,128)(2,1)S(1)}, bf16[64,2048]{1,0:T(8,128)(2,1)S(1)}, bf16[64,2048]{1,0:T(8,128)(2,1)S(1)}, bf16[64,2048]{1,0:T(8,128)(2,1)S(1)}) custom-call(s32[3]{0:T(128)S(1)} %stage_weights.2.me_ref.where_ref, bf16[3,256,512]{2,1,0:T(8,128)(2,1)S(1)} %copy-done.3, f32[4,256]{1,0:T(4,128)S(1)} %bitcast.52, f32[1,512]{1,0:T(1,128)S(1)} %bitcast.58, ...), custom_call_target="tpu_custom_call" | custom-call | tf_op jit(solution)/shard_map/core_out/pallas_call | solution.py:223
  36.6 1.7 collective-permute-start.8
  38.3 3.6 %collective-permute-start.7 = (bf16[64,2048]{1,0:T(8,128)(2,1)S(1)}, bf16[64,2048]{1,0:T(8,128)(2,1)S(1)}, u32[]{:S(2)}, u32[]{:S(2)}) collective-permute-start(bf16[64,2048]{1,0:T(8,128)(2,1)S(1)} %get-tuple-element.74), channel_id=1, source_target_pairs={{0,3},{1,2},{2,1},{3,0},{4,7},{5,6},{6,5},{7,4},{8,11},{9,10},{10,... | collective-permute-start | bytes 786440 | tf_op jit(solution)/shard_map/ppermute | solution.py:444
  42.7 1.6 copy-done.6
  44.2 1.1 stage_weights.3.where_ref.me_ref
  45.4 3.9 %collective-permute-done.7.refs_3_ = bf16[64,2048]{1,0:T(8,128)(2,1)S(1)} collective-permute-done((bf16[64,2048]{1,0:T(8,128)(2,1)S(1)}, bf16[64,2048]{1,0:T(8,128)(2,1)S(1)}, u32[]{:S(2)}, u32[]{:S(2)}) %collective-permute-start.7) | collective-permute-done | bytes 262176 | tf_op jit(solution)/shard_map/ppermute | solution.py:444
  49.4 14.9 %collective-permute-done.6.refs_2_ = bf16[64,2048]{1,0:T(8,128)(2,1)S(1)} collective-permute-done((bf16[64,2048]{1,0:T(8,128)(2,1)S(1)}, bf16[64,2048]{1,0:T(8,128)(2,1)S(1)}, u32[]{:S(2)}, u32[]{:S(2)}) %collective-permute-start.6) | collective-permute-done | bytes 262176 | tf_op jit(solution)/shard_map/ppermute | solution.py:444
  65.1 1.0 collective-permute-start.12
  66.1 2.5 %collective-permute-start.11 = (bf16[32,2048]{1,0:T(8,128)(2,1)S(1)}, bf16[32,2048]{1,0:T(8,128)(2,1)S(1)}, u32[]{:S(2)}, u32[]{:S(2)}) collective-permute-start(bf16[32,2048]{1,0:T(8,128)(2,1)S(1)} %get-tuple-element.89.refs_0_), channel_id=1, source_target_pairs={{0,3},{1,2},{2,1},{3,0},{4,7},{5,6},{6,5},{7,4},{8,11},{9,10},{10,... | collective-permute-start | bytes 393224 | tf_op jit(solution)/shard_map/ppermute | solution.py:444
  68.6 1.9 %collective-permute-start.9 = (bf16[32,2048]{1,0:T(8,128)(2,1)S(1)}, bf16[32,2048]{1,0:T(8,128)(2,1)S(1)}, u32[]{:S(2)}, u32[]{:S(2)}) collective-permute-start(bf16[32,2048]{1,0:T(8,128)(2,1)S(1)} %get-tuple-element.89.refs_0_), channel_id=1, source_target_pairs={{0,1},{1,0},{2,3},{3,2},{4,5},{5,4},{6,7},{7,6},{8,9},{9,8},{10,11... | collective-permute-start | bytes 393224 | tf_op jit(solution)/shard_map/ppermute | solution.py:444
  70.5 2.8 %collective-permute-done.12 = bf16[2,576,128]{2,1,0:T(8,128)(2,1)S(1)} collective-permute-done((bf16[2,576,128]{2,1,0:T(8,128)(2,1)S(1)}, bf16[2,576,128]{2,1,0:T(8,128)(2,1)S(1)}, u32[]{:S(2)}, u32[]{:S(2)}) %collective-permute-start.12) | collective-permute-done | bytes 294944 | tf_op jit(solution)/shard_map/ppermute | solution.py:438
  73.4 1.0 collective-permute-done.11.refs_3_
  74.3 4.3 %collective-permute-done.10.refs_2_ = bf16[32,2048]{1,0:T(8,128)(2,1)S(1)} collective-permute-done((bf16[32,2048]{1,0:T(8,128)(2,1)S(1)}, bf16[32,2048]{1,0:T(8,128)(2,1)S(1)}, u32[]{:S(2)}, u32[]{:S(2)}) %collective-permute-start.10) | collective-permute-done | bytes 131104 | tf_op jit(solution)/shard_map/ppermute | solution.py:444
  79.2 1.2 collective-permute-start.14
  80.8 1.8 collective-permute-start.17
  82.6 2.6 %collective-permute-start.15 = (bf16[32,2048]{1,0:T(8,128)(2,1)S(1)}, bf16[32,2048]{1,0:T(8,128)(2,1)S(1)}, u32[]{:S(2)}, u32[]{:S(2)}) collective-permute-start(bf16[32,2048]{1,0:T(8,128)(2,1)S(1)} %get-tuple-element.93.refs_0_), channel_id=1, source_target_pairs={{0,1},{1,0},{2,3},{3,2},{4,5},{5,4},{6,7},{7,6},{8,9},{9,8},{10,11... | collective-permute-start | bytes 393224 | tf_op jit(solution)/shard_map/ppermute | solution.py:444
  85.2 3.8 %collective-permute-done.17.refs_3_ = bf16[32,2048]{1,0:T(8,128)(2,1)S(1)} collective-permute-done((bf16[32,2048]{1,0:T(8,128)(2,1)S(1)}, bf16[32,2048]{1,0:T(8,128)(2,1)S(1)}, u32[]{:S(2)}, u32[]{:S(2)}) %collective-permute-start.17) | collective-permute-done | bytes 131104 | tf_op jit(solution)/shard_map/ppermute | solution.py:444
  89.1 4.6 %collective-permute-done.16.refs_2_ = bf16[32,2048]{1,0:T(8,128)(2,1)S(1)} collective-permute-done((bf16[32,2048]{1,0:T(8,128)(2,1)S(1)}, bf16[32,2048]{1,0:T(8,128)(2,1)S(1)}, u32[]{:S(2)}, u32[]{:S(2)}) %collective-permute-start.16) | collective-permute-done | bytes 131104 | tf_op jit(solution)/shard_map/ppermute | solution.py:444
  94.2 1.7 collective-permute-start.21
  97.3 4.6 %collective-permute-done.21 = bf16[64,2048]{1,0:T(8,128)(2,1)S(1)} collective-permute-done((bf16[64,2048]{1,0:T(8,128)(2,1)S(1)}, bf16[64,2048]{1,0:T(8,128)(2,1)S(1)}, u32[]{:S(2)}, u32[]{:S(2)}) %collective-permute-start.21) | collective-permute-done | bytes 262176 | tf_op jit(solution)/shard_map/ppermute | solution.py:438
  101.9 1.5 collective-permute-done.22
  104.3 1.5 collective-permute-start.25
  105.8 9.1 %expert_pieces.2 = (bf16[4,128,2048]{2,1,0:T(8,128)(2,1)S(1)}, bf16[4,128,2048]{2,1,0:T(8,128)(2,1)S(1)}) custom-call(s32[3]{0:T(128)S(1)} %stage_weights.3.where_ref.me_ref, bf16[4,672,128]{2,1,0:T(8,128)(2,1)S(1)} %pad_maximum_fusion.near_ref.near_routes.fwd_near, bf16[4,672,128]{2,1,0:T(8,128)(2,1)S(1)} %collective-permute-done.4.far_ref.far_routes.fwd_far, ...), custom_call_target="tpu_custom_call" | custom-call | flops 6442450944 | bytes 8388608 | tf_op jit(solution)/shard_map/expert_pieces/pallas_call | solution.py:411
  115.0 2.9 %collective-permute-done.26.refs_4_ = bf16[128,2048]{1,0:T(8,128)(2,1)S(1)} collective-permute-done((bf16[128,2048]{1,0:T(8,128)(2,1)S(1)}, bf16[128,2048]{1,0:T(8,128)(2,1)S(1)}, u32[]{:S(2)}, u32[]{:S(2)}) %collective-permute-start.26) | collective-permute-done | bytes 524320 | tf_op jit(solution)/shard_map/ppermute | solution.py:438
  118.5 1.5 collective-permute-start.36
  120.1 0.9 collective-permute-start.35
  121.0 1.8 collective-permute-done.30.refs_5_
  124.1 3.2 %collective-permute-done.36 = bf16[64,2048]{1,0:T(8,128)(2,1)S(1)} collective-permute-done((bf16[64,2048]{1,0:T(8,128)(2,1)S(1)}, bf16[64,2048]{1,0:T(8,128)(2,1)S(1)}, u32[]{:S(2)}, u32[]{:S(2)}) %collective-permute-start.36) | collective-permute-done | bytes 262176 | tf_op jit(solution)/shard_map/ppermute | solution.py:438
  127.3 1.3 collective-permute-done.35
  129.3 1.7 collective-permute-start.32
  131.0 9.1 %expert_pieces.3 = (bf16[4,128,2048]{2,1,0:T(8,128)(2,1)S(1)}, bf16[4,128,2048]{2,1,0:T(8,128)(2,1)S(1)}) custom-call(s32[3]{0:T(128)S(1)} %stage_weights.3.where_ref.me_ref, bf16[4,672,128]{2,1,0:T(8,128)(2,1)S(1)} %pad_maximum_fusion.near_ref.near_routes.fwd_near, bf16[4,672,128]{2,1,0:T(8,128)(2,1)S(1)} %collective-permute-done.4.far_ref.far_routes.fwd_far, ...), custom_call_target="tpu_custom_call" | custom-call | flops 6442450944 | bytes 8388608 | tf_op jit(solution)/shard_map/expert_pieces/pallas_call | solution.py:411
  140.1 2.9 %collective-permute-done.31.refs_0_ = bf16[128,2048]{1,0:T(8,128)(2,1)S(1)} collective-permute-done((bf16[128,2048]{1,0:T(8,128)(2,1)S(1)}, bf16[128,2048]{1,0:T(8,128)(2,1)S(1)}, u32[]{:S(2)}, u32[]{:S(2)}) %collective-permute-start.31) | collective-permute-done | bytes 524320 | tf_op jit(solution)/shard_map/ppermute | solution.py:438
  143.5 1.6 collective-permute-start.34
  145.1 0.9 collective-permute-start.33
  146.0 6.3 %collective-permute-done.34.refs_3_ = bf16[64,2048]{1,0:T(8,128)(2,1)S(1)} collective-permute-done((bf16[64,2048]{1,0:T(8,128)(2,1)S(1)}, bf16[64,2048]{1,0:T(8,128)(2,1)S(1)}, u32[]{:S(2)}, u32[]{:S(2)}) %collective-permute-start.34) | collective-permute-done | bytes 262176 | tf_op jit(solution)/shard_map/ppermute | solution.py:438
  152.3 1.2 collective-permute-done.33.refs_2_
  154.6 1.7 collective-permute-start.43
  156.4 1.0 sum_terms.2
  157.4 2.7 %collective-permute-start.41 = (bf16[128,512]{1,0:T(8,128)(2,1)S(1)}, bf16[128,512]{1,0:T(8,128)(2,1)S(1)}, u32[]{:S(2)}, u32[]{:S(2)}) collective-permute-start(bf16[128,512]{1,0:T(8,128)(2,1)S(1)} %get-tuple-element.122), channel_id=1, source_target_pairs={{0,1},{1,0},{2,3},{3,2},{4,5},{5,4},{6,7},{7,6},{8,9},{9,8},{10,11... | collective-permute-start | bytes 393224 | tf_op jit(solution)/shard_map/ppermute | solution.py:444
  160.1 4.8 %collective-permute-done.40.refs_1_ = bf16[128,512]{1,0:T(8,128)(2,1)S(1)} collective-permute-done((bf16[128,512]{1,0:T(8,128)(2,1)S(1)}, bf16[128,512]{1,0:T(8,128)(2,1)S(1)}, u32[]{:S(2)}, u32[]{:S(2)}) %collective-permute-start.40) | collective-permute-done | bytes 131104 | tf_op jit(solution)/shard_map/ppermute | solution.py:444
  165.2 2.1 %collective-permute-done.42.refs_0_ = bf16[128,2048]{1,0:T(8,128)(2,1)S(1)} collective-permute-done((bf16[128,2048]{1,0:T(8,128)(2,1)S(1)}, bf16[128,2048]{1,0:T(8,128)(2,1)S(1)}, u32[]{:S(2)}, u32[]{:S(2)}) %collective-permute-start.42) | collective-permute-done | bytes 524320 | tf_op jit(solution)/shard_map/ppermute | solution.py:438
  168.0 1.5 collective-permute-start.45
  169.5 0.9 collective-permute-start.44
  170.3 2.2 %collective-permute-start.39 = (bf16[128,512]{1,0:T(8,128)(2,1)S(1)}, bf16[128,512]{1,0:T(8,128)(2,1)S(1)}, u32[]{:S(2)}, u32[]{:S(2)}) collective-permute-start(bf16[128,512]{1,0:T(8,128)(2,1)S(1)} %get-tuple-element.120), channel_id=1, source_target_pairs={{0,3},{1,2},{2,1},{3,0},{4,7},{5,6},{6,5},{7,4},{8,11},{9,10},{10,... | collective-permute-start | bytes 393224 | tf_op jit(solution)/shard_map/ppermute | solution.py:444
  172.5 2.0 %collective-permute-done.45.refs_3_ = bf16[64,2048]{1,0:T(8,128)(2,1)S(1)} collective-permute-done((bf16[64,2048]{1,0:T(8,128)(2,1)S(1)}, bf16[64,2048]{1,0:T(8,128)(2,1)S(1)}, u32[]{:S(2)}, u32[]{:S(2)}) %collective-permute-start.45) | collective-permute-done | bytes 262176 | tf_op jit(solution)/shard_map/ppermute | solution.py:438
  174.5 1.3 collective-permute-done.44.refs_2_
  175.8 1.0 sum_terms.3
  176.8 2.2 %collective-permute-start.46 = (bf16[128,512]{1,0:T(8,128)(2,1)S(1)}, bf16[128,512]{1,0:T(8,128)(2,1)S(1)}, u32[]{:S(2)}, u32[]{:S(2)}) collective-permute-start(bf16[128,512]{1,0:T(8,128)(2,1)S(1)} %get-tuple-element.127), channel_id=1, source_target_pairs={{0,3},{1,2},{2,1},{3,0},{4,7},{5,6},{6,5},{7,4},{8,11},{9,10},{10,... | collective-permute-start | bytes 393224 | tf_op jit(solution)/shard_map/ppermute | solution.py:444
  179.0 2.2 %collective-permute-start.48 = (bf16[128,512]{1,0:T(8,128)(2,1)S(1)}, bf16[128,512]{1,0:T(8,128)(2,1)S(1)}, u32[]{:S(2)}, u32[]{:S(2)}) collective-permute-start(bf16[128,512]{1,0:T(8,128)(2,1)S(1)} %get-tuple-element.129), channel_id=1, source_target_pairs={{0,1},{1,0},{2,3},{3,2},{4,5},{5,4},{6,7},{7,6},{8,9},{9,8},{10,11... | collective-permute-start | bytes 393224 | tf_op jit(solution)/shard_map/ppermute | solution.py:444
  181.3 4.7 %core_grads.1 = (bf16[256,512]{1,0:T(8,128)(2,1)}, bf16[256,512]{1,0:T(8,128)(2,1)}, bf16[256,512]{1,0:T(8,128)(2,1)}) custom-call(s32[3]{0:T(128)S(1)} %stage_weights.3.where_ref.me_ref, bf16[3,256,512]{2,1,0:T(8,128)(2,1)S(1)} %copy-done.3, bf16[256,512]{1,0:T(8,128)(2,1)S(1)} %copy-done.9, f32[4,256]{1,0:T(4,128)S(1)} %bitcast.53, ...), custom_call_target="tpu_custom_call" | custom-call | tf_op jit(solution)/shard_map/core_grads/pallas_call | solution.py:268
  186.0 2.2 %collective-permute-done.47.refs_5_ = bf16[128,512]{1,0:T(8,128)(2,1)S(1)} collective-permute-done((bf16[128,512]{1,0:T(8,128)(2,1)S(1)}, bf16[128,512]{1,0:T(8,128)(2,1)S(1)}, u32[]{:S(2)}, u32[]{:S(2)}) %collective-permute-start.47) | collective-permute-done | bytes 131104 | tf_op jit(solution)/shard_map/ppermute | solution.py:444
  188.2 1.4 layer_out.1
  (107 shorter events, 12.3 us)
Async XLA Ops:
  0.6 10.9 %copy-start.8 = (bf16[256,512]{1,0:T(8,128)(2,1)S(1)}, bf16[256,512]{1,0:T(8,128)(2,1)}, u32[]{:S(2)}) copy-start(bf16[256,512]{1,0:T(8,128)(2,1)} %cot_ref.3) | copy-start | bytes 786436
  0.6 10.9 %copy-start.13 = (f32[256,4]{0,1:T(4,128)S(1)}, f32[256,4]{0,1:T(4,128)}, u32[]{:S(2)}) copy-start(f32[256,4]{0,1:T(4,128)} %param.18) | copy-start | bytes 12292
  0.7 10.9 %copy-start.14 = (f32[4,3,512]{2,0,1:T(4,128)S(1)}, f32[4,3,512]{2,0,1:T(4,128)}, u32[]{:S(2)}) copy-start(f32[4,3,512]{2,0,1:T(4,128)} %param.17) | copy-start | bytes 73732
  0.7 10.9 %copy-start.15 = (s32[256,8]{0,1:T(8,128)S(1)}, s32[256,8]{0,1:T(8,128)}, u32[]{:S(2)}) copy-start(s32[256,8]{0,1:T(8,128)} %param.22) | copy-start | bytes 24580
  0.7 10.9 %copy-start.16 = (f32[256,8]{0,1:T(8,128)S(1)}, f32[256,8]{0,1:T(8,128)}, u32[]{:S(2)}) copy-start(f32[256,8]{0,1:T(8,128)} %param.23) | copy-start | bytes 24580
  8.0 22.7 %copy-start.1 = (bf16[512,2048]{1,0:T(8,128)(2,1)S(1)}, bf16[512,2048]{1,0:T(8,128)(2,1)}, u32[]{:S(2)}) copy-start(bf16[512,2048]{1,0:T(8,128)(2,1)} %w_ref.1) | copy-start | bytes 6291460
  8.0 3.6 %collective-permute-start = (bf16[3,16,512]{2,1,0:T(8,128)(2,1)}, bf16[3,16,512]{2,1,0:T(8,128)(2,1)S(1)}, u32[]{:S(2)}, u32[]{:S(2)}) collective-permute-start(bf16[3,16,512]{2,1,0:T(8,128)(2,1)} %get-tuple-element.70), channel_id=1, source_target_pairs={{0,4},{4,8},{8,12},{12,16},{16,20},{20,24},{24,28},{1,5},{5,9},{9,... | collective-permute-start | bytes 147464 | tf_op jit(solution)/shard_map/ppermute | solution.py:610
  12.7 20.0 %copy-start.18 = (f32[512]{0:T(512)S(1)}, f32[512]{0:T(512)}, u32[]{:S(2)}) copy-start(f32[512]{0:T(512)} %param.19) | copy-start | bytes 6148
  16.5 11.4 %collective-permute-start.3 = (bf16[672,128]{1,0:T(8,128)(2,1)S(1)}, bf16[672,128]{1,0:T(8,128)(2,1)S(1)}, u32[]{:S(2)}, u32[]{:S(2)}) collective-permute-start(bf16[672,128]{1,0:T(8,128)(2,1)S(1)} %get-tuple-element.73), channel_id=1, source_target_pairs={{0,24},{4,28},{8,16},{12,20},{16,8},{20,12},{24,0},{28,4},{1,25},{... | collective-permute-start | bytes 516104 | tf_op jit(solution)/shard_map/ppermute | solution.py:438
  22.5 7.8 %collective-permute-start.2 = (bf16[672,128]{1,0:T(8,128)(2,1)S(1)}, bf16[672,128]{1,0:T(8,128)(2,1)S(1)}, u32[]{:S(2)}, u32[]{:S(2)}) collective-permute-start(bf16[672,128]{1,0:T(8,128)(2,1)S(1)} %get-tuple-element.73), channel_id=1, source_target_pairs={{0,16},{4,20},{8,24},{12,28},{16,0},{20,4},{24,8},{28,12},{1,17},{... | collective-permute-start | bytes 516104 | tf_op jit(solution)/shard_map/ppermute | solution.py:438
  23.1 7.3 %collective-permute-start.1 = (bf16[672,128]{1,0:T(8,128)(2,1)S(1)}, bf16[672,128]{1,0:T(8,128)(2,1)S(1)}, u32[]{:S(2)}, u32[]{:S(2)}) collective-permute-start(bf16[672,128]{1,0:T(8,128)(2,1)S(1)} %get-tuple-element.73), channel_id=1, source_target_pairs={{0,8},{4,12},{8,0},{12,4},{16,24},{20,28},{24,16},{28,20},{1,9},{5... | collective-permute-start | bytes 516104 | tf_op jit(solution)/shard_map/ppermute | solution.py:438
  30.5 2.2 %collective-permute-start.4 = (bf16[4,672,128]{2,1,0:T(8,128)(2,1)S(1)}, bf16[4,672,128]{2,1,0:T(8,128)(2,1)S(1)}, u32[]{:S(2)}, u32[]{:S(2)}) collective-permute-start(bf16[4,672,128]{2,1,0:T(8,128)(2,1)S(1)} %pad_maximum_fusion.near_ref.near_routes.fwd_near), channel_id=1, source_target_pairs={{0,4},{4,0},{8,12},{12,8},{16,20},{20,16},{24,28},{28,24},{1,5},{5... | collective-permute-start | bytes 2064392 | tf_op jit(solution)/shard_map/ppermute | solution.py:438
  30.6 2.1 %copy-start.3 = (bf16[3,256,512]{2,1,0:T(8,128)(2,1)S(1)}, bf16[3,256,512]{2,1,0:T(8,128)(2,1)}, u32[]{:S(2)}) copy-start(bf16[3,256,512]{2,1,0:T(8,128)(2,1)} %copy-done.2) | copy-start | bytes 2359300
  30.7 5.9 %copy-start.12 = (bf16[576,128]{1,0:T(8,128)(2,1)S(1)}, bf16[576,128]{1,0:T(8,128)(2,1)}, u32[]{:S(2)}) copy-start(bf16[576,128]{1,0:T(8,128)(2,1)} %copy-done.11) | copy-start | bytes 442372
  32.7 9.9 %copy-start.4 = (bf16[1,2048,512]{2,1,0:T(8,128)(2,1)S(1)}, bf16[1,2048,512]{2,1,0:T(8,128)(2,1)}, u32[]{:S(2)}) copy-start(bf16[1,2048,512]{2,1,0:T(8,128)(2,1)} %gate_ref.3) | copy-start | bytes 6291460
  32.7 9.9 %copy-start.5 = (bf16[1,2048,512]{2,1,0:T(8,128)(2,1)S(1)}, bf16[1,2048,512]{2,1,0:T(8,128)(2,1)}, u32[]{:S(2)}) copy-start(bf16[1,2048,512]{2,1,0:T(8,128)(2,1)} %up_ref.3) | copy-start | bytes 6291460
  36.6 27.7 %copy-start = (bf16[256,2048]{1,0:T(8,128)(2,1)S(1)}, bf16[256,2048]{1,0:T(8,128)(2,1)}, u32[]{:S(2)}) copy-start(bf16[256,2048]{1,0:T(8,128)(2,1)} %x_ref.3) | copy-start | bytes 3145732
  36.6 8.8 %collective-permute-start.8 = (bf16[1,576,128]{2,1,0:T(8,128)(2,1)S(1)}, bf16[1,576,128]{2,1,0:T(8,128)(2,1)S(1)}, u32[]{:S(2)}, u32[]{:S(2)}) collective-permute-start(bf16[1,576,128]{2,1,0:T(8,128)(2,1)S(1)} %bitcast.49), channel_id=1, source_target_pairs={{0,8},{4,12},{8,0},{12,4},{16,24},{20,28},{24,16},{28,20},{1,9},{5... | collective-permute-start | bytes 442376 | tf_op jit(solution)/shard_map/ppermute | solution.py:438
  38.3 11.1 %collective-permute-start.7 = (bf16[64,2048]{1,0:T(8,128)(2,1)S(1)}, bf16[64,2048]{1,0:T(8,128)(2,1)S(1)}, u32[]{:S(2)}, u32[]{:S(2)}) collective-permute-start(bf16[64,2048]{1,0:T(8,128)(2,1)S(1)} %get-tuple-element.74), channel_id=1, source_target_pairs={{0,3},{1,2},{2,1},{3,0},{4,7},{5,6},{6,5},{7,4},{8,11},{9,10},{10,... | collective-permute-start | bytes 786440 | tf_op jit(solution)/shard_map/ppermute | solution.py:444
  41.9 22.4 %collective-permute-start.6 = (bf16[64,2048]{1,0:T(8,128)(2,1)S(1)}, bf16[64,2048]{1,0:T(8,128)(2,1)S(1)}, u32[]{:S(2)}, u32[]{:S(2)}) collective-permute-start(bf16[64,2048]{1,0:T(8,128)(2,1)S(1)} %get-tuple-element.75), channel_id=1, source_target_pairs={{0,2},{1,3},{2,0},{3,1},{4,6},{5,7},{6,4},{7,5},{8,10},{9,11},{10,... | collective-permute-start | bytes 786440 | tf_op jit(solution)/shard_map/ppermute | solution.py:444
  41.9 22.4 %collective-permute-start.5 = (bf16[64,2048]{1,0:T(8,128)(2,1)S(1)}, bf16[64,2048]{1,0:T(8,128)(2,1)S(1)}, u32[]{:S(2)}, u32[]{:S(2)}) collective-permute-start(bf16[64,2048]{1,0:T(8,128)(2,1)S(1)} %get-tuple-element.76), channel_id=1, source_target_pairs={{0,1},{1,0},{2,3},{3,2},{4,5},{5,4},{6,7},{7,6},{8,9},{9,8},{10,11... | collective-permute-start | bytes 786440 | tf_op jit(solution)/shard_map/ppermute | solution.py:444
  44.2 20.0 %copy-start.17 = (f32[2048]{0:T(1024)S(1)}, f32[2048]{0:T(1024)}, u32[]{:S(2)}) copy-start(f32[2048]{0:T(1024)} %param.21) | copy-start | bytes 24580
  65.1 8.2 %collective-permute-start.12 = (bf16[2,576,128]{2,1,0:T(8,128)(2,1)S(1)}, bf16[2,576,128]{2,1,0:T(8,128)(2,1)S(1)}, u32[]{:S(2)}, u32[]{:S(2)}) collective-permute-start(bf16[2,576,128]{2,1,0:T(8,128)(2,1)S(1)} %pad_maximum_fusion.5), channel_id=1, source_target_pairs={{0,16},{4,20},{8,24},{12,28},{16,0},{20,4},{24,8},{28,12},{1,17},{... | collective-permute-start | bytes 884744 | tf_op jit(solution)/shard_map/ppermute | solution.py:438
  66.1 8.2 %collective-permute-start.11 = (bf16[32,2048]{1,0:T(8,128)(2,1)S(1)}, bf16[32,2048]{1,0:T(8,128)(2,1)S(1)}, u32[]{:S(2)}, u32[]{:S(2)}) collective-permute-start(bf16[32,2048]{1,0:T(8,128)(2,1)S(1)} %get-tuple-element.89.refs_0_), channel_id=1, source_target_pairs={{0,3},{1,2},{2,1},{3,0},{4,7},{5,6},{6,5},{7,4},{8,11},{9,10},{10,... | collective-permute-start | bytes 393224 | tf_op jit(solution)/shard_map/ppermute | solution.py:444
  68.6 10.0 %collective-permute-start.10 = (bf16[32,2048]{1,0:T(8,128)(2,1)S(1)}, bf16[32,2048]{1,0:T(8,128)(2,1)S(1)}, u32[]{:S(2)}, u32[]{:S(2)}) collective-permute-start(bf16[32,2048]{1,0:T(8,128)(2,1)S(1)} %get-tuple-element.89.refs_0_), channel_id=1, source_target_pairs={{0,2},{1,3},{2,0},{3,1},{4,6},{5,7},{6,4},{7,5},{8,10},{9,11},{10,... | collective-permute-start | bytes 393224 | tf_op jit(solution)/shard_map/ppermute | solution.py:444
  68.6 10.0 %collective-permute-start.9 = (bf16[32,2048]{1,0:T(8,128)(2,1)S(1)}, bf16[32,2048]{1,0:T(8,128)(2,1)S(1)}, u32[]{:S(2)}, u32[]{:S(2)}) collective-permute-start(bf16[32,2048]{1,0:T(8,128)(2,1)S(1)} %get-tuple-element.89.refs_0_), channel_id=1, source_target_pairs={{0,1},{1,0},{2,3},{3,2},{4,5},{5,4},{6,7},{7,6},{8,9},{9,8},{10,11... | collective-permute-start | bytes 393224 | tf_op jit(solution)/shard_map/ppermute | solution.py:444
  73.3 32.5 %copy-start.7 = (bf16[1,512,2048]{2,1,0:T(8,128)(2,1)S(1)}, bf16[1,512,2048]{2,1,0:T(8,128)(2,1)}, u32[]{:S(2)}) copy-start(bf16[1,512,2048]{2,1,0:T(8,128)(2,1)} %down_ref.3) | copy-start | bytes 6291460
  79.2 15.0 %collective-permute-start.14 = (bf16[128,2048]{1,0:T(8,128)(2,1)S(1)}, bf16[128,2048]{1,0:T(8,128)(2,1)S(1)}, u32[]{:S(2)}, u32[]{:S(2)}) collective-permute-start(bf16[128,2048]{1,0:T(8,128)(2,1)S(1)} %join_rows.2.refs_0_), channel_id=1, source_target_pairs={{0,16},{4,20},{8,24},{12,28},{16,0},{20,4},{24,8},{28,12},{1,17},{... | collective-permute-start | bytes 1572872 | tf_op jit(solution)/shard_map/ppermute | solution.py:438
  80.4 13.8 %collective-permute-start.13 = (bf16[128,2048]{1,0:T(8,128)(2,1)S(1)}, bf16[128,2048]{1,0:T(8,128)(2,1)S(1)}, u32[]{:S(2)}, u32[]{:S(2)}) collective-permute-start(bf16[128,2048]{1,0:T(8,128)(2,1)S(1)} %join_rows.2.refs_0_), channel_id=1, source_target_pairs={{0,8},{4,12},{8,0},{12,4},{16,24},{20,28},{24,16},{28,20},{1,9},{5... | collective-permute-start | bytes 1572872 | tf_op jit(solution)/shard_map/ppermute | solution.py:438
  80.8 8.2 %collective-permute-start.17 = (bf16[32,2048]{1,0:T(8,128)(2,1)S(1)}, bf16[32,2048]{1,0:T(8,128)(2,1)S(1)}, u32[]{:S(2)}, u32[]{:S(2)}) collective-permute-start(bf16[32,2048]{1,0:T(8,128)(2,1)S(1)} %get-tuple-element.93.refs_0_), channel_id=1, source_target_pairs={{0,3},{1,2},{2,1},{3,0},{4,7},{5,6},{6,5},{7,4},{8,11},{9,10},{10,... | collective-permute-start | bytes 393224 | tf_op jit(solution)/shard_map/ppermute | solution.py:444
  82.6 11.0 %collective-permute-start.16 = (bf16[32,2048]{1,0:T(8,128)(2,1)S(1)}, bf16[32,2048]{1,0:T(8,128)(2,1)S(1)}, u32[]{:S(2)}, u32[]{:S(2)}) collective-permute-start(bf16[32,2048]{1,0:T(8,128)(2,1)S(1)} %get-tuple-element.93.refs_0_), channel_id=1, source_target_pairs={{0,2},{1,3},{2,0},{3,1},{4,6},{5,7},{6,4},{7,5},{8,10},{9,11},{10,... | collective-permute-start | bytes 393224 | tf_op jit(solution)/shard_map/ppermute | solution.py:444
  82.6 11.0 %collective-permute-start.15 = (bf16[32,2048]{1,0:T(8,128)(2,1)S(1)}, bf16[32,2048]{1,0:T(8,128)(2,1)S(1)}, u32[]{:S(2)}, u32[]{:S(2)}) collective-permute-start(bf16[32,2048]{1,0:T(8,128)(2,1)S(1)} %get-tuple-element.93.refs_0_), channel_id=1, source_target_pairs={{0,1},{1,0},{2,3},{3,2},{4,5},{5,4},{6,7},{7,6},{8,9},{9,8},{10,11... | collective-permute-start | bytes 393224 | tf_op jit(solution)/shard_map/ppermute | solution.py:444
  94.2 7.6 %collective-permute-start.21 = (bf16[64,2048]{1,0:T(8,128)(2,1)S(1)}, bf16[64,2048]{1,0:T(8,128)(2,1)S(1)}, u32[]{:S(2)}, u32[]{:S(2)}) collective-permute-start(bf16[64,2048]{1,0:T(8,128)(2,1)S(1)} %slice.96), channel_id=1, source_target_pairs={{0,16},{4,20},{8,24},{12,28},{16,0},{20,4},{24,8},{28,12},{1,17},{... | collective-permute-start | bytes 786440 | tf_op jit(solution)/shard_map/ppermute | solution.py:438
  96.0 7.3 %collective-permute-start.22 = (bf16[64,2048]{1,0:T(8,128)(2,1)S(1)}, bf16[64,2048]{1,0:T(8,128)(2,1)S(1)}, u32[]{:S(2)}, u32[]{:S(2)}) collective-permute-start(bf16[64,2048]{1,0:T(8,128)(2,1)S(1)} %slice.97), channel_id=1, source_target_pairs={{0,8},{4,12},{8,0},{12,4},{16,24},{20,28},{24,16},{28,20},{1,9},{5... | collective-permute-start | bytes 786440 | tf_op jit(solution)/shard_map/ppermute | solution.py:438
  96.8 7.5 %collective-permute-start.19 = (bf16[128,2048]{1,0:T(8,128)(2,1)S(1)}, bf16[128,2048]{1,0:T(8,128)(2,1)S(1)}, u32[]{:S(2)}, u32[]{:S(2)}) collective-permute-start(bf16[128,2048]{1,0:T(8,128)(2,1)S(1)} %collective-permute-done.13.refs_2_), channel_id=1, source_target_pairs={{0,4},{4,0},{8,12},{12,8},{16,20},{20,16},{24,28},{28,24},{1,5},{5... | collective-permute-start | bytes 1572872 | tf_op jit(solution)/shard_map/ppermute | solution.py:438
  96.8 9.0 %collective-permute-start.20 = (bf16[128,2048]{1,0:T(8,128)(2,1)S(1)}, bf16[128,2048]{1,0:T(8,128)(2,1)S(1)}, u32[]{:S(2)}, u32[]{:S(2)}) collective-permute-start(bf16[128,2048]{1,0:T(8,128)(2,1)S(1)} %collective-permute-done.14.refs_4_), channel_id=1, source_target_pairs={{0,4},{4,0},{8,12},{12,8},{16,20},{20,16},{24,28},{28,24},{1,5},{5... | collective-permute-start | bytes 1572872 | tf_op jit(solution)/shard_map/ppermute | solution.py:438
  97.3 6.7 %collective-permute-start.18 = (bf16[128,2048]{1,0:T(8,128)(2,1)S(1)}, bf16[128,2048]{1,0:T(8,128)(2,1)S(1)}, u32[]{:S(2)}, u32[]{:S(2)}) collective-permute-start(bf16[128,2048]{1,0:T(8,128)(2,1)S(1)} %join_rows.2.refs_0_), channel_id=1, source_target_pairs={{0,4},{4,0},{8,12},{12,8},{16,20},{20,16},{24,28},{28,24},{1,5},{5... | collective-permute-start | bytes 1572872 | tf_op jit(solution)/shard_map/ppermute | solution.py:438
  103.4 2.5 %collective-permute-start.23 = (bf16[128,2048]{1,0:T(8,128)(2,1)S(1)}, bf16[128,2048]{1,0:T(8,128)(2,1)S(1)}, u32[]{:S(2)}, u32[]{:S(2)}) collective-permute-start(bf16[128,2048]{1,0:T(8,128)(2,1)S(1)} %constant_dynamic-update-slice_fusion.2.refs_6_), channel_id=1, source_target_pairs={{0,4},{4,0},{8,12},{12,8},{16,20},{20,16},{24,28},{28,24},{1,5},{5... | collective-permute-start | bytes 1572872 | tf_op jit(solution)/shard_map/ppermute | solution.py:438
  103.4 11.5 %collective-permute-start.27 = (bf16[4,576,128]{2,1,0:T(8,128)(2,1)S(1)}, bf16[4,576,128]{2,1,0:T(8,128)(2,1)S(1)}, u32[]{:S(2)}, u32[]{:S(2)}) collective-permute-start(bf16[4,576,128]{2,1,0:T(8,128)(2,1)S(1)} %constant_dynamic-update-slice_fusion.bwd_near), channel_id=1, source_target_pairs={{0,4},{4,0},{8,12},{12,8},{16,20},{20,16},{24,28},{28,24},{1,5},{5... | collective-permute-start | bytes 1769480 | tf_op jit(solution)/shard_map/ppermute | solution.py:438
  103.9 13.9 %collective-permute-start.26 = (bf16[128,2048]{1,0:T(8,128)(2,1)S(1)}, bf16[128,2048]{1,0:T(8,128)(2,1)S(1)}, u32[]{:S(2)}, u32[]{:S(2)}) collective-permute-start(bf16[128,2048]{1,0:T(8,128)(2,1)S(1)} %join_rows.3.refs_0_), channel_id=1, source_target_pairs={{0,16},{4,20},{8,24},{12,28},{16,0},{20,4},{24,8},{28,12},{1,17},{... | collective-permute-start | bytes 1572872 | tf_op jit(solution)/shard_map/ppermute | solution.py:438
  104.3 13.6 %collective-permute-start.25 = (bf16[128,2048]{1,0:T(8,128)(2,1)S(1)}, bf16[128,2048]{1,0:T(8,128)(2,1)S(1)}, u32[]{:S(2)}, u32[]{:S(2)}) collective-permute-start(bf16[128,2048]{1,0:T(8,128)(2,1)S(1)} %join_rows.3.refs_0_), channel_id=1, source_target_pairs={{0,8},{4,12},{8,0},{12,4},{16,24},{20,28},{24,16},{28,20},{1,9},{5... | collective-permute-start | bytes 1572872 | tf_op jit(solution)/shard_map/ppermute | solution.py:438
  105.8 12.1 %collective-permute-start.24 = (bf16[128,2048]{1,0:T(8,128)(2,1)S(1)}, bf16[128,2048]{1,0:T(8,128)(2,1)S(1)}, u32[]{:S(2)}, u32[]{:S(2)}) collective-permute-start(bf16[128,2048]{1,0:T(8,128)(2,1)S(1)} %join_rows.3.refs_0_), channel_id=1, source_target_pairs={{0,4},{4,0},{8,12},{12,8},{16,20},{20,16},{24,28},{28,24},{1,5},{5... | collective-permute-start | bytes 1572872 | tf_op jit(solution)/shard_map/ppermute | solution.py:438
  117.9 5.7 %collective-permute-start.28 = (bf16[4,128,2048]{2,1,0:T(8,128)(2,1)S(1)}, bf16[4,128,2048]{2,1,0:T(8,128)(2,1)S(1)}, u32[]{:S(2)}, u32[]{:S(2)}) collective-permute-start(bf16[4,128,2048]{2,1,0:T(8,128)(2,1)S(1)} %get-tuple-element.100), channel_id=1, source_target_pairs={{0,4},{4,0},{8,12},{12,8},{16,20},{20,16},{24,28},{28,24},{1,5},{5... | collective-permute-start | bytes 6291464 | tf_op jit(solution)/shard_map/ppermute | solution.py:438
  117.9 4.9 %collective-permute-start.30 = (bf16[128,2048]{1,0:T(8,128)(2,1)S(1)}, bf16[128,2048]{1,0:T(8,128)(2,1)S(1)}, u32[]{:S(2)}, u32[]{:S(2)}) collective-permute-start(bf16[128,2048]{1,0:T(8,128)(2,1)S(1)} %collective-permute-done.26.refs_4_), channel_id=1, source_target_pairs={{0,4},{4,0},{8,12},{12,8},{16,20},{20,16},{24,28},{28,24},{1,5},{5... | collective-permute-start | bytes 1572872 | tf_op jit(solution)/shard_map/ppermute | solution.py:438
  118.4 5.1 %collective-permute-start.29 = (bf16[128,2048]{1,0:T(8,128)(2,1)S(1)}, bf16[128,2048]{1,0:T(8,128)(2,1)S(1)}, u32[]{:S(2)}, u32[]{:S(2)}) collective-permute-start(bf16[128,2048]{1,0:T(8,128)(2,1)S(1)} %collective-permute-done.25.refs_2_), channel_id=1, source_target_pairs={{0,4},{4,0},{8,12},{12,8},{16,20},{20,16},{24,28},{28,24},{1,5},{5... | collective-permute-start | bytes 1572872 | tf_op jit(solution)/shard_map/ppermute | solution.py:438
  118.5 8.8 %collective-permute-start.36 = (bf16[64,2048]{1,0:T(8,128)(2,1)S(1)}, bf16[64,2048]{1,0:T(8,128)(2,1)S(1)}, u32[]{:S(2)}, u32[]{:S(2)}) collective-permute-start(bf16[64,2048]{1,0:T(8,128)(2,1)S(1)} %slice.131), channel_id=1, source_target_pairs={{0,8},{4,12},{8,0},{12,4},{16,24},{20,28},{24,16},{28,20},{1,9},{5... | collective-permute-start | bytes 786440 | tf_op jit(solution)/shard_map/ppermute | solution.py:438
  120.1 8.5 %collective-permute-start.35 = (bf16[64,2048]{1,0:T(8,128)(2,1)S(1)}, bf16[64,2048]{1,0:T(8,128)(2,1)S(1)}, u32[]{:S(2)}, u32[]{:S(2)}) collective-permute-start(bf16[64,2048]{1,0:T(8,128)(2,1)S(1)} %slice.130), channel_id=1, source_target_pairs={{0,16},{4,20},{8,24},{12,28},{16,0},{20,4},{24,8},{28,12},{1,17},{... | collective-permute-start | bytes 786440 | tf_op jit(solution)/shard_map/ppermute | solution.py:438
  128.6 2.3 %collective-permute-start.37 = (bf16[128,2048]{1,0:T(8,128)(2,1)S(1)}, bf16[128,2048]{1,0:T(8,128)(2,1)S(1)}, u32[]{:S(2)}, u32[]{:S(2)}) collective-permute-start(bf16[128,2048]{1,0:T(8,128)(2,1)S(1)} %constant_dynamic-update-slice_fusion.4.refs_6_), channel_id=1, source_target_pairs={{0,4},{4,0},{8,12},{12,8},{16,20},{20,16},{24,28},{28,24},{1,5},{5... | collective-permute-start | bytes 1572872 | tf_op jit(solution)/shard_map/ppermute | solution.py:438
  128.7 14.3 %collective-permute-start.31 = (bf16[128,2048]{1,0:T(8,128)(2,1)S(1)}, bf16[128,2048]{1,0:T(8,128)(2,1)S(1)}, u32[]{:S(2)}, u32[]{:S(2)}) collective-permute-start(bf16[128,2048]{1,0:T(8,128)(2,1)S(1)} %pad_maximum_fusion.1), channel_id=1, source_target_pairs={{0,8},{4,12},{8,0},{12,4},{16,24},{20,28},{24,16},{28,20},{1,9},{5... | collective-permute-start | bytes 1572872 | tf_op jit(solution)/shard_map/ppermute | solution.py:438
  129.3 14.0 %collective-permute-start.32 = (bf16[128,2048]{1,0:T(8,128)(2,1)S(1)}, bf16[128,2048]{1,0:T(8,128)(2,1)S(1)}, u32[]{:S(2)}, u32[]{:S(2)}) collective-permute-start(bf16[128,2048]{1,0:T(8,128)(2,1)S(1)} %pad_maximum_fusion.2), channel_id=1, source_target_pairs={{0,16},{4,20},{8,24},{12,28},{16,0},{20,4},{24,8},{28,12},{1,17},{... | collective-permute-start | bytes 1572872 | tf_op jit(solution)/shard_map/ppermute | solution.py:438
  143.3 10.3 %collective-permute-start.38 = (bf16[4,128,2048]{2,1,0:T(8,128)(2,1)S(1)}, bf16[4,128,2048]{2,1,0:T(8,128)(2,1)S(1)}, u32[]{:S(2)}, u32[]{:S(2)}) collective-permute-start(bf16[4,128,2048]{2,1,0:T(8,128)(2,1)S(1)} %get-tuple-element.114), channel_id=1, source_target_pairs={{0,4},{4,0},{8,12},{12,8},{16,20},{20,16},{24,28},{28,24},{1,5},{5... | collective-permute-start | bytes 6291464 | tf_op jit(solution)/shard_map/ppermute | solution.py:438
  143.5 8.8 %collective-permute-start.34 = (bf16[64,2048]{1,0:T(8,128)(2,1)S(1)}, bf16[64,2048]{1,0:T(8,128)(2,1)S(1)}, u32[]{:S(2)}, u32[]{:S(2)}) collective-permute-start(bf16[64,2048]{1,0:T(8,128)(2,1)S(1)} %get-tuple-element.140), channel_id=1, source_target_pairs={{0,8},{4,12},{8,0},{12,4},{16,24},{20,28},{24,16},{28,20},{1,9},{5... | collective-permute-start | bytes 786440 | tf_op jit(solution)/shard_map/ppermute | solution.py:438
  145.1 8.4 %collective-permute-start.33 = (bf16[64,2048]{1,0:T(8,128)(2,1)S(1)}, bf16[64,2048]{1,0:T(8,128)(2,1)S(1)}, u32[]{:S(2)}, u32[]{:S(2)}) collective-permute-start(bf16[64,2048]{1,0:T(8,128)(2,1)S(1)} %get-tuple-element.141), channel_id=1, source_target_pairs={{0,16},{4,20},{8,24},{12,28},{16,0},{20,4},{24,8},{28,12},{1,17},{... | collective-permute-start | bytes 786440 | tf_op jit(solution)/shard_map/ppermute | solution.py:438
  154.0 13.3 %collective-permute-start.42 = (bf16[128,2048]{1,0:T(8,128)(2,1)S(1)}, bf16[128,2048]{1,0:T(8,128)(2,1)S(1)}, u32[]{:S(2)}, u32[]{:S(2)}) collective-permute-start(bf16[128,2048]{1,0:T(8,128)(2,1)S(1)} %pad_maximum_fusion.3), channel_id=1, source_target_pairs={{0,8},{4,12},{8,0},{12,4},{16,24},{20,28},{24,16},{28,20},{1,9},{5... | collective-permute-start | bytes 1572872 | tf_op jit(solution)/shard_map/ppermute | solution.py:438
  154.6 13.1 %collective-permute-start.43 = (bf16[128,2048]{1,0:T(8,128)(2,1)S(1)}, bf16[128,2048]{1,0:T(8,128)(2,1)S(1)}, u32[]{:S(2)}, u32[]{:S(2)}) collective-permute-start(bf16[128,2048]{1,0:T(8,128)(2,1)S(1)} %pad_maximum_fusion.4), channel_id=1, source_target_pairs={{0,16},{4,20},{8,24},{12,28},{16,0},{20,4},{24,8},{28,12},{1,17},{... | collective-permute-start | bytes 1572872 | tf_op jit(solution)/shard_map/ppermute | solution.py:438
  157.3 7.6 %collective-permute-start.40 = (bf16[128,512]{1,0:T(8,128)(2,1)S(1)}, bf16[128,512]{1,0:T(8,128)(2,1)S(1)}, u32[]{:S(2)}, u32[]{:S(2)}) collective-permute-start(bf16[128,512]{1,0:T(8,128)(2,1)S(1)} %get-tuple-element.121), channel_id=1, source_target_pairs={{0,2},{1,3},{2,0},{3,1},{4,6},{5,7},{6,4},{7,5},{8,10},{9,11},{10,... | collective-permute-start | bytes 393224 | tf_op jit(solution)/shard_map/ppermute | solution.py:444
  157.4 7.8 %collective-permute-start.41 = (bf16[128,512]{1,0:T(8,128)(2,1)S(1)}, bf16[128,512]{1,0:T(8,128)(2,1)S(1)}, u32[]{:S(2)}, u32[]{:S(2)}) collective-permute-start(bf16[128,512]{1,0:T(8,128)(2,1)S(1)} %get-tuple-element.122), channel_id=1, source_target_pairs={{0,1},{1,0},{2,3},{3,2},{4,5},{5,4},{6,7},{7,6},{8,9},{9,8},{10,11... | collective-permute-start | bytes 393224 | tf_op jit(solution)/shard_map/ppermute | solution.py:444
  168.0 6.6 %collective-permute-start.45 = (bf16[64,2048]{1,0:T(8,128)(2,1)S(1)}, bf16[64,2048]{1,0:T(8,128)(2,1)S(1)}, u32[]{:S(2)}, u32[]{:S(2)}) collective-permute-start(bf16[64,2048]{1,0:T(8,128)(2,1)S(1)} %get-tuple-element.134), channel_id=1, source_target_pairs={{0,8},{4,12},{8,0},{12,4},{16,24},{20,28},{24,16},{28,20},{1,9},{5... | collective-permute-start | bytes 786440 | tf_op jit(solution)/shard_map/ppermute | solution.py:438
  169.5 6.4 %collective-permute-start.44 = (bf16[64,2048]{1,0:T(8,128)(2,1)S(1)}, bf16[64,2048]{1,0:T(8,128)(2,1)S(1)}, u32[]{:S(2)}, u32[]{:S(2)}) collective-permute-start(bf16[64,2048]{1,0:T(8,128)(2,1)S(1)} %get-tuple-element.135), channel_id=1, source_target_pairs={{0,16},{4,20},{8,24},{12,28},{16,0},{20,4},{24,8},{28,12},{1,17},{... | collective-permute-start | bytes 786440 | tf_op jit(solution)/shard_map/ppermute | solution.py:438
  170.3 15.6 %collective-permute-start.39 = (bf16[128,512]{1,0:T(8,128)(2,1)S(1)}, bf16[128,512]{1,0:T(8,128)(2,1)S(1)}, u32[]{:S(2)}, u32[]{:S(2)}) collective-permute-start(bf16[128,512]{1,0:T(8,128)(2,1)S(1)} %get-tuple-element.120), channel_id=1, source_target_pairs={{0,3},{1,2},{2,1},{3,0},{4,7},{5,6},{6,5},{7,4},{8,11},{9,10},{10,... | collective-permute-start | bytes 393224 | tf_op jit(solution)/shard_map/ppermute | solution.py:444
  175.8 5.4 %copy-start.9 = (bf16[256,512]{1,0:T(8,128)(2,1)S(1)}, bf16[256,512]{1,0:T(8,128)(2,1)}, u32[]{:S(2)}) copy-start(bf16[256,512]{1,0:T(8,128)(2,1)} %cot_ref.3) | copy-start | bytes 786436
  176.8 9.2 %collective-permute-start.46 = (bf16[128,512]{1,0:T(8,128)(2,1)S(1)}, bf16[128,512]{1,0:T(8,128)(2,1)S(1)}, u32[]{:S(2)}, u32[]{:S(2)}) collective-permute-start(bf16[128,512]{1,0:T(8,128)(2,1)S(1)} %get-tuple-element.127), channel_id=1, source_target_pairs={{0,3},{1,2},{2,1},{3,0},{4,7},{5,6},{6,5},{7,4},{8,11},{9,10},{10,... | collective-permute-start | bytes 393224 | tf_op jit(solution)/shard_map/ppermute | solution.py:444
  179.0 9.1 %collective-permute-start.47 = (bf16[128,512]{1,0:T(8,128)(2,1)S(1)}, bf16[128,512]{1,0:T(8,128)(2,1)S(1)}, u32[]{:S(2)}, u32[]{:S(2)}) collective-permute-start(bf16[128,512]{1,0:T(8,128)(2,1)S(1)} %get-tuple-element.128), channel_id=1, source_target_pairs={{0,2},{1,3},{2,0},{3,1},{4,6},{5,7},{6,4},{7,5},{8,10},{9,11},{10,... | collective-permute-start | bytes 393224 | tf_op jit(solution)/shard_map/ppermute | solution.py:444
  179.0 9.1 %collective-permute-start.48 = (bf16[128,512]{1,0:T(8,128)(2,1)S(1)}, bf16[128,512]{1,0:T(8,128)(2,1)S(1)}, u32[]{:S(2)}, u32[]{:S(2)}) collective-permute-start(bf16[128,512]{1,0:T(8,128)(2,1)S(1)} %get-tuple-element.129), channel_id=1, source_target_pairs={{0,1},{1,0},{2,3},{3,2},{4,5},{5,4},{6,7},{7,6},{8,9},{9,8},{10,11... | collective-permute-start | bytes 393224 | tf_op jit(solution)/shard_map/ppermute | solution.py:444
  (4 other events, 4.3 us)

commit v16 on v14

--- a/solution.py
+++ b/solution.py
@@ -78,7 +78,7 @@
             pltpu.VMEM((kinds, width, chans), BF),
             pltpu.VMEM((rows, width), BF),
             pltpu.SemaphoreType.DMA,
-            pltpu.SemaphoreType.DMA((kinds, 4)),
+            pltpu.SemaphoreType.DMA((kinds, 1)),
         ],
         compiler_params=params(60),
         name="qkv_projection",

time: 187 us -> 186 us (level)
  no operation moved by 1% of the time
where the time goes in v16:
time: 186 us
  waiting for transfers between devices  77 us (41%)
  starting transfers between devices  58.6 us (32%)
  Pallas kernels  43.3 us (23%)
  local copies, waits for them, and re-layouts  4.58 us (2%)
    ppermute x33, waiting for transfers between devices, swap(): lax.ppermute(value, 'ctx', [(at, at ^ mask) for at in range(lax.axis_size...  38.9 us
    ppermute x15, waiting for transfers between devices, send_heads(): lax.ppermute(parts[mask], 'head', [(at, at ^ mask) for at in range(count)])  37 us
    ppermute x33, starting transfers between devices, swap(): lax.ppermute(value, 'ctx', [(at, at ^ mask) for at in range(lax.axis_size...  29.9 us
    ppermute x15, starting transfers between devices, send_heads(): lax.ppermute(parts[mask], 'head', [(at, at ^ mask) for at in range(count)])  26.2 us
    pallas_call x2, Pallas kernels, expert_pieces(): pl.pallas_call(functools.partial(expert_kernel, tuple(masks), chunk, expe...  18.3 us
    pallas_call x1, Pallas kernels, project(): pl.pallas_call(qkv_kernel, in_specs=[hbm, vmem, hbm], out_specs=[vmem, vm...  6.71 us
    pallas_call x1, Pallas kernels, core_grads(): pl.pallas_call(grad_kernel, in_specs=[pl.BlockSpec(memory_space=pltpu.SME...  4.71 us
    unnamed x41, local copies, waits for them, and re-layouts  4.43 us
  transfers between devices with their start and end apart: 49, of which 29 were waited for; matrix products, arithmetic and copies ran while one was open for 1% of the time, Pallas kernels for 15%

profile of v16, /device:TPU:0, one launch (start us, length us, event | category | flops | bytes accessed | tf_op | source)
XLA Modules:
  0.0 186.2 jit_solution(11864256978513026731)
XLA Ops:
  0.7 6.7 %qkv_projection.1 = (bf16[3,256,512]{2,1,0:T(8,128)(2,1)}, bf16[3,16,512]{2,1,0:T(8,128)(2,1)}) custom-call(bf16[256,2048]{1,0:T(8,128)(2,1)} %x_ref.3, f32[1,2048]{1,0:T(1,128)} %bitcast.63, bf16[3,2048,512]{2,1,0:T(8,128)(2,1)} %bitcast.59), custom_call_target="tpu_custom_call" | custom-call | tf_op jit(solution)/shard_map/qkv_projection/pallas_call | solution.py:68
  7.4 2.5 %collective-permute-start = (bf16[3,16,512]{2,1,0:T(8,128)(2,1)}, bf16[3,16,512]{2,1,0:T(8,128)(2,1)S(1)}, u32[]{:S(2)}, u32[]{:S(2)}) collective-permute-start(bf16[3,16,512]{2,1,0:T(8,128)(2,1)} %get-tuple-element.70), channel_id=1, source_target_pairs={{0,4},{4,8},{8,12},{12,16},{16,20},{20,24},{24,28},{1,5},{5,9},{9,... | collective-permute-start | bytes 147464 | tf_op jit(solution)/shard_map/ppermute | solution.py:610
  9.9 1.1 collective-permute-done.rim_ref
  11.0 1.1 copy-done.10
  12.1 2.2 %conv_states.1 = (bf16[3,256,512]{2,1,0:T(8,128)(2,1)S(1)}, bf16[672,128]{1,0:T(8,128)(2,1)S(1)}, bf16[576,128]{1,0:T(8,128)(2,1)S(1)}) custom-call(bf16[3,256,512]{2,1,0:T(8,128)(2,1)S(1)} %copy-done.10, bf16[3,16,512]{2,1,0:T(8,128)(2,1)S(1)} %collective-permute-done.rim_ref, f32[3,4,512]{2,1,0:T(4,128)S(1)} %bitcast.54, f32[4,256]{1,0:T(4,128)S(1)} %bitcast.51, ...), custom_call_target="tpu_custom_call" | custom-call | tf_op jit(solution)/shard_map/conv_states/pallas_call | solution.py:161
  14.3 0.9 copy-done.2
  15.9 6.1 %collective-permute-start.3 = (bf16[672,128]{1,0:T(8,128)(2,1)S(1)}, bf16[672,128]{1,0:T(8,128)(2,1)S(1)}, u32[]{:S(2)}, u32[]{:S(2)}) collective-permute-start(bf16[672,128]{1,0:T(8,128)(2,1)S(1)} %get-tuple-element.73), channel_id=1, source_target_pairs={{0,24},{4,28},{8,16},{12,20},{16,8},{20,12},{24,0},{28,4},{1,25},{... | collective-permute-start | bytes 516104 | tf_op jit(solution)/shard_map/ppermute | solution.py:438
  22.5 0.9 collective-permute-start.1
  23.4 3.9 %collective-permute-done.3 = bf16[672,128]{1,0:T(8,128)(2,1)S(1)} collective-permute-done((bf16[672,128]{1,0:T(8,128)(2,1)S(1)}, bf16[672,128]{1,0:T(8,128)(2,1)S(1)}, u32[]{:S(2)}, u32[]{:S(2)}) %collective-permute-start.3) | collective-permute-done | bytes 172064 | tf_op jit(solution)/shard_map/ppermute | solution.py:438
  27.3 2.5 %collective-permute-done.2 = bf16[672,128]{1,0:T(8,128)(2,1)S(1)} collective-permute-done((bf16[672,128]{1,0:T(8,128)(2,1)S(1)}, bf16[672,128]{1,0:T(8,128)(2,1)S(1)}, u32[]{:S(2)}, u32[]{:S(2)}) %collective-permute-start.2) | collective-permute-done | bytes 172064 | tf_op jit(solution)/shard_map/ppermute | solution.py:438
  30.1 1.1 stage_weights.2.me_ref.where_ref
  31.3 0.9 collective-permute-done.4.far_ref.far_routes.fwd_far
  32.1 3.8 %core_out.1 = (bf16[64,2048]{1,0:T(8,128)(2,1)S(1)}, bf16[64,2048]{1,0:T(8,128)(2,1)S(1)}, bf16[64,2048]{1,0:T(8,128)(2,1)S(1)}, bf16[64,2048]{1,0:T(8,128)(2,1)S(1)}) custom-call(s32[3]{0:T(128)S(1)} %stage_weights.2.me_ref.where_ref, bf16[3,256,512]{2,1,0:T(8,128)(2,1)S(1)} %copy-done.3, f32[4,256]{1,0:T(4,128)S(1)} %bitcast.52, f32[1,512]{1,0:T(1,128)S(1)} %bitcast.58, ...), custom_call_target="tpu_custom_call" | custom-call | tf_op jit(solution)/shard_map/core_out/pallas_call | solution.py:223
  36.0 1.7 collective-permute-start.8
  37.7 1.6 collective-permute-start.5
  39.3 2.6 %collective-permute-start.6 = (bf16[64,2048]{1,0:T(8,128)(2,1)S(1)}, bf16[64,2048]{1,0:T(8,128)(2,1)S(1)}, u32[]{:S(2)}, u32[]{:S(2)}) collective-permute-start(bf16[64,2048]{1,0:T(8,128)(2,1)S(1)} %get-tuple-element.76), channel_id=1, source_target_pairs={{0,2},{1,3},{2,0},{3,1},{4,6},{5,7},{6,4},{7,5},{8,10},{9,11},{10,... | collective-permute-start | bytes 786440 | tf_op jit(solution)/shard_map/ppermute | solution.py:444
  42.1 1.6 copy-done.6
  43.7 1.1 stage_weights.3.where_ref.me_ref
  44.9 5.9 %collective-permute-done.5.refs_1_ = bf16[64,2048]{1,0:T(8,128)(2,1)S(1)} collective-permute-done((bf16[64,2048]{1,0:T(8,128)(2,1)S(1)}, bf16[64,2048]{1,0:T(8,128)(2,1)S(1)}, u32[]{:S(2)}, u32[]{:S(2)}) %collective-permute-start.5) | collective-permute-done | bytes 262176 | tf_op jit(solution)/shard_map/ppermute | solution.py:444
  50.7 9.9 %collective-permute-done.6.refs_2_ = bf16[64,2048]{1,0:T(8,128)(2,1)S(1)} collective-permute-done((bf16[64,2048]{1,0:T(8,128)(2,1)S(1)}, bf16[64,2048]{1,0:T(8,128)(2,1)S(1)}, u32[]{:S(2)}, u32[]{:S(2)}) %collective-permute-start.6) | collective-permute-done | bytes 262176 | tf_op jit(solution)/shard_map/ppermute | solution.py:444
  61.5 1.0 collective-permute-start.12
  62.5 2.5 %collective-permute-start.11 = (bf16[32,2048]{1,0:T(8,128)(2,1)S(1)}, bf16[32,2048]{1,0:T(8,128)(2,1)S(1)}, u32[]{:S(2)}, u32[]{:S(2)}) collective-permute-start(bf16[32,2048]{1,0:T(8,128)(2,1)S(1)} %get-tuple-element.89.refs_0_), channel_id=1, source_target_pairs={{0,3},{1,2},{2,1},{3,0},{4,7},{5,6},{6,5},{7,4},{8,11},{9,10},{10,... | collective-permute-start | bytes 393224 | tf_op jit(solution)/shard_map/ppermute | solution.py:444
  64.9 5.3 %collective-permute-start.10 = (bf16[32,2048]{1,0:T(8,128)(2,1)S(1)}, bf16[32,2048]{1,0:T(8,128)(2,1)S(1)}, u32[]{:S(2)}, u32[]{:S(2)}) collective-permute-start(bf16[32,2048]{1,0:T(8,128)(2,1)S(1)} %get-tuple-element.89.refs_0_), channel_id=1, source_target_pairs={{0,2},{1,3},{2,0},{3,1},{4,6},{5,7},{6,4},{7,5},{8,10},{9,11},{10,... | collective-permute-start | bytes 393224 | tf_op jit(solution)/shard_map/ppermute | solution.py:444
  70.4 7.3 %collective-permute-done.10.refs_2_ = bf16[32,2048]{1,0:T(8,128)(2,1)S(1)} collective-permute-done((bf16[32,2048]{1,0:T(8,128)(2,1)S(1)}, bf16[32,2048]{1,0:T(8,128)(2,1)S(1)}, u32[]{:S(2)}, u32[]{:S(2)}) %collective-permute-start.10) | collective-permute-done | bytes 131104 | tf_op jit(solution)/shard_map/ppermute | solution.py:444
  78.3 1.2 collective-permute-start.14
  79.9 2.6 %collective-permute-start.17 = (bf16[32,2048]{1,0:T(8,128)(2,1)S(1)}, bf16[32,2048]{1,0:T(8,128)(2,1)S(1)}, u32[]{:S(2)}, u32[]{:S(2)}) collective-permute-start(bf16[32,2048]{1,0:T(8,128)(2,1)S(1)} %get-tuple-element.93.refs_0_), channel_id=1, source_target_pairs={{0,3},{1,2},{2,1},{3,0},{4,7},{5,6},{6,5},{7,4},{8,11},{9,10},{10,... | collective-permute-start | bytes 393224 | tf_op jit(solution)/shard_map/ppermute | solution.py:444
  82.5 1.7 collective-permute-start.15
  84.3 3.7 %collective-permute-done.17.refs_3_ = bf16[32,2048]{1,0:T(8,128)(2,1)S(1)} collective-permute-done((bf16[32,2048]{1,0:T(8,128)(2,1)S(1)}, bf16[32,2048]{1,0:T(8,128)(2,1)S(1)}, u32[]{:S(2)}, u32[]{:S(2)}) %collective-permute-start.17) | collective-permute-done | bytes 131104 | tf_op jit(solution)/shard_map/ppermute | solution.py:444
  87.9 3.7 %collective-permute-done.16.refs_2_ = bf16[32,2048]{1,0:T(8,128)(2,1)S(1)} collective-permute-done((bf16[32,2048]{1,0:T(8,128)(2,1)S(1)}, bf16[32,2048]{1,0:T(8,128)(2,1)S(1)}, u32[]{:S(2)}, u32[]{:S(2)}) %collective-permute-start.16) | collective-permute-done | bytes 131104 | tf_op jit(solution)/shard_map/ppermute | solution.py:444
  92.3 1.7 collective-permute-start.21
  95.3 4.0 %collective-permute-done.21 = bf16[64,2048]{1,0:T(8,128)(2,1)S(1)} collective-permute-done((bf16[64,2048]{1,0:T(8,128)(2,1)S(1)}, bf16[64,2048]{1,0:T(8,128)(2,1)S(1)}, u32[]{:S(2)}, u32[]{:S(2)}) %collective-permute-start.21) | collective-permute-done | bytes 262176 | tf_op jit(solution)/shard_map/ppermute | solution.py:438
  99.4 1.5 collective-permute-done.22
  101.8 1.5 collective-permute-start.25
  103.3 9.2 %expert_pieces.2 = (bf16[4,128,2048]{2,1,0:T(8,128)(2,1)S(1)}, bf16[4,128,2048]{2,1,0:T(8,128)(2,1)S(1)}) custom-call(s32[3]{0:T(128)S(1)} %stage_weights.3.where_ref.me_ref, bf16[4,672,128]{2,1,0:T(8,128)(2,1)S(1)} %pad_maximum_fusion.near_ref.near_routes.fwd_near, bf16[4,672,128]{2,1,0:T(8,128)(2,1)S(1)} %collective-permute-done.4.far_ref.far_routes.fwd_far, ...), custom_call_target="tpu_custom_call" | custom-call | flops 6442450944 | bytes 8388608 | tf_op jit(solution)/shard_map/expert_pieces/pallas_call | solution.py:411
  112.5 2.9 %collective-permute-done.26.refs_4_ = bf16[128,2048]{1,0:T(8,128)(2,1)S(1)} collective-permute-done((bf16[128,2048]{1,0:T(8,128)(2,1)S(1)}, bf16[128,2048]{1,0:T(8,128)(2,1)S(1)}, u32[]{:S(2)}, u32[]{:S(2)}) %collective-permute-start.26) | collective-permute-done | bytes 524320 | tf_op jit(solution)/shard_map/ppermute | solution.py:438
  116.0 1.5 collective-permute-start.36
  117.5 1.0 collective-permute-start.35
  118.5 1.8 collective-permute-done.30.refs_5_
  121.5 3.2 %collective-permute-done.36 = bf16[64,2048]{1,0:T(8,128)(2,1)S(1)} collective-permute-done((bf16[64,2048]{1,0:T(8,128)(2,1)S(1)}, bf16[64,2048]{1,0:T(8,128)(2,1)S(1)}, u32[]{:S(2)}, u32[]{:S(2)}) %collective-permute-start.36) | collective-permute-done | bytes 262176 | tf_op jit(solution)/shard_map/ppermute | solution.py:438
  124.7 1.3 collective-permute-done.35
  126.8 1.7 collective-permute-start.32
  128.4 9.1 %expert_pieces.3 = (bf16[4,128,2048]{2,1,0:T(8,128)(2,1)S(1)}, bf16[4,128,2048]{2,1,0:T(8,128)(2,1)S(1)}) custom-call(s32[3]{0:T(128)S(1)} %stage_weights.3.where_ref.me_ref, bf16[4,672,128]{2,1,0:T(8,128)(2,1)S(1)} %pad_maximum_fusion.near_ref.near_routes.fwd_near, bf16[4,672,128]{2,1,0:T(8,128)(2,1)S(1)} %collective-permute-done.4.far_ref.far_routes.fwd_far, ...), custom_call_target="tpu_custom_call" | custom-call | flops 6442450944 | bytes 8388608 | tf_op jit(solution)/shard_map/expert_pieces/pallas_call | solution.py:411
  137.6 2.9 %collective-permute-done.31.refs_0_ = bf16[128,2048]{1,0:T(8,128)(2,1)S(1)} collective-permute-done((bf16[128,2048]{1,0:T(8,128)(2,1)S(1)}, bf16[128,2048]{1,0:T(8,128)(2,1)S(1)}, u32[]{:S(2)}, u32[]{:S(2)}) %collective-permute-start.31) | collective-permute-done | bytes 524320 | tf_op jit(solution)/shard_map/ppermute | solution.py:438
  141.0 1.5 collective-permute-start.34
  142.6 0.9 collective-permute-start.33
  143.5 6.3 %collective-permute-done.34.refs_3_ = bf16[64,2048]{1,0:T(8,128)(2,1)S(1)} collective-permute-done((bf16[64,2048]{1,0:T(8,128)(2,1)S(1)}, bf16[64,2048]{1,0:T(8,128)(2,1)S(1)}, u32[]{:S(2)}, u32[]{:S(2)}) %collective-permute-start.34) | collective-permute-done | bytes 262176 | tf_op jit(solution)/shard_map/ppermute | solution.py:438
  149.8 1.2 collective-permute-done.33.refs_2_
  152.1 1.7 collective-permute-start.43
  153.8 1.0 sum_terms.2
  154.9 2.8 %collective-permute-start.40 = (bf16[128,512]{1,0:T(8,128)(2,1)S(1)}, bf16[128,512]{1,0:T(8,128)(2,1)S(1)}, u32[]{:S(2)}, u32[]{:S(2)}) collective-permute-start(bf16[128,512]{1,0:T(8,128)(2,1)S(1)} %get-tuple-element.122), channel_id=1, source_target_pairs={{0,2},{1,3},{2,0},{3,1},{4,6},{5,7},{6,4},{7,5},{8,10},{9,11},{10,... | collective-permute-start | bytes 393224 | tf_op jit(solution)/shard_map/ppermute | solution.py:444
  157.7 3.9 %collective-permute-done.39.refs_1_ = bf16[128,512]{1,0:T(8,128)(2,1)S(1)} collective-permute-done((bf16[128,512]{1,0:T(8,128)(2,1)S(1)}, bf16[128,512]{1,0:T(8,128)(2,1)S(1)}, u32[]{:S(2)}, u32[]{:S(2)}) %collective-permute-start.39) | collective-permute-done | bytes 131104 | tf_op jit(solution)/shard_map/ppermute | solution.py:444
  161.6 1.4 collective-permute-done.40.refs_2_
  163.0 1.8 collective-permute-done.42.refs_0_
  165.4 1.5 collective-permute-start.45
  166.9 0.9 collective-permute-start.44
  167.8 2.3 %collective-permute-start.41 = (bf16[128,512]{1,0:T(8,128)(2,1)S(1)}, bf16[128,512]{1,0:T(8,128)(2,1)S(1)}, u32[]{:S(2)}, u32[]{:S(2)}) collective-permute-start(bf16[128,512]{1,0:T(8,128)(2,1)S(1)} %get-tuple-element.123), channel_id=1, source_target_pairs={{0,3},{1,2},{2,1},{3,0},{4,7},{5,6},{6,5},{7,4},{8,11},{9,10},{10,... | collective-permute-start | bytes 393224 | tf_op jit(solution)/shard_map/ppermute | solution.py:444
  170.1 1.9 collective-permute-done.45.refs_3_
  172.0 1.3 collective-permute-done.44.refs_2_
  173.3 1.0 sum_terms.3
  174.4 2.8 %collective-permute-start.47 = (bf16[128,512]{1,0:T(8,128)(2,1)S(1)}, bf16[128,512]{1,0:T(8,128)(2,1)S(1)}, u32[]{:S(2)}, u32[]{:S(2)}) collective-permute-start(bf16[128,512]{1,0:T(8,128)(2,1)S(1)} %get-tuple-element.129), channel_id=1, source_target_pairs={{0,2},{1,3},{2,0},{3,1},{4,6},{5,7},{6,4},{7,5},{8,10},{9,11},{10,... | collective-permute-start | bytes 393224 | tf_op jit(solution)/shard_map/ppermute | solution.py:444
  177.2 1.6 collective-permute-start.48
  178.7 4.7 %core_grads.1 = (bf16[256,512]{1,0:T(8,128)(2,1)}, bf16[256,512]{1,0:T(8,128)(2,1)}, bf16[256,512]{1,0:T(8,128)(2,1)}) custom-call(s32[3]{0:T(128)S(1)} %stage_weights.3.where_ref.me_ref, bf16[3,256,512]{2,1,0:T(8,128)(2,1)S(1)} %copy-done.3, bf16[256,512]{1,0:T(8,128)(2,1)S(1)} %copy-done.9, f32[4,256]{1,0:T(4,128)S(1)} %bitcast.53, ...), custom_call_target="tpu_custom_call" | custom-call | tf_op jit(solution)/shard_map/core_grads/pallas_call | solution.py:268
  183.5 1.4 collective-permute-done.47.refs_6_
  184.8 1.4 layer_out.1
  (107 shorter events, 11.7 us)
Async XLA Ops:
  0.6 10.4 %copy-start.8 = (bf16[256,512]{1,0:T(8,128)(2,1)S(1)}, bf16[256,512]{1,0:T(8,128)(2,1)}, u32[]{:S(2)}) copy-start(bf16[256,512]{1,0:T(8,128)(2,1)} %cot_ref.3) | copy-start | bytes 786436
  0.6 10.3 %copy-start.13 = (f32[256,4]{0,1:T(4,128)S(1)}, f32[256,4]{0,1:T(4,128)}, u32[]{:S(2)}) copy-start(f32[256,4]{0,1:T(4,128)} %param.18) | copy-start | bytes 12292
  0.7 10.3 %copy-start.14 = (f32[4,3,512]{2,0,1:T(4,128)S(1)}, f32[4,3,512]{2,0,1:T(4,128)}, u32[]{:S(2)}) copy-start(f32[4,3,512]{2,0,1:T(4,128)} %param.17) | copy-start | bytes 73732
  0.7 10.3 %copy-start.15 = (s32[256,8]{0,1:T(8,128)S(1)}, s32[256,8]{0,1:T(8,128)}, u32[]{:S(2)}) copy-start(s32[256,8]{0,1:T(8,128)} %param.22) | copy-start | bytes 24580
  0.7 10.3 %copy-start.16 = (f32[256,8]{0,1:T(8,128)S(1)}, f32[256,8]{0,1:T(8,128)}, u32[]{:S(2)}) copy-start(f32[256,8]{0,1:T(8,128)} %param.23) | copy-start | bytes 24580
  7.4 22.7 %copy-start.1 = (bf16[512,2048]{1,0:T(8,128)(2,1)S(1)}, bf16[512,2048]{1,0:T(8,128)(2,1)}, u32[]{:S(2)}) copy-start(bf16[512,2048]{1,0:T(8,128)(2,1)} %w_ref.1) | copy-start | bytes 6291460
  7.4 3.6 %collective-permute-start = (bf16[3,16,512]{2,1,0:T(8,128)(2,1)}, bf16[3,16,512]{2,1,0:T(8,128)(2,1)S(1)}, u32[]{:S(2)}, u32[]{:S(2)}) collective-permute-start(bf16[3,16,512]{2,1,0:T(8,128)(2,1)} %get-tuple-element.70), channel_id=1, source_target_pairs={{0,4},{4,8},{8,12},{12,16},{16,20},{20,24},{24,28},{1,5},{5,9},{9,... | collective-permute-start | bytes 147464 | tf_op jit(solution)/shard_map/ppermute | solution.py:610
  12.1 20.0 %copy-start.18 = (f32[512]{0:T(512)S(1)}, f32[512]{0:T(512)}, u32[]{:S(2)}) copy-start(f32[512]{0:T(512)} %param.19) | copy-start | bytes 6148
  15.9 11.4 %collective-permute-start.3 = (bf16[672,128]{1,0:T(8,128)(2,1)S(1)}, bf16[672,128]{1,0:T(8,128)(2,1)S(1)}, u32[]{:S(2)}, u32[]{:S(2)}) collective-permute-start(bf16[672,128]{1,0:T(8,128)(2,1)S(1)} %get-tuple-element.73), channel_id=1, source_target_pairs={{0,24},{4,28},{8,16},{12,20},{16,8},{20,12},{24,0},{28,4},{1,25},{... | collective-permute-start | bytes 516104 | tf_op jit(solution)/shard_map/ppermute | solution.py:438
  22.0 7.8 %collective-permute-start.2 = (bf16[672,128]{1,0:T(8,128)(2,1)S(1)}, bf16[672,128]{1,0:T(8,128)(2,1)S(1)}, u32[]{:S(2)}, u32[]{:S(2)}) collective-permute-start(bf16[672,128]{1,0:T(8,128)(2,1)S(1)} %get-tuple-element.73), channel_id=1, source_target_pairs={{0,16},{4,20},{8,24},{12,28},{16,0},{20,4},{24,8},{28,12},{1,17},{... | collective-permute-start | bytes 516104 | tf_op jit(solution)/shard_map/ppermute | solution.py:438
  22.5 7.3 %collective-permute-start.1 = (bf16[672,128]{1,0:T(8,128)(2,1)S(1)}, bf16[672,128]{1,0:T(8,128)(2,1)S(1)}, u32[]{:S(2)}, u32[]{:S(2)}) collective-permute-start(bf16[672,128]{1,0:T(8,128)(2,1)S(1)} %get-tuple-element.73), channel_id=1, source_target_pairs={{0,8},{4,12},{8,0},{12,4},{16,24},{20,28},{24,16},{28,20},{1,9},{5... | collective-permute-start | bytes 516104 | tf_op jit(solution)/shard_map/ppermute | solution.py:438
  29.9 2.2 %collective-permute-start.4 = (bf16[4,672,128]{2,1,0:T(8,128)(2,1)S(1)}, bf16[4,672,128]{2,1,0:T(8,128)(2,1)S(1)}, u32[]{:S(2)}, u32[]{:S(2)}) collective-permute-start(bf16[4,672,128]{2,1,0:T(8,128)(2,1)S(1)} %pad_maximum_fusion.near_ref.near_routes.fwd_near), channel_id=1, source_target_pairs={{0,4},{4,0},{8,12},{12,8},{16,20},{20,16},{24,28},{28,24},{1,5},{5... | collective-permute-start | bytes 2064392 | tf_op jit(solution)/shard_map/ppermute | solution.py:438
  30.0 2.1 %copy-start.3 = (bf16[3,256,512]{2,1,0:T(8,128)(2,1)S(1)}, bf16[3,256,512]{2,1,0:T(8,128)(2,1)}, u32[]{:S(2)}) copy-start(bf16[3,256,512]{2,1,0:T(8,128)(2,1)} %copy-done.2) | copy-start | bytes 2359300
  30.1 5.9 %copy-start.12 = (bf16[576,128]{1,0:T(8,128)(2,1)S(1)}, bf16[576,128]{1,0:T(8,128)(2,1)}, u32[]{:S(2)}) copy-start(bf16[576,128]{1,0:T(8,128)(2,1)} %copy-done.11) | copy-start | bytes 442372
  32.1 9.9 %copy-start.4 = (bf16[1,2048,512]{2,1,0:T(8,128)(2,1)S(1)}, bf16[1,2048,512]{2,1,0:T(8,128)(2,1)}, u32[]{:S(2)}) copy-start(bf16[1,2048,512]{2,1,0:T(8,128)(2,1)} %gate_ref.3) | copy-start | bytes 6291460
  32.1 9.9 %copy-start.5 = (bf16[1,2048,512]{2,1,0:T(8,128)(2,1)S(1)}, bf16[1,2048,512]{2,1,0:T(8,128)(2,1)}, u32[]{:S(2)}) copy-start(bf16[1,2048,512]{2,1,0:T(8,128)(2,1)} %up_ref.3) | copy-start | bytes 6291460
  36.0 24.6 %copy-start = (bf16[256,2048]{1,0:T(8,128)(2,1)S(1)}, bf16[256,2048]{1,0:T(8,128)(2,1)}, u32[]{:S(2)}) copy-start(bf16[256,2048]{1,0:T(8,128)(2,1)} %x_ref.3) | copy-start | bytes 3145732
  36.0 8.8 %collective-permute-start.8 = (bf16[1,576,128]{2,1,0:T(8,128)(2,1)S(1)}, bf16[1,576,128]{2,1,0:T(8,128)(2,1)S(1)}, u32[]{:S(2)}, u32[]{:S(2)}) collective-permute-start(bf16[1,576,128]{2,1,0:T(8,128)(2,1)S(1)} %bitcast.49), channel_id=1, source_target_pairs={{0,8},{4,12},{8,0},{12,4},{16,24},{20,28},{24,16},{28,20},{1,9},{5... | collective-permute-start | bytes 442376 | tf_op jit(solution)/shard_map/ppermute | solution.py:438
  37.7 13.0 %collective-permute-start.5 = (bf16[64,2048]{1,0:T(8,128)(2,1)S(1)}, bf16[64,2048]{1,0:T(8,128)(2,1)S(1)}, u32[]{:S(2)}, u32[]{:S(2)}) collective-permute-start(bf16[64,2048]{1,0:T(8,128)(2,1)S(1)} %get-tuple-element.75), channel_id=1, source_target_pairs={{0,1},{1,0},{2,3},{3,2},{4,5},{5,4},{6,7},{7,6},{8,9},{9,8},{10,11... | collective-permute-start | bytes 786440 | tf_op jit(solution)/shard_map/ppermute | solution.py:444
  39.3 21.4 %collective-permute-start.6 = (bf16[64,2048]{1,0:T(8,128)(2,1)S(1)}, bf16[64,2048]{1,0:T(8,128)(2,1)S(1)}, u32[]{:S(2)}, u32[]{:S(2)}) collective-permute-start(bf16[64,2048]{1,0:T(8,128)(2,1)S(1)} %get-tuple-element.76), channel_id=1, source_target_pairs={{0,2},{1,3},{2,0},{3,1},{4,6},{5,7},{6,4},{7,5},{8,10},{9,11},{10,... | collective-permute-start | bytes 786440 | tf_op jit(solution)/shard_map/ppermute | solution.py:444
  41.9 18.8 %collective-permute-start.7 = (bf16[64,2048]{1,0:T(8,128)(2,1)S(1)}, bf16[64,2048]{1,0:T(8,128)(2,1)S(1)}, u32[]{:S(2)}, u32[]{:S(2)}) collective-permute-start(bf16[64,2048]{1,0:T(8,128)(2,1)S(1)} %get-tuple-element.77), channel_id=1, source_target_pairs={{0,3},{1,2},{2,1},{3,0},{4,7},{5,6},{6,5},{7,4},{8,11},{9,10},{10,... | collective-permute-start | bytes 786440 | tf_op jit(solution)/shard_map/ppermute | solution.py:444
  43.7 17.0 %copy-start.17 = (f32[2048]{0:T(1024)S(1)}, f32[2048]{0:T(1024)}, u32[]{:S(2)}) copy-start(f32[2048]{0:T(1024)} %param.21) | copy-start | bytes 24580
  61.5 8.8 %collective-permute-start.12 = (bf16[2,576,128]{2,1,0:T(8,128)(2,1)S(1)}, bf16[2,576,128]{2,1,0:T(8,128)(2,1)S(1)}, u32[]{:S(2)}, u32[]{:S(2)}) collective-permute-start(bf16[2,576,128]{2,1,0:T(8,128)(2,1)S(1)} %pad_maximum_fusion.5), channel_id=1, source_target_pairs={{0,16},{4,20},{8,24},{12,28},{16,0},{20,4},{24,8},{28,12},{1,17},{... | collective-permute-start | bytes 884744 | tf_op jit(solution)/shard_map/ppermute | solution.py:438
  62.5 7.9 %collective-permute-start.11 = (bf16[32,2048]{1,0:T(8,128)(2,1)S(1)}, bf16[32,2048]{1,0:T(8,128)(2,1)S(1)}, u32[]{:S(2)}, u32[]{:S(2)}) collective-permute-start(bf16[32,2048]{1,0:T(8,128)(2,1)S(1)} %get-tuple-element.89.refs_0_), channel_id=1, source_target_pairs={{0,3},{1,2},{2,1},{3,0},{4,7},{5,6},{6,5},{7,4},{8,11},{9,10},{10,... | collective-permute-start | bytes 393224 | tf_op jit(solution)/shard_map/ppermute | solution.py:444
  64.9 12.7 %collective-permute-start.10 = (bf16[32,2048]{1,0:T(8,128)(2,1)S(1)}, bf16[32,2048]{1,0:T(8,128)(2,1)S(1)}, u32[]{:S(2)}, u32[]{:S(2)}) collective-permute-start(bf16[32,2048]{1,0:T(8,128)(2,1)S(1)} %get-tuple-element.89.refs_0_), channel_id=1, source_target_pairs={{0,2},{1,3},{2,0},{3,1},{4,6},{5,7},{6,4},{7,5},{8,10},{9,11},{10,... | collective-permute-start | bytes 393224 | tf_op jit(solution)/shard_map/ppermute | solution.py:444
  70.2 7.5 %collective-permute-start.9 = (bf16[32,2048]{1,0:T(8,128)(2,1)S(1)}, bf16[32,2048]{1,0:T(8,128)(2,1)S(1)}, u32[]{:S(2)}, u32[]{:S(2)}) collective-permute-start(bf16[32,2048]{1,0:T(8,128)(2,1)S(1)} %get-tuple-element.89.refs_0_), channel_id=1, source_target_pairs={{0,1},{1,0},{2,3},{3,2},{4,5},{5,4},{6,7},{7,6},{8,9},{9,8},{10,11... | collective-permute-start | bytes 393224 | tf_op jit(solution)/shard_map/ppermute | solution.py:444
  70.4 32.9 %copy-start.7 = (bf16[1,512,2048]{2,1,0:T(8,128)(2,1)S(1)}, bf16[1,512,2048]{2,1,0:T(8,128)(2,1)}, u32[]{:S(2)}) copy-start(bf16[1,512,2048]{2,1,0:T(8,128)(2,1)} %down_ref.3) | copy-start | bytes 6291460
  78.3 14.0 %collective-permute-start.14 = (bf16[128,2048]{1,0:T(8,128)(2,1)S(1)}, bf16[128,2048]{1,0:T(8,128)(2,1)S(1)}, u32[]{:S(2)}, u32[]{:S(2)}) collective-permute-start(bf16[128,2048]{1,0:T(8,128)(2,1)S(1)} %join_rows.2.refs_0_), channel_id=1, source_target_pairs={{0,16},{4,20},{8,24},{12,28},{16,0},{20,4},{24,8},{28,12},{1,17},{... | collective-permute-start | bytes 1572872 | tf_op jit(solution)/shard_map/ppermute | solution.py:438
  79.4 12.8 %collective-permute-start.13 = (bf16[128,2048]{1,0:T(8,128)(2,1)S(1)}, bf16[128,2048]{1,0:T(8,128)(2,1)S(1)}, u32[]{:S(2)}, u32[]{:S(2)}) collective-permute-start(bf16[128,2048]{1,0:T(8,128)(2,1)S(1)} %join_rows.2.refs_0_), channel_id=1, source_target_pairs={{0,8},{4,12},{8,0},{12,4},{16,24},{20,28},{24,16},{28,20},{1,9},{5... | collective-permute-start | bytes 1572872 | tf_op jit(solution)/shard_map/ppermute | solution.py:438
  79.9 8.1 %collective-permute-start.17 = (bf16[32,2048]{1,0:T(8,128)(2,1)S(1)}, bf16[32,2048]{1,0:T(8,128)(2,1)S(1)}, u32[]{:S(2)}, u32[]{:S(2)}) collective-permute-start(bf16[32,2048]{1,0:T(8,128)(2,1)S(1)} %get-tuple-element.93.refs_0_), channel_id=1, source_target_pairs={{0,3},{1,2},{2,1},{3,0},{4,7},{5,6},{6,5},{7,4},{8,11},{9,10},{10,... | collective-permute-start | bytes 393224 | tf_op jit(solution)/shard_map/ppermute | solution.py:444
  82.5 9.1 %collective-permute-start.16 = (bf16[32,2048]{1,0:T(8,128)(2,1)S(1)}, bf16[32,2048]{1,0:T(8,128)(2,1)S(1)}, u32[]{:S(2)}, u32[]{:S(2)}) collective-permute-start(bf16[32,2048]{1,0:T(8,128)(2,1)S(1)} %get-tuple-element.93.refs_0_), channel_id=1, source_target_pairs={{0,2},{1,3},{2,0},{3,1},{4,6},{5,7},{6,4},{7,5},{8,10},{9,11},{10,... | collective-permute-start | bytes 393224 | tf_op jit(solution)/shard_map/ppermute | solution.py:444
  82.5 9.1 %collective-permute-start.15 = (bf16[32,2048]{1,0:T(8,128)(2,1)S(1)}, bf16[32,2048]{1,0:T(8,128)(2,1)S(1)}, u32[]{:S(2)}, u32[]{:S(2)}) collective-permute-start(bf16[32,2048]{1,0:T(8,128)(2,1)S(1)} %get-tuple-element.93.refs_0_), channel_id=1, source_target_pairs={{0,1},{1,0},{2,3},{3,2},{4,5},{5,4},{6,7},{7,6},{8,9},{9,8},{10,11... | collective-permute-start | bytes 393224 | tf_op jit(solution)/shard_map/ppermute | solution.py:444
  92.3 7.1 %collective-permute-start.21 = (bf16[64,2048]{1,0:T(8,128)(2,1)S(1)}, bf16[64,2048]{1,0:T(8,128)(2,1)S(1)}, u32[]{:S(2)}, u32[]{:S(2)}) collective-permute-start(bf16[64,2048]{1,0:T(8,128)(2,1)S(1)} %slice.96), channel_id=1, source_target_pairs={{0,16},{4,20},{8,24},{12,28},{16,0},{20,4},{24,8},{28,12},{1,17},{... | collective-permute-start | bytes 786440 | tf_op jit(solution)/shard_map/ppermute | solution.py:438
  94.0 6.8 %collective-permute-start.22 = (bf16[64,2048]{1,0:T(8,128)(2,1)S(1)}, bf16[64,2048]{1,0:T(8,128)(2,1)S(1)}, u32[]{:S(2)}, u32[]{:S(2)}) collective-permute-start(bf16[64,2048]{1,0:T(8,128)(2,1)S(1)} %slice.97), channel_id=1, source_target_pairs={{0,8},{4,12},{8,0},{12,4},{16,24},{20,28},{24,16},{28,20},{1,9},{5... | collective-permute-start | bytes 786440 | tf_op jit(solution)/shard_map/ppermute | solution.py:438
  94.8 7.0 %collective-permute-start.19 = (bf16[128,2048]{1,0:T(8,128)(2,1)S(1)}, bf16[128,2048]{1,0:T(8,128)(2,1)S(1)}, u32[]{:S(2)}, u32[]{:S(2)}) collective-permute-start(bf16[128,2048]{1,0:T(8,128)(2,1)S(1)} %collective-permute-done.13.refs_2_), channel_id=1, source_target_pairs={{0,4},{4,0},{8,12},{12,8},{16,20},{20,16},{24,28},{28,24},{1,5},{5... | collective-permute-start | bytes 1572872 | tf_op jit(solution)/shard_map/ppermute | solution.py:438
  94.8 8.5 %collective-permute-start.20 = (bf16[128,2048]{1,0:T(8,128)(2,1)S(1)}, bf16[128,2048]{1,0:T(8,128)(2,1)S(1)}, u32[]{:S(2)}, u32[]{:S(2)}) collective-permute-start(bf16[128,2048]{1,0:T(8,128)(2,1)S(1)} %collective-permute-done.14.refs_4_), channel_id=1, source_target_pairs={{0,4},{4,0},{8,12},{12,8},{16,20},{20,16},{24,28},{28,24},{1,5},{5... | collective-permute-start | bytes 1572872 | tf_op jit(solution)/shard_map/ppermute | solution.py:438
  95.3 6.1 %collective-permute-start.18 = (bf16[128,2048]{1,0:T(8,128)(2,1)S(1)}, bf16[128,2048]{1,0:T(8,128)(2,1)S(1)}, u32[]{:S(2)}, u32[]{:S(2)}) collective-permute-start(bf16[128,2048]{1,0:T(8,128)(2,1)S(1)} %join_rows.2.refs_0_), channel_id=1, source_target_pairs={{0,4},{4,0},{8,12},{12,8},{16,20},{20,16},{24,28},{28,24},{1,5},{5... | collective-permute-start | bytes 1572872 | tf_op jit(solution)/shard_map/ppermute | solution.py:438
  100.9 2.4 %collective-permute-start.23 = (bf16[128,2048]{1,0:T(8,128)(2,1)S(1)}, bf16[128,2048]{1,0:T(8,128)(2,1)S(1)}, u32[]{:S(2)}, u32[]{:S(2)}) collective-permute-start(bf16[128,2048]{1,0:T(8,128)(2,1)S(1)} %constant_dynamic-update-slice_fusion.2.refs_6_), channel_id=1, source_target_pairs={{0,4},{4,0},{8,12},{12,8},{16,20},{20,16},{24,28},{28,24},{1,5},{5... | collective-permute-start | bytes 1572872 | tf_op jit(solution)/shard_map/ppermute | solution.py:438
  100.9 11.5 %collective-permute-start.27 = (bf16[4,576,128]{2,1,0:T(8,128)(2,1)S(1)}, bf16[4,576,128]{2,1,0:T(8,128)(2,1)S(1)}, u32[]{:S(2)}, u32[]{:S(2)}) collective-permute-start(bf16[4,576,128]{2,1,0:T(8,128)(2,1)S(1)} %constant_dynamic-update-slice_fusion.bwd_near), channel_id=1, source_target_pairs={{0,4},{4,0},{8,12},{12,8},{16,20},{20,16},{24,28},{28,24},{1,5},{5... | collective-permute-start | bytes 1769480 | tf_op jit(solution)/shard_map/ppermute | solution.py:438
  101.4 13.9 %collective-permute-start.26 = (bf16[128,2048]{1,0:T(8,128)(2,1)S(1)}, bf16[128,2048]{1,0:T(8,128)(2,1)S(1)}, u32[]{:S(2)}, u32[]{:S(2)}) collective-permute-start(bf16[128,2048]{1,0:T(8,128)(2,1)S(1)} %join_rows.3.refs_0_), channel_id=1, source_target_pairs={{0,16},{4,20},{8,24},{12,28},{16,0},{20,4},{24,8},{28,12},{1,17},{... | collective-permute-start | bytes 1572872 | tf_op jit(solution)/shard_map/ppermute | solution.py:438
  101.8 13.6 %collective-permute-start.25 = (bf16[128,2048]{1,0:T(8,128)(2,1)S(1)}, bf16[128,2048]{1,0:T(8,128)(2,1)S(1)}, u32[]{:S(2)}, u32[]{:S(2)}) collective-permute-start(bf16[128,2048]{1,0:T(8,128)(2,1)S(1)} %join_rows.3.refs_0_), channel_id=1, source_target_pairs={{0,8},{4,12},{8,0},{12,4},{16,24},{20,28},{24,16},{28,20},{1,9},{5... | collective-permute-start | bytes 1572872 | tf_op jit(solution)/shard_map/ppermute | solution.py:438
  103.3 12.1 %collective-permute-start.24 = (bf16[128,2048]{1,0:T(8,128)(2,1)S(1)}, bf16[128,2048]{1,0:T(8,128)(2,1)S(1)}, u32[]{:S(2)}, u32[]{:S(2)}) collective-permute-start(bf16[128,2048]{1,0:T(8,128)(2,1)S(1)} %join_rows.3.refs_0_), channel_id=1, source_target_pairs={{0,4},{4,0},{8,12},{12,8},{16,20},{20,16},{24,28},{28,24},{1,5},{5... | collective-permute-start | bytes 1572872 | tf_op jit(solution)/shard_map/ppermute | solution.py:438
  115.4 5.7 %collective-permute-start.28 = (bf16[4,128,2048]{2,1,0:T(8,128)(2,1)S(1)}, bf16[4,128,2048]{2,1,0:T(8,128)(2,1)S(1)}, u32[]{:S(2)}, u32[]{:S(2)}) collective-permute-start(bf16[4,128,2048]{2,1,0:T(8,128)(2,1)S(1)} %get-tuple-element.100), channel_id=1, source_target_pairs={{0,4},{4,0},{8,12},{12,8},{16,20},{20,16},{24,28},{28,24},{1,5},{5... | collective-permute-start | bytes 6291464 | tf_op jit(solution)/shard_map/ppermute | solution.py:438
  115.4 4.9 %collective-permute-start.30 = (bf16[128,2048]{1,0:T(8,128)(2,1)S(1)}, bf16[128,2048]{1,0:T(8,128)(2,1)S(1)}, u32[]{:S(2)}, u32[]{:S(2)}) collective-permute-start(bf16[128,2048]{1,0:T(8,128)(2,1)S(1)} %collective-permute-done.26.refs_4_), channel_id=1, source_target_pairs={{0,4},{4,0},{8,12},{12,8},{16,20},{20,16},{24,28},{28,24},{1,5},{5... | collective-permute-start | bytes 1572872 | tf_op jit(solution)/shard_map/ppermute | solution.py:438
  115.9 5.1 %collective-permute-start.29 = (bf16[128,2048]{1,0:T(8,128)(2,1)S(1)}, bf16[128,2048]{1,0:T(8,128)(2,1)S(1)}, u32[]{:S(2)}, u32[]{:S(2)}) collective-permute-start(bf16[128,2048]{1,0:T(8,128)(2,1)S(1)} %collective-permute-done.25.refs_2_), channel_id=1, source_target_pairs={{0,4},{4,0},{8,12},{12,8},{16,20},{20,16},{24,28},{28,24},{1,5},{5... | collective-permute-start | bytes 1572872 | tf_op jit(solution)/shard_map/ppermute | solution.py:438
  116.0 8.8 %collective-permute-start.36 = (bf16[64,2048]{1,0:T(8,128)(2,1)S(1)}, bf16[64,2048]{1,0:T(8,128)(2,1)S(1)}, u32[]{:S(2)}, u32[]{:S(2)}) collective-permute-start(bf16[64,2048]{1,0:T(8,128)(2,1)S(1)} %slice.131), channel_id=1, source_target_pairs={{0,8},{4,12},{8,0},{12,4},{16,24},{20,28},{24,16},{28,20},{1,9},{5... | collective-permute-start | bytes 786440 | tf_op jit(solution)/shard_map/ppermute | solution.py:438
  117.5 8.5 %collective-permute-start.35 = (bf16[64,2048]{1,0:T(8,128)(2,1)S(1)}, bf16[64,2048]{1,0:T(8,128)(2,1)S(1)}, u32[]{:S(2)}, u32[]{:S(2)}) collective-permute-start(bf16[64,2048]{1,0:T(8,128)(2,1)S(1)} %slice.130), channel_id=1, source_target_pairs={{0,16},{4,20},{8,24},{12,28},{16,0},{20,4},{24,8},{28,12},{1,17},{... | collective-permute-start | bytes 786440 | tf_op jit(solution)/shard_map/ppermute | solution.py:438
  126.1 2.4 %collective-permute-start.37 = (bf16[128,2048]{1,0:T(8,128)(2,1)S(1)}, bf16[128,2048]{1,0:T(8,128)(2,1)S(1)}, u32[]{:S(2)}, u32[]{:S(2)}) collective-permute-start(bf16[128,2048]{1,0:T(8,128)(2,1)S(1)} %constant_dynamic-update-slice_fusion.4.refs_6_), channel_id=1, source_target_pairs={{0,4},{4,0},{8,12},{12,8},{16,20},{20,16},{24,28},{28,24},{1,5},{5... | collective-permute-start | bytes 1572872 | tf_op jit(solution)/shard_map/ppermute | solution.py:438
  126.2 14.3 %collective-permute-start.31 = (bf16[128,2048]{1,0:T(8,128)(2,1)S(1)}, bf16[128,2048]{1,0:T(8,128)(2,1)S(1)}, u32[]{:S(2)}, u32[]{:S(2)}) collective-permute-start(bf16[128,2048]{1,0:T(8,128)(2,1)S(1)} %pad_maximum_fusion.1), channel_id=1, source_target_pairs={{0,8},{4,12},{8,0},{12,4},{16,24},{20,28},{24,16},{28,20},{1,9},{5... | collective-permute-start | bytes 1572872 | tf_op jit(solution)/shard_map/ppermute | solution.py:438
  126.8 14.0 %collective-permute-start.32 = (bf16[128,2048]{1,0:T(8,128)(2,1)S(1)}, bf16[128,2048]{1,0:T(8,128)(2,1)S(1)}, u32[]{:S(2)}, u32[]{:S(2)}) collective-permute-start(bf16[128,2048]{1,0:T(8,128)(2,1)S(1)} %pad_maximum_fusion.2), channel_id=1, source_target_pairs={{0,16},{4,20},{8,24},{12,28},{16,0},{20,4},{24,8},{28,12},{1,17},{... | collective-permute-start | bytes 1572872 | tf_op jit(solution)/shard_map/ppermute | solution.py:438
  140.8 10.2 %collective-permute-start.38 = (bf16[4,128,2048]{2,1,0:T(8,128)(2,1)S(1)}, bf16[4,128,2048]{2,1,0:T(8,128)(2,1)S(1)}, u32[]{:S(2)}, u32[]{:S(2)}) collective-permute-start(bf16[4,128,2048]{2,1,0:T(8,128)(2,1)S(1)} %get-tuple-element.114), channel_id=1, source_target_pairs={{0,4},{4,0},{8,12},{12,8},{16,20},{20,16},{24,28},{28,24},{1,5},{5... | collective-permute-start | bytes 6291464 | tf_op jit(solution)/shard_map/ppermute | solution.py:438
  141.0 8.8 %collective-permute-start.34 = (bf16[64,2048]{1,0:T(8,128)(2,1)S(1)}, bf16[64,2048]{1,0:T(8,128)(2,1)S(1)}, u32[]{:S(2)}, u32[]{:S(2)}) collective-permute-start(bf16[64,2048]{1,0:T(8,128)(2,1)S(1)} %get-tuple-element.140), channel_id=1, source_target_pairs={{0,8},{4,12},{8,0},{12,4},{16,24},{20,28},{24,16},{28,20},{1,9},{5... | collective-permute-start | bytes 786440 | tf_op jit(solution)/shard_map/ppermute | solution.py:438
  142.6 8.4 %collective-permute-start.33 = (bf16[64,2048]{1,0:T(8,128)(2,1)S(1)}, bf16[64,2048]{1,0:T(8,128)(2,1)S(1)}, u32[]{:S(2)}, u32[]{:S(2)}) collective-permute-start(bf16[64,2048]{1,0:T(8,128)(2,1)S(1)} %get-tuple-element.141), channel_id=1, source_target_pairs={{0,16},{4,20},{8,24},{12,28},{16,0},{20,4},{24,8},{28,12},{1,17},{... | collective-permute-start | bytes 786440 | tf_op jit(solution)/shard_map/ppermute | solution.py:438
  151.5 13.3 %collective-permute-start.42 = (bf16[128,2048]{1,0:T(8,128)(2,1)S(1)}, bf16[128,2048]{1,0:T(8,128)(2,1)S(1)}, u32[]{:S(2)}, u32[]{:S(2)}) collective-permute-start(bf16[128,2048]{1,0:T(8,128)(2,1)S(1)} %pad_maximum_fusion.3), channel_id=1, source_target_pairs={{0,8},{4,12},{8,0},{12,4},{16,24},{20,28},{24,16},{28,20},{1,9},{5... | collective-permute-start | bytes 1572872 | tf_op jit(solution)/shard_map/ppermute | solution.py:438
  152.1 13.1 %collective-permute-start.43 = (bf16[128,2048]{1,0:T(8,128)(2,1)S(1)}, bf16[128,2048]{1,0:T(8,128)(2,1)S(1)}, u32[]{:S(2)}, u32[]{:S(2)}) collective-permute-start(bf16[128,2048]{1,0:T(8,128)(2,1)S(1)} %pad_maximum_fusion.4), channel_id=1, source_target_pairs={{0,16},{4,20},{8,24},{12,28},{16,0},{20,4},{24,8},{28,12},{1,17},{... | collective-permute-start | bytes 1572872 | tf_op jit(solution)/shard_map/ppermute | solution.py:438
  154.8 6.8 %collective-permute-start.39 = (bf16[128,512]{1,0:T(8,128)(2,1)S(1)}, bf16[128,512]{1,0:T(8,128)(2,1)S(1)}, u32[]{:S(2)}, u32[]{:S(2)}) collective-permute-start(bf16[128,512]{1,0:T(8,128)(2,1)S(1)} %get-tuple-element.121), channel_id=1, source_target_pairs={{0,1},{1,0},{2,3},{3,2},{4,5},{5,4},{6,7},{7,6},{8,9},{9,8},{10,11... | collective-permute-start | bytes 393224 | tf_op jit(solution)/shard_map/ppermute | solution.py:444
  154.9 8.1 %collective-permute-start.40 = (bf16[128,512]{1,0:T(8,128)(2,1)S(1)}, bf16[128,512]{1,0:T(8,128)(2,1)S(1)}, u32[]{:S(2)}, u32[]{:S(2)}) collective-permute-start(bf16[128,512]{1,0:T(8,128)(2,1)S(1)} %get-tuple-element.122), channel_id=1, source_target_pairs={{0,2},{1,3},{2,0},{3,1},{4,6},{5,7},{6,4},{7,5},{8,10},{9,11},{10,... | collective-permute-start | bytes 393224 | tf_op jit(solution)/shard_map/ppermute | solution.py:444
  165.4 6.5 %collective-permute-start.45 = (bf16[64,2048]{1,0:T(8,128)(2,1)S(1)}, bf16[64,2048]{1,0:T(8,128)(2,1)S(1)}, u32[]{:S(2)}, u32[]{:S(2)}) collective-permute-start(bf16[64,2048]{1,0:T(8,128)(2,1)S(1)} %get-tuple-element.134), channel_id=1, source_target_pairs={{0,8},{4,12},{8,0},{12,4},{16,24},{20,28},{24,16},{28,20},{1,9},{5... | collective-permute-start | bytes 786440 | tf_op jit(solution)/shard_map/ppermute | solution.py:438
  166.9 6.4 %collective-permute-start.44 = (bf16[64,2048]{1,0:T(8,128)(2,1)S(1)}, bf16[64,2048]{1,0:T(8,128)(2,1)S(1)}, u32[]{:S(2)}, u32[]{:S(2)}) collective-permute-start(bf16[64,2048]{1,0:T(8,128)(2,1)S(1)} %get-tuple-element.135), channel_id=1, source_target_pairs={{0,16},{4,20},{8,24},{12,28},{16,0},{20,4},{24,8},{28,12},{1,17},{... | collective-permute-start | bytes 786440 | tf_op jit(solution)/shard_map/ppermute | solution.py:438
  167.8 15.6 %collective-permute-start.41 = (bf16[128,512]{1,0:T(8,128)(2,1)S(1)}, bf16[128,512]{1,0:T(8,128)(2,1)S(1)}, u32[]{:S(2)}, u32[]{:S(2)}) collective-permute-start(bf16[128,512]{1,0:T(8,128)(2,1)S(1)} %get-tuple-element.123), channel_id=1, source_target_pairs={{0,3},{1,2},{2,1},{3,0},{4,7},{5,6},{6,5},{7,4},{8,11},{9,10},{10,... | collective-permute-start | bytes 393224 | tf_op jit(solution)/shard_map/ppermute | solution.py:444
  173.3 5.4 %copy-start.9 = (bf16[256,512]{1,0:T(8,128)(2,1)S(1)}, bf16[256,512]{1,0:T(8,128)(2,1)}, u32[]{:S(2)}) copy-start(bf16[256,512]{1,0:T(8,128)(2,1)} %cot_ref.3) | copy-start | bytes 786436
  174.3 9.2 %collective-permute-start.46 = (bf16[128,512]{1,0:T(8,128)(2,1)S(1)}, bf16[128,512]{1,0:T(8,128)(2,1)S(1)}, u32[]{:S(2)}, u32[]{:S(2)}) collective-permute-start(bf16[128,512]{1,0:T(8,128)(2,1)S(1)} %get-tuple-element.128), channel_id=1, source_target_pairs={{0,1},{1,0},{2,3},{3,2},{4,5},{5,4},{6,7},{7,6},{8,9},{9,8},{10,11... | collective-permute-start | bytes 393224 | tf_op jit(solution)/shard_map/ppermute | solution.py:444
  174.4 10.5 %collective-permute-start.47 = (bf16[128,512]{1,0:T(8,128)(2,1)S(1)}, bf16[128,512]{1,0:T(8,128)(2,1)S(1)}, u32[]{:S(2)}, u32[]{:S(2)}) collective-permute-start(bf16[128,512]{1,0:T(8,128)(2,1)S(1)} %get-tuple-element.129), channel_id=1, source_target_pairs={{0,2},{1,3},{2,0},{3,1},{4,6},{5,7},{6,4},{7,5},{8,10},{9,11},{10,... | collective-permute-start | bytes 393224 | tf_op jit(solution)/shard_map/ppermute | solution.py:444
  177.2 7.6 %collective-permute-start.48 = (bf16[128,512]{1,0:T(8,128)(2,1)S(1)}, bf16[128,512]{1,0:T(8,128)(2,1)S(1)}, u32[]{:S(2)}, u32[]{:S(2)}) collective-permute-start(bf16[128,512]{1,0:T(8,128)(2,1)S(1)} %get-tuple-element.130), channel_id=1, source_target_pairs={{0,3},{1,2},{2,1},{3,0},{4,7},{5,6},{6,5},{7,4},{8,11},{9,10},{10,... | collective-permute-start | bytes 393224 | tf_op jit(solution)/shard_map/ppermute | solution.py:444
  (4 other events, 4.3 us)
